TPU v7x, 32 devices: a whole 2x2x4 slice. The times are simulated.
32 devices in a mesh: expert: 4 (over y, x), dp: 4 (over z), segment: 2 (over core).
Axes of the slice: x: 2, y: 2, z: 4, core: 2. Of those that a mesh axis runs over, the one named last changes fastest.
Arguments:
- hidden_in: bfloat16 [256, 4, 4096], P(('expert', 'dp'), None, 'segment'), may hold values from -6 to 6
- cotangent: bfloat16 [256, 4, 4096], P(('expert', 'dp'), None, 'segment'), may hold values from -6 to 6
- cluster_ids: int32 [256], P(('expert', 'dp')), may hold values from 0 to 3, as said below
- w_down: bfloat16 [4, 2, 4096, 256], P('expert', 'segment'), may hold values from -0.09375 to 0.09375
- w_up: bfloat16 [4, 2, 256, 4096], P('expert', 'segment'), may hold values from -0.375 to 0.375
- gain: bfloat16 [4, 2, 4096], P('expert', 'segment'), may hold values from 0.25 to 1.75
Outputs:
- out_hidden: bfloat16 [256, 4, 4096], P(('expert', 'dp'), None, 'segment')
- grad_down: bfloat16 [4, 2, 4096, 256], P('expert', 'segment', 'dp')
- grad_up: bfloat16 [4, 2, 256, 4096], P('expert', 'segment', None, 'dp')
Inputs may be any that keep to these rules, and one draw needn't show every extreme that they name: `cluster_ids`: within each aligned block of 16 sequences (the sequences of one loader) no cluster appears more than 8 times, and one cluster, the same in every block, appears exactly 8 times in each block.
All inputs are finite; a program needn't handle non-finite values.
Results may differ from a plain program's by a relative error of at most 0.034.
Values may be sent and summed in bfloat16 or wider, within the bound.
No kernel may reach another device: no remote copies, remote signals or barrier semaphores. Data moves between devices by JAX's collectives and lax.ppermute only.
A program may use at most 64 MiB of HBM per device.

v0:
```python
import jax
import jax.numpy as jnp
from jax import lax
from jax.sharding import PartitionSpec as P

MICRO = 4


EPS = 1e-05
C_ZERO = 0.7978845608028654
C_ONE = 0.044715


def shifted(block, axis, distance):
    devices = range(lax.axis_size(axis))
    route = [(i - distance, i) for i in devices if i - distance in devices]
    return lax.ppermute(block, axis, route)


def from_root(block, axis, holder):
    block = jnp.where(lax.axis_index(axis) == holder, block, jnp.zeros_like(block))
    return lax.psum(block, axis)


def gelu_value(z):
    return 0.5 * z * (1.0 + jnp.tanh(C_ZERO * (z + C_ONE * z * z * z)))


def gelu_slope(z):
    tval = jnp.tanh(C_ZERO * (z + C_ONE * z * z * z))
    return 0.5 * (1.0 + tval) + 0.5 * z * (1.0 - tval * tval) * C_ZERO * (1.0 + 3.0 * C_ONE * z * z)


def normalize(hidden):
    wide = hidden.astype(jnp.float32)
    center = wide - jnp.mean(wide, axis=-1, keepdims=True)
    inverse = lax.rsqrt(jnp.mean(center * center, axis=-1, keepdims=True) + EPS)
    return (wide, center * inverse, inverse)


def phase_forward(hidden, w_dn, w_upper, scale):
    wide, normed, inverse = normalize(hidden)
    lowered = (normed * scale).astype(jnp.bfloat16)
    pre = jnp.dot(lowered, w_dn, preferred_element_type=jnp.float32)
    act = gelu_value(pre).astype(jnp.bfloat16)
    leaving = (wide + jnp.dot(act, w_upper, preferred_element_type=jnp.float32)).astype(
        jnp.bfloat16
    )
    return (leaving, pre)


def phase_backward(hidden, grad_in, pre, w_dn, w_upper, scale):
    wide, normed, inverse = normalize(hidden)
    lowered = (normed * scale).astype(jnp.bfloat16)
    act = gelu_value(pre).astype(jnp.bfloat16)
    d_act = jnp.dot(grad_in, w_upper.T, preferred_element_type=jnp.float32)
    d_pre = (d_act * gelu_slope(pre)).astype(jnp.bfloat16)
    d_low = jnp.dot(d_pre, w_dn.T, preferred_element_type=jnp.float32)
    d_norm = d_low * scale
    d_wide = inverse * (
        d_norm
        - jnp.mean(d_norm, axis=-1, keepdims=True)
        - normed * jnp.mean(d_norm * normed, axis=-1, keepdims=True)
    )
    grad_out = (grad_in.astype(jnp.float32) + d_wide).astype(jnp.bfloat16)
    return (grad_out, lowered, act, d_pre)


def put_slot(buffer, value, slot, valid):
    old_value = lax.dynamic_index_in_dim(buffer, slot, 0, keepdims=False)
    return lax.dynamic_update_index_in_dim(buffer, jnp.where(valid, value, old_value), slot, 0)


def on_device(hidden_in, cotangent, cluster_ids, w_down, w_up, gain):
    experts = lax.axis_size("expert")
    phases = lax.axis_size("segment")
    phase = lax.axis_index("segment")
    s_local, length, quarter = hidden_in.shape
    capacity = 2 * s_local // experts
    slots = experts * capacity
    same = (cluster_ids[:, None] == cluster_ids[None, :]).astype(jnp.int32)
    earlier = jnp.sum(jnp.tril(same, -1), axis=1)
    target = cluster_ids * capacity + earlier
    place = (jnp.arange(slots, dtype=jnp.int32)[:, None] == target[None, :]).astype(jnp.bfloat16)

    def to_slots(local):
        flat = local.reshape(s_local, -1)
        moved = jnp.dot(place, flat, preferred_element_type=jnp.float32).astype(jnp.bfloat16)
        return moved.reshape((slots,) + local.shape[1:])

    full_in, full_cot = (
        lax.all_gather(hidden_in, "segment", axis=2, tiled=True),
        lax.all_gather(cotangent, "segment", axis=2, tiled=True),
    )
    slot_in, slot_cot = (
        lax.all_to_all(to_slots(full_in), "expert", split_axis=0, concat_axis=0, tiled=True),
        lax.all_to_all(to_slots(full_cot), "expert", split_axis=0, concat_axis=0, tiled=True),
    )
    width = slot_in.shape[2]
    micro_rows = slots * length // MICRO
    inputs = slot_in.reshape(MICRO, micro_rows, width)
    cots = slot_cot.reshape(MICRO, micro_rows, width)
    w_dn = w_down[0, 0]
    w_upper = w_up[0, 0]
    rank = w_dn.shape[1]
    scale = gain[0, 0].astype(jnp.float32)
    ticks = MICRO + phases - 1

    def forward_tick(tick, carry):
        received, saved, pres, results = carry
        which = tick - phase
        valid = (which >= 0) & (which < MICRO)
        slot = jnp.clip(which, 0, MICRO - 1)
        first = lax.dynamic_index_in_dim(inputs, jnp.minimum(tick, MICRO - 1), 0, keepdims=False)
        entering = jnp.where(phase == 0, first, received)
        leaving, pre = phase_forward(entering, w_dn, w_upper, scale)
        saved = put_slot(saved, entering, slot, valid)
        pres = put_slot(pres, pre, slot, valid)
        results = put_slot(results, leaving, slot, valid & (phase == phases - 1))
        received = shifted(leaving, "segment", 1)
        return (received, saved, pres, results)

    start = (
        jnp.zeros((micro_rows, width), jnp.bfloat16),
        jnp.zeros((MICRO, micro_rows, width), jnp.bfloat16),
        jnp.zeros((MICRO, micro_rows, rank), jnp.float32),
        jnp.zeros((MICRO, micro_rows, width), jnp.bfloat16),
    )
    received, saved, pres, results = lax.fori_loop(0, ticks, forward_tick, start)

    def backward_tick(tick, carry):
        received, lows, acts, dpres, grads = carry
        which = tick - (phases - 1 - phase)
        valid = (which >= 0) & (which < MICRO)
        slot = jnp.clip(which, 0, MICRO - 1)
        last = lax.dynamic_index_in_dim(cots, jnp.minimum(tick, MICRO - 1), 0, keepdims=False)
        grad_in = jnp.where(phase == phases - 1, last, received)
        hidden = lax.dynamic_index_in_dim(saved, slot, 0, keepdims=False)
        pre = lax.dynamic_index_in_dim(pres, slot, 0, keepdims=False)
        grad_out, lowered, act, d_pre = phase_backward(hidden, grad_in, pre, w_dn, w_upper, scale)
        lows = put_slot(lows, lowered, slot, valid)
        acts = put_slot(acts, act, slot, valid)
        dpres = put_slot(dpres, d_pre, slot, valid)
        grads = put_slot(grads, grad_in, slot, valid)
        received = shifted(grad_out, "segment", -1)
        return (received, lows, acts, dpres, grads)

    start_back = (
        jnp.zeros((micro_rows, width), jnp.bfloat16),
        jnp.zeros((MICRO, micro_rows, width), jnp.bfloat16),
        jnp.zeros((MICRO, micro_rows, rank), jnp.bfloat16),
        jnp.zeros((MICRO, micro_rows, rank), jnp.bfloat16),
        jnp.zeros((MICRO, micro_rows, width), jnp.bfloat16),
    )
    received, lows, acts, dpres, grads = lax.fori_loop(0, ticks, backward_tick, start_back)
    contract = (((0,), (0,)), ((), ()))
    grad_dn = lax.dot_general(
        lows.reshape(-1, width),
        dpres.reshape(-1, rank),
        contract,
        preferred_element_type=jnp.float32,
    )
    grad_upper = lax.dot_general(
        acts.reshape(-1, rank),
        grads.reshape(-1, width),
        contract,
        preferred_element_type=jnp.float32,
    )
    summed_dn, summed_upper = (
        lax.psum_scatter(
            grad_dn.astype(jnp.bfloat16), "dp", scatter_dimension=0, tiled=True
        ).astype(jnp.float32),
        lax.psum_scatter(
            grad_upper.astype(jnp.bfloat16), "dp", scatter_dimension=1, tiled=True
        ).astype(jnp.float32),
    )
    returned = from_root(results, "segment", phases - 1)
    returned = returned.reshape(slots, length, width)
    own = lax.dynamic_slice_in_dim(returned, phase * quarter, quarter, 2)
    back = lax.all_to_all(own, "expert", split_axis=0, concat_axis=0, tiled=True)
    out_hidden = jnp.dot(place.T, back.reshape(slots, -1), preferred_element_type=jnp.float32)
    out_hidden = out_hidden.astype(jnp.bfloat16).reshape(s_local, length, quarter)
    return (
        out_hidden,
        summed_dn.astype(jnp.bfloat16)[None, None],
        summed_upper.astype(jnp.bfloat16)[None, None],
    )


def solution(mesh):
    return jax.shard_map(
        on_device,
        mesh=mesh,
        in_specs=(
            P(("expert", "dp"), None, "segment"),
            P(("expert", "dp"), None, "segment"),
            P(("expert", "dp")),
            P("expert", "segment", None, None),
            P("expert", "segment", None, None),
            P("expert", "segment", None),
        ),
        out_specs=(
            P(("expert", "dp"), None, "segment"),
            P("expert", "segment", "dp", None),
            P("expert", "segment", None, "dp"),
        ),
        check_vma=False,
    )
```

profile of v0, /device:TPU:0, one launch (start us, length us, event | category | flops | bytes accessed | tf_op | source)
XLA Modules:
  0.0 274.2 jit_solution(1920991320475464455)
XLA Ops:
  8.0 2.5 all_gather.6
  14.4 5.1 %all-to-all-start = ((bf16[32,4,4096]{2,1,0:T(4,128)(2,1)}), bf16[32,4,4096]{2,1,0:T(4,128)(2,1)S(1)}, u32[]{:S(2)}, u32[]{:S(2)}) async-start(bf16[32,4,4096]{2,1,0:T(4,128)(2,1)} %reshape.121), calls=%async_computation | async-start | bytes 2097152 | tf_op jit(solution)/shard_map/all_to_all | solution.py:96
  19.5 2.2 all_gather.7
  24.0 9.4 %all-to-all-done = bf16[32,4,4096]{2,1,0:T(4,128)(2,1)S(1)} async-done(((bf16[32,4,4096]{2,1,0:T(4,128)(2,1)}), bf16[32,4,4096]{2,1,0:T(4,128)(2,1)S(1)}, u32[]{:S(2)}, u32[]{:S(2)}) %all-to-all-start) | async-done | bytes 1048608 | tf_op jit(solution)/shard_map/all_to_all | solution.py:96
  33.4 4.3 %all-to-all-start.2 = ((bf16[32,4,4096]{2,1,0:T(4,128)(2,1)}), bf16[32,4,4096]{2,1,0:T(4,128)(2,1)}, u32[]{:S(2)}, u32[]{:S(2)}) async-start(bf16[32,4,4096]{2,1,0:T(4,128)(2,1)} %reshape.127), calls=%async_computation.2 | async-start | bytes 2097152 | tf_op jit(solution)/shard_map/all_to_all | solution.py:97
  41.4 45.5 %while.43 = (s32[]{:T(128)}, bf16[32,4096]{1,0:T(8,128)(2,1)}, bf16[4,32,4096]{2,1,0:T(8,128)(2,1)S(1)}, f32[4,32,256]{2,1,0:T(8,128)}, bf16[4,32,4096]{2,1,0:T(...) while((s32[]{:T(128)}, bf16[32,4096]{1,0:T(8,128)(2,1)}, ...), condition=%wide.region_4.5_spmd, body=%wide.region_1.4_spmd.sunk | while | flops 136527920 | bytes 19088892 | solution.py:129
  54.6 2.4 collective-permute-start
  63.9 2.4 collective-permute-start
  73.2 2.4 collective-permute-start
  82.5 2.4 collective-permute-start
  88.0 2.2 reshape.123
  90.3 2.1 reshape.128
  96.6 75.3 %while.44 = (s32[]{:T(128)}, bf16[32,4096]{1,0:T(8,128)(2,1)}, bf16[4,32,4096]{2,1,0:T(8,128)(2,1)}, bf16[4,32,256]{2,1,0:T(8,128)(2,1)}, bf16[4,32,256]{2,1,0:T...) while((s32[]{:T(128)}, bf16[32,4096]{1,0:T(8,128)(2,1)}, ...), condition=%wide.region_11.12_spmd, body=%wide.region_6.11_spmd.sunk | while | flops 138526752 | bytes 12031060 | solution.py:155
  99.9 1.9 bitcast_dynamic-update-slice_fusion.13
  101.8 2.9 %bitcast_dynamic-update-slice_fusion.14 = (bf16[4,32,256]{2,1,0:T(8,128)(2,1)}, bf16[32,256]{1,0:T(8,128)(2,1)S(1)}) fusion(bf16[4,32,256]{2,1,0:T(8,128)(2,1)} %get-tuple-element.861, s32[]{:T(128)S(6)} %min.41, bf16[1,32,256]{2,1,0:T(8,128)(2,1)} %constant_dynamic-slice_fusion.12, pred[]{:T(512)S(6)} %and.31, ...), kind=kOutput, calls=%fused_computation.82.clone.1 | convolution fusion | flops 67272704 | bytes 2441221 | tf_op jit(solution)/shard_map/while/body/eval_jaxpr/dot_general | solution.py:56
  107.8 1.8 fusion.97
  115.0 1.9 bitcast_dynamic-update-slice_fusion.13
  116.8 2.9 %bitcast_dynamic-update-slice_fusion.14 = (bf16[4,32,256]{2,1,0:T(8,128)(2,1)}, bf16[32,256]{1,0:T(8,128)(2,1)S(1)}) fusion(bf16[4,32,256]{2,1,0:T(8,128)(2,1)} %get-tuple-element.861, s32[]{:T(128)S(6)} %min.41, bf16[1,32,256]{2,1,0:T(8,128)(2,1)} %constant_dynamic-slice_fusion.12, pred[]{:T(512)S(6)} %and.31, ...), kind=kOutput, calls=%fused_computation.82.clone.1 | convolution fusion | flops 67272704 | bytes 2441221 | tf_op jit(solution)/shard_map/while/body/eval_jaxpr/dot_general | solution.py:56
  122.8 1.8 fusion.97
  130.0 1.9 bitcast_dynamic-update-slice_fusion.13
  131.9 2.9 %bitcast_dynamic-update-slice_fusion.14 = (bf16[4,32,256]{2,1,0:T(8,128)(2,1)}, bf16[32,256]{1,0:T(8,128)(2,1)S(1)}) fusion(bf16[4,32,256]{2,1,0:T(8,128)(2,1)} %get-tuple-element.861, s32[]{:T(128)S(6)} %min.41, bf16[1,32,256]{2,1,0:T(8,128)(2,1)} %constant_dynamic-slice_fusion.12, pred[]{:T(512)S(6)} %and.31, ...), kind=kOutput, calls=%fused_computation.82.clone.1 | convolution fusion | flops 67272704 | bytes 2441221 | tf_op jit(solution)/shard_map/while/body/eval_jaxpr/dot_general | solution.py:56
  145.1 1.8 bitcast_dynamic-update-slice_fusion.13
  146.9 2.9 %bitcast_dynamic-update-slice_fusion.14 = (bf16[4,32,256]{2,1,0:T(8,128)(2,1)}, bf16[32,256]{1,0:T(8,128)(2,1)S(1)}) fusion(bf16[4,32,256]{2,1,0:T(8,128)(2,1)} %get-tuple-element.861, s32[]{:T(128)S(6)} %min.41, bf16[1,32,256]{2,1,0:T(8,128)(2,1)} %constant_dynamic-slice_fusion.12, pred[]{:T(512)S(6)} %and.31, ...), kind=kOutput, calls=%fused_computation.82.clone.1 | convolution fusion | flops 67272704 | bytes 2441221 | tf_op jit(solution)/shard_map/while/body/eval_jaxpr/dot_general | solution.py:56
  152.9 1.8 fusion.97
  160.1 1.8 bitcast_dynamic-update-slice_fusion.13
  161.9 2.9 %bitcast_dynamic-update-slice_fusion.14 = (bf16[4,32,256]{2,1,0:T(8,128)(2,1)}, bf16[32,256]{1,0:T(8,128)(2,1)S(1)}) fusion(bf16[4,32,256]{2,1,0:T(8,128)(2,1)} %get-tuple-element.861, s32[]{:T(128)S(6)} %min.41, bf16[1,32,256]{2,1,0:T(8,128)(2,1)} %constant_dynamic-slice_fusion.12, pred[]{:T(512)S(6)} %and.31, ...), kind=kOutput, calls=%fused_computation.82.clone.1 | convolution fusion | flops 67272704 | bytes 2441221 | tf_op jit(solution)/shard_map/while/body/eval_jaxpr/dot_general | solution.py:56
  168.0 1.8 fusion.97
  171.8 3.3 %fusion.56 = bf16[4096,256]{1,0:T(8,128)(2,1)} fusion(bf16[4,32,4096]{2,1,0:T(8,128)(2,1)} %get-tuple-element.529, bf16[4,32,256]{2,1,0:T(8,128)(2,1)} %get-tuple-element.530), kind=kOutput, calls=%fused_computation.95 | convolution fusion | flops 269484032 | bytes 3211264 | tf_op jit(solution)/shard_map/dot_general | solution.py:157
  176.4 2.0 fusion.57
  179.8 13.4 %all_to_all.15 = bf16[32,4,2048]{2,1,0:T(4,128)(2,1)S(1)} all-to-all(bf16[32,4,2048]{2,1,0:T(4,128)(2,1)S(1)} %constant_dynamic-slice_fusion.5), channel_id=1, replica_groups=mesh['expert'=4,'dp'=4,'segment'=2] {'expert'}, dimensions={0} | all-to-all | bytes 1048576 | tf_op jit(solution)/shard_map/all_to_all | solution.py:180
  194.7 26.6 %reduce-scatter.3.cloned.1.call-done = bf16[1024,256]{1,0:T(8,128)(2,1)} async-done(((bf16[4096,256]{1,0:T(8,128)(2,1)}), bf16[1024,256]{1,0:T(8,128)(2,1)}) %reduce-scatter.3.cloned.1.call-update) | async-done | bytes 524304 | tf_op jit(solution)/shard_map/reduce_scatter | solution.py:170
  221.3 45.5 %reduce-scatter.5.cloned.1.call-done = bf16[256,1024]{1,0:T(8,128)(2,1)} async-done(((bf16[256,4096]{1,0:T(8,128)(2,1)}), bf16[256,1024]{1,0:T(8,128)(2,1)}) %reduce-scatter.5.cloned.1.call-update) | async-done | bytes 524304 | tf_op jit(solution)/shard_map/reduce_scatter | solution.py:173
  (221 shorter events, 98.8 us)
Async XLA Ops:
  12.3 9.6 %copy-start.12 = (s32[16]{0:T(128)}, s32[16]{0:T(128)S(1)}, u32[]{:S(2)}) copy-start(s32[16]{0:T(128)S(1)} %multiply_add_fusion.3) | copy-start | bytes 196
  12.8 6.7 %copy-start.11 = (bf16[1,1,4096]{2,1,0:T(2,128)(2,1)S(1)}, bf16[1,1,4096]{2,1,0:T(2,128)(2,1)}, u32[]{:S(2)}) copy-start(bf16[1,1,4096]{2,1,0:T(2,128)(2,1)} %param.15) | copy-start | bytes 24580
  12.8 6.7 %copy-start.7 = (bf16[16,4,2048]{2,1,0:T(4,128)(2,1)S(1)}, bf16[16,4,2048]{2,1,0:T(4,128)(2,1)}, u32[]{:S(2)}) copy-start(bf16[16,4,2048]{2,1,0:T(4,128)(2,1)} %param.11) | copy-start | bytes 786436
  14.4 19.0 %all-to-all-start = ((bf16[32,4,4096]{2,1,0:T(4,128)(2,1)}), bf16[32,4,4096]{2,1,0:T(4,128)(2,1)S(1)}, u32[]{:S(2)}, u32[]{:S(2)}) async-start(bf16[32,4,4096]{2,1,0:T(4,128)(2,1)} %reshape.121), calls=%async_computation | async-start | bytes 2097152 | tf_op jit(solution)/shard_map/all_to_all | solution.py:96
  33.4 56.9 %all-to-all-start.2 = ((bf16[32,4,4096]{2,1,0:T(4,128)(2,1)}), bf16[32,4,4096]{2,1,0:T(4,128)(2,1)}, u32[]{:S(2)}, u32[]{:S(2)}) async-start(bf16[32,4,4096]{2,1,0:T(4,128)(2,1)} %reshape.127), calls=%async_computation.2 | async-start | bytes 2097152 | tf_op jit(solution)/shard_map/all_to_all | solution.py:97
  37.7 3.8 %copy-start = (bf16[1,1,4096,256]{3,2,1,0:T(8,128)(2,1)S(1)}, bf16[1,1,4096,256]{3,2,1,0:T(8,128)(2,1)}, u32[]{:S(2)}) copy-start(bf16[1,1,4096,256]{3,2,1,0:T(8,128)(2,1)} %param.13) | copy-start | bytes 6291460
  37.7 140.8 %all-reduce.2.cloned.1.call-start = ((), (), s32[]{:S(2)}) async-start(), calls=%async_computation.5 | async-start | bytes 2097152 | tf_op jit(solution)/shard_map/psum | solution.py:22
  46.3 2.6 collective-permute-start
  54.6 3.7 %collective-permute-start = (bf16[32,4096]{1,0:T(8,128)(2,1)}, bf16[32,4096]{1,0:T(8,128)(2,1)S(1)}, u32[]{:S(2)}, u32[]{:S(2)}) collective-permute-start(bf16[32,4096]{1,0:T(8,128)(2,1)} %get-tuple-element.764), channel_id=1, source_target_pairs={{0,1},{2,3},{4,5},{6,7},{8,9},{10,11},{12,13},{14,15},{16,17},{18,... | collective-permute-start | bytes 786440 | tf_op jit(solution)/shard_map/while/body/eval_jaxpr/ppermute | solution.py:17
  59.8 2.9 %copy-start.1 = (bf16[256,4096]{1,0:T(8,128)(2,1)S(1)}, bf16[256,4096]{1,0:T(8,128)(2,1)}, u32[]{:S(2)}) copy-start(bf16[256,4096]{1,0:T(8,128)(2,1)} %get-tuple-element.832) | copy-start | bytes 6291460 | tf_op jit(solution)/shard_map/while
  63.9 3.7 %collective-permute-start = (bf16[32,4096]{1,0:T(8,128)(2,1)}, bf16[32,4096]{1,0:T(8,128)(2,1)S(1)}, u32[]{:S(2)}, u32[]{:S(2)}) collective-permute-start(bf16[32,4096]{1,0:T(8,128)(2,1)} %get-tuple-element.764), channel_id=1, source_target_pairs={{0,1},{2,3},{4,5},{6,7},{8,9},{10,11},{12,13},{14,15},{16,17},{18,... | collective-permute-start | bytes 786440 | tf_op jit(solution)/shard_map/while/body/eval_jaxpr/ppermute | solution.py:17
  73.2 3.7 %collective-permute-start = (bf16[32,4096]{1,0:T(8,128)(2,1)}, bf16[32,4096]{1,0:T(8,128)(2,1)S(1)}, u32[]{:S(2)}, u32[]{:S(2)}) collective-permute-start(bf16[32,4096]{1,0:T(8,128)(2,1)} %get-tuple-element.764), channel_id=1, source_target_pairs={{0,1},{2,3},{4,5},{6,7},{8,9},{10,11},{12,13},{14,15},{16,17},{18,... | collective-permute-start | bytes 786440 | tf_op jit(solution)/shard_map/while/body/eval_jaxpr/ppermute | solution.py:17
  82.5 3.7 %collective-permute-start = (bf16[32,4096]{1,0:T(8,128)(2,1)}, bf16[32,4096]{1,0:T(8,128)(2,1)S(1)}, u32[]{:S(2)}, u32[]{:S(2)}) collective-permute-start(bf16[32,4096]{1,0:T(8,128)(2,1)} %get-tuple-element.764), channel_id=1, source_target_pairs={{0,1},{2,3},{4,5},{6,7},{8,9},{10,11},{12,13},{14,15},{16,17},{18,... | collective-permute-start | bytes 786440 | tf_op jit(solution)/shard_map/while/body/eval_jaxpr/ppermute | solution.py:17
  90.2 6.4 %copy-start.5 = (f32[4,32,256]{2,1,0:T(8,128)S(1)}, f32[4,32,256]{2,1,0:T(8,128)}, u32[]{:S(2)}) copy-start(f32[4,32,256]{2,1,0:T(8,128)} %get-tuple-element.850) | copy-start | bytes 393220
  90.2 131.1 %reduce-scatter.3.cloned.1.call-start = ((), (), s32[]{:S(2)}) async-start(), calls=%async_computation.6 | async-start | bytes 2621440 | tf_op jit(solution)/shard_map/reduce_scatter | solution.py:170
  99.9 4.8 %copy-start.9 = (f32[32]{0:T(128)S(1)}, f32[32]{0:T(128)}, u32[]{:S(2)}) copy-start(f32[32]{0:T(128)} %copy-done.8) | copy-start | bytes 388 | tf_op jit(solution)/shard_map/while
  99.9 4.8 %copy-start.10 = (f32[32]{0:T(128)S(1)}, f32[32]{0:T(128)}, u32[]{:S(2)}) copy-start(f32[32]{0:T(128)} %add_rsqrt_fusion.5) | copy-start | bytes 388 | tf_op jit(solution)/shard_map/while
  106.5 4.5 %collective-permute-start.1 = (bf16[32,4096]{1,0:T(8,128)(2,1)}, bf16[32,4096]{1,0:T(8,128)(2,1)S(1)}, u32[]{:S(2)}, u32[]{:S(2)}) collective-permute-start(bf16[32,4096]{1,0:T(8,128)(2,1)} %fusion.96), channel_id=1, source_target_pairs={{1,0},{3,2},{5,4},{7,6},{9,8},{11,10},{13,12},{15,14},{17,16},{19,... | collective-permute-start | bytes 786440 | tf_op jit(solution)/shard_map/while/body/eval_jaxpr/ppermute | solution.py:17
  114.9 4.8 %copy-start.9 = (f32[32]{0:T(128)S(1)}, f32[32]{0:T(128)}, u32[]{:S(2)}) copy-start(f32[32]{0:T(128)} %copy-done.8) | copy-start | bytes 388 | tf_op jit(solution)/shard_map/while
  114.9 4.8 %copy-start.10 = (f32[32]{0:T(128)S(1)}, f32[32]{0:T(128)}, u32[]{:S(2)}) copy-start(f32[32]{0:T(128)} %add_rsqrt_fusion.5) | copy-start | bytes 388 | tf_op jit(solution)/shard_map/while
  121.5 4.5 %collective-permute-start.1 = (bf16[32,4096]{1,0:T(8,128)(2,1)}, bf16[32,4096]{1,0:T(8,128)(2,1)S(1)}, u32[]{:S(2)}, u32[]{:S(2)}) collective-permute-start(bf16[32,4096]{1,0:T(8,128)(2,1)} %fusion.96), channel_id=1, source_target_pairs={{1,0},{3,2},{5,4},{7,6},{9,8},{11,10},{13,12},{15,14},{17,16},{19,... | collective-permute-start | bytes 786440 | tf_op jit(solution)/shard_map/while/body/eval_jaxpr/ppermute | solution.py:17
  130.0 4.8 %copy-start.9 = (f32[32]{0:T(128)S(1)}, f32[32]{0:T(128)}, u32[]{:S(2)}) copy-start(f32[32]{0:T(128)} %copy-done.8) | copy-start | bytes 388 | tf_op jit(solution)/shard_map/while
  130.0 4.8 %copy-start.10 = (f32[32]{0:T(128)S(1)}, f32[32]{0:T(128)}, u32[]{:S(2)}) copy-start(f32[32]{0:T(128)} %add_rsqrt_fusion.5) | copy-start | bytes 388 | tf_op jit(solution)/shard_map/while
  136.6 4.5 %collective-permute-start.1 = (bf16[32,4096]{1,0:T(8,128)(2,1)}, bf16[32,4096]{1,0:T(8,128)(2,1)S(1)}, u32[]{:S(2)}, u32[]{:S(2)}) collective-permute-start(bf16[32,4096]{1,0:T(8,128)(2,1)} %fusion.96), channel_id=1, source_target_pairs={{1,0},{3,2},{5,4},{7,6},{9,8},{11,10},{13,12},{15,14},{17,16},{19,... | collective-permute-start | bytes 786440 | tf_op jit(solution)/shard_map/while/body/eval_jaxpr/ppermute | solution.py:17
  145.0 4.8 %copy-start.9 = (f32[32]{0:T(128)S(1)}, f32[32]{0:T(128)}, u32[]{:S(2)}) copy-start(f32[32]{0:T(128)} %copy-done.8) | copy-start | bytes 388 | tf_op jit(solution)/shard_map/while
  145.0 4.8 %copy-start.10 = (f32[32]{0:T(128)S(1)}, f32[32]{0:T(128)}, u32[]{:S(2)}) copy-start(f32[32]{0:T(128)} %add_rsqrt_fusion.5) | copy-start | bytes 388 | tf_op jit(solution)/shard_map/while
  151.6 4.5 %collective-permute-start.1 = (bf16[32,4096]{1,0:T(8,128)(2,1)}, bf16[32,4096]{1,0:T(8,128)(2,1)S(1)}, u32[]{:S(2)}, u32[]{:S(2)}) collective-permute-start(bf16[32,4096]{1,0:T(8,128)(2,1)} %fusion.96), channel_id=1, source_target_pairs={{1,0},{3,2},{5,4},{7,6},{9,8},{11,10},{13,12},{15,14},{17,16},{19,... | collective-permute-start | bytes 786440 | tf_op jit(solution)/shard_map/while/body/eval_jaxpr/ppermute | solution.py:17
  160.1 4.8 %copy-start.9 = (f32[32]{0:T(128)S(1)}, f32[32]{0:T(128)}, u32[]{:S(2)}) copy-start(f32[32]{0:T(128)} %copy-done.8) | copy-start | bytes 388 | tf_op jit(solution)/shard_map/while
  160.1 4.8 %copy-start.10 = (f32[32]{0:T(128)S(1)}, f32[32]{0:T(128)}, u32[]{:S(2)}) copy-start(f32[32]{0:T(128)} %add_rsqrt_fusion.5) | copy-start | bytes 388 | tf_op jit(solution)/shard_map/while
  166.7 4.5 %collective-permute-start.1 = (bf16[32,4096]{1,0:T(8,128)(2,1)}, bf16[32,4096]{1,0:T(8,128)(2,1)S(1)}, u32[]{:S(2)}, u32[]{:S(2)}) collective-permute-start(bf16[32,4096]{1,0:T(8,128)(2,1)} %fusion.96), channel_id=1, source_target_pairs={{1,0},{3,2},{5,4},{7,6},{9,8},{11,10},{13,12},{15,14},{17,16},{19,... | collective-permute-start | bytes 786440 | tf_op jit(solution)/shard_map/while/body/eval_jaxpr/ppermute | solution.py:17
  175.2 91.6 %reduce-scatter.5.cloned.1.call-start = ((), (), s32[]{:S(2)}) async-start(), calls=%async_computation.7 | async-start | bytes 2621440 | tf_op jit(solution)/shard_map/reduce_scatter | solution.py:173
  178.4 15.0 %copy-start.13 = (s32[16]{0:T(128)S(1)}, s32[16]{0:T(128)}, u32[]{:S(2)}) copy-start(s32[16]{0:T(128)} %copy-done.12) | copy-start | bytes 196
  (21 other events, 31.6 us)
Sparse Core Ops, SparseCore 0:
  90.3 22.4 all-reduce.1
Sparse Core Ops, SparseCore 1:
  175.3 46.0 reduce-scatter.2
  224.0 42.7 reduce-scatter.4
where the time goes:
time: 276 us; the launch traced here: 274 us
  waiting for transfers between devices  88.3 us (32%)
  other arithmetic  45.8 us (17%)
  local copies, waits for them, and re-layouts  42.1 us (15%)
  matrix products  37.2 us (13%)
  starting transfers between devices  26.6 us (10%)
  blocking collectives  18.1 us (7%)
  between operations  15.6 us (6%)
    reduce_scatter x1, waiting for transfers between devices, on_device(): lax.psum_scatter(grad_upper.astype(jnp.bfloat16), 'dp', scatter_dimension...  45.5 us
    dynamic_update_slice x20, other arithmetic, put_slot(): lax.dynamic_update_index_in_dim(buffer, jnp.where(valid, value, old_value...  31.6 us
    reduce_scatter x1, waiting for transfers between devices, on_device(): lax.psum_scatter(grad_dn.astype(jnp.bfloat16), 'dp', scatter_dimension=0,...  26.6 us
    ppermute x10, starting transfers between devices, shifted(): return lax.ppermute(block, axis, route)  17.1 us
    dynamic_slice x20, local copies, waits for them, and re-layouts, put_slot(): old_value = lax.dynamic_index_in_dim(buffer, slot, 0, keepdims=False)  15.4 us
    dot_general x5, matrix products, phase_backward(): d_act = jnp.dot(grad_in, w_upper.T, preferred_element_type=jnp.float32)  14.6 us
    all_to_all x1, blocking collectives, on_device(): lax.all_to_all(own, 'expert', split_axis=0, concat_axis=0, tiled=True)  13.4 us
    all_to_all x1, waiting for transfers between devices, on_device(): lax.all_to_all(to_slots(full_in), 'expert', split_axis=0, concat_axis=0,...  9.41 us
  transfers between devices with their start and end apart: 15, of which 8 were waited for; matrix products, arithmetic and copies ran while one was open for 41% of the time, Pallas kernels for 0%

commit v1 on v0

--- a/solution.py
+++ b/solution.py
@@ -1,6 +1,10 @@
+import functools
+
 import jax
 import jax.numpy as jnp
 from jax import lax
+from jax.experimental import pallas as pl
+from jax.experimental.pallas import tpu as pltpu
 from jax.sharding import PartitionSpec as P
 
 MICRO = 4
@@ -71,7 +75,7 @@
     return lax.dynamic_update_index_in_dim(buffer, jnp.where(valid, value, old_value), slot, 0)
 
 
-def on_device(hidden_in, cotangent, cluster_ids, w_down, w_up, gain):
+def on_device_pipelined(hidden_in, cotangent, cluster_ids, w_down, w_up, gain):
     experts = lax.axis_size("expert")
     phases = lax.axis_size("segment")
     phase = lax.axis_index("segment")
@@ -187,7 +191,412 @@
     )
 
 
+CHUNK = 512
+VMEM_LIMIT = 56 * 1024 * 1024
+TRANS_RHS = (((1,), (1,)), ((), ()))
+TRANS_LHS = (((0,), (0,)), ((), ()))
+
+
+def matmul(left, right):
+    return jnp.dot(left, right, preferred_element_type=jnp.float32)
+
+
+def placement(ids_row, ids_col, length, capacity, slots):
+    rows = ids_row.shape[1]
+    at_col = lax.broadcasted_iota(jnp.int32, (rows, rows), 0)
+    at_row = lax.broadcasted_iota(jnp.int32, (rows, rows), 1)
+    first_token = lax.rem(at_col, length) == 0
+    before = at_col // length < at_row // length
+    counted = (ids_col == ids_row) & first_token & before
+    rank = jnp.sum(counted.astype(jnp.int32), axis=0, keepdims=True)
+    token = lax.rem(at_row[:1], length)
+    target = (ids_row * capacity + rank) * length + token
+    packed = lax.broadcasted_iota(jnp.int32, (slots * length, rows), 0)
+    return (packed == target).astype(jnp.float32).astype(jnp.bfloat16)
+
+
+def pack_kernel(length, capacity, slots, ids_row, ids_col, hidden, cot, send):
+    place = placement(ids_row[...], ids_col[...], length, capacity, slots)
+    groups, _, rows, _ = send.shape
+    for which, source in enumerate((hidden, cot)):
+        moved = matmul(place, source[...]).astype(jnp.bfloat16)
+        for group in range(groups):
+            send[group, which] = moved[group * rows : (group + 1) * rows]
+
+
+def unpack_kernel(length, capacity, slots, ids_row, ids_col, back, out):
+    place = placement(ids_row[...], ids_col[...], length, capacity, slots)
+    groups, rows, width = back.shape
+    stacked = back[...].reshape(groups * rows, width)
+    out[...] = lax.dot_general(
+        place, stacked, TRANS_LHS, preferred_element_type=jnp.float32
+    ).astype(jnp.bfloat16)
+
+
+def split_three(value):
+    top = value.astype(jnp.bfloat16)
+    rest = value - top.astype(jnp.float32)
+    mid = rest.astype(jnp.bfloat16)
+    low = (rest - mid.astype(jnp.float32)).astype(jnp.bfloat16)
+    return [top.astype(jnp.float32), mid.astype(jnp.float32), low.astype(jnp.float32)]
+
+
+def chain_kernel(
+    recv, own_dn, own_up, own_gain, other_dn, other_up, other_gain,
+    out, small,
+    dn_buf, up_buf, gain_buf, entering, middle, d_norms, sems,
+):
+    phase = lax.axis_index("segment")
+    experts, phases, _, rows, part = recv.shape
+    tokens = experts * rows
+    width = phases * part
+    rank = dn_buf.shape[2]
+
+    def fetch(source, buffer, index):
+        return pltpu.make_async_copy(source, buffer.at[index], sems.at[index])
+
+    own = ((own_dn, dn_buf, 0), (own_up, up_buf, 2), (own_gain, gain_buf, 4))
+    other = ((other_dn, dn_buf, 0), (other_up, up_buf, 2), (other_gain, gain_buf, 4))
+
+    def copies(sources, at):
+        return [
+            pltpu.make_async_copy(source, buffer.at[at], sems.at[base + at])
+            for source, buffer, base in sources
+        ]
+
+    for at in range(2):
+        mine = phase == at
+
+        @pl.when(mine)
+        def _():
+            for copy in copies(own, at):
+                copy.start()
+
+        @pl.when(jnp.logical_not(mine))
+        def _():
+            for copy in copies(other, at):
+                copy.start()
+
+    waits = [copies(own, at) for at in range(2)]
+
+    def block(which, col):
+        half, start = col // part, col % part
+        return jnp.concatenate(
+            [recv[e, half, which, :, start : start + CHUNK] for e in range(experts)], axis=0
+        )
+
+    def lanes(value):
+        total = value[:, :128]
+        for start in range(128, value.shape[1], 128):
+            total = total + value[:, start : start + 128]
+        return total
+
+    def row_sum(parts):
+        return jnp.sum(parts, axis=1, keepdims=True)
+
+    cols = range(0, width, CHUNK)
+    total = jnp.zeros((tokens, 128), jnp.float32)
+    for col in cols:
+        value = block(0, col)
+        entering[:, col : col + CHUNK] = value
+        total = total + lanes(value.astype(jnp.float32))
+    mean_0 = row_sum(total) / width
+    total = jnp.zeros((tokens, 128), jnp.float32)
+    for col in cols:
+        center = entering[:, col : col + CHUNK].astype(jnp.float32) - mean_0
+        total = total + lanes(center * center)
+    inverse_0 = lax.rsqrt(row_sum(total) / width + EPS)
+
+    waits[0][0].wait()
+    waits[0][2].wait()
+    pre_0 = jnp.zeros((tokens, rank), jnp.float32)
+    for col in cols:
+        at = slice(col, col + CHUNK)
+        normed = (entering[:, at].astype(jnp.float32) - mean_0) * inverse_0
+        lowered = (normed * gain_buf[0, :, at].astype(jnp.float32)).astype(jnp.bfloat16)
+        pre_0 = pre_0 + matmul(lowered, dn_buf[0, at, :])
+    act_0 = gelu_value(pre_0).astype(jnp.bfloat16)
+    slope_0 = gelu_slope(pre_0)
+
+    waits[0][1].wait()
+    total = jnp.zeros((tokens, 128), jnp.float32)
+    for col in cols:
+        at = slice(col, col + CHUNK)
+        value = (
+            entering[:, at].astype(jnp.float32) + matmul(act_0, up_buf[0, :, at])
+        ).astype(jnp.bfloat16)
+        middle[:, at] = value
+        total = total + lanes(value.astype(jnp.float32))
+    mean_1 = row_sum(total) / width
+    total = jnp.zeros((tokens, 128), jnp.float32)
+    for col in cols:
+        center = middle[:, col : col + CHUNK].astype(jnp.float32) - mean_1
+        total = total + lanes(center * center)
+    inverse_1 = lax.rsqrt(row_sum(total) / width + EPS)
+
+    waits[1][0].wait()
+    waits[1][2].wait()
+    pre_1 = jnp.zeros((tokens, rank), jnp.float32)
+    for col in cols:
+        at = slice(col, col + CHUNK)
+        normed = (middle[:, at].astype(jnp.float32) - mean_1) * inverse_1
+        lowered = (normed * gain_buf[1, :, at].astype(jnp.float32)).astype(jnp.bfloat16)
+        pre_1 = pre_1 + matmul(lowered, dn_buf[1, at, :])
+    act_1 = gelu_value(pre_1).astype(jnp.bfloat16)
+    slope_1 = gelu_slope(pre_1)
+
+    waits[1][1].wait()
+    d_act = jnp.zeros((tokens, rank), jnp.float32)
+    for col in cols:
+        at = slice(col, col + CHUNK)
+        leaving = (
+            middle[:, at].astype(jnp.float32) + matmul(act_1, up_buf[1, :, at])
+        ).astype(jnp.bfloat16)
+        half, start = col // part, col % part
+        for e in range(experts):
+            out[e, half, :, start : start + CHUNK] = leaving[e * rows : (e + 1) * rows]
+        d_act = d_act + lax.dot_general(
+            block(1, col), up_buf[1, :, at], TRANS_RHS, preferred_element_type=jnp.float32
+        )
+    d_pre_1 = (d_act * slope_1).astype(jnp.bfloat16)
+
+    total = jnp.zeros((tokens, 128), jnp.float32)
+    cross = jnp.zeros((tokens, 128), jnp.float32)
+    for col in cols:
+        at = slice(col, col + CHUNK)
+        d_low = lax.dot_general(
+            d_pre_1, dn_buf[1, at, :], TRANS_RHS, preferred_element_type=jnp.float32
+        )
+        d_norm = d_low * gain_buf[1, :, at].astype(jnp.float32)
+        normed = (middle[:, at].astype(jnp.float32) - mean_1) * inverse_1
+        d_norms[:, at] = d_norm
+        total = total + lanes(d_norm)
+        cross = cross + lanes(d_norm * normed)
+    shift = row_sum(total) / width
+    along = row_sum(cross) / width
+    d_act = jnp.zeros((tokens, rank), jnp.float32)
+    for col in cols:
+        at = slice(col, col + CHUNK)
+        normed = (middle[:, at].astype(jnp.float32) - mean_1) * inverse_1
+        grad = (
+            block(1, col).astype(jnp.float32)
+            + inverse_1 * (d_norms[:, at] - shift - normed * along)
+        ).astype(jnp.bfloat16)
+        d_act = d_act + lax.dot_general(
+            grad, up_buf[0, :, at], TRANS_RHS, preferred_element_type=jnp.float32
+        )
+    d_pre_0 = (d_act * slope_0).astype(jnp.bfloat16)
+
+    for at, value in enumerate((act_0, act_1, d_pre_0, d_pre_1)):
+        small[:, at * rank : (at + 1) * rank] = value
+    lane = lax.broadcasted_iota(jnp.int32, (tokens, 128), 1)
+    stats = jnp.zeros((tokens, 128), jnp.float32)
+    at = 0
+    for column in (mean_0, inverse_0, mean_1, inverse_1, shift, along):
+        for piece in split_three(column):
+            stats = jnp.where(lane == at, piece, stats)
+            at += 1
+    small[:, 4 * rank :] = stats.astype(jnp.bfloat16)
+
+
+def gradient_kernel(
+    mine, theirs, small, own_dn, own_up, own_gain, other_dn, other_up, other_gain,
+    grad_dn, grad_upper,
+    dn_buf, up_buf, gain_buf, lows, grads, sems,
+):
+    phase = lax.axis_index("segment")
+    place = lax.axis_index("dp")
+    sources, _, rows, half = mine.shape
+    tokens = sources * rows
+    slab = 2 * half
+    rank = dn_buf.shape[1]
+    features = pl.ds(pl.multiple_of(place * slab, slab), slab)
+
+    def copies(up, gain_first, dn, gain_second):
+        return (
+            pltpu.make_async_copy(up.at[:, features], up_buf, sems.at[0]),
+            pltpu.make_async_copy(dn.at[features, :], dn_buf, sems.at[1]),
+            pltpu.make_async_copy(gain_first.at[:, features], gain_buf.at[0], sems.at[2]),
+            pltpu.make_async_copy(gain_second.at[:, features], gain_buf.at[1], sems.at[3]),
+        )
+
+    @pl.when(phase == 0)
+    def _():
+        for copy in copies(own_up, own_gain, other_dn, other_gain):
+            copy.start()
+
+    @pl.when(phase != 0)
+    def _():
+        for copy in copies(other_up, other_gain, own_dn, own_gain):
+            copy.start()
+
+    for copy in copies(own_up, own_gain, other_dn, other_gain):
+        copy.wait()
+
+    def column(at, index):
+        stats = small[at, 4 * rank :].astype(jnp.float32)
+        base = 3 * index
+        return (
+            stats[:, base : base + 1]
+            + stats[:, base + 1 : base + 2]
+            + stats[:, base + 2 : base + 3]
+        )
+
+    for source in range(sources):
+        at = slice(source * rows, (source + 1) * rows)
+        mean_0, inverse_0, mean_1, inverse_1, shift, along = [
+            column(at, index) for index in range(6)
+        ]
+        act_0 = small[at, :rank]
+        d_pre_1 = small[at, 3 * rank : 4 * rank]
+        for near, data in ((True, mine), (False, theirs)):
+            core = phase if near else 1 - phase
+            cols = pl.ds(pl.multiple_of(core * half, half), half)
+            wide = data[source, 0].astype(jnp.float32)
+            grad_in = data[source, 1]
+            middle = (wide + matmul(act_0, up_buf[:, cols])).astype(jnp.bfloat16)
+            normed = (middle.astype(jnp.float32) - mean_1) * inverse_1
+
+            @pl.when(phase == 0)
+            def _():
+                first = (wide - mean_0) * inverse_0 * gain_buf[0, :, cols].astype(jnp.float32)
+                lows[at, cols] = first.astype(jnp.bfloat16)
+                d_norm = lax.dot_general(
+                    d_pre_1, dn_buf[cols, :], TRANS_RHS, preferred_element_type=jnp.float32
+                ) * gain_buf[1, :, cols].astype(jnp.float32)
+                grads[at, cols] = (
+                    grad_in.astype(jnp.float32)
+                    + inverse_1 * (d_norm - shift - normed * along)
+                ).astype(jnp.bfloat16)
+
+            @pl.when(phase != 0)
+            def _():
+                second = normed * gain_buf[1, :, cols].astype(jnp.float32)
+                lows[at, cols] = second.astype(jnp.bfloat16)
+                grads[at, cols] = grad_in
+
+    def finish(act, d_pre):
+        grad_dn[...] = lax.dot_general(
+            lows[...], d_pre, TRANS_LHS, preferred_element_type=jnp.float32
+        ).astype(jnp.bfloat16)
+        grad_upper[...] = lax.dot_general(
+            act, grads[...], TRANS_LHS, preferred_element_type=jnp.float32
+        ).astype(jnp.bfloat16)
+
+    @pl.when(phase == 0)
+    def _():
+        finish(small[:, :rank], small[:, 2 * rank : 3 * rank])
+
+    @pl.when(phase != 0)
+    def _():
+        finish(small[:, rank : 2 * rank], small[:, 3 * rank : 4 * rank])
+
+
+VMEM = pl.BlockSpec(memory_space=pltpu.VMEM)
+HBM = pl.BlockSpec(memory_space=pl.ANY)
+PARAMS = pltpu.CompilerParams(vmem_limit_bytes=VMEM_LIMIT)
+
+
+def on_device_two_phases(hidden_in, cotangent, cluster_ids, w_down, w_up, gain):
+    experts = lax.axis_size("expert")
+    replicas = lax.axis_size("dp")
+    phases = lax.axis_size("segment")
+    s_local, length, part = hidden_in.shape
+    width = part * phases
+    capacity = 2 * s_local // experts
+    slots = experts * capacity
+    groups = experts * phases
+    rows = slots * length // groups
+    tokens = experts * rows
+    locals_ = s_local * length
+    own = (w_down[0, 0], w_up[0, 0], gain[0])
+    rank = own[0].shape[1]
+    bf16 = jnp.bfloat16
+    swap = [(i, phases - 1 - i) for i in range(phases)]
+    other = tuple(lax.ppermute(array, "segment", swap) for array in own)
+
+    ids = jnp.repeat(cluster_ids, length)
+    ids_row, ids_col = ids[None, :], ids[:, None]
+    sizes = (length, capacity, slots)
+    send = pl.pallas_call(
+        functools.partial(pack_kernel, *sizes),
+        out_shape=jax.ShapeDtypeStruct((groups, 2, rows, part), bf16),
+        in_specs=[VMEM] * 4,
+        out_specs=VMEM,
+        compiler_params=PARAMS,
+        name="pack",
+    )(ids_row, ids_col, hidden_in.reshape(locals_, part), cotangent.reshape(locals_, part))
+    recv = lax.all_to_all(send, ("expert", "segment"), split_axis=0, concat_axis=0, tiled=True)
+    recv = recv.reshape(experts, phases, 2, rows, part)
+
+    lanes = replicas * phases
+    piece = width // lanes
+    per_half = part // piece
+    slabs = recv.reshape(experts, phases, 2, rows, per_half, piece)
+    slabs = slabs.transpose(1, 4, 2, 0, 3, 5).reshape(lanes, 2, tokens, piece)
+    mine = lax.all_to_all(slabs, ("dp", "segment"), split_axis=0, concat_axis=0, tiled=True)
+    theirs = lax.ppermute(mine, "segment", swap)
+
+    out, small = pl.pallas_call(
+        chain_kernel,
+        out_shape=(
+            jax.ShapeDtypeStruct((experts, phases, rows, part), bf16),
+            jax.ShapeDtypeStruct((tokens, 4 * rank + 128), bf16),
+        ),
+        in_specs=[VMEM] + [HBM] * 6,
+        out_specs=(VMEM, VMEM),
+        scratch_shapes=[
+            pltpu.VMEM((2, width, rank), bf16),
+            pltpu.VMEM((2, rank, width), bf16),
+            pltpu.VMEM((2, 1, width), bf16),
+            pltpu.VMEM((tokens, width), bf16),
+            pltpu.VMEM((tokens, width), bf16),
+            pltpu.VMEM((tokens, width), jnp.float32),
+            pltpu.SemaphoreType.DMA((6,)),
+        ],
+        compiler_params=PARAMS,
+        name="chain",
+    )(recv, *own, *other)
+
+    back = lax.all_to_all(
+        out.reshape(groups, rows, part), ("expert", "segment"), split_axis=0, concat_axis=0, tiled=True
+    )
+    out_hidden = pl.pallas_call(
+        functools.partial(unpack_kernel, *sizes),
+        out_shape=jax.ShapeDtypeStruct((locals_, part), bf16),
+        in_specs=[VMEM] * 3,
+        out_specs=VMEM,
+        compiler_params=PARAMS,
+        name="unpack",
+    )(ids_row, ids_col, back).reshape(s_local, length, part)
+
+    gathered = lax.all_gather(small, ("dp", "segment"), axis=0, tiled=True)
+    slab = width // replicas
+    grad_dn, grad_upper = pl.pallas_call(
+        gradient_kernel,
+        out_shape=(
+            jax.ShapeDtypeStruct((slab, rank), bf16),
+            jax.ShapeDtypeStruct((rank, slab), bf16),
+        ),
+        in_specs=[VMEM] * 3 + [HBM] * 6,
+        out_specs=(VMEM, VMEM),
+        scratch_shapes=[
+            pltpu.VMEM((slab, rank), bf16),
+            pltpu.VMEM((rank, slab), bf16),
+            pltpu.VMEM((2, 1, slab), bf16),
+            pltpu.VMEM((lanes * tokens, slab), bf16),
+            pltpu.VMEM((lanes * tokens, slab), bf16),
+            pltpu.SemaphoreType.DMA((4,)),
+        ],
+        compiler_params=PARAMS,
+        name="gradients",
+    )(mine, theirs, gathered, *own, *other)
+    return (out_hidden, grad_dn[None, None], grad_upper[None, None])
+
+
 def solution(mesh):
+    two = mesh.shape["segment"] == 2
+    on_device = on_device_two_phases if two else on_device_pipelined
     return jax.shard_map(
         on_device,
         mesh=mesh,

time: 276 us -> 116 us (0.42)
  waiting for transfers between devices: 88.3 us -> 21.5 us
  other arithmetic: 45.8 us -> 0 us
  matrix products: 37.2 us -> 0 us
  local copies, waits for them, and re-layouts: 42.1 us -> 13.5 us
  Pallas kernels: 0 us -> 26.3 us
  starting transfers between devices: 26.6 us -> 6.04 us
  blocking collectives: 18.1 us -> 34.4 us
    reduce_scatter x2 -> x0, waiting for transfers between devices: 72.1 us -> none  [the longest x1 45.5 us: on_device(): lax.psum_scatter(grad_upper.astype(jnp.bfloat16), 'dp', scatter_dimension...]
    dot_general x25 -> x0, matrix products: 37.2 us -> none  [the longest x5 14.6 us: phase_backward(): d_act = jnp.dot(grad_in, w_upper.T, preferred_element_type=jnp.float32)]
    dynamic_update_slice x20 -> x0, other arithmetic: 31.6 us -> none  [put_slot(): lax.dynamic_update_index_in_dim(buffer, jnp.where(valid, value, old_value...]
    pallas_call x0 -> x4, Pallas kernels: none -> 26.3 us  [the longest x1 11.5 us: on_device_two_phases(): pl.pallas_call(gradient_kernel, out_shape=(jax.ShapeDtypeStruct((slab, ra...]
    all_to_all x1 -> x2, blocking collectives: 13.4 us -> 34.4 us  [the longest x1 20.5 us: on_device_two_phases(): lax.all_to_all(send, ('expert', 'segment'), split_axis=0, concat_axis=0,...]
    dynamic_slice x21 -> x0, local copies, waits for them, and re-layouts: 16.6 us -> none  [the longest x20 15.4 us: put_slot(): old_value = lax.dynamic_index_in_dim(buffer, slot, 0, keepdims=False)]
    ppermute x10 -> x4, starting transfers between devices: 17.1 us -> 1.12 us  [the longest x3 1.12 us: on_device_two_phases(): other = tuple((lax.ppermute(array, 'segment', swap) for array in own))]
    all_to_all x2 -> x1, waiting for transfers between devices: 9.41 us -> 20.6 us  [on_device_two_phases(): lax.all_to_all(slabs, ('dp', 'segment'), split_axis=0, concat_axis=0, til...]
  transfers between devices with their start and end apart: 15 -> 6, of which waited for: 8 -> 2; matrix products, arithmetic and copies ran while one was open for 41% -> 10% of each run, Pallas kernels for 0% -> 13%
where the time goes in v1:
time: 116 us
  blocking collectives  34.4 us (30%)
  Pallas kernels  26.3 us (23%)
  waiting for transfers between devices  21.5 us (19%)
  between operations  14.1 us (12%)
  local copies, waits for them, and re-layouts  13.5 us (12%)
  starting transfers between devices  6.04 us (5%)
    all_to_all x1, waiting for transfers between devices, on_device_two_phases(): lax.all_to_all(slabs, ('dp', 'segment'), split_axis=0, concat_axis=0, til...  20.6 us
    all_to_all x1, blocking collectives, on_device_two_phases(): lax.all_to_all(send, ('expert', 'segment'), split_axis=0, concat_axis=0,...  20.5 us
    all_to_all x1, blocking collectives, on_device_two_phases(): lax.all_to_all(out.reshape(groups, rows, part), ('expert', 'segment'), sp...  13.9 us
    pallas_call x1, Pallas kernels, on_device_two_phases(): pl.pallas_call(gradient_kernel, out_shape=(jax.ShapeDtypeStruct((slab, ra...  11.5 us
    pallas_call x1, Pallas kernels, on_device_two_phases(): pl.pallas_call(chain_kernel, out_shape=(jax.ShapeDtypeStruct((experts, ph...  10.2 us
    all_to_all x1, starting transfers between devices, on_device_two_phases(): lax.all_to_all(slabs, ('dp', 'segment'), split_axis=0, concat_axis=0, til...  4.88 us
    another operation x2, local copies, waits for them, and re-layouts, on_device_two_phases(): slabs = recv.reshape(experts, phases, 2, rows, per_half, piece)  4.04 us
    pallas_call x1, Pallas kernels, on_device_two_phases(): pl.pallas_call(functools.partial(pack_kernel, *sizes), out_shape=jax.Shap...  2.51 us
  transfers between devices with their start and end apart: 6, of which 2 were waited for; matrix products, arithmetic and copies ran while one was open for 10% of the time, Pallas kernels for 13%

profile of v1, /device:TPU:0, one launch (start us, length us, event | category | flops | bytes accessed | tf_op | source)
XLA Modules:
  0.0 115.9 jit_solution(11661582682390881820)
XLA Ops:
  7.2 0.5 collective-permute-start
  7.7 0.1 collective-permute-start.1
  7.8 0.7 broadcast_in_dim.9
  8.5 0.6 broadcast_in_dim_reshape.6.ids_row
  9.1 0.7 broadcast_in_dim_reshape.8.ids_col
  9.8 1.7 %reshape.24.hidden = bf16[64,2048]{1,0:T(8,128)(2,1)} reshape(bf16[16,4,2048]{2,1,0:T(4,128)(2,1)} %param.6) | data formatting | bytes 524288 | tf_op jit(solution)/shard_map/reshape | solution.py:528
  11.5 1.7 %reshape.25.cot = bf16[64,2048]{1,0:T(8,128)(2,1)} reshape(bf16[16,4,2048]{2,1,0:T(4,128)(2,1)} %param.7) | data formatting | bytes 524288 | tf_op jit(solution)/shard_map/reshape | solution.py:528
  13.2 2.5 %pack.1 = bf16[8,2,16,2048]{3,2,1,0:T(8,128)(2,1)} custom-call(s32[1,64]{1,0:T(1,128)} %broadcast_in_dim_reshape.6.ids_row, s32[64,1]{1,0:T(8,128)} %broadcast_in_dim_reshape.8.ids_col, bf16[64,2048]{1,0:T(8,128)(2,1)} %reshape.24.hidden, bf16[64,2048]{1,0:T(8,128)(2,1)} %reshape.25.cot), custom_call_target="tpu_custom_call" | custom-call | tf_op jit(solution)/shard_map/pack/pallas_call | solution.py:521
  15.7 20.5 %all_to_all.15 = bf16[8,2,16,2048]{3,2,1,0:T(8,128)(2,1)S(1)} all-to-all(bf16[8,2,16,2048]{3,2,1,0:T(8,128)(2,1)} %pack.1), channel_id=1, replica_groups=mesh['expert'=4,'dp'=4,'segment'=2] {'expert','segment'}, dimensions={0} | all-to-all | bytes 2097152 | tf_op jit(solution)/shard_map/all_to_all | solution.py:529
  36.2 1.6 %reshape_reshape.3 = bf16[4,2,2,16,4,512]{5,4,3,2,1,0:T(4,128)(2,1)} reshape(bf16[8,2,16,2048]{3,2,1,0:T(8,128)(2,1)S(1)} %all_to_all.15) | data formatting | bytes 2097152 | tf_op jit(solution)/shard_map/reshape;reshape | solution.py:535
  37.8 2.5 %copy.14 = bf16[4,2,2,16,4,512]{5,3,0,2,4,1:T(8,128)(2,1)} copy(bf16[4,2,2,16,4,512]{5,4,3,2,1,0:T(4,128)(2,1)} %reshape_reshape.3) | data formatting | bytes 2097152 | tf_op jit(solution)/shard_map/reshape;reshape | solution.py:535
  40.3 0.0 copy-done
  40.3 4.9 %all-to-all-start.2 = ((bf16[8,2,64,512]{3,2,1,0:T(8,128)(2,1)}), bf16[8,2,64,512]{3,2,1,0:T(8,128)(2,1)S(1)}, u32[]{:S(2)}, u32[]{:S(2)}) async-start(bf16[8,2,64,512]{3,2,1,0:T(8,128)(2,1)} %bitcast.19), calls=%async_computation.2 | async-start | bytes 2097152 | tf_op jit(solution)/shard_map/all_to_all | solution.py:537
  45.2 0.0 all-gather.2.cloned.1.call-start
  45.2 0.0 copy-done.4
  45.2 0.5 collective-permute-start.2
  45.7 0.8 collective-permute-done.2.other_gain
  46.6 0.0 collective-permute-done.other_dn
  46.6 0.0 collective-permute-done.1.other_up
  46.6 0.6 copy-done.5
  47.2 0.7 copy-done.1
  47.9 10.2 %chain.1 = (bf16[4,2,16,2048]{3,2,1,0:T(8,128)(2,1)}, bf16[64,1152]{1,0:T(8,128)(2,1)}) custom-call(bf16[4,2,2,16,2048]{4,3,2,1,0:T(8,128)(2,1)} %bitcast.12, bf16[4096,256]{1,0:T(8,128)(2,1)} %bitcast.14, bf16[256,4096]{1,0:T(8,128)(2,1)} %bitcast.17, bf16[1,4096]{1,0:T(2,128)(2,1)} %bitcast.21, bf16[4096,256]{1,0:T(8,128)(2,1)} %copy-done.1, ...), custom_call_target="tpu_custom_call" | custom-call | tf_op jit(solution)/shard_map/chain/pallas_call | solution.py:540
  58.2 0.0 all-gather.2.cloned.1.call-update
  58.2 20.6 %all-to-all-done.2.mine = bf16[8,2,64,512]{3,2,1,0:T(8,128)(2,1)S(1)} async-done(((bf16[8,2,64,512]{3,2,1,0:T(8,128)(2,1)}), bf16[8,2,64,512]{3,2,1,0:T(8,128)(2,1)S(1)}, u32[]{:S(2)}, u32[]{:S(2)}) %all-to-all-start.2) | async-done | bytes 1048608 | tf_op jit(solution)/shard_map/all_to_all | solution.py:537
  78.8 0.0 collective-permute-start.3
  78.8 13.9 %all_to_all.16.back = bf16[8,16,2048]{2,1,0:T(8,128)(2,1)} all-to-all(bf16[8,16,2048]{2,1,0:T(8,128)(2,1)} %bitcast.20), channel_id=1, replica_groups=mesh['expert'=4,'dp'=4,'segment'=2] {'expert','segment'}, dimensions={0} | all-to-all | bytes 1048576 | tf_op jit(solution)/shard_map/all_to_all | solution.py:561
  92.7 2.1 %unpack.1 = bf16[64,2048]{1,0:T(8,128)(2,1)} custom-call(s32[1,64]{1,0:T(1,128)} %broadcast_in_dim_reshape.6.ids_row, s32[64,1]{1,0:T(8,128)} %broadcast_in_dim_reshape.8.ids_col, bf16[8,16,2048]{2,1,0:T(8,128)(2,1)} %all_to_all.16.back), custom_call_target="tpu_custom_call" | custom-call | tf_op jit(solution)/shard_map/unpack/pallas_call | solution.py:564
  94.8 1.8 %reshape.28 = bf16[16,4,2048]{2,1,0:T(4,128)(2,1)} reshape(bf16[64,2048]{1,0:T(8,128)(2,1)} %unpack.1) | data formatting | bytes 524288 | tf_op jit(solution)/shard_map/reshape | solution.py:571
  96.6 0.0 collective-permute-done.3.theirs
  96.6 0.0 copy-done.2
  96.6 1.0 copy-done.3
  97.5 11.5 %gradients.1 = (bf16[1024,256]{1,0:T(8,128)(2,1)}, bf16[256,1024]{1,0:T(8,128)(2,1)}) custom-call(bf16[8,2,64,512]{3,2,1,0:T(8,128)(2,1)} %copy-done.2, bf16[8,2,64,512]{3,2,1,0:T(8,128)(2,1)} %copy-done.3, bf16[512,1152]{1,0:T(8,128)(2,1)} %all-gather.2.cloned.1.call-done.small, bf16[4096,256]{1,0:T(8,128)(2,1)} %bitcast.15, bf16[256,4096]{1,0:T(8,128)(2,1)} %bitcast.18, ...), custom_call_target="tpu_custom_call" | custom-call | tf_op jit(solution)/shard_map/gradients/pallas_call | solution.py:575
  (7 shorter events, 0.0 us)
Async XLA Ops:
  7.2 39.4 %collective-permute-start = (bf16[4096,256]{1,0:T(8,128)(2,1)}, bf16[4096,256]{1,0:T(8,128)(2,1)S(1)}, u32[]{:S(2)}, u32[]{:S(2)}) collective-permute-start(bf16[4096,256]{1,0:T(8,128)(2,1)} %bitcast.13), channel_id=1, source_target_pairs={{0,1},{1,0},{2,3},{3,2},{4,5},{5,4},{6,7},{7,6},{8,9},{9,8},{10,11... | collective-permute-start | bytes 6291464 | tf_op jit(solution)/shard_map/ppermute | solution.py:516
  7.7 38.9 %collective-permute-start.1 = (bf16[256,4096]{1,0:T(8,128)(2,1)}, bf16[256,4096]{1,0:T(8,128)(2,1)}, u32[]{:S(2)}, u32[]{:S(2)}) collective-permute-start(bf16[256,4096]{1,0:T(8,128)(2,1)} %bitcast.16), channel_id=1, source_target_pairs={{0,1},{1,0},{2,3},{3,2},{4,5},{5,4},{6,7},{7,6},{8,9},{9,8},{10,11... | collective-permute-start | bytes 6291464 | tf_op jit(solution)/shard_map/ppermute | solution.py:516
  36.2 4.0 %copy-start = (bf16[8,2,16,2048]{3,2,1,0:T(8,128)(2,1)}, bf16[8,2,16,2048]{3,2,1,0:T(8,128)(2,1)S(1)}, u32[]{:S(2)}) copy-start(bf16[8,2,16,2048]{3,2,1,0:T(8,128)(2,1)S(1)} %all_to_all.15) | copy-start | bytes 3145732
  37.8 7.4 %copy-start.4 = (bf16[1,1,4096]{2,1,0:T(2,128)(2,1)S(1)}, bf16[1,1,4096]{2,1,0:T(2,128)(2,1)}, u32[]{:S(2)}) copy-start(bf16[1,1,4096]{2,1,0:T(2,128)(2,1)} %param.11) | copy-start | bytes 24580
  40.3 38.5 %all-to-all-start.2 = ((bf16[8,2,64,512]{3,2,1,0:T(8,128)(2,1)}), bf16[8,2,64,512]{3,2,1,0:T(8,128)(2,1)S(1)}, u32[]{:S(2)}, u32[]{:S(2)}) async-start(bf16[8,2,64,512]{3,2,1,0:T(8,128)(2,1)} %bitcast.19), calls=%async_computation.2 | async-start | bytes 2097152 | tf_op jit(solution)/shard_map/all_to_all | solution.py:537
  45.2 51.4 %all-gather.2.cloned.1.call-start = ((), (), s32[]{:S(2)}) async-start(), calls=%async_computation.3 | async-start | bytes 1327104 | tf_op jit(solution)/shard_map/all_gather | solution.py:573
  45.2 1.4 %collective-permute-start.2 = (bf16[1,4096]{1,0:T(2,128)(2,1)S(1)}, bf16[1,4096]{1,0:T(2,128)(2,1)S(1)}, u32[]{:S(2)}, u32[]{:S(2)}) collective-permute-start(bf16[1,4096]{1,0:T(2,128)(2,1)S(1)} %bitcast.23), channel_id=1, source_target_pairs={{0,1},{1,0},{2,3},{3,2},{4,5},{5,4},{6,7},{7,6},{8,9},{9,8},{10,11... | collective-permute-start | bytes 24584 | tf_op jit(solution)/shard_map/ppermute | solution.py:516
  46.6 0.6 copy-start.5
  46.6 1.3 %copy-start.1 = (bf16[4096,256]{1,0:T(8,128)(2,1)}, bf16[4096,256]{1,0:T(8,128)(2,1)S(1)}, u32[]{:S(2)}) copy-start(bf16[4096,256]{1,0:T(8,128)(2,1)S(1)} %collective-permute-done.other_dn) | copy-start | bytes 6291460
  78.8 17.8 %copy-start.2 = (bf16[8,2,64,512]{3,2,1,0:T(8,128)(2,1)}, bf16[8,2,64,512]{3,2,1,0:T(8,128)(2,1)S(1)}, u32[]{:S(2)}) copy-start(bf16[8,2,64,512]{3,2,1,0:T(8,128)(2,1)S(1)} %all-to-all-done.2.mine) | copy-start | bytes 3145732
  78.8 17.8 %collective-permute-start.3 = (bf16[8,2,64,512]{3,2,1,0:T(8,128)(2,1)S(1)}, bf16[8,2,64,512]{3,2,1,0:T(8,128)(2,1)S(1)}, u32[]{:S(2)}, u32[]{:S(2)}) collective-permute-start(bf16[8,2,64,512]{3,2,1,0:T(8,128)(2,1)S(1)} %all-to-all-done.2.mine), channel_id=1, source_target_pairs={{0,1},{1,0},{2,3},{3,2},{4,5},{5,4},{6,7},{7,6},{8,9},{9,8},{10,11... | collective-permute-start | bytes 3145736 | tf_op jit(solution)/shard_map/ppermute | solution.py:538
  96.6 1.0 copy-start.3
Sparse Core Ops, SparseCore 0:
  58.3 24.3 all-gather.1

commit v2 on v0

--- a/solution.py
+++ b/solution.py
@@ -1,6 +1,10 @@
+import functools
+
 import jax
 import jax.numpy as jnp
 from jax import lax
+from jax.experimental import pallas as pl
+from jax.experimental.pallas import tpu as pltpu
 from jax.sharding import PartitionSpec as P
 
 MICRO = 4
@@ -71,7 +75,7 @@
     return lax.dynamic_update_index_in_dim(buffer, jnp.where(valid, value, old_value), slot, 0)
 
 
-def on_device(hidden_in, cotangent, cluster_ids, w_down, w_up, gain):
+def on_device_pipelined(hidden_in, cotangent, cluster_ids, w_down, w_up, gain):
     experts = lax.axis_size("expert")
     phases = lax.axis_size("segment")
     phase = lax.axis_index("segment")
@@ -187,7 +191,563 @@
     )
 
 
+CHUNK = 512
+VMEM_LIMIT = 56 * 1024 * 1024
+TRANS_RHS = (((1,), (1,)), ((), ()))
+TRANS_LHS = (((0,), (0,)), ((), ()))
+
+
+def matmul(left, right, dims=(((1,), (0,)), ((), ()))):
+    return lax.dot_general(left, right, dims, preferred_element_type=jnp.float32)
+
+
+def spread_ids(ids, shape, length):
+    lane = lax.broadcasted_iota(jnp.int32, shape, 1)
+    spread = jnp.zeros(shape, jnp.int32)
+    for n in range(ids.shape[0]):
+        spread = jnp.where(lane // length == n, ids[n], spread)
+    return spread
+
+
+def placement(ids_row, length, capacity, slots):
+    tokens = ids_row.shape[1]
+    expert, core = lax.axis_index("expert"), lax.axis_index("segment")
+    per_core = capacity // 2
+    kinds = lax.broadcasted_iota(jnp.int32, (8, tokens), 0)
+    member = (kinds == ids_row).astype(jnp.float32)
+    at_col = lax.broadcasted_iota(jnp.int32, (tokens, tokens), 0)
+    at_row = lax.broadcasted_iota(jnp.int32, (tokens, tokens), 1)
+    before = (lax.rem(at_col, length) == 0) & (at_col // length < at_row // length)
+    counts = matmul(member.astype(jnp.bfloat16), before.astype(jnp.float32).astype(jnp.bfloat16))
+    rank = jnp.sum(member * counts, axis=0, keepdims=True).astype(jnp.int32)
+    token = lax.rem(at_row[:1], length)
+    group = (ids_row ^ expert) * 2 + ((rank // per_core) ^ core)
+    target = (group * per_core + lax.rem(rank, per_core)) * length + token
+    packed = lax.broadcasted_iota(jnp.int32, (slots * length, tokens), 0)
+    return (packed == target).astype(jnp.float32).astype(jnp.bfloat16)
+
+
+def pack_kernel(length, capacity, slots, ids, hidden, cot, *outs):
+    groups = len(outs) - 4
+    sends, slabs = outs[:groups], outs[groups:]
+    s_local, _, part = hidden.shape
+    tokens = s_local * length
+    piece = part // 4
+    replica = lax.axis_index("dp")
+    ids_row = spread_ids(ids, (8, tokens), length)[:1]
+    place = placement(ids_row, length, capacity, slots)
+    rows = slots * length // groups
+    wide_ids = spread_ids(ids, (16, piece), length).astype(jnp.float32).astype(jnp.bfloat16)
+    for which, source in enumerate((hidden, cot)):
+        for quarter_pair in range(2):
+            for low in range(2):
+                turn = (quarter_pair ^ (replica & 1)) * 2 + (low ^ (replica >> 1))
+                cols = pl.ds(pl.multiple_of(turn * piece, piece), piece)
+                slabs[2 * quarter_pair + low][which * tokens : (which + 1) * tokens] = source[
+                    :, :, cols
+                ].reshape(tokens, piece)
+        moved = matmul(place, source[...].reshape(tokens, part)).astype(jnp.bfloat16)
+        for group in range(groups):
+            sends[group][which] = moved[group * rows : (group + 1) * rows]
+    for slab in slabs:
+        slab[2 * tokens :] = wide_ids
+
+
+def repack_kernel(length, capacity, slots, *refs):
+    slabs, outs = refs[:4], refs[4:]
+    tokens = (slabs[0].shape[0] - 16) // 2
+    rows = slots * length // len(outs)
+    core, replica = lax.axis_index("segment"), lax.axis_index("dp")
+    for turn, slab in enumerate(slabs):
+        near = turn // 2 + 2 * ((turn % 2) ^ (replica >> 1) ^ core)
+        ids_row = slab[2 * tokens :, :tokens].astype(jnp.float32)[:1].astype(jnp.int32)
+        place = placement(ids_row, length, capacity, slots)
+        for which in range(2):
+            moved = matmul(place, slab[which * tokens : (which + 1) * tokens])
+            moved = moved.astype(jnp.bfloat16)
+            for step, out in enumerate(outs):
+                out[which, near] = moved[step * rows : (step + 1) * rows]
+
+
+def unpack_kernel(length, capacity, slots, ids, *refs):
+    backs, out, stacked = refs[:-2], refs[-2], refs[-1]
+    rows, width = backs[0].shape
+    s_local = out.shape[0]
+    for group, back in enumerate(backs):
+        stacked[group * rows : (group + 1) * rows] = back[...]
+    ids_row = spread_ids(ids, (8, s_local * length), length)[:1]
+    place = placement(ids_row, length, capacity, slots)
+    moved = matmul(place, stacked[...], TRANS_LHS).astype(jnp.bfloat16)
+    out[...] = moved.reshape(s_local, length, width)
+
+
+def split_three(value):
+    top = value.astype(jnp.bfloat16).astype(jnp.float32)
+    mid = (value - top).astype(jnp.bfloat16).astype(jnp.float32)
+    low = (value - top - mid).astype(jnp.bfloat16).astype(jnp.float32)
+    return [top, mid, low]
+
+
+def side_by_side(columns, tokens):
+    lane = lax.broadcasted_iota(jnp.int32, (tokens, 128), 1)
+    block = jnp.zeros((tokens, 128), jnp.float32)
+    at = 0
+    for column in columns:
+        for piece in split_three(column):
+            block = jnp.where(lane == at, piece, block)
+            at += 1
+    return block.astype(jnp.bfloat16)
+
+
+def column(block, index):
+    at = 3 * index
+    return block[:, at : at + 1] + block[:, at + 1 : at + 2] + block[:, at + 2 : at + 3]
+
+
+def lanes(value):
+    total = value[:, :128]
+    for start in range(128, value.shape[1], 128):
+        total = total + value[:, start : start + 128]
+    return total
+
+
+def row_sum(parts):
+    return jnp.sum(parts, axis=1, keepdims=True)
+
+
+def weight_copies(core, half, sources, buffers, sems):
+    copies = []
+    for at, (source, buffer, axis) in enumerate(zip(sources, buffers, (0, 1, 1))):
+        for near in range(2):
+            start = (near ^ core) * half
+            part = pl.ds(start, half)
+            here = pl.ds(near * half, half)
+            from_, to = (part, here) if axis == 0 else ((slice(None), part), (slice(None), here))
+            copies.append(pltpu.make_async_copy(source.at[from_], buffer.at[to], sems.at[at, near]))
+    return copies
+
+
+def forward_kernel(groups, *refs):
+    recvs, refs = refs[:groups], refs[groups:]
+    own, other, refs = refs[:3], refs[3:6], refs[6:]
+    outs, refs = refs[:groups], refs[groups:]
+    small, middle, slope_out, moments, dn_buf, up_buf, gain_buf, entering, sems = refs
+    core = lax.axis_index("segment")
+    _, rows, part = recvs[0].shape
+    experts = groups // 2
+    tokens = experts * rows
+    width = 2 * part
+    rank = dn_buf.shape[2]
+
+    def copies(at, this):
+        sources = own if at == this else other
+        buffers = (dn_buf.at[at], up_buf.at[at], gain_buf.at[at])
+        return weight_copies(this, part, sources, buffers, sems.at[at])
+
+    for this in range(2):
+
+        @pl.when(core == this)
+        def _():
+            for at in range(2):
+                for copy in copies(at, this):
+                    copy.start()
+
+    waits = [copies(at, 0) for at in range(2)]
+
+    def wait(at, which):
+        for copy in waits[at][2 * which : 2 * which + 2]:
+            copy.wait()
+
+    cols = range(0, width, CHUNK)
+
+    def block(which, col):
+        near, start = col // part, col % part
+        return jnp.concatenate(
+            [recvs[2 * e + near][which, :, start : start + CHUNK] for e in range(experts)], axis=0
+        )
+
+    def inverse_of(ref, mean):
+        total = jnp.zeros((tokens, 128), jnp.float32)
+        for col in cols:
+            center = ref[:, col : col + CHUNK].astype(jnp.float32) - mean
+            total = total + lanes(center * center)
+        return lax.rsqrt(row_sum(total) / width + EPS)
+
+    def down(ref, mean, inverse, at):
+        pre = jnp.zeros((tokens, rank), jnp.float32)
+        for col in cols:
+            here = slice(col, col + CHUNK)
+            normed = (ref[:, here].astype(jnp.float32) - mean) * inverse
+            lowered = (normed * gain_buf[at, :, here].astype(jnp.float32)).astype(jnp.bfloat16)
+            pre = pre + matmul(lowered, dn_buf[at, here, :])
+        return pre
+
+    total = jnp.zeros((tokens, 128), jnp.float32)
+    for col in cols:
+        value = block(0, col)
+        entering[:, col : col + CHUNK] = value
+        total = total + lanes(value.astype(jnp.float32))
+    mean_0 = row_sum(total) / width
+    inverse_0 = inverse_of(entering, mean_0)
+    wait(0, 0)
+    wait(0, 2)
+    pre_0 = down(entering, mean_0, inverse_0, 0)
+    act_0 = gelu_value(pre_0).astype(jnp.bfloat16)
+    slope_out[...] = gelu_slope(pre_0)
+
+    wait(0, 1)
+    total = jnp.zeros((tokens, 128), jnp.float32)
+    for col in cols:
+        here = slice(col, col + CHUNK)
+        value = entering[:, here].astype(jnp.float32) + matmul(act_0, up_buf[0, :, here])
+        value = value.astype(jnp.bfloat16)
+        middle[:, here] = value
+        total = total + lanes(value.astype(jnp.float32))
+    mean_1 = row_sum(total) / width
+    inverse_1 = inverse_of(middle, mean_1)
+    wait(1, 0)
+    wait(1, 2)
+    pre_1 = down(middle, mean_1, inverse_1, 1)
+    act_1 = gelu_value(pre_1).astype(jnp.bfloat16)
+
+    wait(1, 1)
+    d_act = jnp.zeros((tokens, rank), jnp.float32)
+    for col in cols:
+        here = slice(col, col + CHUNK)
+        d_act = d_act + matmul(block(1, col), up_buf[1, :, here], TRANS_RHS)
+        leaving = middle[:, here].astype(jnp.float32) + matmul(act_1, up_buf[1, :, here])
+        leaving = leaving.astype(jnp.bfloat16)
+        near, start = col // part, col % part
+        for e in range(experts):
+            outs[2 * e + near][:, start : start + CHUNK] = leaving[e * rows : (e + 1) * rows]
+    d_pre_1 = (d_act * gelu_slope(pre_1)).astype(jnp.bfloat16)
+    for at, value in enumerate((act_0, act_1, d_pre_1)):
+        small[:, at * rank : (at + 1) * rank] = value
+    small[:, 3 * rank :] = side_by_side((mean_0, inverse_0, mean_1, inverse_1), tokens)
+    moments[...] = jnp.concatenate(
+        [jnp.broadcast_to(mean_1, (tokens, 128)), jnp.broadcast_to(inverse_1, (tokens, 128))], axis=1
+    )
+
+
+def backward_kernel(groups, *refs):
+    recvs, refs = refs[:groups], refs[groups:]
+    own, other, refs = refs[:3], refs[3:6], refs[6:]
+    small_in, middle, slope, moments, small, dn_buf, up_buf, gain_buf, d_norms, sems = refs
+    core = lax.axis_index("segment")
+    _, rows, part = recvs[0].shape
+    experts = groups // 2
+    tokens = experts * rows
+    width = 2 * part
+    rank = dn_buf.shape[1]
+    buffers = (dn_buf, up_buf, gain_buf)
+
+    def copies(this):
+        first, second = (own, other) if this == 0 else (other, own)
+        return weight_copies(this, part, (second[0], first[1], second[2]), buffers, sems)
+
+    for this in range(2):
+
+        @pl.when(core == this)
+        def _():
+            for copy in copies(this):
+                copy.start()
+
+    waits = copies(0)
+    mean_1, inverse_1 = moments[:, :1], moments[:, 128:129]
+    d_pre_1 = small_in[:, 2 * rank : 3 * rank]
+    for copy in waits[:2] + waits[4:]:
+        copy.wait()
+    total = jnp.zeros((tokens, 128), jnp.float32)
+    cross = jnp.zeros((tokens, 128), jnp.float32)
+    cols = range(0, width, CHUNK)
+    for col in cols:
+        here = slice(col, col + CHUNK)
+        d_norm = matmul(d_pre_1, dn_buf[here, :], TRANS_RHS) * gain_buf[:, here].astype(jnp.float32)
+        normed = (middle[:, here].astype(jnp.float32) - mean_1) * inverse_1
+        d_norms[:, here] = d_norm
+        total = total + lanes(d_norm)
+        cross = cross + lanes(d_norm * normed)
+    shift = row_sum(total) / width
+    along = row_sum(cross) / width
+    for copy in waits[2:4]:
+        copy.wait()
+    d_act = jnp.zeros((tokens, rank), jnp.float32)
+    for col in cols:
+        here = slice(col, col + CHUNK)
+        near, start = col // part, col % part
+        grad_in = jnp.concatenate(
+            [recvs[2 * e + near][1, :, start : start + CHUNK] for e in range(experts)], axis=0
+        )
+        normed = (middle[:, here].astype(jnp.float32) - mean_1) * inverse_1
+        grad = grad_in.astype(jnp.float32) + inverse_1 * (d_norms[:, here] - shift - normed * along)
+        d_act = d_act + matmul(grad.astype(jnp.bfloat16), up_buf[:, here], TRANS_RHS)
+    small[:, :rank] = (d_act * slope[...]).astype(jnp.bfloat16)
+    small[:, rank:] = side_by_side((shift, along), tokens)
+
+
+def gradient_kernel(experts, replicas, *refs):
+    mine, refs = refs[:experts], refs[experts:]
+    theirs, refs = refs[:experts], refs[experts:]
+    firsts, refs = refs[: 2 * replicas], refs[2 * replicas :]
+    seconds, refs = refs[: 2 * replicas], refs[2 * replicas :]
+    own, other, refs = refs[:3], refs[3:6], refs[6:]
+    (grad_dn, grad_upper, dn_buf, up_buf, gain_buf, first, second, hiddens, grads, lows, ups, downs,
+     sems) = refs
+    core = lax.axis_index("segment")
+    place = lax.axis_index("dp")
+    half = mine[0].shape[3]
+    rows = mine[0].shape[2] // 2
+    slab = 2 * half
+    rank = dn_buf.shape[1]
+    tokens = hiddens.shape[0]
+
+    def copies(up, gain_first, dn, gain_second):
+        started = []
+        for near in range(2):
+            start = pl.multiple_of(place * slab + (near ^ core) * half, half)
+            part, here = pl.ds(start, half), pl.ds(near * half, half)
+            moves = (
+                (up.at[:, part], up_buf.at[:, here]),
+                (dn.at[part, :], dn_buf.at[here, :]),
+                (gain_first.at[:, part], gain_buf.at[0, :, here]),
+                (gain_second.at[:, part], gain_buf.at[1, :, here]),
+            )
+            for at, (source, target) in enumerate(moves):
+                started.append(pltpu.make_async_copy(source, target, sems.at[near, at]))
+        return started
+
+    @pl.when(core == 0)
+    def _():
+        for copy in copies(own[1], own[2], other[0], other[2]):
+            copy.start()
+
+    @pl.when(core != 0)
+    def _():
+        for copy in copies(other[1], other[2], own[0], own[2]):
+            copy.start()
+
+    block_rows = experts * rows
+    for source in range(2 * replicas):
+        near_core, turn = source // replicas, source % replicas
+        at = slice(source * block_rows, (source + 1) * block_rows)
+        first[at] = firsts[source][...]
+        second[at] = seconds[source][...]
+        for near, (data, core_at) in enumerate(((mine, near_core), (theirs, 1 - near_core))):
+            for step in range(experts):
+                to = slice(at.start + step * rows, at.start + (step + 1) * rows)
+                from_ = slice(core_at * rows, (core_at + 1) * rows)
+                hiddens[to, near * half : (near + 1) * half] = data[step][0, turn, from_, :]
+                grads[to, near * half : (near + 1) * half] = data[step][1, turn, from_, :]
+
+    for copy in copies(own[1], own[2], other[0], other[2]):
+        copy.wait()
+
+    columns = 256
+    strip = 128
+    for col in range(0, slab, columns):
+        here = slice(col, col + columns)
+        ups[...] = matmul(first[:, :rank], up_buf[:, here])
+
+        @pl.when(core == 0)
+        def _():
+            downs[...] = matmul(first[:, 2 * rank : 3 * rank], dn_buf[here, :], TRANS_RHS)
+
+        for start in range(0, tokens, strip):
+            at = slice(start, start + strip)
+            stats = first[at, 3 * rank :].astype(jnp.float32)
+            mean_1, inverse_1 = column(stats, 2), column(stats, 3)
+            wide = hiddens[at, here].astype(jnp.float32)
+            middle = (wide + ups[at]).astype(jnp.bfloat16).astype(jnp.float32)
+            normed = (middle - mean_1) * inverse_1
+
+            @pl.when(core == 0)
+            def _():
+                mean_0, inverse_0 = column(stats, 0), column(stats, 1)
+                normed_0 = (wide - mean_0) * inverse_0
+                lows[at, here] = (normed_0 * gain_buf[0, :, here].astype(jnp.float32)).astype(jnp.bfloat16)
+                more = second[at, rank:].astype(jnp.float32)
+                shift, along = column(more, 0), column(more, 1)
+                d_norm = downs[at] * gain_buf[1, :, here].astype(jnp.float32)
+                grads[at, here] = (
+                    grads[at, here].astype(jnp.float32)
+                    + inverse_1 * (d_norm - shift - normed * along)
+                ).astype(jnp.bfloat16)
+
+            @pl.when(core != 0)
+            def _():
+                lows[at, here] = (normed * gain_buf[1, :, here].astype(jnp.float32)).astype(jnp.bfloat16)
+
+    def finish(act, d_pre):
+        for near in range(2):
+            here = slice(near * half, (near + 1) * half)
+            there = pl.ds(pl.multiple_of((near ^ core) * half, half), half)
+            grad_dn[there, :] = matmul(lows[:, here], d_pre, TRANS_LHS).astype(jnp.bfloat16)
+            grad_upper[:, there] = matmul(act, grads[:, here], TRANS_LHS).astype(jnp.bfloat16)
+
+    @pl.when(core == 0)
+    def _():
+        finish(first[:, :rank], second[:, :rank])
+
+    @pl.when(core != 0)
+    def _():
+        finish(first[:, rank : 2 * rank], first[:, 2 * rank : 3 * rank])
+
+
+VMEM = pl.BlockSpec(memory_space=pltpu.VMEM)
+SMEM = pl.BlockSpec(memory_space=pltpu.SMEM)
+HBM = pl.BlockSpec(memory_space=pl.ANY)
+
+
+def call(kernel, name, in_specs, outs, scratch=()):
+    return pl.pallas_call(
+        kernel,
+        out_shape=tuple(jax.ShapeDtypeStruct(*out) for out in outs),
+        in_specs=in_specs,
+        out_specs=tuple(VMEM for _ in outs),
+        scratch_shapes=list(scratch),
+        compiler_params=pltpu.CompilerParams(vmem_limit_bytes=VMEM_LIMIT),
+        name=name,
+    )
+
+
+def across(block, axis, distance):
+    size = lax.axis_size(axis)
+    return lax.ppermute(block, axis, [(i, i ^ distance) for i in range(size)])
+
+
+def exchanged(blocks):
+    cores = lax.axis_size("segment")
+    size = lax.axis_size("expert") * cores
+    return [
+        block
+        if step == 0
+        else lax.ppermute(block, ("expert", "segment"), [(i, i ^ step) for i in range(size)])
+        for step, block in enumerate(blocks)
+    ]
+
+
+def slab_route(replicas, pair, low):
+    route = []
+    for replica in range(replicas):
+        for core in range(2):
+            chip = 2 * core + ((replica & 1) ^ pair)
+            route.append((2 * replica + core, 2 * chip + ((replica >> 1) ^ low)))
+    return route
+
+
+def on_device_two_phases(hidden_in, cotangent, cluster_ids, w_down, w_up, gain):
+    experts = lax.axis_size("expert")
+    replicas = lax.axis_size("dp")
+    s_local, length, part = hidden_in.shape
+    width = 2 * part
+    capacity = 2 * s_local // experts
+    slots = experts * capacity
+    groups = 2 * experts
+    rows = slots * length // groups
+    tokens = experts * rows
+    own = (w_down[0, 0], w_up[0, 0], gain[0])
+    rank = own[0].shape[1]
+    piece = part // 4
+    slab = width // replicas
+    bf16, f32 = jnp.bfloat16, jnp.float32
+    sizes = (length, capacity, slots)
+
+    other = tuple(across(array, "segment", 1) for array in own)
+    packed = call(
+        functools.partial(pack_kernel, *sizes),
+        "pack",
+        [SMEM, VMEM, VMEM],
+        [((2, rows, part), bf16)] * groups + [((2 * s_local * length + 16, piece), bf16)] * 4,
+    )(cluster_ids, hidden_in, cotangent)
+    recvs = exchanged(packed[:groups])
+    slabs = [
+        lax.ppermute(block, ("dp", "segment"), slab_route(replicas, turn // 2, turn % 2))
+        for turn, block in enumerate(packed[groups:])
+    ]
+    repacked = call(
+        functools.partial(repack_kernel, *sizes),
+        "repack",
+        [VMEM] * 4,
+        [((2, replicas, 2 * rows, piece), bf16)] * experts,
+    )(*slabs)
+    mine = [repacked[0]] + [across(repacked[step], "expert", step) for step in range(1, experts)]
+    theirs = [across(block, "segment", 1) for block in mine]
+
+    *outs, small, middle, slope, moments = call(
+        functools.partial(forward_kernel, groups),
+        "forward",
+        [VMEM] * groups + [HBM] * 6,
+        [((rows, part), bf16)] * groups
+        + [
+            ((tokens, 3 * rank + 128), bf16),
+            ((tokens, width), bf16),
+            ((tokens, rank), f32),
+            ((tokens, 256), f32),
+        ],
+        [
+            pltpu.VMEM((2, width, rank), bf16),
+            pltpu.VMEM((2, rank, width), bf16),
+            pltpu.VMEM((2, 1, width), bf16),
+            pltpu.VMEM((tokens, width), bf16),
+            pltpu.SemaphoreType.DMA((2, 3, 2)),
+        ],
+    )(*recvs, *own, *other)
+
+    def gathered(block):
+        near = [block] + [across(block, "dp", step) for step in range(1, replicas)]
+        return near + [across(piece, "segment", 1) for piece in near]
+
+    firsts = gathered(small)
+    (small_back,) = call(
+        functools.partial(backward_kernel, groups),
+        "backward",
+        [VMEM] * groups + [HBM] * 6 + [VMEM] * 4,
+        [((tokens, rank + 128), bf16)],
+        [
+            pltpu.VMEM((width, rank), bf16),
+            pltpu.VMEM((rank, width), bf16),
+            pltpu.VMEM((1, width), bf16),
+            pltpu.VMEM((tokens, width), f32),
+            pltpu.SemaphoreType.DMA((3, 2)),
+        ],
+    )(*recvs, *own, *other, small, middle, slope, moments)
+    seconds = gathered(small_back)
+
+    backs = exchanged(outs)
+    (out_hidden,) = call(
+        functools.partial(unpack_kernel, *sizes),
+        "unpack",
+        [SMEM] + [VMEM] * groups,
+        [(hidden_in.shape, bf16)],
+        [pltpu.VMEM((slots * length, part), bf16)],
+    )(cluster_ids, *backs)
+
+    all_tokens = 2 * replicas * tokens
+    grad_dn, grad_upper = call(
+        functools.partial(gradient_kernel, experts, replicas),
+        "gradients",
+        [VMEM] * (2 * experts + 4 * replicas) + [HBM] * 6,
+        [((slab, rank), bf16), ((rank, slab), bf16)],
+        [
+            pltpu.VMEM((slab, rank), bf16),
+            pltpu.VMEM((rank, slab), bf16),
+            pltpu.VMEM((2, 1, slab), bf16),
+            pltpu.VMEM((all_tokens, 3 * rank + 128), bf16),
+            pltpu.VMEM((all_tokens, rank + 128), bf16),
+            pltpu.VMEM((all_tokens, slab), bf16),
+            pltpu.VMEM((all_tokens, slab), bf16),
+            pltpu.VMEM((all_tokens, slab), bf16),
+            pltpu.VMEM((all_tokens, 256), f32),
+            pltpu.VMEM((all_tokens, 256), f32),
+            pltpu.SemaphoreType.DMA((2, 4)),
+        ],
+    )(*mine, *theirs, *firsts, *seconds, *own, *other)
+    return (out_hidden, grad_dn[None, None], grad_upper[None, None])
+
+
 def solution(mesh):
+    two = dict(mesh.shape) == {"expert": 4, "dp": 4, "segment": 2}
+    on_device = on_device_two_phases if two else on_device_pipelined
     return jax.shard_map(
         on_device,
         mesh=mesh,

time: 276 us -> 113 us (0.41)
  waiting for transfers between devices: 88.3 us -> 29 us
  other arithmetic: 45.8 us -> 0 us
  local copies, waits for them, and re-layouts: 42.1 us -> 3.86 us
  matrix products: 37.2 us -> 0 us
  Pallas kernels: 0 us -> 36.4 us
  blocking collectives: 18.1 us -> 0 us
  starting transfers between devices: 26.6 us -> 41.6 us
  between operations: 15.6 us -> 1.38 us
    reduce_scatter x2 -> x0, waiting for transfers between devices: 72.1 us -> none  [the longest x1 45.5 us: on_device(): lax.psum_scatter(grad_upper.astype(jnp.bfloat16), 'dp', scatter_dimension...]
    dot_general x25 -> x0, matrix products: 37.2 us -> none  [the longest x5 14.6 us: phase_backward(): d_act = jnp.dot(grad_in, w_upper.T, preferred_element_type=jnp.float32)]
    pallas_call x0 -> x6, Pallas kernels: none -> 36.4 us  [the longest x1 13.4 us: on_device_two_phases(): call(functools.partial(gradient_kernel, experts, replicas), 'gradients',...]
    dynamic_update_slice x20 -> x0, other arithmetic: 31.6 us -> none  [put_slot(): lax.dynamic_update_index_in_dim(buffer, jnp.where(valid, value, old_value...]
    ppermute x10 -> x42, starting transfers between devices: 17.1 us -> 41.6 us  [the longest x24 17.7 us: across(): return lax.ppermute(block, axis, [(i, i ^ distance) for i in range(size)])]
    ppermute x10 -> x42, waiting for transfers between devices: 6.69 us -> 29 us  [the longest x24 15.2 us: across(): return lax.ppermute(block, axis, [(i, i ^ distance) for i in range(size)])]
    dynamic_slice x21 -> x0, local copies, waits for them, and re-layouts: 16.6 us -> none  [the longest x20 15.4 us: put_slot(): old_value = lax.dynamic_index_in_dim(buffer, slot, 0, keepdims=False)]
    all_to_all x1 -> x0, blocking collectives: 13.4 us -> none  [on_device(): lax.all_to_all(own, 'expert', split_axis=0, concat_axis=0, tiled=True)]
  transfers between devices with their start and end apart: 15 -> 42, of which waited for: 8 -> 13; matrix products, arithmetic and copies ran while one was open for 41% -> 0% of each run, Pallas kernels for 0% -> 21%
where the time goes in v2:
time: 113 us; the launch traced here: 112 us
  starting transfers between devices  41.6 us (37%)
  Pallas kernels  36.4 us (32%)
  waiting for transfers between devices  29 us (26%)
  local copies, waits for them, and re-layouts  3.86 us (3%)
  between operations  1.38 us (1%)
    ppermute x24, starting transfers between devices, across(): return lax.ppermute(block, axis, [(i, i ^ distance) for i in range(size)])  17.7 us
    ppermute x24, waiting for transfers between devices, across(): return lax.ppermute(block, axis, [(i, i ^ distance) for i in range(size)])  15.2 us
    pallas_call x1, Pallas kernels, on_device_two_phases(): call(functools.partial(gradient_kernel, experts, replicas), 'gradients',...  13.4 us
    ppermute x14, starting transfers between devices, exchanged(): lax.ppermute(block, ('expert', 'segment'), [(i, i ^ step) for i in range(...  12.8 us
    ppermute x4, starting transfers between devices, on_device_two_phases(): lax.ppermute(block, ('dp', 'segment'), slab_route(replicas, turn // 2, tu...  11.1 us
    pallas_call x1, Pallas kernels, on_device_two_phases(): call(functools.partial(forward_kernel, groups), 'forward', [VMEM] * group...  8.32 us
    ppermute x14, waiting for transfers between devices, exchanged(): lax.ppermute(block, ('expert', 'segment'), [(i, i ^ step) for i in range(...  7.3 us
    pallas_call x1, Pallas kernels, on_device_two_phases(): call(functools.partial(backward_kernel, groups), 'backward', [VMEM] * gro...  6.81 us
  transfers between devices with their start and end apart: 42, of which 13 were waited for; matrix products, arithmetic and copies ran while one was open for 0% of the time, Pallas kernels for 21%

profile of v2, /device:TPU:0, one launch (start us, length us, event | category | flops | bytes accessed | tf_op | source)
XLA Modules:
  0.0 112.2 jit_solution(16490868388417033927)
XLA Ops:
  1.2 2.6 %pack.1 = (bf16[2,16,2048]{2,1,0:T(8,128)(2,1)}, bf16[2,16,2048]{2,1,0:T(8,128)(2,1)}, bf16[2,16,2048]{2,1,0:T(8,128)(2,1)}, bf16[2,16,2048]{2,1,0:T(8,128)(2,1)...) custom-call(s32[16]{0:T(128)} %ids.3, ...), custom_call_target="tpu_custom_call" | custom-call | tf_op jit(solution)/shard_map/pack/pallas_call | solution.py:656
  4.3 2.6 %collective-permute-start.1 = (bf16[2,16,2048]{2,1,0:T(8,128)(2,1)}, bf16[2,16,2048]{2,1,0:T(8,128)(2,1)S(1)}, u32[]{:S(2)}, u32[]{:S(2)}) collective-permute-start(bf16[2,16,2048]{2,1,0:T(8,128)(2,1)} %get-tuple-element.35), channel_id=1, source_target_pairs={{0,8},{1,9},{8,0},{9,1},{16,24},{17,25},{24,16},{25,17},{2,10},{3,... | collective-permute-start | bytes 393224 | tf_op jit(solution)/shard_map/ppermute | solution.py:624
  7.0 1.4 %collective-permute-done.9.refs_13_.refs_29_ = bf16[1,4096]{1,0:T(2,128)(2,1)S(1)} collective-permute-done((bf16[1,4096]{1,0:T(2,128)(2,1)}, bf16[1,4096]{1,0:T(2,128)(2,1)S(1)}, u32[]{:S(2)}, u32[]{:S(2)}) %collective-permute-start.9) | collective-permute-done | bytes 8224 | tf_op jit(solution)/shard_map/ppermute | solution.py:615
  8.4 2.6 %collective-permute-start.2 = (bf16[2,16,2048]{2,1,0:T(8,128)(2,1)}, bf16[2,16,2048]{2,1,0:T(8,128)(2,1)S(1)}, u32[]{:S(2)}, u32[]{:S(2)}) collective-permute-start(bf16[2,16,2048]{2,1,0:T(8,128)(2,1)} %get-tuple-element.36), channel_id=1, source_target_pairs={{0,9},{1,8},{8,1},{9,0},{16,25},{17,24},{24,17},{25,16},{2,11},{3,... | collective-permute-start | bytes 393224 | tf_op jit(solution)/shard_map/ppermute | solution.py:624
  11.0 1.5 %collective-permute-start.3 = (bf16[2,16,2048]{2,1,0:T(8,128)(2,1)}, bf16[2,16,2048]{2,1,0:T(8,128)(2,1)S(1)}, u32[]{:S(2)}, u32[]{:S(2)}) collective-permute-start(bf16[2,16,2048]{2,1,0:T(8,128)(2,1)} %get-tuple-element.37), channel_id=1, source_target_pairs={{0,16},{1,17},{8,24},{9,25},{16,0},{17,1},{24,8},{25,9},{2,18},{3,... | collective-permute-start | bytes 393224 | tf_op jit(solution)/shard_map/ppermute | solution.py:624
  12.5 1.6 %collective-permute-start.17 = (bf16[144,512]{1,0:T(8,128)(2,1)}, bf16[144,512]{1,0:T(8,128)(2,1)S(1)}, u32[]{:S(2)}, u32[]{:S(2)}) collective-permute-start(bf16[144,512]{1,0:T(8,128)(2,1)} %get-tuple-element.49), channel_id=1, source_target_pairs={{0,0},{1,4},{2,2},{3,6},{4,1},{5,5},{6,3},{7,7},{8,8},{9,12},{10,1... | collective-permute-start | bytes 442376 | tf_op jit(solution)/shard_map/ppermute | solution.py:664
  14.1 0.8 collective-permute-done.2.refs_3_
  14.9 2.3 %collective-permute-start.18 = (bf16[144,512]{1,0:T(8,128)(2,1)}, bf16[144,512]{1,0:T(8,128)(2,1)S(1)}, u32[]{:S(2)}, u32[]{:S(2)}) collective-permute-start(bf16[144,512]{1,0:T(8,128)(2,1)} %get-tuple-element.50), channel_id=1, source_target_pairs={{0,1},{1,5},{2,3},{3,7},{4,0},{5,4},{6,2},{7,6},{8,9},{9,13},{10,1... | collective-permute-start | bytes 442376 | tf_op jit(solution)/shard_map/ppermute | solution.py:664
  17.2 1.6 %collective-permute-start.19 = (bf16[144,512]{1,0:T(8,128)(2,1)}, bf16[144,512]{1,0:T(8,128)(2,1)S(1)}, u32[]{:S(2)}, u32[]{:S(2)}) collective-permute-start(bf16[144,512]{1,0:T(8,128)(2,1)} %get-tuple-element.51), channel_id=1, source_target_pairs={{0,2},{1,6},{2,0},{3,4},{4,3},{5,7},{6,1},{7,5},{8,10},{9,14},{10,... | collective-permute-start | bytes 442376 | tf_op jit(solution)/shard_map/ppermute | solution.py:664
  18.8 5.6 %collective-permute-start.20 = (bf16[144,512]{1,0:T(8,128)(2,1)}, bf16[144,512]{1,0:T(8,128)(2,1)S(1)}, u32[]{:S(2)}, u32[]{:S(2)}) collective-permute-start(bf16[144,512]{1,0:T(8,128)(2,1)} %get-tuple-element.52), channel_id=1, source_target_pairs={{0,3},{1,7},{2,1},{3,5},{4,2},{5,6},{6,0},{7,4},{8,11},{9,15},{10,... | collective-permute-start | bytes 442376 | tf_op jit(solution)/shard_map/ppermute | solution.py:664
  24.4 2.2 %collective-permute-done.18.refs_1_ = bf16[144,512]{1,0:T(8,128)(2,1)S(1)} collective-permute-done((bf16[144,512]{1,0:T(8,128)(2,1)}, bf16[144,512]{1,0:T(8,128)(2,1)S(1)}, u32[]{:S(2)}, u32[]{:S(2)}) %collective-permute-start.18) | collective-permute-done | bytes 147488 | tf_op jit(solution)/shard_map/ppermute | solution.py:664
  26.7 4.2 %collective-permute-done.20.refs_3_ = bf16[144,512]{1,0:T(8,128)(2,1)S(1)} collective-permute-done((bf16[144,512]{1,0:T(8,128)(2,1)}, bf16[144,512]{1,0:T(8,128)(2,1)S(1)}, u32[]{:S(2)}, u32[]{:S(2)}) %collective-permute-start.20) | collective-permute-done | bytes 147488 | tf_op jit(solution)/shard_map/ppermute | solution.py:664
  31.6 3.1 %repack.1 = (bf16[2,4,32,512]{3,2,1,0:T(8,128)(2,1)}, bf16[2,4,32,512]{3,2,1,0:T(8,128)(2,1)}, bf16[2,4,32,512]{3,2,1,0:T(8,128)(2,1)}, bf16[2,4,32,512]{3,2,1,0:T(8,128)(2,1)}) custom-call(bf16[144,512]{1,0:T(8,128)(2,1)} %copy-done.18, bf16[144,512]{1,0:T(8,128)(2,1)} %copy-done.19, bf16[144,512]{1,0:T(8,128)(2,1)} %copy-done.20, bf16[144,512]{1,0:T(8,128)(2,1)} %copy-done.21), custom_call_target="tpu_custom_call" | custom-call | tf_op jit(solution)/shard_map/repack/pallas_call | solution.py:667
  34.7 2.1 %collective-permute-done.4.refs_5_ = bf16[2,16,2048]{2,1,0:T(8,128)(2,1)S(1)} collective-permute-done((bf16[2,16,2048]{2,1,0:T(8,128)(2,1)}, bf16[2,16,2048]{2,1,0:T(8,128)(2,1)S(1)}, u32[]{:S(2)}, u32[]{:S(2)}) %collective-permute-start.4) | collective-permute-done | bytes 131104 | tf_op jit(solution)/shard_map/ppermute | solution.py:624
  36.9 3.4 %collective-permute-start.23 = (bf16[2,4,32,512]{3,2,1,0:T(8,128)(2,1)}, bf16[2,4,32,512]{3,2,1,0:T(8,128)(2,1)S(1)}, u32[]{:S(2)}, u32[]{:S(2)}) collective-permute-start(bf16[2,4,32,512]{3,2,1,0:T(8,128)(2,1)} %get-tuple-element.56), channel_id=1, source_target_pairs={{0,24},{8,16},{16,8},{24,0},{1,25},{9,17},{17,9},{25,1},{2,26},{10... | collective-permute-start | bytes 786440 | tf_op jit(solution)/shard_map/ppermute | solution.py:615
  40.3 5.4 %collective-permute-done.21.refs_1_ = bf16[2,4,32,512]{3,2,1,0:T(8,128)(2,1)S(1)} collective-permute-done((bf16[2,4,32,512]{3,2,1,0:T(8,128)(2,1)}, bf16[2,4,32,512]{3,2,1,0:T(8,128)(2,1)S(1)}, u32[]{:S(2)}, u32[]{:S(2)}) %collective-permute-start.21) | collective-permute-done | bytes 262176 | tf_op jit(solution)/shard_map/ppermute | solution.py:615
  45.7 4.0 %collective-permute-done.22.refs_2_ = bf16[2,4,32,512]{3,2,1,0:T(8,128)(2,1)S(1)} collective-permute-done((bf16[2,4,32,512]{3,2,1,0:T(8,128)(2,1)}, bf16[2,4,32,512]{3,2,1,0:T(8,128)(2,1)S(1)}, u32[]{:S(2)}, u32[]{:S(2)}) %collective-permute-start.22) | collective-permute-done | bytes 262176 | tf_op jit(solution)/shard_map/ppermute | solution.py:615
  50.4 1.1 %copy-done = bf16[4096,256]{1,0:T(8,128)(2,1)} copy-done((bf16[4096,256]{1,0:T(8,128)(2,1)}, bf16[4096,256]{1,0:T(8,128)(2,1)S(1)}, u32[]{:S(2)}) %copy-start) | copy-done | bytes 2097176
  52.3 8.3 %forward.1 = (bf16[16,2048]{1,0:T(8,128)(2,1)}, bf16[16,2048]{1,0:T(8,128)(2,1)}, bf16[16,2048]{1,0:T(8,128)(2,1)}, bf16[16,2048]{1,0:T(8,128)(2,1)}, bf16[16,20...) custom-call(bf16[2,16,2048]{2,1,0:T(8,128)(2,1)} %get-tuple-element., ...), custom_call_target="tpu_custom_call" | custom-call | tf_op jit(solution)/shard_map/forward/pallas_call | solution.py:676
  60.7 6.8 %backward.1.refs_16_ = bf16[64,384]{1,0:T(8,128)(2,1)} custom-call(bf16[2,16,2048]{2,1,0:T(8,128)(2,1)} %get-tuple-element.33.refs_0_, bf16[2,16,2048]{2,1,0:T(8,128)(2,1)} %copy-done.2, bf16[2,16,2048]{2,1,0:T(8,128)(2,1)} %copy-done.3, bf16[2,16,2048]{2,1,0:T(8,128)(2,1)} %copy-done.4, bf16[2,16,2048]{2,1,0:T(8,128)(2,1)} %copy-done.5, ...), custom_call_target="tpu_custom_call" | custom-call | tf_op jit(solution)/shard_map/backward/pallas_call | solution.py:701
  67.7 6.4 %collective-permute-start.37 = (bf16[64,384]{1,0:T(8,128)(2,1)}, bf16[64,384]{1,0:T(8,128)(2,1)S(1)}, u32[]{:S(2)}, u32[]{:S(2)}) collective-permute-start(bf16[64,384]{1,0:T(8,128)(2,1)} %backward.1.refs_16_), channel_id=1, source_target_pairs={{0,6},{2,4},{4,2},{6,0},{1,7},{3,5},{5,3},{7,1},{8,14},{10,12},{12... | collective-permute-start | bytes 147464 | tf_op jit(solution)/shard_map/ppermute | solution.py:615
  74.8 1.4 %collective-permute-start.11 = (bf16[16,2048]{1,0:T(8,128)(2,1)S(1)}, bf16[16,2048]{1,0:T(8,128)(2,1)S(1)}, u32[]{:S(2)}, u32[]{:S(2)}) collective-permute-start(bf16[16,2048]{1,0:T(8,128)(2,1)S(1)} %copy-done.48), channel_id=1, source_target_pairs={{0,8},{1,9},{8,0},{9,1},{16,24},{17,25},{24,16},{25,17},{2,10},{3,... | collective-permute-start | bytes 196616 | tf_op jit(solution)/shard_map/ppermute | solution.py:624
  77.3 2.0 %collective-permute-done.36.refs_18_ = bf16[64,384]{1,0:T(8,128)(2,1)S(1)} collective-permute-done((bf16[64,384]{1,0:T(8,128)(2,1)}, bf16[64,384]{1,0:T(8,128)(2,1)S(1)}, u32[]{:S(2)}, u32[]{:S(2)}) %collective-permute-start.36) | collective-permute-done | bytes 49184 | tf_op jit(solution)/shard_map/ppermute | solution.py:615
  80.1 3.6 %collective-permute-start.30 = (bf16[64,896]{1,0:T(8,128)(2,1)S(1)}, bf16[64,896]{1,0:T(8,128)(2,1)S(1)}, u32[]{:S(2)}, u32[]{:S(2)}) collective-permute-start(bf16[64,896]{1,0:T(8,128)(2,1)S(1)} %copy-done.9), channel_id=1, source_target_pairs={{0,6},{2,4},{4,2},{6,0},{1,7},{3,5},{5,3},{7,1},{8,14},{10,12},{12... | collective-permute-start | bytes 344072 | tf_op jit(solution)/shard_map/ppermute | solution.py:615
  83.7 0.8 collective-permute-start.28
  84.5 2.2 %collective-permute-start.15 = (bf16[16,2048]{1,0:T(8,128)(2,1)S(1)}, bf16[16,2048]{1,0:T(8,128)(2,1)S(1)}, u32[]{:S(2)}, u32[]{:S(2)}) collective-permute-start(bf16[16,2048]{1,0:T(8,128)(2,1)S(1)} %copy-done.44), channel_id=1, source_target_pairs={{0,24},{1,25},{8,16},{9,17},{16,8},{17,9},{24,0},{25,1},{2,26},{3,... | collective-permute-start | bytes 196616 | tf_op jit(solution)/shard_map/ppermute | solution.py:624
  86.7 0.8 collective-permute-start.16
  87.5 2.6 %collective-permute-done.15.refs_6_ = bf16[16,2048]{1,0:T(8,128)(2,1)S(1)} collective-permute-done((bf16[16,2048]{1,0:T(8,128)(2,1)S(1)}, bf16[16,2048]{1,0:T(8,128)(2,1)S(1)}, u32[]{:S(2)}, u32[]{:S(2)}) %collective-permute-start.15) | collective-permute-done | bytes 65568 | tf_op jit(solution)/shard_map/ppermute | solution.py:624
  90.1 1.8 %collective-permute-done.16.refs_7_ = bf16[16,2048]{1,0:T(8,128)(2,1)S(1)} collective-permute-done((bf16[16,2048]{1,0:T(8,128)(2,1)S(1)}, bf16[16,2048]{1,0:T(8,128)(2,1)S(1)}, u32[]{:S(2)}, u32[]{:S(2)}) %collective-permute-start.16) | collective-permute-done | bytes 65568 | tf_op jit(solution)/shard_map/ppermute | solution.py:624
  93.7 1.1 collective-permute-done.40.refs_22_
  95.0 2.2 %unpack.1 = bf16[16,4,2048]{2,1,0:T(4,128)(2,1)} custom-call(s32[16]{0:T(128)} %ids.3, bf16[16,2048]{1,0:T(8,128)(2,1)} %get-tuple-element.41.refs_0_, bf16[16,2048]{1,0:T(8,128)(2,1)} %copy-done.29, bf16[16,2048]{1,0:T(8,128)(2,1)} %copy-done.30, bf16[16,2048]{1,0:T(8,128)(2,1)} %copy-done.31, bf16[16,2048]{1,0:T(8,128)(2,1)} %copy-done.32, ...), custom_call_target="tpu_custom_call" | custom-call | tf_op jit(solution)/shard_map/unpack/pallas_call | solution.py:717
  98.6 13.4 %gradients.1 = (bf16[1024,256]{1,0:T(8,128)(2,1)}, bf16[256,1024]{1,0:T(8,128)(2,1)}) custom-call(bf16[2,4,32,512]{3,2,1,0:T(8,128)(2,1)} %get-tuple-element.53.refs_0_, bf16[2,4,32,512]{3,2,1,0:T(8,128)(2,1)} %copy-done.10, bf16[2,4,32,512]{3,2,1,0:T(8,128)(2,1)} %copy-done.11, bf16[2,4,32,512]{3,2,1,0:T(8,128)(2,1)} %copy-done.12, ...), custom_call_target="tpu_custom_call" | custom-call | tf_op jit(solution)/shard_map/gradients/pallas_call | solution.py:726
  (158 shorter events, 9.4 us)
Async XLA Ops:
  0.6 49.6 %collective-permute-start.7 = (bf16[4096,256]{1,0:T(8,128)(2,1)}, bf16[4096,256]{1,0:T(8,128)(2,1)S(1)}, u32[]{:S(2)}, u32[]{:S(2)}) collective-permute-start(bf16[4096,256]{1,0:T(8,128)(2,1)} %bitcast.5), channel_id=1, source_target_pairs={{0,1},{1,0},{2,3},{3,2},{4,5},{5,4},{6,7},{7,6},{8,9},{9,8},{10,11... | collective-permute-start | bytes 6291464 | tf_op jit(solution)/shard_map/ppermute | solution.py:615
  1.1 49.2 %collective-permute-start.8 = (bf16[256,4096]{1,0:T(8,128)(2,1)}, bf16[256,4096]{1,0:T(8,128)(2,1)S(1)}, u32[]{:S(2)}, u32[]{:S(2)}) collective-permute-start(bf16[256,4096]{1,0:T(8,128)(2,1)} %bitcast.9), channel_id=1, source_target_pairs={{0,1},{1,0},{2,3},{3,2},{4,5},{5,4},{6,7},{7,6},{8,9},{9,8},{10,11... | collective-permute-start | bytes 6291464 | tf_op jit(solution)/shard_map/ppermute | solution.py:615
  3.8 7.1 %collective-permute-start = (bf16[2,16,2048]{2,1,0:T(8,128)(2,1)}, bf16[2,16,2048]{2,1,0:T(8,128)(2,1)S(1)}, u32[]{:S(2)}, u32[]{:S(2)}) collective-permute-start(bf16[2,16,2048]{2,1,0:T(8,128)(2,1)} %get-tuple-element.34), channel_id=1, source_target_pairs={{0,1},{1,0},{8,9},{9,8},{16,17},{17,16},{24,25},{25,24},{2,3},{3,2... | collective-permute-start | bytes 393224 | tf_op jit(solution)/shard_map/ppermute | solution.py:624
  4.3 8.3 %collective-permute-start.1 = (bf16[2,16,2048]{2,1,0:T(8,128)(2,1)}, bf16[2,16,2048]{2,1,0:T(8,128)(2,1)S(1)}, u32[]{:S(2)}, u32[]{:S(2)}) collective-permute-start(bf16[2,16,2048]{2,1,0:T(8,128)(2,1)} %get-tuple-element.35), channel_id=1, source_target_pairs={{0,8},{1,9},{8,0},{9,1},{16,24},{17,25},{24,16},{25,17},{2,10},{3,... | collective-permute-start | bytes 393224 | tf_op jit(solution)/shard_map/ppermute | solution.py:624
  8.4 6.5 %collective-permute-start.2 = (bf16[2,16,2048]{2,1,0:T(8,128)(2,1)}, bf16[2,16,2048]{2,1,0:T(8,128)(2,1)S(1)}, u32[]{:S(2)}, u32[]{:S(2)}) collective-permute-start(bf16[2,16,2048]{2,1,0:T(8,128)(2,1)} %get-tuple-element.36), channel_id=1, source_target_pairs={{0,9},{1,8},{8,1},{9,0},{16,25},{17,24},{24,17},{25,16},{2,11},{3,... | collective-permute-start | bytes 393224 | tf_op jit(solution)/shard_map/ppermute | solution.py:624
  11.0 6.2 %collective-permute-start.3 = (bf16[2,16,2048]{2,1,0:T(8,128)(2,1)}, bf16[2,16,2048]{2,1,0:T(8,128)(2,1)S(1)}, u32[]{:S(2)}, u32[]{:S(2)}) collective-permute-start(bf16[2,16,2048]{2,1,0:T(8,128)(2,1)} %get-tuple-element.37), channel_id=1, source_target_pairs={{0,16},{1,17},{8,24},{9,25},{16,0},{17,1},{24,8},{25,9},{2,18},{3,... | collective-permute-start | bytes 393224 | tf_op jit(solution)/shard_map/ppermute | solution.py:624
  12.5 6.3 %collective-permute-start.17 = (bf16[144,512]{1,0:T(8,128)(2,1)}, bf16[144,512]{1,0:T(8,128)(2,1)S(1)}, u32[]{:S(2)}, u32[]{:S(2)}) collective-permute-start(bf16[144,512]{1,0:T(8,128)(2,1)} %get-tuple-element.49), channel_id=1, source_target_pairs={{0,0},{1,4},{2,2},{3,6},{4,1},{5,5},{6,3},{7,7},{8,8},{9,12},{10,1... | collective-permute-start | bytes 442376 | tf_op jit(solution)/shard_map/ppermute | solution.py:664
  14.9 11.7 %collective-permute-start.18 = (bf16[144,512]{1,0:T(8,128)(2,1)}, bf16[144,512]{1,0:T(8,128)(2,1)S(1)}, u32[]{:S(2)}, u32[]{:S(2)}) collective-permute-start(bf16[144,512]{1,0:T(8,128)(2,1)} %get-tuple-element.50), channel_id=1, source_target_pairs={{0,1},{1,5},{2,3},{3,7},{4,0},{5,4},{6,2},{7,6},{8,9},{9,13},{10,1... | collective-permute-start | bytes 442376 | tf_op jit(solution)/shard_map/ppermute | solution.py:664
  17.2 9.4 %collective-permute-start.19 = (bf16[144,512]{1,0:T(8,128)(2,1)}, bf16[144,512]{1,0:T(8,128)(2,1)S(1)}, u32[]{:S(2)}, u32[]{:S(2)}) collective-permute-start(bf16[144,512]{1,0:T(8,128)(2,1)} %get-tuple-element.51), channel_id=1, source_target_pairs={{0,2},{1,6},{2,0},{3,4},{4,3},{5,7},{6,1},{7,5},{8,10},{9,14},{10,... | collective-permute-start | bytes 442376 | tf_op jit(solution)/shard_map/ppermute | solution.py:664
  18.8 12.1 %collective-permute-start.20 = (bf16[144,512]{1,0:T(8,128)(2,1)}, bf16[144,512]{1,0:T(8,128)(2,1)S(1)}, u32[]{:S(2)}, u32[]{:S(2)}) collective-permute-start(bf16[144,512]{1,0:T(8,128)(2,1)} %get-tuple-element.52), channel_id=1, source_target_pairs={{0,3},{1,7},{2,1},{3,5},{4,2},{5,6},{6,0},{7,4},{8,11},{9,15},{10,... | collective-permute-start | bytes 442376 | tf_op jit(solution)/shard_map/ppermute | solution.py:664
  26.6 10.2 %collective-permute-start.4 = (bf16[2,16,2048]{2,1,0:T(8,128)(2,1)}, bf16[2,16,2048]{2,1,0:T(8,128)(2,1)S(1)}, u32[]{:S(2)}, u32[]{:S(2)}) collective-permute-start(bf16[2,16,2048]{2,1,0:T(8,128)(2,1)} %get-tuple-element.38), channel_id=1, source_target_pairs={{0,17},{1,16},{8,25},{9,24},{16,1},{17,0},{24,9},{25,8},{2,19},{3,... | collective-permute-start | bytes 393224 | tf_op jit(solution)/shard_map/ppermute | solution.py:624
  26.6 10.2 %collective-permute-start.5 = (bf16[2,16,2048]{2,1,0:T(8,128)(2,1)}, bf16[2,16,2048]{2,1,0:T(8,128)(2,1)S(1)}, u32[]{:S(2)}, u32[]{:S(2)}) collective-permute-start(bf16[2,16,2048]{2,1,0:T(8,128)(2,1)} %get-tuple-element.39), channel_id=1, source_target_pairs={{0,24},{1,25},{8,16},{9,17},{16,8},{17,9},{24,0},{25,1},{2,26},{3,... | collective-permute-start | bytes 393224 | tf_op jit(solution)/shard_map/ppermute | solution.py:624
  30.9 6.0 %collective-permute-start.6 = (bf16[2,16,2048]{2,1,0:T(8,128)(2,1)}, bf16[2,16,2048]{2,1,0:T(8,128)(2,1)S(1)}, u32[]{:S(2)}, u32[]{:S(2)}) collective-permute-start(bf16[2,16,2048]{2,1,0:T(8,128)(2,1)} %get-tuple-element.40), channel_id=1, source_target_pairs={{0,25},{1,24},{8,17},{9,16},{16,9},{17,8},{24,1},{25,0},{2,27},{3,... | collective-permute-start | bytes 393224 | tf_op jit(solution)/shard_map/ppermute | solution.py:624
  36.8 8.9 %collective-permute-start.21 = (bf16[2,4,32,512]{3,2,1,0:T(8,128)(2,1)}, bf16[2,4,32,512]{3,2,1,0:T(8,128)(2,1)S(1)}, u32[]{:S(2)}, u32[]{:S(2)}) collective-permute-start(bf16[2,4,32,512]{3,2,1,0:T(8,128)(2,1)} %get-tuple-element.54), channel_id=1, source_target_pairs={{0,8},{8,0},{16,24},{24,16},{1,9},{9,1},{17,25},{25,17},{2,10},{10... | collective-permute-start | bytes 786440 | tf_op jit(solution)/shard_map/ppermute | solution.py:615
  36.8 12.9 %collective-permute-start.22 = (bf16[2,4,32,512]{3,2,1,0:T(8,128)(2,1)}, bf16[2,4,32,512]{3,2,1,0:T(8,128)(2,1)S(1)}, u32[]{:S(2)}, u32[]{:S(2)}) collective-permute-start(bf16[2,4,32,512]{3,2,1,0:T(8,128)(2,1)} %get-tuple-element.55), channel_id=1, source_target_pairs={{0,16},{8,24},{16,0},{24,8},{1,17},{9,25},{17,1},{25,9},{2,18},{10... | collective-permute-start | bytes 786440 | tf_op jit(solution)/shard_map/ppermute | solution.py:615
  36.9 12.8 %collective-permute-start.23 = (bf16[2,4,32,512]{3,2,1,0:T(8,128)(2,1)}, bf16[2,4,32,512]{3,2,1,0:T(8,128)(2,1)S(1)}, u32[]{:S(2)}, u32[]{:S(2)}) collective-permute-start(bf16[2,4,32,512]{3,2,1,0:T(8,128)(2,1)} %get-tuple-element.56), channel_id=1, source_target_pairs={{0,24},{8,16},{16,8},{24,0},{1,25},{9,17},{17,9},{25,1},{2,26},{10... | collective-permute-start | bytes 786440 | tf_op jit(solution)/shard_map/ppermute | solution.py:615
  45.7 22.0 %collective-permute-start.24 = (bf16[2,4,32,512]{3,2,1,0:T(8,128)(2,1)}, bf16[2,4,32,512]{3,2,1,0:T(8,128)(2,1)S(1)}, u32[]{:S(2)}, u32[]{:S(2)}) collective-permute-start(bf16[2,4,32,512]{3,2,1,0:T(8,128)(2,1)} %get-tuple-element.53.refs_0_), channel_id=1, source_target_pairs={{0,1},{1,0},{2,3},{3,2},{4,5},{5,4},{6,7},{7,6},{8,9},{9,8},{10,11... | collective-permute-start | bytes 786440 | tf_op jit(solution)/shard_map/ppermute | solution.py:615
  49.7 24.3 %collective-permute-start.25 = (bf16[2,4,32,512]{3,2,1,0:T(8,128)(2,1)S(1)}, bf16[2,4,32,512]{3,2,1,0:T(8,128)(2,1)S(1)}, u32[]{:S(2)}, u32[]{:S(2)}) collective-permute-start(bf16[2,4,32,512]{3,2,1,0:T(8,128)(2,1)S(1)} %collective-permute-done.21.refs_1_), channel_id=1, source_target_pairs={{0,1},{1,0},{2,3},{3,2},{4,5},{5,4},{6,7},{7,6},{8,9},{9,8},{10,11... | collective-permute-start | bytes 786440 | tf_op jit(solution)/shard_map/ppermute | solution.py:615
  49.8 24.3 %collective-permute-start.26 = (bf16[2,4,32,512]{3,2,1,0:T(8,128)(2,1)S(1)}, bf16[2,4,32,512]{3,2,1,0:T(8,128)(2,1)S(1)}, u32[]{:S(2)}, u32[]{:S(2)}) collective-permute-start(bf16[2,4,32,512]{3,2,1,0:T(8,128)(2,1)S(1)} %collective-permute-done.22.refs_2_), channel_id=1, source_target_pairs={{0,1},{1,0},{2,3},{3,2},{4,5},{5,4},{6,7},{7,6},{8,9},{9,8},{10,11... | collective-permute-start | bytes 786440 | tf_op jit(solution)/shard_map/ppermute | solution.py:615
  50.3 24.5 %collective-permute-start.27 = (bf16[2,4,32,512]{3,2,1,0:T(8,128)(2,1)S(1)}, bf16[2,4,32,512]{3,2,1,0:T(8,128)(2,1)S(1)}, u32[]{:S(2)}, u32[]{:S(2)}) collective-permute-start(bf16[2,4,32,512]{3,2,1,0:T(8,128)(2,1)S(1)} %collective-permute-done.23.refs_3_), channel_id=1, source_target_pairs={{0,1},{1,0},{2,3},{3,2},{4,5},{5,4},{6,7},{7,6},{8,9},{9,8},{10,11... | collective-permute-start | bytes 786440 | tf_op jit(solution)/shard_map/ppermute | solution.py:615
  67.5 7.3 %collective-permute-start.38 = (bf16[64,384]{1,0:T(8,128)(2,1)}, bf16[64,384]{1,0:T(8,128)(2,1)S(1)}, u32[]{:S(2)}, u32[]{:S(2)}) collective-permute-start(bf16[64,384]{1,0:T(8,128)(2,1)} %backward.1.refs_16_), channel_id=1, source_target_pairs={{0,1},{1,0},{2,3},{3,2},{4,5},{5,4},{6,7},{7,6},{8,9},{9,8},{10,11... | collective-permute-start | bytes 147464 | tf_op jit(solution)/shard_map/ppermute | solution.py:615
  67.7 9.1 %collective-permute-start.37 = (bf16[64,384]{1,0:T(8,128)(2,1)}, bf16[64,384]{1,0:T(8,128)(2,1)S(1)}, u32[]{:S(2)}, u32[]{:S(2)}) collective-permute-start(bf16[64,384]{1,0:T(8,128)(2,1)} %backward.1.refs_16_), channel_id=1, source_target_pairs={{0,6},{2,4},{4,2},{6,0},{1,7},{3,5},{5,3},{7,1},{8,14},{10,12},{12... | collective-permute-start | bytes 147464 | tf_op jit(solution)/shard_map/ppermute | solution.py:615
  74.1 5.9 %collective-permute-start.35 = (bf16[64,384]{1,0:T(8,128)(2,1)}, bf16[64,384]{1,0:T(8,128)(2,1)S(1)}, u32[]{:S(2)}, u32[]{:S(2)}) collective-permute-start(bf16[64,384]{1,0:T(8,128)(2,1)} %backward.1.refs_16_), channel_id=1, source_target_pairs={{0,2},{2,0},{4,6},{6,4},{1,3},{3,1},{5,7},{7,5},{8,10},{10,8},{12,... | collective-permute-start | bytes 147464 | tf_op jit(solution)/shard_map/ppermute | solution.py:615
  74.7 5.3 %collective-permute-start.10 = (bf16[16,2048]{1,0:T(8,128)(2,1)S(1)}, bf16[16,2048]{1,0:T(8,128)(2,1)S(1)}, u32[]{:S(2)}, u32[]{:S(2)}) collective-permute-start(bf16[16,2048]{1,0:T(8,128)(2,1)S(1)} %copy-done.49), channel_id=1, source_target_pairs={{0,1},{1,0},{8,9},{9,8},{16,17},{17,16},{24,25},{25,24},{2,3},{3,2... | collective-permute-start | bytes 196616 | tf_op jit(solution)/shard_map/ppermute | solution.py:624
  74.8 8.9 %collective-permute-start.11 = (bf16[16,2048]{1,0:T(8,128)(2,1)S(1)}, bf16[16,2048]{1,0:T(8,128)(2,1)S(1)}, u32[]{:S(2)}, u32[]{:S(2)}) collective-permute-start(bf16[16,2048]{1,0:T(8,128)(2,1)S(1)} %copy-done.48), channel_id=1, source_target_pairs={{0,8},{1,9},{8,0},{9,1},{16,24},{17,25},{24,16},{25,17},{2,10},{3,... | collective-permute-start | bytes 196616 | tf_op jit(solution)/shard_map/ppermute | solution.py:624
  76.8 6.9 %collective-permute-start.12 = (bf16[16,2048]{1,0:T(8,128)(2,1)S(1)}, bf16[16,2048]{1,0:T(8,128)(2,1)S(1)}, u32[]{:S(2)}, u32[]{:S(2)}) collective-permute-start(bf16[16,2048]{1,0:T(8,128)(2,1)S(1)} %copy-done.47), channel_id=1, source_target_pairs={{0,9},{1,8},{8,1},{9,0},{16,25},{17,24},{24,17},{25,16},{2,11},{3,... | collective-permute-start | bytes 196616 | tf_op jit(solution)/shard_map/ppermute | solution.py:624
  80.0 6.8 %collective-permute-start.14 = (bf16[16,2048]{1,0:T(8,128)(2,1)S(1)}, bf16[16,2048]{1,0:T(8,128)(2,1)S(1)}, u32[]{:S(2)}, u32[]{:S(2)}) collective-permute-start(bf16[16,2048]{1,0:T(8,128)(2,1)S(1)} %copy-done.45), channel_id=1, source_target_pairs={{0,17},{1,16},{8,25},{9,24},{16,1},{17,0},{24,9},{25,8},{2,19},{3,... | collective-permute-start | bytes 196616 | tf_op jit(solution)/shard_map/ppermute | solution.py:624
  80.1 12.1 %collective-permute-start.30 = (bf16[64,896]{1,0:T(8,128)(2,1)S(1)}, bf16[64,896]{1,0:T(8,128)(2,1)S(1)}, u32[]{:S(2)}, u32[]{:S(2)}) collective-permute-start(bf16[64,896]{1,0:T(8,128)(2,1)S(1)} %copy-done.9), channel_id=1, source_target_pairs={{0,6},{2,4},{4,2},{6,0},{1,7},{3,5},{5,3},{7,1},{8,14},{10,12},{12... | collective-permute-start | bytes 344072 | tf_op jit(solution)/shard_map/ppermute | solution.py:615
  83.7 9.3 %collective-permute-start.29 = (bf16[64,896]{1,0:T(8,128)(2,1)S(1)}, bf16[64,896]{1,0:T(8,128)(2,1)S(1)}, u32[]{:S(2)}, u32[]{:S(2)}) collective-permute-start(bf16[64,896]{1,0:T(8,128)(2,1)S(1)} %copy-done.9), channel_id=1, source_target_pairs={{0,4},{2,6},{4,0},{6,2},{1,5},{3,7},{5,1},{7,3},{8,12},{10,14},{12... | collective-permute-start | bytes 344072 | tf_op jit(solution)/shard_map/ppermute | solution.py:615
  83.7 9.4 %collective-permute-start.28 = (bf16[64,896]{1,0:T(8,128)(2,1)S(1)}, bf16[64,896]{1,0:T(8,128)(2,1)S(1)}, u32[]{:S(2)}, u32[]{:S(2)}) collective-permute-start(bf16[64,896]{1,0:T(8,128)(2,1)S(1)} %copy-done.9), channel_id=1, source_target_pairs={{0,2},{2,0},{4,6},{6,4},{1,3},{3,1},{5,7},{7,5},{8,10},{10,8},{12,... | collective-permute-start | bytes 344072 | tf_op jit(solution)/shard_map/ppermute | solution.py:615
  84.5 5.5 %collective-permute-start.15 = (bf16[16,2048]{1,0:T(8,128)(2,1)S(1)}, bf16[16,2048]{1,0:T(8,128)(2,1)S(1)}, u32[]{:S(2)}, u32[]{:S(2)}) collective-permute-start(bf16[16,2048]{1,0:T(8,128)(2,1)S(1)} %copy-done.44), channel_id=1, source_target_pairs={{0,24},{1,25},{8,16},{9,17},{16,8},{17,9},{24,0},{25,1},{2,26},{3,... | collective-permute-start | bytes 196616 | tf_op jit(solution)/shard_map/ppermute | solution.py:624
  91.9 5.4 %collective-permute-start.31 = (bf16[64,896]{1,0:T(8,128)(2,1)S(1)}, bf16[64,896]{1,0:T(8,128)(2,1)S(1)}, u32[]{:S(2)}, u32[]{:S(2)}) collective-permute-start(bf16[64,896]{1,0:T(8,128)(2,1)S(1)} %copy-done.9), channel_id=1, source_target_pairs={{0,1},{1,0},{2,3},{3,2},{4,5},{5,4},{6,7},{7,6},{8,9},{9,8},{10,11... | collective-permute-start | bytes 344072 | tf_op jit(solution)/shard_map/ppermute | solution.py:615
  (60 other events, 764.7 us)

commit v3 on v0

--- a/solution.py
+++ b/solution.py
@@ -1,6 +1,10 @@
+import functools
+
 import jax
 import jax.numpy as jnp
 from jax import lax
+from jax.experimental import pallas as pl
+from jax.experimental.pallas import tpu as pltpu
 from jax.sharding import PartitionSpec as P
 
 MICRO = 4
@@ -71,7 +75,7 @@
     return lax.dynamic_update_index_in_dim(buffer, jnp.where(valid, value, old_value), slot, 0)
 
 
-def on_device(hidden_in, cotangent, cluster_ids, w_down, w_up, gain):
+def on_device_pipelined(hidden_in, cotangent, cluster_ids, w_down, w_up, gain):
     experts = lax.axis_size("expert")
     phases = lax.axis_size("segment")
     phase = lax.axis_index("segment")
@@ -187,7 +191,421 @@
     )
 
 
+CHUNK = 512
+VMEM_LIMIT = 56 * 1024 * 1024
+TRANS_RHS = (((1,), (1,)), ((), ()))
+TRANS_LHS = (((0,), (0,)), ((), ()))
+
+
+def matmul(left, right, dims=(((1,), (0,)), ((), ()))):
+    return lax.dot_general(left, right, dims, preferred_element_type=jnp.float32)
+
+
+def spread_ids(ids, shape, length):
+    lane = lax.broadcasted_iota(jnp.int32, shape, 1)
+    spread = jnp.zeros(shape, jnp.int32)
+    for n in range(ids.shape[0]):
+        spread = jnp.where(lane // length == n, ids[n], spread)
+    return spread
+
+
+def placement(ids_row, length, capacity, slots):
+    tokens = ids_row.shape[1]
+    kinds = lax.broadcasted_iota(jnp.int32, (8, tokens), 0)
+    member = (kinds == ids_row).astype(jnp.float32)
+    at_col = lax.broadcasted_iota(jnp.int32, (tokens, tokens), 0)
+    at_row = lax.broadcasted_iota(jnp.int32, (tokens, tokens), 1)
+    before = (lax.rem(at_col, length) == 0) & (at_col // length < at_row // length)
+    counts = matmul(member.astype(jnp.bfloat16), before.astype(jnp.float32).astype(jnp.bfloat16))
+    rank = jnp.sum(member * counts, axis=0, keepdims=True).astype(jnp.int32)
+    target = (ids_row * capacity + rank) * length + lax.rem(at_row[:1], length)
+    packed = lax.broadcasted_iota(jnp.int32, (slots * length, tokens), 0)
+    return (packed == target).astype(jnp.float32).astype(jnp.bfloat16)
+
+
+def pack_kernel(length, capacity, slots, ids, hidden, cot, send):
+    groups, _, rows, part = send.shape
+    tokens = hidden.shape[0] * length
+    ids_row = spread_ids(ids, (8, tokens), length)[:1]
+    place = placement(ids_row, length, capacity, slots)
+    for which, source in enumerate((hidden, cot)):
+        moved = matmul(place, source[...].reshape(tokens, part)).astype(jnp.bfloat16)
+        for group in range(groups):
+            send[group, which] = moved[group * rows : (group + 1) * rows]
+
+
+def slice_kernel(recv, *outs):
+    experts, _, _, rows, part = recv.shape
+    slab = outs[0].shape[2]
+    place = lax.axis_index("dp")
+    per_half = part // slab
+    for step, out in enumerate(outs):
+        chip = place ^ step
+        half = chip // per_half
+        cols = pl.ds(pl.multiple_of((chip - half * per_half) * slab, slab), slab)
+        for which in range(2):
+            for e in range(experts):
+                out[which, e * rows : (e + 1) * rows] = recv[e, half, which, :, cols]
+
+
+def unpack_kernel(length, capacity, slots, ids, back, out):
+    groups, rows, width = back.shape
+    s_local = out.shape[0]
+    ids_row = spread_ids(ids, (8, s_local * length), length)[:1]
+    place = placement(ids_row, length, capacity, slots)
+    moved = matmul(place, back[...].reshape(groups * rows, width), TRANS_LHS)
+    out[...] = moved.astype(jnp.bfloat16).reshape(s_local, length, width)
+
+
+def split_three(value):
+    top = value.astype(jnp.bfloat16).astype(jnp.float32)
+    mid = (value - top).astype(jnp.bfloat16).astype(jnp.float32)
+    low = (value - top - mid).astype(jnp.bfloat16).astype(jnp.float32)
+    return [top, mid, low]
+
+
+def side_by_side(columns, tokens):
+    lane = lax.broadcasted_iota(jnp.int32, (tokens, 128), 1)
+    block = jnp.zeros((tokens, 128), jnp.float32)
+    at = 0
+    for column in columns:
+        for piece in split_three(column):
+            block = jnp.where(lane == at, piece, block)
+            at += 1
+    return block.astype(jnp.bfloat16)
+
+
+def lanes(value):
+    total = value[:, :128]
+    for start in range(128, value.shape[1], 128):
+        total = total + value[:, start : start + 128]
+    return total
+
+
+def row_sum(parts):
+    return jnp.sum(parts, axis=1, keepdims=True)
+
+
+def chain_kernel(
+    recv, own_dn, own_up, own_gain, other_dn, other_up, other_gain,
+    out, small,
+    dn_buf, up_buf, gain_buf, entering, middle, d_norms, sems,
+):
+    phase = lax.axis_index("segment")
+    experts, phases, _, rows, part = recv.shape
+    tokens = experts * rows
+    width = phases * part
+    rank = dn_buf.shape[2]
+    own, other = (own_dn, own_up, own_gain), (other_dn, other_up, other_gain)
+
+    def copies(sources, at):
+        return [
+            pltpu.make_async_copy(source, buffer.at[at], sems.at[at, which])
+            for which, (source, buffer) in enumerate(zip(sources, (dn_buf, up_buf, gain_buf)))
+        ]
+
+    for this in range(2):
+
+        @pl.when(phase == this)
+        def _():
+            for at in range(2):
+                for copy in copies(own if at == this else other, at):
+                    copy.start()
+
+    waits = [copies(own, at) for at in range(2)]
+    cols = range(0, width, CHUNK)
+
+    def block(which, col):
+        half, start = col // part, col % part
+        return jnp.concatenate(
+            [recv[e, half, which, :, start : start + CHUNK] for e in range(experts)], axis=0
+        )
+
+    def inverse_of(ref, mean):
+        total = jnp.zeros((tokens, 128), jnp.float32)
+        for col in cols:
+            center = ref[:, col : col + CHUNK].astype(jnp.float32) - mean
+            total = total + lanes(center * center)
+        return lax.rsqrt(row_sum(total) / width + EPS)
+
+    def down(ref, mean, inverse, at):
+        pre = jnp.zeros((tokens, rank), jnp.float32)
+        for col in cols:
+            here = slice(col, col + CHUNK)
+            normed = (ref[:, here].astype(jnp.float32) - mean) * inverse
+            lowered = (normed * gain_buf[at, :, here].astype(jnp.float32)).astype(jnp.bfloat16)
+            pre = pre + matmul(lowered, dn_buf[at, here, :])
+        return pre
+
+    total = jnp.zeros((tokens, 128), jnp.float32)
+    for col in cols:
+        value = block(0, col)
+        entering[:, col : col + CHUNK] = value
+        total = total + lanes(value.astype(jnp.float32))
+    mean_0 = row_sum(total) / width
+    inverse_0 = inverse_of(entering, mean_0)
+    waits[0][0].wait()
+    waits[0][2].wait()
+    pre_0 = down(entering, mean_0, inverse_0, 0)
+    act_0 = gelu_value(pre_0).astype(jnp.bfloat16)
+    slope_0 = gelu_slope(pre_0)
+
+    waits[0][1].wait()
+    total = jnp.zeros((tokens, 128), jnp.float32)
+    for col in cols:
+        here = slice(col, col + CHUNK)
+        value = entering[:, here].astype(jnp.float32) + matmul(act_0, up_buf[0, :, here])
+        value = value.astype(jnp.bfloat16)
+        middle[:, here] = value
+        total = total + lanes(value.astype(jnp.float32))
+    mean_1 = row_sum(total) / width
+    inverse_1 = inverse_of(middle, mean_1)
+    for copy in waits[1]:
+        copy.wait()
+    d_act = jnp.zeros((tokens, rank), jnp.float32)
+    for col in cols:
+        d_act = d_act + matmul(block(1, col), up_buf[1, :, col : col + CHUNK], TRANS_RHS)
+    pre_1 = down(middle, mean_1, inverse_1, 1)
+    act_1 = gelu_value(pre_1).astype(jnp.bfloat16)
+    d_pre_1 = (d_act * gelu_slope(pre_1)).astype(jnp.bfloat16)
+
+    total = jnp.zeros((tokens, 128), jnp.float32)
+    cross = jnp.zeros((tokens, 128), jnp.float32)
+    for col in cols:
+        here = slice(col, col + CHUNK)
+        wide = middle[:, here].astype(jnp.float32)
+        d_norm = matmul(d_pre_1, dn_buf[1, here, :], TRANS_RHS)
+        d_norm = d_norm * gain_buf[1, :, here].astype(jnp.float32)
+        d_norms[:, here] = d_norm
+        total = total + lanes(d_norm)
+        cross = cross + lanes(d_norm * ((wide - mean_1) * inverse_1))
+        leaving = (wide + matmul(act_1, up_buf[1, :, here])).astype(jnp.bfloat16)
+        half, start = col // part, col % part
+        for e in range(experts):
+            out[e, half, :, start : start + CHUNK] = leaving[e * rows : (e + 1) * rows]
+    shift = row_sum(total) / width
+    along = row_sum(cross) / width
+    d_act = jnp.zeros((tokens, rank), jnp.float32)
+    for col in cols:
+        here = slice(col, col + CHUNK)
+        normed = (middle[:, here].astype(jnp.float32) - mean_1) * inverse_1
+        grad = block(1, col).astype(jnp.float32) + inverse_1 * (
+            d_norms[:, here] - shift - normed * along
+        )
+        d_act = d_act + matmul(grad.astype(jnp.bfloat16), up_buf[0, :, here], TRANS_RHS)
+    d_pre_0 = (d_act * slope_0).astype(jnp.bfloat16)
+    for at, value in enumerate((act_0, act_1, d_pre_0, d_pre_1)):
+        small[:, at * rank : (at + 1) * rank] = value
+    moments = (mean_0, inverse_0, mean_1, inverse_1, shift, along)
+    small[:, 4 * rank :] = side_by_side(moments, tokens)
+
+
+def gradient_kernel(sources, *refs):
+    slices, refs = refs[:sources], refs[sources:]
+    smalls, refs = refs[:sources], refs[sources:]
+    own, other, refs = refs[:3], refs[3:6], refs[6:]
+    (grad_dn, grad_upper, dn_buf, up_buf, gain_buf, small, moments, lows, grads, ups, downs,
+     sems) = refs
+    core = lax.axis_index("segment")
+    place = lax.axis_index("dp")
+    _, rows, slab = slices[0].shape
+    rank = dn_buf.shape[1]
+    features = pl.ds(pl.multiple_of(place * slab, slab), slab)
+
+    def copies(up, gain_first, dn, gain_second):
+        moves = (
+            (up.at[:, features], up_buf),
+            (dn.at[features, :], dn_buf),
+            (gain_first.at[:, features], gain_buf.at[0]),
+            (gain_second.at[:, features], gain_buf.at[1]),
+        )
+        return [
+            pltpu.make_async_copy(source, target, sems.at[at])
+            for at, (source, target) in enumerate(moves)
+        ]
+
+    @pl.when(core == 0)
+    def _():
+        for copy in copies(own[1], own[2], other[0], other[2]):
+            copy.start()
+
+    @pl.when(core != 0)
+    def _():
+        for copy in copies(other[1], other[2], own[0], own[2]):
+            copy.start()
+
+    for source in range(sources):
+        small[source * rows : (source + 1) * rows] = smalls[source][...]
+    held = lax.broadcasted_iota(jnp.int32, (128, 6 * 128), 0)
+    wanted = lax.broadcasted_iota(jnp.int32, (128, 6 * 128), 1) // 128
+    adds = (held // 3 == wanted).astype(jnp.float32).astype(jnp.bfloat16)
+    moments[...] = matmul(small[:, 4 * rank :], adds)
+    for copy in copies(own[1], own[2], other[0], other[2]):
+        copy.wait()
+
+    columns = 256
+
+    def moment(at, index):
+        value = moments[at, index * 128 : (index + 1) * 128]
+        return jnp.concatenate([value] * (columns // 128), axis=1)
+
+    for col in range(0, slab, columns):
+        here = slice(col, col + columns)
+        ups[...] = matmul(small[:, :rank], up_buf[:, here])
+        scales = [gain_buf[at, :, here].astype(jnp.float32) for at in range(2)]
+
+        @pl.when(core == 0)
+        def _():
+            downs[...] = matmul(small[:, 3 * rank : 4 * rank], dn_buf[here, :], TRANS_RHS)
+            for source in range(sources):
+                at = slice(source * rows, (source + 1) * rows)
+                wide = slices[source][0, :, here].astype(jnp.float32)
+                normed = (wide - moment(at, 0)) * moment(at, 1)
+                lows[at, here] = (normed * scales[0]).astype(jnp.bfloat16)
+                middle = (wide + ups[at]).astype(jnp.bfloat16).astype(jnp.float32)
+                inverse = moment(at, 3)
+                normed = (middle - moment(at, 2)) * inverse
+                d_norm = downs[at] * scales[1]
+                grads[at, here] = (
+                    slices[source][1, :, here].astype(jnp.float32)
+                    + inverse * (d_norm - moment(at, 4) - normed * moment(at, 5))
+                ).astype(jnp.bfloat16)
+
+        @pl.when(core != 0)
+        def _():
+            for source in range(sources):
+                at = slice(source * rows, (source + 1) * rows)
+                wide = slices[source][0, :, here].astype(jnp.float32)
+                middle = (wide + ups[at]).astype(jnp.bfloat16).astype(jnp.float32)
+                normed = (middle - moment(at, 2)) * moment(at, 3)
+                lows[at, here] = (normed * scales[1]).astype(jnp.bfloat16)
+                grads[at, here] = slices[source][1, :, here]
+
+    def finish(act, d_pre):
+        for col in range(0, slab, columns):
+            here = slice(col, col + columns)
+            turned = matmul(d_pre, lows[:, here], TRANS_LHS).astype(jnp.bfloat16)
+            grad_dn[here, :] = turned.T
+            grad_upper[:, here] = matmul(act, grads[:, here], TRANS_LHS).astype(jnp.bfloat16)
+
+    @pl.when(core == 0)
+    def _():
+        finish(small[:, :rank], small[:, 2 * rank : 3 * rank])
+
+    @pl.when(core != 0)
+    def _():
+        finish(small[:, rank : 2 * rank], small[:, 3 * rank : 4 * rank])
+
+
+VMEM = pl.BlockSpec(memory_space=pltpu.VMEM)
+SMEM = pl.BlockSpec(memory_space=pltpu.SMEM)
+HBM = pl.BlockSpec(memory_space=pl.ANY)
+
+
+def call(kernel, name, in_specs, outs, scratch=()):
+    return pl.pallas_call(
+        kernel,
+        out_shape=tuple(jax.ShapeDtypeStruct(*out) for out in outs),
+        in_specs=in_specs,
+        out_specs=tuple(VMEM for _ in outs),
+        scratch_shapes=list(scratch),
+        compiler_params=pltpu.CompilerParams(vmem_limit_bytes=VMEM_LIMIT),
+        name=name,
+    )
+
+
+def across(block, axis, distance):
+    size = lax.axis_size(axis)
+    return lax.ppermute(block, axis, [(i, i ^ distance) for i in range(size)])
+
+
+def on_device_two_phases(hidden_in, cotangent, cluster_ids, w_down, w_up, gain):
+    experts = lax.axis_size("expert")
+    replicas = lax.axis_size("dp")
+    s_local, length, part = hidden_in.shape
+    width = 2 * part
+    capacity = 2 * s_local // experts
+    slots = experts * capacity
+    groups = 2 * experts
+    rows = slots * length // groups
+    tokens = experts * rows
+    own = (w_down[0, 0], w_up[0, 0], gain[0])
+    rank = own[0].shape[1]
+    slab = width // replicas
+    bf16, f32 = jnp.bfloat16, jnp.float32
+    sizes = (length, capacity, slots)
+    sections = ("expert", "segment")
+
+    other = tuple(across(array, "segment", 1) for array in own)
+    (send,) = call(
+        functools.partial(pack_kernel, *sizes),
+        "pack",
+        [SMEM, VMEM, VMEM],
+        [((groups, 2, rows, part), bf16)],
+    )(cluster_ids, hidden_in, cotangent)
+    recv = lax.all_to_all(send, sections, split_axis=0, concat_axis=0, tiled=True)
+    recv = recv.reshape(experts, 2, 2, rows, part)
+
+    def gathered(blocks):
+        near = [blocks[0]] + [across(blocks[step], "dp", step) for step in range(1, replicas)]
+        return near + [across(piece, "segment", 1) for piece in near]
+
+    slices = gathered(
+        call(slice_kernel, "slices", [VMEM], [((2, tokens, slab), bf16)] * replicas)(recv)
+    )
+    out, small = call(
+        chain_kernel,
+        "chain",
+        [VMEM] + [HBM] * 6,
+        [((experts, 2, rows, part), bf16), ((tokens, 4 * rank + 128), bf16)],
+        [
+            pltpu.VMEM((2, width, rank), bf16),
+            pltpu.VMEM((2, rank, width), bf16),
+            pltpu.VMEM((2, 1, width), bf16),
+            pltpu.VMEM((tokens, width), bf16),
+            pltpu.VMEM((tokens, width), bf16),
+            pltpu.VMEM((tokens, width), f32),
+            pltpu.SemaphoreType.DMA((2, 3)),
+        ],
+    )(recv, *own, *other)
+    smalls = gathered([small] * replicas)
+
+    back = lax.all_to_all(
+        out.reshape(groups, rows, part), sections, split_axis=0, concat_axis=0, tiled=True
+    )
+    (out_hidden,) = call(
+        functools.partial(unpack_kernel, *sizes),
+        "unpack",
+        [SMEM, VMEM],
+        [(hidden_in.shape, bf16)],
+    )(cluster_ids, back)
+
+    sources = 2 * replicas
+    all_tokens = sources * tokens
+    grad_dn, grad_upper = call(
+        functools.partial(gradient_kernel, sources),
+        "gradients",
+        [VMEM] * (2 * sources) + [HBM] * 6,
+        [((slab, rank), bf16), ((rank, slab), bf16)],
+        [
+            pltpu.VMEM((slab, rank), bf16),
+            pltpu.VMEM((rank, slab), bf16),
+            pltpu.VMEM((2, 1, slab), bf16),
+            pltpu.VMEM((all_tokens, 4 * rank + 128), bf16),
+            pltpu.VMEM((all_tokens, 6 * 128), f32),
+            pltpu.VMEM((all_tokens, slab), bf16),
+            pltpu.VMEM((all_tokens, slab), bf16),
+            pltpu.VMEM((all_tokens, 256), f32),
+            pltpu.VMEM((all_tokens, 256), f32),
+            pltpu.SemaphoreType.DMA((4,)),
+        ],
+    )(*slices, *smalls, *own, *other)
+    return (out_hidden, grad_dn[None, None], grad_upper[None, None])
+
+
 def solution(mesh):
+    two = dict(mesh.shape) == {"expert": 4, "dp": 4, "segment": 2}
+    on_device = on_device_two_phases if two else on_device_pipelined
     return jax.shard_map(
         on_device,
         mesh=mesh,

time: 276 us -> 84.4 us (0.31)
  waiting for transfers between devices: 88.3 us -> 19.3 us
  other arithmetic: 45.8 us -> 0 us
  local copies, waits for them, and re-layouts: 42.1 us -> 4.06 us
  matrix products: 37.2 us -> 0 us
  Pallas kernels: 0 us -> 24.1 us
  between operations: 15.6 us -> 0.87 us
  starting transfers between devices: 26.6 us -> 15.1 us
    reduce_scatter x2 -> x0, waiting for transfers between devices: 72.1 us -> none  [the longest x1 45.5 us: on_device(): lax.psum_scatter(grad_upper.astype(jnp.bfloat16), 'dp', scatter_dimension...]
    dot_general x25 -> x0, matrix products: 37.2 us -> none  [the longest x5 14.6 us: phase_backward(): d_act = jnp.dot(grad_in, w_upper.T, preferred_element_type=jnp.float32)]
    dynamic_update_slice x20 -> x0, other arithmetic: 31.6 us -> none  [put_slot(): lax.dynamic_update_index_in_dim(buffer, jnp.where(valid, value, old_value...]
    pallas_call x0 -> x5, Pallas kernels: none -> 24.1 us  [the longest x1 9.62 us: on_device_two_phases(): call(chain_kernel, 'chain', [VMEM] + [HBM] * 6, [((experts, 2, rows, part...]
    dynamic_slice x21 -> x0, local copies, waits for them, and re-layouts: 16.6 us -> none  [the longest x20 15.4 us: put_slot(): old_value = lax.dynamic_index_in_dim(buffer, slot, 0, keepdims=False)]
    ppermute x10 -> x17, waiting for transfers between devices: 6.69 us -> 19.3 us  [across(): return lax.ppermute(block, axis, [(i, i ^ distance) for i in range(size)])]
    reshape x6 -> x0, local copies, waits for them, and re-layouts: 9.58 us -> none  [the longest x2 3.18 us: to_slots(): return moved.reshape((slots,) + local.shape[1:])]
    all_to_all x2 -> x1, waiting for transfers between devices: 9.41 us -> 0.01 us  [on_device_two_phases(): lax.all_to_all(out.reshape(groups, rows, part), sections, split_axis=0, c...]
  transfers between devices with their start and end apart: 15 -> 18, of which waited for: 8 -> 6; matrix products, arithmetic and copies ran while one was open for 41% -> 0% of each run, Pallas kernels for 0% -> 26%
where the time goes in v3:
time: 84.4 us; the launch traced here: 84 us
  Pallas kernels  24.1 us (29%)
  blocking collectives  20.6 us (24%)
  waiting for transfers between devices  19.3 us (23%)
  starting transfers between devices  15.1 us (18%)
  local copies, waits for them, and re-layouts  4.06 us (5%)
  between operations  0.87 us (1%)
    all_to_all x1, blocking collectives, on_device_two_phases(): lax.all_to_all(send, sections, split_axis=0, concat_axis=0, tiled=True)  20.6 us
    ppermute x17, waiting for transfers between devices, across(): return lax.ppermute(block, axis, [(i, i ^ distance) for i in range(size)])  19.3 us
    ppermute x17, starting transfers between devices, across(): return lax.ppermute(block, axis, [(i, i ^ distance) for i in range(size)])  11.6 us
    pallas_call x1, Pallas kernels, on_device_two_phases(): call(chain_kernel, 'chain', [VMEM] + [HBM] * 6, [((experts, 2, rows, part...  9.62 us
    pallas_call x1, Pallas kernels, on_device_two_phases(): call(functools.partial(gradient_kernel, sources), 'gradients', [VMEM] * (...  7.51 us
    unnamed x38, local copies, waits for them, and re-layouts  4.06 us
    all_to_all x1, starting transfers between devices, on_device_two_phases(): lax.all_to_all(out.reshape(groups, rows, part), sections, split_axis=0, c...  3.5 us
    pallas_call x1, Pallas kernels, on_device_two_phases(): call(functools.partial(pack_kernel, *sizes), 'pack', [SMEM, VMEM, VMEM],...  2.57 us
  transfers between devices with their start and end apart: 18, of which 6 were waited for; matrix products, arithmetic and copies ran while one was open for 0% of the time, Pallas kernels for 26%

profile of v3, /device:TPU:0, one launch (start us, length us, event | category | flops | bytes accessed | tf_op | source)
XLA Modules:
  0.0 84.0 jit_solution(16848155067752520335)
XLA Ops:
  0.6 0.5 collective-permute-start
  1.2 0.1 collective-permute-start.1
  1.2 2.6 %pack.1 = bf16[8,2,16,2048]{3,2,1,0:T(8,128)(2,1)} custom-call(s32[16]{0:T(128)} %ids.3, bf16[16,4,2048]{2,1,0:T(4,128)(2,1)} %hidden.1, bf16[16,4,2048]{2,1,0:T(4,128)(2,1)} %cot.1), custom_call_target="tpu_custom_call" | custom-call | tf_op jit(solution)/shard_map/pack/pallas_call | solution.py:540
  3.8 20.6 %all_to_all.10 = bf16[8,2,16,2048]{3,2,1,0:T(8,128)(2,1)} all-to-all(bf16[8,2,16,2048]{3,2,1,0:T(8,128)(2,1)} %pack.1), channel_id=1, replica_groups=mesh['expert'=4,'dp'=4,'segment'=2] {'expert','segment'}, dimensions={0} | all-to-all | bytes 2097152 | tf_op jit(solution)/shard_map/all_to_all | solution.py:546
  24.4 2.3 %slices.1 = (bf16[2,64,1024]{2,1,0:T(8,128)(2,1)}, bf16[2,64,1024]{2,1,0:T(8,128)(2,1)}, bf16[2,64,1024]{2,1,0:T(8,128)(2,1)}, bf16[2,64,1024]{2,1,0:T(8,128)(2,1)}) custom-call(bf16[4,2,2,16,2048]{4,3,2,1,0:T(8,128)(2,1)} %bitcast.7), custom_call_target="tpu_custom_call" | custom-call | tf_op jit(solution)/shard_map/slices/pallas_call | solution.py:554
  26.7 2.0 %collective-permute-start.3 = (bf16[2,64,1024]{2,1,0:T(8,128)(2,1)}, bf16[2,64,1024]{2,1,0:T(8,128)(2,1)S(1)}, u32[]{:S(2)}, u32[]{:S(2)}) collective-permute-start(bf16[2,64,1024]{2,1,0:T(8,128)(2,1)} %get-tuple-element.13), channel_id=1, source_target_pairs={{0,2},{2,0},{4,6},{6,4},{1,3},{3,1},{5,7},{7,5},{8,10},{10,8},{12,... | collective-permute-start | bytes 786440 | tf_op jit(solution)/shard_map/ppermute | solution.py:519
  28.6 2.6 %collective-permute-start.4 = (bf16[2,64,1024]{2,1,0:T(8,128)(2,1)}, bf16[2,64,1024]{2,1,0:T(8,128)(2,1)S(1)}, u32[]{:S(2)}, u32[]{:S(2)}) collective-permute-start(bf16[2,64,1024]{2,1,0:T(8,128)(2,1)} %get-tuple-element.14), channel_id=1, source_target_pairs={{0,4},{2,6},{4,0},{6,2},{1,5},{3,7},{5,1},{7,3},{8,12},{10,14},{12... | collective-permute-start | bytes 786440 | tf_op jit(solution)/shard_map/ppermute | solution.py:519
  31.3 0.0 collective-permute-start.2
  31.3 1.2 %collective-permute-done.2.other_gain.refs_21_ = bf16[1,4096]{1,0:T(2,128)(2,1)S(1)} collective-permute-done((bf16[1,4096]{1,0:T(2,128)(2,1)S(1)}, bf16[1,4096]{1,0:T(2,128)(2,1)S(1)}, u32[]{:S(2)}, u32[]{:S(2)}) %collective-permute-start.2) | collective-permute-done | bytes 8224 | tf_op jit(solution)/shard_map/ppermute | solution.py:519
  32.4 0.0 collective-permute-start.5
  32.4 6.7 %collective-permute-done.3.refs_1_ = bf16[2,64,1024]{2,1,0:T(8,128)(2,1)S(1)} collective-permute-done((bf16[2,64,1024]{2,1,0:T(8,128)(2,1)}, bf16[2,64,1024]{2,1,0:T(8,128)(2,1)S(1)}, u32[]{:S(2)}, u32[]{:S(2)}) %collective-permute-start.3) | collective-permute-done | bytes 262176 | tf_op jit(solution)/shard_map/ppermute | solution.py:519
  39.2 0.0 collective-permute-start.6
  39.2 0.0 collective-permute-done.other_dn.refs_19_
  39.2 0.5 collective-permute-start.7
  39.7 0.9 %copy-done = bf16[4096,256]{1,0:T(8,128)(2,1)} copy-done((bf16[4096,256]{1,0:T(8,128)(2,1)}, bf16[4096,256]{1,0:T(8,128)(2,1)S(1)}, u32[]{:S(2)}) %copy-start) | copy-done | bytes 2097176
  40.6 1.3 %copy-done.1 = bf16[256,4096]{1,0:T(8,128)(2,1)} copy-done((bf16[256,4096]{1,0:T(8,128)(2,1)}, bf16[256,4096]{1,0:T(8,128)(2,1)S(1)}, u32[]{:S(2)}) %copy-start.1) | copy-done | bytes 2097176
  41.9 9.6 %chain.1 = (bf16[4,2,16,2048]{3,2,1,0:T(8,128)(2,1)}, bf16[64,1152]{1,0:T(8,128)(2,1)}) custom-call(bf16[4,2,2,16,2048]{4,3,2,1,0:T(8,128)(2,1)} %bitcast.8, bf16[4096,256]{1,0:T(8,128)(2,1)} %bitcast.10, bf16[256,4096]{1,0:T(8,128)(2,1)} %bitcast.13, bf16[1,4096]{1,0:T(2,128)(2,1)} %bitcast.16, bf16[4096,256]{1,0:T(8,128)(2,1)} %copy-done, ...), custom_call_target="tpu_custom_call" | custom-call | tf_op jit(solution)/shard_map/chain/pallas_call | solution.py:556
  51.5 3.5 %all-to-all-start.1 = ((bf16[8,16,2048]{2,1,0:T(8,128)(2,1)}), bf16[8,16,2048]{2,1,0:T(8,128)(2,1)S(1)}, u32[]{:S(2)}, u32[]{:S(2)}) async-start(bf16[8,16,2048]{2,1,0:T(8,128)(2,1)} %bitcast.15), calls=%async_computation.1 | async-start | bytes 1048576 | tf_op jit(solution)/shard_map/all_to_all | solution.py:573
  55.1 0.6 collective-permute-start.8
  55.6 3.4 %collective-permute-start.12 = (bf16[64,1152]{1,0:T(8,128)(2,1)}, bf16[64,1152]{1,0:T(8,128)(2,1)S(1)}, u32[]{:S(2)}, u32[]{:S(2)}) collective-permute-start(bf16[64,1152]{1,0:T(8,128)(2,1)} %get-tuple-element.16.refs_8_), channel_id=1, source_target_pairs={{0,6},{2,4},{4,2},{6,0},{1,7},{3,5},{5,3},{7,1},{8,14},{10,12},{12... | collective-permute-start | bytes 442376 | tf_op jit(solution)/shard_map/ppermute | solution.py:519
  59.1 1.0 %collective-permute-start.10 = (bf16[64,1152]{1,0:T(8,128)(2,1)}, bf16[64,1152]{1,0:T(8,128)(2,1)S(1)}, u32[]{:S(2)}, u32[]{:S(2)}) collective-permute-start(bf16[64,1152]{1,0:T(8,128)(2,1)} %get-tuple-element.16.refs_8_), channel_id=1, source_target_pairs={{0,2},{2,0},{4,6},{6,4},{1,3},{3,1},{5,7},{7,5},{8,10},{10,8},{12,... | collective-permute-start | bytes 442376 | tf_op jit(solution)/shard_map/ppermute | solution.py:519
  60.1 0.5 collective-permute-start.13
  60.5 3.9 %collective-permute-done.12.refs_11_ = bf16[64,1152]{1,0:T(8,128)(2,1)S(1)} collective-permute-done((bf16[64,1152]{1,0:T(8,128)(2,1)}, bf16[64,1152]{1,0:T(8,128)(2,1)S(1)}, u32[]{:S(2)}, u32[]{:S(2)}) %collective-permute-start.12) | collective-permute-done | bytes 147488 | tf_op jit(solution)/shard_map/ppermute | solution.py:519
  64.4 6.4 %collective-permute-done.11.refs_10_ = bf16[64,1152]{1,0:T(8,128)(2,1)S(1)} collective-permute-done((bf16[64,1152]{1,0:T(8,128)(2,1)}, bf16[64,1152]{1,0:T(8,128)(2,1)S(1)}, u32[]{:S(2)}, u32[]{:S(2)}) %collective-permute-start.11) | collective-permute-done | bytes 147488 | tf_op jit(solution)/shard_map/ppermute | solution.py:519
  70.9 0.5 collective-permute-start.14
  71.4 0.8 collective-permute-done.15.refs_14_
  72.2 0.2 collective-permute-done.14.refs_13_
  72.5 0.3 copy-done.15
  72.9 0.7 copy-done.16
  73.5 7.5 %gradients.1 = (bf16[1024,256]{1,0:T(8,128)(2,1)}, bf16[256,1024]{1,0:T(8,128)(2,1)}) custom-call(bf16[2,64,1024]{2,1,0:T(8,128)(2,1)} %get-tuple-element.12.refs_0_, bf16[2,64,1024]{2,1,0:T(8,128)(2,1)} %copy-done.3, bf16[2,64,1024]{2,1,0:T(8,128)(2,1)} %copy-done.4, bf16[2,64,1024]{2,1,0:T(8,128)(2,1)} %copy-done.5, bf16[2,64,1024]{2,1,0:T(8,128)(2,1)} %copy-done.6, ...), custom_call_target="tpu_custom_call" | custom-call | tf_op jit(solution)/shard_map/gradients/pallas_call | solution.py:585
  81.1 0.8 copy-done.2
  81.9 2.2 %unpack.1 = bf16[16,4,2048]{2,1,0:T(4,128)(2,1)} custom-call(s32[16]{0:T(128)} %ids.3, bf16[8,16,2048]{2,1,0:T(8,128)(2,1)} %copy-done.2), custom_call_target="tpu_custom_call" | custom-call | tf_op jit(solution)/shard_map/unpack/pallas_call | solution.py:576
  (48 shorter events, 0.1 us)
Async XLA Ops:
  0.6 38.6 %collective-permute-start = (bf16[4096,256]{1,0:T(8,128)(2,1)}, bf16[4096,256]{1,0:T(8,128)(2,1)S(1)}, u32[]{:S(2)}, u32[]{:S(2)}) collective-permute-start(bf16[4096,256]{1,0:T(8,128)(2,1)} %bitcast.9), channel_id=1, source_target_pairs={{0,1},{1,0},{2,3},{3,2},{4,5},{5,4},{6,7},{7,6},{8,9},{9,8},{10,11... | collective-permute-start | bytes 6291464 | tf_op jit(solution)/shard_map/ppermute | solution.py:519
  1.1 30.1 %copy-start.17 = (bf16[1,1,4096]{2,1,0:T(2,128)(2,1)S(1)}, bf16[1,1,4096]{2,1,0:T(2,128)(2,1)}, u32[]{:S(2)}) copy-start(bf16[1,1,4096]{2,1,0:T(2,128)(2,1)} %param.11) | copy-start | bytes 24580
  1.2 38.6 %collective-permute-start.1 = (bf16[256,4096]{1,0:T(8,128)(2,1)}, bf16[256,4096]{1,0:T(8,128)(2,1)S(1)}, u32[]{:S(2)}, u32[]{:S(2)}) collective-permute-start(bf16[256,4096]{1,0:T(8,128)(2,1)} %bitcast.12), channel_id=1, source_target_pairs={{0,1},{1,0},{2,3},{3,2},{4,5},{5,4},{6,7},{7,6},{8,9},{9,8},{10,11... | collective-permute-start | bytes 6291464 | tf_op jit(solution)/shard_map/ppermute | solution.py:519
  26.7 12.5 %collective-permute-start.3 = (bf16[2,64,1024]{2,1,0:T(8,128)(2,1)}, bf16[2,64,1024]{2,1,0:T(8,128)(2,1)S(1)}, u32[]{:S(2)}, u32[]{:S(2)}) collective-permute-start(bf16[2,64,1024]{2,1,0:T(8,128)(2,1)} %get-tuple-element.13), channel_id=1, source_target_pairs={{0,2},{2,0},{4,6},{6,4},{1,3},{3,1},{5,7},{7,5},{8,10},{10,8},{12,... | collective-permute-start | bytes 786440 | tf_op jit(solution)/shard_map/ppermute | solution.py:519
  28.6 26.4 %collective-permute-start.4 = (bf16[2,64,1024]{2,1,0:T(8,128)(2,1)}, bf16[2,64,1024]{2,1,0:T(8,128)(2,1)S(1)}, u32[]{:S(2)}, u32[]{:S(2)}) collective-permute-start(bf16[2,64,1024]{2,1,0:T(8,128)(2,1)} %get-tuple-element.14), channel_id=1, source_target_pairs={{0,4},{2,6},{4,0},{6,2},{1,5},{3,7},{5,1},{7,3},{8,12},{10,14},{12... | collective-permute-start | bytes 786440 | tf_op jit(solution)/shard_map/ppermute | solution.py:519
  31.3 1.2 %collective-permute-start.2 = (bf16[1,4096]{1,0:T(2,128)(2,1)S(1)}, bf16[1,4096]{1,0:T(2,128)(2,1)S(1)}, u32[]{:S(2)}, u32[]{:S(2)}) collective-permute-start(bf16[1,4096]{1,0:T(2,128)(2,1)S(1)} %bitcast.18), channel_id=1, source_target_pairs={{0,1},{1,0},{2,3},{3,2},{4,5},{5,4},{6,7},{7,6},{8,9},{9,8},{10,11... | collective-permute-start | bytes 24584 | tf_op jit(solution)/shard_map/ppermute | solution.py:519
  32.4 7.3 %copy-start.18 = (bf16[1,4096]{1,0:T(2,128)(2,1)}, bf16[1,4096]{1,0:T(2,128)(2,1)S(1)}, u32[]{:S(2)}) copy-start(bf16[1,4096]{1,0:T(2,128)(2,1)S(1)} %collective-permute-done.2.other_gain.refs_21_) | copy-start | bytes 24580
  32.4 26.6 %collective-permute-start.5 = (bf16[2,64,1024]{2,1,0:T(8,128)(2,1)}, bf16[2,64,1024]{2,1,0:T(8,128)(2,1)S(1)}, u32[]{:S(2)}, u32[]{:S(2)}) collective-permute-start(bf16[2,64,1024]{2,1,0:T(8,128)(2,1)} %get-tuple-element.15), channel_id=1, source_target_pairs={{0,6},{2,4},{4,2},{6,0},{1,7},{3,5},{5,3},{7,1},{8,14},{10,12},{12... | collective-permute-start | bytes 786440 | tf_op jit(solution)/shard_map/ppermute | solution.py:519
  39.2 33.3 %copy-start.3 = (bf16[2,64,1024]{2,1,0:T(8,128)(2,1)}, bf16[2,64,1024]{2,1,0:T(8,128)(2,1)S(1)}, u32[]{:S(2)}) copy-start(bf16[2,64,1024]{2,1,0:T(8,128)(2,1)S(1)} %collective-permute-done.3.refs_1_) | copy-start | bytes 786436
  39.2 19.9 %collective-permute-start.6 = (bf16[2,64,1024]{2,1,0:T(8,128)(2,1)}, bf16[2,64,1024]{2,1,0:T(8,128)(2,1)S(1)}, u32[]{:S(2)}, u32[]{:S(2)}) collective-permute-start(bf16[2,64,1024]{2,1,0:T(8,128)(2,1)} %get-tuple-element.12.refs_0_), channel_id=1, source_target_pairs={{0,1},{1,0},{2,3},{3,2},{4,5},{5,4},{6,7},{7,6},{8,9},{9,8},{10,11... | collective-permute-start | bytes 786440 | tf_op jit(solution)/shard_map/ppermute | solution.py:519
  39.2 1.4 %copy-start = (bf16[4096,256]{1,0:T(8,128)(2,1)}, bf16[4096,256]{1,0:T(8,128)(2,1)S(1)}, u32[]{:S(2)}) copy-start(bf16[4096,256]{1,0:T(8,128)(2,1)S(1)} %collective-permute-done.other_dn.refs_19_) | copy-start | bytes 6291460
  39.2 20.8 %collective-permute-start.7 = (bf16[2,64,1024]{2,1,0:T(8,128)(2,1)S(1)}, bf16[2,64,1024]{2,1,0:T(8,128)(2,1)S(1)}, u32[]{:S(2)}, u32[]{:S(2)}) collective-permute-start(bf16[2,64,1024]{2,1,0:T(8,128)(2,1)S(1)} %collective-permute-done.3.refs_1_), channel_id=1, source_target_pairs={{0,1},{1,0},{2,3},{3,2},{4,5},{5,4},{6,7},{7,6},{8,9},{9,8},{10,11... | collective-permute-start | bytes 786440 | tf_op jit(solution)/shard_map/ppermute | solution.py:519
  40.6 1.3 %copy-start.1 = (bf16[256,4096]{1,0:T(8,128)(2,1)}, bf16[256,4096]{1,0:T(8,128)(2,1)S(1)}, u32[]{:S(2)}) copy-start(bf16[256,4096]{1,0:T(8,128)(2,1)S(1)} %collective-permute-done.1.other_up.refs_20_) | copy-start | bytes 6291460
  51.5 29.5 %all-to-all-start.1 = ((bf16[8,16,2048]{2,1,0:T(8,128)(2,1)}), bf16[8,16,2048]{2,1,0:T(8,128)(2,1)S(1)}, u32[]{:S(2)}, u32[]{:S(2)}) async-start(bf16[8,16,2048]{2,1,0:T(8,128)(2,1)} %bitcast.15), calls=%async_computation.1 | async-start | bytes 1048576 | tf_op jit(solution)/shard_map/all_to_all | solution.py:573
  55.1 17.4 %copy-start.4 = (bf16[2,64,1024]{2,1,0:T(8,128)(2,1)}, bf16[2,64,1024]{2,1,0:T(8,128)(2,1)S(1)}, u32[]{:S(2)}) copy-start(bf16[2,64,1024]{2,1,0:T(8,128)(2,1)S(1)} %collective-permute-done.4.refs_2_) | copy-start | bytes 786436
  55.1 5.0 %collective-permute-start.8 = (bf16[2,64,1024]{2,1,0:T(8,128)(2,1)S(1)}, bf16[2,64,1024]{2,1,0:T(8,128)(2,1)S(1)}, u32[]{:S(2)}, u32[]{:S(2)}) collective-permute-start(bf16[2,64,1024]{2,1,0:T(8,128)(2,1)S(1)} %collective-permute-done.4.refs_2_), channel_id=1, source_target_pairs={{0,1},{1,0},{2,3},{3,2},{4,5},{5,4},{6,7},{7,6},{8,9},{9,8},{10,11... | collective-permute-start | bytes 786440 | tf_op jit(solution)/shard_map/ppermute | solution.py:519
  55.6 8.8 %collective-permute-start.12 = (bf16[64,1152]{1,0:T(8,128)(2,1)}, bf16[64,1152]{1,0:T(8,128)(2,1)S(1)}, u32[]{:S(2)}, u32[]{:S(2)}) collective-permute-start(bf16[64,1152]{1,0:T(8,128)(2,1)} %get-tuple-element.16.refs_8_), channel_id=1, source_target_pairs={{0,6},{2,4},{4,2},{6,0},{1,7},{3,5},{5,3},{7,1},{8,14},{10,12},{12... | collective-permute-start | bytes 442376 | tf_op jit(solution)/shard_map/ppermute | solution.py:519
  59.0 13.4 %copy-start.5 = (bf16[2,64,1024]{2,1,0:T(8,128)(2,1)}, bf16[2,64,1024]{2,1,0:T(8,128)(2,1)S(1)}, u32[]{:S(2)}) copy-start(bf16[2,64,1024]{2,1,0:T(8,128)(2,1)S(1)} %collective-permute-done.5.refs_3_) | copy-start | bytes 786436
  59.0 11.8 %collective-permute-start.11 = (bf16[64,1152]{1,0:T(8,128)(2,1)}, bf16[64,1152]{1,0:T(8,128)(2,1)S(1)}, u32[]{:S(2)}, u32[]{:S(2)}) collective-permute-start(bf16[64,1152]{1,0:T(8,128)(2,1)} %get-tuple-element.16.refs_8_), channel_id=1, source_target_pairs={{0,4},{2,6},{4,0},{6,2},{1,5},{3,7},{5,1},{7,3},{8,12},{10,14},{12... | collective-permute-start | bytes 442376 | tf_op jit(solution)/shard_map/ppermute | solution.py:519
  59.0 13.4 %copy-start.6 = (bf16[2,64,1024]{2,1,0:T(8,128)(2,1)}, bf16[2,64,1024]{2,1,0:T(8,128)(2,1)S(1)}, u32[]{:S(2)}) copy-start(bf16[2,64,1024]{2,1,0:T(8,128)(2,1)S(1)} %collective-permute-done.6.refs_4_) | copy-start | bytes 786436
  59.1 11.8 %collective-permute-start.10 = (bf16[64,1152]{1,0:T(8,128)(2,1)}, bf16[64,1152]{1,0:T(8,128)(2,1)S(1)}, u32[]{:S(2)}, u32[]{:S(2)}) collective-permute-start(bf16[64,1152]{1,0:T(8,128)(2,1)} %get-tuple-element.16.refs_8_), channel_id=1, source_target_pairs={{0,2},{2,0},{4,6},{6,4},{1,3},{3,1},{5,7},{7,5},{8,10},{10,8},{12,... | collective-permute-start | bytes 442376 | tf_op jit(solution)/shard_map/ppermute | solution.py:519
  60.0 12.4 %copy-start.7 = (bf16[2,64,1024]{2,1,0:T(8,128)(2,1)}, bf16[2,64,1024]{2,1,0:T(8,128)(2,1)S(1)}, u32[]{:S(2)}) copy-start(bf16[2,64,1024]{2,1,0:T(8,128)(2,1)S(1)} %collective-permute-done.7.refs_5_) | copy-start | bytes 786436
  60.0 11.3 %collective-permute-start.9 = (bf16[2,64,1024]{2,1,0:T(8,128)(2,1)S(1)}, bf16[2,64,1024]{2,1,0:T(8,128)(2,1)S(1)}, u32[]{:S(2)}, u32[]{:S(2)}) collective-permute-start(bf16[2,64,1024]{2,1,0:T(8,128)(2,1)S(1)} %collective-permute-done.5.refs_3_), channel_id=1, source_target_pairs={{0,1},{1,0},{2,3},{3,2},{4,5},{5,4},{6,7},{7,6},{8,9},{9,8},{10,11... | collective-permute-start | bytes 786440 | tf_op jit(solution)/shard_map/ppermute | solution.py:519
  60.0 12.4 %copy-start.8 = (bf16[2,64,1024]{2,1,0:T(8,128)(2,1)}, bf16[2,64,1024]{2,1,0:T(8,128)(2,1)S(1)}, u32[]{:S(2)}) copy-start(bf16[2,64,1024]{2,1,0:T(8,128)(2,1)S(1)} %collective-permute-done.8.refs_6_) | copy-start | bytes 786436
  60.1 11.3 %collective-permute-start.13 = (bf16[64,1152]{1,0:T(8,128)(2,1)}, bf16[64,1152]{1,0:T(8,128)(2,1)S(1)}, u32[]{:S(2)}, u32[]{:S(2)}) collective-permute-start(bf16[64,1152]{1,0:T(8,128)(2,1)} %get-tuple-element.16.refs_8_), channel_id=1, source_target_pairs={{0,1},{1,0},{2,3},{3,2},{4,5},{5,4},{6,7},{7,6},{8,9},{9,8},{10,11... | collective-permute-start | bytes 442376 | tf_op jit(solution)/shard_map/ppermute | solution.py:519
  64.4 8.0 %copy-start.10 = (bf16[64,1152]{1,0:T(8,128)(2,1)}, bf16[64,1152]{1,0:T(8,128)(2,1)S(1)}, u32[]{:S(2)}) copy-start(bf16[64,1152]{1,0:T(8,128)(2,1)S(1)} %collective-permute-done.12.refs_11_) | copy-start | bytes 442372
  64.4 6.9 %collective-permute-start.16 = (bf16[64,1152]{1,0:T(8,128)(2,1)S(1)}, bf16[64,1152]{1,0:T(8,128)(2,1)S(1)}, u32[]{:S(2)}, u32[]{:S(2)}) collective-permute-start(bf16[64,1152]{1,0:T(8,128)(2,1)S(1)} %collective-permute-done.12.refs_11_), channel_id=1, source_target_pairs={{0,1},{1,0},{2,3},{3,2},{4,5},{5,4},{6,7},{7,6},{8,9},{9,8},{10,11... | collective-permute-start | bytes 442376 | tf_op jit(solution)/shard_map/ppermute | solution.py:519
  70.8 1.6 %copy-start.11 = (bf16[64,1152]{1,0:T(8,128)(2,1)}, bf16[64,1152]{1,0:T(8,128)(2,1)S(1)}, u32[]{:S(2)}) copy-start(bf16[64,1152]{1,0:T(8,128)(2,1)S(1)} %collective-permute-done.11.refs_10_) | copy-start | bytes 442372
  70.8 1.4 %collective-permute-start.15 = (bf16[64,1152]{1,0:T(8,128)(2,1)S(1)}, bf16[64,1152]{1,0:T(8,128)(2,1)S(1)}, u32[]{:S(2)}, u32[]{:S(2)}) collective-permute-start(bf16[64,1152]{1,0:T(8,128)(2,1)S(1)} %collective-permute-done.11.refs_10_), channel_id=1, source_target_pairs={{0,1},{1,0},{2,3},{3,2},{4,5},{5,4},{6,7},{7,6},{8,9},{9,8},{10,11... | collective-permute-start | bytes 442376 | tf_op jit(solution)/shard_map/ppermute | solution.py:519
  70.9 1.6 %copy-start.12 = (bf16[64,1152]{1,0:T(8,128)(2,1)}, bf16[64,1152]{1,0:T(8,128)(2,1)S(1)}, u32[]{:S(2)}) copy-start(bf16[64,1152]{1,0:T(8,128)(2,1)S(1)} %collective-permute-done.10.refs_9_) | copy-start | bytes 442372
  70.9 1.6 %collective-permute-start.14 = (bf16[64,1152]{1,0:T(8,128)(2,1)S(1)}, bf16[64,1152]{1,0:T(8,128)(2,1)S(1)}, u32[]{:S(2)}, u32[]{:S(2)}) collective-permute-start(bf16[64,1152]{1,0:T(8,128)(2,1)S(1)} %collective-permute-done.10.refs_9_), channel_id=1, source_target_pairs={{0,1},{1,0},{2,3},{3,2},{4,5},{5,4},{6,7},{7,6},{8,9},{9,8},{10,11... | collective-permute-start | bytes 442376 | tf_op jit(solution)/shard_map/ppermute | solution.py:519
  71.4 1.1 %copy-start.13 = (bf16[64,1152]{1,0:T(8,128)(2,1)}, bf16[64,1152]{1,0:T(8,128)(2,1)S(1)}, u32[]{:S(2)}) copy-start(bf16[64,1152]{1,0:T(8,128)(2,1)S(1)} %collective-permute-done.13.refs_12_) | copy-start | bytes 442372
  (5 other events, 4.4 us)

commit v4 on v3

--- a/solution.py
+++ b/solution.py
@@ -192,7 +192,7 @@
 
 
 CHUNK = 512
-VMEM_LIMIT = 56 * 1024 * 1024
+MIB = 1024 * 1024
 TRANS_RHS = (((1,), (1,)), ((), ()))
 TRANS_LHS = (((0,), (0,)), ((), ()))
 
@@ -234,7 +234,7 @@
             send[group, which] = moved[group * rows : (group + 1) * rows]
 
 
-def slice_kernel(recv, *outs):
+def slice_kernel(recv, _dn, _up, _gain, *outs):
     experts, _, _, rows, part = recv.shape
     slab = outs[0].shape[2]
     place = lax.axis_index("dp")
@@ -288,8 +288,8 @@
 
 def chain_kernel(
     recv, own_dn, own_up, own_gain, other_dn, other_up, other_gain,
-    out, small,
-    dn_buf, up_buf, gain_buf, entering, middle, d_norms, sems,
+    small, middle,
+    dn_buf, up_buf, gain_buf, entering, d_norms, sems,
 ):
     phase = lax.axis_index("segment")
     experts, phases, _, rows, part = recv.shape
@@ -304,14 +304,15 @@
             for which, (source, buffer) in enumerate(zip(sources, (dn_buf, up_buf, gain_buf)))
         ]
 
-    for this in range(2):
-
-        @pl.when(phase == this)
-        def _():
-            for at in range(2):
+    def fetch(at):
+        for this in range(2):
+
+            @pl.when(phase == this)
+            def _():
                 for copy in copies(own if at == this else other, at):
                     copy.start()
 
+    fetch(0)
     waits = [copies(own, at) for at in range(2)]
     cols = range(0, width, CHUNK)
 
@@ -346,6 +347,7 @@
     inverse_0 = inverse_of(entering, mean_0)
     waits[0][0].wait()
     waits[0][2].wait()
+    fetch(1)
     pre_0 = down(entering, mean_0, inverse_0, 0)
     act_0 = gelu_value(pre_0).astype(jnp.bfloat16)
     slope_0 = gelu_slope(pre_0)
@@ -379,10 +381,6 @@
         d_norms[:, here] = d_norm
         total = total + lanes(d_norm)
         cross = cross + lanes(d_norm * ((wide - mean_1) * inverse_1))
-        leaving = (wide + matmul(act_1, up_buf[1, :, here])).astype(jnp.bfloat16)
-        half, start = col // part, col % part
-        for e in range(experts):
-            out[e, half, :, start : start + CHUNK] = leaving[e * rows : (e + 1) * rows]
     shift = row_sum(total) / width
     along = row_sum(cross) / width
     d_act = jnp.zeros((tokens, rank), jnp.float32)
@@ -400,10 +398,35 @@
     small[:, 4 * rank :] = side_by_side(moments, tokens)
 
 
+def result_kernel(middle, small, own_up, other_up, out, up_buf, sem):
+    phase = lax.axis_index("segment")
+    experts, _, rows, part = out.shape
+    rank, width = up_buf.shape
+    copies = [pltpu.make_async_copy(source, up_buf, sem) for source in (own_up, other_up)]
+
+    @pl.when(phase == 1)
+    def _():
+        copies[0].start()
+
+    @pl.when(phase != 1)
+    def _():
+        copies[1].start()
+
+    copies[0].wait()
+    act = small[:, rank : 2 * rank]
+    for col in range(0, width, CHUNK):
+        here = slice(col, col + CHUNK)
+        leaving = middle[:, here].astype(jnp.float32) + matmul(act, up_buf[:, here])
+        leaving = leaving.astype(jnp.bfloat16)
+        half, start = col // part, col % part
+        for e in range(experts):
+            out[e, half, :, start : start + CHUNK] = leaving[e * rows : (e + 1) * rows]
+
+
 def gradient_kernel(sources, *refs):
     slices, refs = refs[:sources], refs[sources:]
     smalls, refs = refs[:sources], refs[sources:]
-    own, other, refs = refs[:3], refs[3:6], refs[6:]
+    own, other, refs = refs[:3], refs[3:6], refs[7:]
     (grad_dn, grad_upper, dn_buf, up_buf, gain_buf, small, moments, lows, grads, ups, downs,
      sems) = refs
     core = lax.axis_index("segment")
@@ -502,14 +525,14 @@
 HBM = pl.BlockSpec(memory_space=pl.ANY)
 
 
-def call(kernel, name, in_specs, outs, scratch=()):
+def call(kernel, name, grant, in_specs, outs, scratch=()):
     return pl.pallas_call(
         kernel,
         out_shape=tuple(jax.ShapeDtypeStruct(*out) for out in outs),
         in_specs=in_specs,
         out_specs=tuple(VMEM for _ in outs),
         scratch_shapes=list(scratch),
-        compiler_params=pltpu.CompilerParams(vmem_limit_bytes=VMEM_LIMIT),
+        compiler_params=pltpu.CompilerParams(vmem_limit_bytes=grant * MIB),
         name=name,
     )
 
@@ -540,6 +563,7 @@
     (send,) = call(
         functools.partial(pack_kernel, *sizes),
         "pack",
+        8,
         [SMEM, VMEM, VMEM],
         [((groups, 2, rows, part), bf16)],
     )(cluster_ids, hidden_in, cotangent)
@@ -551,18 +575,20 @@
         return near + [across(piece, "segment", 1) for piece in near]
 
     slices = gathered(
-        call(slice_kernel, "slices", [VMEM], [((2, tokens, slab), bf16)] * replicas)(recv)
-    )
-    out, small = call(
+        call(
+            slice_kernel, "slices", 8, [VMEM] + [HBM] * 3, [((2, tokens, slab), bf16)] * replicas
+        )(recv, *other)
+    )
+    small, middle = call(
         chain_kernel,
         "chain",
+        24,
         [VMEM] + [HBM] * 6,
-        [((experts, 2, rows, part), bf16), ((tokens, 4 * rank + 128), bf16)],
+        [((tokens, 4 * rank + 128), bf16), ((tokens, width), bf16)],
         [
             pltpu.VMEM((2, width, rank), bf16),
             pltpu.VMEM((2, rank, width), bf16),
             pltpu.VMEM((2, 1, width), bf16),
-            pltpu.VMEM((tokens, width), bf16),
             pltpu.VMEM((tokens, width), bf16),
             pltpu.VMEM((tokens, width), f32),
             pltpu.SemaphoreType.DMA((2, 3)),
@@ -570,12 +596,21 @@
     )(recv, *own, *other)
     smalls = gathered([small] * replicas)
 
+    (out,) = call(
+        result_kernel,
+        "results",
+        12,
+        [VMEM] * 2 + [HBM] * 2,
+        [((experts, 2, rows, part), bf16)],
+        [pltpu.VMEM((rank, width), bf16), pltpu.SemaphoreType.DMA],
+    )(middle, small, own[1], other[1])
     back = lax.all_to_all(
         out.reshape(groups, rows, part), sections, split_axis=0, concat_axis=0, tiled=True
     )
     (out_hidden,) = call(
         functools.partial(unpack_kernel, *sizes),
         "unpack",
+        8,
         [SMEM, VMEM],
         [(hidden_in.shape, bf16)],
     )(cluster_ids, back)
@@ -585,7 +620,8 @@
     grad_dn, grad_upper = call(
         functools.partial(gradient_kernel, sources),
         "gradients",
-        [VMEM] * (2 * sources) + [HBM] * 6,
+        24,
+        [VMEM] * (2 * sources) + [HBM] * 7,
         [((slab, rank), bf16), ((rank, slab), bf16)],
         [
             pltpu.VMEM((slab, rank), bf16),
@@ -599,7 +635,7 @@
             pltpu.VMEM((all_tokens, 256), f32),
             pltpu.SemaphoreType.DMA((4,)),
         ],
-    )(*slices, *smalls, *own, *other)
+    )(*slices, *smalls, *own, *other, out_hidden)
     return (out_hidden, grad_dn[None, None], grad_upper[None, None])
 
 

time: 84.4 us -> 93.5 us (1.11)
  the two profiles are of different devices: /device:TPU:0 before, /device:TPU:16 now
where the time goes in v4:
time: 93.5 us; the launch traced here: 92.7 us
  waiting for transfers between devices  37 us (40%)
  Pallas kernels  18.6 us (20%)
  local copies, waits for them, and re-layouts  18.4 us (20%)
  starting transfers between devices  17.9 us (19%)
    ppermute x17, waiting for transfers between devices, across(): return lax.ppermute(block, axis, [(i, i ^ distance) for i in range(size)])  22.9 us
    unnamed x42, local copies, waits for them, and re-layouts  18.4 us
    all_to_all x1, waiting for transfers between devices, on_device_two_phases(): lax.all_to_all(send, sections, split_axis=0, concat_axis=0, tiled=True)  14 us
    ppermute x17, starting transfers between devices, across(): return lax.ppermute(block, axis, [(i, i ^ distance) for i in range(size)])  10.7 us
    pallas_call x1, Pallas kernels, on_device_two_phases(): call(functools.partial(gradient_kernel, sources), 'gradients', 24, [VMEM]...  6.99 us
    pallas_call x1, Pallas kernels, on_device_two_phases(): call(chain_kernel, 'chain', 24, [VMEM] + [HBM] * 6, [((tokens, 4 * rank +...  6.46 us
    all_to_all x1, starting transfers between devices, on_device_two_phases(): lax.all_to_all(send, sections, split_axis=0, concat_axis=0, tiled=True)  3.73 us
    all_to_all x1, starting transfers between devices, on_device_two_phases(): lax.all_to_all(out.reshape(groups, rows, part), sections, split_axis=0, c...  3.51 us
  transfers between devices with their start and end apart: 19, of which 5 were waited for; matrix products, arithmetic and copies ran while one was open for 0% of the time, Pallas kernels for 6%

profile of v4, /device:TPU:16, one launch (start us, length us, event | category | flops | bytes accessed | tf_op | source)
XLA Modules:
  0.0 92.7 jit_solution(2533421896072918532)
XLA Ops:
  1.2 0.9 %copy-done.8 = bf16[16,4,2048]{2,1,0:T(4,128)(2,1)S(1)} copy-done((bf16[16,4,2048]{2,1,0:T(4,128)(2,1)S(1)}, bf16[16,4,2048]{2,1,0:T(4,128)(2,1)}, u32[]{:S(2)}) %copy-start.8) | copy-done | bytes 262168
  2.2 0.9 %copy-done.9 = bf16[16,4,2048]{2,1,0:T(4,128)(2,1)S(1)} copy-done((bf16[16,4,2048]{2,1,0:T(4,128)(2,1)S(1)}, bf16[16,4,2048]{2,1,0:T(4,128)(2,1)}, u32[]{:S(2)}) %copy-start.9) | copy-done | bytes 262168
  3.8 1.1 %pack.1 = bf16[8,2,16,2048]{3,2,1,0:T(8,128)(2,1)S(1)} custom-call(s32[16]{0:T(128)S(1)} %copy-done.19, bf16[16,4,2048]{2,1,0:T(4,128)(2,1)S(1)} %copy-done.8, bf16[16,4,2048]{2,1,0:T(4,128)(2,1)S(1)} %copy-done.9), custom_call_target="tpu_custom_call" | custom-call | tf_op jit(solution)/shard_map/pack/pallas_call | solution.py:563
  4.9 1.0 %copy-done.4 = bf16[8,2,16,2048]{3,2,1,0:T(8,128)(2,1)} copy-done((bf16[8,2,16,2048]{3,2,1,0:T(8,128)(2,1)}, bf16[8,2,16,2048]{3,2,1,0:T(8,128)(2,1)S(1)}, u32[]{:S(2)}) %copy-start.4) | copy-done | bytes 1048600
  5.8 3.7 %all-to-all-start = ((bf16[8,2,16,2048]{3,2,1,0:T(8,128)(2,1)}), bf16[8,2,16,2048]{3,2,1,0:T(8,128)(2,1)S(1)}, u32[]{:S(2)}, u32[]{:S(2)}) async-start(bf16[8,2,16,2048]{3,2,1,0:T(8,128)(2,1)} %copy-done.4), calls=%async_computation | async-start | bytes 2097152 | tf_op jit(solution)/shard_map/all_to_all | solution.py:570
  10.1 0.9 collective-permute-done.2.other_gain._gain.refs_21_
  10.9 14.0 %all-to-all-done = bf16[8,2,16,2048]{3,2,1,0:T(8,128)(2,1)S(1)} async-done(((bf16[8,2,16,2048]{3,2,1,0:T(8,128)(2,1)}), bf16[8,2,16,2048]{3,2,1,0:T(8,128)(2,1)S(1)}, u32[]{:S(2)}, u32[]{:S(2)}) %all-to-all-start) | async-done | bytes 1048608 | tf_op jit(solution)/shard_map/all_to_all | solution.py:570
  25.0 1.6 %copy-done = bf16[1,1,256,4096]{3,2,1,0:T(8,128)(2,1)S(1)} copy-done((bf16[1,1,256,4096]{3,2,1,0:T(8,128)(2,1)S(1)}, bf16[1,1,256,4096]{3,2,1,0:T(8,128)(2,1)}, u32[]{:S(2)}) %copy-start) | copy-done | bytes 2097176
  26.6 1.6 %copy-done.2 = bf16[1,1,4096,256]{3,2,1,0:T(8,128)(2,1)S(1)} copy-done((bf16[1,1,4096,256]{3,2,1,0:T(8,128)(2,1)S(1)}, bf16[1,1,4096,256]{3,2,1,0:T(8,128)(2,1)}, u32[]{:S(2)}) %copy-start.2) | copy-done | bytes 2097176
  28.2 6.5 %chain.1 = (bf16[64,1152]{1,0:T(8,128)(2,1)S(1)}, bf16[64,4096]{1,0:T(8,128)(2,1)S(1)}) custom-call(bf16[4,2,2,16,2048]{4,3,2,1,0:T(8,128)(2,1)S(1)} %bitcast.11, bf16[4096,256]{1,0:T(8,128)(2,1)S(1)} %bitcast.14, bf16[256,4096]{1,0:T(8,128)(2,1)S(1)} %bitcast.8, bf16[1,4096]{1,0:T(2,128)(2,1)S(1)} %bitcast.17, ...), custom_call_target="tpu_custom_call" | custom-call | tf_op jit(solution)/shard_map/chain/pallas_call | solution.py:582
  35.2 3.5 %collective-permute-start.11 = (bf16[64,1152]{1,0:T(8,128)(2,1)S(1)}, bf16[64,1152]{1,0:T(8,128)(2,1)}, u32[]{:S(2)}, u32[]{:S(2)}) collective-permute-start(bf16[64,1152]{1,0:T(8,128)(2,1)S(1)} %get-tuple-element.12.small.refs_8_), channel_id=1, source_target_pairs={{0,4},{2,6},{4,0},{6,2},{1,5},{3,7},{5,1},{7,3},{8,12},{10,14},{12... | collective-permute-start | bytes 442376 | tf_op jit(solution)/shard_map/ppermute | solution.py:542
  38.7 0.7 copy-done.11
  39.5 0.9 %slices.1 = (bf16[2,64,1024]{2,1,0:T(8,128)(2,1)S(1)}, bf16[2,64,1024]{2,1,0:T(8,128)(2,1)}, bf16[2,64,1024]{2,1,0:T(8,128)(2,1)}, bf16[2,64,1024]{2,1,0:T(8,128)(2,1)}) custom-call(bf16[4,2,2,16,2048]{4,3,2,1,0:T(8,128)(2,1)S(1)} %bitcast.12, bf16[4096,256]{1,0:T(8,128)(2,1)} %collective-permute-done.other_dn._dn.refs_19_, ...), custom_call_target="tpu_custom_call" | custom-call | tf_op jit(solution)/shard_map/slices/pallas_call | solution.py:578
  40.4 0.8 collective-permute-start.4
  41.8 2.7 %collective-permute-start.5 = (bf16[2,64,1024]{2,1,0:T(8,128)(2,1)}, bf16[2,64,1024]{2,1,0:T(8,128)(2,1)}, u32[]{:S(2)}, u32[]{:S(2)}) collective-permute-start(bf16[2,64,1024]{2,1,0:T(8,128)(2,1)} %get-tuple-element.16), channel_id=1, source_target_pairs={{0,6},{2,4},{4,2},{6,0},{1,7},{3,5},{5,3},{7,1},{8,14},{10,12},{12... | collective-permute-start | bytes 786440 | tf_op jit(solution)/shard_map/ppermute | solution.py:542
  44.5 1.4 %results.1 = bf16[4,2,16,2048]{3,2,1,0:T(8,128)(2,1)} custom-call(bf16[64,4096]{1,0:T(8,128)(2,1)S(1)} %get-tuple-element.11.middle, bf16[64,1152]{1,0:T(8,128)(2,1)S(1)} %get-tuple-element.12.small.refs_8_, bf16[256,4096]{1,0:T(8,128)(2,1)S(1)} %bitcast.9, bf16[256,4096]{1,0:T(8,128)(2,1)S(1)} %collective-permute-done.1.other_up._up.refs_20_), custom_call_target="tpu_custom_call" | custom-call | tf_op jit(solution)/shard_map/results/pallas_call | solution.py:599
  46.0 3.5 %all-to-all-start.1 = ((bf16[8,16,2048]{2,1,0:T(8,128)(2,1)}), bf16[8,16,2048]{2,1,0:T(8,128)(2,1)S(1)}, u32[]{:S(2)}, u32[]{:S(2)}) async-start(bf16[8,16,2048]{2,1,0:T(8,128)(2,1)} %bitcast.4), calls=%async_computation.1 | async-start | bytes 1048576 | tf_op jit(solution)/shard_map/all_to_all | solution.py:607
  49.5 1.0 %collective-permute-start.10 = (bf16[64,1152]{1,0:T(8,128)(2,1)S(1)}, bf16[64,1152]{1,0:T(8,128)(2,1)}, u32[]{:S(2)}, u32[]{:S(2)}) collective-permute-start(bf16[64,1152]{1,0:T(8,128)(2,1)S(1)} %get-tuple-element.12.small.refs_8_), channel_id=1, source_target_pairs={{0,2},{2,0},{4,6},{6,4},{1,3},{3,1},{5,7},{7,5},{8,10},{10,8},{12,... | collective-permute-start | bytes 442376 | tf_op jit(solution)/shard_map/ppermute | solution.py:542
  50.5 13.7 %collective-permute-done.10.refs_9_ = bf16[64,1152]{1,0:T(8,128)(2,1)} collective-permute-done((bf16[64,1152]{1,0:T(8,128)(2,1)S(1)}, bf16[64,1152]{1,0:T(8,128)(2,1)}, u32[]{:S(2)}, u32[]{:S(2)}) %collective-permute-start.10) | collective-permute-done | bytes 147488 | tf_op jit(solution)/shard_map/ppermute | solution.py:542
  64.7 1.2 %collective-permute-done.4.refs_2_ = bf16[2,64,1024]{2,1,0:T(8,128)(2,1)S(1)} collective-permute-done((bf16[2,64,1024]{2,1,0:T(8,128)(2,1)}, bf16[2,64,1024]{2,1,0:T(8,128)(2,1)S(1)}, u32[]{:S(2)}, u32[]{:S(2)}) %collective-permute-start.4) | collective-permute-done | bytes 262176 | tf_op jit(solution)/shard_map/ppermute | solution.py:542
  65.9 7.2 %collective-permute-done.5.refs_3_ = bf16[2,64,1024]{2,1,0:T(8,128)(2,1)} collective-permute-done((bf16[2,64,1024]{2,1,0:T(8,128)(2,1)}, bf16[2,64,1024]{2,1,0:T(8,128)(2,1)}, u32[]{:S(2)}, u32[]{:S(2)}) %collective-permute-start.5) | collective-permute-done | bytes 262176 | tf_op jit(solution)/shard_map/ppermute | solution.py:542
  73.1 0.7 copy-done.6
  75.6 1.7 %unpack.1.refs_22_ = bf16[16,4,2048]{2,1,0:T(4,128)(2,1)} custom-call(s32[16]{0:T(128)S(1)} %copy-done.20, bf16[8,16,2048]{2,1,0:T(8,128)(2,1)S(1)} %all-to-all-done.1.back), custom_call_target="tpu_custom_call" | custom-call | tf_op jit(solution)/shard_map/unpack/pallas_call | solution.py:610
  77.4 1.6 %copy-done.1 = bf16[1,1,256,4096]{3,2,1,0:T(8,128)(2,1)S(1)} copy-done((bf16[1,1,256,4096]{3,2,1,0:T(8,128)(2,1)S(1)}, bf16[1,1,256,4096]{3,2,1,0:T(8,128)(2,1)}, u32[]{:S(2)}) %copy-start.1) | copy-done | bytes 2097176
  78.9 1.6 %copy-done.3 = bf16[1,1,4096,256]{3,2,1,0:T(8,128)(2,1)S(1)} copy-done((bf16[1,1,4096,256]{3,2,1,0:T(8,128)(2,1)S(1)}, bf16[1,1,4096,256]{3,2,1,0:T(8,128)(2,1)}, u32[]{:S(2)}) %copy-start.3) | copy-done | bytes 2097176
  80.5 0.9 %copy-done.5 = bf16[16,4,2048]{2,1,0:T(4,128)(2,1)S(1)} copy-done((bf16[16,4,2048]{2,1,0:T(4,128)(2,1)S(1)}, bf16[16,4,2048]{2,1,0:T(4,128)(2,1)}, u32[]{:S(2)}) %copy-start.5) | copy-done | bytes 262168
  81.5 0.9 %copy-done.7 = bf16[2,64,1024]{2,1,0:T(8,128)(2,1)S(1)} copy-done((bf16[2,64,1024]{2,1,0:T(8,128)(2,1)S(1)}, bf16[2,64,1024]{2,1,0:T(8,128)(2,1)}, u32[]{:S(2)}) %copy-start.7) | copy-done | bytes 262168
  82.4 0.7 copy-done.12
  83.1 0.9 copy-done.14
  84.1 0.9 copy-done.16
  85.0 0.7 copy-done.18
  85.7 7.0 %gradients.1 = (bf16[1024,256]{1,0:T(8,128)(2,1)}, bf16[256,1024]{1,0:T(8,128)(2,1)}) custom-call(bf16[2,64,1024]{2,1,0:T(8,128)(2,1)S(1)} %get-tuple-element.13.refs_0_, bf16[2,64,1024]{2,1,0:T(8,128)(2,1)S(1)} %collective-permute-done.3.refs_1_, bf16[2,64,1024]{2,1,0:T(8,128)(2,1)S(1)} %collective-permute-done.4.refs_2_, ...), custom_call_target="tpu_custom_call" | custom-call | tf_op jit(solution)/shard_map/gradients/pallas_call | solution.py:620
  (54 shorter events, 5.4 us)
Async XLA Ops:
  0.6 24.4 %collective-permute-start = (bf16[4096,256]{1,0:T(8,128)(2,1)}, bf16[4096,256]{1,0:T(8,128)(2,1)}, u32[]{:S(2)}, u32[]{:S(2)}) collective-permute-start(bf16[4096,256]{1,0:T(8,128)(2,1)} %bitcast.13), channel_id=1, source_target_pairs={{0,1},{1,0},{2,3},{3,2},{4,5},{5,4},{6,7},{7,6},{8,9},{9,8},{10,11... | collective-permute-start | bytes 6291464 | tf_op jit(solution)/shard_map/ppermute | solution.py:542
  0.7 24.3 %collective-permute-start.1 = (bf16[256,4096]{1,0:T(8,128)(2,1)}, bf16[256,4096]{1,0:T(8,128)(2,1)S(1)}, u32[]{:S(2)}, u32[]{:S(2)}) collective-permute-start(bf16[256,4096]{1,0:T(8,128)(2,1)} %bitcast.7), channel_id=1, source_target_pairs={{0,1},{1,0},{2,3},{3,2},{4,5},{5,4},{6,7},{7,6},{8,9},{9,8},{10,11... | collective-permute-start | bytes 6291464 | tf_op jit(solution)/shard_map/ppermute | solution.py:542
  1.2 0.9 %copy-start.8 = (bf16[16,4,2048]{2,1,0:T(4,128)(2,1)S(1)}, bf16[16,4,2048]{2,1,0:T(4,128)(2,1)}, u32[]{:S(2)}) copy-start(bf16[16,4,2048]{2,1,0:T(4,128)(2,1)} %hidden.1) | copy-start | bytes 786436
  2.2 0.9 %copy-start.9 = (bf16[16,4,2048]{2,1,0:T(4,128)(2,1)S(1)}, bf16[16,4,2048]{2,1,0:T(4,128)(2,1)}, u32[]{:S(2)}) copy-start(bf16[16,4,2048]{2,1,0:T(4,128)(2,1)} %cot.1) | copy-start | bytes 786436
  3.8 5.8 %copy-start.17 = (bf16[1,1,4096]{2,1,0:T(2,128)(2,1)S(1)}, bf16[1,1,4096]{2,1,0:T(2,128)(2,1)}, u32[]{:S(2)}) copy-start(bf16[1,1,4096]{2,1,0:T(2,128)(2,1)} %param.11) | copy-start | bytes 24580
  4.9 1.0 %copy-start.4 = (bf16[8,2,16,2048]{3,2,1,0:T(8,128)(2,1)}, bf16[8,2,16,2048]{3,2,1,0:T(8,128)(2,1)S(1)}, u32[]{:S(2)}) copy-start(bf16[8,2,16,2048]{3,2,1,0:T(8,128)(2,1)S(1)} %pack.1) | copy-start | bytes 3145732
  5.8 19.1 %all-to-all-start = ((bf16[8,2,16,2048]{3,2,1,0:T(8,128)(2,1)}), bf16[8,2,16,2048]{3,2,1,0:T(8,128)(2,1)S(1)}, u32[]{:S(2)}, u32[]{:S(2)}) async-start(bf16[8,2,16,2048]{3,2,1,0:T(8,128)(2,1)} %copy-done.4), calls=%async_computation | async-start | bytes 2097152 | tf_op jit(solution)/shard_map/all_to_all | solution.py:570
  9.6 1.4 %collective-permute-start.2 = (bf16[1,4096]{1,0:T(2,128)(2,1)S(1)}, bf16[1,4096]{1,0:T(2,128)(2,1)S(1)}, u32[]{:S(2)}, u32[]{:S(2)}) collective-permute-start(bf16[1,4096]{1,0:T(2,128)(2,1)S(1)} %bitcast.16), channel_id=1, source_target_pairs={{0,1},{1,0},{2,3},{3,2},{4,5},{5,4},{6,7},{7,6},{8,9},{9,8},{10,11... | collective-permute-start | bytes 24584 | tf_op jit(solution)/shard_map/ppermute | solution.py:542
  10.9 23.7 %copy-start.10 = (bf16[1,4096]{1,0:T(2,128)(2,1)}, bf16[1,4096]{1,0:T(2,128)(2,1)S(1)}, u32[]{:S(2)}) copy-start(bf16[1,4096]{1,0:T(2,128)(2,1)S(1)} %collective-permute-done.2.other_gain._gain.refs_21_) | copy-start | bytes 24580
  25.0 1.6 %copy-start = (bf16[1,1,256,4096]{3,2,1,0:T(8,128)(2,1)S(1)}, bf16[1,1,256,4096]{3,2,1,0:T(8,128)(2,1)}, u32[]{:S(2)}) copy-start(bf16[1,1,256,4096]{3,2,1,0:T(8,128)(2,1)} %param.10) | copy-start | bytes 6291460
  26.6 1.6 %copy-start.2 = (bf16[1,1,4096,256]{3,2,1,0:T(8,128)(2,1)S(1)}, bf16[1,1,4096,256]{3,2,1,0:T(8,128)(2,1)}, u32[]{:S(2)}) copy-start(bf16[1,1,4096,256]{3,2,1,0:T(8,128)(2,1)} %param.9) | copy-start | bytes 6291460
  34.7 6.5 %collective-permute-start.13 = (bf16[64,1152]{1,0:T(8,128)(2,1)S(1)}, bf16[64,1152]{1,0:T(8,128)(2,1)S(1)}, u32[]{:S(2)}, u32[]{:S(2)}) collective-permute-start(bf16[64,1152]{1,0:T(8,128)(2,1)S(1)} %get-tuple-element.12.small.refs_8_), channel_id=1, source_target_pairs={{0,1},{1,0},{2,3},{3,2},{4,5},{5,4},{6,7},{7,6},{8,9},{9,8},{10,11... | collective-permute-start | bytes 442376 | tf_op jit(solution)/shard_map/ppermute | solution.py:542
  34.7 14.8 %collective-permute-start.12 = (bf16[64,1152]{1,0:T(8,128)(2,1)S(1)}, bf16[64,1152]{1,0:T(8,128)(2,1)}, u32[]{:S(2)}, u32[]{:S(2)}) collective-permute-start(bf16[64,1152]{1,0:T(8,128)(2,1)S(1)} %get-tuple-element.12.small.refs_8_), channel_id=1, source_target_pairs={{0,6},{2,4},{4,2},{6,0},{1,7},{3,5},{5,3},{7,1},{8,14},{10,12},{12... | collective-permute-start | bytes 442376 | tf_op jit(solution)/shard_map/ppermute | solution.py:542
  35.2 15.2 %collective-permute-start.11 = (bf16[64,1152]{1,0:T(8,128)(2,1)S(1)}, bf16[64,1152]{1,0:T(8,128)(2,1)}, u32[]{:S(2)}, u32[]{:S(2)}) collective-permute-start(bf16[64,1152]{1,0:T(8,128)(2,1)S(1)} %get-tuple-element.12.small.refs_8_), channel_id=1, source_target_pairs={{0,4},{2,6},{4,0},{6,2},{1,5},{3,7},{5,1},{7,3},{8,12},{10,14},{12... | collective-permute-start | bytes 442376 | tf_op jit(solution)/shard_map/ppermute | solution.py:542
  40.4 23.8 %collective-permute-start.3 = (bf16[2,64,1024]{2,1,0:T(8,128)(2,1)}, bf16[2,64,1024]{2,1,0:T(8,128)(2,1)S(1)}, u32[]{:S(2)}, u32[]{:S(2)}) collective-permute-start(bf16[2,64,1024]{2,1,0:T(8,128)(2,1)} %get-tuple-element.14), channel_id=1, source_target_pairs={{0,2},{2,0},{4,6},{6,4},{1,3},{3,1},{5,7},{7,5},{8,10},{10,8},{12,... | collective-permute-start | bytes 786440 | tf_op jit(solution)/shard_map/ppermute | solution.py:542
  40.4 25.5 %collective-permute-start.4 = (bf16[2,64,1024]{2,1,0:T(8,128)(2,1)}, bf16[2,64,1024]{2,1,0:T(8,128)(2,1)S(1)}, u32[]{:S(2)}, u32[]{:S(2)}) collective-permute-start(bf16[2,64,1024]{2,1,0:T(8,128)(2,1)} %get-tuple-element.15), channel_id=1, source_target_pairs={{0,4},{2,6},{4,0},{6,2},{1,5},{3,7},{5,1},{7,3},{8,12},{10,14},{12... | collective-permute-start | bytes 786440 | tf_op jit(solution)/shard_map/ppermute | solution.py:542
  41.8 31.3 %collective-permute-start.5 = (bf16[2,64,1024]{2,1,0:T(8,128)(2,1)}, bf16[2,64,1024]{2,1,0:T(8,128)(2,1)}, u32[]{:S(2)}, u32[]{:S(2)}) collective-permute-start(bf16[2,64,1024]{2,1,0:T(8,128)(2,1)} %get-tuple-element.16), channel_id=1, source_target_pairs={{0,6},{2,4},{4,2},{6,0},{1,7},{3,5},{5,3},{7,1},{8,14},{10,12},{12... | collective-permute-start | bytes 786440 | tf_op jit(solution)/shard_map/ppermute | solution.py:542
  46.0 29.0 %all-to-all-start.1 = ((bf16[8,16,2048]{2,1,0:T(8,128)(2,1)}), bf16[8,16,2048]{2,1,0:T(8,128)(2,1)S(1)}, u32[]{:S(2)}, u32[]{:S(2)}) async-start(bf16[8,16,2048]{2,1,0:T(8,128)(2,1)} %bitcast.4), calls=%async_computation.1 | async-start | bytes 1048576 | tf_op jit(solution)/shard_map/all_to_all | solution.py:607
  49.5 14.7 %collective-permute-start.10 = (bf16[64,1152]{1,0:T(8,128)(2,1)S(1)}, bf16[64,1152]{1,0:T(8,128)(2,1)}, u32[]{:S(2)}, u32[]{:S(2)}) collective-permute-start(bf16[64,1152]{1,0:T(8,128)(2,1)S(1)} %get-tuple-element.12.small.refs_8_), channel_id=1, source_target_pairs={{0,2},{2,0},{4,6},{6,4},{1,3},{3,1},{5,7},{7,5},{8,10},{10,8},{12,... | collective-permute-start | bytes 442376 | tf_op jit(solution)/shard_map/ppermute | solution.py:542
  50.5 22.6 %collective-permute-start.6 = (bf16[2,64,1024]{2,1,0:T(8,128)(2,1)S(1)}, bf16[2,64,1024]{2,1,0:T(8,128)(2,1)S(1)}, u32[]{:S(2)}, u32[]{:S(2)}) collective-permute-start(bf16[2,64,1024]{2,1,0:T(8,128)(2,1)S(1)} %get-tuple-element.13.refs_0_), channel_id=1, source_target_pairs={{0,1},{1,0},{2,3},{3,2},{4,5},{5,4},{6,7},{7,6},{8,9},{9,8},{10,11... | collective-permute-start | bytes 786440 | tf_op jit(solution)/shard_map/ppermute | solution.py:542
  64.2 10.1 %collective-permute-start.16 = (bf16[64,1152]{1,0:T(8,128)(2,1)}, bf16[64,1152]{1,0:T(8,128)(2,1)S(1)}, u32[]{:S(2)}, u32[]{:S(2)}) collective-permute-start(bf16[64,1152]{1,0:T(8,128)(2,1)} %collective-permute-done.12.refs_11_), channel_id=1, source_target_pairs={{0,1},{1,0},{2,3},{3,2},{4,5},{5,4},{6,7},{7,6},{8,9},{9,8},{10,11... | collective-permute-start | bytes 442376 | tf_op jit(solution)/shard_map/ppermute | solution.py:542
  64.2 13.1 %collective-permute-start.7 = (bf16[2,64,1024]{2,1,0:T(8,128)(2,1)S(1)}, bf16[2,64,1024]{2,1,0:T(8,128)(2,1)}, u32[]{:S(2)}, u32[]{:S(2)}) collective-permute-start(bf16[2,64,1024]{2,1,0:T(8,128)(2,1)S(1)} %collective-permute-done.3.refs_1_), channel_id=1, source_target_pairs={{0,1},{1,0},{2,3},{3,2},{4,5},{5,4},{6,7},{7,6},{8,9},{9,8},{10,11... | collective-permute-start | bytes 786440 | tf_op jit(solution)/shard_map/ppermute | solution.py:542
  65.9 11.4 %collective-permute-start.8 = (bf16[2,64,1024]{2,1,0:T(8,128)(2,1)S(1)}, bf16[2,64,1024]{2,1,0:T(8,128)(2,1)}, u32[]{:S(2)}, u32[]{:S(2)}) collective-permute-start(bf16[2,64,1024]{2,1,0:T(8,128)(2,1)S(1)} %collective-permute-done.4.refs_2_), channel_id=1, source_target_pairs={{0,1},{1,0},{2,3},{3,2},{4,5},{5,4},{6,7},{7,6},{8,9},{9,8},{10,11... | collective-permute-start | bytes 786440 | tf_op jit(solution)/shard_map/ppermute | solution.py:542
  73.1 4.2 %collective-permute-start.9 = (bf16[2,64,1024]{2,1,0:T(8,128)(2,1)}, bf16[2,64,1024]{2,1,0:T(8,128)(2,1)}, u32[]{:S(2)}, u32[]{:S(2)}) collective-permute-start(bf16[2,64,1024]{2,1,0:T(8,128)(2,1)} %collective-permute-done.5.refs_3_), channel_id=1, source_target_pairs={{0,1},{1,0},{2,3},{3,2},{4,5},{5,4},{6,7},{7,6},{8,9},{9,8},{10,11... | collective-permute-start | bytes 786440 | tf_op jit(solution)/shard_map/ppermute | solution.py:542
  73.8 3.5 %collective-permute-start.15 = (bf16[64,1152]{1,0:T(8,128)(2,1)}, bf16[64,1152]{1,0:T(8,128)(2,1)}, u32[]{:S(2)}, u32[]{:S(2)}) collective-permute-start(bf16[64,1152]{1,0:T(8,128)(2,1)} %collective-permute-done.11.refs_10_), channel_id=1, source_target_pairs={{0,1},{1,0},{2,3},{3,2},{4,5},{5,4},{6,7},{7,6},{8,9},{9,8},{10,11... | collective-permute-start | bytes 442376 | tf_op jit(solution)/shard_map/ppermute | solution.py:542
  75.0 2.3 %collective-permute-start.14 = (bf16[64,1152]{1,0:T(8,128)(2,1)}, bf16[64,1152]{1,0:T(8,128)(2,1)}, u32[]{:S(2)}, u32[]{:S(2)}) collective-permute-start(bf16[64,1152]{1,0:T(8,128)(2,1)} %collective-permute-done.10.refs_9_), channel_id=1, source_target_pairs={{0,1},{1,0},{2,3},{3,2},{4,5},{5,4},{6,7},{7,6},{8,9},{9,8},{10,11... | collective-permute-start | bytes 442376 | tf_op jit(solution)/shard_map/ppermute | solution.py:542
  77.3 1.6 %copy-start.1 = (bf16[1,1,256,4096]{3,2,1,0:T(8,128)(2,1)S(1)}, bf16[1,1,256,4096]{3,2,1,0:T(8,128)(2,1)}, u32[]{:S(2)}) copy-start(bf16[1,1,256,4096]{3,2,1,0:T(8,128)(2,1)} %param.10) | copy-start | bytes 6291460
  78.9 1.6 %copy-start.3 = (bf16[1,1,4096,256]{3,2,1,0:T(8,128)(2,1)S(1)}, bf16[1,1,4096,256]{3,2,1,0:T(8,128)(2,1)}, u32[]{:S(2)}) copy-start(bf16[1,1,4096,256]{3,2,1,0:T(8,128)(2,1)} %param.9) | copy-start | bytes 6291460
  80.5 0.9 %copy-start.5 = (bf16[16,4,2048]{2,1,0:T(4,128)(2,1)S(1)}, bf16[16,4,2048]{2,1,0:T(4,128)(2,1)}, u32[]{:S(2)}) copy-start(bf16[16,4,2048]{2,1,0:T(4,128)(2,1)} %unpack.1.refs_22_) | copy-start | bytes 786436
  81.5 0.9 %copy-start.7 = (bf16[2,64,1024]{2,1,0:T(8,128)(2,1)S(1)}, bf16[2,64,1024]{2,1,0:T(8,128)(2,1)}, u32[]{:S(2)}) copy-start(bf16[2,64,1024]{2,1,0:T(8,128)(2,1)} %copy-done.6) | copy-start | bytes 786436
  83.1 0.9 copy-start.14
  84.1 0.9 copy-start.16
  (8 other events, 5.5 us)

commit v5 on v3

--- a/solution.py
+++ b/solution.py
@@ -192,7 +192,7 @@
 
 
 CHUNK = 512
-VMEM_LIMIT = 56 * 1024 * 1024
+MIB = 1024 * 1024
 TRANS_RHS = (((1,), (1,)), ((), ()))
 TRANS_LHS = (((0,), (0,)), ((), ()))
 
@@ -223,18 +223,34 @@
     return (packed == target).astype(jnp.float32).astype(jnp.bfloat16)
 
 
-def pack_kernel(length, capacity, slots, ids, hidden, cot, send):
+def pack_kernel(length, capacity, slots, ids, hidden, cot, send, id_buf, buf, packed, sems):
     groups, _, rows, part = send.shape
     tokens = hidden.shape[0] * length
-    ids_row = spread_ids(ids, (8, tokens), length)[:1]
+    arriving = [
+        pltpu.make_async_copy(source, target, sems.at[at])
+        for at, (source, target) in enumerate(
+            ((ids, id_buf), (hidden, buf.at[0]), (cot, buf.at[1]))
+        )
+    ]
+    leaving = [
+        pltpu.make_async_copy(packed.at[:, at], send.at[:, at], sems.at[3 + at]) for at in range(2)
+    ]
+    for copy in arriving:
+        copy.start()
+    arriving[0].wait()
+    ids_row = spread_ids(id_buf, (8, tokens), length)[:1]
     place = placement(ids_row, length, capacity, slots)
-    for which, source in enumerate((hidden, cot)):
-        moved = matmul(place, source[...].reshape(tokens, part)).astype(jnp.bfloat16)
+    for which in range(2):
+        arriving[1 + which].wait()
+        moved = matmul(place, buf[which].reshape(tokens, part)).astype(jnp.bfloat16)
         for group in range(groups):
-            send[group, which] = moved[group * rows : (group + 1) * rows]
-
-
-def slice_kernel(recv, *outs):
+            packed[group, which] = moved[group * rows : (group + 1) * rows]
+        leaving[which].start()
+    for copy in leaving:
+        copy.wait()
+
+
+def slice_kernel(recv, _dn, _up, _gain, *outs):
     experts, _, _, rows, part = recv.shape
     slab = outs[0].shape[2]
     place = lax.axis_index("dp")
@@ -248,10 +264,11 @@
                 out[which, e * rows : (e + 1) * rows] = recv[e, half, which, :, cols]
 
 
-def unpack_kernel(length, capacity, slots, ids, back, out):
+def unpack(sizes, id_buf, back, out):
+    length, capacity, slots = sizes
     groups, rows, width = back.shape
     s_local = out.shape[0]
-    ids_row = spread_ids(ids, (8, s_local * length), length)[:1]
+    ids_row = spread_ids(id_buf, (8, s_local * length), length)[:1]
     place = placement(ids_row, length, capacity, slots)
     moved = matmul(place, back[...].reshape(groups * rows, width), TRANS_LHS)
     out[...] = moved.astype(jnp.bfloat16).reshape(s_local, length, width)
@@ -287,7 +304,7 @@
 
 
 def chain_kernel(
-    recv, own_dn, own_up, own_gain, other_dn, other_up, other_gain,
+    recv, own_dn, own_up, own_gain, other_dn, other_up, other_gain, _slice,
     out, small,
     dn_buf, up_buf, gain_buf, entering, middle, d_norms, sems,
 ):
@@ -304,14 +321,15 @@
             for which, (source, buffer) in enumerate(zip(sources, (dn_buf, up_buf, gain_buf)))
         ]
 
-    for this in range(2):
-
-        @pl.when(phase == this)
-        def _():
-            for at in range(2):
+    def fetch(at):
+        for this in range(2):
+
+            @pl.when(phase == this)
+            def _():
                 for copy in copies(own if at == this else other, at):
                     copy.start()
 
+    fetch(0)
     waits = [copies(own, at) for at in range(2)]
     cols = range(0, width, CHUNK)
 
@@ -346,6 +364,7 @@
     inverse_0 = inverse_of(entering, mean_0)
     waits[0][0].wait()
     waits[0][2].wait()
+    fetch(1)
     pre_0 = down(entering, mean_0, inverse_0, 0)
     act_0 = gelu_value(pre_0).astype(jnp.bfloat16)
     slope_0 = gelu_slope(pre_0)
@@ -400,12 +419,20 @@
     small[:, 4 * rank :] = side_by_side(moments, tokens)
 
 
-def gradient_kernel(sources, *refs):
+def join_kernel(pieces, *refs):
+    rows = refs[0].shape[0]
+    for at, piece in enumerate(refs[:pieces]):
+        refs[-1][at * rows : (at + 1) * rows] = piece[...]
+
+
+def gradient_kernel(sources, sizes, *refs):
     slices, refs = refs[:sources], refs[sources:]
-    smalls, refs = refs[:sources], refs[sources:]
+    smalls, refs = refs[:2], refs[2:]
     own, other, refs = refs[:3], refs[3:6], refs[6:]
-    (grad_dn, grad_upper, dn_buf, up_buf, gain_buf, small, moments, lows, grads, ups, downs,
-     sems) = refs
+    (ids, back, out_hidden, grad_dn, grad_upper, id_buf, dn_buf, up_buf, gain_buf, small, moments,
+     lows, grads, ups, downs, sems) = refs
+    id_copy = pltpu.make_async_copy(ids, id_buf, sems.at[4])
+    id_copy.start()
     core = lax.axis_index("segment")
     place = lax.axis_index("dp")
     _, rows, slab = slices[0].shape
@@ -434,8 +461,10 @@
         for copy in copies(other[1], other[2], own[0], own[2]):
             copy.start()
 
-    for source in range(sources):
-        small[source * rows : (source + 1) * rows] = smalls[source][...]
+    for core_at, source in enumerate(smalls):
+        small[core_at * source.shape[0] : (core_at + 1) * source.shape[0]] = source[...]
+    id_copy.wait()
+    unpack(sizes, id_buf, back, out_hidden)
     held = lax.broadcasted_iota(jnp.int32, (128, 6 * 128), 0)
     wanted = lax.broadcasted_iota(jnp.int32, (128, 6 * 128), 1) // 128
     adds = (held // 3 == wanted).astype(jnp.float32).astype(jnp.bfloat16)
@@ -498,18 +527,18 @@
 
 
 VMEM = pl.BlockSpec(memory_space=pltpu.VMEM)
-SMEM = pl.BlockSpec(memory_space=pltpu.SMEM)
-HBM = pl.BlockSpec(memory_space=pl.ANY)
-
-
-def call(kernel, name, in_specs, outs, scratch=()):
+HBM = pl.BlockSpec(memory_space=pltpu.HBM)
+
+
+def call(kernel, name, grant, in_specs, outs, scratch=(), outs_in=VMEM, flops=0, moved=MIB):
     return pl.pallas_call(
         kernel,
         out_shape=tuple(jax.ShapeDtypeStruct(*out) for out in outs),
         in_specs=in_specs,
-        out_specs=tuple(VMEM for _ in outs),
+        out_specs=tuple(outs_in for _ in outs),
         scratch_shapes=list(scratch),
-        compiler_params=pltpu.CompilerParams(vmem_limit_bytes=VMEM_LIMIT),
+        compiler_params=pltpu.CompilerParams(vmem_limit_bytes=grant * MIB),
+        cost_estimate=pl.CostEstimate(flops=flops, bytes_accessed=moved, transcendentals=0),
         name=name,
     )
 
@@ -540,8 +569,16 @@
     (send,) = call(
         functools.partial(pack_kernel, *sizes),
         "pack",
-        [SMEM, VMEM, VMEM],
+        56,
+        [HBM] * 3,
         [((groups, 2, rows, part), bf16)],
+        [
+            pltpu.SMEM(cluster_ids.shape, jnp.int32),
+            pltpu.VMEM((2,) + hidden_in.shape, bf16),
+            pltpu.VMEM((groups, 2, rows, part), bf16),
+            pltpu.SemaphoreType.DMA((5,)),
+        ],
+        outs_in=HBM,
     )(cluster_ids, hidden_in, cotangent)
     recv = lax.all_to_all(send, sections, split_axis=0, concat_axis=0, tiled=True)
     recv = recv.reshape(experts, 2, 2, rows, part)
@@ -551,12 +588,15 @@
         return near + [across(piece, "segment", 1) for piece in near]
 
     slices = gathered(
-        call(slice_kernel, "slices", [VMEM], [((2, tokens, slab), bf16)] * replicas)(recv)
+        call(
+            slice_kernel, "slices", 8, [VMEM] + [HBM] * 3, [((2, tokens, slab), bf16)] * replicas
+        )(recv, *other)
     )
     out, small = call(
         chain_kernel,
         "chain",
-        [VMEM] + [HBM] * 6,
+        24,
+        [VMEM] + [HBM] * 6 + [pl.BlockSpec(memory_space=pl.ANY)],
         [((experts, 2, rows, part), bf16), ((tokens, 4 * rank + 128), bf16)],
         [
             pltpu.VMEM((2, width, rank), bf16),
@@ -567,27 +607,32 @@
             pltpu.VMEM((tokens, width), f32),
             pltpu.SemaphoreType.DMA((2, 3)),
         ],
-    )(recv, *own, *other)
-    smalls = gathered([small] * replicas)
-
+        flops=7 * 2 * tokens * width * rank,
+        moved=10 * MIB,
+    )(recv, *own, *other, slices[0])
     back = lax.all_to_all(
         out.reshape(groups, rows, part), sections, split_axis=0, concat_axis=0, tiled=True
     )
-    (out_hidden,) = call(
-        functools.partial(unpack_kernel, *sizes),
-        "unpack",
-        [SMEM, VMEM],
-        [(hidden_in.shape, bf16)],
-    )(cluster_ids, back)
-
+    near = [small] + [across(small, "dp", step) for step in range(1, replicas)]
+    waited = slices[replicas:] + [back]
+    (joined,) = call(
+        functools.partial(join_kernel, replicas),
+        "join",
+        8,
+        [VMEM] * replicas + [HBM] * len(waited),
+        [((replicas * tokens, 4 * rank + 128), bf16)],
+    )(*near, *waited)
+    smalls = (joined, across(joined, "segment", 1))
     sources = 2 * replicas
     all_tokens = sources * tokens
-    grad_dn, grad_upper = call(
-        functools.partial(gradient_kernel, sources),
+    out_hidden, grad_dn, grad_upper = call(
+        functools.partial(gradient_kernel, sources, sizes),
         "gradients",
-        [VMEM] * (2 * sources) + [HBM] * 6,
-        [((slab, rank), bf16), ((rank, slab), bf16)],
+        24,
+        [VMEM] * (sources + 2) + [HBM] * 7 + [VMEM],
+        [(hidden_in.shape, bf16), ((slab, rank), bf16), ((rank, slab), bf16)],
         [
+            pltpu.SMEM(cluster_ids.shape, jnp.int32),
             pltpu.VMEM((slab, rank), bf16),
             pltpu.VMEM((rank, slab), bf16),
             pltpu.VMEM((2, 1, slab), bf16),
@@ -597,9 +642,9 @@
             pltpu.VMEM((all_tokens, slab), bf16),
             pltpu.VMEM((all_tokens, 256), f32),
             pltpu.VMEM((all_tokens, 256), f32),
-            pltpu.SemaphoreType.DMA((4,)),
+            pltpu.SemaphoreType.DMA((5,)),
         ],
-    )(*slices, *smalls, *own, *other)
+    )(*slices, *smalls, *own, *other, cluster_ids, back)
     return (out_hidden, grad_dn[None, None], grad_upper[None, None])
 
 

time: 84.4 us -> 84.6 us (level)
  blocking collectives: 20.6 us -> 0 us
  waiting for transfers between devices: 19.3 us -> 37.2 us
  Pallas kernels: 24.1 us -> 17.2 us
  local copies, waits for them, and re-layouts: 4.06 us -> 8.83 us
  starting transfers between devices: 15.1 us -> 19.7 us
    all_to_all x1 -> x0, blocking collectives: 20.6 us -> none  [on_device_two_phases(): lax.all_to_all(send, sections, split_axis=0, concat_axis=0, tiled=True)]
    all_to_all x0 -> x1, waiting for transfers between devices: none -> 14 us  [on_device_two_phases(): lax.all_to_all(send, sections, split_axis=0, concat_axis=0, tiled=True)]
    pallas_call x5, Pallas kernels: 24.1 us -> 17.2 us  [the longest x1 7.04 us: on_device_two_phases(): call(functools.partial(gradient_kernel, sources, sizes), 'gradients', 24,...]
    all_to_all x0 -> x1, starting transfers between devices: none -> 5.16 us  [on_device_two_phases(): lax.all_to_all(send, sections, split_axis=0, concat_axis=0, tiled=True)]
    unnamed x38 -> x30, local copies, waits for them, and re-layouts: 4.06 us -> 8.83 us
    ppermute x17 -> x14, waiting for transfers between devices: 19.3 us -> 23.1 us  [across(): return lax.ppermute(block, axis, [(i, i ^ distance) for i in range(size)])]
    ppermute x17 -> x14, starting transfers between devices: 11.6 us -> 10.9 us  [across(): return lax.ppermute(block, axis, [(i, i ^ distance) for i in range(size)])]
  transfers between devices with their start and end apart: 18 -> 16, of which waited for: 6 -> 7; matrix products, arithmetic and copies ran while one was open for 0% -> 0% of each run, Pallas kernels for 26% -> 11%
where the time goes in v5:
time: 84.6 us; the launch traced here: 83.6 us
  waiting for transfers between devices  37.2 us (44%)
  starting transfers between devices  19.7 us (23%)
  Pallas kernels  17.2 us (20%)
  local copies, waits for them, and re-layouts  8.83 us (10%)
    ppermute x14, waiting for transfers between devices, across(): return lax.ppermute(block, axis, [(i, i ^ distance) for i in range(size)])  23.1 us
    all_to_all x1, waiting for transfers between devices, on_device_two_phases(): lax.all_to_all(send, sections, split_axis=0, concat_axis=0, tiled=True)  14 us
    ppermute x14, starting transfers between devices, across(): return lax.ppermute(block, axis, [(i, i ^ distance) for i in range(size)])  10.9 us
    unnamed x30, local copies, waits for them, and re-layouts  8.83 us
    pallas_call x1, Pallas kernels, on_device_two_phases(): call(functools.partial(gradient_kernel, sources, sizes), 'gradients', 24,...  7.04 us
    pallas_call x1, Pallas kernels, on_device_two_phases(): call(chain_kernel, 'chain', 24, [VMEM] + [HBM] * 6 + [pl.BlockSpec(memory...  6.77 us
    all_to_all x1, starting transfers between devices, on_device_two_phases(): lax.all_to_all(send, sections, split_axis=0, concat_axis=0, tiled=True)  5.16 us
    all_to_all x1, starting transfers between devices, on_device_two_phases(): lax.all_to_all(out.reshape(groups, rows, part), sections, split_axis=0, c...  3.63 us
  transfers between devices with their start and end apart: 16, of which 7 were waited for; matrix products, arithmetic and copies ran while one was open for 0% of the time, Pallas kernels for 11%

profile of v5, /device:TPU:0, one launch (start us, length us, event | category | flops | bytes accessed | tf_op | source)
XLA Modules:
  0.0 83.6 jit_solution(15553453544879068340)
XLA Ops:
  0.6 0.5 collective-permute-start
  1.2 2.4 %pack.1 = bf16[8,2,16,2048]{3,2,1,0:T(8,128)(2,1)} custom-call(s32[16]{0:T(128)} %refs_16_.1, bf16[16,4,2048]{2,1,0:T(4,128)(2,1)} %hidden.1, bf16[16,4,2048]{2,1,0:T(4,128)(2,1)} %cot.1), custom_call_target="tpu_custom_call" | custom-call | bytes 1048576 | tf_op jit(solution)/shard_map/pack/pallas_call | solution.py:569
  3.6 5.2 %all-to-all-start = ((bf16[8,2,16,2048]{3,2,1,0:T(8,128)(2,1)}), bf16[8,2,16,2048]{3,2,1,0:T(8,128)(2,1)S(1)}, u32[]{:S(2)}, u32[]{:S(2)}) async-start(bf16[8,2,16,2048]{3,2,1,0:T(8,128)(2,1)} %pack.1), calls=%async_computation | async-start | bytes 2097152 | tf_op jit(solution)/shard_map/all_to_all | solution.py:583
  8.8 0.5 collective-permute-start.2
  9.3 0.9 %collective-permute-done.2._gain.other_gain.refs_15_ = bf16[1,4096]{1,0:T(2,128)(2,1)S(1)} collective-permute-done((bf16[1,4096]{1,0:T(2,128)(2,1)S(1)}, bf16[1,4096]{1,0:T(2,128)(2,1)S(1)}, u32[]{:S(2)}, u32[]{:S(2)}) %collective-permute-start.2) | collective-permute-done | bytes 8224 | tf_op jit(solution)/shard_map/ppermute | solution.py:548
  10.1 14.0 %all-to-all-done = bf16[8,2,16,2048]{3,2,1,0:T(8,128)(2,1)S(1)} async-done(((bf16[8,2,16,2048]{3,2,1,0:T(8,128)(2,1)}), bf16[8,2,16,2048]{3,2,1,0:T(8,128)(2,1)S(1)}, u32[]{:S(2)}, u32[]{:S(2)}) %all-to-all-start) | async-done | bytes 1048608 | tf_op jit(solution)/shard_map/all_to_all | solution.py:583
  24.2 0.9 %slices.1 = (bf16[2,64,1024]{2,1,0:T(8,128)(2,1)S(1)}, bf16[2,64,1024]{2,1,0:T(8,128)(2,1)}, bf16[2,64,1024]{2,1,0:T(8,128)(2,1)}, bf16[2,64,1024]{2,1,0:T(8,128)(2,1)}) custom-call(bf16[4,2,2,16,2048]{4,3,2,1,0:T(8,128)(2,1)S(1)} %bitcast.7, bf16[4096,256]{1,0:T(8,128)(2,1)S(1)} %collective-permute-done._dn.other_dn.refs_13_, ...), custom_call_target="tpu_custom_call" | custom-call | bytes 1048576 | tf_op jit(solution)/shard_map/slices/pallas_call | solution.py:591
  25.1 1.6 %collective-permute-start.3 = (bf16[2,64,1024]{2,1,0:T(8,128)(2,1)}, bf16[2,64,1024]{2,1,0:T(8,128)(2,1)}, u32[]{:S(2)}, u32[]{:S(2)}) collective-permute-start(bf16[2,64,1024]{2,1,0:T(8,128)(2,1)} %get-tuple-element.13), channel_id=1, source_target_pairs={{0,2},{2,0},{4,6},{6,4},{1,3},{3,1},{5,7},{7,5},{8,10},{10,8},{12,... | collective-permute-start | bytes 786440 | tf_op jit(solution)/shard_map/ppermute | solution.py:548
  26.7 2.6 %collective-permute-start.4 = (bf16[2,64,1024]{2,1,0:T(8,128)(2,1)}, bf16[2,64,1024]{2,1,0:T(8,128)(2,1)}, u32[]{:S(2)}, u32[]{:S(2)}) collective-permute-start(bf16[2,64,1024]{2,1,0:T(8,128)(2,1)} %get-tuple-element.14), channel_id=1, source_target_pairs={{0,4},{2,6},{4,0},{6,2},{1,5},{3,7},{5,1},{7,3},{8,12},{10,14},{12... | collective-permute-start | bytes 786440 | tf_op jit(solution)/shard_map/ppermute | solution.py:548
  29.3 0.2 collective-permute-start.5
  29.5 6.8 %chain.1 = (bf16[4,2,16,2048]{3,2,1,0:T(8,128)(2,1)S(1)}, bf16[64,1152]{1,0:T(8,128)(2,1)S(1)}) custom-call(bf16[4,2,2,16,2048]{4,3,2,1,0:T(8,128)(2,1)S(1)} %bitcast.8, bf16[4096,256]{1,0:T(8,128)(2,1)S(1)} %bitcast.10, bf16[256,4096]{1,0:T(8,128)(2,1)S(1)} %bitcast.13, bf16[1,4096]{1,0:T(2,128)(2,1)S(1)} %bitcast.17, ...), custom_call_target="tpu_custom_call" | custom-call | flops 939524096 | bytes 10485760 | tf_op jit(solution)/shard_map/chain/pallas_call | solution.py:595
  36.3 0.8 copy-done.4
  37.1 0.7 copy-done.5
  37.8 3.6 %all-to-all-start.1 = ((bf16[8,16,2048]{2,1,0:T(8,128)(2,1)}), bf16[8,16,2048]{2,1,0:T(8,128)(2,1)S(1)}, u32[]{:S(2)}, u32[]{:S(2)}) async-start(bf16[8,16,2048]{2,1,0:T(8,128)(2,1)} %bitcast.15), calls=%async_computation.1 | async-start | bytes 1048576 | tf_op jit(solution)/shard_map/all_to_all | solution.py:613
  41.4 3.7 %collective-permute-start.12 = (bf16[64,1152]{1,0:T(8,128)(2,1)}, bf16[64,1152]{1,0:T(8,128)(2,1)S(1)}, u32[]{:S(2)}, u32[]{:S(2)}) collective-permute-start(bf16[64,1152]{1,0:T(8,128)(2,1)} %copy-done.5), channel_id=1, source_target_pairs={{0,6},{2,4},{4,2},{6,0},{1,7},{3,5},{5,3},{7,1},{8,14},{10,12},{12... | collective-permute-start | bytes 442376 | tf_op jit(solution)/shard_map/ppermute | solution.py:548
  45.1 5.2 %collective-permute-done.12.refs_3_ = bf16[64,1152]{1,0:T(8,128)(2,1)S(1)} collective-permute-done((bf16[64,1152]{1,0:T(8,128)(2,1)}, bf16[64,1152]{1,0:T(8,128)(2,1)S(1)}, u32[]{:S(2)}, u32[]{:S(2)}) %collective-permute-start.12) | collective-permute-done | bytes 147488 | tf_op jit(solution)/shard_map/ppermute | solution.py:548
  50.3 0.7 copy-done.7
  50.9 0.5 collective-permute-start.7
  51.4 2.0 %collective-permute-done.4.refs_2_ = bf16[2,64,1024]{2,1,0:T(8,128)(2,1)} collective-permute-done((bf16[2,64,1024]{2,1,0:T(8,128)(2,1)}, bf16[2,64,1024]{2,1,0:T(8,128)(2,1)}, u32[]{:S(2)}, u32[]{:S(2)}) %collective-permute-start.4) | collective-permute-done | bytes 262176 | tf_op jit(solution)/shard_map/ppermute | solution.py:548
  53.4 0.5 collective-permute-start.9
  53.9 8.4 %collective-permute-done.11.refs_2_ = bf16[64,1152]{1,0:T(8,128)(2,1)S(1)} collective-permute-done((bf16[64,1152]{1,0:T(8,128)(2,1)}, bf16[64,1152]{1,0:T(8,128)(2,1)S(1)}, u32[]{:S(2)}, u32[]{:S(2)}) %collective-permute-start.11) | collective-permute-done | bytes 147488 | tf_op jit(solution)/shard_map/ppermute | solution.py:548
  62.3 0.7 copy-done.9
  63.0 0.7 collective-permute-start.10
  63.7 4.7 %collective-permute-done.10.refs_1_ = bf16[64,1152]{1,0:T(8,128)(2,1)S(1)} collective-permute-done((bf16[64,1152]{1,0:T(8,128)(2,1)}, bf16[64,1152]{1,0:T(8,128)(2,1)S(1)}, u32[]{:S(2)}, u32[]{:S(2)}) %collective-permute-start.10) | collective-permute-done | bytes 147488 | tf_op jit(solution)/shard_map/ppermute | solution.py:548
  68.4 0.7 copy-done.11
  69.1 1.0 %copy-done.6 = bf16[64,1152]{1,0:T(8,128)(2,1)S(1)} copy-done((bf16[64,1152]{1,0:T(8,128)(2,1)S(1)}, bf16[64,1152]{1,0:T(8,128)(2,1)}, u32[]{:S(2)}) %copy-start.6) | copy-done | bytes 147480
  70.1 0.9 %copy-done.8 = bf16[64,1152]{1,0:T(8,128)(2,1)S(1)} copy-done((bf16[64,1152]{1,0:T(8,128)(2,1)S(1)}, bf16[64,1152]{1,0:T(8,128)(2,1)}, u32[]{:S(2)}) %copy-start.8) | copy-done | bytes 147480
  71.0 0.9 %copy-done.10 = bf16[64,1152]{1,0:T(8,128)(2,1)S(1)} copy-done((bf16[64,1152]{1,0:T(8,128)(2,1)S(1)}, bf16[64,1152]{1,0:T(8,128)(2,1)}, u32[]{:S(2)}) %copy-start.10) | copy-done | bytes 147480
  71.9 0.9 %copy-done.12 = bf16[64,1152]{1,0:T(8,128)(2,1)S(1)} copy-done((bf16[64,1152]{1,0:T(8,128)(2,1)S(1)}, bf16[64,1152]{1,0:T(8,128)(2,1)}, u32[]{:S(2)}) %copy-start.12) | copy-done | bytes 147480
  73.0 2.0 %collective-permute-done.13.refs_9_ = bf16[256,1152]{1,0:T(8,128)(2,1)S(1)} collective-permute-done((bf16[256,1152]{1,0:T(8,128)(2,1)S(1)}, bf16[256,1152]{1,0:T(8,128)(2,1)S(1)}, u32[]{:S(2)}, u32[]{:S(2)}) %collective-permute-start.13) | collective-permute-done | bytes 589856 | tf_op jit(solution)/shard_map/ppermute | solution.py:548
  75.0 1.6 %copy-done.3 = bf16[1,1,256,4096]{3,2,1,0:T(8,128)(2,1)S(1)} copy-done((bf16[1,1,256,4096]{3,2,1,0:T(8,128)(2,1)S(1)}, bf16[1,1,256,4096]{3,2,1,0:T(8,128)(2,1)}, u32[]{:S(2)}) %copy-start.3) | copy-done | bytes 2097176
  76.6 7.0 %gradients.1 = (bf16[16,4,2048]{2,1,0:T(4,128)(2,1)}, bf16[1024,256]{1,0:T(8,128)(2,1)}, bf16[256,1024]{1,0:T(8,128)(2,1)}) custom-call(bf16[2,64,1024]{2,1,0:T(8,128)(2,1)S(1)} %get-tuple-element.12._slice.refs_0_, bf16[2,64,1024]{2,1,0:T(8,128)(2,1)} %collective-permute-done.3.refs_1_, bf16[2,64,1024]{2,1,0:T(8,128)(2,1)} %collective-permute-done.4.refs_2_, ...), custom_call_target="tpu_custom_call" | custom-call | bytes 1048576 | tf_op jit(solution)/shard_map/gradients/pallas_call | solution.py:628
  (35 shorter events, 0.3 us)
Async XLA Ops:
  0.6 8.1 %copy-start.13 = (bf16[1,1,4096]{2,1,0:T(2,128)(2,1)S(1)}, bf16[1,1,4096]{2,1,0:T(2,128)(2,1)}, u32[]{:S(2)}) copy-start(bf16[1,1,4096]{2,1,0:T(2,128)(2,1)} %param.11) | copy-start | bytes 24580
  0.6 23.5 %collective-permute-start = (bf16[4096,256]{1,0:T(8,128)(2,1)}, bf16[4096,256]{1,0:T(8,128)(2,1)S(1)}, u32[]{:S(2)}, u32[]{:S(2)}) collective-permute-start(bf16[4096,256]{1,0:T(8,128)(2,1)} %bitcast.9), channel_id=1, source_target_pairs={{0,1},{1,0},{2,3},{3,2},{4,5},{5,4},{6,7},{7,6},{8,9},{9,8},{10,11... | collective-permute-start | bytes 6291464 | tf_op jit(solution)/shard_map/ppermute | solution.py:548
  1.2 23.0 %collective-permute-start.1 = (bf16[256,4096]{1,0:T(8,128)(2,1)}, bf16[256,4096]{1,0:T(8,128)(2,1)}, u32[]{:S(2)}, u32[]{:S(2)}) collective-permute-start(bf16[256,4096]{1,0:T(8,128)(2,1)} %bitcast.12), channel_id=1, source_target_pairs={{0,1},{1,0},{2,3},{3,2},{4,5},{5,4},{6,7},{7,6},{8,9},{9,8},{10,11... | collective-permute-start | bytes 6291464 | tf_op jit(solution)/shard_map/ppermute | solution.py:548
  3.6 20.6 %all-to-all-start = ((bf16[8,2,16,2048]{3,2,1,0:T(8,128)(2,1)}), bf16[8,2,16,2048]{3,2,1,0:T(8,128)(2,1)S(1)}, u32[]{:S(2)}, u32[]{:S(2)}) async-start(bf16[8,2,16,2048]{3,2,1,0:T(8,128)(2,1)} %pack.1), calls=%async_computation | async-start | bytes 2097152 | tf_op jit(solution)/shard_map/all_to_all | solution.py:583
  8.8 1.4 %collective-permute-start.2 = (bf16[1,4096]{1,0:T(2,128)(2,1)S(1)}, bf16[1,4096]{1,0:T(2,128)(2,1)S(1)}, u32[]{:S(2)}, u32[]{:S(2)}) collective-permute-start(bf16[1,4096]{1,0:T(2,128)(2,1)S(1)} %bitcast.16), channel_id=1, source_target_pairs={{0,1},{1,0},{2,3},{3,2},{4,5},{5,4},{6,7},{7,6},{8,9},{9,8},{10,11... | collective-permute-start | bytes 24584 | tf_op jit(solution)/shard_map/ppermute | solution.py:548
  24.2 5.3 %copy-start = (bf16[1,1,4096,256]{3,2,1,0:T(8,128)(2,1)S(1)}, bf16[1,1,4096,256]{3,2,1,0:T(8,128)(2,1)}, u32[]{:S(2)}) copy-start(bf16[1,1,4096,256]{3,2,1,0:T(8,128)(2,1)} %param.9) | copy-start | bytes 6291460
  24.2 5.3 %copy-start.2 = (bf16[1,1,256,4096]{3,2,1,0:T(8,128)(2,1)S(1)}, bf16[1,1,256,4096]{3,2,1,0:T(8,128)(2,1)}, u32[]{:S(2)}) copy-start(bf16[1,1,256,4096]{3,2,1,0:T(8,128)(2,1)} %param.10) | copy-start | bytes 6291460
  25.1 25.8 %collective-permute-start.3 = (bf16[2,64,1024]{2,1,0:T(8,128)(2,1)}, bf16[2,64,1024]{2,1,0:T(8,128)(2,1)}, u32[]{:S(2)}, u32[]{:S(2)}) collective-permute-start(bf16[2,64,1024]{2,1,0:T(8,128)(2,1)} %get-tuple-element.13), channel_id=1, source_target_pairs={{0,2},{2,0},{4,6},{6,4},{1,3},{3,1},{5,7},{7,5},{8,10},{10,8},{12,... | collective-permute-start | bytes 786440 | tf_op jit(solution)/shard_map/ppermute | solution.py:548
  26.7 26.7 %collective-permute-start.4 = (bf16[2,64,1024]{2,1,0:T(8,128)(2,1)}, bf16[2,64,1024]{2,1,0:T(8,128)(2,1)}, u32[]{:S(2)}, u32[]{:S(2)}) collective-permute-start(bf16[2,64,1024]{2,1,0:T(8,128)(2,1)} %get-tuple-element.14), channel_id=1, source_target_pairs={{0,4},{2,6},{4,0},{6,2},{1,5},{3,7},{5,1},{7,3},{8,12},{10,14},{12... | collective-permute-start | bytes 786440 | tf_op jit(solution)/shard_map/ppermute | solution.py:548
  29.3 24.1 %collective-permute-start.5 = (bf16[2,64,1024]{2,1,0:T(8,128)(2,1)}, bf16[2,64,1024]{2,1,0:T(8,128)(2,1)}, u32[]{:S(2)}, u32[]{:S(2)}) collective-permute-start(bf16[2,64,1024]{2,1,0:T(8,128)(2,1)} %get-tuple-element.15), channel_id=1, source_target_pairs={{0,6},{2,4},{4,2},{6,0},{1,7},{3,5},{5,3},{7,1},{8,14},{10,12},{12... | collective-permute-start | bytes 786440 | tf_op jit(solution)/shard_map/ppermute | solution.py:548
  36.3 0.8 copy-start.4
  37.1 0.7 copy-start.5
  37.8 37.2 %copy-start.14 = (s32[16]{0:T(128)S(1)}, s32[16]{0:T(128)}, u32[]{:S(2)}) copy-start(s32[16]{0:T(128)} %refs_16_.1) | copy-start | bytes 196
  37.8 31.2 %all-to-all-start.1 = ((bf16[8,16,2048]{2,1,0:T(8,128)(2,1)}), bf16[8,16,2048]{2,1,0:T(8,128)(2,1)S(1)}, u32[]{:S(2)}, u32[]{:S(2)}) async-start(bf16[8,16,2048]{2,1,0:T(8,128)(2,1)} %bitcast.15), calls=%async_computation.1 | async-start | bytes 1048576 | tf_op jit(solution)/shard_map/all_to_all | solution.py:613
  41.4 8.8 %collective-permute-start.12 = (bf16[64,1152]{1,0:T(8,128)(2,1)}, bf16[64,1152]{1,0:T(8,128)(2,1)S(1)}, u32[]{:S(2)}, u32[]{:S(2)}) collective-permute-start(bf16[64,1152]{1,0:T(8,128)(2,1)} %copy-done.5), channel_id=1, source_target_pairs={{0,6},{2,4},{4,2},{6,0},{1,7},{3,5},{5,3},{7,1},{8,14},{10,12},{12... | collective-permute-start | bytes 442376 | tf_op jit(solution)/shard_map/ppermute | solution.py:548
  45.1 17.3 %collective-permute-start.11 = (bf16[64,1152]{1,0:T(8,128)(2,1)}, bf16[64,1152]{1,0:T(8,128)(2,1)S(1)}, u32[]{:S(2)}, u32[]{:S(2)}) collective-permute-start(bf16[64,1152]{1,0:T(8,128)(2,1)} %copy-done.5), channel_id=1, source_target_pairs={{0,4},{2,6},{4,0},{6,2},{1,5},{3,7},{5,1},{7,3},{8,12},{10,14},{12... | collective-permute-start | bytes 442376 | tf_op jit(solution)/shard_map/ppermute | solution.py:548
  50.3 0.7 copy-start.7
  50.9 18.1 %collective-permute-start.6 = (bf16[2,64,1024]{2,1,0:T(8,128)(2,1)S(1)}, bf16[2,64,1024]{2,1,0:T(8,128)(2,1)S(1)}, u32[]{:S(2)}, u32[]{:S(2)}) collective-permute-start(bf16[2,64,1024]{2,1,0:T(8,128)(2,1)S(1)} %get-tuple-element.12._slice.refs_0_), channel_id=1, source_target_pairs={{0,1},{1,0},{2,3},{3,2},{4,5},{5,4},{6,7},{7,6},{8,9},{9,8},{10,11... | collective-permute-start | bytes 786440 | tf_op jit(solution)/shard_map/ppermute | solution.py:548
  50.9 18.1 %collective-permute-start.7 = (bf16[2,64,1024]{2,1,0:T(8,128)(2,1)}, bf16[2,64,1024]{2,1,0:T(8,128)(2,1)S(1)}, u32[]{:S(2)}, u32[]{:S(2)}) collective-permute-start(bf16[2,64,1024]{2,1,0:T(8,128)(2,1)} %collective-permute-done.3.refs_1_), channel_id=1, source_target_pairs={{0,1},{1,0},{2,3},{3,2},{4,5},{5,4},{6,7},{7,6},{8,9},{9,8},{10,11... | collective-permute-start | bytes 786440 | tf_op jit(solution)/shard_map/ppermute | solution.py:548
  53.4 15.6 %collective-permute-start.8 = (bf16[2,64,1024]{2,1,0:T(8,128)(2,1)}, bf16[2,64,1024]{2,1,0:T(8,128)(2,1)}, u32[]{:S(2)}, u32[]{:S(2)}) collective-permute-start(bf16[2,64,1024]{2,1,0:T(8,128)(2,1)} %collective-permute-done.4.refs_2_), channel_id=1, source_target_pairs={{0,1},{1,0},{2,3},{3,2},{4,5},{5,4},{6,7},{7,6},{8,9},{9,8},{10,11... | collective-permute-start | bytes 786440 | tf_op jit(solution)/shard_map/ppermute | solution.py:548
  53.4 15.6 %collective-permute-start.9 = (bf16[2,64,1024]{2,1,0:T(8,128)(2,1)}, bf16[2,64,1024]{2,1,0:T(8,128)(2,1)}, u32[]{:S(2)}, u32[]{:S(2)}) collective-permute-start(bf16[2,64,1024]{2,1,0:T(8,128)(2,1)} %collective-permute-done.5.refs_3_), channel_id=1, source_target_pairs={{0,1},{1,0},{2,3},{3,2},{4,5},{5,4},{6,7},{7,6},{8,9},{9,8},{10,11... | collective-permute-start | bytes 786440 | tf_op jit(solution)/shard_map/ppermute | solution.py:548
  62.3 0.7 copy-start.9
  63.0 5.4 %collective-permute-start.10 = (bf16[64,1152]{1,0:T(8,128)(2,1)}, bf16[64,1152]{1,0:T(8,128)(2,1)S(1)}, u32[]{:S(2)}, u32[]{:S(2)}) collective-permute-start(bf16[64,1152]{1,0:T(8,128)(2,1)} %copy-done.5), channel_id=1, source_target_pairs={{0,2},{2,0},{4,6},{6,4},{1,3},{3,1},{5,7},{7,5},{8,10},{10,8},{12,... | collective-permute-start | bytes 442376 | tf_op jit(solution)/shard_map/ppermute | solution.py:548
  68.4 0.7 copy-start.11
  69.0 5.9 %copy-start.1 = (bf16[1,1,4096,256]{3,2,1,0:T(8,128)(2,1)S(1)}, bf16[1,1,4096,256]{3,2,1,0:T(8,128)(2,1)}, u32[]{:S(2)}) copy-start(bf16[1,1,4096,256]{3,2,1,0:T(8,128)(2,1)} %param.9) | copy-start | bytes 6291460
  69.1 1.1 %copy-start.6 = (bf16[64,1152]{1,0:T(8,128)(2,1)S(1)}, bf16[64,1152]{1,0:T(8,128)(2,1)}, u32[]{:S(2)}) copy-start(bf16[64,1152]{1,0:T(8,128)(2,1)} %copy-done.5) | copy-start | bytes 442372
  70.1 0.9 %copy-start.8 = (bf16[64,1152]{1,0:T(8,128)(2,1)S(1)}, bf16[64,1152]{1,0:T(8,128)(2,1)}, u32[]{:S(2)}) copy-start(bf16[64,1152]{1,0:T(8,128)(2,1)} %copy-done.7) | copy-start | bytes 442372
  71.0 0.9 %copy-start.10 = (bf16[64,1152]{1,0:T(8,128)(2,1)S(1)}, bf16[64,1152]{1,0:T(8,128)(2,1)}, u32[]{:S(2)}) copy-start(bf16[64,1152]{1,0:T(8,128)(2,1)} %copy-done.9) | copy-start | bytes 442372
  71.9 0.9 %copy-start.12 = (bf16[64,1152]{1,0:T(8,128)(2,1)S(1)}, bf16[64,1152]{1,0:T(8,128)(2,1)}, u32[]{:S(2)}) copy-start(bf16[64,1152]{1,0:T(8,128)(2,1)} %copy-done.11) | copy-start | bytes 442372
  72.9 2.1 %collective-permute-start.13 = (bf16[256,1152]{1,0:T(8,128)(2,1)S(1)}, bf16[256,1152]{1,0:T(8,128)(2,1)S(1)}, u32[]{:S(2)}, u32[]{:S(2)}) collective-permute-start(bf16[256,1152]{1,0:T(8,128)(2,1)S(1)} %join.1.refs_8_), channel_id=1, source_target_pairs={{0,1},{1,0},{2,3},{3,2},{4,5},{5,4},{6,7},{7,6},{8,9},{9,8},{10,11... | collective-permute-start | bytes 1769480 | tf_op jit(solution)/shard_map/ppermute | solution.py:548
  75.0 1.6 %copy-start.3 = (bf16[1,1,256,4096]{3,2,1,0:T(8,128)(2,1)S(1)}, bf16[1,1,256,4096]{3,2,1,0:T(8,128)(2,1)}, u32[]{:S(2)}) copy-start(bf16[1,1,256,4096]{3,2,1,0:T(8,128)(2,1)} %param.10) | copy-start | bytes 6291460

commit v6 on v5

--- a/solution.py
+++ b/solution.py
@@ -304,9 +304,9 @@
 
 
 def chain_kernel(
-    recv, own_dn, own_up, own_gain, other_dn, other_up, other_gain, _slice,
+    recv_in, own_dn, own_up, own_gain, other_dn, other_up, other_gain,
     out, small,
-    dn_buf, up_buf, gain_buf, entering, middle, d_norms, sems,
+    recv, dn_buf, up_buf, gain_buf, entering, middle, d_norms, sems,
 ):
     phase = lax.axis_index("segment")
     experts, phases, _, rows, part = recv.shape
@@ -329,6 +329,11 @@
                 for copy in copies(own if at == this else other, at):
                     copy.start()
 
+    arriving = [
+        pltpu.make_async_copy(recv_in.at[:, :, at], recv.at[:, :, at], sems.at[2, at])
+        for at in range(2)
+    ]
+    arriving[0].start()
     fetch(0)
     waits = [copies(own, at) for at in range(2)]
     cols = range(0, width, CHUNK)
@@ -356,6 +361,7 @@
         return pre
 
     total = jnp.zeros((tokens, 128), jnp.float32)
+    arriving[0].wait()
     for col in cols:
         value = block(0, col)
         entering[:, col : col + CHUNK] = value
@@ -364,6 +370,7 @@
     inverse_0 = inverse_of(entering, mean_0)
     waits[0][0].wait()
     waits[0][2].wait()
+    arriving[1].start()
     fetch(1)
     pre_0 = down(entering, mean_0, inverse_0, 0)
     act_0 = gelu_value(pre_0).astype(jnp.bfloat16)
@@ -379,7 +386,7 @@
         total = total + lanes(value.astype(jnp.float32))
     mean_1 = row_sum(total) / width
     inverse_1 = inverse_of(middle, mean_1)
-    for copy in waits[1]:
+    for copy in waits[1] + arriving[1:]:
         copy.wait()
     d_act = jnp.zeros((tokens, rank), jnp.float32)
     for col in cols:
@@ -595,30 +602,32 @@
     out, small = call(
         chain_kernel,
         "chain",
-        24,
-        [VMEM] + [HBM] * 6 + [pl.BlockSpec(memory_space=pl.ANY)],
+        60,
+        [HBM] * 7,
         [((experts, 2, rows, part), bf16), ((tokens, 4 * rank + 128), bf16)],
         [
+            pltpu.VMEM(recv.shape, bf16),
             pltpu.VMEM((2, width, rank), bf16),
             pltpu.VMEM((2, rank, width), bf16),
             pltpu.VMEM((2, 1, width), bf16),
             pltpu.VMEM((tokens, width), bf16),
             pltpu.VMEM((tokens, width), bf16),
             pltpu.VMEM((tokens, width), f32),
-            pltpu.SemaphoreType.DMA((2, 3)),
+            pltpu.SemaphoreType.DMA((3, 3)),
         ],
         flops=7 * 2 * tokens * width * rank,
         moved=10 * MIB,
-    )(recv, *own, *other, slices[0])
+    )(recv, *own, *other)
     back = lax.all_to_all(
         out.reshape(groups, rows, part), sections, split_axis=0, concat_axis=0, tiled=True
     )
-    near = [small] + [across(small, "dp", step) for step in range(1, replicas)]
+    two_away = across(small, "dp", 2)
+    near = [small, across(small, "dp", 1), two_away, across(two_away, "dp", 1)]
     waited = slices[replicas:] + [back]
     (joined,) = call(
         functools.partial(join_kernel, replicas),
         "join",
-        8,
+        60,
         [VMEM] * replicas + [HBM] * len(waited),
         [((replicas * tokens, 4 * rank + 128), bf16)],
     )(*near, *waited)
@@ -628,7 +637,7 @@
     out_hidden, grad_dn, grad_upper = call(
         functools.partial(gradient_kernel, sources, sizes),
         "gradients",
-        24,
+        60,
         [VMEM] * (sources + 2) + [HBM] * 7 + [VMEM],
         [(hidden_in.shape, bf16), ((slab, rank), bf16), ((rank, slab), bf16)],
         [

time: 84.6 us -> 79.5 us (0.940)
  local copies, waits for them, and re-layouts: 8.83 us -> 3.33 us
  Pallas kernels: 17.2 us -> 22.6 us
  waiting for transfers between devices: 37.2 us -> 32.5 us
    unnamed x30 -> x34, local copies, waits for them, and re-layouts: 8.83 us -> 3.33 us
    pallas_call x3, Pallas kernels: 13.9 us -> 19.1 us  [the longest x1 9.22 us: on_device_two_phases(): call(chain_kernel, 'chain', 60, [HBM] * 7, [((experts, 2, rows, part), bf...]
    ppermute x14, waiting for transfers between devices: 23.1 us -> 18.5 us  [across(): return lax.ppermute(block, axis, [(i, i ^ distance) for i in range(size)])]
  transfers between devices with their start and end apart: 16 -> 16, of which waited for: 7 -> 6; matrix products, arithmetic and copies ran while one was open for 0% -> 0% of each run, Pallas kernels for 11% -> 15%
where the time goes in v6:
time: 79.5 us; the launch traced here: 78.6 us
  waiting for transfers between devices  32.5 us (41%)
  Pallas kernels  22.6 us (28%)
  starting transfers between devices  19.4 us (24%)
  local copies, waits for them, and re-layouts  3.33 us (4%)
    ppermute x14, waiting for transfers between devices, across(): return lax.ppermute(block, axis, [(i, i ^ distance) for i in range(size)])  18.5 us
    all_to_all x1, waiting for transfers between devices, on_device_two_phases(): lax.all_to_all(send, sections, split_axis=0, concat_axis=0, tiled=True)  14 us
    ppermute x14, starting transfers between devices, across(): return lax.ppermute(block, axis, [(i, i ^ distance) for i in range(size)])  10.7 us
    pallas_call x1, Pallas kernels, on_device_two_phases(): call(chain_kernel, 'chain', 60, [HBM] * 7, [((experts, 2, rows, part), bf...  9.22 us
    pallas_call x1, Pallas kernels, on_device_two_phases(): call(functools.partial(gradient_kernel, sources, sizes), 'gradients', 60,...  7.88 us
    all_to_all x1, starting transfers between devices, on_device_two_phases(): lax.all_to_all(send, sections, split_axis=0, concat_axis=0, tiled=True)  5.16 us
    all_to_all x1, starting transfers between devices, on_device_two_phases(): lax.all_to_all(out.reshape(groups, rows, part), sections, split_axis=0, c...  3.51 us
    unnamed x34, local copies, waits for them, and re-layouts  3.33 us
  transfers between devices with their start and end apart: 16, of which 6 were waited for; matrix products, arithmetic and copies ran while one was open for 0% of the time, Pallas kernels for 15%

profile of v6, /device:TPU:0, one launch (start us, length us, event | category | flops | bytes accessed | tf_op | source)
XLA Modules:
  0.0 78.6 jit_solution(8405575554255334320)
XLA Ops:
  0.6 0.5 collective-permute-start
  1.2 0.1 collective-permute-start.1
  1.2 2.4 %pack.1 = bf16[8,2,16,2048]{3,2,1,0:T(8,128)(2,1)} custom-call(s32[16]{0:T(128)} %refs_16_.1, bf16[16,4,2048]{2,1,0:T(4,128)(2,1)} %hidden.1, bf16[16,4,2048]{2,1,0:T(4,128)(2,1)} %cot.1), custom_call_target="tpu_custom_call" | custom-call | bytes 1048576 | tf_op jit(solution)/shard_map/pack/pallas_call | solution.py:576
  3.6 5.2 %all-to-all-start = ((bf16[8,2,16,2048]{3,2,1,0:T(8,128)(2,1)}), bf16[8,2,16,2048]{3,2,1,0:T(8,128)(2,1)S(1)}, u32[]{:S(2)}, u32[]{:S(2)}) async-start(bf16[8,2,16,2048]{3,2,1,0:T(8,128)(2,1)} %pack.1), calls=%async_computation | async-start | bytes 2097152 | tf_op jit(solution)/shard_map/all_to_all | solution.py:590
  8.8 0.5 collective-permute-start.2
  9.3 0.9 %collective-permute-done.2._gain.other_gain.refs_15_ = bf16[1,4096]{1,0:T(2,128)(2,1)S(1)} collective-permute-done((bf16[1,4096]{1,0:T(2,128)(2,1)S(1)}, bf16[1,4096]{1,0:T(2,128)(2,1)S(1)}, u32[]{:S(2)}, u32[]{:S(2)}) %collective-permute-start.2) | collective-permute-done | bytes 8224 | tf_op jit(solution)/shard_map/ppermute | solution.py:555
  10.2 14.0 %all-to-all-done = bf16[8,2,16,2048]{3,2,1,0:T(8,128)(2,1)S(1)} async-done(((bf16[8,2,16,2048]{3,2,1,0:T(8,128)(2,1)}), bf16[8,2,16,2048]{3,2,1,0:T(8,128)(2,1)S(1)}, u32[]{:S(2)}, u32[]{:S(2)}) %all-to-all-start) | async-done | bytes 1048608 | tf_op jit(solution)/shard_map/all_to_all | solution.py:590
  24.2 1.1 %slices.1 = (bf16[2,64,1024]{2,1,0:T(8,128)(2,1)S(1)}, bf16[2,64,1024]{2,1,0:T(8,128)(2,1)}, bf16[2,64,1024]{2,1,0:T(8,128)(2,1)}, bf16[2,64,1024]{2,1,0:T(8,128)(2,1)}) custom-call(bf16[4,2,2,16,2048]{4,3,2,1,0:T(8,128)(2,1)S(1)} %bitcast.7, bf16[4096,256]{1,0:T(8,128)(2,1)S(1)} %collective-permute-done._dn.other_dn.refs_13_, ...), custom_call_target="tpu_custom_call" | custom-call | bytes 1048576 | tf_op jit(solution)/shard_map/slices/pallas_call | solution.py:598
  25.3 0.2 copy-done.1
  25.5 0.6 copy-done
  26.1 1.6 %collective-permute-start.3 = (bf16[2,64,1024]{2,1,0:T(8,128)(2,1)}, bf16[2,64,1024]{2,1,0:T(8,128)(2,1)S(1)}, u32[]{:S(2)}, u32[]{:S(2)}) collective-permute-start(bf16[2,64,1024]{2,1,0:T(8,128)(2,1)} %get-tuple-element.13), channel_id=1, source_target_pairs={{0,2},{2,0},{4,6},{6,4},{1,3},{3,1},{5,7},{7,5},{8,10},{10,8},{12,... | collective-permute-start | bytes 786440 | tf_op jit(solution)/shard_map/ppermute | solution.py:555
  27.7 2.6 %collective-permute-start.4 = (bf16[2,64,1024]{2,1,0:T(8,128)(2,1)}, bf16[2,64,1024]{2,1,0:T(8,128)(2,1)S(1)}, u32[]{:S(2)}, u32[]{:S(2)}) collective-permute-start(bf16[2,64,1024]{2,1,0:T(8,128)(2,1)} %get-tuple-element.14), channel_id=1, source_target_pairs={{0,4},{2,6},{4,0},{6,2},{1,5},{3,7},{5,1},{7,3},{8,12},{10,14},{12... | collective-permute-start | bytes 786440 | tf_op jit(solution)/shard_map/ppermute | solution.py:555
  30.3 0.2 collective-permute-start.5
  30.5 9.2 %chain.1 = (bf16[4,2,16,2048]{3,2,1,0:T(8,128)(2,1)}, bf16[64,1152]{1,0:T(8,128)(2,1)}) custom-call(bf16[4,2,2,16,2048]{4,3,2,1,0:T(8,128)(2,1)} %bitcast.8, bf16[4096,256]{1,0:T(8,128)(2,1)} %bitcast.10, bf16[256,4096]{1,0:T(8,128)(2,1)} %bitcast.13, bf16[1,4096]{1,0:T(2,128)(2,1)} %bitcast.16, bf16[4096,256]{1,0:T(8,128)(2,1)} %copy-done, ...), custom_call_target="tpu_custom_call" | custom-call | flops 939524096 | bytes 10485760 | tf_op jit(solution)/shard_map/chain/pallas_call | solution.py:602
  39.8 3.5 %all-to-all-start.1 = ((bf16[8,16,2048]{2,1,0:T(8,128)(2,1)}), bf16[8,16,2048]{2,1,0:T(8,128)(2,1)S(1)}, u32[]{:S(2)}, u32[]{:S(2)}) async-start(bf16[8,16,2048]{2,1,0:T(8,128)(2,1)} %bitcast.15), calls=%async_computation.1 | async-start | bytes 1048576 | tf_op jit(solution)/shard_map/all_to_all | solution.py:621
  43.3 1.8 %collective-permute-start.11 = (bf16[64,1152]{1,0:T(8,128)(2,1)}, bf16[64,1152]{1,0:T(8,128)(2,1)S(1)}, u32[]{:S(2)}, u32[]{:S(2)}) collective-permute-start(bf16[64,1152]{1,0:T(8,128)(2,1)} %get-tuple-element.16.refs_0_), channel_id=1, source_target_pairs={{0,4},{2,6},{4,0},{6,2},{1,5},{3,7},{5,1},{7,3},{8,12},{10,14},{12... | collective-permute-start | bytes 442376 | tf_op jit(solution)/shard_map/ppermute | solution.py:555
  45.0 2.5 %collective-permute-start.10 = (bf16[64,1152]{1,0:T(8,128)(2,1)}, bf16[64,1152]{1,0:T(8,128)(2,1)S(1)}, u32[]{:S(2)}, u32[]{:S(2)}) collective-permute-start(bf16[64,1152]{1,0:T(8,128)(2,1)} %get-tuple-element.16.refs_0_), channel_id=1, source_target_pairs={{0,2},{2,0},{4,6},{6,4},{1,3},{3,1},{5,7},{7,5},{8,10},{10,8},{12,... | collective-permute-start | bytes 442376 | tf_op jit(solution)/shard_map/ppermute | solution.py:555
  47.5 9.5 %collective-permute-done.11.refs_2_ = bf16[64,1152]{1,0:T(8,128)(2,1)S(1)} collective-permute-done((bf16[64,1152]{1,0:T(8,128)(2,1)}, bf16[64,1152]{1,0:T(8,128)(2,1)S(1)}, u32[]{:S(2)}, u32[]{:S(2)}) %collective-permute-start.11) | collective-permute-done | bytes 147488 | tf_op jit(solution)/shard_map/ppermute | solution.py:555
  57.1 0.5 collective-permute-start.7
  57.6 0.1 collective-permute-start.8
  57.7 0.4 collective-permute-start.9
  58.1 0.5 collective-permute-done.6.refs_4_
  58.6 5.3 %collective-permute-done.12.refs_3_ = bf16[64,1152]{1,0:T(8,128)(2,1)S(1)} collective-permute-done((bf16[64,1152]{1,0:T(8,128)(2,1)S(1)}, bf16[64,1152]{1,0:T(8,128)(2,1)S(1)}, u32[]{:S(2)}, u32[]{:S(2)}) %collective-permute-start.12) | collective-permute-done | bytes 147488 | tf_op jit(solution)/shard_map/ppermute | solution.py:555
  64.0 0.6 copy-done.15
  64.6 0.2 copy-done.4
  64.8 0.1 copy-done.6
  64.9 0.1 copy-done.7
  64.9 0.7 copy-done.8
  65.6 2.0 %join.1.refs_8_ = bf16[256,1152]{1,0:T(8,128)(2,1)} custom-call(bf16[64,1152]{1,0:T(8,128)(2,1)} %get-tuple-element.16.refs_0_, bf16[64,1152]{1,0:T(8,128)(2,1)} %copy-done.14, bf16[64,1152]{1,0:T(8,128)(2,1)} %copy-done.13, bf16[64,1152]{1,0:T(8,128)(2,1)} %copy-done.15, bf16[2,64,1024]{2,1,0:T(8,128)(2,1)} %copy-done.5, bf16[2,64,1024]{2,1,0:T(8,128)(2,1)} %copy-done.6, ...), custom_call_target="tpu_custom_call" | custom-call | bytes 1048576 | tf_op jit(solution)/shard_map/join/pallas_call | solution.py:627
  67.6 2.2 %collective-permute-done.13.refs_9_ = bf16[256,1152]{1,0:T(8,128)(2,1)S(1)} collective-permute-done((bf16[256,1152]{1,0:T(8,128)(2,1)}, bf16[256,1152]{1,0:T(8,128)(2,1)S(1)}, u32[]{:S(2)}, u32[]{:S(2)}) %collective-permute-start.13) | collective-permute-done | bytes 589856 | tf_op jit(solution)/shard_map/ppermute | solution.py:555
  69.9 0.8 %copy-done.9 = bf16[256,1152]{1,0:T(8,128)(2,1)} copy-done((bf16[256,1152]{1,0:T(8,128)(2,1)}, bf16[256,1152]{1,0:T(8,128)(2,1)S(1)}, u32[]{:S(2)}) %copy-start.9) | copy-done | bytes 589848
  70.7 7.9 %gradients.1 = (bf16[16,4,2048]{2,1,0:T(4,128)(2,1)}, bf16[1024,256]{1,0:T(8,128)(2,1)}, bf16[256,1024]{1,0:T(8,128)(2,1)}) custom-call(bf16[2,64,1024]{2,1,0:T(8,128)(2,1)} %copy-done.2, bf16[2,64,1024]{2,1,0:T(8,128)(2,1)} %copy-done.10, bf16[2,64,1024]{2,1,0:T(8,128)(2,1)} %copy-done.11, bf16[2,64,1024]{2,1,0:T(8,128)(2,1)} %copy-done.12, ...), custom_call_target="tpu_custom_call" | custom-call | bytes 1048576 | tf_op jit(solution)/shard_map/gradients/pallas_call | solution.py:637
  (39 shorter events, 0.1 us)
Async XLA Ops:
  0.6 8.2 %copy-start.16 = (bf16[1,1,4096]{2,1,0:T(2,128)(2,1)S(1)}, bf16[1,1,4096]{2,1,0:T(2,128)(2,1)}, u32[]{:S(2)}) copy-start(bf16[1,1,4096]{2,1,0:T(2,128)(2,1)} %param.11) | copy-start | bytes 24580
  0.6 23.6 %collective-permute-start = (bf16[4096,256]{1,0:T(8,128)(2,1)}, bf16[4096,256]{1,0:T(8,128)(2,1)S(1)}, u32[]{:S(2)}, u32[]{:S(2)}) collective-permute-start(bf16[4096,256]{1,0:T(8,128)(2,1)} %bitcast.9), channel_id=1, source_target_pairs={{0,1},{1,0},{2,3},{3,2},{4,5},{5,4},{6,7},{7,6},{8,9},{9,8},{10,11... | collective-permute-start | bytes 6291464 | tf_op jit(solution)/shard_map/ppermute | solution.py:555
  1.2 23.1 %collective-permute-start.1 = (bf16[256,4096]{1,0:T(8,128)(2,1)}, bf16[256,4096]{1,0:T(8,128)(2,1)}, u32[]{:S(2)}, u32[]{:S(2)}) collective-permute-start(bf16[256,4096]{1,0:T(8,128)(2,1)} %bitcast.12), channel_id=1, source_target_pairs={{0,1},{1,0},{2,3},{3,2},{4,5},{5,4},{6,7},{7,6},{8,9},{9,8},{10,11... | collective-permute-start | bytes 6291464 | tf_op jit(solution)/shard_map/ppermute | solution.py:555
  3.6 20.6 %all-to-all-start = ((bf16[8,2,16,2048]{3,2,1,0:T(8,128)(2,1)}), bf16[8,2,16,2048]{3,2,1,0:T(8,128)(2,1)S(1)}, u32[]{:S(2)}, u32[]{:S(2)}) async-start(bf16[8,2,16,2048]{3,2,1,0:T(8,128)(2,1)} %pack.1), calls=%async_computation | async-start | bytes 2097152 | tf_op jit(solution)/shard_map/all_to_all | solution.py:590
  8.8 1.4 %collective-permute-start.2 = (bf16[1,4096]{1,0:T(2,128)(2,1)S(1)}, bf16[1,4096]{1,0:T(2,128)(2,1)S(1)}, u32[]{:S(2)}, u32[]{:S(2)}) collective-permute-start(bf16[1,4096]{1,0:T(2,128)(2,1)S(1)} %bitcast.18), channel_id=1, source_target_pairs={{0,1},{1,0},{2,3},{3,2},{4,5},{5,4},{6,7},{7,6},{8,9},{9,8},{10,11... | collective-permute-start | bytes 24584 | tf_op jit(solution)/shard_map/ppermute | solution.py:555
  10.2 15.2 %copy-start.3 = (bf16[1,4096]{1,0:T(2,128)(2,1)}, bf16[1,4096]{1,0:T(2,128)(2,1)S(1)}, u32[]{:S(2)}) copy-start(bf16[1,4096]{1,0:T(2,128)(2,1)S(1)} %collective-permute-done.2._gain.other_gain.refs_15_) | copy-start | bytes 24580
  24.2 1.3 %copy-start.1 = (bf16[8,2,16,2048]{3,2,1,0:T(8,128)(2,1)}, bf16[8,2,16,2048]{3,2,1,0:T(8,128)(2,1)S(1)}, u32[]{:S(2)}) copy-start(bf16[8,2,16,2048]{3,2,1,0:T(8,128)(2,1)S(1)} %all-to-all-done) | copy-start | bytes 3145732
  24.2 1.9 %copy-start = (bf16[4096,256]{1,0:T(8,128)(2,1)}, bf16[4096,256]{1,0:T(8,128)(2,1)S(1)}, u32[]{:S(2)}) copy-start(bf16[4096,256]{1,0:T(8,128)(2,1)S(1)} %collective-permute-done._dn.other_dn.refs_13_) | copy-start | bytes 6291460
  26.1 30.9 %copy-start.2 = (bf16[2,64,1024]{2,1,0:T(8,128)(2,1)}, bf16[2,64,1024]{2,1,0:T(8,128)(2,1)S(1)}, u32[]{:S(2)}) copy-start(bf16[2,64,1024]{2,1,0:T(8,128)(2,1)S(1)} %get-tuple-element.12.refs_0_) | copy-start | bytes 786436
  26.1 30.9 %collective-permute-start.3 = (bf16[2,64,1024]{2,1,0:T(8,128)(2,1)}, bf16[2,64,1024]{2,1,0:T(8,128)(2,1)S(1)}, u32[]{:S(2)}, u32[]{:S(2)}) collective-permute-start(bf16[2,64,1024]{2,1,0:T(8,128)(2,1)} %get-tuple-element.13), channel_id=1, source_target_pairs={{0,2},{2,0},{4,6},{6,4},{1,3},{3,1},{5,7},{7,5},{8,10},{10,8},{12,... | collective-permute-start | bytes 786440 | tf_op jit(solution)/shard_map/ppermute | solution.py:555
  27.7 29.8 %collective-permute-start.4 = (bf16[2,64,1024]{2,1,0:T(8,128)(2,1)}, bf16[2,64,1024]{2,1,0:T(8,128)(2,1)S(1)}, u32[]{:S(2)}, u32[]{:S(2)}) collective-permute-start(bf16[2,64,1024]{2,1,0:T(8,128)(2,1)} %get-tuple-element.14), channel_id=1, source_target_pairs={{0,4},{2,6},{4,0},{6,2},{1,5},{3,7},{5,1},{7,3},{8,12},{10,14},{12... | collective-permute-start | bytes 786440 | tf_op jit(solution)/shard_map/ppermute | solution.py:555
  30.3 27.3 %collective-permute-start.5 = (bf16[2,64,1024]{2,1,0:T(8,128)(2,1)}, bf16[2,64,1024]{2,1,0:T(8,128)(2,1)S(1)}, u32[]{:S(2)}, u32[]{:S(2)}) collective-permute-start(bf16[2,64,1024]{2,1,0:T(8,128)(2,1)} %get-tuple-element.15), channel_id=1, source_target_pairs={{0,6},{2,4},{4,2},{6,0},{1,7},{3,5},{5,3},{7,1},{8,14},{10,12},{12... | collective-permute-start | bytes 786440 | tf_op jit(solution)/shard_map/ppermute | solution.py:555
  39.8 24.2 %all-to-all-start.1 = ((bf16[8,16,2048]{2,1,0:T(8,128)(2,1)}), bf16[8,16,2048]{2,1,0:T(8,128)(2,1)S(1)}, u32[]{:S(2)}, u32[]{:S(2)}) async-start(bf16[8,16,2048]{2,1,0:T(8,128)(2,1)} %bitcast.15), calls=%async_computation.1 | async-start | bytes 1048576 | tf_op jit(solution)/shard_map/all_to_all | solution.py:621
  43.3 13.8 %collective-permute-start.11 = (bf16[64,1152]{1,0:T(8,128)(2,1)}, bf16[64,1152]{1,0:T(8,128)(2,1)S(1)}, u32[]{:S(2)}, u32[]{:S(2)}) collective-permute-start(bf16[64,1152]{1,0:T(8,128)(2,1)} %get-tuple-element.16.refs_0_), channel_id=1, source_target_pairs={{0,4},{2,6},{4,0},{6,2},{1,5},{3,7},{5,1},{7,3},{8,12},{10,14},{12... | collective-permute-start | bytes 442376 | tf_op jit(solution)/shard_map/ppermute | solution.py:555
  45.0 13.1 %collective-permute-start.10 = (bf16[64,1152]{1,0:T(8,128)(2,1)}, bf16[64,1152]{1,0:T(8,128)(2,1)S(1)}, u32[]{:S(2)}, u32[]{:S(2)}) collective-permute-start(bf16[64,1152]{1,0:T(8,128)(2,1)} %get-tuple-element.16.refs_0_), channel_id=1, source_target_pairs={{0,2},{2,0},{4,6},{6,4},{1,3},{3,1},{5,7},{7,5},{8,10},{10,8},{12,... | collective-permute-start | bytes 442376 | tf_op jit(solution)/shard_map/ppermute | solution.py:555
  57.0 6.9 %copy-start.13 = (bf16[64,1152]{1,0:T(8,128)(2,1)}, bf16[64,1152]{1,0:T(8,128)(2,1)S(1)}, u32[]{:S(2)}) copy-start(bf16[64,1152]{1,0:T(8,128)(2,1)S(1)} %collective-permute-done.11.refs_2_) | copy-start | bytes 442372
  57.0 1.5 %collective-permute-start.6 = (bf16[2,64,1024]{2,1,0:T(8,128)(2,1)S(1)}, bf16[2,64,1024]{2,1,0:T(8,128)(2,1)S(1)}, u32[]{:S(2)}, u32[]{:S(2)}) collective-permute-start(bf16[2,64,1024]{2,1,0:T(8,128)(2,1)S(1)} %get-tuple-element.12.refs_0_), channel_id=1, source_target_pairs={{0,1},{1,0},{2,3},{3,2},{4,5},{5,4},{6,7},{7,6},{8,9},{9,8},{10,11... | collective-permute-start | bytes 786440 | tf_op jit(solution)/shard_map/ppermute | solution.py:555
  57.1 12.8 %copy-start.10 = (bf16[2,64,1024]{2,1,0:T(8,128)(2,1)}, bf16[2,64,1024]{2,1,0:T(8,128)(2,1)S(1)}, u32[]{:S(2)}) copy-start(bf16[2,64,1024]{2,1,0:T(8,128)(2,1)S(1)} %collective-permute-done.3.refs_1_) | copy-start | bytes 786436
  57.1 6.9 %collective-permute-start.7 = (bf16[2,64,1024]{2,1,0:T(8,128)(2,1)S(1)}, bf16[2,64,1024]{2,1,0:T(8,128)(2,1)S(1)}, u32[]{:S(2)}, u32[]{:S(2)}) collective-permute-start(bf16[2,64,1024]{2,1,0:T(8,128)(2,1)S(1)} %collective-permute-done.3.refs_1_), channel_id=1, source_target_pairs={{0,1},{1,0},{2,3},{3,2},{4,5},{5,4},{6,7},{7,6},{8,9},{9,8},{10,11... | collective-permute-start | bytes 786440 | tf_op jit(solution)/shard_map/ppermute | solution.py:555
  57.6 12.3 %copy-start.11 = (bf16[2,64,1024]{2,1,0:T(8,128)(2,1)}, bf16[2,64,1024]{2,1,0:T(8,128)(2,1)S(1)}, u32[]{:S(2)}) copy-start(bf16[2,64,1024]{2,1,0:T(8,128)(2,1)S(1)} %collective-permute-done.4.refs_2_) | copy-start | bytes 786436
  57.6 6.4 %collective-permute-start.8 = (bf16[2,64,1024]{2,1,0:T(8,128)(2,1)S(1)}, bf16[2,64,1024]{2,1,0:T(8,128)(2,1)S(1)}, u32[]{:S(2)}, u32[]{:S(2)}) collective-permute-start(bf16[2,64,1024]{2,1,0:T(8,128)(2,1)S(1)} %collective-permute-done.4.refs_2_), channel_id=1, source_target_pairs={{0,1},{1,0},{2,3},{3,2},{4,5},{5,4},{6,7},{7,6},{8,9},{9,8},{10,11... | collective-permute-start | bytes 786440 | tf_op jit(solution)/shard_map/ppermute | solution.py:555
  57.7 12.2 %copy-start.12 = (bf16[2,64,1024]{2,1,0:T(8,128)(2,1)}, bf16[2,64,1024]{2,1,0:T(8,128)(2,1)S(1)}, u32[]{:S(2)}) copy-start(bf16[2,64,1024]{2,1,0:T(8,128)(2,1)S(1)} %collective-permute-done.5.refs_3_) | copy-start | bytes 786436
  57.7 6.3 %collective-permute-start.9 = (bf16[2,64,1024]{2,1,0:T(8,128)(2,1)S(1)}, bf16[2,64,1024]{2,1,0:T(8,128)(2,1)S(1)}, u32[]{:S(2)}, u32[]{:S(2)}) collective-permute-start(bf16[2,64,1024]{2,1,0:T(8,128)(2,1)S(1)} %collective-permute-done.5.refs_3_), channel_id=1, source_target_pairs={{0,1},{1,0},{2,3},{3,2},{4,5},{5,4},{6,7},{7,6},{8,9},{9,8},{10,11... | collective-permute-start | bytes 786440 | tf_op jit(solution)/shard_map/ppermute | solution.py:555
  58.1 5.9 %copy-start.14 = (bf16[64,1152]{1,0:T(8,128)(2,1)}, bf16[64,1152]{1,0:T(8,128)(2,1)S(1)}, u32[]{:S(2)}) copy-start(bf16[64,1152]{1,0:T(8,128)(2,1)S(1)} %collective-permute-done.10.refs_1_) | copy-start | bytes 442372
  58.1 5.8 %collective-permute-start.12 = (bf16[64,1152]{1,0:T(8,128)(2,1)S(1)}, bf16[64,1152]{1,0:T(8,128)(2,1)S(1)}, u32[]{:S(2)}, u32[]{:S(2)}) collective-permute-start(bf16[64,1152]{1,0:T(8,128)(2,1)S(1)} %collective-permute-done.11.refs_2_), channel_id=1, source_target_pairs={{0,2},{2,0},{4,6},{6,4},{1,3},{3,1},{5,7},{7,5},{8,10},{10,8},{12,... | collective-permute-start | bytes 442376 | tf_op jit(solution)/shard_map/ppermute | solution.py:555
  58.6 5.4 %copy-start.5 = (bf16[2,64,1024]{2,1,0:T(8,128)(2,1)}, bf16[2,64,1024]{2,1,0:T(8,128)(2,1)S(1)}, u32[]{:S(2)}) copy-start(bf16[2,64,1024]{2,1,0:T(8,128)(2,1)S(1)} %collective-permute-done.6.refs_4_) | copy-start | bytes 786436
  63.9 0.8 %copy-start.4 = (bf16[8,16,2048]{2,1,0:T(8,128)(2,1)}, bf16[8,16,2048]{2,1,0:T(8,128)(2,1)S(1)}, u32[]{:S(2)}) copy-start(bf16[8,16,2048]{2,1,0:T(8,128)(2,1)S(1)} %all-to-all-done.1.refs_8_.refs_17_) | copy-start | bytes 1572868
  63.9 0.9 %copy-start.6 = (bf16[2,64,1024]{2,1,0:T(8,128)(2,1)}, bf16[2,64,1024]{2,1,0:T(8,128)(2,1)S(1)}, u32[]{:S(2)}) copy-start(bf16[2,64,1024]{2,1,0:T(8,128)(2,1)S(1)} %collective-permute-done.7.refs_5_) | copy-start | bytes 786436
  64.0 1.0 %copy-start.7 = (bf16[2,64,1024]{2,1,0:T(8,128)(2,1)}, bf16[2,64,1024]{2,1,0:T(8,128)(2,1)S(1)}, u32[]{:S(2)}) copy-start(bf16[2,64,1024]{2,1,0:T(8,128)(2,1)S(1)} %collective-permute-done.8.refs_6_) | copy-start | bytes 786436
  64.9 0.7 copy-start.8
  67.6 2.2 %collective-permute-start.13 = (bf16[256,1152]{1,0:T(8,128)(2,1)}, bf16[256,1152]{1,0:T(8,128)(2,1)S(1)}, u32[]{:S(2)}, u32[]{:S(2)}) collective-permute-start(bf16[256,1152]{1,0:T(8,128)(2,1)} %join.1.refs_8_), channel_id=1, source_target_pairs={{0,1},{1,0},{2,3},{3,2},{4,5},{5,4},{6,7},{7,6},{8,9},{9,8},{10,11... | collective-permute-start | bytes 1769480 | tf_op jit(solution)/shard_map/ppermute | solution.py:555
  69.8 0.9 %copy-start.9 = (bf16[256,1152]{1,0:T(8,128)(2,1)}, bf16[256,1152]{1,0:T(8,128)(2,1)S(1)}, u32[]{:S(2)}) copy-start(bf16[256,1152]{1,0:T(8,128)(2,1)S(1)} %collective-permute-done.13.refs_9_) | copy-start | bytes 1769476
  (1 other events, 0.7 us)

commit v7 on v6

--- a/solution.py
+++ b/solution.py
@@ -209,7 +209,7 @@
     return spread
 
 
-def placement(ids_row, length, capacity, slots):
+def ranked(ids_row, length):
     tokens = ids_row.shape[1]
     kinds = lax.broadcasted_iota(jnp.int32, (8, tokens), 0)
     member = (kinds == ids_row).astype(jnp.float32)
@@ -217,15 +217,37 @@
     at_row = lax.broadcasted_iota(jnp.int32, (tokens, tokens), 1)
     before = (lax.rem(at_col, length) == 0) & (at_col // length < at_row // length)
     counts = matmul(member.astype(jnp.bfloat16), before.astype(jnp.float32).astype(jnp.bfloat16))
-    rank = jnp.sum(member * counts, axis=0, keepdims=True).astype(jnp.int32)
-    target = (ids_row * capacity + rank) * length + lax.rem(at_row[:1], length)
-    packed = lax.broadcasted_iota(jnp.int32, (slots * length, tokens), 0)
-    return (packed == target).astype(jnp.float32).astype(jnp.bfloat16)
-
-
-def pack_kernel(length, capacity, slots, ids, hidden, cot, send, id_buf, buf, packed, sems):
+    rank = jnp.sum(member * counts, axis=0, keepdims=True)
+    total = jnp.sum(member, axis=1, keepdims=True) * (1.0 / length)
+    lower = jnp.sum(jnp.where(kinds < ids_row, total, 0.0), axis=0, keepdims=True)
+    return rank.astype(jnp.int32), lower.astype(jnp.int32)
+
+
+def one_hot(target, rows):
+    wanted = lax.broadcasted_iota(jnp.int32, (rows, target.shape[1]), 0)
+    return (wanted == target).astype(jnp.float32).astype(jnp.bfloat16)
+
+
+def placements(ids_row, length, capacity, slots):
+    rank, lower = ranked(ids_row, length)
+    token = lax.rem(lax.broadcasted_iota(jnp.int32, ids_row.shape, 1), length)
+    place = rank + lower
+    group = lax.rem(place, 2)
+    per_core = capacity // 2
+    packed = ((ids_row * 2 + group) * per_core + rank // 2) * length + token
+    tokens = ids_row.shape[1]
+    ordered = group * (tokens // 2) + (place // 2) * length + token
+    return one_hot(packed, slots * length), one_hot(ordered, tokens)
+
+
+def pack_kernel(length, capacity, slots, ids, hidden, cot, *refs):
+    send, slabs, refs = refs[0], refs[1:5], refs[5:]
+    id_buf, buf, packed, ordered, turned, out_slabs, sems = refs
     groups, _, rows, part = send.shape
     tokens = hidden.shape[0] * length
+    slab = part // 2
+    half = tokens // 2
+    replica = lax.axis_index("dp")
     arriving = [
         pltpu.make_async_copy(source, target, sems.at[at])
         for at, (source, target) in enumerate(
@@ -235,33 +257,58 @@
     leaving = [
         pltpu.make_async_copy(packed.at[:, at], send.at[:, at], sems.at[3 + at]) for at in range(2)
     ]
+    sliding = [
+        pltpu.make_async_copy(out_slabs.at[at], slabs[at], sems.at[5 + at]) for at in range(4)
+    ]
     for copy in arriving:
         copy.start()
     arriving[0].wait()
-    ids_row = spread_ids(id_buf, (8, tokens), length)[:1]
-    place = placement(ids_row, length, capacity, slots)
+    ids_row = spread_ids(id_buf, (16, tokens), length)
+    by_slot, by_group = placements(ids_row[:1], length, capacity, slots)
+    for group in range(2):
+        mine = by_group[group * half : (group + 1) * half]
+        clusters = matmul(ids_row.astype(jnp.float32).astype(jnp.bfloat16), mine, TRANS_RHS)
+        turned[group] = jnp.concatenate(
+            [clusters.astype(jnp.bfloat16), jnp.zeros((16, 128 - half), jnp.bfloat16)], axis=1
+        )
     for which in range(2):
         arriving[1 + which].wait()
-        moved = matmul(place, buf[which].reshape(tokens, part)).astype(jnp.bfloat16)
+        flat = buf[which].reshape(tokens, part)
+        moved = matmul(by_slot, flat).astype(jnp.bfloat16)
         for group in range(groups):
             packed[group, which] = moved[group * rows : (group + 1) * rows]
         leaving[which].start()
-    for copy in leaving:
+        ordered[which] = matmul(by_group, flat).astype(jnp.bfloat16)
+    for turn in range(4):
+        pair = (turn // 2) ^ (replica & 1)
+        group = (turn % 2) ^ (replica >> 1)
+        cols = pl.ds(pl.multiple_of(pair * slab, slab), slab)
+        at = pl.ds(pl.multiple_of(group * half, half), half)
+        for which in range(2):
+            out_slabs[turn, which * half : (which + 1) * half] = ordered[which, at, cols]
+        out_slabs[turn, tokens:] = jnp.zeros((16, slab), jnp.bfloat16)
+        out_slabs[turn, tokens:, :128] = turned[group]
+        sliding[turn].start()
+    for copy in leaving + sliding:
         copy.wait()
 
 
-def slice_kernel(recv, _dn, _up, _gain, *outs):
-    experts, _, _, rows, part = recv.shape
-    slab = outs[0].shape[2]
-    place = lax.axis_index("dp")
-    per_half = part // slab
-    for step, out in enumerate(outs):
-        chip = place ^ step
-        half = chip // per_half
-        cols = pl.ds(pl.multiple_of((chip - half * per_half) * slab, slab), slab)
+def repack_kernel(length, capacity, *refs):
+    slabs, outs = refs[:4], refs[5:]
+    experts, rows = len(outs), outs[0].shape[2]
+    half = (slabs[0].shape[0] - 16) // 2
+    core, replica = lax.axis_index("segment"), lax.axis_index("dp")
+    for turn, slab in enumerate(slabs):
+        near = turn // 2 + 2 * ((turn % 2) ^ (replica >> 1) ^ core)
+        ids_row = slab[2 * half :, :128].astype(jnp.float32)[:1, :half].astype(jnp.int32)
+        rank, _ = ranked(ids_row, length)
+        token = lax.rem(lax.broadcasted_iota(jnp.int32, ids_row.shape, 1), length)
+        step = ids_row ^ lax.axis_index("expert")
+        place = one_hot((step * (capacity // 2) + rank) * length + token, experts * rows)
         for which in range(2):
+            moved = matmul(place, slab[which * half : (which + 1) * half]).astype(jnp.bfloat16)
             for e in range(experts):
-                out[which, e * rows : (e + 1) * rows] = recv[e, half, which, :, cols]
+                outs[e][which, near] = moved[e * rows : (e + 1) * rows]
 
 
 def unpack(sizes, id_buf, back, out):
@@ -269,7 +316,7 @@
     groups, rows, width = back.shape
     s_local = out.shape[0]
     ids_row = spread_ids(id_buf, (8, s_local * length), length)[:1]
-    place = placement(ids_row, length, capacity, slots)
+    place, _ = placements(ids_row, length, capacity, slots)
     moved = matmul(place, back[...].reshape(groups * rows, width), TRANS_LHS)
     out[...] = moved.astype(jnp.bfloat16).reshape(s_local, length, width)
 
@@ -305,8 +352,8 @@
 
 def chain_kernel(
     recv_in, own_dn, own_up, own_gain, other_dn, other_up, other_gain,
-    out, small,
-    recv, dn_buf, up_buf, gain_buf, entering, middle, d_norms, sems,
+    small, middle,
+    recv, dn_buf, up_buf, gain_buf, entering, d_norms, sems,
 ):
     phase = lax.axis_index("segment")
     experts, phases, _, rows, part = recv.shape
@@ -405,10 +452,6 @@
         d_norms[:, here] = d_norm
         total = total + lanes(d_norm)
         cross = cross + lanes(d_norm * ((wide - mean_1) * inverse_1))
-        leaving = (wide + matmul(act_1, up_buf[1, :, here])).astype(jnp.bfloat16)
-        half, start = col // part, col % part
-        for e in range(experts):
-            out[e, half, :, start : start + CHUNK] = leaving[e * rows : (e + 1) * rows]
     shift = row_sum(total) / width
     along = row_sum(cross) / width
     d_act = jnp.zeros((tokens, rank), jnp.float32)
@@ -426,15 +469,34 @@
     small[:, 4 * rank :] = side_by_side(moments, tokens)
 
 
-def join_kernel(pieces, *refs):
-    rows = refs[0].shape[0]
-    for at, piece in enumerate(refs[:pieces]):
-        refs[-1][at * rows : (at + 1) * rows] = piece[...]
-
-
-def gradient_kernel(sources, sizes, *refs):
-    slices, refs = refs[:sources], refs[sources:]
-    smalls, refs = refs[:2], refs[2:]
+def result_kernel(middle, small, own_up, other_up, out, up_buf, sem):
+    phase = lax.axis_index("segment")
+    experts, _, rows, part = out.shape
+    rank, width = up_buf.shape
+    copies = [pltpu.make_async_copy(source, up_buf, sem) for source in (own_up, other_up)]
+
+    @pl.when(phase == 1)
+    def _():
+        copies[0].start()
+
+    @pl.when(phase != 1)
+    def _():
+        copies[1].start()
+
+    copies[0].wait()
+    act = small[:, rank : 2 * rank]
+    for col in range(0, width, CHUNK):
+        here = slice(col, col + CHUNK)
+        leaving = middle[:, here].astype(jnp.float32) + matmul(act, up_buf[:, here])
+        leaving = leaving.astype(jnp.bfloat16)
+        half, start = col // part, col % part
+        for e in range(experts):
+            out[e, half, :, start : start + CHUNK] = leaving[e * rows : (e + 1) * rows]
+
+
+def gradient_kernel(experts, sources, sizes, *refs):
+    sides, refs = (refs[:experts], refs[experts : 2 * experts]), refs[2 * experts :]
+    smalls, refs = refs[:sources], refs[sources:]
     own, other, refs = refs[:3], refs[3:6], refs[6:]
     (ids, back, out_hidden, grad_dn, grad_upper, id_buf, dn_buf, up_buf, gain_buf, small, moments,
      lows, grads, ups, downs, sems) = refs
@@ -442,7 +504,8 @@
     id_copy.start()
     core = lax.axis_index("segment")
     place = lax.axis_index("dp")
-    _, rows, slab = slices[0].shape
+    _, replicas, _, slab = sides[0][0].shape
+    rows = smalls[0].shape[0]
     rank = dn_buf.shape[1]
     features = pl.ds(pl.multiple_of(place * slab, slab), slab)
 
@@ -468,8 +531,19 @@
         for copy in copies(other[1], other[2], own[0], own[2]):
             copy.start()
 
-    for core_at, source in enumerate(smalls):
-        small[core_at * source.shape[0] : (core_at + 1) * source.shape[0]] = source[...]
+    per_expert = rows // experts
+    for source in range(sources):
+        for step in range(experts):
+            to = source * rows + step * per_expert
+            start = (lax.axis_index("expert") ^ step) * per_expert
+            small[to : to + per_expert] = smalls[source][
+                pl.ds(pl.multiple_of(start, per_expert), per_expert)
+            ]
+
+    def sliced(source, which, here):
+        side, near = sides[source // replicas], source % replicas
+        return jnp.concatenate([side[e][which, near, :, here] for e in range(experts)], axis=0)
+
     id_copy.wait()
     unpack(sizes, id_buf, back, out_hidden)
     held = lax.broadcasted_iota(jnp.int32, (128, 6 * 128), 0)
@@ -495,7 +569,7 @@
             downs[...] = matmul(small[:, 3 * rank : 4 * rank], dn_buf[here, :], TRANS_RHS)
             for source in range(sources):
                 at = slice(source * rows, (source + 1) * rows)
-                wide = slices[source][0, :, here].astype(jnp.float32)
+                wide = sliced(source, 0, here).astype(jnp.float32)
                 normed = (wide - moment(at, 0)) * moment(at, 1)
                 lows[at, here] = (normed * scales[0]).astype(jnp.bfloat16)
                 middle = (wide + ups[at]).astype(jnp.bfloat16).astype(jnp.float32)
@@ -503,7 +577,7 @@
                 normed = (middle - moment(at, 2)) * inverse
                 d_norm = downs[at] * scales[1]
                 grads[at, here] = (
-                    slices[source][1, :, here].astype(jnp.float32)
+                    sliced(source, 1, here).astype(jnp.float32)
                     + inverse * (d_norm - moment(at, 4) - normed * moment(at, 5))
                 ).astype(jnp.bfloat16)
 
@@ -511,11 +585,11 @@
         def _():
             for source in range(sources):
                 at = slice(source * rows, (source + 1) * rows)
-                wide = slices[source][0, :, here].astype(jnp.float32)
+                wide = sliced(source, 0, here).astype(jnp.float32)
                 middle = (wide + ups[at]).astype(jnp.bfloat16).astype(jnp.float32)
                 normed = (middle - moment(at, 2)) * moment(at, 3)
                 lows[at, here] = (normed * scales[1]).astype(jnp.bfloat16)
-                grads[at, here] = slices[source][1, :, here]
+                grads[at, here] = sliced(source, 1, here)
 
     def finish(act, d_pre):
         for col in range(0, slab, columns):
@@ -553,6 +627,15 @@
 def across(block, axis, distance):
     size = lax.axis_size(axis)
     return lax.ppermute(block, axis, [(i, i ^ distance) for i in range(size)])
+
+
+def slab_route(replicas, pair, low):
+    route = []
+    for replica in range(replicas):
+        for core in range(2):
+            chip = 2 * core + ((replica & 1) ^ pair)
+            route.append((2 * replica + core, 2 * chip + ((replica >> 1) ^ low)))
+    return route
 
 
 def on_device_two_phases(hidden_in, cotangent, cluster_ids, w_down, w_up, gain):
@@ -572,45 +655,53 @@
     sizes = (length, capacity, slots)
     sections = ("expert", "segment")
 
-    other = tuple(across(array, "segment", 1) for array in own)
-    (send,) = call(
+    other_dn = across(own[0], "segment", 1)
+    half = s_local * length // 2
+    send, *slabs = call(
         functools.partial(pack_kernel, *sizes),
         "pack",
-        56,
+        60,
         [HBM] * 3,
-        [((groups, 2, rows, part), bf16)],
+        [((groups, 2, rows, part), bf16)] + [((2 * half + 16, slab), bf16)] * 4,
         [
             pltpu.SMEM(cluster_ids.shape, jnp.int32),
             pltpu.VMEM((2,) + hidden_in.shape, bf16),
             pltpu.VMEM((groups, 2, rows, part), bf16),
-            pltpu.SemaphoreType.DMA((5,)),
+            pltpu.VMEM((2, 2 * half, part), bf16),
+            pltpu.VMEM((2, 16, 128), bf16),
+            pltpu.VMEM((4, 2 * half + 16, slab), bf16),
+            pltpu.SemaphoreType.DMA((9,)),
         ],
         outs_in=HBM,
     )(cluster_ids, hidden_in, cotangent)
     recv = lax.all_to_all(send, sections, split_axis=0, concat_axis=0, tiled=True)
     recv = recv.reshape(experts, 2, 2, rows, part)
-
-    def gathered(blocks):
-        near = [blocks[0]] + [across(blocks[step], "dp", step) for step in range(1, replicas)]
-        return near + [across(piece, "segment", 1) for piece in near]
-
-    slices = gathered(
-        call(
-            slice_kernel, "slices", 8, [VMEM] + [HBM] * 3, [((2, tokens, slab), bf16)] * replicas
-        )(recv, *other)
-    )
-    out, small = call(
+    recv, up, scale = lax.optimization_barrier((recv, own[1], own[2]))
+    other = (other_dn, across(up, "segment", 1), across(scale, "segment", 1))
+    slabs = [
+        lax.ppermute(block, ("dp", "segment"), slab_route(replicas, turn // 2, turn % 2))
+        for turn, block in enumerate(slabs)
+    ]
+    slices = call(
+        functools.partial(repack_kernel, length, capacity),
+        "repack",
+        60,
+        [VMEM] * 4 + [HBM],
+        [((2, replicas, rows, slab), bf16)] * experts,
+    )(*slabs, recv)
+    mine = [slices[0]] + [across(slices[step], "expert", step) for step in range(1, experts)]
+
+    small, middle = call(
         chain_kernel,
         "chain",
         60,
         [HBM] * 7,
-        [((experts, 2, rows, part), bf16), ((tokens, 4 * rank + 128), bf16)],
+        [((tokens, 4 * rank + 128), bf16), ((tokens, width), bf16)],
         [
             pltpu.VMEM(recv.shape, bf16),
             pltpu.VMEM((2, width, rank), bf16),
             pltpu.VMEM((2, rank, width), bf16),
             pltpu.VMEM((2, 1, width), bf16),
-            pltpu.VMEM((tokens, width), bf16),
             pltpu.VMEM((tokens, width), bf16),
             pltpu.VMEM((tokens, width), f32),
             pltpu.SemaphoreType.DMA((3, 3)),
@@ -618,27 +709,30 @@
         flops=7 * 2 * tokens * width * rank,
         moved=10 * MIB,
     )(recv, *own, *other)
+    mine, small, middle = lax.optimization_barrier((mine, small, middle))
+    theirs = [across(block, "segment", 1) for block in mine]
+    near = [small] + [across(small, "dp", step) for step in range(1, replicas)]
+    smalls = near + [across(piece, "segment", 1) for piece in near]
+
+    (out,) = call(
+        result_kernel,
+        "results",
+        60,
+        [VMEM] * 2 + [HBM] * 2,
+        [((experts, 2, rows, part), bf16)],
+        [pltpu.VMEM((rank, width), bf16), pltpu.SemaphoreType.DMA],
+    )(middle, small, own[1], other[1])
     back = lax.all_to_all(
         out.reshape(groups, rows, part), sections, split_axis=0, concat_axis=0, tiled=True
     )
-    two_away = across(small, "dp", 2)
-    near = [small, across(small, "dp", 1), two_away, across(two_away, "dp", 1)]
-    waited = slices[replicas:] + [back]
-    (joined,) = call(
-        functools.partial(join_kernel, replicas),
-        "join",
-        60,
-        [VMEM] * replicas + [HBM] * len(waited),
-        [((replicas * tokens, 4 * rank + 128), bf16)],
-    )(*near, *waited)
-    smalls = (joined, across(joined, "segment", 1))
+
     sources = 2 * replicas
     all_tokens = sources * tokens
     out_hidden, grad_dn, grad_upper = call(
-        functools.partial(gradient_kernel, sources, sizes),
+        functools.partial(gradient_kernel, experts, sources, sizes),
         "gradients",
         60,
-        [VMEM] * (sources + 2) + [HBM] * 7 + [VMEM],
+        [VMEM] * (2 * experts + sources) + [HBM] * 7 + [VMEM],
         [(hidden_in.shape, bf16), ((slab, rank), bf16), ((rank, slab), bf16)],
         [
             pltpu.SMEM(cluster_ids.shape, jnp.int32),
@@ -653,7 +747,7 @@
             pltpu.VMEM((all_tokens, 256), f32),
             pltpu.SemaphoreType.DMA((5,)),
         ],
-    )(*slices, *smalls, *own, *other, cluster_ids, back)
+    )(*mine, *theirs, *smalls, *own, *other, cluster_ids, back)
     return (out_hidden, grad_dn[None, None], grad_upper[None, None])
 
 

time: 79.5 us -> 96.7 us (1.22)
  starting transfers between devices: 19.4 us -> 32.5 us
  Pallas kernels: 22.6 us -> 27.1 us
  local copies, waits for them, and re-layouts: 3.33 us -> 2.09 us
  waiting for transfers between devices: 32.5 us -> 33.6 us
    ppermute x0 -> x4, starting transfers between devices: none -> 12.1 us  [on_device_two_phases(): lax.ppermute(block, ('dp', 'segment'), slab_route(replicas, turn // 2, tu...]
    ppermute x0 -> x4, waiting for transfers between devices: none -> 6.62 us  [on_device_two_phases(): lax.ppermute(block, ('dp', 'segment'), slab_route(replicas, turn // 2, tu...]
    ppermute x14 -> x17, waiting for transfers between devices: 18.5 us -> 12.1 us  [across(): return lax.ppermute(block, axis, [(i, i ^ distance) for i in range(size)])]
    pallas_call x5, Pallas kernels: 22.6 us -> 27.1 us  [the longest x1 9.05 us: on_device_two_phases(): call(chain_kernel, 'chain', 60, [HBM] * 7, [((tokens, 4 * rank + 128), bf...]
    unnamed x34 -> x54, local copies, waits for them, and re-layouts: 3.33 us -> 2.09 us
    ppermute x14 -> x17, starting transfers between devices: 10.7 us -> 11.6 us  [across(): return lax.ppermute(block, axis, [(i, i ^ distance) for i in range(size)])]
  transfers between devices with their start and end apart: 16 -> 23, of which waited for: 6 -> 9; matrix products, arithmetic and copies ran while one was open for 0% -> 0% of each run, Pallas kernels for 15% -> 13%
where the time goes in v7:
time: 96.7 us; the launch traced here: 96.3 us
  waiting for transfers between devices  33.6 us (35%)
  starting transfers between devices  32.5 us (34%)
  Pallas kernels  27.1 us (28%)
  local copies, waits for them, and re-layouts  2.09 us (2%)
    all_to_all x1, waiting for transfers between devices, on_device_two_phases(): lax.all_to_all(send, sections, split_axis=0, concat_axis=0, tiled=True)  14.9 us
    ppermute x17, waiting for transfers between devices, across(): return lax.ppermute(block, axis, [(i, i ^ distance) for i in range(size)])  12.1 us
    ppermute x4, starting transfers between devices, on_device_two_phases(): lax.ppermute(block, ('dp', 'segment'), slab_route(replicas, turn // 2, tu...  12.1 us
    ppermute x17, starting transfers between devices, across(): return lax.ppermute(block, axis, [(i, i ^ distance) for i in range(size)])  11.6 us
    pallas_call x1, Pallas kernels, on_device_two_phases(): call(chain_kernel, 'chain', 60, [HBM] * 7, [((tokens, 4 * rank + 128), bf...  9.05 us
    pallas_call x1, Pallas kernels, on_device_two_phases(): call(functools.partial(gradient_kernel, experts, sources, sizes), 'gradie...  7.99 us
    ppermute x4, waiting for transfers between devices, on_device_two_phases(): lax.ppermute(block, ('dp', 'segment'), slab_route(replicas, turn // 2, tu...  6.62 us
    all_to_all x1, starting transfers between devices, on_device_two_phases(): lax.all_to_all(send, sections, split_axis=0, concat_axis=0, tiled=True)  5.31 us
  transfers between devices with their start and end apart: 23, of which 9 were waited for; matrix products, arithmetic and copies ran while one was open for 0% of the time, Pallas kernels for 13%

profile of v7, /device:TPU:0, one launch (start us, length us, event | category | flops | bytes accessed | tf_op | source)
XLA Modules:
  0.0 96.3 jit_solution(839505534276117649)
XLA Ops:
  0.7 2.8 %pack.1 = (bf16[8,2,16,2048]{3,2,1,0:T(8,128)(2,1)}, bf16[80,1024]{1,0:T(8,128)(2,1)}, bf16[80,1024]{1,0:T(8,128)(2,1)}, bf16[80,1024]{1,0:T(8,128)(2,1)}, bf16[80,1024]{1,0:T(8,128)(2,1)}) custom-call(s32[16]{0:T(128)} %refs_22_.1, bf16[16,4,2048]{2,1,0:T(4,128)(2,1)} %hidden.1, bf16[16,4,2048]{2,1,0:T(4,128)(2,1)} %cot.1), custom_call_target="tpu_custom_call" | custom-call | bytes 1048576 | tf_op jit(solution)/shard_map/pack/pallas_call | solution.py:660
  3.5 5.3 %all-to-all-start = ((bf16[8,2,16,2048]{3,2,1,0:T(8,128)(2,1)}), bf16[8,2,16,2048]{3,2,1,0:T(8,128)(2,1)S(1)}, u32[]{:S(2)}, u32[]{:S(2)}) async-start(bf16[8,2,16,2048]{3,2,1,0:T(8,128)(2,1)} %get-tuple-element.30), calls=%async_computation | async-start | bytes 2097152 | tf_op jit(solution)/shard_map/all_to_all | solution.py:677
  8.8 0.5 collective-permute-start.7
  9.3 14.9 %all-to-all-done = bf16[8,2,16,2048]{3,2,1,0:T(8,128)(2,1)S(1)} async-done(((bf16[8,2,16,2048]{3,2,1,0:T(8,128)(2,1)}), bf16[8,2,16,2048]{3,2,1,0:T(8,128)(2,1)S(1)}, u32[]{:S(2)}, u32[]{:S(2)}) %all-to-all-start) | async-done | bytes 1048608 | tf_op jit(solution)/shard_map/all_to_all | solution.py:677
  24.2 0.7 collective-permute-start
  24.9 4.0 %collective-permute-start.1 = (bf16[80,1024]{1,0:T(8,128)(2,1)}, bf16[80,1024]{1,0:T(8,128)(2,1)S(1)}, u32[]{:S(2)}, u32[]{:S(2)}) collective-permute-start(bf16[80,1024]{1,0:T(8,128)(2,1)} %get-tuple-element.27), channel_id=1, source_target_pairs={{0,1},{1,5},{2,3},{3,7},{4,0},{5,4},{6,2},{7,6},{8,9},{9,13},{10,1... | collective-permute-start | bytes 491528 | tf_op jit(solution)/shard_map/ppermute | solution.py:682
  28.9 1.6 %collective-permute-start.2 = (bf16[80,1024]{1,0:T(8,128)(2,1)}, bf16[80,1024]{1,0:T(8,128)(2,1)S(1)}, u32[]{:S(2)}, u32[]{:S(2)}) collective-permute-start(bf16[80,1024]{1,0:T(8,128)(2,1)} %get-tuple-element.28), channel_id=1, source_target_pairs={{0,2},{1,6},{2,0},{3,4},{4,3},{5,7},{6,1},{7,5},{8,10},{9,14},{10,... | collective-permute-start | bytes 491528 | tf_op jit(solution)/shard_map/ppermute | solution.py:682
  30.5 5.8 %collective-permute-start.3 = (bf16[80,1024]{1,0:T(8,128)(2,1)S(1)}, bf16[80,1024]{1,0:T(8,128)(2,1)S(1)}, u32[]{:S(2)}, u32[]{:S(2)}) collective-permute-start(bf16[80,1024]{1,0:T(8,128)(2,1)S(1)} %copy-done.25), channel_id=1, source_target_pairs={{0,3},{1,7},{2,1},{3,5},{4,2},{5,6},{6,0},{7,4},{8,11},{9,15},{10,... | collective-permute-start | bytes 491528 | tf_op jit(solution)/shard_map/ppermute | solution.py:682
  36.3 2.3 %collective-permute-done.1.refs_1_ = bf16[80,1024]{1,0:T(8,128)(2,1)S(1)} collective-permute-done((bf16[80,1024]{1,0:T(8,128)(2,1)}, bf16[80,1024]{1,0:T(8,128)(2,1)S(1)}, u32[]{:S(2)}, u32[]{:S(2)}) %collective-permute-start.1) | collective-permute-done | bytes 163872 | tf_op jit(solution)/shard_map/ppermute | solution.py:682
  38.6 4.4 %collective-permute-done.3.refs_3_ = bf16[80,1024]{1,0:T(8,128)(2,1)S(1)} collective-permute-done((bf16[80,1024]{1,0:T(8,128)(2,1)S(1)}, bf16[80,1024]{1,0:T(8,128)(2,1)S(1)}, u32[]{:S(2)}, u32[]{:S(2)}) %collective-permute-start.3) | collective-permute-done | bytes 163872 | tf_op jit(solution)/shard_map/ppermute | solution.py:682
  43.0 0.6 copy-done.15
  43.6 3.0 %repack.1 = (bf16[2,4,16,1024]{3,2,1,0:T(8,128)(2,1)}, bf16[2,4,16,1024]{3,2,1,0:T(8,128)(2,1)}, bf16[2,4,16,1024]{3,2,1,0:T(8,128)(2,1)}, bf16[2,4,16,1024]{3,2,1,0:T(8,128)(2,1)}) custom-call(bf16[80,1024]{1,0:T(8,128)(2,1)} %copy-done.12, bf16[80,1024]{1,0:T(8,128)(2,1)} %copy-done.13, bf16[80,1024]{1,0:T(8,128)(2,1)} %copy-done.14, ...), custom_call_target="tpu_custom_call" | custom-call | bytes 1048576 | tf_op jit(solution)/shard_map/repack/pallas_call | solution.py:685
  46.7 0.6 collective-permute-start.4
  47.3 0.6 collective-permute-start.5
  47.9 2.3 %collective-permute-start.6 = (bf16[2,4,16,1024]{3,2,1,0:T(8,128)(2,1)}, bf16[2,4,16,1024]{3,2,1,0:T(8,128)(2,1)S(1)}, u32[]{:S(2)}, u32[]{:S(2)}) collective-permute-start(bf16[2,4,16,1024]{3,2,1,0:T(8,128)(2,1)} %get-tuple-element.35), channel_id=1, source_target_pairs={{0,24},{8,16},{16,8},{24,0},{1,25},{9,17},{17,9},{25,1},{2,26},{10... | collective-permute-start | bytes 786440 | tf_op jit(solution)/shard_map/ppermute | solution.py:629
  50.2 9.0 %chain.1 = (bf16[64,1152]{1,0:T(8,128)(2,1)}, bf16[64,4096]{1,0:T(8,128)(2,1)}) custom-call(bf16[4,2,2,16,2048]{4,3,2,1,0:T(8,128)(2,1)} %bitcast.12, bf16[4096,256]{1,0:T(8,128)(2,1)} %bitcast.14, bf16[256,4096]{1,0:T(8,128)(2,1)} %bitcast.7, bf16[1,4096]{1,0:T(2,128)(2,1)} %bitcast.17, bf16[4096,256]{1,0:T(8,128)(2,1)} %collective-permute-done.7.other_dn.refs_19_, ...), custom_call_target="tpu_custom_call" | custom-call | flops 939524096 | bytes 10485760 | tf_op jit(solution)/shard_map/chain/pallas_call | solution.py:694
  59.3 4.2 %results.1 = bf16[4,2,16,2048]{3,2,1,0:T(8,128)(2,1)} custom-call(bf16[64,4096]{1,0:T(8,128)(2,1)} %get-tuple-element.45.middle, bf16[64,1152]{1,0:T(8,128)(2,1)} %get-tuple-element.44.small.refs_8_, bf16[256,4096]{1,0:T(8,128)(2,1)} %bitcast.8, bf16[256,4096]{1,0:T(8,128)(2,1)} %collective-permute-done.8.other_up.refs_20_), custom_call_target="tpu_custom_call" | custom-call | bytes 1048576 | tf_op jit(solution)/shard_map/results/pallas_call | solution.py:717
  63.6 3.5 %all-to-all-start.1 = ((bf16[8,16,2048]{2,1,0:T(8,128)(2,1)}), bf16[8,16,2048]{2,1,0:T(8,128)(2,1)S(1)}, u32[]{:S(2)}, u32[]{:S(2)}) async-start(bf16[8,16,2048]{2,1,0:T(8,128)(2,1)} %bitcast.16), calls=%async_computation.1 | async-start | bytes 1048576 | tf_op jit(solution)/shard_map/all_to_all | solution.py:725
  67.1 0.4 collective-permute-start.17
  67.5 3.3 %collective-permute-start.16 = (bf16[64,1152]{1,0:T(8,128)(2,1)S(1)}, bf16[64,1152]{1,0:T(8,128)(2,1)S(1)}, u32[]{:S(2)}, u32[]{:S(2)}) collective-permute-start(bf16[64,1152]{1,0:T(8,128)(2,1)S(1)} %copy-done.3), channel_id=1, source_target_pairs={{0,6},{2,4},{4,2},{6,0},{1,7},{3,5},{5,3},{7,1},{8,14},{10,12},{12... | collective-permute-start | bytes 442376 | tf_op jit(solution)/shard_map/ppermute | solution.py:629
  70.8 1.8 %collective-permute-start.15 = (bf16[64,1152]{1,0:T(8,128)(2,1)S(1)}, bf16[64,1152]{1,0:T(8,128)(2,1)S(1)}, u32[]{:S(2)}, u32[]{:S(2)}) collective-permute-start(bf16[64,1152]{1,0:T(8,128)(2,1)S(1)} %copy-done.3), channel_id=1, source_target_pairs={{0,4},{2,6},{4,0},{6,2},{1,5},{3,7},{5,1},{7,3},{8,12},{10,14},{12... | collective-permute-start | bytes 442376 | tf_op jit(solution)/shard_map/ppermute | solution.py:629
  72.6 0.5 collective-permute-start.11
  73.2 0.6 collective-permute-start.14
  73.7 1.6 %collective-permute-done.16.refs_11_ = bf16[64,1152]{1,0:T(8,128)(2,1)S(1)} collective-permute-done((bf16[64,1152]{1,0:T(8,128)(2,1)S(1)}, bf16[64,1152]{1,0:T(8,128)(2,1)S(1)}, u32[]{:S(2)}, u32[]{:S(2)}) %collective-permute-start.16) | collective-permute-done | bytes 147488 | tf_op jit(solution)/shard_map/ppermute | solution.py:629
  75.3 9.4 %collective-permute-done.15.refs_10_ = bf16[64,1152]{1,0:T(8,128)(2,1)S(1)} collective-permute-done((bf16[64,1152]{1,0:T(8,128)(2,1)S(1)}, bf16[64,1152]{1,0:T(8,128)(2,1)S(1)}, u32[]{:S(2)}, u32[]{:S(2)}) %collective-permute-start.15) | collective-permute-done | bytes 147488 | tf_op jit(solution)/shard_map/ppermute | solution.py:629
  84.8 0.4 collective-permute-start.20
  85.3 0.4 collective-permute-start.18
  85.7 0.5 collective-permute-done.13.refs_7_
  86.2 0.2 collective-permute-done.20.refs_15_
  87.1 0.2 copy-done.21
  87.5 0.8 copy-done.2
  88.3 8.0 %gradients.1 = (bf16[16,4,2048]{2,1,0:T(4,128)(2,1)}, bf16[1024,256]{1,0:T(8,128)(2,1)}, bf16[256,1024]{1,0:T(8,128)(2,1)}) custom-call(bf16[2,4,16,1024]{3,2,1,0:T(8,128)(2,1)} %get-tuple-element.40.refs_0_, bf16[2,4,16,1024]{3,2,1,0:T(8,128)(2,1)} %copy-done.5, bf16[2,4,16,1024]{3,2,1,0:T(8,128)(2,1)} %copy-done.6, bf16[2,4,16,1024]{3,2,1,0:T(8,128)(2,1)} %copy-done.7, ...), custom_call_target="tpu_custom_call" | custom-call | bytes 1048576 | tf_op jit(solution)/shard_map/gradients/pallas_call | solution.py:731
  (73 shorter events, 1.1 us)
Async XLA Ops:
  0.6 38.0 %copy-start.23 = (bf16[1,1,4096]{2,1,0:T(2,128)(2,1)S(1)}, bf16[1,1,4096]{2,1,0:T(2,128)(2,1)}, u32[]{:S(2)}) copy-start(bf16[1,1,4096]{2,1,0:T(2,128)(2,1)} %param.11) | copy-start | bytes 24580
  0.6 23.6 %copy-start = (bf16[1,1,256,4096]{3,2,1,0:T(8,128)(2,1)S(1)}, bf16[1,1,256,4096]{3,2,1,0:T(8,128)(2,1)}, u32[]{:S(2)}) copy-start(bf16[1,1,256,4096]{3,2,1,0:T(8,128)(2,1)} %param.10) | copy-start | bytes 6291460
  3.5 20.8 %copy-start.26 = (bf16[80,1024]{1,0:T(8,128)(2,1)S(1)}, bf16[80,1024]{1,0:T(8,128)(2,1)}, u32[]{:S(2)}) copy-start(bf16[80,1024]{1,0:T(8,128)(2,1)} %get-tuple-element.26) | copy-start | bytes 491524
  3.5 27.0 %copy-start.25 = (bf16[80,1024]{1,0:T(8,128)(2,1)S(1)}, bf16[80,1024]{1,0:T(8,128)(2,1)}, u32[]{:S(2)}) copy-start(bf16[80,1024]{1,0:T(8,128)(2,1)} %get-tuple-element.29) | copy-start | bytes 491524
  3.5 20.7 %all-to-all-start = ((bf16[8,2,16,2048]{3,2,1,0:T(8,128)(2,1)}), bf16[8,2,16,2048]{3,2,1,0:T(8,128)(2,1)S(1)}, u32[]{:S(2)}, u32[]{:S(2)}) async-start(bf16[8,2,16,2048]{3,2,1,0:T(8,128)(2,1)} %get-tuple-element.30), calls=%async_computation | async-start | bytes 2097152 | tf_op jit(solution)/shard_map/all_to_all | solution.py:677
  8.8 41.4 %collective-permute-start.7 = (bf16[4096,256]{1,0:T(8,128)(2,1)}, bf16[4096,256]{1,0:T(8,128)(2,1)}, u32[]{:S(2)}, u32[]{:S(2)}) collective-permute-start(bf16[4096,256]{1,0:T(8,128)(2,1)} %bitcast.13), channel_id=1, source_target_pairs={{0,1},{1,0},{2,3},{3,2},{4,5},{5,4},{6,7},{7,6},{8,9},{9,8},{10,11... | collective-permute-start | bytes 6291464 | tf_op jit(solution)/shard_map/ppermute | solution.py:629
  24.2 18.8 %copy-start.1 = (bf16[8,2,16,2048]{3,2,1,0:T(8,128)(2,1)}, bf16[8,2,16,2048]{3,2,1,0:T(8,128)(2,1)S(1)}, u32[]{:S(2)}) copy-start(bf16[8,2,16,2048]{3,2,1,0:T(8,128)(2,1)S(1)} %all-to-all-done) | copy-start | bytes 3145732
  24.2 26.0 %collective-permute-start.8 = (bf16[256,4096]{1,0:T(8,128)(2,1)S(1)}, bf16[256,4096]{1,0:T(8,128)(2,1)}, u32[]{:S(2)}, u32[]{:S(2)}) collective-permute-start(bf16[256,4096]{1,0:T(8,128)(2,1)S(1)} %bitcast.10), channel_id=1, source_target_pairs={{0,1},{1,0},{2,3},{3,2},{4,5},{5,4},{6,7},{7,6},{8,9},{9,8},{10,11... | collective-permute-start | bytes 6291464 | tf_op jit(solution)/shard_map/ppermute | solution.py:629
  24.2 6.3 %collective-permute-start = (bf16[80,1024]{1,0:T(8,128)(2,1)S(1)}, bf16[80,1024]{1,0:T(8,128)(2,1)S(1)}, u32[]{:S(2)}, u32[]{:S(2)}) collective-permute-start(bf16[80,1024]{1,0:T(8,128)(2,1)S(1)} %copy-done.26), channel_id=1, source_target_pairs={{0,0},{1,4},{2,2},{3,6},{4,1},{5,5},{6,3},{7,7},{8,8},{9,12},{10,1... | collective-permute-start | bytes 491528 | tf_op jit(solution)/shard_map/ppermute | solution.py:682
  24.9 13.7 %collective-permute-start.1 = (bf16[80,1024]{1,0:T(8,128)(2,1)}, bf16[80,1024]{1,0:T(8,128)(2,1)S(1)}, u32[]{:S(2)}, u32[]{:S(2)}) collective-permute-start(bf16[80,1024]{1,0:T(8,128)(2,1)} %get-tuple-element.27), channel_id=1, source_target_pairs={{0,1},{1,5},{2,3},{3,7},{4,0},{5,4},{6,2},{7,6},{8,9},{9,13},{10,1... | collective-permute-start | bytes 491528 | tf_op jit(solution)/shard_map/ppermute | solution.py:682
  28.9 9.7 %collective-permute-start.2 = (bf16[80,1024]{1,0:T(8,128)(2,1)}, bf16[80,1024]{1,0:T(8,128)(2,1)S(1)}, u32[]{:S(2)}, u32[]{:S(2)}) collective-permute-start(bf16[80,1024]{1,0:T(8,128)(2,1)} %get-tuple-element.28), channel_id=1, source_target_pairs={{0,2},{1,6},{2,0},{3,4},{4,3},{5,7},{6,1},{7,5},{8,10},{9,14},{10,... | collective-permute-start | bytes 491528 | tf_op jit(solution)/shard_map/ppermute | solution.py:682
  30.5 12.5 %collective-permute-start.3 = (bf16[80,1024]{1,0:T(8,128)(2,1)S(1)}, bf16[80,1024]{1,0:T(8,128)(2,1)S(1)}, u32[]{:S(2)}, u32[]{:S(2)}) collective-permute-start(bf16[80,1024]{1,0:T(8,128)(2,1)S(1)} %copy-done.25), channel_id=1, source_target_pairs={{0,3},{1,7},{2,1},{3,5},{4,2},{5,6},{6,0},{7,4},{8,11},{9,15},{10,... | collective-permute-start | bytes 491528 | tf_op jit(solution)/shard_map/ppermute | solution.py:682
  38.6 9.3 %collective-permute-start.9 = (bf16[1,4096]{1,0:T(2,128)(2,1)S(1)}, bf16[1,4096]{1,0:T(2,128)(2,1)S(1)}, u32[]{:S(2)}, u32[]{:S(2)}) collective-permute-start(bf16[1,4096]{1,0:T(2,128)(2,1)S(1)} %bitcast.19), channel_id=1, source_target_pairs={{0,1},{1,0},{2,3},{3,2},{4,5},{5,4},{6,7},{7,6},{8,9},{9,8},{10,11... | collective-permute-start | bytes 24584 | tf_op jit(solution)/shard_map/ppermute | solution.py:629
  46.7 12.6 %collective-permute-start.4 = (bf16[2,4,16,1024]{3,2,1,0:T(8,128)(2,1)}, bf16[2,4,16,1024]{3,2,1,0:T(8,128)(2,1)S(1)}, u32[]{:S(2)}, u32[]{:S(2)}) collective-permute-start(bf16[2,4,16,1024]{3,2,1,0:T(8,128)(2,1)} %get-tuple-element.33), channel_id=1, source_target_pairs={{0,8},{8,0},{16,24},{24,16},{1,9},{9,1},{17,25},{25,17},{2,10},{10... | collective-permute-start | bytes 786440 | tf_op jit(solution)/shard_map/ppermute | solution.py:629
  47.3 12.0 %collective-permute-start.5 = (bf16[2,4,16,1024]{3,2,1,0:T(8,128)(2,1)}, bf16[2,4,16,1024]{3,2,1,0:T(8,128)(2,1)S(1)}, u32[]{:S(2)}, u32[]{:S(2)}) collective-permute-start(bf16[2,4,16,1024]{3,2,1,0:T(8,128)(2,1)} %get-tuple-element.34), channel_id=1, source_target_pairs={{0,16},{8,24},{16,0},{24,8},{1,17},{9,25},{17,1},{25,9},{2,18},{10... | collective-permute-start | bytes 786440 | tf_op jit(solution)/shard_map/ppermute | solution.py:629
  47.9 11.4 %collective-permute-start.6 = (bf16[2,4,16,1024]{3,2,1,0:T(8,128)(2,1)}, bf16[2,4,16,1024]{3,2,1,0:T(8,128)(2,1)S(1)}, u32[]{:S(2)}, u32[]{:S(2)}) collective-permute-start(bf16[2,4,16,1024]{3,2,1,0:T(8,128)(2,1)} %get-tuple-element.35), channel_id=1, source_target_pairs={{0,24},{8,16},{16,8},{24,0},{1,25},{9,17},{17,9},{25,1},{2,26},{10... | collective-permute-start | bytes 786440 | tf_op jit(solution)/shard_map/ppermute | solution.py:629
  59.3 13.4 %copy-start.5 = (bf16[2,4,16,1024]{3,2,1,0:T(8,128)(2,1)}, bf16[2,4,16,1024]{3,2,1,0:T(8,128)(2,1)S(1)}, u32[]{:S(2)}) copy-start(bf16[2,4,16,1024]{3,2,1,0:T(8,128)(2,1)S(1)} %collective-permute-done.4.refs_1_) | copy-start | bytes 786436
  59.3 16.0 %copy-start.6 = (bf16[2,4,16,1024]{3,2,1,0:T(8,128)(2,1)}, bf16[2,4,16,1024]{3,2,1,0:T(8,128)(2,1)S(1)}, u32[]{:S(2)}) copy-start(bf16[2,4,16,1024]{3,2,1,0:T(8,128)(2,1)S(1)} %collective-permute-done.5.refs_2_) | copy-start | bytes 786436
  59.3 25.4 %copy-start.7 = (bf16[2,4,16,1024]{3,2,1,0:T(8,128)(2,1)}, bf16[2,4,16,1024]{3,2,1,0:T(8,128)(2,1)S(1)}, u32[]{:S(2)}) copy-start(bf16[2,4,16,1024]{3,2,1,0:T(8,128)(2,1)S(1)} %collective-permute-done.6.refs_3_) | copy-start | bytes 786436
  63.6 23.3 %all-to-all-start.1 = ((bf16[8,16,2048]{2,1,0:T(8,128)(2,1)}), bf16[8,16,2048]{2,1,0:T(8,128)(2,1)S(1)}, u32[]{:S(2)}, u32[]{:S(2)}) async-start(bf16[8,16,2048]{2,1,0:T(8,128)(2,1)} %bitcast.16), calls=%async_computation.1 | async-start | bytes 1048576 | tf_op jit(solution)/shard_map/all_to_all | solution.py:725
  67.1 6.1 %collective-permute-start.17 = (bf16[64,1152]{1,0:T(8,128)(2,1)S(1)}, bf16[64,1152]{1,0:T(8,128)(2,1)S(1)}, u32[]{:S(2)}, u32[]{:S(2)}) collective-permute-start(bf16[64,1152]{1,0:T(8,128)(2,1)S(1)} %copy-done.3), channel_id=1, source_target_pairs={{0,1},{1,0},{2,3},{3,2},{4,5},{5,4},{6,7},{7,6},{8,9},{9,8},{10,11... | collective-permute-start | bytes 442376 | tf_op jit(solution)/shard_map/ppermute | solution.py:629
  67.5 7.8 %collective-permute-start.16 = (bf16[64,1152]{1,0:T(8,128)(2,1)S(1)}, bf16[64,1152]{1,0:T(8,128)(2,1)S(1)}, u32[]{:S(2)}, u32[]{:S(2)}) collective-permute-start(bf16[64,1152]{1,0:T(8,128)(2,1)S(1)} %copy-done.3), channel_id=1, source_target_pairs={{0,6},{2,4},{4,2},{6,0},{1,7},{3,5},{5,3},{7,1},{8,14},{10,12},{12... | collective-permute-start | bytes 442376 | tf_op jit(solution)/shard_map/ppermute | solution.py:629
  70.8 13.9 %collective-permute-start.15 = (bf16[64,1152]{1,0:T(8,128)(2,1)S(1)}, bf16[64,1152]{1,0:T(8,128)(2,1)S(1)}, u32[]{:S(2)}, u32[]{:S(2)}) collective-permute-start(bf16[64,1152]{1,0:T(8,128)(2,1)S(1)} %copy-done.3), channel_id=1, source_target_pairs={{0,4},{2,6},{4,0},{6,2},{1,5},{3,7},{5,1},{7,3},{8,12},{10,14},{12... | collective-permute-start | bytes 442376 | tf_op jit(solution)/shard_map/ppermute | solution.py:629
  72.6 12.6 %collective-permute-start.10 = (bf16[2,4,16,1024]{3,2,1,0:T(8,128)(2,1)S(1)}, bf16[2,4,16,1024]{3,2,1,0:T(8,128)(2,1)S(1)}, u32[]{:S(2)}, u32[]{:S(2)}) collective-permute-start(bf16[2,4,16,1024]{3,2,1,0:T(8,128)(2,1)S(1)} %copy-done.4), channel_id=1, source_target_pairs={{0,1},{1,0},{2,3},{3,2},{4,5},{5,4},{6,7},{7,6},{8,9},{9,8},{10,11... | collective-permute-start | bytes 786440 | tf_op jit(solution)/shard_map/ppermute | solution.py:629
  72.6 12.7 %collective-permute-start.11 = (bf16[2,4,16,1024]{3,2,1,0:T(8,128)(2,1)S(1)}, bf16[2,4,16,1024]{3,2,1,0:T(8,128)(2,1)S(1)}, u32[]{:S(2)}, u32[]{:S(2)}) collective-permute-start(bf16[2,4,16,1024]{3,2,1,0:T(8,128)(2,1)S(1)} %collective-permute-done.4.refs_1_), channel_id=1, source_target_pairs={{0,1},{1,0},{2,3},{3,2},{4,5},{5,4},{6,7},{7,6},{8,9},{9,8},{10,11... | collective-permute-start | bytes 786440 | tf_op jit(solution)/shard_map/ppermute | solution.py:629
  73.2 13.7 %copy-start.16 = (bf16[64,1152]{1,0:T(8,128)(2,1)}, bf16[64,1152]{1,0:T(8,128)(2,1)S(1)}, u32[]{:S(2)}) copy-start(bf16[64,1152]{1,0:T(8,128)(2,1)S(1)} %collective-permute-done.17.refs_12_) | copy-start | bytes 442372
  73.2 11.6 %collective-permute-start.14 = (bf16[64,1152]{1,0:T(8,128)(2,1)S(1)}, bf16[64,1152]{1,0:T(8,128)(2,1)S(1)}, u32[]{:S(2)}, u32[]{:S(2)}) collective-permute-start(bf16[64,1152]{1,0:T(8,128)(2,1)S(1)} %copy-done.3), channel_id=1, source_target_pairs={{0,2},{2,0},{4,6},{6,4},{1,3},{3,1},{5,7},{7,5},{8,10},{10,8},{12,... | collective-permute-start | bytes 442376 | tf_op jit(solution)/shard_map/ppermute | solution.py:629
  75.3 10.4 %collective-permute-start.12 = (bf16[2,4,16,1024]{3,2,1,0:T(8,128)(2,1)S(1)}, bf16[2,4,16,1024]{3,2,1,0:T(8,128)(2,1)S(1)}, u32[]{:S(2)}, u32[]{:S(2)}) collective-permute-start(bf16[2,4,16,1024]{3,2,1,0:T(8,128)(2,1)S(1)} %collective-permute-done.5.refs_2_), channel_id=1, source_target_pairs={{0,1},{1,0},{2,3},{3,2},{4,5},{5,4},{6,7},{7,6},{8,9},{9,8},{10,11... | collective-permute-start | bytes 786440 | tf_op jit(solution)/shard_map/ppermute | solution.py:629
  84.7 1.5 %collective-permute-start.13 = (bf16[2,4,16,1024]{3,2,1,0:T(8,128)(2,1)S(1)}, bf16[2,4,16,1024]{3,2,1,0:T(8,128)(2,1)S(1)}, u32[]{:S(2)}, u32[]{:S(2)}) collective-permute-start(bf16[2,4,16,1024]{3,2,1,0:T(8,128)(2,1)S(1)} %collective-permute-done.6.refs_3_), channel_id=1, source_target_pairs={{0,1},{1,0},{2,3},{3,2},{4,5},{5,4},{6,7},{7,6},{8,9},{9,8},{10,11... | collective-permute-start | bytes 786440 | tf_op jit(solution)/shard_map/ppermute | solution.py:629
  84.8 1.7 %collective-permute-start.20 = (bf16[64,1152]{1,0:T(8,128)(2,1)S(1)}, bf16[64,1152]{1,0:T(8,128)(2,1)S(1)}, u32[]{:S(2)}, u32[]{:S(2)}) collective-permute-start(bf16[64,1152]{1,0:T(8,128)(2,1)S(1)} %collective-permute-done.16.refs_11_), channel_id=1, source_target_pairs={{0,1},{1,0},{2,3},{3,2},{4,5},{5,4},{6,7},{7,6},{8,9},{9,8},{10,11... | collective-permute-start | bytes 442376 | tf_op jit(solution)/shard_map/ppermute | solution.py:629
  85.2 1.4 %collective-permute-start.19 = (bf16[64,1152]{1,0:T(8,128)(2,1)S(1)}, bf16[64,1152]{1,0:T(8,128)(2,1)S(1)}, u32[]{:S(2)}, u32[]{:S(2)}) collective-permute-start(bf16[64,1152]{1,0:T(8,128)(2,1)S(1)} %collective-permute-done.15.refs_10_), channel_id=1, source_target_pairs={{0,1},{1,0},{2,3},{3,2},{4,5},{5,4},{6,7},{7,6},{8,9},{9,8},{10,11... | collective-permute-start | bytes 442376 | tf_op jit(solution)/shard_map/ppermute | solution.py:629
  85.3 1.6 %collective-permute-start.18 = (bf16[64,1152]{1,0:T(8,128)(2,1)S(1)}, bf16[64,1152]{1,0:T(8,128)(2,1)S(1)}, u32[]{:S(2)}, u32[]{:S(2)}) collective-permute-start(bf16[64,1152]{1,0:T(8,128)(2,1)S(1)} %collective-permute-done.14.refs_9_), channel_id=1, source_target_pairs={{0,1},{1,0},{2,3},{3,2},{4,5},{5,4},{6,7},{7,6},{8,9},{9,8},{10,11... | collective-permute-start | bytes 442376 | tf_op jit(solution)/shard_map/ppermute | solution.py:629
  (18 other events, 69.1 us)

commit v8 on v7

--- a/solution.py
+++ b/solution.py
@@ -240,11 +240,38 @@
     return one_hot(packed, slots * length), one_hot(ordered, tokens)
 
 
-def pack_kernel(length, capacity, slots, ids, hidden, cot, *refs):
-    send, slabs, refs = refs[0], refs[1:5], refs[5:]
-    id_buf, buf, packed, ordered, turned, out_slabs, sems = refs
+def pack_kernel(length, capacity, slots, ids, hidden, cot, send, id_buf, buf, packed, sems):
     groups, _, rows, part = send.shape
     tokens = hidden.shape[0] * length
+    arriving = [
+        pltpu.make_async_copy(source, target, sems.at[at])
+        for at, (source, target) in enumerate(
+            ((ids, id_buf), (hidden, buf.at[0]), (cot, buf.at[1]))
+        )
+    ]
+    leaving = [
+        pltpu.make_async_copy(packed.at[:, at], send.at[:, at], sems.at[3 + at]) for at in range(2)
+    ]
+    for copy in arriving:
+        copy.start()
+    arriving[0].wait()
+    ids_row = spread_ids(id_buf, (8, tokens), length)[:1]
+    place, _ = placements(ids_row, length, capacity, slots)
+    for which in range(2):
+        arriving[1 + which].wait()
+        moved = matmul(place, buf[which].reshape(tokens, part)).astype(jnp.bfloat16)
+        for group in range(groups):
+            packed[group, which] = moved[group * rows : (group + 1) * rows]
+        leaving[which].start()
+    for copy in leaving:
+        copy.wait()
+
+
+def slab_kernel(length, capacity, slots, ids, hidden, cot, _, *refs):
+    slabs, refs = refs[:4], refs[4:]
+    id_buf, buf, ordered, turned, out_slabs, sems = refs
+    s_local, _, part = hidden.shape
+    tokens = s_local * length
     slab = part // 2
     half = tokens // 2
     replica = lax.axis_index("dp")
@@ -255,16 +282,13 @@
         )
     ]
     leaving = [
-        pltpu.make_async_copy(packed.at[:, at], send.at[:, at], sems.at[3 + at]) for at in range(2)
-    ]
-    sliding = [
-        pltpu.make_async_copy(out_slabs.at[at], slabs[at], sems.at[5 + at]) for at in range(4)
+        pltpu.make_async_copy(out_slabs.at[at], slabs[at], sems.at[3 + at]) for at in range(4)
     ]
     for copy in arriving:
         copy.start()
     arriving[0].wait()
     ids_row = spread_ids(id_buf, (16, tokens), length)
-    by_slot, by_group = placements(ids_row[:1], length, capacity, slots)
+    _, by_group = placements(ids_row[:1], length, capacity, slots)
     for group in range(2):
         mine = by_group[group * half : (group + 1) * half]
         clusters = matmul(ids_row.astype(jnp.float32).astype(jnp.bfloat16), mine, TRANS_RHS)
@@ -274,10 +298,6 @@
     for which in range(2):
         arriving[1 + which].wait()
         flat = buf[which].reshape(tokens, part)
-        moved = matmul(by_slot, flat).astype(jnp.bfloat16)
-        for group in range(groups):
-            packed[group, which] = moved[group * rows : (group + 1) * rows]
-        leaving[which].start()
         ordered[which] = matmul(by_group, flat).astype(jnp.bfloat16)
     for turn in range(4):
         pair = (turn // 2) ^ (replica & 1)
@@ -288,13 +308,13 @@
             out_slabs[turn, which * half : (which + 1) * half] = ordered[which, at, cols]
         out_slabs[turn, tokens:] = jnp.zeros((16, slab), jnp.bfloat16)
         out_slabs[turn, tokens:, :128] = turned[group]
-        sliding[turn].start()
-    for copy in leaving + sliding:
+        leaving[turn].start()
+    for copy in leaving:
         copy.wait()
 
 
 def repack_kernel(length, capacity, *refs):
-    slabs, outs = refs[:4], refs[5:]
+    slabs, outs = refs[:4], refs[4:]
     experts, rows = len(outs), outs[0].shape[2]
     half = (slabs[0].shape[0] - 16) // 2
     core, replica = lax.axis_index("segment"), lax.axis_index("dp")
@@ -352,8 +372,8 @@
 
 def chain_kernel(
     recv_in, own_dn, own_up, own_gain, other_dn, other_up, other_gain,
-    small, middle,
-    recv, dn_buf, up_buf, gain_buf, entering, d_norms, sems,
+    out, small,
+    recv, dn_buf, up_buf, gain_buf, entering, middle, d_norms, sems,
 ):
     phase = lax.axis_index("segment")
     experts, phases, _, rows, part = recv.shape
@@ -452,6 +472,10 @@
         d_norms[:, here] = d_norm
         total = total + lanes(d_norm)
         cross = cross + lanes(d_norm * ((wide - mean_1) * inverse_1))
+        leaving = (wide + matmul(act_1, up_buf[1, :, here])).astype(jnp.bfloat16)
+        half, start = col // part, col % part
+        for e in range(experts):
+            out[e, half, :, start : start + CHUNK] = leaving[e * rows : (e + 1) * rows]
     shift = row_sum(total) / width
     along = row_sum(cross) / width
     d_act = jnp.zeros((tokens, rank), jnp.float32)
@@ -467,31 +491,6 @@
         small[:, at * rank : (at + 1) * rank] = value
     moments = (mean_0, inverse_0, mean_1, inverse_1, shift, along)
     small[:, 4 * rank :] = side_by_side(moments, tokens)
-
-
-def result_kernel(middle, small, own_up, other_up, out, up_buf, sem):
-    phase = lax.axis_index("segment")
-    experts, _, rows, part = out.shape
-    rank, width = up_buf.shape
-    copies = [pltpu.make_async_copy(source, up_buf, sem) for source in (own_up, other_up)]
-
-    @pl.when(phase == 1)
-    def _():
-        copies[0].start()
-
-    @pl.when(phase != 1)
-    def _():
-        copies[1].start()
-
-    copies[0].wait()
-    act = small[:, rank : 2 * rank]
-    for col in range(0, width, CHUNK):
-        here = slice(col, col + CHUNK)
-        leaving = middle[:, here].astype(jnp.float32) + matmul(act, up_buf[:, here])
-        leaving = leaving.astype(jnp.bfloat16)
-        half, start = col // part, col % part
-        for e in range(experts):
-            out[e, half, :, start : start + CHUNK] = leaving[e * rows : (e + 1) * rows]
 
 
 def gradient_kernel(experts, sources, sizes, *refs):
@@ -655,29 +654,40 @@
     sizes = (length, capacity, slots)
     sections = ("expert", "segment")
 
-    other_dn = across(own[0], "segment", 1)
+    other = tuple(across(array, "segment", 1) for array in own)
     half = s_local * length // 2
-    send, *slabs = call(
+    (send,) = call(
         functools.partial(pack_kernel, *sizes),
         "pack",
         60,
         [HBM] * 3,
-        [((groups, 2, rows, part), bf16)] + [((2 * half + 16, slab), bf16)] * 4,
+        [((groups, 2, rows, part), bf16)],
         [
             pltpu.SMEM(cluster_ids.shape, jnp.int32),
             pltpu.VMEM((2,) + hidden_in.shape, bf16),
             pltpu.VMEM((groups, 2, rows, part), bf16),
+            pltpu.SemaphoreType.DMA((5,)),
+        ],
+        outs_in=HBM,
+    )(cluster_ids, hidden_in, cotangent)
+    slabs = call(
+        functools.partial(slab_kernel, *sizes),
+        "slabs",
+        60,
+        [HBM] * 4,
+        [((2 * half + 16, slab), bf16)] * 4,
+        [
+            pltpu.SMEM(cluster_ids.shape, jnp.int32),
+            pltpu.VMEM((2,) + hidden_in.shape, bf16),
             pltpu.VMEM((2, 2 * half, part), bf16),
             pltpu.VMEM((2, 16, 128), bf16),
             pltpu.VMEM((4, 2 * half + 16, slab), bf16),
-            pltpu.SemaphoreType.DMA((9,)),
+            pltpu.SemaphoreType.DMA((7,)),
         ],
         outs_in=HBM,
-    )(cluster_ids, hidden_in, cotangent)
+    )(cluster_ids, hidden_in, cotangent, send)
     recv = lax.all_to_all(send, sections, split_axis=0, concat_axis=0, tiled=True)
     recv = recv.reshape(experts, 2, 2, rows, part)
-    recv, up, scale = lax.optimization_barrier((recv, own[1], own[2]))
-    other = (other_dn, across(up, "segment", 1), across(scale, "segment", 1))
     slabs = [
         lax.ppermute(block, ("dp", "segment"), slab_route(replicas, turn // 2, turn % 2))
         for turn, block in enumerate(slabs)
@@ -686,22 +696,23 @@
         functools.partial(repack_kernel, length, capacity),
         "repack",
         60,
-        [VMEM] * 4 + [HBM],
+        [VMEM] * 4,
         [((2, replicas, rows, slab), bf16)] * experts,
-    )(*slabs, recv)
+    )(*slabs)
     mine = [slices[0]] + [across(slices[step], "expert", step) for step in range(1, experts)]
 
-    small, middle = call(
+    out, small = call(
         chain_kernel,
         "chain",
         60,
         [HBM] * 7,
-        [((tokens, 4 * rank + 128), bf16), ((tokens, width), bf16)],
+        [((experts, 2, rows, part), bf16), ((tokens, 4 * rank + 128), bf16)],
         [
             pltpu.VMEM(recv.shape, bf16),
             pltpu.VMEM((2, width, rank), bf16),
             pltpu.VMEM((2, rank, width), bf16),
             pltpu.VMEM((2, 1, width), bf16),
+            pltpu.VMEM((tokens, width), bf16),
             pltpu.VMEM((tokens, width), bf16),
             pltpu.VMEM((tokens, width), f32),
             pltpu.SemaphoreType.DMA((3, 3)),
@@ -709,19 +720,11 @@
         flops=7 * 2 * tokens * width * rank,
         moved=10 * MIB,
     )(recv, *own, *other)
-    mine, small, middle = lax.optimization_barrier((mine, small, middle))
+    mine, small = lax.optimization_barrier((mine, small))
     theirs = [across(block, "segment", 1) for block in mine]
     near = [small] + [across(small, "dp", step) for step in range(1, replicas)]
     smalls = near + [across(piece, "segment", 1) for piece in near]
 
-    (out,) = call(
-        result_kernel,
-        "results",
-        60,
-        [VMEM] * 2 + [HBM] * 2,
-        [((experts, 2, rows, part), bf16)],
-        [pltpu.VMEM((rank, width), bf16), pltpu.SemaphoreType.DMA],
-    )(middle, small, own[1], other[1])
     back = lax.all_to_all(
         out.reshape(groups, rows, part), sections, split_axis=0, concat_axis=0, tiled=True
     )

time: 96.7 us -> 82.1 us (0.85)
  waiting for transfers between devices: 33.6 us -> 19.9 us
  Pallas kernels: 27.1 us -> 25 us
  local copies, waits for them, and re-layouts: 2.09 us -> 3.8 us
    all_to_all x1, waiting for transfers between devices: 14.9 us -> 0.01 us  [on_device_two_phases(): lax.all_to_all(send, sections, split_axis=0, concat_axis=0, tiled=True)]
    pallas_call x2, Pallas kernels: 13.3 us -> 11.5 us  [the longest x1 9.25 us: on_device_two_phases(): call(chain_kernel, 'chain', 60, [HBM] * 7, [((experts, 2, rows, part), bf...]
    unnamed x54 -> x42, local copies, waits for them, and re-layouts: 2.09 us -> 3.8 us
    ppermute x17, waiting for transfers between devices: 12.1 us -> 13.2 us  [across(): return lax.ppermute(block, axis, [(i, i ^ distance) for i in range(size)])]
    ppermute x17, starting transfers between devices: 11.6 us -> 10.6 us  [across(): return lax.ppermute(block, axis, [(i, i ^ distance) for i in range(size)])]
  transfers between devices with their start and end apart: 23 -> 23, of which waited for: 9 -> 7; matrix products, arithmetic and copies ran while one was open for 0% -> 0% of each run, Pallas kernels for 13% -> 21%
where the time goes in v8:
time: 82.1 us; the launch traced here: 81.7 us
  starting transfers between devices  32.1 us (39%)
  Pallas kernels  25 us (30%)
  waiting for transfers between devices  19.9 us (24%)
  local copies, waits for them, and re-layouts  3.8 us (5%)
  between operations  0.83 us (1%)
    ppermute x17, waiting for transfers between devices, across(): return lax.ppermute(block, axis, [(i, i ^ distance) for i in range(size)])  13.2 us
    ppermute x4, starting transfers between devices, on_device_two_phases(): lax.ppermute(block, ('dp', 'segment'), slab_route(replicas, turn // 2, tu...  12.2 us
    ppermute x17, starting transfers between devices, across(): return lax.ppermute(block, axis, [(i, i ^ distance) for i in range(size)])  10.6 us
    pallas_call x1, Pallas kernels, on_device_two_phases(): call(chain_kernel, 'chain', 60, [HBM] * 7, [((experts, 2, rows, part), bf...  9.25 us
    pallas_call x1, Pallas kernels, on_device_two_phases(): call(functools.partial(gradient_kernel, experts, sources, sizes), 'gradie...  7.99 us
    ppermute x4, waiting for transfers between devices, on_device_two_phases(): lax.ppermute(block, ('dp', 'segment'), slab_route(replicas, turn // 2, tu...  6.72 us
    all_to_all x1, starting transfers between devices, on_device_two_phases(): lax.all_to_all(send, sections, split_axis=0, concat_axis=0, tiled=True)  5.16 us
    all_to_all x1, starting transfers between devices, on_device_two_phases(): lax.all_to_all(out.reshape(groups, rows, part), sections, split_axis=0, c...  4.14 us
  transfers between devices with their start and end apart: 23, of which 7 were waited for; matrix products, arithmetic and copies ran while one was open for 0% of the time, Pallas kernels for 21%

profile of v8, /device:TPU:0, one launch (start us, length us, event | category | flops | bytes accessed | tf_op | source)
XLA Modules:
  0.0 81.7 jit_solution(4263113246611924340)
XLA Ops:
  0.6 0.5 collective-permute-start.7
  1.2 2.4 %pack.1._ = bf16[8,2,16,2048]{3,2,1,0:T(8,128)(2,1)} custom-call(s32[16]{0:T(128)} %refs_22_.1, bf16[16,4,2048]{2,1,0:T(4,128)(2,1)} %hidden.3, bf16[16,4,2048]{2,1,0:T(4,128)(2,1)} %cot.3), custom_call_target="tpu_custom_call" | custom-call | bytes 1048576 | tf_op jit(solution)/shard_map/pack/pallas_call | solution.py:659
  3.6 5.2 %all-to-all-start = ((bf16[8,2,16,2048]{3,2,1,0:T(8,128)(2,1)}), bf16[8,2,16,2048]{3,2,1,0:T(8,128)(2,1)S(1)}, u32[]{:S(2)}, u32[]{:S(2)}) async-start(bf16[8,2,16,2048]{3,2,1,0:T(8,128)(2,1)} %pack.1._), calls=%async_computation | async-start | bytes 2097152 | tf_op jit(solution)/shard_map/all_to_all | solution.py:689
  8.8 2.3 %slabs.1 = (bf16[80,1024]{1,0:T(8,128)(2,1)}, bf16[80,1024]{1,0:T(8,128)(2,1)}, bf16[80,1024]{1,0:T(8,128)(2,1)}, bf16[80,1024]{1,0:T(8,128)(2,1)}) custom-call(s32[16]{0:T(128)} %refs_22_.1, bf16[16,4,2048]{2,1,0:T(4,128)(2,1)} %hidden.3, bf16[16,4,2048]{2,1,0:T(4,128)(2,1)} %cot.3, bf16[8,2,16,2048]{3,2,1,0:T(8,128)(2,1)} %pack.1._), custom_call_target="tpu_custom_call" | custom-call | bytes 1048576 | tf_op jit(solution)/shard_map/slabs/pallas_call | solution.py:673
  11.0 1.6 %collective-permute-start = (bf16[80,1024]{1,0:T(8,128)(2,1)}, bf16[80,1024]{1,0:T(8,128)(2,1)S(1)}, u32[]{:S(2)}, u32[]{:S(2)}) collective-permute-start(bf16[80,1024]{1,0:T(8,128)(2,1)} %get-tuple-element.21), channel_id=1, source_target_pairs={{0,0},{1,4},{2,2},{3,6},{4,1},{5,5},{6,3},{7,7},{8,8},{9,12},{10,1... | collective-permute-start | bytes 491528 | tf_op jit(solution)/shard_map/ppermute | solution.py:692
  12.6 3.1 %collective-permute-start.1 = (bf16[80,1024]{1,0:T(8,128)(2,1)}, bf16[80,1024]{1,0:T(8,128)(2,1)S(1)}, u32[]{:S(2)}, u32[]{:S(2)}) collective-permute-start(bf16[80,1024]{1,0:T(8,128)(2,1)} %get-tuple-element.22), channel_id=1, source_target_pairs={{0,1},{1,5},{2,3},{3,7},{4,0},{5,4},{6,2},{7,6},{8,9},{9,13},{10,1... | collective-permute-start | bytes 491528 | tf_op jit(solution)/shard_map/ppermute | solution.py:692
  15.7 1.6 %collective-permute-start.2 = (bf16[80,1024]{1,0:T(8,128)(2,1)}, bf16[80,1024]{1,0:T(8,128)(2,1)S(1)}, u32[]{:S(2)}, u32[]{:S(2)}) collective-permute-start(bf16[80,1024]{1,0:T(8,128)(2,1)} %get-tuple-element.23), channel_id=1, source_target_pairs={{0,2},{1,6},{2,0},{3,4},{4,3},{5,7},{6,1},{7,5},{8,10},{9,14},{10,... | collective-permute-start | bytes 491528 | tf_op jit(solution)/shard_map/ppermute | solution.py:692
  17.3 5.9 %collective-permute-start.3 = (bf16[80,1024]{1,0:T(8,128)(2,1)}, bf16[80,1024]{1,0:T(8,128)(2,1)S(1)}, u32[]{:S(2)}, u32[]{:S(2)}) collective-permute-start(bf16[80,1024]{1,0:T(8,128)(2,1)} %get-tuple-element.24), channel_id=1, source_target_pairs={{0,3},{1,7},{2,1},{3,5},{4,2},{5,6},{6,0},{7,4},{8,11},{9,15},{10,... | collective-permute-start | bytes 491528 | tf_op jit(solution)/shard_map/ppermute | solution.py:692
  23.2 2.6 %collective-permute-done.1.refs_1_ = bf16[80,1024]{1,0:T(8,128)(2,1)S(1)} collective-permute-done((bf16[80,1024]{1,0:T(8,128)(2,1)}, bf16[80,1024]{1,0:T(8,128)(2,1)S(1)}, u32[]{:S(2)}, u32[]{:S(2)}) %collective-permute-start.1) | collective-permute-done | bytes 163872 | tf_op jit(solution)/shard_map/ppermute | solution.py:692
  25.8 4.1 %collective-permute-done.3.refs_3_ = bf16[80,1024]{1,0:T(8,128)(2,1)S(1)} collective-permute-done((bf16[80,1024]{1,0:T(8,128)(2,1)}, bf16[80,1024]{1,0:T(8,128)(2,1)S(1)}, u32[]{:S(2)}, u32[]{:S(2)}) %collective-permute-start.3) | collective-permute-done | bytes 163872 | tf_op jit(solution)/shard_map/ppermute | solution.py:692
  30.0 0.7 copy-done.11
  30.7 3.1 %repack.1 = (bf16[2,4,16,1024]{3,2,1,0:T(8,128)(2,1)}, bf16[2,4,16,1024]{3,2,1,0:T(8,128)(2,1)}, bf16[2,4,16,1024]{3,2,1,0:T(8,128)(2,1)}, bf16[2,4,16,1024]{3,2,1,0:T(8,128)(2,1)}) custom-call(bf16[80,1024]{1,0:T(8,128)(2,1)} %copy-done.8, bf16[80,1024]{1,0:T(8,128)(2,1)} %copy-done.9, bf16[80,1024]{1,0:T(8,128)(2,1)} %copy-done.10, bf16[80,1024]{1,0:T(8,128)(2,1)} %copy-done.11), custom_call_target="tpu_custom_call" | custom-call | bytes 1048576 | tf_op jit(solution)/shard_map/repack/pallas_call | solution.py:695
  33.8 2.0 %collective-permute-start.4 = (bf16[2,4,16,1024]{3,2,1,0:T(8,128)(2,1)}, bf16[2,4,16,1024]{3,2,1,0:T(8,128)(2,1)}, u32[]{:S(2)}, u32[]{:S(2)}) collective-permute-start(bf16[2,4,16,1024]{3,2,1,0:T(8,128)(2,1)} %get-tuple-element.26), channel_id=1, source_target_pairs={{0,8},{8,0},{16,24},{24,16},{1,9},{9,1},{17,25},{25,17},{2,10},{10... | collective-permute-start | bytes 786440 | tf_op jit(solution)/shard_map/ppermute | solution.py:628
  35.8 1.5 %collective-permute-start.5 = (bf16[2,4,16,1024]{3,2,1,0:T(8,128)(2,1)}, bf16[2,4,16,1024]{3,2,1,0:T(8,128)(2,1)}, u32[]{:S(2)}, u32[]{:S(2)}) collective-permute-start(bf16[2,4,16,1024]{3,2,1,0:T(8,128)(2,1)} %get-tuple-element.27), channel_id=1, source_target_pairs={{0,16},{8,24},{16,0},{24,8},{1,17},{9,25},{17,1},{25,9},{2,18},{10... | collective-permute-start | bytes 786440 | tf_op jit(solution)/shard_map/ppermute | solution.py:628
  37.4 0.5 copy-done.20
  37.9 0.5 copy-done.1
  38.3 0.7 copy-done
  39.0 9.2 %chain.1 = (bf16[4,2,16,2048]{3,2,1,0:T(8,128)(2,1)}, bf16[64,1152]{1,0:T(8,128)(2,1)}) custom-call(bf16[4,2,2,16,2048]{4,3,2,1,0:T(8,128)(2,1)} %bitcast.13, bf16[4096,256]{1,0:T(8,128)(2,1)} %bitcast.8, bf16[256,4096]{1,0:T(8,128)(2,1)} %bitcast.11, bf16[1,4096]{1,0:T(2,128)(2,1)} %bitcast.15, bf16[4096,256]{1,0:T(8,128)(2,1)} %copy-done, ...), custom_call_target="tpu_custom_call" | custom-call | flops 939524096 | bytes 10485760 | tf_op jit(solution)/shard_map/chain/pallas_call | solution.py:704
  48.3 4.1 %all-to-all-start.1 = ((bf16[8,16,2048]{2,1,0:T(8,128)(2,1)}), bf16[8,16,2048]{2,1,0:T(8,128)(2,1)S(1)}, u32[]{:S(2)}, u32[]{:S(2)}) async-start(bf16[8,16,2048]{2,1,0:T(8,128)(2,1)} %bitcast.14), calls=%async_computation.1 | async-start | bytes 1048576 | tf_op jit(solution)/shard_map/all_to_all | solution.py:728
  52.5 0.6 collective-permute-start.17
  53.0 2.8 %collective-permute-start.16 = (bf16[64,1152]{1,0:T(8,128)(2,1)}, bf16[64,1152]{1,0:T(8,128)(2,1)S(1)}, u32[]{:S(2)}, u32[]{:S(2)}) collective-permute-start(bf16[64,1152]{1,0:T(8,128)(2,1)} %get-tuple-element.34.refs_8_), channel_id=1, source_target_pairs={{0,6},{2,4},{4,2},{6,0},{1,7},{3,5},{5,3},{7,1},{8,14},{10,12},{12... | collective-permute-start | bytes 442376 | tf_op jit(solution)/shard_map/ppermute | solution.py:628
  55.9 0.7 collective-permute-start.15
  56.5 0.5 collective-permute-start.11
  57.0 0.9 %collective-permute-start.14 = (bf16[64,1152]{1,0:T(8,128)(2,1)}, bf16[64,1152]{1,0:T(8,128)(2,1)S(1)}, u32[]{:S(2)}, u32[]{:S(2)}) collective-permute-start(bf16[64,1152]{1,0:T(8,128)(2,1)} %get-tuple-element.34.refs_8_), channel_id=1, source_target_pairs={{0,2},{2,0},{4,6},{6,4},{1,3},{3,1},{5,7},{7,5},{8,10},{10,8},{12,... | collective-permute-start | bytes 442376 | tf_op jit(solution)/shard_map/ppermute | solution.py:628
  57.9 3.9 %collective-permute-done.16.refs_11_ = bf16[64,1152]{1,0:T(8,128)(2,1)S(1)} collective-permute-done((bf16[64,1152]{1,0:T(8,128)(2,1)}, bf16[64,1152]{1,0:T(8,128)(2,1)S(1)}, u32[]{:S(2)}, u32[]{:S(2)}) %collective-permute-start.16) | collective-permute-done | bytes 147488 | tf_op jit(solution)/shard_map/ppermute | solution.py:628
  61.9 8.2 %collective-permute-done.15.refs_10_ = bf16[64,1152]{1,0:T(8,128)(2,1)S(1)} collective-permute-done((bf16[64,1152]{1,0:T(8,128)(2,1)}, bf16[64,1152]{1,0:T(8,128)(2,1)S(1)}, u32[]{:S(2)}, u32[]{:S(2)}) %collective-permute-start.15) | collective-permute-done | bytes 147488 | tf_op jit(solution)/shard_map/ppermute | solution.py:628
  70.0 0.5 collective-permute-start.20
  70.6 0.4 collective-permute-start.18
  71.1 0.7 collective-permute-done.13.refs_7_
  72.7 0.2 copy-done.18
  72.9 0.8 copy-done.2
  73.7 8.0 %gradients.1 = (bf16[16,4,2048]{2,1,0:T(4,128)(2,1)}, bf16[1024,256]{1,0:T(8,128)(2,1)}, bf16[256,1024]{1,0:T(8,128)(2,1)}) custom-call(bf16[2,4,16,1024]{3,2,1,0:T(8,128)(2,1)} %get-tuple-element.30.refs_0_, bf16[2,4,16,1024]{3,2,1,0:T(8,128)(2,1)} %collective-permute-done.4.refs_1_, bf16[2,4,16,1024]{3,2,1,0:T(8,128)(2,1)} %collective-permute-done.5.refs_2_, ...), custom_call_target="tpu_custom_call" | custom-call | bytes 1048576 | tf_op jit(solution)/shard_map/gradients/pallas_call | solution.py:734
  (61 shorter events, 1.2 us)
Async XLA Ops:
  0.6 36.7 %collective-permute-start.7 = (bf16[4096,256]{1,0:T(8,128)(2,1)}, bf16[4096,256]{1,0:T(8,128)(2,1)S(1)}, u32[]{:S(2)}, u32[]{:S(2)}) collective-permute-start(bf16[4096,256]{1,0:T(8,128)(2,1)} %bitcast.7), channel_id=1, source_target_pairs={{0,1},{1,0},{2,3},{3,2},{4,5},{5,4},{6,7},{7,6},{8,9},{9,8},{10,11... | collective-permute-start | bytes 6291464 | tf_op jit(solution)/shard_map/ppermute | solution.py:628
  1.1 36.2 %collective-permute-start.8 = (bf16[256,4096]{1,0:T(8,128)(2,1)}, bf16[256,4096]{1,0:T(8,128)(2,1)}, u32[]{:S(2)}, u32[]{:S(2)}) collective-permute-start(bf16[256,4096]{1,0:T(8,128)(2,1)} %bitcast.10), channel_id=1, source_target_pairs={{0,1},{1,0},{2,3},{3,2},{4,5},{5,4},{6,7},{7,6},{8,9},{9,8},{10,11... | collective-permute-start | bytes 6291464 | tf_op jit(solution)/shard_map/ppermute | solution.py:628
  3.6 22.2 %copy-start.19 = (bf16[1,1,4096]{2,1,0:T(2,128)(2,1)S(1)}, bf16[1,1,4096]{2,1,0:T(2,128)(2,1)}, u32[]{:S(2)}) copy-start(bf16[1,1,4096]{2,1,0:T(2,128)(2,1)} %param.11) | copy-start | bytes 24580
  3.6 33.7 %all-to-all-start = ((bf16[8,2,16,2048]{3,2,1,0:T(8,128)(2,1)}), bf16[8,2,16,2048]{3,2,1,0:T(8,128)(2,1)S(1)}, u32[]{:S(2)}, u32[]{:S(2)}) async-start(bf16[8,2,16,2048]{3,2,1,0:T(8,128)(2,1)} %pack.1._), calls=%async_computation | async-start | bytes 2097152 | tf_op jit(solution)/shard_map/all_to_all | solution.py:689
  11.0 6.3 %collective-permute-start = (bf16[80,1024]{1,0:T(8,128)(2,1)}, bf16[80,1024]{1,0:T(8,128)(2,1)S(1)}, u32[]{:S(2)}, u32[]{:S(2)}) collective-permute-start(bf16[80,1024]{1,0:T(8,128)(2,1)} %get-tuple-element.21), channel_id=1, source_target_pairs={{0,0},{1,4},{2,2},{3,6},{4,1},{5,5},{6,3},{7,7},{8,8},{9,12},{10,1... | collective-permute-start | bytes 491528 | tf_op jit(solution)/shard_map/ppermute | solution.py:692
  12.6 13.2 %collective-permute-start.1 = (bf16[80,1024]{1,0:T(8,128)(2,1)}, bf16[80,1024]{1,0:T(8,128)(2,1)S(1)}, u32[]{:S(2)}, u32[]{:S(2)}) collective-permute-start(bf16[80,1024]{1,0:T(8,128)(2,1)} %get-tuple-element.22), channel_id=1, source_target_pairs={{0,1},{1,5},{2,3},{3,7},{4,0},{5,4},{6,2},{7,6},{8,9},{9,13},{10,1... | collective-permute-start | bytes 491528 | tf_op jit(solution)/shard_map/ppermute | solution.py:692
  15.7 10.1 %collective-permute-start.2 = (bf16[80,1024]{1,0:T(8,128)(2,1)}, bf16[80,1024]{1,0:T(8,128)(2,1)S(1)}, u32[]{:S(2)}, u32[]{:S(2)}) collective-permute-start(bf16[80,1024]{1,0:T(8,128)(2,1)} %get-tuple-element.23), channel_id=1, source_target_pairs={{0,2},{1,6},{2,0},{3,4},{4,3},{5,7},{6,1},{7,5},{8,10},{9,14},{10,... | collective-permute-start | bytes 491528 | tf_op jit(solution)/shard_map/ppermute | solution.py:692
  17.3 12.7 %copy-start.8 = (bf16[80,1024]{1,0:T(8,128)(2,1)}, bf16[80,1024]{1,0:T(8,128)(2,1)S(1)}, u32[]{:S(2)}) copy-start(bf16[80,1024]{1,0:T(8,128)(2,1)S(1)} %collective-permute-done.refs_0_) | copy-start | bytes 491524
  17.3 12.7 %collective-permute-start.3 = (bf16[80,1024]{1,0:T(8,128)(2,1)}, bf16[80,1024]{1,0:T(8,128)(2,1)S(1)}, u32[]{:S(2)}, u32[]{:S(2)}) collective-permute-start(bf16[80,1024]{1,0:T(8,128)(2,1)} %get-tuple-element.24), channel_id=1, source_target_pairs={{0,3},{1,7},{2,1},{3,5},{4,2},{5,6},{6,0},{7,4},{8,11},{9,15},{10,... | collective-permute-start | bytes 491528 | tf_op jit(solution)/shard_map/ppermute | solution.py:692
  25.8 4.2 %copy-start.9 = (bf16[80,1024]{1,0:T(8,128)(2,1)}, bf16[80,1024]{1,0:T(8,128)(2,1)S(1)}, u32[]{:S(2)}) copy-start(bf16[80,1024]{1,0:T(8,128)(2,1)S(1)} %collective-permute-done.1.refs_1_) | copy-start | bytes 491524
  25.8 11.5 %collective-permute-start.9 = (bf16[1,4096]{1,0:T(2,128)(2,1)S(1)}, bf16[1,4096]{1,0:T(2,128)(2,1)S(1)}, u32[]{:S(2)}, u32[]{:S(2)}) collective-permute-start(bf16[1,4096]{1,0:T(2,128)(2,1)S(1)} %bitcast.17), channel_id=1, source_target_pairs={{0,1},{1,0},{2,3},{3,2},{4,5},{5,4},{6,7},{7,6},{8,9},{9,8},{10,11... | collective-permute-start | bytes 24584 | tf_op jit(solution)/shard_map/ppermute | solution.py:628
  25.8 4.2 %copy-start.10 = (bf16[80,1024]{1,0:T(8,128)(2,1)}, bf16[80,1024]{1,0:T(8,128)(2,1)S(1)}, u32[]{:S(2)}) copy-start(bf16[80,1024]{1,0:T(8,128)(2,1)S(1)} %collective-permute-done.2.refs_2_) | copy-start | bytes 491524
  33.8 18.7 %collective-permute-start.4 = (bf16[2,4,16,1024]{3,2,1,0:T(8,128)(2,1)}, bf16[2,4,16,1024]{3,2,1,0:T(8,128)(2,1)}, u32[]{:S(2)}, u32[]{:S(2)}) collective-permute-start(bf16[2,4,16,1024]{3,2,1,0:T(8,128)(2,1)} %get-tuple-element.26), channel_id=1, source_target_pairs={{0,8},{8,0},{16,24},{24,16},{1,9},{9,1},{17,25},{25,17},{2,10},{10... | collective-permute-start | bytes 786440 | tf_op jit(solution)/shard_map/ppermute | solution.py:628
  35.8 16.7 %collective-permute-start.5 = (bf16[2,4,16,1024]{3,2,1,0:T(8,128)(2,1)}, bf16[2,4,16,1024]{3,2,1,0:T(8,128)(2,1)}, u32[]{:S(2)}, u32[]{:S(2)}) collective-permute-start(bf16[2,4,16,1024]{3,2,1,0:T(8,128)(2,1)} %get-tuple-element.27), channel_id=1, source_target_pairs={{0,16},{8,24},{16,0},{24,8},{1,17},{9,25},{17,1},{25,9},{2,18},{10... | collective-permute-start | bytes 786440 | tf_op jit(solution)/shard_map/ppermute | solution.py:628
  37.3 15.2 %collective-permute-start.6 = (bf16[2,4,16,1024]{3,2,1,0:T(8,128)(2,1)}, bf16[2,4,16,1024]{3,2,1,0:T(8,128)(2,1)}, u32[]{:S(2)}, u32[]{:S(2)}) collective-permute-start(bf16[2,4,16,1024]{3,2,1,0:T(8,128)(2,1)} %get-tuple-element.28), channel_id=1, source_target_pairs={{0,24},{8,16},{16,8},{24,0},{1,25},{9,17},{17,9},{25,1},{2,26},{10... | collective-permute-start | bytes 786440 | tf_op jit(solution)/shard_map/ppermute | solution.py:628
  39.0 17.5 %copy-start.3 = (bf16[2,4,16,1024]{3,2,1,0:T(8,128)(2,1)S(1)}, bf16[2,4,16,1024]{3,2,1,0:T(8,128)(2,1)}, u32[]{:S(2)}) copy-start(bf16[2,4,16,1024]{3,2,1,0:T(8,128)(2,1)} %get-tuple-element.30.refs_0_) | copy-start | bytes 786436
  48.3 23.9 %all-to-all-start.1 = ((bf16[8,16,2048]{2,1,0:T(8,128)(2,1)}), bf16[8,16,2048]{2,1,0:T(8,128)(2,1)S(1)}, u32[]{:S(2)}, u32[]{:S(2)}) async-start(bf16[8,16,2048]{2,1,0:T(8,128)(2,1)} %bitcast.14), calls=%async_computation.1 | async-start | bytes 1048576 | tf_op jit(solution)/shard_map/all_to_all | solution.py:728
  52.5 4.6 %collective-permute-start.17 = (bf16[64,1152]{1,0:T(8,128)(2,1)}, bf16[64,1152]{1,0:T(8,128)(2,1)S(1)}, u32[]{:S(2)}, u32[]{:S(2)}) collective-permute-start(bf16[64,1152]{1,0:T(8,128)(2,1)} %get-tuple-element.34.refs_8_), channel_id=1, source_target_pairs={{0,1},{1,0},{2,3},{3,2},{4,5},{5,4},{6,7},{7,6},{8,9},{9,8},{10,11... | collective-permute-start | bytes 442376 | tf_op jit(solution)/shard_map/ppermute | solution.py:628
  53.0 8.8 %collective-permute-start.16 = (bf16[64,1152]{1,0:T(8,128)(2,1)}, bf16[64,1152]{1,0:T(8,128)(2,1)S(1)}, u32[]{:S(2)}, u32[]{:S(2)}) collective-permute-start(bf16[64,1152]{1,0:T(8,128)(2,1)} %get-tuple-element.34.refs_8_), channel_id=1, source_target_pairs={{0,6},{2,4},{4,2},{6,0},{1,7},{3,5},{5,3},{7,1},{8,14},{10,12},{12... | collective-permute-start | bytes 442376 | tf_op jit(solution)/shard_map/ppermute | solution.py:628
  55.9 14.2 %collective-permute-start.15 = (bf16[64,1152]{1,0:T(8,128)(2,1)}, bf16[64,1152]{1,0:T(8,128)(2,1)S(1)}, u32[]{:S(2)}, u32[]{:S(2)}) collective-permute-start(bf16[64,1152]{1,0:T(8,128)(2,1)} %get-tuple-element.34.refs_8_), channel_id=1, source_target_pairs={{0,4},{2,6},{4,0},{6,2},{1,5},{3,7},{5,1},{7,3},{8,12},{10,14},{12... | collective-permute-start | bytes 442376 | tf_op jit(solution)/shard_map/ppermute | solution.py:628
  56.5 14.0 %collective-permute-start.10 = (bf16[2,4,16,1024]{3,2,1,0:T(8,128)(2,1)S(1)}, bf16[2,4,16,1024]{3,2,1,0:T(8,128)(2,1)S(1)}, u32[]{:S(2)}, u32[]{:S(2)}) collective-permute-start(bf16[2,4,16,1024]{3,2,1,0:T(8,128)(2,1)S(1)} %copy-done.3), channel_id=1, source_target_pairs={{0,1},{1,0},{2,3},{3,2},{4,5},{5,4},{6,7},{7,6},{8,9},{9,8},{10,11... | collective-permute-start | bytes 786440 | tf_op jit(solution)/shard_map/ppermute | solution.py:628
  56.5 14.1 %collective-permute-start.11 = (bf16[2,4,16,1024]{3,2,1,0:T(8,128)(2,1)}, bf16[2,4,16,1024]{3,2,1,0:T(8,128)(2,1)S(1)}, u32[]{:S(2)}, u32[]{:S(2)}) collective-permute-start(bf16[2,4,16,1024]{3,2,1,0:T(8,128)(2,1)} %collective-permute-done.4.refs_1_), channel_id=1, source_target_pairs={{0,1},{1,0},{2,3},{3,2},{4,5},{5,4},{6,7},{7,6},{8,9},{9,8},{10,11... | collective-permute-start | bytes 786440 | tf_op jit(solution)/shard_map/ppermute | solution.py:628
  57.0 15.2 %copy-start.12 = (bf16[64,1152]{1,0:T(8,128)(2,1)}, bf16[64,1152]{1,0:T(8,128)(2,1)S(1)}, u32[]{:S(2)}) copy-start(bf16[64,1152]{1,0:T(8,128)(2,1)S(1)} %collective-permute-done.17.refs_12_) | copy-start | bytes 442372
  57.0 13.0 %collective-permute-start.14 = (bf16[64,1152]{1,0:T(8,128)(2,1)}, bf16[64,1152]{1,0:T(8,128)(2,1)S(1)}, u32[]{:S(2)}, u32[]{:S(2)}) collective-permute-start(bf16[64,1152]{1,0:T(8,128)(2,1)} %get-tuple-element.34.refs_8_), channel_id=1, source_target_pairs={{0,2},{2,0},{4,6},{6,4},{1,3},{3,1},{5,7},{7,5},{8,10},{10,8},{12,... | collective-permute-start | bytes 442376 | tf_op jit(solution)/shard_map/ppermute | solution.py:628
  61.9 10.4 %copy-start.13 = (bf16[64,1152]{1,0:T(8,128)(2,1)}, bf16[64,1152]{1,0:T(8,128)(2,1)S(1)}, u32[]{:S(2)}) copy-start(bf16[64,1152]{1,0:T(8,128)(2,1)S(1)} %collective-permute-done.16.refs_11_) | copy-start | bytes 442372
  61.9 9.2 %collective-permute-start.12 = (bf16[2,4,16,1024]{3,2,1,0:T(8,128)(2,1)}, bf16[2,4,16,1024]{3,2,1,0:T(8,128)(2,1)S(1)}, u32[]{:S(2)}, u32[]{:S(2)}) collective-permute-start(bf16[2,4,16,1024]{3,2,1,0:T(8,128)(2,1)} %collective-permute-done.5.refs_2_), channel_id=1, source_target_pairs={{0,1},{1,0},{2,3},{3,2},{4,5},{5,4},{6,7},{7,6},{8,9},{9,8},{10,11... | collective-permute-start | bytes 786440 | tf_op jit(solution)/shard_map/ppermute | solution.py:628
  70.0 2.2 %copy-start.14 = (bf16[64,1152]{1,0:T(8,128)(2,1)}, bf16[64,1152]{1,0:T(8,128)(2,1)S(1)}, u32[]{:S(2)}) copy-start(bf16[64,1152]{1,0:T(8,128)(2,1)S(1)} %collective-permute-done.15.refs_10_) | copy-start | bytes 442372
  70.0 1.7 %collective-permute-start.13 = (bf16[2,4,16,1024]{3,2,1,0:T(8,128)(2,1)}, bf16[2,4,16,1024]{3,2,1,0:T(8,128)(2,1)S(1)}, u32[]{:S(2)}, u32[]{:S(2)}) collective-permute-start(bf16[2,4,16,1024]{3,2,1,0:T(8,128)(2,1)} %collective-permute-done.6.refs_3_), channel_id=1, source_target_pairs={{0,1},{1,0},{2,3},{3,2},{4,5},{5,4},{6,7},{7,6},{8,9},{9,8},{10,11... | collective-permute-start | bytes 786440 | tf_op jit(solution)/shard_map/ppermute | solution.py:628
  70.0 2.2 %copy-start.15 = (bf16[64,1152]{1,0:T(8,128)(2,1)}, bf16[64,1152]{1,0:T(8,128)(2,1)S(1)}, u32[]{:S(2)}) copy-start(bf16[64,1152]{1,0:T(8,128)(2,1)S(1)} %collective-permute-done.14.refs_9_) | copy-start | bytes 442372
  70.0 1.7 %collective-permute-start.20 = (bf16[64,1152]{1,0:T(8,128)(2,1)S(1)}, bf16[64,1152]{1,0:T(8,128)(2,1)S(1)}, u32[]{:S(2)}, u32[]{:S(2)}) collective-permute-start(bf16[64,1152]{1,0:T(8,128)(2,1)S(1)} %collective-permute-done.16.refs_11_), channel_id=1, source_target_pairs={{0,1},{1,0},{2,3},{3,2},{4,5},{5,4},{6,7},{7,6},{8,9},{9,8},{10,11... | collective-permute-start | bytes 442376 | tf_op jit(solution)/shard_map/ppermute | solution.py:628
  70.5 1.4 %collective-permute-start.19 = (bf16[64,1152]{1,0:T(8,128)(2,1)S(1)}, bf16[64,1152]{1,0:T(8,128)(2,1)S(1)}, u32[]{:S(2)}, u32[]{:S(2)}) collective-permute-start(bf16[64,1152]{1,0:T(8,128)(2,1)S(1)} %collective-permute-done.15.refs_10_), channel_id=1, source_target_pairs={{0,1},{1,0},{2,3},{3,2},{4,5},{5,4},{6,7},{7,6},{8,9},{9,8},{10,11... | collective-permute-start | bytes 442376 | tf_op jit(solution)/shard_map/ppermute | solution.py:628
  70.6 1.6 %collective-permute-start.18 = (bf16[64,1152]{1,0:T(8,128)(2,1)S(1)}, bf16[64,1152]{1,0:T(8,128)(2,1)S(1)}, u32[]{:S(2)}, u32[]{:S(2)}) collective-permute-start(bf16[64,1152]{1,0:T(8,128)(2,1)S(1)} %collective-permute-done.14.refs_9_), channel_id=1, source_target_pairs={{0,1},{1,0},{2,3},{3,2},{4,5},{5,4},{6,7},{7,6},{8,9},{9,8},{10,11... | collective-permute-start | bytes 442376 | tf_op jit(solution)/shard_map/ppermute | solution.py:628
  (12 other events, 12.0 us)

commit v9 on v8

--- a/solution.py
+++ b/solution.py
@@ -314,7 +314,7 @@
 
 
 def repack_kernel(length, capacity, *refs):
-    slabs, outs = refs[:4], refs[4:]
+    slabs, outs = refs[:4], refs[5:]
     experts, rows = len(outs), outs[0].shape[2]
     half = (slabs[0].shape[0] - 16) // 2
     core, replica = lax.axis_index("segment"), lax.axis_index("dp")
@@ -692,15 +692,6 @@
         lax.ppermute(block, ("dp", "segment"), slab_route(replicas, turn // 2, turn % 2))
         for turn, block in enumerate(slabs)
     ]
-    slices = call(
-        functools.partial(repack_kernel, length, capacity),
-        "repack",
-        60,
-        [VMEM] * 4,
-        [((2, replicas, rows, slab), bf16)] * experts,
-    )(*slabs)
-    mine = [slices[0]] + [across(slices[step], "expert", step) for step in range(1, experts)]
-
     out, small = call(
         chain_kernel,
         "chain",
@@ -720,7 +711,14 @@
         flops=7 * 2 * tokens * width * rank,
         moved=10 * MIB,
     )(recv, *own, *other)
-    mine, small = lax.optimization_barrier((mine, small))
+    slices = call(
+        functools.partial(repack_kernel, length, capacity),
+        "repack",
+        60,
+        [VMEM] * 4 + [HBM],
+        [((2, replicas, rows, slab), bf16)] * experts,
+    )(*slabs, small)
+    mine = [slices[0]] + [across(slices[step], "expert", step) for step in range(1, experts)]
     theirs = [across(block, "segment", 1) for block in mine]
     near = [small] + [across(small, "dp", step) for step in range(1, replicas)]
     smalls = near + [across(piece, "segment", 1) for piece in near]

time: 82.1 us -> 72 us (0.88)
  starting transfers between devices: 32.1 us -> 24.8 us
  waiting for transfers between devices: 19.9 us -> 17.8 us
    ppermute x4, waiting for transfers between devices: 6.72 us -> 0.01 us  [on_device_two_phases(): lax.ppermute(block, ('dp', 'segment'), slab_route(replicas, turn // 2, tu...]
    all_to_all x1, waiting for transfers between devices: 0.01 us -> 6.31 us  [on_device_two_phases(): lax.all_to_all(send, sections, split_axis=0, concat_axis=0, tiled=True)]
    ppermute x4, starting transfers between devices: 12.2 us -> 6.29 us  [on_device_two_phases(): lax.ppermute(block, ('dp', 'segment'), slab_route(replicas, turn // 2, tu...]
    ppermute x17, waiting for transfers between devices: 13.2 us -> 8.42 us  [across(): return lax.ppermute(block, axis, [(i, i ^ distance) for i in range(size)])]
    all_to_all x1, waiting for transfers between devices: 0.01 us -> 3.02 us  [on_device_two_phases(): lax.all_to_all(out.reshape(groups, rows, part), sections, split_axis=0, c...]
  transfers between devices with their start and end apart: 23 -> 23, of which waited for: 7 -> 7; matrix products, arithmetic and copies ran while one was open for 0% -> 0% of each run, Pallas kernels for 21% -> 24%
where the time goes in v9:
time: 72 us; the launch traced here: 71.7 us
  Pallas kernels  24.9 us (35%)
  starting transfers between devices  24.8 us (34%)
  waiting for transfers between devices  17.8 us (25%)
  local copies, waits for them, and re-layouts  3.24 us (4%)
  between operations  0.91 us (1%)
    ppermute x17, starting transfers between devices, across(): return lax.ppermute(block, axis, [(i, i ^ distance) for i in range(size)])  9.86 us
    pallas_call x1, Pallas kernels, on_device_two_phases(): call(chain_kernel, 'chain', 60, [HBM] * 7, [((experts, 2, rows, part), bf...  9.23 us
    ppermute x17, waiting for transfers between devices, across(): return lax.ppermute(block, axis, [(i, i ^ distance) for i in range(size)])  8.42 us
    pallas_call x1, Pallas kernels, on_device_two_phases(): call(functools.partial(gradient_kernel, experts, sources, sizes), 'gradie...  7.98 us
    all_to_all x1, waiting for transfers between devices, on_device_two_phases(): lax.all_to_all(send, sections, split_axis=0, concat_axis=0, tiled=True)  6.31 us
    ppermute x4, starting transfers between devices, on_device_two_phases(): lax.ppermute(block, ('dp', 'segment'), slab_route(replicas, turn // 2, tu...  6.29 us
    all_to_all x1, starting transfers between devices, on_device_two_phases(): lax.all_to_all(send, sections, split_axis=0, concat_axis=0, tiled=True)  5.16 us
    all_to_all x1, starting transfers between devices, on_device_two_phases(): lax.all_to_all(out.reshape(groups, rows, part), sections, split_axis=0, c...  3.49 us
  transfers between devices with their start and end apart: 23, of which 7 were waited for; matrix products, arithmetic and copies ran while one was open for 0% of the time, Pallas kernels for 24%

profile of v9, /device:TPU:0, one launch (start us, length us, event | category | flops | bytes accessed | tf_op | source)
XLA Modules:
  0.0 71.7 jit_solution(5904547238638231680)
XLA Ops:
  0.6 0.5 collective-permute-start.4
  1.2 2.4 %pack.1._ = bf16[8,2,16,2048]{3,2,1,0:T(8,128)(2,1)} custom-call(s32[16]{0:T(128)} %refs_22_.1, bf16[16,4,2048]{2,1,0:T(4,128)(2,1)} %hidden.3, bf16[16,4,2048]{2,1,0:T(4,128)(2,1)} %cot.3), custom_call_target="tpu_custom_call" | custom-call | bytes 1048576 | tf_op jit(solution)/shard_map/pack/pallas_call | solution.py:659
  3.6 5.2 %all-to-all-start = ((bf16[8,2,16,2048]{3,2,1,0:T(8,128)(2,1)}), bf16[8,2,16,2048]{3,2,1,0:T(8,128)(2,1)S(1)}, u32[]{:S(2)}, u32[]{:S(2)}) async-start(bf16[8,2,16,2048]{3,2,1,0:T(8,128)(2,1)} %pack.1._), calls=%async_computation | async-start | bytes 2097152 | tf_op jit(solution)/shard_map/all_to_all | solution.py:689
  8.8 0.5 collective-permute-start.6
  9.3 2.3 %slabs.1 = (bf16[80,1024]{1,0:T(8,128)(2,1)}, bf16[80,1024]{1,0:T(8,128)(2,1)}, bf16[80,1024]{1,0:T(8,128)(2,1)}, bf16[80,1024]{1,0:T(8,128)(2,1)}) custom-call(s32[16]{0:T(128)} %refs_22_.1, bf16[16,4,2048]{2,1,0:T(4,128)(2,1)} %hidden.3, bf16[16,4,2048]{2,1,0:T(4,128)(2,1)} %cot.3, bf16[8,2,16,2048]{3,2,1,0:T(8,128)(2,1)} %pack.1._), custom_call_target="tpu_custom_call" | custom-call | bytes 1048576 | tf_op jit(solution)/shard_map/slabs/pallas_call | solution.py:673
  11.6 1.6 %collective-permute-start = (bf16[80,1024]{1,0:T(8,128)(2,1)}, bf16[80,1024]{1,0:T(8,128)(2,1)S(1)}, u32[]{:S(2)}, u32[]{:S(2)}) collective-permute-start(bf16[80,1024]{1,0:T(8,128)(2,1)} %get-tuple-element.16), channel_id=1, source_target_pairs={{0,0},{1,4},{2,2},{3,6},{4,1},{5,5},{6,3},{7,7},{8,8},{9,12},{10,1... | collective-permute-start | bytes 491528 | tf_op jit(solution)/shard_map/ppermute | solution.py:692
  13.1 3.1 %collective-permute-start.1 = (bf16[80,1024]{1,0:T(8,128)(2,1)}, bf16[80,1024]{1,0:T(8,128)(2,1)S(1)}, u32[]{:S(2)}, u32[]{:S(2)}) collective-permute-start(bf16[80,1024]{1,0:T(8,128)(2,1)} %get-tuple-element.17), channel_id=1, source_target_pairs={{0,1},{1,5},{2,3},{3,7},{4,0},{5,4},{6,2},{7,6},{8,9},{9,13},{10,1... | collective-permute-start | bytes 491528 | tf_op jit(solution)/shard_map/ppermute | solution.py:692
  16.3 1.6 %collective-permute-start.2 = (bf16[80,1024]{1,0:T(8,128)(2,1)}, bf16[80,1024]{1,0:T(8,128)(2,1)}, u32[]{:S(2)}, u32[]{:S(2)}) collective-permute-start(bf16[80,1024]{1,0:T(8,128)(2,1)} %get-tuple-element.18), channel_id=1, source_target_pairs={{0,2},{1,6},{2,0},{3,4},{4,3},{5,7},{6,1},{7,5},{8,10},{9,14},{10,... | collective-permute-start | bytes 491528 | tf_op jit(solution)/shard_map/ppermute | solution.py:692
  17.9 6.3 %all-to-all-done = bf16[8,2,16,2048]{3,2,1,0:T(8,128)(2,1)S(1)} async-done(((bf16[8,2,16,2048]{3,2,1,0:T(8,128)(2,1)}), bf16[8,2,16,2048]{3,2,1,0:T(8,128)(2,1)S(1)}, u32[]{:S(2)}, u32[]{:S(2)}) %all-to-all-start) | async-done | bytes 1048608 | tf_op jit(solution)/shard_map/all_to_all | solution.py:689
  24.2 1.0 %copy-done.1 = bf16[8,2,16,2048]{3,2,1,0:T(8,128)(2,1)} copy-done((bf16[8,2,16,2048]{3,2,1,0:T(8,128)(2,1)}, bf16[8,2,16,2048]{3,2,1,0:T(8,128)(2,1)S(1)}, u32[]{:S(2)}) %copy-start.1) | copy-done | bytes 1048600
  25.2 9.2 %chain.1 = (bf16[4,2,16,2048]{3,2,1,0:T(8,128)(2,1)}, bf16[64,1152]{1,0:T(8,128)(2,1)}) custom-call(bf16[4,2,2,16,2048]{4,3,2,1,0:T(8,128)(2,1)} %bitcast.13, bf16[4096,256]{1,0:T(8,128)(2,1)} %bitcast.8, bf16[256,4096]{1,0:T(8,128)(2,1)} %bitcast.11, bf16[1,4096]{1,0:T(2,128)(2,1)} %bitcast.15, bf16[4096,256]{1,0:T(8,128)(2,1)} %copy-done, ...), custom_call_target="tpu_custom_call" | custom-call | flops 939524096 | bytes 10485760 | tf_op jit(solution)/shard_map/chain/pallas_call | solution.py:695
  34.5 3.7 %collective-permute-start.16 = (bf16[64,1152]{1,0:T(8,128)(2,1)}, bf16[64,1152]{1,0:T(8,128)(2,1)S(1)}, u32[]{:S(2)}, u32[]{:S(2)}) collective-permute-start(bf16[64,1152]{1,0:T(8,128)(2,1)} %get-tuple-element.20.refs_4_.refs_8_), channel_id=1, source_target_pairs={{0,6},{2,4},{4,2},{6,0},{1,7},{3,5},{5,3},{7,1},{8,14},{10,12},{12... | collective-permute-start | bytes 442376 | tf_op jit(solution)/shard_map/ppermute | solution.py:628
  38.2 0.6 copy-done.11
  38.9 3.1 %repack.1 = (bf16[2,4,16,1024]{3,2,1,0:T(8,128)(2,1)}, bf16[2,4,16,1024]{3,2,1,0:T(8,128)(2,1)}, bf16[2,4,16,1024]{3,2,1,0:T(8,128)(2,1)}, bf16[2,4,16,1024]{3,2,1,0:T(8,128)(2,1)}) custom-call(bf16[80,1024]{1,0:T(8,128)(2,1)} %copy-done.10, bf16[80,1024]{1,0:T(8,128)(2,1)} %copy-done.11, bf16[80,1024]{1,0:T(8,128)(2,1)} %collective-permute-done.2.refs_2_, ...), custom_call_target="tpu_custom_call" | custom-call | bytes 1048576 | tf_op jit(solution)/shard_map/repack/pallas_call | solution.py:714
  42.0 0.6 collective-permute-start.7
  42.5 0.6 collective-permute-start.8
  43.1 2.3 %collective-permute-start.9 = (bf16[2,4,16,1024]{3,2,1,0:T(8,128)(2,1)}, bf16[2,4,16,1024]{3,2,1,0:T(8,128)(2,1)S(1)}, u32[]{:S(2)}, u32[]{:S(2)}) collective-permute-start(bf16[2,4,16,1024]{3,2,1,0:T(8,128)(2,1)} %get-tuple-element.24), channel_id=1, source_target_pairs={{0,24},{8,16},{16,8},{24,0},{1,25},{9,17},{17,9},{25,1},{2,26},{10... | collective-permute-start | bytes 786440 | tf_op jit(solution)/shard_map/ppermute | solution.py:628
  45.4 3.5 %all-to-all-start.1 = ((bf16[8,16,2048]{2,1,0:T(8,128)(2,1)}), bf16[8,16,2048]{2,1,0:T(8,128)(2,1)S(1)}, u32[]{:S(2)}, u32[]{:S(2)}) async-start(bf16[8,16,2048]{2,1,0:T(8,128)(2,1)} %bitcast.14), calls=%async_computation.1 | async-start | bytes 1048576 | tf_op jit(solution)/shard_map/all_to_all | solution.py:726
  49.0 0.4 collective-permute-start.14
  49.3 2.1 %collective-permute-done.15.refs_10_ = bf16[64,1152]{1,0:T(8,128)(2,1)S(1)} collective-permute-done((bf16[64,1152]{1,0:T(8,128)(2,1)}, bf16[64,1152]{1,0:T(8,128)(2,1)S(1)}, u32[]{:S(2)}, u32[]{:S(2)}) %collective-permute-start.15) | collective-permute-done | bytes 147488 | tf_op jit(solution)/shard_map/ppermute | solution.py:628
  51.5 3.9 %collective-permute-done.14.refs_9_ = bf16[64,1152]{1,0:T(8,128)(2,1)S(1)} collective-permute-done((bf16[64,1152]{1,0:T(8,128)(2,1)}, bf16[64,1152]{1,0:T(8,128)(2,1)S(1)}, u32[]{:S(2)}, u32[]{:S(2)}) %collective-permute-start.14) | collective-permute-done | bytes 147488 | tf_op jit(solution)/shard_map/ppermute | solution.py:628
  55.4 0.5 collective-permute-start.11
  56.0 1.0 %collective-permute-done.9.refs_3_ = bf16[2,4,16,1024]{3,2,1,0:T(8,128)(2,1)S(1)} collective-permute-done((bf16[2,4,16,1024]{3,2,1,0:T(8,128)(2,1)}, bf16[2,4,16,1024]{3,2,1,0:T(8,128)(2,1)S(1)}, u32[]{:S(2)}, u32[]{:S(2)}) %collective-permute-start.9) | collective-permute-done | bytes 262176 | tf_op jit(solution)/shard_map/ppermute | solution.py:628
  57.0 0.5 collective-permute-start.19
  57.6 1.1 %collective-permute-done.19.refs_14_ = bf16[64,1152]{1,0:T(8,128)(2,1)S(1)} collective-permute-done((bf16[64,1152]{1,0:T(8,128)(2,1)S(1)}, bf16[64,1152]{1,0:T(8,128)(2,1)S(1)}, u32[]{:S(2)}, u32[]{:S(2)}) %collective-permute-start.19) | collective-permute-done | bytes 147488 | tf_op jit(solution)/shard_map/ppermute | solution.py:628
  58.7 0.2 collective-permute-done.18.refs_13_
  58.9 3.0 %all-to-all-done.1.refs_23_ = bf16[8,16,2048]{2,1,0:T(8,128)(2,1)S(1)} async-done(((bf16[8,16,2048]{2,1,0:T(8,128)(2,1)}), bf16[8,16,2048]{2,1,0:T(8,128)(2,1)S(1)}, u32[]{:S(2)}, u32[]{:S(2)}) %all-to-all-start.1) | async-done | bytes 524320 | tf_op jit(solution)/shard_map/all_to_all | solution.py:726
  62.1 0.7 copy-done.2
  62.8 0.1 copy-done.7
  62.9 0.1 copy-done.8
  63.0 0.7 copy-done.9
  63.7 8.0 %gradients.1 = (bf16[16,4,2048]{2,1,0:T(4,128)(2,1)}, bf16[1024,256]{1,0:T(8,128)(2,1)}, bf16[256,1024]{1,0:T(8,128)(2,1)}) custom-call(bf16[2,4,16,1024]{3,2,1,0:T(8,128)(2,1)} %get-tuple-element.21.refs_0_, bf16[2,4,16,1024]{3,2,1,0:T(8,128)(2,1)} %copy-done.3, bf16[2,4,16,1024]{3,2,1,0:T(8,128)(2,1)} %copy-done.4, bf16[2,4,16,1024]{3,2,1,0:T(8,128)(2,1)} %copy-done.5, ...), custom_call_target="tpu_custom_call" | custom-call | bytes 1048576 | tf_op jit(solution)/shard_map/gradients/pallas_call | solution.py:732
  (61 shorter events, 0.4 us)
Async XLA Ops:
  0.6 8.1 %copy-start.19 = (bf16[1,1,4096]{2,1,0:T(2,128)(2,1)S(1)}, bf16[1,1,4096]{2,1,0:T(2,128)(2,1)}, u32[]{:S(2)}) copy-start(bf16[1,1,4096]{2,1,0:T(2,128)(2,1)} %param.11) | copy-start | bytes 24580
  0.6 17.2 %collective-permute-start.4 = (bf16[4096,256]{1,0:T(8,128)(2,1)}, bf16[4096,256]{1,0:T(8,128)(2,1)S(1)}, u32[]{:S(2)}, u32[]{:S(2)}) collective-permute-start(bf16[4096,256]{1,0:T(8,128)(2,1)} %bitcast.7), channel_id=1, source_target_pairs={{0,1},{1,0},{2,3},{3,2},{4,5},{5,4},{6,7},{7,6},{8,9},{9,8},{10,11... | collective-permute-start | bytes 6291464 | tf_op jit(solution)/shard_map/ppermute | solution.py:628
  1.2 23.0 %collective-permute-start.5 = (bf16[256,4096]{1,0:T(8,128)(2,1)}, bf16[256,4096]{1,0:T(8,128)(2,1)}, u32[]{:S(2)}, u32[]{:S(2)}) collective-permute-start(bf16[256,4096]{1,0:T(8,128)(2,1)} %bitcast.10), channel_id=1, source_target_pairs={{0,1},{1,0},{2,3},{3,2},{4,5},{5,4},{6,7},{7,6},{8,9},{9,8},{10,11... | collective-permute-start | bytes 6291464 | tf_op jit(solution)/shard_map/ppermute | solution.py:628
  3.6 20.6 %all-to-all-start = ((bf16[8,2,16,2048]{3,2,1,0:T(8,128)(2,1)}), bf16[8,2,16,2048]{3,2,1,0:T(8,128)(2,1)S(1)}, u32[]{:S(2)}, u32[]{:S(2)}) async-start(bf16[8,2,16,2048]{3,2,1,0:T(8,128)(2,1)} %pack.1._), calls=%async_computation | async-start | bytes 2097152 | tf_op jit(solution)/shard_map/all_to_all | solution.py:689
  8.8 7.5 %collective-permute-start.6 = (bf16[1,4096]{1,0:T(2,128)(2,1)S(1)}, bf16[1,4096]{1,0:T(2,128)(2,1)S(1)}, u32[]{:S(2)}, u32[]{:S(2)}) collective-permute-start(bf16[1,4096]{1,0:T(2,128)(2,1)S(1)} %bitcast.17), channel_id=1, source_target_pairs={{0,1},{1,0},{2,3},{3,2},{4,5},{5,4},{6,7},{7,6},{8,9},{9,8},{10,11... | collective-permute-start | bytes 24584 | tf_op jit(solution)/shard_map/ppermute | solution.py:628
  11.6 22.9 %collective-permute-start = (bf16[80,1024]{1,0:T(8,128)(2,1)}, bf16[80,1024]{1,0:T(8,128)(2,1)S(1)}, u32[]{:S(2)}, u32[]{:S(2)}) collective-permute-start(bf16[80,1024]{1,0:T(8,128)(2,1)} %get-tuple-element.16), channel_id=1, source_target_pairs={{0,0},{1,4},{2,2},{3,6},{4,1},{5,5},{6,3},{7,7},{8,8},{9,12},{10,1... | collective-permute-start | bytes 491528 | tf_op jit(solution)/shard_map/ppermute | solution.py:692
  13.1 25.1 %collective-permute-start.1 = (bf16[80,1024]{1,0:T(8,128)(2,1)}, bf16[80,1024]{1,0:T(8,128)(2,1)S(1)}, u32[]{:S(2)}, u32[]{:S(2)}) collective-permute-start(bf16[80,1024]{1,0:T(8,128)(2,1)} %get-tuple-element.17), channel_id=1, source_target_pairs={{0,1},{1,5},{2,3},{3,7},{4,0},{5,4},{6,2},{7,6},{8,9},{9,13},{10,1... | collective-permute-start | bytes 491528 | tf_op jit(solution)/shard_map/ppermute | solution.py:692
  16.3 7.9 %copy-start.20 = (bf16[1,4096]{1,0:T(2,128)(2,1)}, bf16[1,4096]{1,0:T(2,128)(2,1)S(1)}, u32[]{:S(2)}) copy-start(bf16[1,4096]{1,0:T(2,128)(2,1)S(1)} %collective-permute-done.6.other_gain.refs_21_) | copy-start | bytes 24580
  16.3 21.9 %collective-permute-start.2 = (bf16[80,1024]{1,0:T(8,128)(2,1)}, bf16[80,1024]{1,0:T(8,128)(2,1)}, u32[]{:S(2)}, u32[]{:S(2)}) collective-permute-start(bf16[80,1024]{1,0:T(8,128)(2,1)} %get-tuple-element.18), channel_id=1, source_target_pairs={{0,2},{1,6},{2,0},{3,4},{4,3},{5,7},{6,1},{7,5},{8,10},{9,14},{10,... | collective-permute-start | bytes 491528 | tf_op jit(solution)/shard_map/ppermute | solution.py:692
  17.8 6.3 %copy-start = (bf16[4096,256]{1,0:T(8,128)(2,1)}, bf16[4096,256]{1,0:T(8,128)(2,1)S(1)}, u32[]{:S(2)}) copy-start(bf16[4096,256]{1,0:T(8,128)(2,1)S(1)} %collective-permute-done.4.other_dn.refs_19_) | copy-start | bytes 6291460
  17.9 20.4 %collective-permute-start.3 = (bf16[80,1024]{1,0:T(8,128)(2,1)}, bf16[80,1024]{1,0:T(8,128)(2,1)}, u32[]{:S(2)}, u32[]{:S(2)}) collective-permute-start(bf16[80,1024]{1,0:T(8,128)(2,1)} %get-tuple-element.19), channel_id=1, source_target_pairs={{0,3},{1,7},{2,1},{3,5},{4,2},{5,6},{6,0},{7,4},{8,11},{9,15},{10,... | collective-permute-start | bytes 491528 | tf_op jit(solution)/shard_map/ppermute | solution.py:692
  34.4 8.7 %collective-permute-start.17 = (bf16[64,1152]{1,0:T(8,128)(2,1)}, bf16[64,1152]{1,0:T(8,128)(2,1)S(1)}, u32[]{:S(2)}, u32[]{:S(2)}) collective-permute-start(bf16[64,1152]{1,0:T(8,128)(2,1)} %get-tuple-element.20.refs_4_.refs_8_), channel_id=1, source_target_pairs={{0,1},{1,0},{2,3},{3,2},{4,5},{5,4},{6,7},{7,6},{8,9},{9,8},{10,11... | collective-permute-start | bytes 442376 | tf_op jit(solution)/shard_map/ppermute | solution.py:628
  34.5 14.4 %collective-permute-start.16 = (bf16[64,1152]{1,0:T(8,128)(2,1)}, bf16[64,1152]{1,0:T(8,128)(2,1)S(1)}, u32[]{:S(2)}, u32[]{:S(2)}) collective-permute-start(bf16[64,1152]{1,0:T(8,128)(2,1)} %get-tuple-element.20.refs_4_.refs_8_), channel_id=1, source_target_pairs={{0,6},{2,4},{4,2},{6,0},{1,7},{3,5},{5,3},{7,1},{8,14},{10,12},{12... | collective-permute-start | bytes 442376 | tf_op jit(solution)/shard_map/ppermute | solution.py:628
  38.2 13.3 %collective-permute-start.15 = (bf16[64,1152]{1,0:T(8,128)(2,1)}, bf16[64,1152]{1,0:T(8,128)(2,1)S(1)}, u32[]{:S(2)}, u32[]{:S(2)}) collective-permute-start(bf16[64,1152]{1,0:T(8,128)(2,1)} %get-tuple-element.20.refs_4_.refs_8_), channel_id=1, source_target_pairs={{0,4},{2,6},{4,0},{6,2},{1,5},{3,7},{5,1},{7,3},{8,12},{10,14},{12... | collective-permute-start | bytes 442376 | tf_op jit(solution)/shard_map/ppermute | solution.py:628
  42.0 13.4 %collective-permute-start.7 = (bf16[2,4,16,1024]{3,2,1,0:T(8,128)(2,1)}, bf16[2,4,16,1024]{3,2,1,0:T(8,128)(2,1)S(1)}, u32[]{:S(2)}, u32[]{:S(2)}) collective-permute-start(bf16[2,4,16,1024]{3,2,1,0:T(8,128)(2,1)} %get-tuple-element.22), channel_id=1, source_target_pairs={{0,8},{8,0},{16,24},{24,16},{1,9},{9,1},{17,25},{25,17},{2,10},{10... | collective-permute-start | bytes 786440 | tf_op jit(solution)/shard_map/ppermute | solution.py:628
  42.5 13.4 %collective-permute-start.8 = (bf16[2,4,16,1024]{3,2,1,0:T(8,128)(2,1)}, bf16[2,4,16,1024]{3,2,1,0:T(8,128)(2,1)S(1)}, u32[]{:S(2)}, u32[]{:S(2)}) collective-permute-start(bf16[2,4,16,1024]{3,2,1,0:T(8,128)(2,1)} %get-tuple-element.23), channel_id=1, source_target_pairs={{0,16},{8,24},{16,0},{24,8},{1,17},{9,25},{17,1},{25,9},{2,18},{10... | collective-permute-start | bytes 786440 | tf_op jit(solution)/shard_map/ppermute | solution.py:628
  43.1 18.9 %copy-start.12 = (bf16[64,1152]{1,0:T(8,128)(2,1)}, bf16[64,1152]{1,0:T(8,128)(2,1)S(1)}, u32[]{:S(2)}) copy-start(bf16[64,1152]{1,0:T(8,128)(2,1)S(1)} %collective-permute-done.17.refs_12_) | copy-start | bytes 442372
  43.1 13.9 %collective-permute-start.9 = (bf16[2,4,16,1024]{3,2,1,0:T(8,128)(2,1)}, bf16[2,4,16,1024]{3,2,1,0:T(8,128)(2,1)S(1)}, u32[]{:S(2)}, u32[]{:S(2)}) collective-permute-start(bf16[2,4,16,1024]{3,2,1,0:T(8,128)(2,1)} %get-tuple-element.24), channel_id=1, source_target_pairs={{0,24},{8,16},{16,8},{24,0},{1,25},{9,17},{17,9},{25,1},{2,26},{10... | collective-permute-start | bytes 786440 | tf_op jit(solution)/shard_map/ppermute | solution.py:628
  45.4 16.5 %all-to-all-start.1 = ((bf16[8,16,2048]{2,1,0:T(8,128)(2,1)}), bf16[8,16,2048]{2,1,0:T(8,128)(2,1)S(1)}, u32[]{:S(2)}, u32[]{:S(2)}) async-start(bf16[8,16,2048]{2,1,0:T(8,128)(2,1)} %bitcast.14), calls=%async_computation.1 | async-start | bytes 1048576 | tf_op jit(solution)/shard_map/all_to_all | solution.py:726
  49.0 13.1 %copy-start.13 = (bf16[64,1152]{1,0:T(8,128)(2,1)}, bf16[64,1152]{1,0:T(8,128)(2,1)S(1)}, u32[]{:S(2)}) copy-start(bf16[64,1152]{1,0:T(8,128)(2,1)S(1)} %collective-permute-done.16.refs_11_) | copy-start | bytes 442372
  49.0 6.4 %collective-permute-start.14 = (bf16[64,1152]{1,0:T(8,128)(2,1)}, bf16[64,1152]{1,0:T(8,128)(2,1)S(1)}, u32[]{:S(2)}, u32[]{:S(2)}) collective-permute-start(bf16[64,1152]{1,0:T(8,128)(2,1)} %get-tuple-element.20.refs_4_.refs_8_), channel_id=1, source_target_pairs={{0,2},{2,0},{4,6},{6,4},{1,3},{3,1},{5,7},{7,5},{8,10},{10,8},{12,... | collective-permute-start | bytes 442376 | tf_op jit(solution)/shard_map/ppermute | solution.py:628
  51.5 10.6 %copy-start.14 = (bf16[64,1152]{1,0:T(8,128)(2,1)}, bf16[64,1152]{1,0:T(8,128)(2,1)S(1)}, u32[]{:S(2)}) copy-start(bf16[64,1152]{1,0:T(8,128)(2,1)S(1)} %collective-permute-done.15.refs_10_) | copy-start | bytes 442372
  51.5 5.5 %collective-permute-start.10 = (bf16[2,4,16,1024]{3,2,1,0:T(8,128)(2,1)}, bf16[2,4,16,1024]{3,2,1,0:T(8,128)(2,1)S(1)}, u32[]{:S(2)}, u32[]{:S(2)}) collective-permute-start(bf16[2,4,16,1024]{3,2,1,0:T(8,128)(2,1)} %get-tuple-element.21.refs_0_), channel_id=1, source_target_pairs={{0,1},{1,0},{2,3},{3,2},{4,5},{5,4},{6,7},{7,6},{8,9},{9,8},{10,11... | collective-permute-start | bytes 786440 | tf_op jit(solution)/shard_map/ppermute | solution.py:628
  55.4 6.6 %copy-start.15 = (bf16[64,1152]{1,0:T(8,128)(2,1)}, bf16[64,1152]{1,0:T(8,128)(2,1)S(1)}, u32[]{:S(2)}) copy-start(bf16[64,1152]{1,0:T(8,128)(2,1)S(1)} %collective-permute-done.14.refs_9_) | copy-start | bytes 442372
  55.4 2.1 %collective-permute-start.20 = (bf16[64,1152]{1,0:T(8,128)(2,1)S(1)}, bf16[64,1152]{1,0:T(8,128)(2,1)S(1)}, u32[]{:S(2)}, u32[]{:S(2)}) collective-permute-start(bf16[64,1152]{1,0:T(8,128)(2,1)S(1)} %collective-permute-done.16.refs_11_), channel_id=1, source_target_pairs={{0,1},{1,0},{2,3},{3,2},{4,5},{5,4},{6,7},{7,6},{8,9},{9,8},{10,11... | collective-permute-start | bytes 442376 | tf_op jit(solution)/shard_map/ppermute | solution.py:628
  55.4 6.6 %copy-start.3 = (bf16[2,4,16,1024]{3,2,1,0:T(8,128)(2,1)}, bf16[2,4,16,1024]{3,2,1,0:T(8,128)(2,1)S(1)}, u32[]{:S(2)}) copy-start(bf16[2,4,16,1024]{3,2,1,0:T(8,128)(2,1)S(1)} %collective-permute-done.7.refs_1_) | copy-start | bytes 786436
  55.4 6.6 %collective-permute-start.11 = (bf16[2,4,16,1024]{3,2,1,0:T(8,128)(2,1)S(1)}, bf16[2,4,16,1024]{3,2,1,0:T(8,128)(2,1)S(1)}, u32[]{:S(2)}, u32[]{:S(2)}) collective-permute-start(bf16[2,4,16,1024]{3,2,1,0:T(8,128)(2,1)S(1)} %collective-permute-done.7.refs_1_), channel_id=1, source_target_pairs={{0,1},{1,0},{2,3},{3,2},{4,5},{5,4},{6,7},{7,6},{8,9},{9,8},{10,11... | collective-permute-start | bytes 786440 | tf_op jit(solution)/shard_map/ppermute | solution.py:628
  55.9 6.1 %copy-start.4 = (bf16[2,4,16,1024]{3,2,1,0:T(8,128)(2,1)}, bf16[2,4,16,1024]{3,2,1,0:T(8,128)(2,1)S(1)}, u32[]{:S(2)}) copy-start(bf16[2,4,16,1024]{3,2,1,0:T(8,128)(2,1)S(1)} %collective-permute-done.8.refs_2_) | copy-start | bytes 786436
  55.9 6.1 %collective-permute-start.12 = (bf16[2,4,16,1024]{3,2,1,0:T(8,128)(2,1)S(1)}, bf16[2,4,16,1024]{3,2,1,0:T(8,128)(2,1)S(1)}, u32[]{:S(2)}, u32[]{:S(2)}) collective-permute-start(bf16[2,4,16,1024]{3,2,1,0:T(8,128)(2,1)S(1)} %collective-permute-done.8.refs_2_), channel_id=1, source_target_pairs={{0,1},{1,0},{2,3},{3,2},{4,5},{5,4},{6,7},{7,6},{8,9},{9,8},{10,11... | collective-permute-start | bytes 786440 | tf_op jit(solution)/shard_map/ppermute | solution.py:628
  57.0 5.0 %collective-permute-start.13 = (bf16[2,4,16,1024]{3,2,1,0:T(8,128)(2,1)S(1)}, bf16[2,4,16,1024]{3,2,1,0:T(8,128)(2,1)S(1)}, u32[]{:S(2)}, u32[]{:S(2)}) collective-permute-start(bf16[2,4,16,1024]{3,2,1,0:T(8,128)(2,1)S(1)} %collective-permute-done.9.refs_3_), channel_id=1, source_target_pairs={{0,1},{1,0},{2,3},{3,2},{4,5},{5,4},{6,7},{7,6},{8,9},{9,8},{10,11... | collective-permute-start | bytes 786440 | tf_op jit(solution)/shard_map/ppermute | solution.py:628
  57.0 1.7 %collective-permute-start.19 = (bf16[64,1152]{1,0:T(8,128)(2,1)S(1)}, bf16[64,1152]{1,0:T(8,128)(2,1)S(1)}, u32[]{:S(2)}, u32[]{:S(2)}) collective-permute-start(bf16[64,1152]{1,0:T(8,128)(2,1)S(1)} %collective-permute-done.15.refs_10_), channel_id=1, source_target_pairs={{0,1},{1,0},{2,3},{3,2},{4,5},{5,4},{6,7},{7,6},{8,9},{9,8},{10,11... | collective-permute-start | bytes 442376 | tf_op jit(solution)/shard_map/ppermute | solution.py:628
  57.5 1.4 %collective-permute-start.18 = (bf16[64,1152]{1,0:T(8,128)(2,1)S(1)}, bf16[64,1152]{1,0:T(8,128)(2,1)S(1)}, u32[]{:S(2)}, u32[]{:S(2)}) collective-permute-start(bf16[64,1152]{1,0:T(8,128)(2,1)S(1)} %collective-permute-done.14.refs_9_), channel_id=1, source_target_pairs={{0,1},{1,0},{2,3},{3,2},{4,5},{5,4},{6,7},{7,6},{8,9},{9,8},{10,11... | collective-permute-start | bytes 442376 | tf_op jit(solution)/shard_map/ppermute | solution.py:628
  (12 other events, 30.1 us)

commit v10 on v9

--- a/solution.py
+++ b/solution.py
@@ -487,123 +487,159 @@
         )
         d_act = d_act + matmul(grad.astype(jnp.bfloat16), up_buf[0, :, here], TRANS_RHS)
     d_pre_0 = (d_act * slope_0).astype(jnp.bfloat16)
-    for at, value in enumerate((act_0, act_1, d_pre_0, d_pre_1)):
-        small[:, at * rank : (at + 1) * rank] = value
     moments = (mean_0, inverse_0, mean_1, inverse_1, shift, along)
-    small[:, 4 * rank :] = side_by_side(moments, tokens)
+    kept = (act_0, act_1, d_pre_0, d_pre_1, side_by_side(moments, tokens))
+    for e in range(experts):
+        start = pl.multiple_of((e ^ lax.axis_index("expert")) * rows, rows)
+        for at, value in enumerate(kept):
+            cols = slice(at * rank, at * rank + value.shape[1])
+            small[pl.ds(start, rows), cols] = value[e * rows : (e + 1) * rows]
 
 
 def gradient_kernel(experts, sources, sizes, *refs):
-    sides, refs = (refs[:experts], refs[experts : 2 * experts]), refs[2 * experts :]
+    sides, refs = refs[: 2 * experts], refs[2 * experts :]
     smalls, refs = refs[:sources], refs[sources:]
     own, other, refs = refs[:3], refs[3:6], refs[6:]
-    (ids, back, out_hidden, grad_dn, grad_upper, id_buf, dn_buf, up_buf, gain_buf, small, moments,
-     lows, grads, ups, downs, sems) = refs
-    id_copy = pltpu.make_async_copy(ids, id_buf, sems.at[4])
-    id_copy.start()
+    ids, back_in, out_hidden, grad_dn, grad_upper = refs[:5]
+    (id_buf, back, result, dn_buf, up_buf, gain_buf, wide_buf, small, moments, turned, lows, grads,
+     dn_out, up_out, small_sems, wide_sems, sems) = refs[5:]
     core = lax.axis_index("segment")
     place = lax.axis_index("dp")
-    _, replicas, _, slab = sides[0][0].shape
-    rows = smalls[0].shape[0]
+    rows, slab = smalls[0].shape[0], sides[0].shape[3]
+    replicas = sources // 2
     rank = dn_buf.shape[1]
+    columns = 256
+    chunks = range(0, slab, columns)
     features = pl.ds(pl.multiple_of(place * slab, slab), slab)
 
-    def copies(up, gain_first, dn, gain_second):
+    def weight_copies(up, gain_first, dn, gain_second):
         moves = (
             (up.at[:, features], up_buf),
-            (dn.at[features, :], dn_buf),
             (gain_first.at[:, features], gain_buf.at[0]),
             (gain_second.at[:, features], gain_buf.at[1]),
+            (dn.at[features, :], dn_buf),
         )
         return [
             pltpu.make_async_copy(source, target, sems.at[at])
             for at, (source, target) in enumerate(moves)
         ]
 
+    early = [
+        pltpu.make_async_copy(ids, id_buf, sems.at[4]),
+        pltpu.make_async_copy(back_in, back, sems.at[5]),
+    ]
+    small_copies = [
+        pltpu.make_async_copy(
+            source, small.at[at * rows : (at + 1) * rows], small_sems.at[at]
+        )
+        for at, source in enumerate(smalls)
+    ]
+    wide_copies = [
+        [
+            pltpu.make_async_copy(
+                side.at[:, :, :, col : col + columns],
+                wide_buf.at[at, :, :, :, col : col + columns],
+                wide_sems.at[col // columns, at],
+            )
+            for at, side in enumerate(sides)
+        ]
+        for col in chunks
+    ]
+    for copy in early + small_copies:
+        copy.start()
+
     @pl.when(core == 0)
     def _():
-        for copy in copies(own[1], own[2], other[0], other[2]):
+        for copy in weight_copies(own[1], own[2], other[0], other[2]):
             copy.start()
 
     @pl.when(core != 0)
     def _():
-        for copy in copies(other[1], other[2], own[0], own[2]):
+        for copy in weight_copies(other[1], other[2], own[0], own[2]):
             copy.start()
 
-    per_expert = rows // experts
-    for source in range(sources):
-        for step in range(experts):
-            to = source * rows + step * per_expert
-            start = (lax.axis_index("expert") ^ step) * per_expert
-            small[to : to + per_expert] = smalls[source][
-                pl.ds(pl.multiple_of(start, per_expert), per_expert)
-            ]
+    for copies in wide_copies:
+        for copy in copies:
+            copy.start()
+    for copy in early:
+        copy.wait()
+    unpack(sizes, id_buf, back, result)
+    leaving = [pltpu.make_async_copy(result, out_hidden, sems.at[6])]
+    leaving[0].start()
+    for copy in small_copies + weight_copies(own[1], own[2], other[0], other[2]):
+        copy.wait()
 
     def sliced(source, which, here):
-        side, near = sides[source // replicas], source % replicas
-        return jnp.concatenate([side[e][which, near, :, here] for e in range(experts)], axis=0)
-
-    id_copy.wait()
-    unpack(sizes, id_buf, back, out_hidden)
-    held = lax.broadcasted_iota(jnp.int32, (128, 6 * 128), 0)
-    wanted = lax.broadcasted_iota(jnp.int32, (128, 6 * 128), 1) // 128
-    adds = (held // 3 == wanted).astype(jnp.float32).astype(jnp.bfloat16)
-    moments[...] = matmul(small[:, 4 * rank :], adds)
-    for copy in copies(own[1], own[2], other[0], other[2]):
-        copy.wait()
-
-    columns = 256
+        first, near = (source // replicas) * experts, source % replicas
+        return jnp.concatenate(
+            [wide_buf[first + step, which, near, :, here] for step in range(experts)], axis=0
+        )
 
     def moment(at, index):
         value = moments[at, index * 128 : (index + 1) * 128]
         return jnp.concatenate([value] * (columns // 128), axis=1)
 
-    for col in range(0, slab, columns):
-        here = slice(col, col + columns)
-        ups[...] = matmul(small[:, :rank], up_buf[:, here])
-        scales = [gain_buf[at, :, here].astype(jnp.float32) for at in range(2)]
-
-        @pl.when(core == 0)
-        def _():
-            downs[...] = matmul(small[:, 3 * rank : 4 * rank], dn_buf[here, :], TRANS_RHS)
+    def work(first):
+        held = lax.broadcasted_iota(jnp.int32, (128, 6 * 128), 0)
+        wanted = lax.broadcasted_iota(jnp.int32, (128, 6 * 128), 1) // 128
+        adds = (held // 3 == wanted).astype(jnp.float32).astype(jnp.bfloat16)
+        moments[...] = matmul(small[:, 4 * rank :], adds)
+        act, d_pre = (0, 2) if first else (1, 3)
+        turned[0] = small[:, act * rank : (act + 1) * rank].T
+        turned[1] = small[:, d_pre * rank : (d_pre + 1) * rank].T
+        for index, col in enumerate(chunks):
+            here = slice(col, col + columns)
+            for copy in wide_copies[index]:
+                copy.wait()
+            ups = matmul(small[:, :rank], up_buf[:, here])
+            scales = [gain_buf[at, :, here].astype(jnp.float32) for at in range(2)]
+            if first:
+                downs = matmul(small[:, 3 * rank : 4 * rank], dn_buf[here, :], TRANS_RHS)
             for source in range(sources):
                 at = slice(source * rows, (source + 1) * rows)
                 wide = sliced(source, 0, here).astype(jnp.float32)
-                normed = (wide - moment(at, 0)) * moment(at, 1)
-                lows[at, here] = (normed * scales[0]).astype(jnp.bfloat16)
+                grad_in = sliced(source, 1, here)
                 middle = (wide + ups[at]).astype(jnp.bfloat16).astype(jnp.float32)
                 inverse = moment(at, 3)
                 normed = (middle - moment(at, 2)) * inverse
-                d_norm = downs[at] * scales[1]
-                grads[at, here] = (
-                    sliced(source, 1, here).astype(jnp.float32)
-                    + inverse * (d_norm - moment(at, 4) - normed * moment(at, 5))
-                ).astype(jnp.bfloat16)
-
-        @pl.when(core != 0)
-        def _():
-            for source in range(sources):
-                at = slice(source * rows, (source + 1) * rows)
-                wide = sliced(source, 0, here).astype(jnp.float32)
-                middle = (wide + ups[at]).astype(jnp.bfloat16).astype(jnp.float32)
-                normed = (middle - moment(at, 2)) * moment(at, 3)
-                lows[at, here] = (normed * scales[1]).astype(jnp.bfloat16)
-                grads[at, here] = sliced(source, 1, here)
-
-    def finish(act, d_pre):
-        for col in range(0, slab, columns):
-            here = slice(col, col + columns)
-            turned = matmul(d_pre, lows[:, here], TRANS_LHS).astype(jnp.bfloat16)
-            grad_dn[here, :] = turned.T
-            grad_upper[:, here] = matmul(act, grads[:, here], TRANS_LHS).astype(jnp.bfloat16)
+                if first:
+                    entered = (wide - moment(at, 0)) * moment(at, 1)
+                    lows[index, at] = (entered * scales[0]).astype(jnp.bfloat16)
+                    d_norm = downs[at] * scales[1]
+                    grads[index, at] = (
+                        grad_in.astype(jnp.float32)
+                        + inverse * (d_norm - moment(at, 4) - normed * moment(at, 5))
+                    ).astype(jnp.bfloat16)
+                else:
+                    lows[index, at] = (normed * scales[1]).astype(jnp.bfloat16)
+                    grads[index, at] = grad_in
+            dn_out[here, :] = matmul(turned[1], lows[index]).astype(jnp.bfloat16).T
+            up_out[index] = matmul(turned[0], grads[index]).astype(jnp.bfloat16)
+            for copy in out_copies(index, here):
+                copy.start()
+
+    def out_copies(index, here):
+        return [
+            pltpu.make_async_copy(
+                dn_out.at[here, :], grad_dn.at[here, :], sems.at[7 + 2 * index]
+            ),
+            pltpu.make_async_copy(
+                up_out.at[index], grad_upper.at[:, here], sems.at[8 + 2 * index]
+            ),
+        ]
 
     @pl.when(core == 0)
     def _():
-        finish(small[:, :rank], small[:, 2 * rank : 3 * rank])
+        work(True)
 
     @pl.when(core != 0)
     def _():
-        finish(small[:, rank : 2 * rank], small[:, 3 * rank : 4 * rank])
+        work(False)
+
+    for index, col in enumerate(chunks):
+        leaving += out_copies(index, slice(col, col + columns))
+    for copy in leaving:
+        copy.wait()
 
 
 VMEM = pl.BlockSpec(memory_space=pltpu.VMEM)
@@ -695,7 +731,7 @@
     out, small = call(
         chain_kernel,
         "chain",
-        60,
+        50,
         [HBM] * 7,
         [((experts, 2, rows, part), bf16), ((tokens, 4 * rank + 128), bf16)],
         [
@@ -714,13 +750,14 @@
     slices = call(
         functools.partial(repack_kernel, length, capacity),
         "repack",
-        60,
+        16,
         [VMEM] * 4 + [HBM],
         [((2, replicas, rows, slab), bf16)] * experts,
     )(*slabs, small)
     mine = [slices[0]] + [across(slices[step], "expert", step) for step in range(1, experts)]
     theirs = [across(block, "segment", 1) for block in mine]
-    near = [small] + [across(small, "dp", step) for step in range(1, replicas)]
+    one_away = across(small, "dp", 1)
+    near = [small, one_away, across(small, "dp", 2), across(one_away, "dp", 2)]
     smalls = near + [across(piece, "segment", 1) for piece in near]
 
     back = lax.all_to_all(
@@ -733,21 +770,28 @@
         functools.partial(gradient_kernel, experts, sources, sizes),
         "gradients",
         60,
-        [VMEM] * (2 * experts + sources) + [HBM] * 7 + [VMEM],
+        [HBM] * (2 * experts + sources + 8),
         [(hidden_in.shape, bf16), ((slab, rank), bf16), ((rank, slab), bf16)],
         [
             pltpu.SMEM(cluster_ids.shape, jnp.int32),
+            pltpu.VMEM(back.shape, bf16),
+            pltpu.VMEM(hidden_in.shape, bf16),
             pltpu.VMEM((slab, rank), bf16),
             pltpu.VMEM((rank, slab), bf16),
             pltpu.VMEM((2, 1, slab), bf16),
+            pltpu.VMEM((2 * experts, 2, replicas, rows, slab), bf16),
             pltpu.VMEM((all_tokens, 4 * rank + 128), bf16),
             pltpu.VMEM((all_tokens, 6 * 128), f32),
-            pltpu.VMEM((all_tokens, slab), bf16),
-            pltpu.VMEM((all_tokens, slab), bf16),
-            pltpu.VMEM((all_tokens, 256), f32),
-            pltpu.VMEM((all_tokens, 256), f32),
-            pltpu.SemaphoreType.DMA((5,)),
+            pltpu.VMEM((2, rank, all_tokens), bf16),
+            pltpu.VMEM((slab // 256, all_tokens, 256), bf16),
+            pltpu.VMEM((slab // 256, all_tokens, 256), bf16),
+            pltpu.VMEM((slab, rank), bf16),
+            pltpu.VMEM((slab // 256, rank, 256), bf16),
+            pltpu.SemaphoreType.DMA((sources,)),
+            pltpu.SemaphoreType.DMA((slab // 256, 2 * experts)),
+            pltpu.SemaphoreType.DMA((7 + 2 * (slab // 256),)),
         ],
+        outs_in=HBM,
     )(*mine, *theirs, *smalls, *own, *other, cluster_ids, back)
     return (out_hidden, grad_dn[None, None], grad_upper[None, None])
 

time: 72 us -> 70.2 us (0.975)
  Pallas kernels: 24.9 us -> 20.4 us
  waiting for transfers between devices: 17.8 us -> 20.6 us
  local copies, waits for them, and re-layouts: 3.24 us -> 2.34 us
    ppermute x17, waiting for transfers between devices: 8.42 us -> 14.3 us  [across(): return lax.ppermute(block, axis, [(i, i ^ distance) for i in range(size)])]
    pallas_call x2, Pallas kernels: 12.3 us -> 9.16 us  [the longest x1 7.1 us: on_device_two_phases(): call(chain_kernel, 'chain', 50, [HBM] * 7, [((experts, 2, rows, part), bf...]
    all_to_all x1, waiting for transfers between devices: 3.02 us -> 0.01 us  [on_device_two_phases(): lax.all_to_all(out.reshape(groups, rows, part), sections, split_axis=0, c...]
    pallas_call x1, Pallas kernels: 7.98 us -> 6.58 us  [on_device_two_phases(): call(functools.partial(gradient_kernel, experts, sources, sizes), 'gradie...]
    unnamed x42 -> x40, local copies, waits for them, and re-layouts: 3.24 us -> 2.34 us
  transfers between devices with their start and end apart: 23 -> 23, of which waited for: 7 -> 5; matrix products, arithmetic and copies ran while one was open for 0% -> 0% of each run, Pallas kernels for 24% -> 20%
where the time goes in v10:
time: 70.2 us; the launch traced here: 69.8 us
  starting transfers between devices  25.5 us (36%)
  waiting for transfers between devices  20.6 us (29%)
  Pallas kernels  20.4 us (29%)
  local copies, waits for them, and re-layouts  2.34 us (3%)
  between operations  0.94 us (1%)
    ppermute x17, waiting for transfers between devices, across(): return lax.ppermute(block, axis, [(i, i ^ distance) for i in range(size)])  14.3 us
    ppermute x17, starting transfers between devices, across(): return lax.ppermute(block, axis, [(i, i ^ distance) for i in range(size)])  10.4 us
    pallas_call x1, Pallas kernels, on_device_two_phases(): call(chain_kernel, 'chain', 50, [HBM] * 7, [((experts, 2, rows, part), bf...  7.1 us
    pallas_call x1, Pallas kernels, on_device_two_phases(): call(functools.partial(gradient_kernel, experts, sources, sizes), 'gradie...  6.58 us
    all_to_all x1, waiting for transfers between devices, on_device_two_phases(): lax.all_to_all(send, sections, split_axis=0, concat_axis=0, tiled=True)  6.33 us
    ppermute x4, starting transfers between devices, on_device_two_phases(): lax.ppermute(block, ('dp', 'segment'), slab_route(replicas, turn // 2, tu...  6.29 us
    all_to_all x1, starting transfers between devices, on_device_two_phases(): lax.all_to_all(send, sections, split_axis=0, concat_axis=0, tiled=True)  5.29 us
    all_to_all x1, starting transfers between devices, on_device_two_phases(): lax.all_to_all(out.reshape(groups, rows, part), sections, split_axis=0, c...  3.51 us
  transfers between devices with their start and end apart: 23, of which 5 were waited for; matrix products, arithmetic and copies ran while one was open for 0% of the time, Pallas kernels for 20%

profile of v10, /device:TPU:0, one launch (start us, length us, event | category | flops | bytes accessed | tf_op | source)
XLA Modules:
  0.0 69.8 jit_solution(14404831132084691307)
XLA Ops:
  0.6 0.5 collective-permute-start.4
  1.2 0.1 collective-permute-start.5
  1.2 2.4 %pack.1._ = bf16[8,2,16,2048]{3,2,1,0:T(8,128)(2,1)} custom-call(s32[16]{0:T(128)} %refs_22_.1, bf16[16,4,2048]{2,1,0:T(4,128)(2,1)} %hidden.3, bf16[16,4,2048]{2,1,0:T(4,128)(2,1)} %cot.3), custom_call_target="tpu_custom_call" | custom-call | bytes 1048576 | tf_op jit(solution)/shard_map/pack/pallas_call | solution.py:695
  3.6 5.3 %all-to-all-start = ((bf16[8,2,16,2048]{3,2,1,0:T(8,128)(2,1)}), bf16[8,2,16,2048]{3,2,1,0:T(8,128)(2,1)S(1)}, u32[]{:S(2)}, u32[]{:S(2)}) async-start(bf16[8,2,16,2048]{3,2,1,0:T(8,128)(2,1)} %pack.1._), calls=%async_computation | async-start | bytes 2097152 | tf_op jit(solution)/shard_map/all_to_all | solution.py:725
  8.9 0.5 collective-permute-start.6
  9.4 2.3 %slabs.1 = (bf16[80,1024]{1,0:T(8,128)(2,1)}, bf16[80,1024]{1,0:T(8,128)(2,1)}, bf16[80,1024]{1,0:T(8,128)(2,1)}, bf16[80,1024]{1,0:T(8,128)(2,1)}) custom-call(s32[16]{0:T(128)} %refs_22_.1, bf16[16,4,2048]{2,1,0:T(4,128)(2,1)} %hidden.3, bf16[16,4,2048]{2,1,0:T(4,128)(2,1)} %cot.3, bf16[8,2,16,2048]{3,2,1,0:T(8,128)(2,1)} %pack.1._), custom_call_target="tpu_custom_call" | custom-call | bytes 1048576 | tf_op jit(solution)/shard_map/slabs/pallas_call | solution.py:709
  11.7 1.6 %collective-permute-start = (bf16[80,1024]{1,0:T(8,128)(2,1)}, bf16[80,1024]{1,0:T(8,128)(2,1)S(1)}, u32[]{:S(2)}, u32[]{:S(2)}) collective-permute-start(bf16[80,1024]{1,0:T(8,128)(2,1)} %get-tuple-element.16), channel_id=1, source_target_pairs={{0,0},{1,4},{2,2},{3,6},{4,1},{5,5},{6,3},{7,7},{8,8},{9,12},{10,1... | collective-permute-start | bytes 491528 | tf_op jit(solution)/shard_map/ppermute | solution.py:728
  13.3 3.1 %collective-permute-start.1 = (bf16[80,1024]{1,0:T(8,128)(2,1)}, bf16[80,1024]{1,0:T(8,128)(2,1)}, u32[]{:S(2)}, u32[]{:S(2)}) collective-permute-start(bf16[80,1024]{1,0:T(8,128)(2,1)} %get-tuple-element.17), channel_id=1, source_target_pairs={{0,1},{1,5},{2,3},{3,7},{4,0},{5,4},{6,2},{7,6},{8,9},{9,13},{10,1... | collective-permute-start | bytes 491528 | tf_op jit(solution)/shard_map/ppermute | solution.py:728
  16.4 1.6 %collective-permute-start.2 = (bf16[80,1024]{1,0:T(8,128)(2,1)}, bf16[80,1024]{1,0:T(8,128)(2,1)}, u32[]{:S(2)}, u32[]{:S(2)}) collective-permute-start(bf16[80,1024]{1,0:T(8,128)(2,1)} %get-tuple-element.18), channel_id=1, source_target_pairs={{0,2},{1,6},{2,0},{3,4},{4,3},{5,7},{6,1},{7,5},{8,10},{9,14},{10,... | collective-permute-start | bytes 491528 | tf_op jit(solution)/shard_map/ppermute | solution.py:728
  18.0 6.3 %all-to-all-done = bf16[8,2,16,2048]{3,2,1,0:T(8,128)(2,1)S(1)} async-done(((bf16[8,2,16,2048]{3,2,1,0:T(8,128)(2,1)}), bf16[8,2,16,2048]{3,2,1,0:T(8,128)(2,1)S(1)}, u32[]{:S(2)}, u32[]{:S(2)}) %all-to-all-start) | async-done | bytes 1048608 | tf_op jit(solution)/shard_map/all_to_all | solution.py:725
  24.4 7.1 %chain.1 = (bf16[4,2,16,2048]{3,2,1,0:T(8,128)(2,1)S(1)}, bf16[64,1152]{1,0:T(8,128)(2,1)S(1)}) custom-call(bf16[4,2,2,16,2048]{4,3,2,1,0:T(8,128)(2,1)S(1)} %bitcast.10, bf16[4096,256]{1,0:T(8,128)(2,1)S(1)} %bitcast.9, bf16[256,4096]{1,0:T(8,128)(2,1)} %bitcast.16, bf16[1,4096]{1,0:T(2,128)(2,1)S(1)} %bitcast.14, ...), custom_call_target="tpu_custom_call" | custom-call | flops 939524096 | bytes 10485760 | tf_op jit(solution)/shard_map/chain/pallas_call | solution.py:731
  31.6 2.6 %collective-permute-start.15 = (bf16[64,1152]{1,0:T(8,128)(2,1)S(1)}, bf16[64,1152]{1,0:T(8,128)(2,1)S(1)}, u32[]{:S(2)}, u32[]{:S(2)}) collective-permute-start(bf16[64,1152]{1,0:T(8,128)(2,1)S(1)} %get-tuple-element.20.refs_4_.refs_8_), channel_id=1, source_target_pairs={{0,4},{2,6},{4,0},{6,2},{1,5},{3,7},{5,1},{7,3},{8,12},{10,14},{12... | collective-permute-start | bytes 442376 | tf_op jit(solution)/shard_map/ppermute | solution.py:664
  34.2 2.1 %repack.1 = (bf16[2,4,16,1024]{3,2,1,0:T(8,128)(2,1)S(1)}, bf16[2,4,16,1024]{3,2,1,0:T(8,128)(2,1)S(1)}, bf16[2,4,16,1024]{3,2,1,0:T(8,128)(2,1)S(1)}, bf16[2,4,16,1024]{3,2,1,0:T(8,128)(2,1)S(1)}) custom-call(bf16[80,1024]{1,0:T(8,128)(2,1)S(1)} %collective-permute-done.refs_0_, bf16[80,1024]{1,0:T(8,128)(2,1)} %collective-permute-done.1.refs_1_, ...), custom_call_target="tpu_custom_call" | custom-call | bytes 1048576 | tf_op jit(solution)/shard_map/repack/pallas_call | solution.py:750
  36.3 1.2 %collective-permute-start.7 = (bf16[2,4,16,1024]{3,2,1,0:T(8,128)(2,1)S(1)}, bf16[2,4,16,1024]{3,2,1,0:T(8,128)(2,1)S(1)}, u32[]{:S(2)}, u32[]{:S(2)}) collective-permute-start(bf16[2,4,16,1024]{3,2,1,0:T(8,128)(2,1)S(1)} %get-tuple-element.22), channel_id=1, source_target_pairs={{0,8},{8,0},{16,24},{24,16},{1,9},{9,1},{17,25},{25,17},{2,10},{10... | collective-permute-start | bytes 786440 | tf_op jit(solution)/shard_map/ppermute | solution.py:664
  37.5 0.4 collective-permute-start.8
  37.9 2.0 %collective-permute-start.9 = (bf16[2,4,16,1024]{3,2,1,0:T(8,128)(2,1)S(1)}, bf16[2,4,16,1024]{3,2,1,0:T(8,128)(2,1)S(1)}, u32[]{:S(2)}, u32[]{:S(2)}) collective-permute-start(bf16[2,4,16,1024]{3,2,1,0:T(8,128)(2,1)S(1)} %get-tuple-element.24), channel_id=1, source_target_pairs={{0,24},{8,16},{16,8},{24,0},{1,25},{9,17},{17,9},{25,1},{2,26},{10... | collective-permute-start | bytes 786440 | tf_op jit(solution)/shard_map/ppermute | solution.py:664
  39.9 3.5 %all-to-all-start.1 = ((bf16[8,16,2048]{2,1,0:T(8,128)(2,1)}), bf16[8,16,2048]{2,1,0:T(8,128)(2,1)S(1)}, u32[]{:S(2)}, u32[]{:S(2)}) async-start(bf16[8,16,2048]{2,1,0:T(8,128)(2,1)} %bitcast.11), calls=%async_computation.1 | async-start | bytes 1048576 | tf_op jit(solution)/shard_map/all_to_all | solution.py:763
  43.4 1.6 %collective-permute-start.14 = (bf16[64,1152]{1,0:T(8,128)(2,1)S(1)}, bf16[64,1152]{1,0:T(8,128)(2,1)S(1)}, u32[]{:S(2)}, u32[]{:S(2)}) collective-permute-start(bf16[64,1152]{1,0:T(8,128)(2,1)S(1)} %get-tuple-element.20.refs_4_.refs_8_), channel_id=1, source_target_pairs={{0,2},{2,0},{4,6},{6,4},{1,3},{3,1},{5,7},{7,5},{8,10},{10,8},{12,... | collective-permute-start | bytes 442376 | tf_op jit(solution)/shard_map/ppermute | solution.py:664
  45.1 4.6 %collective-permute-done.14.refs_9_ = bf16[64,1152]{1,0:T(8,128)(2,1)S(1)} collective-permute-done((bf16[64,1152]{1,0:T(8,128)(2,1)S(1)}, bf16[64,1152]{1,0:T(8,128)(2,1)S(1)}, u32[]{:S(2)}, u32[]{:S(2)}) %collective-permute-start.14) | collective-permute-done | bytes 147488 | tf_op jit(solution)/shard_map/ppermute | solution.py:664
  49.7 0.4 collective-permute-start.16
  50.1 1.2 %collective-permute-done.8.refs_2_ = bf16[2,4,16,1024]{3,2,1,0:T(8,128)(2,1)S(1)} collective-permute-done((bf16[2,4,16,1024]{3,2,1,0:T(8,128)(2,1)S(1)}, bf16[2,4,16,1024]{3,2,1,0:T(8,128)(2,1)S(1)}, u32[]{:S(2)}, u32[]{:S(2)}) %collective-permute-start.8) | collective-permute-done | bytes 262176 | tf_op jit(solution)/shard_map/ppermute | solution.py:664
  51.3 0.5 collective-permute-start.12
  51.8 0.1 collective-permute-start.13
  51.9 0.4 collective-permute-start.18
  52.3 7.7 %collective-permute-done.16.refs_11_ = bf16[64,1152]{1,0:T(8,128)(2,1)S(1)} collective-permute-done((bf16[64,1152]{1,0:T(8,128)(2,1)S(1)}, bf16[64,1152]{1,0:T(8,128)(2,1)S(1)}, u32[]{:S(2)}, u32[]{:S(2)}) %collective-permute-start.16) | collective-permute-done | bytes 147488 | tf_op jit(solution)/shard_map/ppermute | solution.py:664
  60.1 0.7 %copy-done.19 = bf16[64,1152]{1,0:T(8,128)(2,1)} copy-done((bf16[64,1152]{1,0:T(8,128)(2,1)}, bf16[64,1152]{1,0:T(8,128)(2,1)S(1)}, u32[]{:S(2)}) %copy-start.19) | copy-done | bytes 147480
  60.8 0.8 %collective-permute-done.20.refs_15_ = bf16[64,1152]{1,0:T(8,128)(2,1)} collective-permute-done((bf16[64,1152]{1,0:T(8,128)(2,1)S(1)}, bf16[64,1152]{1,0:T(8,128)(2,1)}, u32[]{:S(2)}, u32[]{:S(2)}) %collective-permute-start.20) | collective-permute-done | bytes 147488 | tf_op jit(solution)/shard_map/ppermute | solution.py:664
  61.7 0.6 copy-done.6
  62.3 0.1 copy-done.11
  62.5 0.1 copy-done.12
  62.5 0.7 copy-done.13
  63.2 6.6 %gradients.1 = (bf16[16,4,2048]{2,1,0:T(4,128)(2,1)}, bf16[1024,256]{1,0:T(8,128)(2,1)}, bf16[256,1024]{1,0:T(8,128)(2,1)}) custom-call(bf16[2,4,16,1024]{3,2,1,0:T(8,128)(2,1)} %copy-done.3, bf16[2,4,16,1024]{3,2,1,0:T(8,128)(2,1)} %copy-done.7, bf16[2,4,16,1024]{3,2,1,0:T(8,128)(2,1)} %copy-done.8, bf16[2,4,16,1024]{3,2,1,0:T(8,128)(2,1)} %copy-done.9, ...), custom_call_target="tpu_custom_call" | custom-call | bytes 1048576 | tf_op jit(solution)/shard_map/gradients/pallas_call | solution.py:769
  (59 shorter events, 0.2 us)
Async XLA Ops:
  0.6 17.4 %collective-permute-start.4 = (bf16[4096,256]{1,0:T(8,128)(2,1)}, bf16[4096,256]{1,0:T(8,128)(2,1)}, u32[]{:S(2)}, u32[]{:S(2)}) collective-permute-start(bf16[4096,256]{1,0:T(8,128)(2,1)} %bitcast.7), channel_id=1, source_target_pairs={{0,1},{1,0},{2,3},{3,2},{4,5},{5,4},{6,7},{7,6},{8,9},{9,8},{10,11... | collective-permute-start | bytes 6291464 | tf_op jit(solution)/shard_map/ppermute | solution.py:664
  1.2 23.2 %collective-permute-start.5 = (bf16[256,4096]{1,0:T(8,128)(2,1)}, bf16[256,4096]{1,0:T(8,128)(2,1)}, u32[]{:S(2)}, u32[]{:S(2)}) collective-permute-start(bf16[256,4096]{1,0:T(8,128)(2,1)} %bitcast.15), channel_id=1, source_target_pairs={{0,1},{1,0},{2,3},{3,2},{4,5},{5,4},{6,7},{7,6},{8,9},{9,8},{10,11... | collective-permute-start | bytes 6291464 | tf_op jit(solution)/shard_map/ppermute | solution.py:664
  3.6 20.7 %copy-start = (bf16[1,1,4096,256]{3,2,1,0:T(8,128)(2,1)S(1)}, bf16[1,1,4096,256]{3,2,1,0:T(8,128)(2,1)}, u32[]{:S(2)}) copy-start(bf16[1,1,4096,256]{3,2,1,0:T(8,128)(2,1)} %param.9) | copy-start | bytes 6291460
  3.6 20.7 %all-to-all-start = ((bf16[8,2,16,2048]{3,2,1,0:T(8,128)(2,1)}), bf16[8,2,16,2048]{3,2,1,0:T(8,128)(2,1)S(1)}, u32[]{:S(2)}, u32[]{:S(2)}) async-start(bf16[8,2,16,2048]{3,2,1,0:T(8,128)(2,1)} %pack.1._), calls=%async_computation | async-start | bytes 2097152 | tf_op jit(solution)/shard_map/all_to_all | solution.py:725
  8.9 7.5 %collective-permute-start.6 = (bf16[1,4096]{1,0:T(2,128)(2,1)S(1)}, bf16[1,4096]{1,0:T(2,128)(2,1)S(1)}, u32[]{:S(2)}, u32[]{:S(2)}) collective-permute-start(bf16[1,4096]{1,0:T(2,128)(2,1)S(1)} %bitcast.13), channel_id=1, source_target_pairs={{0,1},{1,0},{2,3},{3,2},{4,5},{5,4},{6,7},{7,6},{8,9},{9,8},{10,11... | collective-permute-start | bytes 24584 | tf_op jit(solution)/shard_map/ppermute | solution.py:664
  11.7 19.9 %collective-permute-start = (bf16[80,1024]{1,0:T(8,128)(2,1)}, bf16[80,1024]{1,0:T(8,128)(2,1)S(1)}, u32[]{:S(2)}, u32[]{:S(2)}) collective-permute-start(bf16[80,1024]{1,0:T(8,128)(2,1)} %get-tuple-element.16), channel_id=1, source_target_pairs={{0,0},{1,4},{2,2},{3,6},{4,1},{5,5},{6,3},{7,7},{8,8},{9,12},{10,1... | collective-permute-start | bytes 491528 | tf_op jit(solution)/shard_map/ppermute | solution.py:728
  13.3 20.9 %collective-permute-start.1 = (bf16[80,1024]{1,0:T(8,128)(2,1)}, bf16[80,1024]{1,0:T(8,128)(2,1)}, u32[]{:S(2)}, u32[]{:S(2)}) collective-permute-start(bf16[80,1024]{1,0:T(8,128)(2,1)} %get-tuple-element.17), channel_id=1, source_target_pairs={{0,1},{1,5},{2,3},{3,7},{4,0},{5,4},{6,2},{7,6},{8,9},{9,13},{10,1... | collective-permute-start | bytes 491528 | tf_op jit(solution)/shard_map/ppermute | solution.py:728
  16.4 15.0 %copy-start.5 = (bf16[1,4096]{1,0:T(2,128)(2,1)}, bf16[1,4096]{1,0:T(2,128)(2,1)S(1)}, u32[]{:S(2)}) copy-start(bf16[1,4096]{1,0:T(2,128)(2,1)S(1)} %collective-permute-done.6.other_gain.refs_21_) | copy-start | bytes 24580
  16.4 17.8 %collective-permute-start.2 = (bf16[80,1024]{1,0:T(8,128)(2,1)}, bf16[80,1024]{1,0:T(8,128)(2,1)}, u32[]{:S(2)}, u32[]{:S(2)}) collective-permute-start(bf16[80,1024]{1,0:T(8,128)(2,1)} %get-tuple-element.18), channel_id=1, source_target_pairs={{0,2},{1,6},{2,0},{3,4},{4,3},{5,7},{6,1},{7,5},{8,10},{9,14},{10,... | collective-permute-start | bytes 491528 | tf_op jit(solution)/shard_map/ppermute | solution.py:728
  18.0 16.2 %collective-permute-start.3 = (bf16[80,1024]{1,0:T(8,128)(2,1)}, bf16[80,1024]{1,0:T(8,128)(2,1)}, u32[]{:S(2)}, u32[]{:S(2)}) collective-permute-start(bf16[80,1024]{1,0:T(8,128)(2,1)} %get-tuple-element.19), channel_id=1, source_target_pairs={{0,3},{1,7},{2,1},{3,5},{4,2},{5,6},{6,0},{7,4},{8,11},{9,15},{10,... | collective-permute-start | bytes 491528 | tf_op jit(solution)/shard_map/ppermute | solution.py:728
  31.5 30.1 %copy-start.1 = (bf16[64,1152]{1,0:T(8,128)(2,1)}, bf16[64,1152]{1,0:T(8,128)(2,1)S(1)}, u32[]{:S(2)}) copy-start(bf16[64,1152]{1,0:T(8,128)(2,1)S(1)} %get-tuple-element.20.refs_4_.refs_8_) | copy-start | bytes 442372
  31.5 8.4 %collective-permute-start.17 = (bf16[64,1152]{1,0:T(8,128)(2,1)S(1)}, bf16[64,1152]{1,0:T(8,128)(2,1)S(1)}, u32[]{:S(2)}, u32[]{:S(2)}) collective-permute-start(bf16[64,1152]{1,0:T(8,128)(2,1)S(1)} %get-tuple-element.20.refs_4_.refs_8_), channel_id=1, source_target_pairs={{0,1},{1,0},{2,3},{3,2},{4,5},{5,4},{6,7},{7,6},{8,9},{9,8},{10,11... | collective-permute-start | bytes 442376 | tf_op jit(solution)/shard_map/ppermute | solution.py:664
  31.6 11.8 %collective-permute-start.15 = (bf16[64,1152]{1,0:T(8,128)(2,1)S(1)}, bf16[64,1152]{1,0:T(8,128)(2,1)S(1)}, u32[]{:S(2)}, u32[]{:S(2)}) collective-permute-start(bf16[64,1152]{1,0:T(8,128)(2,1)S(1)} %get-tuple-element.20.refs_4_.refs_8_), channel_id=1, source_target_pairs={{0,4},{2,6},{4,0},{6,2},{1,5},{3,7},{5,1},{7,3},{8,12},{10,14},{12... | collective-permute-start | bytes 442376 | tf_op jit(solution)/shard_map/ppermute | solution.py:664
  36.3 25.3 %copy-start.3 = (bf16[2,4,16,1024]{3,2,1,0:T(8,128)(2,1)}, bf16[2,4,16,1024]{3,2,1,0:T(8,128)(2,1)S(1)}, u32[]{:S(2)}) copy-start(bf16[2,4,16,1024]{3,2,1,0:T(8,128)(2,1)S(1)} %get-tuple-element.21.refs_0_) | copy-start | bytes 786436
  36.3 13.4 %collective-permute-start.7 = (bf16[2,4,16,1024]{3,2,1,0:T(8,128)(2,1)S(1)}, bf16[2,4,16,1024]{3,2,1,0:T(8,128)(2,1)S(1)}, u32[]{:S(2)}, u32[]{:S(2)}) collective-permute-start(bf16[2,4,16,1024]{3,2,1,0:T(8,128)(2,1)S(1)} %get-tuple-element.22), channel_id=1, source_target_pairs={{0,8},{8,0},{16,24},{24,16},{1,9},{9,1},{17,25},{25,17},{2,10},{10... | collective-permute-start | bytes 786440 | tf_op jit(solution)/shard_map/ppermute | solution.py:664
  37.5 13.8 %collective-permute-start.8 = (bf16[2,4,16,1024]{3,2,1,0:T(8,128)(2,1)S(1)}, bf16[2,4,16,1024]{3,2,1,0:T(8,128)(2,1)S(1)}, u32[]{:S(2)}, u32[]{:S(2)}) collective-permute-start(bf16[2,4,16,1024]{3,2,1,0:T(8,128)(2,1)S(1)} %get-tuple-element.23), channel_id=1, source_target_pairs={{0,16},{8,24},{16,0},{24,8},{1,17},{9,25},{17,1},{25,9},{2,18},{10... | collective-permute-start | bytes 786440 | tf_op jit(solution)/shard_map/ppermute | solution.py:664
  37.9 13.4 %collective-permute-start.9 = (bf16[2,4,16,1024]{3,2,1,0:T(8,128)(2,1)S(1)}, bf16[2,4,16,1024]{3,2,1,0:T(8,128)(2,1)S(1)}, u32[]{:S(2)}, u32[]{:S(2)}) collective-permute-start(bf16[2,4,16,1024]{3,2,1,0:T(8,128)(2,1)S(1)} %get-tuple-element.24), channel_id=1, source_target_pairs={{0,24},{8,16},{16,8},{24,0},{1,25},{9,17},{17,9},{25,1},{2,26},{10... | collective-permute-start | bytes 786440 | tf_op jit(solution)/shard_map/ppermute | solution.py:664
  39.9 21.7 %copy-start.14 = (bf16[64,1152]{1,0:T(8,128)(2,1)}, bf16[64,1152]{1,0:T(8,128)(2,1)S(1)}, u32[]{:S(2)}) copy-start(bf16[64,1152]{1,0:T(8,128)(2,1)S(1)} %collective-permute-done.17.refs_12_) | copy-start | bytes 442372
  39.9 11.9 %collective-permute-start.10 = (bf16[2,4,16,1024]{3,2,1,0:T(8,128)(2,1)S(1)}, bf16[2,4,16,1024]{3,2,1,0:T(8,128)(2,1)S(1)}, u32[]{:S(2)}, u32[]{:S(2)}) collective-permute-start(bf16[2,4,16,1024]{3,2,1,0:T(8,128)(2,1)S(1)} %get-tuple-element.21.refs_0_), channel_id=1, source_target_pairs={{0,1},{1,0},{2,3},{3,2},{4,5},{5,4},{6,7},{7,6},{8,9},{9,8},{10,11... | collective-permute-start | bytes 786440 | tf_op jit(solution)/shard_map/ppermute | solution.py:664
  39.9 21.6 %all-to-all-start.1 = ((bf16[8,16,2048]{2,1,0:T(8,128)(2,1)}), bf16[8,16,2048]{2,1,0:T(8,128)(2,1)S(1)}, u32[]{:S(2)}, u32[]{:S(2)}) async-start(bf16[8,16,2048]{2,1,0:T(8,128)(2,1)} %bitcast.11), calls=%async_computation.1 | async-start | bytes 1048576 | tf_op jit(solution)/shard_map/all_to_all | solution.py:763
  43.4 18.2 %copy-start.15 = (bf16[64,1152]{1,0:T(8,128)(2,1)}, bf16[64,1152]{1,0:T(8,128)(2,1)S(1)}, u32[]{:S(2)}) copy-start(bf16[64,1152]{1,0:T(8,128)(2,1)S(1)} %collective-permute-done.15.refs_10_) | copy-start | bytes 442372
  43.4 6.3 %collective-permute-start.14 = (bf16[64,1152]{1,0:T(8,128)(2,1)S(1)}, bf16[64,1152]{1,0:T(8,128)(2,1)S(1)}, u32[]{:S(2)}, u32[]{:S(2)}) collective-permute-start(bf16[64,1152]{1,0:T(8,128)(2,1)S(1)} %get-tuple-element.20.refs_4_.refs_8_), channel_id=1, source_target_pairs={{0,2},{2,0},{4,6},{6,4},{1,3},{3,1},{5,7},{7,5},{8,10},{10,8},{12,... | collective-permute-start | bytes 442376 | tf_op jit(solution)/shard_map/ppermute | solution.py:664
  49.7 11.9 %copy-start.16 = (bf16[64,1152]{1,0:T(8,128)(2,1)}, bf16[64,1152]{1,0:T(8,128)(2,1)S(1)}, u32[]{:S(2)}) copy-start(bf16[64,1152]{1,0:T(8,128)(2,1)S(1)} %collective-permute-done.14.refs_9_) | copy-start | bytes 442372
  49.7 2.2 %collective-permute-start.19 = (bf16[64,1152]{1,0:T(8,128)(2,1)S(1)}, bf16[64,1152]{1,0:T(8,128)(2,1)S(1)}, u32[]{:S(2)}, u32[]{:S(2)}) collective-permute-start(bf16[64,1152]{1,0:T(8,128)(2,1)S(1)} %collective-permute-done.15.refs_10_), channel_id=1, source_target_pairs={{0,1},{1,0},{2,3},{3,2},{4,5},{5,4},{6,7},{7,6},{8,9},{9,8},{10,11... | collective-permute-start | bytes 442376 | tf_op jit(solution)/shard_map/ppermute | solution.py:664
  49.7 11.9 %copy-start.7 = (bf16[2,4,16,1024]{3,2,1,0:T(8,128)(2,1)}, bf16[2,4,16,1024]{3,2,1,0:T(8,128)(2,1)S(1)}, u32[]{:S(2)}) copy-start(bf16[2,4,16,1024]{3,2,1,0:T(8,128)(2,1)S(1)} %collective-permute-done.7.refs_1_) | copy-start | bytes 786436
  49.7 10.3 %collective-permute-start.16 = (bf16[64,1152]{1,0:T(8,128)(2,1)S(1)}, bf16[64,1152]{1,0:T(8,128)(2,1)S(1)}, u32[]{:S(2)}, u32[]{:S(2)}) collective-permute-start(bf16[64,1152]{1,0:T(8,128)(2,1)S(1)} %collective-permute-done.14.refs_9_), channel_id=1, source_target_pairs={{0,4},{2,6},{4,0},{6,2},{1,5},{3,7},{5,1},{7,3},{8,12},{10,14},{12... | collective-permute-start | bytes 442376 | tf_op jit(solution)/shard_map/ppermute | solution.py:664
  51.3 10.4 %copy-start.8 = (bf16[2,4,16,1024]{3,2,1,0:T(8,128)(2,1)}, bf16[2,4,16,1024]{3,2,1,0:T(8,128)(2,1)S(1)}, u32[]{:S(2)}) copy-start(bf16[2,4,16,1024]{3,2,1,0:T(8,128)(2,1)S(1)} %collective-permute-done.8.refs_2_) | copy-start | bytes 786436
  51.3 10.3 %collective-permute-start.11 = (bf16[2,4,16,1024]{3,2,1,0:T(8,128)(2,1)S(1)}, bf16[2,4,16,1024]{3,2,1,0:T(8,128)(2,1)S(1)}, u32[]{:S(2)}, u32[]{:S(2)}) collective-permute-start(bf16[2,4,16,1024]{3,2,1,0:T(8,128)(2,1)S(1)} %collective-permute-done.7.refs_1_), channel_id=1, source_target_pairs={{0,1},{1,0},{2,3},{3,2},{4,5},{5,4},{6,7},{7,6},{8,9},{9,8},{10,11... | collective-permute-start | bytes 786440 | tf_op jit(solution)/shard_map/ppermute | solution.py:664
  51.3 10.3 %collective-permute-start.12 = (bf16[2,4,16,1024]{3,2,1,0:T(8,128)(2,1)S(1)}, bf16[2,4,16,1024]{3,2,1,0:T(8,128)(2,1)S(1)}, u32[]{:S(2)}, u32[]{:S(2)}) collective-permute-start(bf16[2,4,16,1024]{3,2,1,0:T(8,128)(2,1)S(1)} %collective-permute-done.8.refs_2_), channel_id=1, source_target_pairs={{0,1},{1,0},{2,3},{3,2},{4,5},{5,4},{6,7},{7,6},{8,9},{9,8},{10,11... | collective-permute-start | bytes 786440 | tf_op jit(solution)/shard_map/ppermute | solution.py:664
  51.8 9.8 %collective-permute-start.13 = (bf16[2,4,16,1024]{3,2,1,0:T(8,128)(2,1)S(1)}, bf16[2,4,16,1024]{3,2,1,0:T(8,128)(2,1)S(1)}, u32[]{:S(2)}, u32[]{:S(2)}) collective-permute-start(bf16[2,4,16,1024]{3,2,1,0:T(8,128)(2,1)S(1)} %collective-permute-done.9.refs_3_), channel_id=1, source_target_pairs={{0,1},{1,0},{2,3},{3,2},{4,5},{5,4},{6,7},{7,6},{8,9},{9,8},{10,11... | collective-permute-start | bytes 786440 | tf_op jit(solution)/shard_map/ppermute | solution.py:664
  51.9 8.1 %collective-permute-start.18 = (bf16[64,1152]{1,0:T(8,128)(2,1)S(1)}, bf16[64,1152]{1,0:T(8,128)(2,1)S(1)}, u32[]{:S(2)}, u32[]{:S(2)}) collective-permute-start(bf16[64,1152]{1,0:T(8,128)(2,1)S(1)} %collective-permute-done.14.refs_9_), channel_id=1, source_target_pairs={{0,1},{1,0},{2,3},{3,2},{4,5},{5,4},{6,7},{7,6},{8,9},{9,8},{10,11... | collective-permute-start | bytes 442376 | tf_op jit(solution)/shard_map/ppermute | solution.py:664
  60.0 1.5 %collective-permute-start.20 = (bf16[64,1152]{1,0:T(8,128)(2,1)S(1)}, bf16[64,1152]{1,0:T(8,128)(2,1)}, u32[]{:S(2)}, u32[]{:S(2)}) collective-permute-start(bf16[64,1152]{1,0:T(8,128)(2,1)S(1)} %collective-permute-done.16.refs_11_), channel_id=1, source_target_pairs={{0,1},{1,0},{2,3},{3,2},{4,5},{5,4},{6,7},{7,6},{8,9},{9,8},{10,11... | collective-permute-start | bytes 442376 | tf_op jit(solution)/shard_map/ppermute | solution.py:664
  (11 other events, 52.5 us)

commit v11 on v10

--- a/solution.py
+++ b/solution.py
@@ -756,8 +756,8 @@
     )(*slabs, small)
     mine = [slices[0]] + [across(slices[step], "expert", step) for step in range(1, experts)]
     theirs = [across(block, "segment", 1) for block in mine]
-    one_away = across(small, "dp", 1)
-    near = [small, one_away, across(small, "dp", 2), across(one_away, "dp", 2)]
+    near = [small] + [across(small, "dp", step) for step in range(1, replicas)]
+    near[:2] = lax.optimization_barrier(tuple(near[:2]))
     smalls = near + [across(piece, "segment", 1) for piece in near]
 
     back = lax.all_to_all(

time: 70.2 us -> 66.8 us (0.952)
  waiting for transfers between devices: 20.6 us -> 14.9 us
  starting transfers between devices: 25.5 us -> 27.9 us
    ppermute x17, waiting for transfers between devices: 14.3 us -> 8.6 us  [across(): return lax.ppermute(block, axis, [(i, i ^ distance) for i in range(size)])]
    ppermute x17, starting transfers between devices: 10.4 us -> 12.8 us  [across(): return lax.ppermute(block, axis, [(i, i ^ distance) for i in range(size)])]
  transfers between devices with their start and end apart: 23 -> 23, of which waited for: 5 -> 5; matrix products, arithmetic and copies ran while one was open for 0% -> 0% of each run, Pallas kernels for 20% -> 21%
where the time goes in v11:
time: 66.8 us; the launch traced here: 66.4 us
  starting transfers between devices  27.9 us (42%)
  Pallas kernels  20.4 us (31%)
  waiting for transfers between devices  14.9 us (22%)
  local copies, waits for them, and re-layouts  2.27 us (3%)
  between operations  0.93 us (1%)
    ppermute x17, starting transfers between devices, across(): return lax.ppermute(block, axis, [(i, i ^ distance) for i in range(size)])  12.8 us
    ppermute x17, waiting for transfers between devices, across(): return lax.ppermute(block, axis, [(i, i ^ distance) for i in range(size)])  8.6 us
    pallas_call x1, Pallas kernels, on_device_two_phases(): call(chain_kernel, 'chain', 50, [HBM] * 7, [((experts, 2, rows, part), bf...  7.1 us
    pallas_call x1, Pallas kernels, on_device_two_phases(): call(functools.partial(gradient_kernel, experts, sources, sizes), 'gradie...  6.57 us
    all_to_all x1, waiting for transfers between devices, on_device_two_phases(): lax.all_to_all(send, sections, split_axis=0, concat_axis=0, tiled=True)  6.33 us
    ppermute x4, starting transfers between devices, on_device_two_phases(): lax.ppermute(block, ('dp', 'segment'), slab_route(replicas, turn // 2, tu...  6.29 us
    all_to_all x1, starting transfers between devices, on_device_two_phases(): lax.all_to_all(send, sections, split_axis=0, concat_axis=0, tiled=True)  5.29 us
    all_to_all x1, starting transfers between devices, on_device_two_phases(): lax.all_to_all(out.reshape(groups, rows, part), sections, split_axis=0, c...  3.51 us
  transfers between devices with their start and end apart: 23, of which 5 were waited for; matrix products, arithmetic and copies ran while one was open for 0% of the time, Pallas kernels for 21%

profile of v11, /device:TPU:0, one launch (start us, length us, event | category | flops | bytes accessed | tf_op | source)
XLA Modules:
  0.0 66.4 jit_solution(7050909016369329837)
XLA Ops:
  0.6 0.5 collective-permute-start.4
  1.2 0.1 collective-permute-start.5
  1.2 2.4 %pack.1._ = bf16[8,2,16,2048]{3,2,1,0:T(8,128)(2,1)} custom-call(s32[16]{0:T(128)} %refs_22_.1, bf16[16,4,2048]{2,1,0:T(4,128)(2,1)} %hidden.3, bf16[16,4,2048]{2,1,0:T(4,128)(2,1)} %cot.3), custom_call_target="tpu_custom_call" | custom-call | bytes 1048576 | tf_op jit(solution)/shard_map/pack/pallas_call | solution.py:695
  3.6 5.3 %all-to-all-start = ((bf16[8,2,16,2048]{3,2,1,0:T(8,128)(2,1)}), bf16[8,2,16,2048]{3,2,1,0:T(8,128)(2,1)S(1)}, u32[]{:S(2)}, u32[]{:S(2)}) async-start(bf16[8,2,16,2048]{3,2,1,0:T(8,128)(2,1)} %pack.1._), calls=%async_computation | async-start | bytes 2097152 | tf_op jit(solution)/shard_map/all_to_all | solution.py:725
  8.9 0.5 collective-permute-start.6
  9.4 2.3 %slabs.1 = (bf16[80,1024]{1,0:T(8,128)(2,1)}, bf16[80,1024]{1,0:T(8,128)(2,1)}, bf16[80,1024]{1,0:T(8,128)(2,1)}, bf16[80,1024]{1,0:T(8,128)(2,1)}) custom-call(s32[16]{0:T(128)} %refs_22_.1, bf16[16,4,2048]{2,1,0:T(4,128)(2,1)} %hidden.3, bf16[16,4,2048]{2,1,0:T(4,128)(2,1)} %cot.3, bf16[8,2,16,2048]{3,2,1,0:T(8,128)(2,1)} %pack.1._), custom_call_target="tpu_custom_call" | custom-call | bytes 1048576 | tf_op jit(solution)/shard_map/slabs/pallas_call | solution.py:709
  11.7 1.6 %collective-permute-start = (bf16[80,1024]{1,0:T(8,128)(2,1)}, bf16[80,1024]{1,0:T(8,128)(2,1)S(1)}, u32[]{:S(2)}, u32[]{:S(2)}) collective-permute-start(bf16[80,1024]{1,0:T(8,128)(2,1)} %get-tuple-element.18), channel_id=1, source_target_pairs={{0,0},{1,4},{2,2},{3,6},{4,1},{5,5},{6,3},{7,7},{8,8},{9,12},{10,1... | collective-permute-start | bytes 491528 | tf_op jit(solution)/shard_map/ppermute | solution.py:728
  13.3 3.1 %collective-permute-start.1 = (bf16[80,1024]{1,0:T(8,128)(2,1)}, bf16[80,1024]{1,0:T(8,128)(2,1)}, u32[]{:S(2)}, u32[]{:S(2)}) collective-permute-start(bf16[80,1024]{1,0:T(8,128)(2,1)} %get-tuple-element.19), channel_id=1, source_target_pairs={{0,1},{1,5},{2,3},{3,7},{4,0},{5,4},{6,2},{7,6},{8,9},{9,13},{10,1... | collective-permute-start | bytes 491528 | tf_op jit(solution)/shard_map/ppermute | solution.py:728
  16.4 1.6 %collective-permute-start.2 = (bf16[80,1024]{1,0:T(8,128)(2,1)}, bf16[80,1024]{1,0:T(8,128)(2,1)}, u32[]{:S(2)}, u32[]{:S(2)}) collective-permute-start(bf16[80,1024]{1,0:T(8,128)(2,1)} %get-tuple-element.20), channel_id=1, source_target_pairs={{0,2},{1,6},{2,0},{3,4},{4,3},{5,7},{6,1},{7,5},{8,10},{9,14},{10,... | collective-permute-start | bytes 491528 | tf_op jit(solution)/shard_map/ppermute | solution.py:728
  18.0 6.3 %all-to-all-done = bf16[8,2,16,2048]{3,2,1,0:T(8,128)(2,1)S(1)} async-done(((bf16[8,2,16,2048]{3,2,1,0:T(8,128)(2,1)}), bf16[8,2,16,2048]{3,2,1,0:T(8,128)(2,1)S(1)}, u32[]{:S(2)}, u32[]{:S(2)}) %all-to-all-start) | async-done | bytes 1048608 | tf_op jit(solution)/shard_map/all_to_all | solution.py:725
  24.4 7.1 %chain.1 = (bf16[4,2,16,2048]{3,2,1,0:T(8,128)(2,1)S(1)}, bf16[64,1152]{1,0:T(8,128)(2,1)S(1)}) custom-call(bf16[4,2,2,16,2048]{4,3,2,1,0:T(8,128)(2,1)S(1)} %bitcast.10, bf16[4096,256]{1,0:T(8,128)(2,1)S(1)} %bitcast.9, bf16[256,4096]{1,0:T(8,128)(2,1)} %bitcast.16, bf16[1,4096]{1,0:T(2,128)(2,1)S(1)} %bitcast.14, ...), custom_call_target="tpu_custom_call" | custom-call | flops 939524096 | bytes 10485760 | tf_op jit(solution)/shard_map/chain/pallas_call | solution.py:731
  31.5 3.7 %collective-permute-start.16 = (bf16[64,1152]{1,0:T(8,128)(2,1)S(1)}, bf16[64,1152]{1,0:T(8,128)(2,1)S(1)}, u32[]{:S(2)}, u32[]{:S(2)}) collective-permute-start(bf16[64,1152]{1,0:T(8,128)(2,1)S(1)} %get-tuple-element.27.refs_4_.refs_8_), channel_id=1, source_target_pairs={{0,6},{2,4},{4,2},{6,0},{1,7},{3,5},{5,3},{7,1},{8,14},{10,12},{12... | collective-permute-start | bytes 442376 | tf_op jit(solution)/shard_map/ppermute | solution.py:664
  35.2 2.1 %repack.1 = (bf16[2,4,16,1024]{3,2,1,0:T(8,128)(2,1)S(1)}, bf16[2,4,16,1024]{3,2,1,0:T(8,128)(2,1)S(1)}, bf16[2,4,16,1024]{3,2,1,0:T(8,128)(2,1)S(1)}, bf16[2,4,16,1024]{3,2,1,0:T(8,128)(2,1)S(1)}) custom-call(bf16[80,1024]{1,0:T(8,128)(2,1)S(1)} %collective-permute-done.refs_0_, bf16[80,1024]{1,0:T(8,128)(2,1)} %collective-permute-done.1.refs_1_, ...), custom_call_target="tpu_custom_call" | custom-call | bytes 1048576 | tf_op jit(solution)/shard_map/repack/pallas_call | solution.py:750
  37.3 0.6 collective-permute-start.7
  37.9 0.7 %collective-permute-start.8 = (bf16[2,4,16,1024]{3,2,1,0:T(8,128)(2,1)S(1)}, bf16[2,4,16,1024]{3,2,1,0:T(8,128)(2,1)S(1)}, u32[]{:S(2)}, u32[]{:S(2)}) collective-permute-start(bf16[2,4,16,1024]{3,2,1,0:T(8,128)(2,1)S(1)} %get-tuple-element.25), channel_id=1, source_target_pairs={{0,16},{8,24},{16,0},{24,8},{1,17},{9,25},{17,1},{25,9},{2,18},{10... | collective-permute-start | bytes 786440 | tf_op jit(solution)/shard_map/ppermute | solution.py:664
  38.5 2.3 %collective-permute-start.9 = (bf16[2,4,16,1024]{3,2,1,0:T(8,128)(2,1)S(1)}, bf16[2,4,16,1024]{3,2,1,0:T(8,128)(2,1)S(1)}, u32[]{:S(2)}, u32[]{:S(2)}) collective-permute-start(bf16[2,4,16,1024]{3,2,1,0:T(8,128)(2,1)S(1)} %get-tuple-element.26), channel_id=1, source_target_pairs={{0,24},{8,16},{16,8},{24,0},{1,25},{9,17},{17,9},{25,1},{2,26},{10... | collective-permute-start | bytes 786440 | tf_op jit(solution)/shard_map/ppermute | solution.py:664
  40.8 3.5 %all-to-all-start.1 = ((bf16[8,16,2048]{2,1,0:T(8,128)(2,1)}), bf16[8,16,2048]{2,1,0:T(8,128)(2,1)S(1)}, u32[]{:S(2)}, u32[]{:S(2)}) async-start(bf16[8,16,2048]{2,1,0:T(8,128)(2,1)} %bitcast.11), calls=%async_computation.1 | async-start | bytes 1048576 | tf_op jit(solution)/shard_map/all_to_all | solution.py:763
  44.4 1.0 %collective-permute-done.15.refs_10_ = bf16[64,1152]{1,0:T(8,128)(2,1)S(1)} collective-permute-done((bf16[64,1152]{1,0:T(8,128)(2,1)S(1)}, bf16[64,1152]{1,0:T(8,128)(2,1)S(1)}, u32[]{:S(2)}, u32[]{:S(2)}) %collective-permute-start.15) | collective-permute-done | bytes 147488 | tf_op jit(solution)/shard_map/ppermute | solution.py:664
  45.4 2.9 %collective-permute-start.14 = (bf16[64,1152]{1,0:T(8,128)(2,1)S(1)}, bf16[64,1152]{1,0:T(8,128)(2,1)S(1)}, u32[]{:S(2)}, u32[]{:S(2)}) collective-permute-start(bf16[64,1152]{1,0:T(8,128)(2,1)S(1)} %get-tuple-element.27.refs_4_.refs_8_), channel_id=1, source_target_pairs={{0,2},{2,0},{4,6},{6,4},{1,3},{3,1},{5,7},{7,5},{8,10},{10,8},{12,... | collective-permute-start | bytes 442376 | tf_op jit(solution)/shard_map/ppermute | solution.py:664
  48.2 4.5 %collective-permute-done.14.refs_9_ = bf16[64,1152]{1,0:T(8,128)(2,1)S(1)} collective-permute-done((bf16[64,1152]{1,0:T(8,128)(2,1)S(1)}, bf16[64,1152]{1,0:T(8,128)(2,1)S(1)}, u32[]{:S(2)}, u32[]{:S(2)}) %collective-permute-start.14) | collective-permute-done | bytes 147488 | tf_op jit(solution)/shard_map/ppermute | solution.py:664
  52.8 0.5 collective-permute-start.19
  53.3 1.5 %collective-permute-done.8.refs_2_ = bf16[2,4,16,1024]{3,2,1,0:T(8,128)(2,1)S(1)} collective-permute-done((bf16[2,4,16,1024]{3,2,1,0:T(8,128)(2,1)S(1)}, bf16[2,4,16,1024]{3,2,1,0:T(8,128)(2,1)S(1)}, u32[]{:S(2)}, u32[]{:S(2)}) %collective-permute-start.8) | collective-permute-done | bytes 262176 | tf_op jit(solution)/shard_map/ppermute | solution.py:664
  54.7 0.5 collective-permute-start.12
  55.3 0.1 collective-permute-start.13
  55.3 0.4 collective-permute-start.17
  55.8 0.1 collective-permute-start.18
  55.9 1.6 %collective-permute-done.17.refs_12_ = bf16[64,1152]{1,0:T(8,128)(2,1)S(1)} collective-permute-done((bf16[64,1152]{1,0:T(8,128)(2,1)S(1)}, bf16[64,1152]{1,0:T(8,128)(2,1)S(1)}, u32[]{:S(2)}, u32[]{:S(2)}) %collective-permute-start.17) | collective-permute-done | bytes 147488 | tf_op jit(solution)/shard_map/ppermute | solution.py:664
  57.4 0.7 %copy-done.19 = bf16[64,1152]{1,0:T(8,128)(2,1)} copy-done((bf16[64,1152]{1,0:T(8,128)(2,1)}, bf16[64,1152]{1,0:T(8,128)(2,1)S(1)}, u32[]{:S(2)}) %copy-start.19) | copy-done | bytes 147480
  58.3 0.6 copy-done.6
  58.9 0.1 copy-done.11
  59.1 0.7 %copy-done.13 = bf16[2,4,16,1024]{3,2,1,0:T(8,128)(2,1)} copy-done((bf16[2,4,16,1024]{3,2,1,0:T(8,128)(2,1)}, bf16[2,4,16,1024]{3,2,1,0:T(8,128)(2,1)S(1)}, u32[]{:S(2)}) %copy-start.13) | copy-done | bytes 262168
  59.8 6.6 %gradients.1 = (bf16[16,4,2048]{2,1,0:T(4,128)(2,1)}, bf16[1024,256]{1,0:T(8,128)(2,1)}, bf16[256,1024]{1,0:T(8,128)(2,1)}) custom-call(bf16[2,4,16,1024]{3,2,1,0:T(8,128)(2,1)} %copy-done.3, bf16[2,4,16,1024]{3,2,1,0:T(8,128)(2,1)} %copy-done.7, bf16[2,4,16,1024]{3,2,1,0:T(8,128)(2,1)} %copy-done.8, bf16[2,4,16,1024]{3,2,1,0:T(8,128)(2,1)} %copy-done.9, ...), custom_call_target="tpu_custom_call" | custom-call | bytes 1048576 | tf_op jit(solution)/shard_map/gradients/pallas_call | solution.py:769
  (59 shorter events, 0.2 us)
Async XLA Ops:
  0.6 8.3 %copy-start.4 = (bf16[1,1,4096]{2,1,0:T(2,128)(2,1)S(1)}, bf16[1,1,4096]{2,1,0:T(2,128)(2,1)}, u32[]{:S(2)}) copy-start(bf16[1,1,4096]{2,1,0:T(2,128)(2,1)} %param.11) | copy-start | bytes 24580
  0.6 17.4 %collective-permute-start.4 = (bf16[4096,256]{1,0:T(8,128)(2,1)}, bf16[4096,256]{1,0:T(8,128)(2,1)}, u32[]{:S(2)}, u32[]{:S(2)}) collective-permute-start(bf16[4096,256]{1,0:T(8,128)(2,1)} %bitcast.7), channel_id=1, source_target_pairs={{0,1},{1,0},{2,3},{3,2},{4,5},{5,4},{6,7},{7,6},{8,9},{9,8},{10,11... | collective-permute-start | bytes 6291464 | tf_op jit(solution)/shard_map/ppermute | solution.py:664
  1.2 23.2 %collective-permute-start.5 = (bf16[256,4096]{1,0:T(8,128)(2,1)}, bf16[256,4096]{1,0:T(8,128)(2,1)}, u32[]{:S(2)}, u32[]{:S(2)}) collective-permute-start(bf16[256,4096]{1,0:T(8,128)(2,1)} %bitcast.15), channel_id=1, source_target_pairs={{0,1},{1,0},{2,3},{3,2},{4,5},{5,4},{6,7},{7,6},{8,9},{9,8},{10,11... | collective-permute-start | bytes 6291464 | tf_op jit(solution)/shard_map/ppermute | solution.py:664
  3.6 20.7 %copy-start = (bf16[1,1,4096,256]{3,2,1,0:T(8,128)(2,1)S(1)}, bf16[1,1,4096,256]{3,2,1,0:T(8,128)(2,1)}, u32[]{:S(2)}) copy-start(bf16[1,1,4096,256]{3,2,1,0:T(8,128)(2,1)} %param.9) | copy-start | bytes 6291460
  3.6 20.7 %all-to-all-start = ((bf16[8,2,16,2048]{3,2,1,0:T(8,128)(2,1)}), bf16[8,2,16,2048]{3,2,1,0:T(8,128)(2,1)S(1)}, u32[]{:S(2)}, u32[]{:S(2)}) async-start(bf16[8,2,16,2048]{3,2,1,0:T(8,128)(2,1)} %pack.1._), calls=%async_computation | async-start | bytes 2097152 | tf_op jit(solution)/shard_map/all_to_all | solution.py:725
  8.9 7.5 %collective-permute-start.6 = (bf16[1,4096]{1,0:T(2,128)(2,1)S(1)}, bf16[1,4096]{1,0:T(2,128)(2,1)S(1)}, u32[]{:S(2)}, u32[]{:S(2)}) collective-permute-start(bf16[1,4096]{1,0:T(2,128)(2,1)S(1)} %bitcast.13), channel_id=1, source_target_pairs={{0,1},{1,0},{2,3},{3,2},{4,5},{5,4},{6,7},{7,6},{8,9},{9,8},{10,11... | collective-permute-start | bytes 24584 | tf_op jit(solution)/shard_map/ppermute | solution.py:664
  11.7 23.4 %collective-permute-start = (bf16[80,1024]{1,0:T(8,128)(2,1)}, bf16[80,1024]{1,0:T(8,128)(2,1)S(1)}, u32[]{:S(2)}, u32[]{:S(2)}) collective-permute-start(bf16[80,1024]{1,0:T(8,128)(2,1)} %get-tuple-element.18), channel_id=1, source_target_pairs={{0,0},{1,4},{2,2},{3,6},{4,1},{5,5},{6,3},{7,7},{8,8},{9,12},{10,1... | collective-permute-start | bytes 491528 | tf_op jit(solution)/shard_map/ppermute | solution.py:728
  13.3 21.9 %collective-permute-start.1 = (bf16[80,1024]{1,0:T(8,128)(2,1)}, bf16[80,1024]{1,0:T(8,128)(2,1)}, u32[]{:S(2)}, u32[]{:S(2)}) collective-permute-start(bf16[80,1024]{1,0:T(8,128)(2,1)} %get-tuple-element.19), channel_id=1, source_target_pairs={{0,1},{1,5},{2,3},{3,7},{4,0},{5,4},{6,2},{7,6},{8,9},{9,13},{10,1... | collective-permute-start | bytes 491528 | tf_op jit(solution)/shard_map/ppermute | solution.py:728
  16.4 15.0 %copy-start.5 = (bf16[1,4096]{1,0:T(2,128)(2,1)}, bf16[1,4096]{1,0:T(2,128)(2,1)S(1)}, u32[]{:S(2)}) copy-start(bf16[1,4096]{1,0:T(2,128)(2,1)S(1)} %collective-permute-done.6.other_gain.refs_21_) | copy-start | bytes 24580
  16.4 18.7 %collective-permute-start.2 = (bf16[80,1024]{1,0:T(8,128)(2,1)}, bf16[80,1024]{1,0:T(8,128)(2,1)}, u32[]{:S(2)}, u32[]{:S(2)}) collective-permute-start(bf16[80,1024]{1,0:T(8,128)(2,1)} %get-tuple-element.20), channel_id=1, source_target_pairs={{0,2},{1,6},{2,0},{3,4},{4,3},{5,7},{6,1},{7,5},{8,10},{9,14},{10,... | collective-permute-start | bytes 491528 | tf_op jit(solution)/shard_map/ppermute | solution.py:728
  18.0 17.2 %collective-permute-start.3 = (bf16[80,1024]{1,0:T(8,128)(2,1)}, bf16[80,1024]{1,0:T(8,128)(2,1)}, u32[]{:S(2)}, u32[]{:S(2)}) collective-permute-start(bf16[80,1024]{1,0:T(8,128)(2,1)} %get-tuple-element.21), channel_id=1, source_target_pairs={{0,3},{1,7},{2,1},{3,5},{4,2},{5,6},{6,0},{7,4},{8,11},{9,15},{10,... | collective-permute-start | bytes 491528 | tf_op jit(solution)/shard_map/ppermute | solution.py:728
  31.5 9.4 %copy-start.2 = (bf16[4,2,16,2048]{3,2,1,0:T(8,128)(2,1)}, bf16[4,2,16,2048]{3,2,1,0:T(8,128)(2,1)S(1)}, u32[]{:S(2)}) copy-start(bf16[4,2,16,2048]{3,2,1,0:T(8,128)(2,1)S(1)} %get-tuple-element.29) | copy-start | bytes 1572868
  31.5 26.7 %copy-start.1 = (bf16[64,1152]{1,0:T(8,128)(2,1)}, bf16[64,1152]{1,0:T(8,128)(2,1)S(1)}, u32[]{:S(2)}) copy-start(bf16[64,1152]{1,0:T(8,128)(2,1)S(1)} %get-tuple-element.27.refs_4_.refs_8_) | copy-start | bytes 442372
  31.5 9.3 %collective-permute-start.16 = (bf16[64,1152]{1,0:T(8,128)(2,1)S(1)}, bf16[64,1152]{1,0:T(8,128)(2,1)S(1)}, u32[]{:S(2)}, u32[]{:S(2)}) collective-permute-start(bf16[64,1152]{1,0:T(8,128)(2,1)S(1)} %get-tuple-element.27.refs_4_.refs_8_), channel_id=1, source_target_pairs={{0,6},{2,4},{4,2},{6,0},{1,7},{3,5},{5,3},{7,1},{8,14},{10,12},{12... | collective-permute-start | bytes 442376 | tf_op jit(solution)/shard_map/ppermute | solution.py:664
  35.2 10.2 %collective-permute-start.15 = (bf16[64,1152]{1,0:T(8,128)(2,1)S(1)}, bf16[64,1152]{1,0:T(8,128)(2,1)S(1)}, u32[]{:S(2)}, u32[]{:S(2)}) collective-permute-start(bf16[64,1152]{1,0:T(8,128)(2,1)S(1)} %get-tuple-element.27.refs_4_.refs_8_), channel_id=1, source_target_pairs={{0,4},{2,6},{4,0},{6,2},{1,5},{3,7},{5,1},{7,3},{8,12},{10,14},{12... | collective-permute-start | bytes 442376 | tf_op jit(solution)/shard_map/ppermute | solution.py:664
  37.3 20.9 %copy-start.3 = (bf16[2,4,16,1024]{3,2,1,0:T(8,128)(2,1)}, bf16[2,4,16,1024]{3,2,1,0:T(8,128)(2,1)S(1)}, u32[]{:S(2)}) copy-start(bf16[2,4,16,1024]{3,2,1,0:T(8,128)(2,1)S(1)} %get-tuple-element.23.refs_0_) | copy-start | bytes 786436
  37.3 15.5 %collective-permute-start.7 = (bf16[2,4,16,1024]{3,2,1,0:T(8,128)(2,1)S(1)}, bf16[2,4,16,1024]{3,2,1,0:T(8,128)(2,1)S(1)}, u32[]{:S(2)}, u32[]{:S(2)}) collective-permute-start(bf16[2,4,16,1024]{3,2,1,0:T(8,128)(2,1)S(1)} %get-tuple-element.24), channel_id=1, source_target_pairs={{0,8},{8,0},{16,24},{24,16},{1,9},{9,1},{17,25},{25,17},{2,10},{10... | collective-permute-start | bytes 786440 | tf_op jit(solution)/shard_map/ppermute | solution.py:664
  37.9 16.9 %collective-permute-start.8 = (bf16[2,4,16,1024]{3,2,1,0:T(8,128)(2,1)S(1)}, bf16[2,4,16,1024]{3,2,1,0:T(8,128)(2,1)S(1)}, u32[]{:S(2)}, u32[]{:S(2)}) collective-permute-start(bf16[2,4,16,1024]{3,2,1,0:T(8,128)(2,1)S(1)} %get-tuple-element.25), channel_id=1, source_target_pairs={{0,16},{8,24},{16,0},{24,8},{1,17},{9,25},{17,1},{25,9},{2,18},{10... | collective-permute-start | bytes 786440 | tf_op jit(solution)/shard_map/ppermute | solution.py:664
  38.5 16.2 %collective-permute-start.9 = (bf16[2,4,16,1024]{3,2,1,0:T(8,128)(2,1)S(1)}, bf16[2,4,16,1024]{3,2,1,0:T(8,128)(2,1)S(1)}, u32[]{:S(2)}, u32[]{:S(2)}) collective-permute-start(bf16[2,4,16,1024]{3,2,1,0:T(8,128)(2,1)S(1)} %get-tuple-element.26), channel_id=1, source_target_pairs={{0,24},{8,16},{16,8},{24,0},{1,25},{9,17},{17,9},{25,1},{2,26},{10... | collective-permute-start | bytes 786440 | tf_op jit(solution)/shard_map/ppermute | solution.py:664
  40.8 17.4 %copy-start.14 = (bf16[64,1152]{1,0:T(8,128)(2,1)}, bf16[64,1152]{1,0:T(8,128)(2,1)S(1)}, u32[]{:S(2)}) copy-start(bf16[64,1152]{1,0:T(8,128)(2,1)S(1)} %collective-permute-done.16.refs_11_) | copy-start | bytes 442372
  40.8 14.4 %collective-permute-start.10 = (bf16[2,4,16,1024]{3,2,1,0:T(8,128)(2,1)S(1)}, bf16[2,4,16,1024]{3,2,1,0:T(8,128)(2,1)S(1)}, u32[]{:S(2)}, u32[]{:S(2)}) collective-permute-start(bf16[2,4,16,1024]{3,2,1,0:T(8,128)(2,1)S(1)} %get-tuple-element.23.refs_0_), channel_id=1, source_target_pairs={{0,1},{1,0},{2,3},{3,2},{4,5},{5,4},{6,7},{7,6},{8,9},{9,8},{10,11... | collective-permute-start | bytes 786440 | tf_op jit(solution)/shard_map/ppermute | solution.py:664
  40.8 17.3 %all-to-all-start.1 = ((bf16[8,16,2048]{2,1,0:T(8,128)(2,1)}), bf16[8,16,2048]{2,1,0:T(8,128)(2,1)S(1)}, u32[]{:S(2)}, u32[]{:S(2)}) async-start(bf16[8,16,2048]{2,1,0:T(8,128)(2,1)} %bitcast.11), calls=%async_computation.1 | async-start | bytes 1048576 | tf_op jit(solution)/shard_map/all_to_all | solution.py:763
  45.4 12.8 %copy-start.15 = (bf16[64,1152]{1,0:T(8,128)(2,1)}, bf16[64,1152]{1,0:T(8,128)(2,1)S(1)}, u32[]{:S(2)}) copy-start(bf16[64,1152]{1,0:T(8,128)(2,1)S(1)} %collective-permute-done.15.refs_10_) | copy-start | bytes 442372
  45.4 7.4 %collective-permute-start.14 = (bf16[64,1152]{1,0:T(8,128)(2,1)S(1)}, bf16[64,1152]{1,0:T(8,128)(2,1)S(1)}, u32[]{:S(2)}, u32[]{:S(2)}) collective-permute-start(bf16[64,1152]{1,0:T(8,128)(2,1)S(1)} %get-tuple-element.27.refs_4_.refs_8_), channel_id=1, source_target_pairs={{0,2},{2,0},{4,6},{6,4},{1,3},{3,1},{5,7},{7,5},{8,10},{10,8},{12,... | collective-permute-start | bytes 442376 | tf_op jit(solution)/shard_map/ppermute | solution.py:664
  52.7 5.5 %copy-start.16 = (bf16[64,1152]{1,0:T(8,128)(2,1)}, bf16[64,1152]{1,0:T(8,128)(2,1)S(1)}, u32[]{:S(2)}) copy-start(bf16[64,1152]{1,0:T(8,128)(2,1)S(1)} %collective-permute-done.14.refs_9_) | copy-start | bytes 442372
  52.7 2.6 %collective-permute-start.20 = (bf16[64,1152]{1,0:T(8,128)(2,1)S(1)}, bf16[64,1152]{1,0:T(8,128)(2,1)S(1)}, u32[]{:S(2)}, u32[]{:S(2)}) collective-permute-start(bf16[64,1152]{1,0:T(8,128)(2,1)S(1)} %collective-permute-done.16.refs_11_), channel_id=1, source_target_pairs={{0,1},{1,0},{2,3},{3,2},{4,5},{5,4},{6,7},{7,6},{8,9},{9,8},{10,11... | collective-permute-start | bytes 442376 | tf_op jit(solution)/shard_map/ppermute | solution.py:664
  52.8 3.0 %collective-permute-start.19 = (bf16[64,1152]{1,0:T(8,128)(2,1)S(1)}, bf16[64,1152]{1,0:T(8,128)(2,1)S(1)}, u32[]{:S(2)}, u32[]{:S(2)}) collective-permute-start(bf16[64,1152]{1,0:T(8,128)(2,1)S(1)} %collective-permute-done.15.refs_10_), channel_id=1, source_target_pairs={{0,1},{1,0},{2,3},{3,2},{4,5},{5,4},{6,7},{7,6},{8,9},{9,8},{10,11... | collective-permute-start | bytes 442376 | tf_op jit(solution)/shard_map/ppermute | solution.py:664
  54.7 3.4 %collective-permute-start.11 = (bf16[2,4,16,1024]{3,2,1,0:T(8,128)(2,1)S(1)}, bf16[2,4,16,1024]{3,2,1,0:T(8,128)(2,1)S(1)}, u32[]{:S(2)}, u32[]{:S(2)}) collective-permute-start(bf16[2,4,16,1024]{3,2,1,0:T(8,128)(2,1)S(1)} %collective-permute-done.7.refs_1_), channel_id=1, source_target_pairs={{0,1},{1,0},{2,3},{3,2},{4,5},{5,4},{6,7},{7,6},{8,9},{9,8},{10,11... | collective-permute-start | bytes 786440 | tf_op jit(solution)/shard_map/ppermute | solution.py:664
  54.7 3.4 %collective-permute-start.12 = (bf16[2,4,16,1024]{3,2,1,0:T(8,128)(2,1)S(1)}, bf16[2,4,16,1024]{3,2,1,0:T(8,128)(2,1)S(1)}, u32[]{:S(2)}, u32[]{:S(2)}) collective-permute-start(bf16[2,4,16,1024]{3,2,1,0:T(8,128)(2,1)S(1)} %collective-permute-done.8.refs_2_), channel_id=1, source_target_pairs={{0,1},{1,0},{2,3},{3,2},{4,5},{5,4},{6,7},{7,6},{8,9},{9,8},{10,11... | collective-permute-start | bytes 786440 | tf_op jit(solution)/shard_map/ppermute | solution.py:664
  55.3 2.9 %collective-permute-start.13 = (bf16[2,4,16,1024]{3,2,1,0:T(8,128)(2,1)S(1)}, bf16[2,4,16,1024]{3,2,1,0:T(8,128)(2,1)S(1)}, u32[]{:S(2)}, u32[]{:S(2)}) collective-permute-start(bf16[2,4,16,1024]{3,2,1,0:T(8,128)(2,1)S(1)} %collective-permute-done.9.refs_3_), channel_id=1, source_target_pairs={{0,1},{1,0},{2,3},{3,2},{4,5},{5,4},{6,7},{7,6},{8,9},{9,8},{10,11... | collective-permute-start | bytes 786440 | tf_op jit(solution)/shard_map/ppermute | solution.py:664
  55.3 2.1 %collective-permute-start.17 = (bf16[64,1152]{1,0:T(8,128)(2,1)S(1)}, bf16[64,1152]{1,0:T(8,128)(2,1)S(1)}, u32[]{:S(2)}, u32[]{:S(2)}) collective-permute-start(bf16[64,1152]{1,0:T(8,128)(2,1)S(1)} %get-tuple-element.27.refs_4_.refs_8_), channel_id=1, source_target_pairs={{0,1},{1,0},{2,3},{3,2},{4,5},{5,4},{6,7},{7,6},{8,9},{9,8},{10,11... | collective-permute-start | bytes 442376 | tf_op jit(solution)/shard_map/ppermute | solution.py:664
  55.8 2.3 %collective-permute-start.18 = (bf16[64,1152]{1,0:T(8,128)(2,1)S(1)}, bf16[64,1152]{1,0:T(8,128)(2,1)}, u32[]{:S(2)}, u32[]{:S(2)}) collective-permute-start(bf16[64,1152]{1,0:T(8,128)(2,1)S(1)} %collective-permute-done.14.refs_9_), channel_id=1, source_target_pairs={{0,1},{1,0},{2,3},{3,2},{4,5},{5,4},{6,7},{7,6},{8,9},{9,8},{10,11... | collective-permute-start | bytes 442376 | tf_op jit(solution)/shard_map/ppermute | solution.py:664
  (11 other events, 25.0 us)

commit v12 on v11

--- a/solution.py
+++ b/solution.py
@@ -755,6 +755,7 @@
         [((2, replicas, rows, slab), bf16)] * experts,
     )(*slabs, small)
     mine = [slices[0]] + [across(slices[step], "expert", step) for step in range(1, experts)]
+    mine[:2] = lax.optimization_barrier(tuple(mine[:2]))
     theirs = [across(block, "segment", 1) for block in mine]
     near = [small] + [across(small, "dp", step) for step in range(1, replicas)]
     near[:2] = lax.optimization_barrier(tuple(near[:2]))

time: 66.8 us -> 67.9 us (1.016)
  waiting for transfers between devices: 14.9 us -> 18 us
  starting transfers between devices: 27.9 us -> 25.9 us
    ppermute x17, waiting for transfers between devices: 8.6 us -> 11.7 us  [across(): return lax.ppermute(block, axis, [(i, i ^ distance) for i in range(size)])]
    ppermute x17, starting transfers between devices: 12.8 us -> 10.8 us  [across(): return lax.ppermute(block, axis, [(i, i ^ distance) for i in range(size)])]
  transfers between devices with their start and end apart: 23 -> 23, of which waited for: 5 -> 4; matrix products, arithmetic and copies ran while one was open for 0% -> 0% of each run, Pallas kernels for 21% -> 20%
where the time goes in v12:
time: 67.9 us; the launch traced here: 67.5 us
  starting transfers between devices  25.9 us (38%)
  Pallas kernels  20.4 us (30%)
  waiting for transfers between devices  18 us (27%)
  local copies, waits for them, and re-layouts  2.29 us (3%)
  between operations  0.91 us (1%)
    ppermute x17, waiting for transfers between devices, across(): return lax.ppermute(block, axis, [(i, i ^ distance) for i in range(size)])  11.7 us
    ppermute x17, starting transfers between devices, across(): return lax.ppermute(block, axis, [(i, i ^ distance) for i in range(size)])  10.8 us
    pallas_call x1, Pallas kernels, on_device_two_phases(): call(chain_kernel, 'chain', 50, [HBM] * 7, [((experts, 2, rows, part), bf...  7.1 us
    pallas_call x1, Pallas kernels, on_device_two_phases(): call(functools.partial(gradient_kernel, experts, sources, sizes), 'gradie...  6.58 us
    all_to_all x1, waiting for transfers between devices, on_device_two_phases(): lax.all_to_all(send, sections, split_axis=0, concat_axis=0, tiled=True)  6.33 us
    ppermute x4, starting transfers between devices, on_device_two_phases(): lax.ppermute(block, ('dp', 'segment'), slab_route(replicas, turn // 2, tu...  6.29 us
    all_to_all x1, starting transfers between devices, on_device_two_phases(): lax.all_to_all(send, sections, split_axis=0, concat_axis=0, tiled=True)  5.29 us
    all_to_all x1, starting transfers between devices, on_device_two_phases(): lax.all_to_all(out.reshape(groups, rows, part), sections, split_axis=0, c...  3.49 us
  transfers between devices with their start and end apart: 23, of which 4 were waited for; matrix products, arithmetic and copies ran while one was open for 0% of the time, Pallas kernels for 20%

profile of v12, /device:TPU:0, one launch (start us, length us, event | category | flops | bytes accessed | tf_op | source)
XLA Modules:
  0.0 67.5 jit_solution(13066486780716433453)
XLA Ops:
  0.6 0.5 collective-permute-start.4
  1.2 2.4 %pack.1._ = bf16[8,2,16,2048]{3,2,1,0:T(8,128)(2,1)} custom-call(s32[16]{0:T(128)} %refs_22_.1, bf16[16,4,2048]{2,1,0:T(4,128)(2,1)} %hidden.3, bf16[16,4,2048]{2,1,0:T(4,128)(2,1)} %cot.3), custom_call_target="tpu_custom_call" | custom-call | bytes 1048576 | tf_op jit(solution)/shard_map/pack/pallas_call | solution.py:695
  3.6 5.3 %all-to-all-start = ((bf16[8,2,16,2048]{3,2,1,0:T(8,128)(2,1)}), bf16[8,2,16,2048]{3,2,1,0:T(8,128)(2,1)S(1)}, u32[]{:S(2)}, u32[]{:S(2)}) async-start(bf16[8,2,16,2048]{3,2,1,0:T(8,128)(2,1)} %pack.1._), calls=%async_computation | async-start | bytes 2097152 | tf_op jit(solution)/shard_map/all_to_all | solution.py:725
  8.9 0.5 collective-permute-start.6
  9.4 2.3 %slabs.1 = (bf16[80,1024]{1,0:T(8,128)(2,1)}, bf16[80,1024]{1,0:T(8,128)(2,1)}, bf16[80,1024]{1,0:T(8,128)(2,1)}, bf16[80,1024]{1,0:T(8,128)(2,1)}) custom-call(s32[16]{0:T(128)} %refs_22_.1, bf16[16,4,2048]{2,1,0:T(4,128)(2,1)} %hidden.3, bf16[16,4,2048]{2,1,0:T(4,128)(2,1)} %cot.3, bf16[8,2,16,2048]{3,2,1,0:T(8,128)(2,1)} %pack.1._), custom_call_target="tpu_custom_call" | custom-call | bytes 1048576 | tf_op jit(solution)/shard_map/slabs/pallas_call | solution.py:709
  11.7 1.6 %collective-permute-start = (bf16[80,1024]{1,0:T(8,128)(2,1)}, bf16[80,1024]{1,0:T(8,128)(2,1)S(1)}, u32[]{:S(2)}, u32[]{:S(2)}) collective-permute-start(bf16[80,1024]{1,0:T(8,128)(2,1)} %get-tuple-element.20), channel_id=1, source_target_pairs={{0,0},{1,4},{2,2},{3,6},{4,1},{5,5},{6,3},{7,7},{8,8},{9,12},{10,1... | collective-permute-start | bytes 491528 | tf_op jit(solution)/shard_map/ppermute | solution.py:728
  13.3 3.1 %collective-permute-start.1 = (bf16[80,1024]{1,0:T(8,128)(2,1)}, bf16[80,1024]{1,0:T(8,128)(2,1)}, u32[]{:S(2)}, u32[]{:S(2)}) collective-permute-start(bf16[80,1024]{1,0:T(8,128)(2,1)} %get-tuple-element.21), channel_id=1, source_target_pairs={{0,1},{1,5},{2,3},{3,7},{4,0},{5,4},{6,2},{7,6},{8,9},{9,13},{10,1... | collective-permute-start | bytes 491528 | tf_op jit(solution)/shard_map/ppermute | solution.py:728
  16.4 1.6 %collective-permute-start.2 = (bf16[80,1024]{1,0:T(8,128)(2,1)}, bf16[80,1024]{1,0:T(8,128)(2,1)}, u32[]{:S(2)}, u32[]{:S(2)}) collective-permute-start(bf16[80,1024]{1,0:T(8,128)(2,1)} %get-tuple-element.22), channel_id=1, source_target_pairs={{0,2},{1,6},{2,0},{3,4},{4,3},{5,7},{6,1},{7,5},{8,10},{9,14},{10,... | collective-permute-start | bytes 491528 | tf_op jit(solution)/shard_map/ppermute | solution.py:728
  18.0 6.3 %all-to-all-done = bf16[8,2,16,2048]{3,2,1,0:T(8,128)(2,1)S(1)} async-done(((bf16[8,2,16,2048]{3,2,1,0:T(8,128)(2,1)}), bf16[8,2,16,2048]{3,2,1,0:T(8,128)(2,1)S(1)}, u32[]{:S(2)}, u32[]{:S(2)}) %all-to-all-start) | async-done | bytes 1048608 | tf_op jit(solution)/shard_map/all_to_all | solution.py:725
  24.4 7.1 %chain.1 = (bf16[4,2,16,2048]{3,2,1,0:T(8,128)(2,1)S(1)}, bf16[64,1152]{1,0:T(8,128)(2,1)S(1)}) custom-call(bf16[4,2,2,16,2048]{4,3,2,1,0:T(8,128)(2,1)S(1)} %bitcast.10, bf16[4096,256]{1,0:T(8,128)(2,1)S(1)} %bitcast.9, bf16[256,4096]{1,0:T(8,128)(2,1)} %bitcast.16, bf16[1,4096]{1,0:T(2,128)(2,1)S(1)} %bitcast.14, ...), custom_call_target="tpu_custom_call" | custom-call | flops 939524096 | bytes 10485760 | tf_op jit(solution)/shard_map/chain/pallas_call | solution.py:731
  31.5 3.7 %collective-permute-start.16 = (bf16[64,1152]{1,0:T(8,128)(2,1)S(1)}, bf16[64,1152]{1,0:T(8,128)(2,1)S(1)}, u32[]{:S(2)}, u32[]{:S(2)}) collective-permute-start(bf16[64,1152]{1,0:T(8,128)(2,1)S(1)} %get-tuple-element.31.refs_4_.refs_8_), channel_id=1, source_target_pairs={{0,6},{2,4},{4,2},{6,0},{1,7},{3,5},{5,3},{7,1},{8,14},{10,12},{12... | collective-permute-start | bytes 442376 | tf_op jit(solution)/shard_map/ppermute | solution.py:664
  35.2 2.1 %repack.1 = (bf16[2,4,16,1024]{3,2,1,0:T(8,128)(2,1)S(1)}, bf16[2,4,16,1024]{3,2,1,0:T(8,128)(2,1)S(1)}, bf16[2,4,16,1024]{3,2,1,0:T(8,128)(2,1)S(1)}, bf16[2,4,16,1024]{3,2,1,0:T(8,128)(2,1)S(1)}) custom-call(bf16[80,1024]{1,0:T(8,128)(2,1)S(1)} %collective-permute-done.refs_0_, bf16[80,1024]{1,0:T(8,128)(2,1)} %collective-permute-done.1.refs_1_, ...), custom_call_target="tpu_custom_call" | custom-call | bytes 1048576 | tf_op jit(solution)/shard_map/repack/pallas_call | solution.py:750
  37.3 0.6 collective-permute-start.7
  37.9 0.7 %collective-permute-start.14 = (bf16[64,1152]{1,0:T(8,128)(2,1)S(1)}, bf16[64,1152]{1,0:T(8,128)(2,1)S(1)}, u32[]{:S(2)}, u32[]{:S(2)}) collective-permute-start(bf16[64,1152]{1,0:T(8,128)(2,1)S(1)} %get-tuple-element.31.refs_4_.refs_8_), channel_id=1, source_target_pairs={{0,2},{2,0},{4,6},{6,4},{1,3},{3,1},{5,7},{7,5},{8,10},{10,8},{12,... | collective-permute-start | bytes 442376 | tf_op jit(solution)/shard_map/ppermute | solution.py:664
  38.6 0.7 collective-permute-start.8
  39.3 2.3 %collective-permute-start.9 = (bf16[2,4,16,1024]{3,2,1,0:T(8,128)(2,1)S(1)}, bf16[2,4,16,1024]{3,2,1,0:T(8,128)(2,1)S(1)}, u32[]{:S(2)}, u32[]{:S(2)}) collective-permute-start(bf16[2,4,16,1024]{3,2,1,0:T(8,128)(2,1)S(1)} %get-tuple-element.30), channel_id=1, source_target_pairs={{0,24},{8,16},{16,8},{24,0},{1,25},{9,17},{17,9},{25,1},{2,26},{10... | collective-permute-start | bytes 786440 | tf_op jit(solution)/shard_map/ppermute | solution.py:664
  41.6 3.5 %all-to-all-start.1 = ((bf16[8,16,2048]{2,1,0:T(8,128)(2,1)}), bf16[8,16,2048]{2,1,0:T(8,128)(2,1)S(1)}, u32[]{:S(2)}, u32[]{:S(2)}) async-start(bf16[8,16,2048]{2,1,0:T(8,128)(2,1)} %bitcast.11), calls=%async_computation.1 | async-start | bytes 1048576 | tf_op jit(solution)/shard_map/all_to_all | solution.py:764
  45.1 1.8 %collective-permute-done.15.refs_10_ = bf16[64,1152]{1,0:T(8,128)(2,1)S(1)} collective-permute-done((bf16[64,1152]{1,0:T(8,128)(2,1)S(1)}, bf16[64,1152]{1,0:T(8,128)(2,1)S(1)}, u32[]{:S(2)}, u32[]{:S(2)}) %collective-permute-start.15) | collective-permute-done | bytes 147488 | tf_op jit(solution)/shard_map/ppermute | solution.py:664
  46.9 0.5 collective-permute-start.19
  47.4 0.1 collective-permute-start.17
  47.5 8.8 %collective-permute-done.8.refs_2_ = bf16[2,4,16,1024]{3,2,1,0:T(8,128)(2,1)S(1)} collective-permute-done((bf16[2,4,16,1024]{3,2,1,0:T(8,128)(2,1)S(1)}, bf16[2,4,16,1024]{3,2,1,0:T(8,128)(2,1)S(1)}, u32[]{:S(2)}, u32[]{:S(2)}) %collective-permute-start.8) | collective-permute-done | bytes 262176 | tf_op jit(solution)/shard_map/ppermute | solution.py:664
  56.3 0.5 collective-permute-start.11
  56.8 0.1 collective-permute-start.12
  56.9 0.4 collective-permute-start.13
  57.4 0.6 copy-done.19
  58.0 1.1 %collective-permute-done.18.refs_13_ = bf16[64,1152]{1,0:T(8,128)(2,1)} collective-permute-done((bf16[64,1152]{1,0:T(8,128)(2,1)S(1)}, bf16[64,1152]{1,0:T(8,128)(2,1)}, u32[]{:S(2)}, u32[]{:S(2)}) %collective-permute-start.18) | collective-permute-done | bytes 147488 | tf_op jit(solution)/shard_map/ppermute | solution.py:664
  59.3 0.6 copy-done.6
  59.9 0.1 copy-done.10
  60.0 0.1 copy-done.11
  60.1 0.1 copy-done.12
  60.2 0.7 %copy-done.13 = bf16[2,4,16,1024]{3,2,1,0:T(8,128)(2,1)} copy-done((bf16[2,4,16,1024]{3,2,1,0:T(8,128)(2,1)}, bf16[2,4,16,1024]{3,2,1,0:T(8,128)(2,1)S(1)}, u32[]{:S(2)}) %copy-start.13) | copy-done | bytes 262168
  60.9 6.6 %gradients.1 = (bf16[16,4,2048]{2,1,0:T(4,128)(2,1)}, bf16[1024,256]{1,0:T(8,128)(2,1)}, bf16[256,1024]{1,0:T(8,128)(2,1)}) custom-call(bf16[2,4,16,1024]{3,2,1,0:T(8,128)(2,1)} %copy-done.3, bf16[2,4,16,1024]{3,2,1,0:T(8,128)(2,1)} %copy-done.7, bf16[2,4,16,1024]{3,2,1,0:T(8,128)(2,1)} %copy-done.8, bf16[2,4,16,1024]{3,2,1,0:T(8,128)(2,1)} %copy-done.9, ...), custom_call_target="tpu_custom_call" | custom-call | bytes 1048576 | tf_op jit(solution)/shard_map/gradients/pallas_call | solution.py:770
  (59 shorter events, 0.3 us)
Async XLA Ops:
  0.6 17.4 %collective-permute-start.4 = (bf16[4096,256]{1,0:T(8,128)(2,1)}, bf16[4096,256]{1,0:T(8,128)(2,1)}, u32[]{:S(2)}, u32[]{:S(2)}) collective-permute-start(bf16[4096,256]{1,0:T(8,128)(2,1)} %bitcast.7), channel_id=1, source_target_pairs={{0,1},{1,0},{2,3},{3,2},{4,5},{5,4},{6,7},{7,6},{8,9},{9,8},{10,11... | collective-permute-start | bytes 6291464 | tf_op jit(solution)/shard_map/ppermute | solution.py:664
  1.2 23.2 %collective-permute-start.5 = (bf16[256,4096]{1,0:T(8,128)(2,1)}, bf16[256,4096]{1,0:T(8,128)(2,1)}, u32[]{:S(2)}, u32[]{:S(2)}) collective-permute-start(bf16[256,4096]{1,0:T(8,128)(2,1)} %bitcast.15), channel_id=1, source_target_pairs={{0,1},{1,0},{2,3},{3,2},{4,5},{5,4},{6,7},{7,6},{8,9},{9,8},{10,11... | collective-permute-start | bytes 6291464 | tf_op jit(solution)/shard_map/ppermute | solution.py:664
  3.6 20.7 %copy-start = (bf16[1,1,4096,256]{3,2,1,0:T(8,128)(2,1)S(1)}, bf16[1,1,4096,256]{3,2,1,0:T(8,128)(2,1)}, u32[]{:S(2)}) copy-start(bf16[1,1,4096,256]{3,2,1,0:T(8,128)(2,1)} %param.9) | copy-start | bytes 6291460
  3.6 20.7 %all-to-all-start = ((bf16[8,2,16,2048]{3,2,1,0:T(8,128)(2,1)}), bf16[8,2,16,2048]{3,2,1,0:T(8,128)(2,1)S(1)}, u32[]{:S(2)}, u32[]{:S(2)}) async-start(bf16[8,2,16,2048]{3,2,1,0:T(8,128)(2,1)} %pack.1._), calls=%async_computation | async-start | bytes 2097152 | tf_op jit(solution)/shard_map/all_to_all | solution.py:725
  8.9 7.5 %collective-permute-start.6 = (bf16[1,4096]{1,0:T(2,128)(2,1)S(1)}, bf16[1,4096]{1,0:T(2,128)(2,1)S(1)}, u32[]{:S(2)}, u32[]{:S(2)}) collective-permute-start(bf16[1,4096]{1,0:T(2,128)(2,1)S(1)} %bitcast.13), channel_id=1, source_target_pairs={{0,1},{1,0},{2,3},{3,2},{4,5},{5,4},{6,7},{7,6},{8,9},{9,8},{10,11... | collective-permute-start | bytes 24584 | tf_op jit(solution)/shard_map/ppermute | solution.py:664
  11.7 23.4 %collective-permute-start = (bf16[80,1024]{1,0:T(8,128)(2,1)}, bf16[80,1024]{1,0:T(8,128)(2,1)S(1)}, u32[]{:S(2)}, u32[]{:S(2)}) collective-permute-start(bf16[80,1024]{1,0:T(8,128)(2,1)} %get-tuple-element.20), channel_id=1, source_target_pairs={{0,0},{1,4},{2,2},{3,6},{4,1},{5,5},{6,3},{7,7},{8,8},{9,12},{10,1... | collective-permute-start | bytes 491528 | tf_op jit(solution)/shard_map/ppermute | solution.py:728
  13.3 21.9 %collective-permute-start.1 = (bf16[80,1024]{1,0:T(8,128)(2,1)}, bf16[80,1024]{1,0:T(8,128)(2,1)}, u32[]{:S(2)}, u32[]{:S(2)}) collective-permute-start(bf16[80,1024]{1,0:T(8,128)(2,1)} %get-tuple-element.21), channel_id=1, source_target_pairs={{0,1},{1,5},{2,3},{3,7},{4,0},{5,4},{6,2},{7,6},{8,9},{9,13},{10,1... | collective-permute-start | bytes 491528 | tf_op jit(solution)/shard_map/ppermute | solution.py:728
  16.4 15.0 %copy-start.5 = (bf16[1,4096]{1,0:T(2,128)(2,1)}, bf16[1,4096]{1,0:T(2,128)(2,1)S(1)}, u32[]{:S(2)}) copy-start(bf16[1,4096]{1,0:T(2,128)(2,1)S(1)} %collective-permute-done.6.other_gain.refs_21_) | copy-start | bytes 24580
  16.4 18.7 %collective-permute-start.2 = (bf16[80,1024]{1,0:T(8,128)(2,1)}, bf16[80,1024]{1,0:T(8,128)(2,1)}, u32[]{:S(2)}, u32[]{:S(2)}) collective-permute-start(bf16[80,1024]{1,0:T(8,128)(2,1)} %get-tuple-element.22), channel_id=1, source_target_pairs={{0,2},{1,6},{2,0},{3,4},{4,3},{5,7},{6,1},{7,5},{8,10},{9,14},{10,... | collective-permute-start | bytes 491528 | tf_op jit(solution)/shard_map/ppermute | solution.py:728
  18.0 17.2 %collective-permute-start.3 = (bf16[80,1024]{1,0:T(8,128)(2,1)}, bf16[80,1024]{1,0:T(8,128)(2,1)}, u32[]{:S(2)}, u32[]{:S(2)}) collective-permute-start(bf16[80,1024]{1,0:T(8,128)(2,1)} %get-tuple-element.23), channel_id=1, source_target_pairs={{0,3},{1,7},{2,1},{3,5},{4,2},{5,6},{6,0},{7,4},{8,11},{9,15},{10,... | collective-permute-start | bytes 491528 | tf_op jit(solution)/shard_map/ppermute | solution.py:728
  31.5 10.1 %copy-start.2 = (bf16[4,2,16,2048]{3,2,1,0:T(8,128)(2,1)}, bf16[4,2,16,2048]{3,2,1,0:T(8,128)(2,1)S(1)}, u32[]{:S(2)}) copy-start(bf16[4,2,16,2048]{3,2,1,0:T(8,128)(2,1)S(1)} %get-tuple-element.33) | copy-start | bytes 1572868
  31.5 27.7 %copy-start.1 = (bf16[64,1152]{1,0:T(8,128)(2,1)}, bf16[64,1152]{1,0:T(8,128)(2,1)S(1)}, u32[]{:S(2)}) copy-start(bf16[64,1152]{1,0:T(8,128)(2,1)S(1)} %get-tuple-element.31.refs_4_.refs_8_) | copy-start | bytes 442372
  31.5 7.8 %collective-permute-start.16 = (bf16[64,1152]{1,0:T(8,128)(2,1)S(1)}, bf16[64,1152]{1,0:T(8,128)(2,1)S(1)}, u32[]{:S(2)}, u32[]{:S(2)}) collective-permute-start(bf16[64,1152]{1,0:T(8,128)(2,1)S(1)} %get-tuple-element.31.refs_4_.refs_8_), channel_id=1, source_target_pairs={{0,6},{2,4},{4,2},{6,0},{1,7},{3,5},{5,3},{7,1},{8,14},{10,12},{12... | collective-permute-start | bytes 442376 | tf_op jit(solution)/shard_map/ppermute | solution.py:664
  37.2 21.9 %copy-start.3 = (bf16[2,4,16,1024]{3,2,1,0:T(8,128)(2,1)}, bf16[2,4,16,1024]{3,2,1,0:T(8,128)(2,1)S(1)}, u32[]{:S(2)}) copy-start(bf16[2,4,16,1024]{3,2,1,0:T(8,128)(2,1)S(1)} %get-tuple-element.27.refs_0_) | copy-start | bytes 786436
  37.3 10.1 %collective-permute-start.7 = (bf16[2,4,16,1024]{3,2,1,0:T(8,128)(2,1)S(1)}, bf16[2,4,16,1024]{3,2,1,0:T(8,128)(2,1)S(1)}, u32[]{:S(2)}, u32[]{:S(2)}) collective-permute-start(bf16[2,4,16,1024]{3,2,1,0:T(8,128)(2,1)S(1)} %get-tuple-element.26), channel_id=1, source_target_pairs={{0,8},{8,0},{16,24},{24,16},{1,9},{9,1},{17,25},{25,17},{2,10},{10... | collective-permute-start | bytes 786440 | tf_op jit(solution)/shard_map/ppermute | solution.py:664
  37.9 9.0 %collective-permute-start.15 = (bf16[64,1152]{1,0:T(8,128)(2,1)S(1)}, bf16[64,1152]{1,0:T(8,128)(2,1)S(1)}, u32[]{:S(2)}, u32[]{:S(2)}) collective-permute-start(bf16[64,1152]{1,0:T(8,128)(2,1)S(1)} %get-tuple-element.31.refs_4_.refs_8_), channel_id=1, source_target_pairs={{0,4},{2,6},{4,0},{6,2},{1,5},{3,7},{5,1},{7,3},{8,12},{10,14},{12... | collective-permute-start | bytes 442376 | tf_op jit(solution)/shard_map/ppermute | solution.py:664
  37.9 9.0 %collective-permute-start.14 = (bf16[64,1152]{1,0:T(8,128)(2,1)S(1)}, bf16[64,1152]{1,0:T(8,128)(2,1)S(1)}, u32[]{:S(2)}, u32[]{:S(2)}) collective-permute-start(bf16[64,1152]{1,0:T(8,128)(2,1)S(1)} %get-tuple-element.31.refs_4_.refs_8_), channel_id=1, source_target_pairs={{0,2},{2,0},{4,6},{6,4},{1,3},{3,1},{5,7},{7,5},{8,10},{10,8},{12,... | collective-permute-start | bytes 442376 | tf_op jit(solution)/shard_map/ppermute | solution.py:664
  38.6 17.6 %collective-permute-start.8 = (bf16[2,4,16,1024]{3,2,1,0:T(8,128)(2,1)S(1)}, bf16[2,4,16,1024]{3,2,1,0:T(8,128)(2,1)S(1)}, u32[]{:S(2)}, u32[]{:S(2)}) collective-permute-start(bf16[2,4,16,1024]{3,2,1,0:T(8,128)(2,1)S(1)} %get-tuple-element.29), channel_id=1, source_target_pairs={{0,16},{8,24},{16,0},{24,8},{1,17},{9,25},{17,1},{25,9},{2,18},{10... | collective-permute-start | bytes 786440 | tf_op jit(solution)/shard_map/ppermute | solution.py:664
  39.3 19.9 %copy-start.14 = (bf16[64,1152]{1,0:T(8,128)(2,1)}, bf16[64,1152]{1,0:T(8,128)(2,1)S(1)}, u32[]{:S(2)}) copy-start(bf16[64,1152]{1,0:T(8,128)(2,1)S(1)} %collective-permute-done.16.refs_11_) | copy-start | bytes 442372
  39.3 17.0 %collective-permute-start.9 = (bf16[2,4,16,1024]{3,2,1,0:T(8,128)(2,1)S(1)}, bf16[2,4,16,1024]{3,2,1,0:T(8,128)(2,1)S(1)}, u32[]{:S(2)}, u32[]{:S(2)}) collective-permute-start(bf16[2,4,16,1024]{3,2,1,0:T(8,128)(2,1)S(1)} %get-tuple-element.30), channel_id=1, source_target_pairs={{0,24},{8,16},{16,8},{24,0},{1,25},{9,17},{17,9},{25,1},{2,26},{10... | collective-permute-start | bytes 786440 | tf_op jit(solution)/shard_map/ppermute | solution.py:664
  41.6 17.5 %all-to-all-start.1 = ((bf16[8,16,2048]{2,1,0:T(8,128)(2,1)}), bf16[8,16,2048]{2,1,0:T(8,128)(2,1)S(1)}, u32[]{:S(2)}, u32[]{:S(2)}) async-start(bf16[8,16,2048]{2,1,0:T(8,128)(2,1)} %bitcast.11), calls=%async_computation.1 | async-start | bytes 1048576 | tf_op jit(solution)/shard_map/all_to_all | solution.py:764
  46.9 12.3 %copy-start.15 = (bf16[64,1152]{1,0:T(8,128)(2,1)}, bf16[64,1152]{1,0:T(8,128)(2,1)S(1)}, u32[]{:S(2)}) copy-start(bf16[64,1152]{1,0:T(8,128)(2,1)S(1)} %collective-permute-done.15.refs_10_) | copy-start | bytes 442372
  46.9 9.9 %collective-permute-start.20 = (bf16[64,1152]{1,0:T(8,128)(2,1)S(1)}, bf16[64,1152]{1,0:T(8,128)(2,1)S(1)}, u32[]{:S(2)}, u32[]{:S(2)}) collective-permute-start(bf16[64,1152]{1,0:T(8,128)(2,1)S(1)} %collective-permute-done.16.refs_11_), channel_id=1, source_target_pairs={{0,1},{1,0},{2,3},{3,2},{4,5},{5,4},{6,7},{7,6},{8,9},{9,8},{10,11... | collective-permute-start | bytes 442376 | tf_op jit(solution)/shard_map/ppermute | solution.py:664
  46.9 12.3 %copy-start.16 = (bf16[64,1152]{1,0:T(8,128)(2,1)}, bf16[64,1152]{1,0:T(8,128)(2,1)S(1)}, u32[]{:S(2)}) copy-start(bf16[64,1152]{1,0:T(8,128)(2,1)S(1)} %collective-permute-done.14.refs_9_) | copy-start | bytes 442372
  46.9 10.0 %collective-permute-start.19 = (bf16[64,1152]{1,0:T(8,128)(2,1)S(1)}, bf16[64,1152]{1,0:T(8,128)(2,1)S(1)}, u32[]{:S(2)}, u32[]{:S(2)}) collective-permute-start(bf16[64,1152]{1,0:T(8,128)(2,1)S(1)} %collective-permute-done.15.refs_10_), channel_id=1, source_target_pairs={{0,1},{1,0},{2,3},{3,2},{4,5},{5,4},{6,7},{7,6},{8,9},{9,8},{10,11... | collective-permute-start | bytes 442376 | tf_op jit(solution)/shard_map/ppermute | solution.py:664
  47.4 11.8 %copy-start.7 = (bf16[2,4,16,1024]{3,2,1,0:T(8,128)(2,1)}, bf16[2,4,16,1024]{3,2,1,0:T(8,128)(2,1)S(1)}, u32[]{:S(2)}) copy-start(bf16[2,4,16,1024]{3,2,1,0:T(8,128)(2,1)S(1)} %collective-permute-done.7.refs_1_) | copy-start | bytes 786436
  47.4 9.9 %collective-permute-start.17 = (bf16[64,1152]{1,0:T(8,128)(2,1)S(1)}, bf16[64,1152]{1,0:T(8,128)(2,1)S(1)}, u32[]{:S(2)}, u32[]{:S(2)}) collective-permute-start(bf16[64,1152]{1,0:T(8,128)(2,1)S(1)} %get-tuple-element.31.refs_4_.refs_8_), channel_id=1, source_target_pairs={{0,1},{1,0},{2,3},{3,2},{4,5},{5,4},{6,7},{7,6},{8,9},{9,8},{10,11... | collective-permute-start | bytes 442376 | tf_op jit(solution)/shard_map/ppermute | solution.py:664
  56.3 2.8 %collective-permute-start.10 = (bf16[2,4,16,1024]{3,2,1,0:T(8,128)(2,1)S(1)}, bf16[2,4,16,1024]{3,2,1,0:T(8,128)(2,1)S(1)}, u32[]{:S(2)}, u32[]{:S(2)}) collective-permute-start(bf16[2,4,16,1024]{3,2,1,0:T(8,128)(2,1)S(1)} %get-tuple-element.27.refs_0_), channel_id=1, source_target_pairs={{0,1},{1,0},{2,3},{3,2},{4,5},{5,4},{6,7},{7,6},{8,9},{9,8},{10,11... | collective-permute-start | bytes 786440 | tf_op jit(solution)/shard_map/ppermute | solution.py:664
  56.3 2.8 %collective-permute-start.11 = (bf16[2,4,16,1024]{3,2,1,0:T(8,128)(2,1)S(1)}, bf16[2,4,16,1024]{3,2,1,0:T(8,128)(2,1)S(1)}, u32[]{:S(2)}, u32[]{:S(2)}) collective-permute-start(bf16[2,4,16,1024]{3,2,1,0:T(8,128)(2,1)S(1)} %collective-permute-done.7.refs_1_), channel_id=1, source_target_pairs={{0,1},{1,0},{2,3},{3,2},{4,5},{5,4},{6,7},{7,6},{8,9},{9,8},{10,11... | collective-permute-start | bytes 786440 | tf_op jit(solution)/shard_map/ppermute | solution.py:664
  56.8 2.4 %collective-permute-start.12 = (bf16[2,4,16,1024]{3,2,1,0:T(8,128)(2,1)S(1)}, bf16[2,4,16,1024]{3,2,1,0:T(8,128)(2,1)S(1)}, u32[]{:S(2)}, u32[]{:S(2)}) collective-permute-start(bf16[2,4,16,1024]{3,2,1,0:T(8,128)(2,1)S(1)} %collective-permute-done.8.refs_2_), channel_id=1, source_target_pairs={{0,1},{1,0},{2,3},{3,2},{4,5},{5,4},{6,7},{7,6},{8,9},{9,8},{10,11... | collective-permute-start | bytes 786440 | tf_op jit(solution)/shard_map/ppermute | solution.py:664
  56.9 2.3 %collective-permute-start.13 = (bf16[2,4,16,1024]{3,2,1,0:T(8,128)(2,1)S(1)}, bf16[2,4,16,1024]{3,2,1,0:T(8,128)(2,1)S(1)}, u32[]{:S(2)}, u32[]{:S(2)}) collective-permute-start(bf16[2,4,16,1024]{3,2,1,0:T(8,128)(2,1)S(1)} %collective-permute-done.9.refs_3_), channel_id=1, source_target_pairs={{0,1},{1,0},{2,3},{3,2},{4,5},{5,4},{6,7},{7,6},{8,9},{9,8},{10,11... | collective-permute-start | bytes 786440 | tf_op jit(solution)/shard_map/ppermute | solution.py:664
  57.3 1.8 %collective-permute-start.18 = (bf16[64,1152]{1,0:T(8,128)(2,1)S(1)}, bf16[64,1152]{1,0:T(8,128)(2,1)}, u32[]{:S(2)}, u32[]{:S(2)}) collective-permute-start(bf16[64,1152]{1,0:T(8,128)(2,1)S(1)} %collective-permute-done.14.refs_9_), channel_id=1, source_target_pairs={{0,1},{1,0},{2,3},{3,2},{4,5},{5,4},{6,7},{7,6},{8,9},{9,8},{10,11... | collective-permute-start | bytes 442376 | tf_op jit(solution)/shard_map/ppermute | solution.py:664
  (11 other events, 24.3 us)

commit v13 on v12

--- a/solution.py
+++ b/solution.py
@@ -314,21 +314,43 @@
 
 
 def repack_kernel(length, capacity, *refs):
-    slabs, outs = refs[:4], refs[5:]
-    experts, rows = len(outs), outs[0].shape[2]
+    slabs, recv, outs, sems = refs[:4], refs[4], refs[6:-1], refs[-1]
+    kept, sent = outs[0], outs[1:]
+    _, _, rows, slab = kept.shape
+    experts = len(outs)
     half = (slabs[0].shape[0] - 16) // 2
     core, replica = lax.axis_index("segment"), lax.axis_index("dp")
-    for turn, slab in enumerate(slabs):
-        near = turn // 2 + 2 * ((turn % 2) ^ (replica >> 1) ^ core)
-        ids_row = slab[2 * half :, :128].astype(jnp.float32)[:1, :half].astype(jnp.int32)
+    expert = lax.axis_index("expert")
+    per_part = recv.shape[4] // slab
+    part = replica // per_part
+    cols = pl.ds(pl.multiple_of((replica - part * per_part) * slab, slab), slab)
+    cuts = [
+        pltpu.make_async_copy(
+            recv.at[e, part, :, :, cols], kept.at[:, 3 + (e ^ expert)], sems.at[e]
+        )
+        for e in range(experts)
+    ]
+    for cut in cuts:
+        cut.start()
+    far_low = (replica >> 1) ^ core ^ 1
+
+    def place_rows(held, near):
+        ids_row = held[2 * half :, :128].astype(jnp.float32)[:1, :half].astype(jnp.int32)
         rank, _ = ranked(ids_row, length)
         token = lax.rem(lax.broadcasted_iota(jnp.int32, ids_row.shape, 1), length)
-        step = ids_row ^ lax.axis_index("expert")
+        step = ids_row ^ expert
         place = one_hot((step * (capacity // 2) + rank) * length + token, experts * rows)
         for which in range(2):
-            moved = matmul(place, slab[which * half : (which + 1) * half]).astype(jnp.bfloat16)
-            for e in range(experts):
-                outs[e][which, near] = moved[e * rows : (e + 1) * rows]
+            moved = matmul(place, held[which * half : (which + 1) * half]).astype(jnp.bfloat16)
+            kept[which, near - 1] = moved[:rows]
+            for step_at, out in enumerate(sent):
+                out[which, near - 1] = moved[(step_at + 1) * rows : (step_at + 2) * rows]
+
+    place_rows(jnp.where(far_low == 1, slabs[1][...], slabs[0][...]), 2)
+    for low in range(2):
+        place_rows(slabs[2 + low][...], 1 + 2 * (low ^ (replica >> 1) ^ core))
+    for cut in cuts:
+        cut.wait()
 
 
 def unpack(sizes, id_buf, back, out):
@@ -507,6 +529,8 @@
     place = lax.axis_index("dp")
     rows, slab = smalls[0].shape[0], sides[0].shape[3]
     replicas = sources // 2
+    blocks = [side.shape[1] for side in sides[:experts]]
+    starts = [sum(blocks[:step]) for step in range(experts)]
     rank = dn_buf.shape[1]
     columns = 256
     chunks = range(0, slab, columns)
@@ -538,7 +562,13 @@
         [
             pltpu.make_async_copy(
                 side.at[:, :, :, col : col + columns],
-                wide_buf.at[at, :, :, :, col : col + columns],
+                wide_buf.at[
+                    at // experts,
+                    :,
+                    starts[at % experts] : starts[at % experts] + blocks[at % experts],
+                    :,
+                    col : col + columns,
+                ],
                 wide_sems.at[col // columns, at],
             )
             for at, side in enumerate(sides)
@@ -570,10 +600,12 @@
         copy.wait()
 
     def sliced(source, which, here):
-        first, near = (source // replicas) * experts, source % replicas
-        return jnp.concatenate(
-            [wide_buf[first + step, which, near, :, here] for step in range(experts)], axis=0
-        )
+        side, near = source // replicas, source % replicas
+        at = [
+            replicas - 1 + step if near == 0 else starts[step] + near - 1
+            for step in range(experts)
+        ]
+        return jnp.concatenate([wide_buf[side, which, one, :, here] for one in at], axis=0)
 
     def moment(at, index):
         value = moments[at, index * 128 : (index + 1) * 128]
@@ -751,14 +783,18 @@
         functools.partial(repack_kernel, length, capacity),
         "repack",
         16,
-        [VMEM] * 4 + [HBM],
-        [((2, replicas, rows, slab), bf16)] * experts,
-    )(*slabs, small)
+        [VMEM] * 4 + [HBM] * 2,
+        [((2, replicas - 1 + experts, rows, slab), bf16)]
+        + [((2, replicas - 1, rows, slab), bf16)] * (experts - 1),
+        [pltpu.SemaphoreType.DMA((experts,))],
+    )(*slabs, recv, small)
+    small, *slices = lax.optimization_barrier((small, *slices))
     mine = [slices[0]] + [across(slices[step], "expert", step) for step in range(1, experts)]
     mine[:2] = lax.optimization_barrier(tuple(mine[:2]))
     theirs = [across(block, "segment", 1) for block in mine]
-    near = [small] + [across(small, "dp", step) for step in range(1, replicas)]
+    near = [small] + [across(small, "dp", step) for step in range(1, replicas - 1)]
     near[:2] = lax.optimization_barrier(tuple(near[:2]))
+    near.append(across(near[0], "dp", replicas - 1))
     smalls = near + [across(piece, "segment", 1) for piece in near]
 
     back = lax.all_to_all(
@@ -780,7 +816,7 @@
             pltpu.VMEM((slab, rank), bf16),
             pltpu.VMEM((rank, slab), bf16),
             pltpu.VMEM((2, 1, slab), bf16),
-            pltpu.VMEM((2 * experts, 2, replicas, rows, slab), bf16),
+            pltpu.VMEM((2, 2, replicas * experts, rows, slab), bf16),
             pltpu.VMEM((all_tokens, 4 * rank + 128), bf16),
             pltpu.VMEM((all_tokens, 6 * 128), f32),
             pltpu.VMEM((2, rank, all_tokens), bf16),

time: 67.9 us -> 65.3 us (0.962)
  waiting for transfers between devices: 18 us -> 14.2 us
  starting transfers between devices: 25.9 us -> 27.9 us
  Pallas kernels: 20.4 us -> 19.7 us
    ppermute x17, waiting for transfers between devices: 11.7 us -> 7.9 us  [across(): return lax.ppermute(block, axis, [(i, i ^ distance) for i in range(size)])]
    ppermute x17, starting transfers between devices: 10.8 us -> 12.9 us  [across(): return lax.ppermute(block, axis, [(i, i ^ distance) for i in range(size)])]
    pallas_call x1, Pallas kernels: 6.58 us -> 5.83 us  [on_device_two_phases(): call(functools.partial(gradient_kernel, experts, sources, sizes), 'gradie...]
    unnamed x40 -> x38, local copies, waits for them, and re-layouts: 2.29 us -> 2.13 us
  transfers between devices with their start and end apart: 23 -> 23, of which waited for: 4 -> 4; matrix products, arithmetic and copies ran while one was open for 0% -> 0% of each run, Pallas kernels for 20% -> 18%
where the time goes in v13:
time: 65.3 us; the launch traced here: 65 us
  starting transfers between devices  27.9 us (43%)
  Pallas kernels  19.7 us (30%)
  waiting for transfers between devices  14.2 us (22%)
  local copies, waits for them, and re-layouts  2.13 us (3%)
  between operations  0.93 us (1%)
    ppermute x17, starting transfers between devices, across(): return lax.ppermute(block, axis, [(i, i ^ distance) for i in range(size)])  12.9 us
    ppermute x17, waiting for transfers between devices, across(): return lax.ppermute(block, axis, [(i, i ^ distance) for i in range(size)])  7.9 us
    pallas_call x1, Pallas kernels, on_device_two_phases(): call(chain_kernel, 'chain', 50, [HBM] * 7, [((experts, 2, rows, part), bf...  7.1 us
    all_to_all x1, waiting for transfers between devices, on_device_two_phases(): lax.all_to_all(send, sections, split_axis=0, concat_axis=0, tiled=True)  6.33 us
    ppermute x4, starting transfers between devices, on_device_two_phases(): lax.ppermute(block, ('dp', 'segment'), slab_route(replicas, turn // 2, tu...  6.29 us
    pallas_call x1, Pallas kernels, on_device_two_phases(): call(functools.partial(gradient_kernel, experts, sources, sizes), 'gradie...  5.83 us
    all_to_all x1, starting transfers between devices, on_device_two_phases(): lax.all_to_all(send, sections, split_axis=0, concat_axis=0, tiled=True)  5.29 us
    all_to_all x1, starting transfers between devices, on_device_two_phases(): lax.all_to_all(out.reshape(groups, rows, part), sections, split_axis=0, c...  3.49 us
  transfers between devices with their start and end apart: 23, of which 4 were waited for; matrix products, arithmetic and copies ran while one was open for 0% of the time, Pallas kernels for 18%

profile of v13, /device:TPU:0, one launch (start us, length us, event | category | flops | bytes accessed | tf_op | source)
XLA Modules:
  0.0 65.0 jit_solution(13029092360258332634)
XLA Ops:
  0.6 0.5 collective-permute-start
  1.2 0.1 collective-permute-start.1
  1.2 2.4 %pack.1._ = bf16[8,2,16,2048]{3,2,1,0:T(8,128)(2,1)} custom-call(s32[16]{0:T(128)} %refs_22_.1, bf16[16,4,2048]{2,1,0:T(4,128)(2,1)} %hidden.3, bf16[16,4,2048]{2,1,0:T(4,128)(2,1)} %cot.3), custom_call_target="tpu_custom_call" | custom-call | bytes 1048576 | tf_op jit(solution)/shard_map/pack/pallas_call | solution.py:727
  3.6 5.3 %all-to-all-start = ((bf16[8,2,16,2048]{3,2,1,0:T(8,128)(2,1)}), bf16[8,2,16,2048]{3,2,1,0:T(8,128)(2,1)S(1)}, u32[]{:S(2)}, u32[]{:S(2)}) async-start(bf16[8,2,16,2048]{3,2,1,0:T(8,128)(2,1)} %pack.1._), calls=%async_computation | async-start | bytes 2097152 | tf_op jit(solution)/shard_map/all_to_all | solution.py:757
  8.9 0.5 collective-permute-start.2
  9.4 2.3 %slabs.1 = (bf16[80,1024]{1,0:T(8,128)(2,1)}, bf16[80,1024]{1,0:T(8,128)(2,1)}, bf16[80,1024]{1,0:T(8,128)(2,1)}, bf16[80,1024]{1,0:T(8,128)(2,1)}) custom-call(s32[16]{0:T(128)} %refs_22_.1, bf16[16,4,2048]{2,1,0:T(4,128)(2,1)} %hidden.3, bf16[16,4,2048]{2,1,0:T(4,128)(2,1)} %cot.3, bf16[8,2,16,2048]{3,2,1,0:T(8,128)(2,1)} %pack.1._), custom_call_target="tpu_custom_call" | custom-call | bytes 1048576 | tf_op jit(solution)/shard_map/slabs/pallas_call | solution.py:741
  11.7 1.6 %collective-permute-start.3 = (bf16[80,1024]{1,0:T(8,128)(2,1)}, bf16[80,1024]{1,0:T(8,128)(2,1)S(1)}, u32[]{:S(2)}, u32[]{:S(2)}) collective-permute-start(bf16[80,1024]{1,0:T(8,128)(2,1)} %get-tuple-element.26), channel_id=1, source_target_pairs={{0,0},{1,4},{2,2},{3,6},{4,1},{5,5},{6,3},{7,7},{8,8},{9,12},{10,1... | collective-permute-start | bytes 491528 | tf_op jit(solution)/shard_map/ppermute | solution.py:760
  13.3 3.1 %collective-permute-start.4 = (bf16[80,1024]{1,0:T(8,128)(2,1)}, bf16[80,1024]{1,0:T(8,128)(2,1)}, u32[]{:S(2)}, u32[]{:S(2)}) collective-permute-start(bf16[80,1024]{1,0:T(8,128)(2,1)} %get-tuple-element.27), channel_id=1, source_target_pairs={{0,1},{1,5},{2,3},{3,7},{4,0},{5,4},{6,2},{7,6},{8,9},{9,13},{10,1... | collective-permute-start | bytes 491528 | tf_op jit(solution)/shard_map/ppermute | solution.py:760
  16.4 1.6 %collective-permute-start.5 = (bf16[80,1024]{1,0:T(8,128)(2,1)}, bf16[80,1024]{1,0:T(8,128)(2,1)}, u32[]{:S(2)}, u32[]{:S(2)}) collective-permute-start(bf16[80,1024]{1,0:T(8,128)(2,1)} %get-tuple-element.28), channel_id=1, source_target_pairs={{0,2},{1,6},{2,0},{3,4},{4,3},{5,7},{6,1},{7,5},{8,10},{9,14},{10,... | collective-permute-start | bytes 491528 | tf_op jit(solution)/shard_map/ppermute | solution.py:760
  18.0 6.3 %all-to-all-done = bf16[8,2,16,2048]{3,2,1,0:T(8,128)(2,1)S(1)} async-done(((bf16[8,2,16,2048]{3,2,1,0:T(8,128)(2,1)}), bf16[8,2,16,2048]{3,2,1,0:T(8,128)(2,1)S(1)}, u32[]{:S(2)}, u32[]{:S(2)}) %all-to-all-start) | async-done | bytes 1048608 | tf_op jit(solution)/shard_map/all_to_all | solution.py:757
  24.3 7.1 %chain.1 = (bf16[4,2,16,2048]{3,2,1,0:T(8,128)(2,1)S(1)}, bf16[64,1152]{1,0:T(8,128)(2,1)S(1)}) custom-call(bf16[4,2,2,16,2048]{4,3,2,1,0:T(8,128)(2,1)S(1)} %bitcast.7, bf16[4096,256]{1,0:T(8,128)(2,1)S(1)} %bitcast.11, bf16[256,4096]{1,0:T(8,128)(2,1)} %bitcast.17, bf16[1,4096]{1,0:T(2,128)(2,1)S(1)} %bitcast.15, ...), custom_call_target="tpu_custom_call" | custom-call | flops 939524096 | bytes 10485760 | tf_op jit(solution)/shard_map/chain/pallas_call | solution.py:763
  31.5 2.2 %repack.1 = (bf16[2,7,16,1024]{3,2,1,0:T(8,128)(2,1)S(1)}, bf16[2,3,16,1024]{3,2,1,0:T(8,128)(2,1)S(1)}, bf16[2,3,16,1024]{3,2,1,0:T(8,128)(2,1)S(1)}, bf16[2,3,16,1024]{3,2,1,0:T(8,128)(2,1)S(1)}) custom-call(bf16[80,1024]{1,0:T(8,128)(2,1)S(1)} %collective-permute-done.3.refs_0_, bf16[80,1024]{1,0:T(8,128)(2,1)} %collective-permute-done.4.refs_1_, ...), custom_call_target="tpu_custom_call" | custom-call | bytes 1048576 | tf_op jit(solution)/shard_map/repack/pallas_call | solution.py:782
  33.7 0.6 collective-permute-start.7
  34.3 0.8 %collective-permute-start.8 = (bf16[2,3,16,1024]{3,2,1,0:T(8,128)(2,1)S(1)}, bf16[2,3,16,1024]{3,2,1,0:T(8,128)(2,1)S(1)}, u32[]{:S(2)}, u32[]{:S(2)}) collective-permute-start(bf16[2,3,16,1024]{3,2,1,0:T(8,128)(2,1)S(1)} %get-tuple-element.38), channel_id=1, source_target_pairs={{0,16},{8,24},{16,0},{24,8},{1,17},{9,25},{17,1},{25,9},{2,18},{10... | collective-permute-start | bytes 589832 | tf_op jit(solution)/shard_map/ppermute | solution.py:696
  35.1 3.0 %collective-permute-start.14 = (bf16[64,1152]{1,0:T(8,128)(2,1)S(1)}, bf16[64,1152]{1,0:T(8,128)(2,1)S(1)}, u32[]{:S(2)}, u32[]{:S(2)}) collective-permute-start(bf16[64,1152]{1,0:T(8,128)(2,1)S(1)} %get-tuple-element.41.refs_5_.refs_8_), channel_id=1, source_target_pairs={{0,2},{2,0},{4,6},{6,4},{1,3},{3,1},{5,7},{7,5},{8,10},{10,8},{12,... | collective-permute-start | bytes 442376 | tf_op jit(solution)/shard_map/ppermute | solution.py:696
  38.1 1.0 %collective-permute-start.15 = (bf16[64,1152]{1,0:T(8,128)(2,1)S(1)}, bf16[64,1152]{1,0:T(8,128)(2,1)S(1)}, u32[]{:S(2)}, u32[]{:S(2)}) collective-permute-start(bf16[64,1152]{1,0:T(8,128)(2,1)S(1)} %get-tuple-element.41.refs_5_.refs_8_), channel_id=1, source_target_pairs={{0,4},{2,6},{4,0},{6,2},{1,5},{3,7},{5,1},{7,3},{8,12},{10,14},{12... | collective-permute-start | bytes 442376 | tf_op jit(solution)/shard_map/ppermute | solution.py:696
  39.1 2.3 %collective-permute-start.9 = (bf16[2,3,16,1024]{3,2,1,0:T(8,128)(2,1)S(1)}, bf16[2,3,16,1024]{3,2,1,0:T(8,128)(2,1)S(1)}, u32[]{:S(2)}, u32[]{:S(2)}) collective-permute-start(bf16[2,3,16,1024]{3,2,1,0:T(8,128)(2,1)S(1)} %get-tuple-element.39), channel_id=1, source_target_pairs={{0,24},{8,16},{16,8},{24,0},{1,25},{9,17},{17,9},{25,1},{2,26},{10... | collective-permute-start | bytes 589832 | tf_op jit(solution)/shard_map/ppermute | solution.py:696
  41.4 3.5 %all-to-all-start.1 = ((bf16[8,16,2048]{2,1,0:T(8,128)(2,1)}), bf16[8,16,2048]{2,1,0:T(8,128)(2,1)S(1)}, u32[]{:S(2)}, u32[]{:S(2)}) async-start(bf16[8,16,2048]{2,1,0:T(8,128)(2,1)} %bitcast.12), calls=%async_computation.1 | async-start | bytes 1048576 | tf_op jit(solution)/shard_map/all_to_all | solution.py:800
  44.9 0.5 collective-permute-start.10
  45.4 1.9 %collective-permute-done.15.refs_10_ = bf16[64,1152]{1,0:T(8,128)(2,1)S(1)} collective-permute-done((bf16[64,1152]{1,0:T(8,128)(2,1)S(1)}, bf16[64,1152]{1,0:T(8,128)(2,1)S(1)}, u32[]{:S(2)}, u32[]{:S(2)}) %collective-permute-start.15) | collective-permute-done | bytes 147488 | tf_op jit(solution)/shard_map/ppermute | solution.py:696
  47.3 0.5 collective-permute-start.18
  47.9 0.1 collective-permute-start.17
  47.9 2.3 %collective-permute-start.16 = (bf16[64,1152]{1,0:T(8,128)(2,1)S(1)}, bf16[64,1152]{1,0:T(8,128)(2,1)S(1)}, u32[]{:S(2)}, u32[]{:S(2)}) collective-permute-start(bf16[64,1152]{1,0:T(8,128)(2,1)S(1)} %get-tuple-element.41.refs_5_.refs_8_), channel_id=1, source_target_pairs={{0,6},{2,4},{4,2},{6,0},{1,7},{3,5},{5,3},{7,1},{8,14},{10,12},{12... | collective-permute-start | bytes 442376 | tf_op jit(solution)/shard_map/ppermute | solution.py:696
  50.3 0.2 collective-permute-start.11
  50.4 0.4 collective-permute-start.12
  50.8 0.2 collective-permute-start.13
  50.9 5.1 %collective-permute-done.16.refs_11_ = bf16[64,1152]{1,0:T(8,128)(2,1)S(1)} collective-permute-done((bf16[64,1152]{1,0:T(8,128)(2,1)S(1)}, bf16[64,1152]{1,0:T(8,128)(2,1)S(1)}, u32[]{:S(2)}, u32[]{:S(2)}) %collective-permute-start.16) | collective-permute-done | bytes 147488 | tf_op jit(solution)/shard_map/ppermute | solution.py:696
  56.1 0.6 copy-done.18
  56.7 0.8 %collective-permute-done.20.refs_15_ = bf16[64,1152]{1,0:T(8,128)(2,1)} collective-permute-done((bf16[64,1152]{1,0:T(8,128)(2,1)S(1)}, bf16[64,1152]{1,0:T(8,128)(2,1)}, u32[]{:S(2)}, u32[]{:S(2)}) %collective-permute-start.20) | collective-permute-done | bytes 147488 | tf_op jit(solution)/shard_map/ppermute | solution.py:696
  57.7 0.7 %copy-done.6 = bf16[8,16,2048]{2,1,0:T(8,128)(2,1)} copy-done((bf16[8,16,2048]{2,1,0:T(8,128)(2,1)}, bf16[8,16,2048]{2,1,0:T(8,128)(2,1)S(1)}, u32[]{:S(2)}) %copy-start.6) | copy-done | bytes 524312
  58.4 0.8 %copy-done.7 = bf16[2,7,16,1024]{3,2,1,0:T(8,128)(2,1)} copy-done((bf16[2,7,16,1024]{3,2,1,0:T(8,128)(2,1)}, bf16[2,7,16,1024]{3,2,1,0:T(8,128)(2,1)S(1)}, u32[]{:S(2)}) %copy-start.7) | copy-done | bytes 458776
  59.1 5.8 %gradients.1 = (bf16[16,4,2048]{2,1,0:T(4,128)(2,1)}, bf16[1024,256]{1,0:T(8,128)(2,1)}, bf16[256,1024]{1,0:T(8,128)(2,1)}) custom-call(bf16[2,7,16,1024]{3,2,1,0:T(8,128)(2,1)} %copy-done.3, bf16[2,3,16,1024]{3,2,1,0:T(8,128)(2,1)} %copy-done.8, bf16[2,3,16,1024]{3,2,1,0:T(8,128)(2,1)} %copy-done.9, bf16[2,3,16,1024]{3,2,1,0:T(8,128)(2,1)} %copy-done.10, ...), custom_call_target="tpu_custom_call" | custom-call | bytes 1048576 | tf_op jit(solution)/shard_map/gradients/pallas_call | solution.py:806
  (57 shorter events, 0.1 us)
Async XLA Ops:
  0.6 17.4 %collective-permute-start = (bf16[4096,256]{1,0:T(8,128)(2,1)}, bf16[4096,256]{1,0:T(8,128)(2,1)}, u32[]{:S(2)}, u32[]{:S(2)}) collective-permute-start(bf16[4096,256]{1,0:T(8,128)(2,1)} %bitcast.9), channel_id=1, source_target_pairs={{0,1},{1,0},{2,3},{3,2},{4,5},{5,4},{6,7},{7,6},{8,9},{9,8},{10,11... | collective-permute-start | bytes 6291464 | tf_op jit(solution)/shard_map/ppermute | solution.py:696
  1.2 23.2 %collective-permute-start.1 = (bf16[256,4096]{1,0:T(8,128)(2,1)}, bf16[256,4096]{1,0:T(8,128)(2,1)}, u32[]{:S(2)}, u32[]{:S(2)}) collective-permute-start(bf16[256,4096]{1,0:T(8,128)(2,1)} %bitcast.16), channel_id=1, source_target_pairs={{0,1},{1,0},{2,3},{3,2},{4,5},{5,4},{6,7},{7,6},{8,9},{9,8},{10,11... | collective-permute-start | bytes 6291464 | tf_op jit(solution)/shard_map/ppermute | solution.py:696
  3.6 20.7 %copy-start = (bf16[1,1,4096,256]{3,2,1,0:T(8,128)(2,1)S(1)}, bf16[1,1,4096,256]{3,2,1,0:T(8,128)(2,1)}, u32[]{:S(2)}) copy-start(bf16[1,1,4096,256]{3,2,1,0:T(8,128)(2,1)} %param.9) | copy-start | bytes 6291460
  3.6 20.7 %all-to-all-start = ((bf16[8,2,16,2048]{3,2,1,0:T(8,128)(2,1)}), bf16[8,2,16,2048]{3,2,1,0:T(8,128)(2,1)S(1)}, u32[]{:S(2)}, u32[]{:S(2)}) async-start(bf16[8,2,16,2048]{3,2,1,0:T(8,128)(2,1)} %pack.1._), calls=%async_computation | async-start | bytes 2097152 | tf_op jit(solution)/shard_map/all_to_all | solution.py:757
  8.9 7.5 %collective-permute-start.2 = (bf16[1,4096]{1,0:T(2,128)(2,1)S(1)}, bf16[1,4096]{1,0:T(2,128)(2,1)S(1)}, u32[]{:S(2)}, u32[]{:S(2)}) collective-permute-start(bf16[1,4096]{1,0:T(2,128)(2,1)S(1)} %bitcast.14), channel_id=1, source_target_pairs={{0,1},{1,0},{2,3},{3,2},{4,5},{5,4},{6,7},{7,6},{8,9},{9,8},{10,11... | collective-permute-start | bytes 24584 | tf_op jit(solution)/shard_map/ppermute | solution.py:696
  11.7 19.8 %collective-permute-start.3 = (bf16[80,1024]{1,0:T(8,128)(2,1)}, bf16[80,1024]{1,0:T(8,128)(2,1)S(1)}, u32[]{:S(2)}, u32[]{:S(2)}) collective-permute-start(bf16[80,1024]{1,0:T(8,128)(2,1)} %get-tuple-element.26), channel_id=1, source_target_pairs={{0,0},{1,4},{2,2},{3,6},{4,1},{5,5},{6,3},{7,7},{8,8},{9,12},{10,1... | collective-permute-start | bytes 491528 | tf_op jit(solution)/shard_map/ppermute | solution.py:760
  13.3 18.2 %collective-permute-start.4 = (bf16[80,1024]{1,0:T(8,128)(2,1)}, bf16[80,1024]{1,0:T(8,128)(2,1)}, u32[]{:S(2)}, u32[]{:S(2)}) collective-permute-start(bf16[80,1024]{1,0:T(8,128)(2,1)} %get-tuple-element.27), channel_id=1, source_target_pairs={{0,1},{1,5},{2,3},{3,7},{4,0},{5,4},{6,2},{7,6},{8,9},{9,13},{10,1... | collective-permute-start | bytes 491528 | tf_op jit(solution)/shard_map/ppermute | solution.py:760
  16.4 15.0 %copy-start.5 = (bf16[1,4096]{1,0:T(2,128)(2,1)}, bf16[1,4096]{1,0:T(2,128)(2,1)S(1)}, u32[]{:S(2)}) copy-start(bf16[1,4096]{1,0:T(2,128)(2,1)S(1)} %collective-permute-done.2.other_gain.refs_21_) | copy-start | bytes 24580
  16.4 15.1 %collective-permute-start.5 = (bf16[80,1024]{1,0:T(8,128)(2,1)}, bf16[80,1024]{1,0:T(8,128)(2,1)}, u32[]{:S(2)}, u32[]{:S(2)}) collective-permute-start(bf16[80,1024]{1,0:T(8,128)(2,1)} %get-tuple-element.28), channel_id=1, source_target_pairs={{0,2},{1,6},{2,0},{3,4},{4,3},{5,7},{6,1},{7,5},{8,10},{9,14},{10,... | collective-permute-start | bytes 491528 | tf_op jit(solution)/shard_map/ppermute | solution.py:760
  18.0 13.5 %collective-permute-start.6 = (bf16[80,1024]{1,0:T(8,128)(2,1)}, bf16[80,1024]{1,0:T(8,128)(2,1)}, u32[]{:S(2)}, u32[]{:S(2)}) collective-permute-start(bf16[80,1024]{1,0:T(8,128)(2,1)} %get-tuple-element.29), channel_id=1, source_target_pairs={{0,3},{1,7},{2,1},{3,5},{4,2},{5,6},{6,0},{7,4},{8,11},{9,15},{10,... | collective-permute-start | bytes 491528 | tf_op jit(solution)/shard_map/ppermute | solution.py:760
  31.5 10.0 %copy-start.2 = (bf16[4,2,16,2048]{3,2,1,0:T(8,128)(2,1)}, bf16[4,2,16,2048]{3,2,1,0:T(8,128)(2,1)S(1)}, u32[]{:S(2)}) copy-start(bf16[4,2,16,2048]{3,2,1,0:T(8,128)(2,1)S(1)} %get-tuple-element.43) | copy-start | bytes 1572868
  31.5 26.1 %copy-start.1 = (bf16[64,1152]{1,0:T(8,128)(2,1)}, bf16[64,1152]{1,0:T(8,128)(2,1)S(1)}, u32[]{:S(2)}) copy-start(bf16[64,1152]{1,0:T(8,128)(2,1)S(1)} %get-tuple-element.41.refs_5_.refs_8_) | copy-start | bytes 442372
  33.7 23.9 %copy-start.3 = (bf16[2,7,16,1024]{3,2,1,0:T(8,128)(2,1)}, bf16[2,7,16,1024]{3,2,1,0:T(8,128)(2,1)S(1)}, u32[]{:S(2)}) copy-start(bf16[2,7,16,1024]{3,2,1,0:T(8,128)(2,1)S(1)} %get-tuple-element.36.refs_0_) | copy-start | bytes 1376260
  33.7 11.2 %collective-permute-start.7 = (bf16[2,3,16,1024]{3,2,1,0:T(8,128)(2,1)S(1)}, bf16[2,3,16,1024]{3,2,1,0:T(8,128)(2,1)S(1)}, u32[]{:S(2)}, u32[]{:S(2)}) collective-permute-start(bf16[2,3,16,1024]{3,2,1,0:T(8,128)(2,1)S(1)} %get-tuple-element.35), channel_id=1, source_target_pairs={{0,8},{8,0},{16,24},{24,16},{1,9},{9,1},{17,25},{25,17},{2,10},{10... | collective-permute-start | bytes 589832 | tf_op jit(solution)/shard_map/ppermute | solution.py:696
  34.3 13.6 %collective-permute-start.8 = (bf16[2,3,16,1024]{3,2,1,0:T(8,128)(2,1)S(1)}, bf16[2,3,16,1024]{3,2,1,0:T(8,128)(2,1)S(1)}, u32[]{:S(2)}, u32[]{:S(2)}) collective-permute-start(bf16[2,3,16,1024]{3,2,1,0:T(8,128)(2,1)S(1)} %get-tuple-element.38), channel_id=1, source_target_pairs={{0,16},{8,24},{16,0},{24,8},{1,17},{9,25},{17,1},{25,9},{2,18},{10... | collective-permute-start | bytes 589832 | tf_op jit(solution)/shard_map/ppermute | solution.py:696
  35.1 10.3 %collective-permute-start.14 = (bf16[64,1152]{1,0:T(8,128)(2,1)S(1)}, bf16[64,1152]{1,0:T(8,128)(2,1)S(1)}, u32[]{:S(2)}, u32[]{:S(2)}) collective-permute-start(bf16[64,1152]{1,0:T(8,128)(2,1)S(1)} %get-tuple-element.41.refs_5_.refs_8_), channel_id=1, source_target_pairs={{0,2},{2,0},{4,6},{6,4},{1,3},{3,1},{5,7},{7,5},{8,10},{10,8},{12,... | collective-permute-start | bytes 442376 | tf_op jit(solution)/shard_map/ppermute | solution.py:696
  38.1 9.2 %collective-permute-start.15 = (bf16[64,1152]{1,0:T(8,128)(2,1)S(1)}, bf16[64,1152]{1,0:T(8,128)(2,1)S(1)}, u32[]{:S(2)}, u32[]{:S(2)}) collective-permute-start(bf16[64,1152]{1,0:T(8,128)(2,1)S(1)} %get-tuple-element.41.refs_5_.refs_8_), channel_id=1, source_target_pairs={{0,4},{2,6},{4,0},{6,2},{1,5},{3,7},{5,1},{7,3},{8,12},{10,14},{12... | collective-permute-start | bytes 442376 | tf_op jit(solution)/shard_map/ppermute | solution.py:696
  39.1 8.8 %collective-permute-start.9 = (bf16[2,3,16,1024]{3,2,1,0:T(8,128)(2,1)S(1)}, bf16[2,3,16,1024]{3,2,1,0:T(8,128)(2,1)S(1)}, u32[]{:S(2)}, u32[]{:S(2)}) collective-permute-start(bf16[2,3,16,1024]{3,2,1,0:T(8,128)(2,1)S(1)} %get-tuple-element.39), channel_id=1, source_target_pairs={{0,24},{8,16},{16,8},{24,0},{1,25},{9,17},{17,9},{25,1},{2,26},{10... | collective-permute-start | bytes 589832 | tf_op jit(solution)/shard_map/ppermute | solution.py:696
  41.4 16.1 %all-to-all-start.1 = ((bf16[8,16,2048]{2,1,0:T(8,128)(2,1)}), bf16[8,16,2048]{2,1,0:T(8,128)(2,1)S(1)}, u32[]{:S(2)}, u32[]{:S(2)}) async-start(bf16[8,16,2048]{2,1,0:T(8,128)(2,1)} %bitcast.12), calls=%async_computation.1 | async-start | bytes 1048576 | tf_op jit(solution)/shard_map/all_to_all | solution.py:800
  44.9 12.7 %copy-start.8 = (bf16[2,3,16,1024]{3,2,1,0:T(8,128)(2,1)}, bf16[2,3,16,1024]{3,2,1,0:T(8,128)(2,1)S(1)}, u32[]{:S(2)}) copy-start(bf16[2,3,16,1024]{3,2,1,0:T(8,128)(2,1)S(1)} %collective-permute-done.7.refs_1_) | copy-start | bytes 589828
  44.9 12.6 %collective-permute-start.10 = (bf16[2,7,16,1024]{3,2,1,0:T(8,128)(2,1)S(1)}, bf16[2,7,16,1024]{3,2,1,0:T(8,128)(2,1)S(1)}, u32[]{:S(2)}, u32[]{:S(2)}) collective-permute-start(bf16[2,7,16,1024]{3,2,1,0:T(8,128)(2,1)S(1)} %get-tuple-element.36.refs_0_), channel_id=1, source_target_pairs={{0,1},{1,0},{2,3},{3,2},{4,5},{5,4},{6,7},{7,6},{8,9},{9,8},{10,11... | collective-permute-start | bytes 1376264 | tf_op jit(solution)/shard_map/ppermute | solution.py:696
  45.4 12.2 %copy-start.14 = (bf16[64,1152]{1,0:T(8,128)(2,1)}, bf16[64,1152]{1,0:T(8,128)(2,1)S(1)}, u32[]{:S(2)}) copy-start(bf16[64,1152]{1,0:T(8,128)(2,1)S(1)} %collective-permute-done.14.refs_9_) | copy-start | bytes 442372
  47.3 10.3 %copy-start.15 = (bf16[64,1152]{1,0:T(8,128)(2,1)}, bf16[64,1152]{1,0:T(8,128)(2,1)S(1)}, u32[]{:S(2)}) copy-start(bf16[64,1152]{1,0:T(8,128)(2,1)S(1)} %collective-permute-done.15.refs_10_) | copy-start | bytes 442372
  47.3 2.9 %collective-permute-start.19 = (bf16[64,1152]{1,0:T(8,128)(2,1)S(1)}, bf16[64,1152]{1,0:T(8,128)(2,1)S(1)}, u32[]{:S(2)}, u32[]{:S(2)}) collective-permute-start(bf16[64,1152]{1,0:T(8,128)(2,1)S(1)} %collective-permute-done.15.refs_10_), channel_id=1, source_target_pairs={{0,1},{1,0},{2,3},{3,2},{4,5},{5,4},{6,7},{7,6},{8,9},{9,8},{10,11... | collective-permute-start | bytes 442376 | tf_op jit(solution)/shard_map/ppermute | solution.py:696
  47.3 3.1 %collective-permute-start.18 = (bf16[64,1152]{1,0:T(8,128)(2,1)S(1)}, bf16[64,1152]{1,0:T(8,128)(2,1)S(1)}, u32[]{:S(2)}, u32[]{:S(2)}) collective-permute-start(bf16[64,1152]{1,0:T(8,128)(2,1)S(1)} %collective-permute-done.14.refs_9_), channel_id=1, source_target_pairs={{0,1},{1,0},{2,3},{3,2},{4,5},{5,4},{6,7},{7,6},{8,9},{9,8},{10,11... | collective-permute-start | bytes 442376 | tf_op jit(solution)/shard_map/ppermute | solution.py:696
  47.9 9.8 %copy-start.9 = (bf16[2,3,16,1024]{3,2,1,0:T(8,128)(2,1)}, bf16[2,3,16,1024]{3,2,1,0:T(8,128)(2,1)S(1)}, u32[]{:S(2)}) copy-start(bf16[2,3,16,1024]{3,2,1,0:T(8,128)(2,1)S(1)} %collective-permute-done.8.refs_2_) | copy-start | bytes 589828
  47.9 2.9 %collective-permute-start.17 = (bf16[64,1152]{1,0:T(8,128)(2,1)S(1)}, bf16[64,1152]{1,0:T(8,128)(2,1)}, u32[]{:S(2)}, u32[]{:S(2)}) collective-permute-start(bf16[64,1152]{1,0:T(8,128)(2,1)S(1)} %get-tuple-element.41.refs_5_.refs_8_), channel_id=1, source_target_pairs={{0,1},{1,0},{2,3},{3,2},{4,5},{5,4},{6,7},{7,6},{8,9},{9,8},{10,11... | collective-permute-start | bytes 442376 | tf_op jit(solution)/shard_map/ppermute | solution.py:696
  47.9 8.1 %collective-permute-start.16 = (bf16[64,1152]{1,0:T(8,128)(2,1)S(1)}, bf16[64,1152]{1,0:T(8,128)(2,1)S(1)}, u32[]{:S(2)}, u32[]{:S(2)}) collective-permute-start(bf16[64,1152]{1,0:T(8,128)(2,1)S(1)} %get-tuple-element.41.refs_5_.refs_8_), channel_id=1, source_target_pairs={{0,6},{2,4},{4,2},{6,0},{1,7},{3,5},{5,3},{7,1},{8,14},{10,12},{12... | collective-permute-start | bytes 442376 | tf_op jit(solution)/shard_map/ppermute | solution.py:696
  50.3 5.8 %collective-permute-start.11 = (bf16[2,3,16,1024]{3,2,1,0:T(8,128)(2,1)S(1)}, bf16[2,3,16,1024]{3,2,1,0:T(8,128)(2,1)S(1)}, u32[]{:S(2)}, u32[]{:S(2)}) collective-permute-start(bf16[2,3,16,1024]{3,2,1,0:T(8,128)(2,1)S(1)} %collective-permute-done.7.refs_1_), channel_id=1, source_target_pairs={{0,1},{1,0},{2,3},{3,2},{4,5},{5,4},{6,7},{7,6},{8,9},{9,8},{10,11... | collective-permute-start | bytes 589832 | tf_op jit(solution)/shard_map/ppermute | solution.py:696
  50.4 5.6 %collective-permute-start.12 = (bf16[2,3,16,1024]{3,2,1,0:T(8,128)(2,1)S(1)}, bf16[2,3,16,1024]{3,2,1,0:T(8,128)(2,1)S(1)}, u32[]{:S(2)}, u32[]{:S(2)}) collective-permute-start(bf16[2,3,16,1024]{3,2,1,0:T(8,128)(2,1)S(1)} %collective-permute-done.8.refs_2_), channel_id=1, source_target_pairs={{0,1},{1,0},{2,3},{3,2},{4,5},{5,4},{6,7},{7,6},{8,9},{9,8},{10,11... | collective-permute-start | bytes 589832 | tf_op jit(solution)/shard_map/ppermute | solution.py:696
  50.8 5.3 %collective-permute-start.13 = (bf16[2,3,16,1024]{3,2,1,0:T(8,128)(2,1)S(1)}, bf16[2,3,16,1024]{3,2,1,0:T(8,128)(2,1)S(1)}, u32[]{:S(2)}, u32[]{:S(2)}) collective-permute-start(bf16[2,3,16,1024]{3,2,1,0:T(8,128)(2,1)S(1)} %collective-permute-done.9.refs_3_), channel_id=1, source_target_pairs={{0,1},{1,0},{2,3},{3,2},{4,5},{5,4},{6,7},{7,6},{8,9},{9,8},{10,11... | collective-permute-start | bytes 589832 | tf_op jit(solution)/shard_map/ppermute | solution.py:696
  56.0 1.5 %collective-permute-start.20 = (bf16[64,1152]{1,0:T(8,128)(2,1)S(1)}, bf16[64,1152]{1,0:T(8,128)(2,1)}, u32[]{:S(2)}, u32[]{:S(2)}) collective-permute-start(bf16[64,1152]{1,0:T(8,128)(2,1)S(1)} %collective-permute-done.16.refs_11_), channel_id=1, source_target_pairs={{0,1},{1,0},{2,3},{3,2},{4,5},{5,4},{6,7},{7,6},{8,9},{9,8},{10,11... | collective-permute-start | bytes 442376 | tf_op jit(solution)/shard_map/ppermute | solution.py:696
  (10 other events, 38.9 us)

commit v14 on v13

--- a/solution.py
+++ b/solution.py
@@ -792,9 +792,8 @@
     mine = [slices[0]] + [across(slices[step], "expert", step) for step in range(1, experts)]
     mine[:2] = lax.optimization_barrier(tuple(mine[:2]))
     theirs = [across(block, "segment", 1) for block in mine]
-    near = [small] + [across(small, "dp", step) for step in range(1, replicas - 1)]
+    near = [small] + [across(small, "dp", step) for step in range(1, replicas)]
     near[:2] = lax.optimization_barrier(tuple(near[:2]))
-    near.append(across(near[0], "dp", replicas - 1))
     smalls = near + [across(piece, "segment", 1) for piece in near]
 
     back = lax.all_to_all(

time: 65.3 us -> 67.8 us (1.038)
  waiting for transfers between devices: 14.2 us -> 17.7 us
  starting transfers between devices: 27.9 us -> 26.7 us
    ppermute x17, waiting for transfers between devices: 7.9 us -> 11.4 us  [across(): return lax.ppermute(block, axis, [(i, i ^ distance) for i in range(size)])]
    ppermute x17, starting transfers between devices: 12.9 us -> 11.7 us  [across(): return lax.ppermute(block, axis, [(i, i ^ distance) for i in range(size)])]
    unnamed x38 -> x40, local copies, waits for them, and re-layouts: 2.13 us -> 2.3 us
  transfers between devices with their start and end apart: 23 -> 23, of which waited for: 4 -> 4; matrix products, arithmetic and copies ran while one was open for 0% -> 0% of each run, Pallas kernels for 18% -> 17%
where the time goes in v14:
time: 67.8 us; the launch traced here: 67.4 us
  starting transfers between devices  26.7 us (39%)
  Pallas kernels  19.7 us (29%)
  waiting for transfers between devices  17.7 us (26%)
  local copies, waits for them, and re-layouts  2.3 us (3%)
  between operations  0.93 us (1%)
    ppermute x17, starting transfers between devices, across(): return lax.ppermute(block, axis, [(i, i ^ distance) for i in range(size)])  11.7 us
    ppermute x17, waiting for transfers between devices, across(): return lax.ppermute(block, axis, [(i, i ^ distance) for i in range(size)])  11.4 us
    pallas_call x1, Pallas kernels, on_device_two_phases(): call(chain_kernel, 'chain', 50, [HBM] * 7, [((experts, 2, rows, part), bf...  7.1 us
    all_to_all x1, waiting for transfers between devices, on_device_two_phases(): lax.all_to_all(send, sections, split_axis=0, concat_axis=0, tiled=True)  6.33 us
    ppermute x4, starting transfers between devices, on_device_two_phases(): lax.ppermute(block, ('dp', 'segment'), slab_route(replicas, turn // 2, tu...  6.29 us
    pallas_call x1, Pallas kernels, on_device_two_phases(): call(functools.partial(gradient_kernel, experts, sources, sizes), 'gradie...  5.83 us
    all_to_all x1, starting transfers between devices, on_device_two_phases(): lax.all_to_all(send, sections, split_axis=0, concat_axis=0, tiled=True)  5.29 us
    all_to_all x1, starting transfers between devices, on_device_two_phases(): lax.all_to_all(out.reshape(groups, rows, part), sections, split_axis=0, c...  3.5 us
  transfers between devices with their start and end apart: 23, of which 4 were waited for; matrix products, arithmetic and copies ran while one was open for 0% of the time, Pallas kernels for 17%

profile of v14, /device:TPU:0, one launch (start us, length us, event | category | flops | bytes accessed | tf_op | source)
XLA Modules:
  0.0 67.4 jit_solution(2587850075919232683)
XLA Ops:
  0.6 0.5 collective-permute-start
  1.2 0.1 collective-permute-start.1
  1.2 2.4 %pack.1._ = bf16[8,2,16,2048]{3,2,1,0:T(8,128)(2,1)} custom-call(s32[16]{0:T(128)} %refs_22_.1, bf16[16,4,2048]{2,1,0:T(4,128)(2,1)} %hidden.3, bf16[16,4,2048]{2,1,0:T(4,128)(2,1)} %cot.3), custom_call_target="tpu_custom_call" | custom-call | bytes 1048576 | tf_op jit(solution)/shard_map/pack/pallas_call | solution.py:727
  3.6 5.3 %all-to-all-start = ((bf16[8,2,16,2048]{3,2,1,0:T(8,128)(2,1)}), bf16[8,2,16,2048]{3,2,1,0:T(8,128)(2,1)S(1)}, u32[]{:S(2)}, u32[]{:S(2)}) async-start(bf16[8,2,16,2048]{3,2,1,0:T(8,128)(2,1)} %pack.1._), calls=%async_computation | async-start | bytes 2097152 | tf_op jit(solution)/shard_map/all_to_all | solution.py:757
  8.9 0.5 collective-permute-start.2
  9.4 2.3 %slabs.1 = (bf16[80,1024]{1,0:T(8,128)(2,1)}, bf16[80,1024]{1,0:T(8,128)(2,1)}, bf16[80,1024]{1,0:T(8,128)(2,1)}, bf16[80,1024]{1,0:T(8,128)(2,1)}) custom-call(s32[16]{0:T(128)} %refs_22_.1, bf16[16,4,2048]{2,1,0:T(4,128)(2,1)} %hidden.3, bf16[16,4,2048]{2,1,0:T(4,128)(2,1)} %cot.3, bf16[8,2,16,2048]{3,2,1,0:T(8,128)(2,1)} %pack.1._), custom_call_target="tpu_custom_call" | custom-call | bytes 1048576 | tf_op jit(solution)/shard_map/slabs/pallas_call | solution.py:741
  11.7 1.6 %collective-permute-start.3 = (bf16[80,1024]{1,0:T(8,128)(2,1)}, bf16[80,1024]{1,0:T(8,128)(2,1)S(1)}, u32[]{:S(2)}, u32[]{:S(2)}) collective-permute-start(bf16[80,1024]{1,0:T(8,128)(2,1)} %get-tuple-element.26), channel_id=1, source_target_pairs={{0,0},{1,4},{2,2},{3,6},{4,1},{5,5},{6,3},{7,7},{8,8},{9,12},{10,1... | collective-permute-start | bytes 491528 | tf_op jit(solution)/shard_map/ppermute | solution.py:760
  13.3 3.1 %collective-permute-start.4 = (bf16[80,1024]{1,0:T(8,128)(2,1)}, bf16[80,1024]{1,0:T(8,128)(2,1)}, u32[]{:S(2)}, u32[]{:S(2)}) collective-permute-start(bf16[80,1024]{1,0:T(8,128)(2,1)} %get-tuple-element.27), channel_id=1, source_target_pairs={{0,1},{1,5},{2,3},{3,7},{4,0},{5,4},{6,2},{7,6},{8,9},{9,13},{10,1... | collective-permute-start | bytes 491528 | tf_op jit(solution)/shard_map/ppermute | solution.py:760
  16.4 1.6 %collective-permute-start.5 = (bf16[80,1024]{1,0:T(8,128)(2,1)}, bf16[80,1024]{1,0:T(8,128)(2,1)}, u32[]{:S(2)}, u32[]{:S(2)}) collective-permute-start(bf16[80,1024]{1,0:T(8,128)(2,1)} %get-tuple-element.28), channel_id=1, source_target_pairs={{0,2},{1,6},{2,0},{3,4},{4,3},{5,7},{6,1},{7,5},{8,10},{9,14},{10,... | collective-permute-start | bytes 491528 | tf_op jit(solution)/shard_map/ppermute | solution.py:760
  18.0 6.3 %all-to-all-done = bf16[8,2,16,2048]{3,2,1,0:T(8,128)(2,1)S(1)} async-done(((bf16[8,2,16,2048]{3,2,1,0:T(8,128)(2,1)}), bf16[8,2,16,2048]{3,2,1,0:T(8,128)(2,1)S(1)}, u32[]{:S(2)}, u32[]{:S(2)}) %all-to-all-start) | async-done | bytes 1048608 | tf_op jit(solution)/shard_map/all_to_all | solution.py:757
  24.4 7.1 %chain.1 = (bf16[4,2,16,2048]{3,2,1,0:T(8,128)(2,1)S(1)}, bf16[64,1152]{1,0:T(8,128)(2,1)S(1)}) custom-call(bf16[4,2,2,16,2048]{4,3,2,1,0:T(8,128)(2,1)S(1)} %bitcast.7, bf16[4096,256]{1,0:T(8,128)(2,1)S(1)} %bitcast.11, bf16[256,4096]{1,0:T(8,128)(2,1)} %bitcast.17, bf16[1,4096]{1,0:T(2,128)(2,1)S(1)} %bitcast.15, ...), custom_call_target="tpu_custom_call" | custom-call | flops 939524096 | bytes 10485760 | tf_op jit(solution)/shard_map/chain/pallas_call | solution.py:763
  31.5 2.2 %repack.1 = (bf16[2,7,16,1024]{3,2,1,0:T(8,128)(2,1)S(1)}, bf16[2,3,16,1024]{3,2,1,0:T(8,128)(2,1)S(1)}, bf16[2,3,16,1024]{3,2,1,0:T(8,128)(2,1)S(1)}, bf16[2,3,16,1024]{3,2,1,0:T(8,128)(2,1)S(1)}) custom-call(bf16[80,1024]{1,0:T(8,128)(2,1)S(1)} %collective-permute-done.3.refs_0_, bf16[80,1024]{1,0:T(8,128)(2,1)} %collective-permute-done.4.refs_1_, ...), custom_call_target="tpu_custom_call" | custom-call | bytes 1048576 | tf_op jit(solution)/shard_map/repack/pallas_call | solution.py:782
  33.7 0.6 collective-permute-start.7
  34.3 3.6 %collective-permute-start.16 = (bf16[64,1152]{1,0:T(8,128)(2,1)S(1)}, bf16[64,1152]{1,0:T(8,128)(2,1)S(1)}, u32[]{:S(2)}, u32[]{:S(2)}) collective-permute-start(bf16[64,1152]{1,0:T(8,128)(2,1)S(1)} %get-tuple-element.41.refs_5_.refs_8_), channel_id=1, source_target_pairs={{0,6},{2,4},{4,2},{6,0},{1,7},{3,5},{5,3},{7,1},{8,14},{10,12},{12... | collective-permute-start | bytes 442376 | tf_op jit(solution)/shard_map/ppermute | solution.py:696
  37.9 0.7 %collective-permute-start.8 = (bf16[2,3,16,1024]{3,2,1,0:T(8,128)(2,1)S(1)}, bf16[2,3,16,1024]{3,2,1,0:T(8,128)(2,1)S(1)}, u32[]{:S(2)}, u32[]{:S(2)}) collective-permute-start(bf16[2,3,16,1024]{3,2,1,0:T(8,128)(2,1)S(1)} %get-tuple-element.38), channel_id=1, source_target_pairs={{0,16},{8,24},{16,0},{24,8},{1,17},{9,25},{17,1},{25,9},{2,18},{10... | collective-permute-start | bytes 589832 | tf_op jit(solution)/shard_map/ppermute | solution.py:696
  38.6 1.0 %collective-permute-start.15 = (bf16[64,1152]{1,0:T(8,128)(2,1)S(1)}, bf16[64,1152]{1,0:T(8,128)(2,1)S(1)}, u32[]{:S(2)}, u32[]{:S(2)}) collective-permute-start(bf16[64,1152]{1,0:T(8,128)(2,1)S(1)} %get-tuple-element.41.refs_5_.refs_8_), channel_id=1, source_target_pairs={{0,4},{2,6},{4,0},{6,2},{1,5},{3,7},{5,1},{7,3},{8,12},{10,14},{12... | collective-permute-start | bytes 442376 | tf_op jit(solution)/shard_map/ppermute | solution.py:696
  39.6 3.5 %all-to-all-start.1 = ((bf16[8,16,2048]{2,1,0:T(8,128)(2,1)}), bf16[8,16,2048]{2,1,0:T(8,128)(2,1)S(1)}, u32[]{:S(2)}, u32[]{:S(2)}) async-start(bf16[8,16,2048]{2,1,0:T(8,128)(2,1)} %bitcast.12), calls=%async_computation.1 | async-start | bytes 1048576 | tf_op jit(solution)/shard_map/all_to_all | solution.py:799
  43.1 0.5 collective-permute-start.10
  43.6 2.6 %collective-permute-start.9 = (bf16[2,3,16,1024]{3,2,1,0:T(8,128)(2,1)S(1)}, bf16[2,3,16,1024]{3,2,1,0:T(8,128)(2,1)S(1)}, u32[]{:S(2)}, u32[]{:S(2)}) collective-permute-start(bf16[2,3,16,1024]{3,2,1,0:T(8,128)(2,1)S(1)} %get-tuple-element.39), channel_id=1, source_target_pairs={{0,24},{8,16},{16,8},{24,0},{1,25},{9,17},{17,9},{25,1},{2,26},{10... | collective-permute-start | bytes 589832 | tf_op jit(solution)/shard_map/ppermute | solution.py:696
  46.2 5.0 %collective-permute-done.15.refs_10_ = bf16[64,1152]{1,0:T(8,128)(2,1)S(1)} collective-permute-done((bf16[64,1152]{1,0:T(8,128)(2,1)S(1)}, bf16[64,1152]{1,0:T(8,128)(2,1)S(1)}, u32[]{:S(2)}, u32[]{:S(2)}) %collective-permute-start.15) | collective-permute-done | bytes 147488 | tf_op jit(solution)/shard_map/ppermute | solution.py:696
  51.2 0.5 collective-permute-start.19
  51.7 0.1 collective-permute-start.17
  51.8 5.2 %collective-permute-done.9.refs_3_ = bf16[2,3,16,1024]{3,2,1,0:T(8,128)(2,1)S(1)} collective-permute-done((bf16[2,3,16,1024]{3,2,1,0:T(8,128)(2,1)S(1)}, bf16[2,3,16,1024]{3,2,1,0:T(8,128)(2,1)S(1)}, u32[]{:S(2)}, u32[]{:S(2)}) %collective-permute-start.9) | collective-permute-done | bytes 196640 | tf_op jit(solution)/shard_map/ppermute | solution.py:696
  57.0 0.5 collective-permute-start.12
  57.5 0.1 collective-permute-start.13
  57.6 0.4 collective-permute-start.18
  58.0 1.2 %collective-permute-done.18.refs_13_ = bf16[64,1152]{1,0:T(8,128)(2,1)S(1)} collective-permute-done((bf16[64,1152]{1,0:T(8,128)(2,1)S(1)}, bf16[64,1152]{1,0:T(8,128)(2,1)S(1)}, u32[]{:S(2)}, u32[]{:S(2)}) %collective-permute-start.18) | collective-permute-done | bytes 147488 | tf_op jit(solution)/shard_map/ppermute | solution.py:696
  59.2 0.7 copy-done.19
  60.0 0.6 copy-done.12
  60.6 0.2 copy-done.6
  60.8 0.8 %copy-done.7 = bf16[2,7,16,1024]{3,2,1,0:T(8,128)(2,1)} copy-done((bf16[2,7,16,1024]{3,2,1,0:T(8,128)(2,1)}, bf16[2,7,16,1024]{3,2,1,0:T(8,128)(2,1)S(1)}, u32[]{:S(2)}) %copy-start.7) | copy-done | bytes 458776
  61.6 5.8 %gradients.1 = (bf16[16,4,2048]{2,1,0:T(4,128)(2,1)}, bf16[1024,256]{1,0:T(8,128)(2,1)}, bf16[256,1024]{1,0:T(8,128)(2,1)}) custom-call(bf16[2,7,16,1024]{3,2,1,0:T(8,128)(2,1)} %copy-done.3, bf16[2,3,16,1024]{3,2,1,0:T(8,128)(2,1)} %copy-done.8, bf16[2,3,16,1024]{3,2,1,0:T(8,128)(2,1)} %copy-done.9, bf16[2,3,16,1024]{3,2,1,0:T(8,128)(2,1)} %copy-done.10, ...), custom_call_target="tpu_custom_call" | custom-call | bytes 1048576 | tf_op jit(solution)/shard_map/gradients/pallas_call | solution.py:805
  (59 shorter events, 0.2 us)
Async XLA Ops:
  0.6 8.3 %copy-start.4 = (bf16[1,1,4096]{2,1,0:T(2,128)(2,1)S(1)}, bf16[1,1,4096]{2,1,0:T(2,128)(2,1)}, u32[]{:S(2)}) copy-start(bf16[1,1,4096]{2,1,0:T(2,128)(2,1)} %param.11) | copy-start | bytes 24580
  0.6 17.4 %collective-permute-start = (bf16[4096,256]{1,0:T(8,128)(2,1)}, bf16[4096,256]{1,0:T(8,128)(2,1)}, u32[]{:S(2)}, u32[]{:S(2)}) collective-permute-start(bf16[4096,256]{1,0:T(8,128)(2,1)} %bitcast.9), channel_id=1, source_target_pairs={{0,1},{1,0},{2,3},{3,2},{4,5},{5,4},{6,7},{7,6},{8,9},{9,8},{10,11... | collective-permute-start | bytes 6291464 | tf_op jit(solution)/shard_map/ppermute | solution.py:696
  1.2 23.2 %collective-permute-start.1 = (bf16[256,4096]{1,0:T(8,128)(2,1)}, bf16[256,4096]{1,0:T(8,128)(2,1)}, u32[]{:S(2)}, u32[]{:S(2)}) collective-permute-start(bf16[256,4096]{1,0:T(8,128)(2,1)} %bitcast.16), channel_id=1, source_target_pairs={{0,1},{1,0},{2,3},{3,2},{4,5},{5,4},{6,7},{7,6},{8,9},{9,8},{10,11... | collective-permute-start | bytes 6291464 | tf_op jit(solution)/shard_map/ppermute | solution.py:696
  3.6 20.7 %copy-start = (bf16[1,1,4096,256]{3,2,1,0:T(8,128)(2,1)S(1)}, bf16[1,1,4096,256]{3,2,1,0:T(8,128)(2,1)}, u32[]{:S(2)}) copy-start(bf16[1,1,4096,256]{3,2,1,0:T(8,128)(2,1)} %param.9) | copy-start | bytes 6291460
  3.6 20.7 %all-to-all-start = ((bf16[8,2,16,2048]{3,2,1,0:T(8,128)(2,1)}), bf16[8,2,16,2048]{3,2,1,0:T(8,128)(2,1)S(1)}, u32[]{:S(2)}, u32[]{:S(2)}) async-start(bf16[8,2,16,2048]{3,2,1,0:T(8,128)(2,1)} %pack.1._), calls=%async_computation | async-start | bytes 2097152 | tf_op jit(solution)/shard_map/all_to_all | solution.py:757
  8.9 7.5 %collective-permute-start.2 = (bf16[1,4096]{1,0:T(2,128)(2,1)S(1)}, bf16[1,4096]{1,0:T(2,128)(2,1)S(1)}, u32[]{:S(2)}, u32[]{:S(2)}) collective-permute-start(bf16[1,4096]{1,0:T(2,128)(2,1)S(1)} %bitcast.14), channel_id=1, source_target_pairs={{0,1},{1,0},{2,3},{3,2},{4,5},{5,4},{6,7},{7,6},{8,9},{9,8},{10,11... | collective-permute-start | bytes 24584 | tf_op jit(solution)/shard_map/ppermute | solution.py:696
  11.7 19.8 %collective-permute-start.3 = (bf16[80,1024]{1,0:T(8,128)(2,1)}, bf16[80,1024]{1,0:T(8,128)(2,1)S(1)}, u32[]{:S(2)}, u32[]{:S(2)}) collective-permute-start(bf16[80,1024]{1,0:T(8,128)(2,1)} %get-tuple-element.26), channel_id=1, source_target_pairs={{0,0},{1,4},{2,2},{3,6},{4,1},{5,5},{6,3},{7,7},{8,8},{9,12},{10,1... | collective-permute-start | bytes 491528 | tf_op jit(solution)/shard_map/ppermute | solution.py:760
  13.3 18.2 %collective-permute-start.4 = (bf16[80,1024]{1,0:T(8,128)(2,1)}, bf16[80,1024]{1,0:T(8,128)(2,1)}, u32[]{:S(2)}, u32[]{:S(2)}) collective-permute-start(bf16[80,1024]{1,0:T(8,128)(2,1)} %get-tuple-element.27), channel_id=1, source_target_pairs={{0,1},{1,5},{2,3},{3,7},{4,0},{5,4},{6,2},{7,6},{8,9},{9,13},{10,1... | collective-permute-start | bytes 491528 | tf_op jit(solution)/shard_map/ppermute | solution.py:760
  16.4 15.0 %copy-start.5 = (bf16[1,4096]{1,0:T(2,128)(2,1)}, bf16[1,4096]{1,0:T(2,128)(2,1)S(1)}, u32[]{:S(2)}) copy-start(bf16[1,4096]{1,0:T(2,128)(2,1)S(1)} %collective-permute-done.2.other_gain.refs_21_) | copy-start | bytes 24580
  16.4 15.1 %collective-permute-start.5 = (bf16[80,1024]{1,0:T(8,128)(2,1)}, bf16[80,1024]{1,0:T(8,128)(2,1)}, u32[]{:S(2)}, u32[]{:S(2)}) collective-permute-start(bf16[80,1024]{1,0:T(8,128)(2,1)} %get-tuple-element.28), channel_id=1, source_target_pairs={{0,2},{1,6},{2,0},{3,4},{4,3},{5,7},{6,1},{7,5},{8,10},{9,14},{10,... | collective-permute-start | bytes 491528 | tf_op jit(solution)/shard_map/ppermute | solution.py:760
  18.0 13.5 %collective-permute-start.6 = (bf16[80,1024]{1,0:T(8,128)(2,1)}, bf16[80,1024]{1,0:T(8,128)(2,1)}, u32[]{:S(2)}, u32[]{:S(2)}) collective-permute-start(bf16[80,1024]{1,0:T(8,128)(2,1)} %get-tuple-element.29), channel_id=1, source_target_pairs={{0,3},{1,7},{2,1},{3,5},{4,2},{5,6},{6,0},{7,4},{8,11},{9,15},{10,... | collective-permute-start | bytes 491528 | tf_op jit(solution)/shard_map/ppermute | solution.py:760
  31.5 28.4 %copy-start.1 = (bf16[64,1152]{1,0:T(8,128)(2,1)}, bf16[64,1152]{1,0:T(8,128)(2,1)S(1)}, u32[]{:S(2)}) copy-start(bf16[64,1152]{1,0:T(8,128)(2,1)S(1)} %get-tuple-element.41.refs_5_.refs_8_) | copy-start | bytes 442372
  33.7 26.2 %copy-start.3 = (bf16[2,7,16,1024]{3,2,1,0:T(8,128)(2,1)}, bf16[2,7,16,1024]{3,2,1,0:T(8,128)(2,1)S(1)}, u32[]{:S(2)}) copy-start(bf16[2,7,16,1024]{3,2,1,0:T(8,128)(2,1)S(1)} %get-tuple-element.36.refs_0_) | copy-start | bytes 1376260
  33.7 9.4 %collective-permute-start.7 = (bf16[2,3,16,1024]{3,2,1,0:T(8,128)(2,1)S(1)}, bf16[2,3,16,1024]{3,2,1,0:T(8,128)(2,1)S(1)}, u32[]{:S(2)}, u32[]{:S(2)}) collective-permute-start(bf16[2,3,16,1024]{3,2,1,0:T(8,128)(2,1)S(1)} %get-tuple-element.35), channel_id=1, source_target_pairs={{0,8},{8,0},{16,24},{24,16},{1,9},{9,1},{17,25},{25,17},{2,10},{10... | collective-permute-start | bytes 589832 | tf_op jit(solution)/shard_map/ppermute | solution.py:696
  34.3 9.3 %collective-permute-start.16 = (bf16[64,1152]{1,0:T(8,128)(2,1)S(1)}, bf16[64,1152]{1,0:T(8,128)(2,1)S(1)}, u32[]{:S(2)}, u32[]{:S(2)}) collective-permute-start(bf16[64,1152]{1,0:T(8,128)(2,1)S(1)} %get-tuple-element.41.refs_5_.refs_8_), channel_id=1, source_target_pairs={{0,6},{2,4},{4,2},{6,0},{1,7},{3,5},{5,3},{7,1},{8,14},{10,12},{12... | collective-permute-start | bytes 442376 | tf_op jit(solution)/shard_map/ppermute | solution.py:696
  37.9 13.8 %collective-permute-start.8 = (bf16[2,3,16,1024]{3,2,1,0:T(8,128)(2,1)S(1)}, bf16[2,3,16,1024]{3,2,1,0:T(8,128)(2,1)S(1)}, u32[]{:S(2)}, u32[]{:S(2)}) collective-permute-start(bf16[2,3,16,1024]{3,2,1,0:T(8,128)(2,1)S(1)} %get-tuple-element.38), channel_id=1, source_target_pairs={{0,16},{8,24},{16,0},{24,8},{1,17},{9,25},{17,1},{25,9},{2,18},{10... | collective-permute-start | bytes 589832 | tf_op jit(solution)/shard_map/ppermute | solution.py:696
  38.6 12.6 %collective-permute-start.15 = (bf16[64,1152]{1,0:T(8,128)(2,1)S(1)}, bf16[64,1152]{1,0:T(8,128)(2,1)S(1)}, u32[]{:S(2)}, u32[]{:S(2)}) collective-permute-start(bf16[64,1152]{1,0:T(8,128)(2,1)S(1)} %get-tuple-element.41.refs_5_.refs_8_), channel_id=1, source_target_pairs={{0,4},{2,6},{4,0},{6,2},{1,5},{3,7},{5,1},{7,3},{8,12},{10,14},{12... | collective-permute-start | bytes 442376 | tf_op jit(solution)/shard_map/ppermute | solution.py:696
  39.6 11.6 %collective-permute-start.14 = (bf16[64,1152]{1,0:T(8,128)(2,1)S(1)}, bf16[64,1152]{1,0:T(8,128)(2,1)S(1)}, u32[]{:S(2)}, u32[]{:S(2)}) collective-permute-start(bf16[64,1152]{1,0:T(8,128)(2,1)S(1)} %get-tuple-element.41.refs_5_.refs_8_), channel_id=1, source_target_pairs={{0,2},{2,0},{4,6},{6,4},{1,3},{3,1},{5,7},{7,5},{8,10},{10,8},{12,... | collective-permute-start | bytes 442376 | tf_op jit(solution)/shard_map/ppermute | solution.py:696
  39.6 20.3 %all-to-all-start.1 = ((bf16[8,16,2048]{2,1,0:T(8,128)(2,1)}), bf16[8,16,2048]{2,1,0:T(8,128)(2,1)S(1)}, u32[]{:S(2)}, u32[]{:S(2)}) async-start(bf16[8,16,2048]{2,1,0:T(8,128)(2,1)} %bitcast.12), calls=%async_computation.1 | async-start | bytes 1048576 | tf_op jit(solution)/shard_map/all_to_all | solution.py:799
  43.1 16.8 %copy-start.8 = (bf16[2,3,16,1024]{3,2,1,0:T(8,128)(2,1)}, bf16[2,3,16,1024]{3,2,1,0:T(8,128)(2,1)S(1)}, u32[]{:S(2)}) copy-start(bf16[2,3,16,1024]{3,2,1,0:T(8,128)(2,1)S(1)} %collective-permute-done.7.refs_1_) | copy-start | bytes 589828
  43.1 16.8 %collective-permute-start.10 = (bf16[2,7,16,1024]{3,2,1,0:T(8,128)(2,1)S(1)}, bf16[2,7,16,1024]{3,2,1,0:T(8,128)(2,1)S(1)}, u32[]{:S(2)}, u32[]{:S(2)}) collective-permute-start(bf16[2,7,16,1024]{3,2,1,0:T(8,128)(2,1)S(1)} %get-tuple-element.36.refs_0_), channel_id=1, source_target_pairs={{0,1},{1,0},{2,3},{3,2},{4,5},{5,4},{6,7},{7,6},{8,9},{9,8},{10,11... | collective-permute-start | bytes 1376264 | tf_op jit(solution)/shard_map/ppermute | solution.py:696
  43.6 16.4 %copy-start.14 = (bf16[64,1152]{1,0:T(8,128)(2,1)}, bf16[64,1152]{1,0:T(8,128)(2,1)S(1)}, u32[]{:S(2)}) copy-start(bf16[64,1152]{1,0:T(8,128)(2,1)S(1)} %collective-permute-done.16.refs_11_) | copy-start | bytes 442372
  43.6 13.4 %collective-permute-start.9 = (bf16[2,3,16,1024]{3,2,1,0:T(8,128)(2,1)S(1)}, bf16[2,3,16,1024]{3,2,1,0:T(8,128)(2,1)S(1)}, u32[]{:S(2)}, u32[]{:S(2)}) collective-permute-start(bf16[2,3,16,1024]{3,2,1,0:T(8,128)(2,1)S(1)} %get-tuple-element.39), channel_id=1, source_target_pairs={{0,24},{8,16},{16,8},{24,0},{1,25},{9,17},{17,9},{25,1},{2,26},{10... | collective-permute-start | bytes 589832 | tf_op jit(solution)/shard_map/ppermute | solution.py:696
  51.2 8.8 %copy-start.15 = (bf16[64,1152]{1,0:T(8,128)(2,1)}, bf16[64,1152]{1,0:T(8,128)(2,1)S(1)}, u32[]{:S(2)}) copy-start(bf16[64,1152]{1,0:T(8,128)(2,1)S(1)} %collective-permute-done.15.refs_10_) | copy-start | bytes 442372
  51.2 5.8 %collective-permute-start.20 = (bf16[64,1152]{1,0:T(8,128)(2,1)S(1)}, bf16[64,1152]{1,0:T(8,128)(2,1)S(1)}, u32[]{:S(2)}, u32[]{:S(2)}) collective-permute-start(bf16[64,1152]{1,0:T(8,128)(2,1)S(1)} %collective-permute-done.16.refs_11_), channel_id=1, source_target_pairs={{0,1},{1,0},{2,3},{3,2},{4,5},{5,4},{6,7},{7,6},{8,9},{9,8},{10,11... | collective-permute-start | bytes 442376 | tf_op jit(solution)/shard_map/ppermute | solution.py:696
  51.2 8.8 %copy-start.16 = (bf16[64,1152]{1,0:T(8,128)(2,1)}, bf16[64,1152]{1,0:T(8,128)(2,1)S(1)}, u32[]{:S(2)}) copy-start(bf16[64,1152]{1,0:T(8,128)(2,1)S(1)} %collective-permute-done.14.refs_9_) | copy-start | bytes 442372
  51.2 6.3 %collective-permute-start.19 = (bf16[64,1152]{1,0:T(8,128)(2,1)S(1)}, bf16[64,1152]{1,0:T(8,128)(2,1)}, u32[]{:S(2)}, u32[]{:S(2)}) collective-permute-start(bf16[64,1152]{1,0:T(8,128)(2,1)S(1)} %collective-permute-done.15.refs_10_), channel_id=1, source_target_pairs={{0,1},{1,0},{2,3},{3,2},{4,5},{5,4},{6,7},{7,6},{8,9},{9,8},{10,11... | collective-permute-start | bytes 442376 | tf_op jit(solution)/shard_map/ppermute | solution.py:696
  51.7 5.9 %collective-permute-start.17 = (bf16[64,1152]{1,0:T(8,128)(2,1)S(1)}, bf16[64,1152]{1,0:T(8,128)(2,1)S(1)}, u32[]{:S(2)}, u32[]{:S(2)}) collective-permute-start(bf16[64,1152]{1,0:T(8,128)(2,1)S(1)} %get-tuple-element.41.refs_5_.refs_8_), channel_id=1, source_target_pairs={{0,1},{1,0},{2,3},{3,2},{4,5},{5,4},{6,7},{7,6},{8,9},{9,8},{10,11... | collective-permute-start | bytes 442376 | tf_op jit(solution)/shard_map/ppermute | solution.py:696
  57.0 2.2 %collective-permute-start.11 = (bf16[2,3,16,1024]{3,2,1,0:T(8,128)(2,1)S(1)}, bf16[2,3,16,1024]{3,2,1,0:T(8,128)(2,1)S(1)}, u32[]{:S(2)}, u32[]{:S(2)}) collective-permute-start(bf16[2,3,16,1024]{3,2,1,0:T(8,128)(2,1)S(1)} %collective-permute-done.7.refs_1_), channel_id=1, source_target_pairs={{0,1},{1,0},{2,3},{3,2},{4,5},{5,4},{6,7},{7,6},{8,9},{9,8},{10,11... | collective-permute-start | bytes 589832 | tf_op jit(solution)/shard_map/ppermute | solution.py:696
  57.0 2.2 %collective-permute-start.12 = (bf16[2,3,16,1024]{3,2,1,0:T(8,128)(2,1)S(1)}, bf16[2,3,16,1024]{3,2,1,0:T(8,128)(2,1)S(1)}, u32[]{:S(2)}, u32[]{:S(2)}) collective-permute-start(bf16[2,3,16,1024]{3,2,1,0:T(8,128)(2,1)S(1)} %collective-permute-done.8.refs_2_), channel_id=1, source_target_pairs={{0,1},{1,0},{2,3},{3,2},{4,5},{5,4},{6,7},{7,6},{8,9},{9,8},{10,11... | collective-permute-start | bytes 589832 | tf_op jit(solution)/shard_map/ppermute | solution.py:696
  57.5 2.4 %collective-permute-start.13 = (bf16[2,3,16,1024]{3,2,1,0:T(8,128)(2,1)S(1)}, bf16[2,3,16,1024]{3,2,1,0:T(8,128)(2,1)S(1)}, u32[]{:S(2)}, u32[]{:S(2)}) collective-permute-start(bf16[2,3,16,1024]{3,2,1,0:T(8,128)(2,1)S(1)} %collective-permute-done.9.refs_3_), channel_id=1, source_target_pairs={{0,1},{1,0},{2,3},{3,2},{4,5},{5,4},{6,7},{7,6},{8,9},{9,8},{10,11... | collective-permute-start | bytes 589832 | tf_op jit(solution)/shard_map/ppermute | solution.py:696
  57.6 1.6 %collective-permute-start.18 = (bf16[64,1152]{1,0:T(8,128)(2,1)S(1)}, bf16[64,1152]{1,0:T(8,128)(2,1)S(1)}, u32[]{:S(2)}, u32[]{:S(2)}) collective-permute-start(bf16[64,1152]{1,0:T(8,128)(2,1)S(1)} %collective-permute-done.14.refs_9_), channel_id=1, source_target_pairs={{0,1},{1,0},{2,3},{3,2},{4,5},{5,4},{6,7},{7,6},{8,9},{9,8},{10,11... | collective-permute-start | bytes 442376 | tf_op jit(solution)/shard_map/ppermute | solution.py:696
  (11 other events, 28.6 us)

commit v15 on v13

--- a/solution.py
+++ b/solution.py
@@ -791,10 +791,12 @@
     small, *slices = lax.optimization_barrier((small, *slices))
     mine = [slices[0]] + [across(slices[step], "expert", step) for step in range(1, experts)]
     mine[:2] = lax.optimization_barrier(tuple(mine[:2]))
-    theirs = [across(block, "segment", 1) for block in mine]
     near = [small] + [across(small, "dp", step) for step in range(1, replicas - 1)]
     near[:2] = lax.optimization_barrier(tuple(near[:2]))
-    near.append(across(near[0], "dp", replicas - 1))
+    last = across(near[0], "dp", replicas - 1)
+    *near, mine[-1] = lax.optimization_barrier((*near, mine[-1]))
+    near.append(last)
+    theirs = [across(block, "segment", 1) for block in mine]
     smalls = near + [across(piece, "segment", 1) for piece in near]
 
     back = lax.all_to_all(

time: 65.3 us -> 63.3 us (0.969)
  starting transfers between devices: 27.9 us -> 26.2 us
    ppermute x17, starting transfers between devices: 12.9 us -> 11.1 us  [across(): return lax.ppermute(block, axis, [(i, i ^ distance) for i in range(size)])]
  transfers between devices with their start and end apart: 23 -> 23, of which waited for: 4 -> 7; matrix products, arithmetic and copies ran while one was open for 0% -> 0% of each run, Pallas kernels for 18% -> 19%
where the time goes in v15:
time: 63.3 us; the launch traced here: 62.9 us
  starting transfers between devices  26.2 us (41%)
  Pallas kernels  19.7 us (31%)
  waiting for transfers between devices  14.6 us (23%)
  local copies, waits for them, and re-layouts  1.52 us (2%)
  between operations  0.91 us (1%)
    ppermute x17, starting transfers between devices, across(): return lax.ppermute(block, axis, [(i, i ^ distance) for i in range(size)])  11.1 us
    ppermute x17, waiting for transfers between devices, across(): return lax.ppermute(block, axis, [(i, i ^ distance) for i in range(size)])  8.27 us
    pallas_call x1, Pallas kernels, on_device_two_phases(): call(chain_kernel, 'chain', 50, [HBM] * 7, [((experts, 2, rows, part), bf...  7.1 us
    all_to_all x1, waiting for transfers between devices, on_device_two_phases(): lax.all_to_all(send, sections, split_axis=0, concat_axis=0, tiled=True)  6.33 us
    ppermute x4, starting transfers between devices, on_device_two_phases(): lax.ppermute(block, ('dp', 'segment'), slab_route(replicas, turn // 2, tu...  6.29 us
    pallas_call x1, Pallas kernels, on_device_two_phases(): call(functools.partial(gradient_kernel, experts, sources, sizes), 'gradie...  5.83 us
    all_to_all x1, starting transfers between devices, on_device_two_phases(): lax.all_to_all(send, sections, split_axis=0, concat_axis=0, tiled=True)  5.29 us
    all_to_all x1, starting transfers between devices, on_device_two_phases(): lax.all_to_all(out.reshape(groups, rows, part), sections, split_axis=0, c...  3.49 us
  transfers between devices with their start and end apart: 23, of which 7 were waited for; matrix products, arithmetic and copies ran while one was open for 0% of the time, Pallas kernels for 19%

profile of v15, /device:TPU:0, one launch (start us, length us, event | category | flops | bytes accessed | tf_op | source)
XLA Modules:
  0.0 62.9 jit_solution(16433328975903097399)
XLA Ops:
  0.6 0.5 collective-permute-start
  1.2 2.4 %pack.1._ = bf16[8,2,16,2048]{3,2,1,0:T(8,128)(2,1)} custom-call(s32[16]{0:T(128)} %refs_22_.1, bf16[16,4,2048]{2,1,0:T(4,128)(2,1)} %hidden.3, bf16[16,4,2048]{2,1,0:T(4,128)(2,1)} %cot.3), custom_call_target="tpu_custom_call" | custom-call | bytes 1048576 | tf_op jit(solution)/shard_map/pack/pallas_call | solution.py:727
  3.6 5.3 %all-to-all-start = ((bf16[8,2,16,2048]{3,2,1,0:T(8,128)(2,1)}), bf16[8,2,16,2048]{3,2,1,0:T(8,128)(2,1)S(1)}, u32[]{:S(2)}, u32[]{:S(2)}) async-start(bf16[8,2,16,2048]{3,2,1,0:T(8,128)(2,1)} %pack.1._), calls=%async_computation | async-start | bytes 2097152 | tf_op jit(solution)/shard_map/all_to_all | solution.py:757
  8.9 0.5 collective-permute-start.2
  9.4 2.3 %slabs.1 = (bf16[80,1024]{1,0:T(8,128)(2,1)}, bf16[80,1024]{1,0:T(8,128)(2,1)}, bf16[80,1024]{1,0:T(8,128)(2,1)}, bf16[80,1024]{1,0:T(8,128)(2,1)}) custom-call(s32[16]{0:T(128)} %refs_22_.1, bf16[16,4,2048]{2,1,0:T(4,128)(2,1)} %hidden.3, bf16[16,4,2048]{2,1,0:T(4,128)(2,1)} %cot.3, bf16[8,2,16,2048]{3,2,1,0:T(8,128)(2,1)} %pack.1._), custom_call_target="tpu_custom_call" | custom-call | bytes 1048576 | tf_op jit(solution)/shard_map/slabs/pallas_call | solution.py:741
  11.7 1.6 %collective-permute-start.3 = (bf16[80,1024]{1,0:T(8,128)(2,1)}, bf16[80,1024]{1,0:T(8,128)(2,1)S(1)}, u32[]{:S(2)}, u32[]{:S(2)}) collective-permute-start(bf16[80,1024]{1,0:T(8,128)(2,1)} %get-tuple-element.30), channel_id=1, source_target_pairs={{0,0},{1,4},{2,2},{3,6},{4,1},{5,5},{6,3},{7,7},{8,8},{9,12},{10,1... | collective-permute-start | bytes 491528 | tf_op jit(solution)/shard_map/ppermute | solution.py:760
  13.3 3.1 %collective-permute-start.4 = (bf16[80,1024]{1,0:T(8,128)(2,1)}, bf16[80,1024]{1,0:T(8,128)(2,1)}, u32[]{:S(2)}, u32[]{:S(2)}) collective-permute-start(bf16[80,1024]{1,0:T(8,128)(2,1)} %get-tuple-element.31), channel_id=1, source_target_pairs={{0,1},{1,5},{2,3},{3,7},{4,0},{5,4},{6,2},{7,6},{8,9},{9,13},{10,1... | collective-permute-start | bytes 491528 | tf_op jit(solution)/shard_map/ppermute | solution.py:760
  16.4 1.6 %collective-permute-start.5 = (bf16[80,1024]{1,0:T(8,128)(2,1)}, bf16[80,1024]{1,0:T(8,128)(2,1)}, u32[]{:S(2)}, u32[]{:S(2)}) collective-permute-start(bf16[80,1024]{1,0:T(8,128)(2,1)} %get-tuple-element.32), channel_id=1, source_target_pairs={{0,2},{1,6},{2,0},{3,4},{4,3},{5,7},{6,1},{7,5},{8,10},{9,14},{10,... | collective-permute-start | bytes 491528 | tf_op jit(solution)/shard_map/ppermute | solution.py:760
  18.0 6.3 %all-to-all-done = bf16[8,2,16,2048]{3,2,1,0:T(8,128)(2,1)S(1)} async-done(((bf16[8,2,16,2048]{3,2,1,0:T(8,128)(2,1)}), bf16[8,2,16,2048]{3,2,1,0:T(8,128)(2,1)S(1)}, u32[]{:S(2)}, u32[]{:S(2)}) %all-to-all-start) | async-done | bytes 1048608 | tf_op jit(solution)/shard_map/all_to_all | solution.py:757
  24.3 7.1 %chain.1 = (bf16[4,2,16,2048]{3,2,1,0:T(8,128)(2,1)S(1)}, bf16[64,1152]{1,0:T(8,128)(2,1)S(1)}) custom-call(bf16[4,2,2,16,2048]{4,3,2,1,0:T(8,128)(2,1)S(1)} %bitcast.7, bf16[4096,256]{1,0:T(8,128)(2,1)S(1)} %bitcast.11, bf16[256,4096]{1,0:T(8,128)(2,1)} %bitcast.17, bf16[1,4096]{1,0:T(2,128)(2,1)S(1)} %bitcast.15, ...), custom_call_target="tpu_custom_call" | custom-call | flops 939524096 | bytes 10485760 | tf_op jit(solution)/shard_map/chain/pallas_call | solution.py:763
  31.5 2.2 %repack.1 = (bf16[2,7,16,1024]{3,2,1,0:T(8,128)(2,1)S(1)}, bf16[2,3,16,1024]{3,2,1,0:T(8,128)(2,1)S(1)}, bf16[2,3,16,1024]{3,2,1,0:T(8,128)(2,1)S(1)}, bf16[2,3,16,1024]{3,2,1,0:T(8,128)(2,1)S(1)}) custom-call(bf16[80,1024]{1,0:T(8,128)(2,1)S(1)} %collective-permute-done.3.refs_0_, bf16[80,1024]{1,0:T(8,128)(2,1)} %collective-permute-done.4.refs_1_, ...), custom_call_target="tpu_custom_call" | custom-call | bytes 1048576 | tf_op jit(solution)/shard_map/repack/pallas_call | solution.py:782
  33.7 0.6 collective-permute-start.7
  34.3 1.5 %collective-permute-start.11 = (bf16[2,3,16,1024]{3,2,1,0:T(8,128)(2,1)S(1)}, bf16[2,3,16,1024]{3,2,1,0:T(8,128)(2,1)S(1)}, u32[]{:S(2)}, u32[]{:S(2)}) collective-permute-start(bf16[2,3,16,1024]{3,2,1,0:T(8,128)(2,1)S(1)} %get-tuple-element.46), channel_id=1, source_target_pairs={{0,24},{8,16},{16,8},{24,0},{1,25},{9,17},{17,9},{25,1},{2,26},{10... | collective-permute-start | bytes 589832 | tf_op jit(solution)/shard_map/ppermute | solution.py:696
  35.8 2.3 %collective-permute-start.9 = (bf16[64,1152]{1,0:T(8,128)(2,1)S(1)}, bf16[64,1152]{1,0:T(8,128)(2,1)S(1)}, u32[]{:S(2)}, u32[]{:S(2)}) collective-permute-start(bf16[64,1152]{1,0:T(8,128)(2,1)S(1)} %get-tuple-element.48.refs_5_.refs_8_), channel_id=1, source_target_pairs={{0,2},{2,0},{4,6},{6,4},{1,3},{3,1},{5,7},{7,5},{8,10},{10,8},{12,... | collective-permute-start | bytes 442376 | tf_op jit(solution)/shard_map/ppermute | solution.py:696
  38.1 1.8 %collective-permute-start.10 = (bf16[64,1152]{1,0:T(8,128)(2,1)S(1)}, bf16[64,1152]{1,0:T(8,128)(2,1)S(1)}, u32[]{:S(2)}, u32[]{:S(2)}) collective-permute-start(bf16[64,1152]{1,0:T(8,128)(2,1)S(1)} %get-tuple-element.48.refs_5_.refs_8_), channel_id=1, source_target_pairs={{0,4},{2,6},{4,0},{6,2},{1,5},{3,7},{5,1},{7,3},{8,12},{10,14},{12... | collective-permute-start | bytes 442376 | tf_op jit(solution)/shard_map/ppermute | solution.py:696
  39.9 1.5 %collective-permute-start.8 = (bf16[2,3,16,1024]{3,2,1,0:T(8,128)(2,1)S(1)}, bf16[2,3,16,1024]{3,2,1,0:T(8,128)(2,1)S(1)}, u32[]{:S(2)}, u32[]{:S(2)}) collective-permute-start(bf16[2,3,16,1024]{3,2,1,0:T(8,128)(2,1)S(1)} %get-tuple-element.42), channel_id=1, source_target_pairs={{0,16},{8,24},{16,0},{24,8},{1,17},{9,25},{17,1},{25,9},{2,18},{10... | collective-permute-start | bytes 589832 | tf_op jit(solution)/shard_map/ppermute | solution.py:696
  41.4 3.5 %all-to-all-start.1 = ((bf16[8,16,2048]{2,1,0:T(8,128)(2,1)}), bf16[8,16,2048]{2,1,0:T(8,128)(2,1)S(1)}, u32[]{:S(2)}, u32[]{:S(2)}) async-start(bf16[8,16,2048]{2,1,0:T(8,128)(2,1)} %bitcast.12), calls=%async_computation.1 | async-start | bytes 1048576 | tf_op jit(solution)/shard_map/all_to_all | solution.py:802
  44.9 0.5 collective-permute-start.12
  45.4 0.2 collective-permute-start.16
  45.7 0.5 collective-permute-start.18
  46.2 1.9 %collective-permute-done.8.refs_2_ = bf16[2,3,16,1024]{3,2,1,0:T(8,128)(2,1)S(1)} collective-permute-done((bf16[2,3,16,1024]{3,2,1,0:T(8,128)(2,1)S(1)}, bf16[2,3,16,1024]{3,2,1,0:T(8,128)(2,1)S(1)}, u32[]{:S(2)}, u32[]{:S(2)}) %collective-permute-start.8) | collective-permute-done | bytes 196640 | tf_op jit(solution)/shard_map/ppermute | solution.py:696
  48.1 5.1 %collective-permute-done.16.refs_11_ = bf16[64,1152]{1,0:T(8,128)(2,1)S(1)} collective-permute-done((bf16[64,1152]{1,0:T(8,128)(2,1)S(1)}, bf16[64,1152]{1,0:T(8,128)(2,1)S(1)}, u32[]{:S(2)}, u32[]{:S(2)}) %collective-permute-start.16) | collective-permute-done | bytes 147488 | tf_op jit(solution)/shard_map/ppermute | solution.py:696
  53.2 0.5 collective-permute-start.14
  53.8 0.4 collective-permute-start.20
  54.2 0.4 collective-permute-done.13.refs_5_
  54.6 0.3 collective-permute-done.14.refs_6_
  54.9 0.3 collective-permute-done.15.refs_7_
  55.2 0.3 collective-permute-done.20.refs_15_
  55.6 0.2 copy-done.13
  55.9 0.5 copy-done.6
  56.3 0.8 %copy-done.7 = bf16[2,7,16,1024]{3,2,1,0:T(8,128)(2,1)} copy-done((bf16[2,7,16,1024]{3,2,1,0:T(8,128)(2,1)}, bf16[2,7,16,1024]{3,2,1,0:T(8,128)(2,1)S(1)}, u32[]{:S(2)}) %copy-start.7) | copy-done | bytes 458776
  57.1 5.8 %gradients.1 = (bf16[16,4,2048]{2,1,0:T(4,128)(2,1)}, bf16[1024,256]{1,0:T(8,128)(2,1)}, bf16[256,1024]{1,0:T(8,128)(2,1)}) custom-call(bf16[2,7,16,1024]{3,2,1,0:T(8,128)(2,1)} %copy-done.3, bf16[2,3,16,1024]{3,2,1,0:T(8,128)(2,1)} %copy-done.8, bf16[2,3,16,1024]{3,2,1,0:T(8,128)(2,1)} %copy-done.10, bf16[2,3,16,1024]{3,2,1,0:T(8,128)(2,1)} %copy-done.9, ...), custom_call_target="tpu_custom_call" | custom-call | bytes 1048576 | tf_op jit(solution)/shard_map/gradients/pallas_call | solution.py:808
  (57 shorter events, 0.4 us)
Async XLA Ops:
  0.6 17.4 %collective-permute-start = (bf16[4096,256]{1,0:T(8,128)(2,1)}, bf16[4096,256]{1,0:T(8,128)(2,1)}, u32[]{:S(2)}, u32[]{:S(2)}) collective-permute-start(bf16[4096,256]{1,0:T(8,128)(2,1)} %bitcast.9), channel_id=1, source_target_pairs={{0,1},{1,0},{2,3},{3,2},{4,5},{5,4},{6,7},{7,6},{8,9},{9,8},{10,11... | collective-permute-start | bytes 6291464 | tf_op jit(solution)/shard_map/ppermute | solution.py:696
  1.2 23.2 %collective-permute-start.1 = (bf16[256,4096]{1,0:T(8,128)(2,1)}, bf16[256,4096]{1,0:T(8,128)(2,1)}, u32[]{:S(2)}, u32[]{:S(2)}) collective-permute-start(bf16[256,4096]{1,0:T(8,128)(2,1)} %bitcast.16), channel_id=1, source_target_pairs={{0,1},{1,0},{2,3},{3,2},{4,5},{5,4},{6,7},{7,6},{8,9},{9,8},{10,11... | collective-permute-start | bytes 6291464 | tf_op jit(solution)/shard_map/ppermute | solution.py:696
  3.6 20.7 %copy-start = (bf16[1,1,4096,256]{3,2,1,0:T(8,128)(2,1)S(1)}, bf16[1,1,4096,256]{3,2,1,0:T(8,128)(2,1)}, u32[]{:S(2)}) copy-start(bf16[1,1,4096,256]{3,2,1,0:T(8,128)(2,1)} %param.9) | copy-start | bytes 6291460
  3.6 20.7 %all-to-all-start = ((bf16[8,2,16,2048]{3,2,1,0:T(8,128)(2,1)}), bf16[8,2,16,2048]{3,2,1,0:T(8,128)(2,1)S(1)}, u32[]{:S(2)}, u32[]{:S(2)}) async-start(bf16[8,2,16,2048]{3,2,1,0:T(8,128)(2,1)} %pack.1._), calls=%async_computation | async-start | bytes 2097152 | tf_op jit(solution)/shard_map/all_to_all | solution.py:757
  8.9 7.5 %collective-permute-start.2 = (bf16[1,4096]{1,0:T(2,128)(2,1)S(1)}, bf16[1,4096]{1,0:T(2,128)(2,1)S(1)}, u32[]{:S(2)}, u32[]{:S(2)}) collective-permute-start(bf16[1,4096]{1,0:T(2,128)(2,1)S(1)} %bitcast.14), channel_id=1, source_target_pairs={{0,1},{1,0},{2,3},{3,2},{4,5},{5,4},{6,7},{7,6},{8,9},{9,8},{10,11... | collective-permute-start | bytes 24584 | tf_op jit(solution)/shard_map/ppermute | solution.py:696
  11.7 19.8 %collective-permute-start.3 = (bf16[80,1024]{1,0:T(8,128)(2,1)}, bf16[80,1024]{1,0:T(8,128)(2,1)S(1)}, u32[]{:S(2)}, u32[]{:S(2)}) collective-permute-start(bf16[80,1024]{1,0:T(8,128)(2,1)} %get-tuple-element.30), channel_id=1, source_target_pairs={{0,0},{1,4},{2,2},{3,6},{4,1},{5,5},{6,3},{7,7},{8,8},{9,12},{10,1... | collective-permute-start | bytes 491528 | tf_op jit(solution)/shard_map/ppermute | solution.py:760
  13.3 18.2 %collective-permute-start.4 = (bf16[80,1024]{1,0:T(8,128)(2,1)}, bf16[80,1024]{1,0:T(8,128)(2,1)}, u32[]{:S(2)}, u32[]{:S(2)}) collective-permute-start(bf16[80,1024]{1,0:T(8,128)(2,1)} %get-tuple-element.31), channel_id=1, source_target_pairs={{0,1},{1,5},{2,3},{3,7},{4,0},{5,4},{6,2},{7,6},{8,9},{9,13},{10,1... | collective-permute-start | bytes 491528 | tf_op jit(solution)/shard_map/ppermute | solution.py:760
  16.4 15.0 %copy-start.5 = (bf16[1,4096]{1,0:T(2,128)(2,1)}, bf16[1,4096]{1,0:T(2,128)(2,1)S(1)}, u32[]{:S(2)}) copy-start(bf16[1,4096]{1,0:T(2,128)(2,1)S(1)} %collective-permute-done.2.other_gain.refs_21_) | copy-start | bytes 24580
  16.4 15.1 %collective-permute-start.5 = (bf16[80,1024]{1,0:T(8,128)(2,1)}, bf16[80,1024]{1,0:T(8,128)(2,1)}, u32[]{:S(2)}, u32[]{:S(2)}) collective-permute-start(bf16[80,1024]{1,0:T(8,128)(2,1)} %get-tuple-element.32), channel_id=1, source_target_pairs={{0,2},{1,6},{2,0},{3,4},{4,3},{5,7},{6,1},{7,5},{8,10},{9,14},{10,... | collective-permute-start | bytes 491528 | tf_op jit(solution)/shard_map/ppermute | solution.py:760
  18.0 13.5 %collective-permute-start.6 = (bf16[80,1024]{1,0:T(8,128)(2,1)}, bf16[80,1024]{1,0:T(8,128)(2,1)}, u32[]{:S(2)}, u32[]{:S(2)}) collective-permute-start(bf16[80,1024]{1,0:T(8,128)(2,1)} %get-tuple-element.33), channel_id=1, source_target_pairs={{0,3},{1,7},{2,1},{3,5},{4,2},{5,6},{6,0},{7,4},{8,11},{9,15},{10,... | collective-permute-start | bytes 491528 | tf_op jit(solution)/shard_map/ppermute | solution.py:760
  31.5 10.0 %copy-start.2 = (bf16[4,2,16,2048]{3,2,1,0:T(8,128)(2,1)}, bf16[4,2,16,2048]{3,2,1,0:T(8,128)(2,1)S(1)}, u32[]{:S(2)}) copy-start(bf16[4,2,16,2048]{3,2,1,0:T(8,128)(2,1)S(1)} %get-tuple-element.51) | copy-start | bytes 1572868
  31.5 24.1 %copy-start.1 = (bf16[64,1152]{1,0:T(8,128)(2,1)}, bf16[64,1152]{1,0:T(8,128)(2,1)S(1)}, u32[]{:S(2)}) copy-start(bf16[64,1152]{1,0:T(8,128)(2,1)S(1)} %get-tuple-element.48.refs_5_.refs_8_) | copy-start | bytes 442372
  33.7 21.9 %copy-start.3 = (bf16[2,7,16,1024]{3,2,1,0:T(8,128)(2,1)}, bf16[2,7,16,1024]{3,2,1,0:T(8,128)(2,1)S(1)}, u32[]{:S(2)}) copy-start(bf16[2,7,16,1024]{3,2,1,0:T(8,128)(2,1)S(1)} %get-tuple-element.40.refs_0_) | copy-start | bytes 1376260
  33.7 11.2 %collective-permute-start.7 = (bf16[2,3,16,1024]{3,2,1,0:T(8,128)(2,1)S(1)}, bf16[2,3,16,1024]{3,2,1,0:T(8,128)(2,1)S(1)}, u32[]{:S(2)}, u32[]{:S(2)}) collective-permute-start(bf16[2,3,16,1024]{3,2,1,0:T(8,128)(2,1)S(1)} %get-tuple-element.39), channel_id=1, source_target_pairs={{0,8},{8,0},{16,24},{24,16},{1,9},{9,1},{17,25},{25,17},{2,10},{10... | collective-permute-start | bytes 589832 | tf_op jit(solution)/shard_map/ppermute | solution.py:696
  34.3 11.4 %collective-permute-start.11 = (bf16[2,3,16,1024]{3,2,1,0:T(8,128)(2,1)S(1)}, bf16[2,3,16,1024]{3,2,1,0:T(8,128)(2,1)S(1)}, u32[]{:S(2)}, u32[]{:S(2)}) collective-permute-start(bf16[2,3,16,1024]{3,2,1,0:T(8,128)(2,1)S(1)} %get-tuple-element.46), channel_id=1, source_target_pairs={{0,24},{8,16},{16,8},{24,0},{1,25},{9,17},{17,9},{25,1},{2,26},{10... | collective-permute-start | bytes 589832 | tf_op jit(solution)/shard_map/ppermute | solution.py:696
  35.8 9.6 %collective-permute-start.9 = (bf16[64,1152]{1,0:T(8,128)(2,1)S(1)}, bf16[64,1152]{1,0:T(8,128)(2,1)S(1)}, u32[]{:S(2)}, u32[]{:S(2)}) collective-permute-start(bf16[64,1152]{1,0:T(8,128)(2,1)S(1)} %get-tuple-element.48.refs_5_.refs_8_), channel_id=1, source_target_pairs={{0,2},{2,0},{4,6},{6,4},{1,3},{3,1},{5,7},{7,5},{8,10},{10,8},{12,... | collective-permute-start | bytes 442376 | tf_op jit(solution)/shard_map/ppermute | solution.py:696
  38.1 7.5 %collective-permute-start.10 = (bf16[64,1152]{1,0:T(8,128)(2,1)S(1)}, bf16[64,1152]{1,0:T(8,128)(2,1)S(1)}, u32[]{:S(2)}, u32[]{:S(2)}) collective-permute-start(bf16[64,1152]{1,0:T(8,128)(2,1)S(1)} %get-tuple-element.48.refs_5_.refs_8_), channel_id=1, source_target_pairs={{0,4},{2,6},{4,0},{6,2},{1,5},{3,7},{5,1},{7,3},{8,12},{10,14},{12... | collective-permute-start | bytes 442376 | tf_op jit(solution)/shard_map/ppermute | solution.py:696
  39.9 8.2 %collective-permute-start.8 = (bf16[2,3,16,1024]{3,2,1,0:T(8,128)(2,1)S(1)}, bf16[2,3,16,1024]{3,2,1,0:T(8,128)(2,1)S(1)}, u32[]{:S(2)}, u32[]{:S(2)}) collective-permute-start(bf16[2,3,16,1024]{3,2,1,0:T(8,128)(2,1)S(1)} %get-tuple-element.42), channel_id=1, source_target_pairs={{0,16},{8,24},{16,0},{24,8},{1,17},{9,25},{17,1},{25,9},{2,18},{10... | collective-permute-start | bytes 589832 | tf_op jit(solution)/shard_map/ppermute | solution.py:696
  41.4 14.1 %all-to-all-start.1 = ((bf16[8,16,2048]{2,1,0:T(8,128)(2,1)}), bf16[8,16,2048]{2,1,0:T(8,128)(2,1)S(1)}, u32[]{:S(2)}, u32[]{:S(2)}) async-start(bf16[8,16,2048]{2,1,0:T(8,128)(2,1)} %bitcast.12), calls=%async_computation.1 | async-start | bytes 1048576 | tf_op jit(solution)/shard_map/all_to_all | solution.py:802
  44.9 10.6 %copy-start.8 = (bf16[2,3,16,1024]{3,2,1,0:T(8,128)(2,1)}, bf16[2,3,16,1024]{3,2,1,0:T(8,128)(2,1)S(1)}, u32[]{:S(2)}) copy-start(bf16[2,3,16,1024]{3,2,1,0:T(8,128)(2,1)S(1)} %collective-permute-done.7.refs_1_) | copy-start | bytes 589828
  44.9 10.6 %collective-permute-start.12 = (bf16[2,7,16,1024]{3,2,1,0:T(8,128)(2,1)S(1)}, bf16[2,7,16,1024]{3,2,1,0:T(8,128)(2,1)S(1)}, u32[]{:S(2)}, u32[]{:S(2)}) collective-permute-start(bf16[2,7,16,1024]{3,2,1,0:T(8,128)(2,1)S(1)} %get-tuple-element.40.refs_0_), channel_id=1, source_target_pairs={{0,1},{1,0},{2,3},{3,2},{4,5},{5,4},{6,7},{7,6},{8,9},{9,8},{10,11... | collective-permute-start | bytes 1376264 | tf_op jit(solution)/shard_map/ppermute | solution.py:696
  45.4 10.2 %copy-start.14 = (bf16[64,1152]{1,0:T(8,128)(2,1)}, bf16[64,1152]{1,0:T(8,128)(2,1)S(1)}, u32[]{:S(2)}) copy-start(bf16[64,1152]{1,0:T(8,128)(2,1)S(1)} %collective-permute-done.9.refs_9_) | copy-start | bytes 442372
  45.4 7.8 %collective-permute-start.16 = (bf16[64,1152]{1,0:T(8,128)(2,1)S(1)}, bf16[64,1152]{1,0:T(8,128)(2,1)S(1)}, u32[]{:S(2)}, u32[]{:S(2)}) collective-permute-start(bf16[64,1152]{1,0:T(8,128)(2,1)S(1)} %get-tuple-element.48.refs_5_.refs_8_), channel_id=1, source_target_pairs={{0,6},{2,4},{4,2},{6,0},{1,7},{3,5},{5,3},{7,1},{8,14},{10,12},{12... | collective-permute-start | bytes 442376 | tf_op jit(solution)/shard_map/ppermute | solution.py:696
  45.6 9.9 %copy-start.15 = (bf16[64,1152]{1,0:T(8,128)(2,1)}, bf16[64,1152]{1,0:T(8,128)(2,1)S(1)}, u32[]{:S(2)}) copy-start(bf16[64,1152]{1,0:T(8,128)(2,1)S(1)} %collective-permute-done.10.refs_10_) | copy-start | bytes 442372
  45.6 9.9 %copy-start.9 = (bf16[2,3,16,1024]{3,2,1,0:T(8,128)(2,1)}, bf16[2,3,16,1024]{3,2,1,0:T(8,128)(2,1)S(1)}, u32[]{:S(2)}) copy-start(bf16[2,3,16,1024]{3,2,1,0:T(8,128)(2,1)S(1)} %collective-permute-done.11.refs_3_) | copy-start | bytes 589828
  45.6 7.5 %collective-permute-start.17 = (bf16[64,1152]{1,0:T(8,128)(2,1)S(1)}, bf16[64,1152]{1,0:T(8,128)(2,1)S(1)}, u32[]{:S(2)}, u32[]{:S(2)}) collective-permute-start(bf16[64,1152]{1,0:T(8,128)(2,1)S(1)} %get-tuple-element.48.refs_5_.refs_8_), channel_id=1, source_target_pairs={{0,1},{1,0},{2,3},{3,2},{4,5},{5,4},{6,7},{7,6},{8,9},{9,8},{10,11... | collective-permute-start | bytes 442376 | tf_op jit(solution)/shard_map/ppermute | solution.py:696
  45.7 8.0 %collective-permute-start.18 = (bf16[64,1152]{1,0:T(8,128)(2,1)S(1)}, bf16[64,1152]{1,0:T(8,128)(2,1)}, u32[]{:S(2)}, u32[]{:S(2)}) collective-permute-start(bf16[64,1152]{1,0:T(8,128)(2,1)S(1)} %collective-permute-done.9.refs_9_), channel_id=1, source_target_pairs={{0,1},{1,0},{2,3},{3,2},{4,5},{5,4},{6,7},{7,6},{8,9},{9,8},{10,11... | collective-permute-start | bytes 442376 | tf_op jit(solution)/shard_map/ppermute | solution.py:696
  48.1 5.7 %collective-permute-start.19 = (bf16[64,1152]{1,0:T(8,128)(2,1)S(1)}, bf16[64,1152]{1,0:T(8,128)(2,1)S(1)}, u32[]{:S(2)}, u32[]{:S(2)}) collective-permute-start(bf16[64,1152]{1,0:T(8,128)(2,1)S(1)} %collective-permute-done.10.refs_10_), channel_id=1, source_target_pairs={{0,1},{1,0},{2,3},{3,2},{4,5},{5,4},{6,7},{7,6},{8,9},{9,8},{10,11... | collective-permute-start | bytes 442376 | tf_op jit(solution)/shard_map/ppermute | solution.py:696
  53.2 1.4 %collective-permute-start.13 = (bf16[2,3,16,1024]{3,2,1,0:T(8,128)(2,1)S(1)}, bf16[2,3,16,1024]{3,2,1,0:T(8,128)(2,1)S(1)}, u32[]{:S(2)}, u32[]{:S(2)}) collective-permute-start(bf16[2,3,16,1024]{3,2,1,0:T(8,128)(2,1)S(1)} %collective-permute-done.7.refs_1_), channel_id=1, source_target_pairs={{0,1},{1,0},{2,3},{3,2},{4,5},{5,4},{6,7},{7,6},{8,9},{9,8},{10,11... | collective-permute-start | bytes 589832 | tf_op jit(solution)/shard_map/ppermute | solution.py:696
  53.2 1.7 %collective-permute-start.14 = (bf16[2,3,16,1024]{3,2,1,0:T(8,128)(2,1)S(1)}, bf16[2,3,16,1024]{3,2,1,0:T(8,128)(2,1)S(1)}, u32[]{:S(2)}, u32[]{:S(2)}) collective-permute-start(bf16[2,3,16,1024]{3,2,1,0:T(8,128)(2,1)S(1)} %collective-permute-done.8.refs_2_), channel_id=1, source_target_pairs={{0,1},{1,0},{2,3},{3,2},{4,5},{5,4},{6,7},{7,6},{8,9},{9,8},{10,11... | collective-permute-start | bytes 589832 | tf_op jit(solution)/shard_map/ppermute | solution.py:696
  53.7 1.5 %collective-permute-start.15 = (bf16[2,3,16,1024]{3,2,1,0:T(8,128)(2,1)S(1)}, bf16[2,3,16,1024]{3,2,1,0:T(8,128)(2,1)S(1)}, u32[]{:S(2)}, u32[]{:S(2)}) collective-permute-start(bf16[2,3,16,1024]{3,2,1,0:T(8,128)(2,1)S(1)} %collective-permute-done.11.refs_3_), channel_id=1, source_target_pairs={{0,1},{1,0},{2,3},{3,2},{4,5},{5,4},{6,7},{7,6},{8,9},{9,8},{10,11... | collective-permute-start | bytes 589832 | tf_op jit(solution)/shard_map/ppermute | solution.py:696
  53.8 1.7 %collective-permute-start.20 = (bf16[64,1152]{1,0:T(8,128)(2,1)S(1)}, bf16[64,1152]{1,0:T(8,128)(2,1)}, u32[]{:S(2)}, u32[]{:S(2)}) collective-permute-start(bf16[64,1152]{1,0:T(8,128)(2,1)S(1)} %collective-permute-done.16.refs_11_), channel_id=1, source_target_pairs={{0,1},{1,0},{2,3},{3,2},{4,5},{5,4},{6,7},{7,6},{8,9},{9,8},{10,11... | collective-permute-start | bytes 442376 | tf_op jit(solution)/shard_map/ppermute | solution.py:696
  (10 other events, 26.0 us)

commit v16 on v14

--- a/solution.py
+++ b/solution.py
@@ -791,9 +791,12 @@
     small, *slices = lax.optimization_barrier((small, *slices))
     mine = [slices[0]] + [across(slices[step], "expert", step) for step in range(1, experts)]
     mine[:2] = lax.optimization_barrier(tuple(mine[:2]))
+    far = [across(small, "dp", step) for step in range(2, replicas)]
+    small, out, mine[1] = lax.optimization_barrier((small, out, mine[1]))
+    beside = across(small, "dp", 1)
     theirs = [across(block, "segment", 1) for block in mine]
-    near = [small] + [across(small, "dp", step) for step in range(1, replicas)]
-    near[:2] = lax.optimization_barrier(tuple(near[:2]))
+    small, *far, theirs[-1] = lax.optimization_barrier((small, *far, theirs[-1]))
+    near = [small, beside, *far]
     smalls = near + [across(piece, "segment", 1) for piece in near]
 
     back = lax.all_to_all(

time: 67.8 us -> 71.4 us (1.053)
  starting transfers between devices: 26.7 us -> 28.4 us
  waiting for transfers between devices: 17.7 us -> 19.4 us
    ppermute x17, starting transfers between devices: 11.7 us -> 13.4 us  [across(): return lax.ppermute(block, axis, [(i, i ^ distance) for i in range(size)])]
    ppermute x17, waiting for transfers between devices: 11.4 us -> 13 us  [across(): return lax.ppermute(block, axis, [(i, i ^ distance) for i in range(size)])]
  transfers between devices with their start and end apart: 23 -> 23, of which waited for: 4 -> 7; matrix products, arithmetic and copies ran while one was open for 0% -> 0% of each run, Pallas kernels for 17% -> 17%
where the time goes in v16:
time: 71.4 us; the launch traced here: 71 us
  starting transfers between devices  28.4 us (40%)
  Pallas kernels  19.7 us (28%)
  waiting for transfers between devices  19.4 us (27%)
  local copies, waits for them, and re-layouts  2.51 us (4%)
  between operations  0.92 us (1%)
    ppermute x17, starting transfers between devices, across(): return lax.ppermute(block, axis, [(i, i ^ distance) for i in range(size)])  13.4 us
    ppermute x17, waiting for transfers between devices, across(): return lax.ppermute(block, axis, [(i, i ^ distance) for i in range(size)])  13 us
    pallas_call x1, Pallas kernels, on_device_two_phases(): call(chain_kernel, 'chain', 50, [HBM] * 7, [((experts, 2, rows, part), bf...  7.1 us
    all_to_all x1, waiting for transfers between devices, on_device_two_phases(): lax.all_to_all(send, sections, split_axis=0, concat_axis=0, tiled=True)  6.33 us
    ppermute x4, starting transfers between devices, on_device_two_phases(): lax.ppermute(block, ('dp', 'segment'), slab_route(replicas, turn // 2, tu...  6.29 us
    pallas_call x1, Pallas kernels, on_device_two_phases(): call(functools.partial(gradient_kernel, experts, sources, sizes), 'gradie...  5.83 us
    all_to_all x1, starting transfers between devices, on_device_two_phases(): lax.all_to_all(send, sections, split_axis=0, concat_axis=0, tiled=True)  5.29 us
    all_to_all x1, starting transfers between devices, on_device_two_phases(): lax.all_to_all(out.reshape(groups, rows, part), sections, split_axis=0, c...  3.5 us
  transfers between devices with their start and end apart: 23, of which 7 were waited for; matrix products, arithmetic and copies ran while one was open for 0% of the time, Pallas kernels for 17%

profile of v16, /device:TPU:0, one launch (start us, length us, event | category | flops | bytes accessed | tf_op | source)
XLA Modules:
  0.0 71.0 jit_solution(14012203269140755915)
XLA Ops:
  0.6 0.5 collective-permute-start
  1.2 2.4 %pack.1._ = bf16[8,2,16,2048]{3,2,1,0:T(8,128)(2,1)} custom-call(s32[16]{0:T(128)} %refs_22_.1, bf16[16,4,2048]{2,1,0:T(4,128)(2,1)} %hidden.3, bf16[16,4,2048]{2,1,0:T(4,128)(2,1)} %cot.3), custom_call_target="tpu_custom_call" | custom-call | bytes 1048576 | tf_op jit(solution)/shard_map/pack/pallas_call | solution.py:727
  3.6 5.3 %all-to-all-start = ((bf16[8,2,16,2048]{3,2,1,0:T(8,128)(2,1)}), bf16[8,2,16,2048]{3,2,1,0:T(8,128)(2,1)S(1)}, u32[]{:S(2)}, u32[]{:S(2)}) async-start(bf16[8,2,16,2048]{3,2,1,0:T(8,128)(2,1)} %pack.1._), calls=%async_computation | async-start | bytes 2097152 | tf_op jit(solution)/shard_map/all_to_all | solution.py:757
  8.9 0.5 collective-permute-start.2
  9.4 2.3 %slabs.1 = (bf16[80,1024]{1,0:T(8,128)(2,1)}, bf16[80,1024]{1,0:T(8,128)(2,1)}, bf16[80,1024]{1,0:T(8,128)(2,1)}, bf16[80,1024]{1,0:T(8,128)(2,1)}) custom-call(s32[16]{0:T(128)} %refs_22_.1, bf16[16,4,2048]{2,1,0:T(4,128)(2,1)} %hidden.3, bf16[16,4,2048]{2,1,0:T(4,128)(2,1)} %cot.3, bf16[8,2,16,2048]{3,2,1,0:T(8,128)(2,1)} %pack.1._), custom_call_target="tpu_custom_call" | custom-call | bytes 1048576 | tf_op jit(solution)/shard_map/slabs/pallas_call | solution.py:741
  11.7 1.6 %collective-permute-start.3 = (bf16[80,1024]{1,0:T(8,128)(2,1)}, bf16[80,1024]{1,0:T(8,128)(2,1)S(1)}, u32[]{:S(2)}, u32[]{:S(2)}) collective-permute-start(bf16[80,1024]{1,0:T(8,128)(2,1)} %get-tuple-element.31), channel_id=1, source_target_pairs={{0,0},{1,4},{2,2},{3,6},{4,1},{5,5},{6,3},{7,7},{8,8},{9,12},{10,1... | collective-permute-start | bytes 491528 | tf_op jit(solution)/shard_map/ppermute | solution.py:760
  13.3 3.1 %collective-permute-start.4 = (bf16[80,1024]{1,0:T(8,128)(2,1)}, bf16[80,1024]{1,0:T(8,128)(2,1)}, u32[]{:S(2)}, u32[]{:S(2)}) collective-permute-start(bf16[80,1024]{1,0:T(8,128)(2,1)} %get-tuple-element.32), channel_id=1, source_target_pairs={{0,1},{1,5},{2,3},{3,7},{4,0},{5,4},{6,2},{7,6},{8,9},{9,13},{10,1... | collective-permute-start | bytes 491528 | tf_op jit(solution)/shard_map/ppermute | solution.py:760
  16.4 1.6 %collective-permute-start.5 = (bf16[80,1024]{1,0:T(8,128)(2,1)}, bf16[80,1024]{1,0:T(8,128)(2,1)}, u32[]{:S(2)}, u32[]{:S(2)}) collective-permute-start(bf16[80,1024]{1,0:T(8,128)(2,1)} %get-tuple-element.33), channel_id=1, source_target_pairs={{0,2},{1,6},{2,0},{3,4},{4,3},{5,7},{6,1},{7,5},{8,10},{9,14},{10,... | collective-permute-start | bytes 491528 | tf_op jit(solution)/shard_map/ppermute | solution.py:760
  18.0 6.3 %all-to-all-done = bf16[8,2,16,2048]{3,2,1,0:T(8,128)(2,1)S(1)} async-done(((bf16[8,2,16,2048]{3,2,1,0:T(8,128)(2,1)}), bf16[8,2,16,2048]{3,2,1,0:T(8,128)(2,1)S(1)}, u32[]{:S(2)}, u32[]{:S(2)}) %all-to-all-start) | async-done | bytes 1048608 | tf_op jit(solution)/shard_map/all_to_all | solution.py:757
  24.4 7.1 %chain.1 = (bf16[4,2,16,2048]{3,2,1,0:T(8,128)(2,1)S(1)}, bf16[64,1152]{1,0:T(8,128)(2,1)S(1)}) custom-call(bf16[4,2,2,16,2048]{4,3,2,1,0:T(8,128)(2,1)S(1)} %bitcast.7, bf16[4096,256]{1,0:T(8,128)(2,1)S(1)} %bitcast.11, bf16[256,4096]{1,0:T(8,128)(2,1)} %bitcast.17, bf16[1,4096]{1,0:T(2,128)(2,1)S(1)} %bitcast.15, ...), custom_call_target="tpu_custom_call" | custom-call | flops 939524096 | bytes 10485760 | tf_op jit(solution)/shard_map/chain/pallas_call | solution.py:763
  31.5 2.2 %repack.1 = (bf16[2,7,16,1024]{3,2,1,0:T(8,128)(2,1)S(1)}, bf16[2,3,16,1024]{3,2,1,0:T(8,128)(2,1)S(1)}, bf16[2,3,16,1024]{3,2,1,0:T(8,128)(2,1)S(1)}, bf16[2,3,16,1024]{3,2,1,0:T(8,128)(2,1)S(1)}) custom-call(bf16[80,1024]{1,0:T(8,128)(2,1)S(1)} %collective-permute-done.3.refs_0_, bf16[80,1024]{1,0:T(8,128)(2,1)} %collective-permute-done.4.refs_1_, ...), custom_call_target="tpu_custom_call" | custom-call | bytes 1048576 | tf_op jit(solution)/shard_map/repack/pallas_call | solution.py:782
  33.7 0.6 collective-permute-start.7
  34.3 1.5 %collective-permute-start.9 = (bf16[2,3,16,1024]{3,2,1,0:T(8,128)(2,1)S(1)}, bf16[2,3,16,1024]{3,2,1,0:T(8,128)(2,1)S(1)}, u32[]{:S(2)}, u32[]{:S(2)}) collective-permute-start(bf16[2,3,16,1024]{3,2,1,0:T(8,128)(2,1)S(1)} %get-tuple-element.47), channel_id=1, source_target_pairs={{0,24},{8,16},{16,8},{24,0},{1,25},{9,17},{17,9},{25,1},{2,26},{10... | collective-permute-start | bytes 589832 | tf_op jit(solution)/shard_map/ppermute | solution.py:696
  35.8 1.5 %collective-permute-start.8 = (bf16[2,3,16,1024]{3,2,1,0:T(8,128)(2,1)S(1)}, bf16[2,3,16,1024]{3,2,1,0:T(8,128)(2,1)S(1)}, u32[]{:S(2)}, u32[]{:S(2)}) collective-permute-start(bf16[2,3,16,1024]{3,2,1,0:T(8,128)(2,1)S(1)} %get-tuple-element.46), channel_id=1, source_target_pairs={{0,16},{8,24},{16,0},{24,8},{1,17},{9,25},{17,1},{25,9},{2,18},{10... | collective-permute-start | bytes 589832 | tf_op jit(solution)/shard_map/ppermute | solution.py:696
  37.3 3.6 %collective-permute-start.14 = (bf16[64,1152]{1,0:T(8,128)(2,1)S(1)}, bf16[64,1152]{1,0:T(8,128)(2,1)S(1)}, u32[]{:S(2)}, u32[]{:S(2)}) collective-permute-start(bf16[64,1152]{1,0:T(8,128)(2,1)S(1)} %get-tuple-element.50.refs_5_.refs_8_), channel_id=1, source_target_pairs={{0,6},{2,4},{4,2},{6,0},{1,7},{3,5},{5,3},{7,1},{8,14},{10,12},{12... | collective-permute-start | bytes 442376 | tf_op jit(solution)/shard_map/ppermute | solution.py:696
  40.9 0.8 %collective-permute-done.7.refs_1_ = bf16[2,3,16,1024]{3,2,1,0:T(8,128)(2,1)S(1)} collective-permute-done((bf16[2,3,16,1024]{3,2,1,0:T(8,128)(2,1)S(1)}, bf16[2,3,16,1024]{3,2,1,0:T(8,128)(2,1)S(1)}, u32[]{:S(2)}, u32[]{:S(2)}) %collective-permute-start.7) | collective-permute-done | bytes 196640 | tf_op jit(solution)/shard_map/ppermute | solution.py:696
  41.6 3.5 %all-to-all-start.1 = ((bf16[8,16,2048]{2,1,0:T(8,128)(2,1)}), bf16[8,16,2048]{2,1,0:T(8,128)(2,1)S(1)}, u32[]{:S(2)}, u32[]{:S(2)}) async-start(bf16[8,16,2048]{2,1,0:T(8,128)(2,1)} %bitcast.12), calls=%async_computation.1 | async-start | bytes 1048576 | tf_op jit(solution)/shard_map/all_to_all | solution.py:802
  45.1 0.4 collective-permute-start.10
  45.5 2.5 %collective-permute-start.13 = (bf16[64,1152]{1,0:T(8,128)(2,1)S(1)}, bf16[64,1152]{1,0:T(8,128)(2,1)S(1)}, u32[]{:S(2)}, u32[]{:S(2)}) collective-permute-start(bf16[64,1152]{1,0:T(8,128)(2,1)S(1)} %get-tuple-element.50.refs_5_.refs_8_), channel_id=1, source_target_pairs={{0,4},{2,6},{4,0},{6,2},{1,5},{3,7},{5,1},{7,3},{8,12},{10,14},{12... | collective-permute-start | bytes 442376 | tf_op jit(solution)/shard_map/ppermute | solution.py:696
  48.1 0.5 collective-permute-start.11
  48.7 6.9 %collective-permute-done.13.refs_10_ = bf16[64,1152]{1,0:T(8,128)(2,1)S(1)} collective-permute-done((bf16[64,1152]{1,0:T(8,128)(2,1)S(1)}, bf16[64,1152]{1,0:T(8,128)(2,1)S(1)}, u32[]{:S(2)}, u32[]{:S(2)}) %collective-permute-start.13) | collective-permute-done | bytes 147488 | tf_op jit(solution)/shard_map/ppermute | solution.py:696
  55.5 0.6 collective-permute-start.16
  56.1 4.5 %collective-permute-done.16.refs_9_ = bf16[64,1152]{1,0:T(8,128)(2,1)S(1)} collective-permute-done((bf16[64,1152]{1,0:T(8,128)(2,1)S(1)}, bf16[64,1152]{1,0:T(8,128)(2,1)S(1)}, u32[]{:S(2)}, u32[]{:S(2)}) %collective-permute-start.16) | collective-permute-done | bytes 147488 | tf_op jit(solution)/shard_map/ppermute | solution.py:696
  60.7 0.5 collective-permute-start.17
  61.3 0.4 collective-permute-start.20
  61.7 0.3 collective-permute-done.18.refs_13_
  62.2 0.3 collective-permute-done.19.refs_14_
  62.6 0.4 copy-done.18
  62.9 0.7 copy-done.19
  63.7 0.7 copy-done.6
  64.4 0.8 %copy-done.7 = bf16[2,7,16,1024]{3,2,1,0:T(8,128)(2,1)} copy-done((bf16[2,7,16,1024]{3,2,1,0:T(8,128)(2,1)}, bf16[2,7,16,1024]{3,2,1,0:T(8,128)(2,1)S(1)}, u32[]{:S(2)}) %copy-start.7) | copy-done | bytes 458776
  65.1 5.8 %gradients.1 = (bf16[16,4,2048]{2,1,0:T(4,128)(2,1)}, bf16[1024,256]{1,0:T(8,128)(2,1)}, bf16[256,1024]{1,0:T(8,128)(2,1)}) custom-call(bf16[2,7,16,1024]{3,2,1,0:T(8,128)(2,1)} %copy-done.3, bf16[2,3,16,1024]{3,2,1,0:T(8,128)(2,1)} %copy-done.8, bf16[2,3,16,1024]{3,2,1,0:T(8,128)(2,1)} %copy-done.10, bf16[2,3,16,1024]{3,2,1,0:T(8,128)(2,1)} %copy-done.9, ...), custom_call_target="tpu_custom_call" | custom-call | bytes 1048576 | tf_op jit(solution)/shard_map/gradients/pallas_call | solution.py:808
  (59 shorter events, 0.6 us)
Async XLA Ops:
  0.6 17.4 %collective-permute-start = (bf16[4096,256]{1,0:T(8,128)(2,1)}, bf16[4096,256]{1,0:T(8,128)(2,1)}, u32[]{:S(2)}, u32[]{:S(2)}) collective-permute-start(bf16[4096,256]{1,0:T(8,128)(2,1)} %bitcast.9), channel_id=1, source_target_pairs={{0,1},{1,0},{2,3},{3,2},{4,5},{5,4},{6,7},{7,6},{8,9},{9,8},{10,11... | collective-permute-start | bytes 6291464 | tf_op jit(solution)/shard_map/ppermute | solution.py:696
  1.2 23.2 %collective-permute-start.1 = (bf16[256,4096]{1,0:T(8,128)(2,1)}, bf16[256,4096]{1,0:T(8,128)(2,1)}, u32[]{:S(2)}, u32[]{:S(2)}) collective-permute-start(bf16[256,4096]{1,0:T(8,128)(2,1)} %bitcast.16), channel_id=1, source_target_pairs={{0,1},{1,0},{2,3},{3,2},{4,5},{5,4},{6,7},{7,6},{8,9},{9,8},{10,11... | collective-permute-start | bytes 6291464 | tf_op jit(solution)/shard_map/ppermute | solution.py:696
  3.6 20.7 %copy-start = (bf16[1,1,4096,256]{3,2,1,0:T(8,128)(2,1)S(1)}, bf16[1,1,4096,256]{3,2,1,0:T(8,128)(2,1)}, u32[]{:S(2)}) copy-start(bf16[1,1,4096,256]{3,2,1,0:T(8,128)(2,1)} %param.9) | copy-start | bytes 6291460
  3.6 20.7 %all-to-all-start = ((bf16[8,2,16,2048]{3,2,1,0:T(8,128)(2,1)}), bf16[8,2,16,2048]{3,2,1,0:T(8,128)(2,1)S(1)}, u32[]{:S(2)}, u32[]{:S(2)}) async-start(bf16[8,2,16,2048]{3,2,1,0:T(8,128)(2,1)} %pack.1._), calls=%async_computation | async-start | bytes 2097152 | tf_op jit(solution)/shard_map/all_to_all | solution.py:757
  8.9 7.5 %collective-permute-start.2 = (bf16[1,4096]{1,0:T(2,128)(2,1)S(1)}, bf16[1,4096]{1,0:T(2,128)(2,1)S(1)}, u32[]{:S(2)}, u32[]{:S(2)}) collective-permute-start(bf16[1,4096]{1,0:T(2,128)(2,1)S(1)} %bitcast.14), channel_id=1, source_target_pairs={{0,1},{1,0},{2,3},{3,2},{4,5},{5,4},{6,7},{7,6},{8,9},{9,8},{10,11... | collective-permute-start | bytes 24584 | tf_op jit(solution)/shard_map/ppermute | solution.py:696
  11.7 19.8 %collective-permute-start.3 = (bf16[80,1024]{1,0:T(8,128)(2,1)}, bf16[80,1024]{1,0:T(8,128)(2,1)S(1)}, u32[]{:S(2)}, u32[]{:S(2)}) collective-permute-start(bf16[80,1024]{1,0:T(8,128)(2,1)} %get-tuple-element.31), channel_id=1, source_target_pairs={{0,0},{1,4},{2,2},{3,6},{4,1},{5,5},{6,3},{7,7},{8,8},{9,12},{10,1... | collective-permute-start | bytes 491528 | tf_op jit(solution)/shard_map/ppermute | solution.py:760
  13.3 18.2 %collective-permute-start.4 = (bf16[80,1024]{1,0:T(8,128)(2,1)}, bf16[80,1024]{1,0:T(8,128)(2,1)}, u32[]{:S(2)}, u32[]{:S(2)}) collective-permute-start(bf16[80,1024]{1,0:T(8,128)(2,1)} %get-tuple-element.32), channel_id=1, source_target_pairs={{0,1},{1,5},{2,3},{3,7},{4,0},{5,4},{6,2},{7,6},{8,9},{9,13},{10,1... | collective-permute-start | bytes 491528 | tf_op jit(solution)/shard_map/ppermute | solution.py:760
  16.4 15.0 %copy-start.5 = (bf16[1,4096]{1,0:T(2,128)(2,1)}, bf16[1,4096]{1,0:T(2,128)(2,1)S(1)}, u32[]{:S(2)}) copy-start(bf16[1,4096]{1,0:T(2,128)(2,1)S(1)} %collective-permute-done.2.other_gain.refs_21_) | copy-start | bytes 24580
  16.4 15.1 %collective-permute-start.5 = (bf16[80,1024]{1,0:T(8,128)(2,1)}, bf16[80,1024]{1,0:T(8,128)(2,1)}, u32[]{:S(2)}, u32[]{:S(2)}) collective-permute-start(bf16[80,1024]{1,0:T(8,128)(2,1)} %get-tuple-element.33), channel_id=1, source_target_pairs={{0,2},{1,6},{2,0},{3,4},{4,3},{5,7},{6,1},{7,5},{8,10},{9,14},{10,... | collective-permute-start | bytes 491528 | tf_op jit(solution)/shard_map/ppermute | solution.py:760
  18.0 13.5 %collective-permute-start.6 = (bf16[80,1024]{1,0:T(8,128)(2,1)}, bf16[80,1024]{1,0:T(8,128)(2,1)}, u32[]{:S(2)}, u32[]{:S(2)}) collective-permute-start(bf16[80,1024]{1,0:T(8,128)(2,1)} %get-tuple-element.34), channel_id=1, source_target_pairs={{0,3},{1,7},{2,1},{3,5},{4,2},{5,6},{6,0},{7,4},{8,11},{9,15},{10,... | collective-permute-start | bytes 491528 | tf_op jit(solution)/shard_map/ppermute | solution.py:760
  31.5 10.2 %copy-start.2 = (bf16[4,2,16,2048]{3,2,1,0:T(8,128)(2,1)}, bf16[4,2,16,2048]{3,2,1,0:T(8,128)(2,1)S(1)}, u32[]{:S(2)}) copy-start(bf16[4,2,16,2048]{3,2,1,0:T(8,128)(2,1)S(1)} %get-tuple-element.53) | copy-start | bytes 1572868
  31.5 32.1 %copy-start.1 = (bf16[64,1152]{1,0:T(8,128)(2,1)}, bf16[64,1152]{1,0:T(8,128)(2,1)S(1)}, u32[]{:S(2)}) copy-start(bf16[64,1152]{1,0:T(8,128)(2,1)S(1)} %get-tuple-element.50.refs_5_.refs_8_) | copy-start | bytes 442372
  33.7 29.9 %copy-start.3 = (bf16[2,7,16,1024]{3,2,1,0:T(8,128)(2,1)}, bf16[2,7,16,1024]{3,2,1,0:T(8,128)(2,1)S(1)}, u32[]{:S(2)}) copy-start(bf16[2,7,16,1024]{3,2,1,0:T(8,128)(2,1)S(1)} %get-tuple-element.41.refs_0_) | copy-start | bytes 1376260
  33.7 7.9 %collective-permute-start.7 = (bf16[2,3,16,1024]{3,2,1,0:T(8,128)(2,1)S(1)}, bf16[2,3,16,1024]{3,2,1,0:T(8,128)(2,1)S(1)}, u32[]{:S(2)}, u32[]{:S(2)}) collective-permute-start(bf16[2,3,16,1024]{3,2,1,0:T(8,128)(2,1)S(1)} %get-tuple-element.40), channel_id=1, source_target_pairs={{0,8},{8,0},{16,24},{24,16},{1,9},{9,1},{17,25},{25,17},{2,10},{10... | collective-permute-start | bytes 589832 | tf_op jit(solution)/shard_map/ppermute | solution.py:696
  34.3 13.8 %collective-permute-start.9 = (bf16[2,3,16,1024]{3,2,1,0:T(8,128)(2,1)S(1)}, bf16[2,3,16,1024]{3,2,1,0:T(8,128)(2,1)S(1)}, u32[]{:S(2)}, u32[]{:S(2)}) collective-permute-start(bf16[2,3,16,1024]{3,2,1,0:T(8,128)(2,1)S(1)} %get-tuple-element.47), channel_id=1, source_target_pairs={{0,24},{8,16},{16,8},{24,0},{1,25},{9,17},{17,9},{25,1},{2,26},{10... | collective-permute-start | bytes 589832 | tf_op jit(solution)/shard_map/ppermute | solution.py:696
  35.8 12.8 %collective-permute-start.8 = (bf16[2,3,16,1024]{3,2,1,0:T(8,128)(2,1)S(1)}, bf16[2,3,16,1024]{3,2,1,0:T(8,128)(2,1)S(1)}, u32[]{:S(2)}, u32[]{:S(2)}) collective-permute-start(bf16[2,3,16,1024]{3,2,1,0:T(8,128)(2,1)S(1)} %get-tuple-element.46), channel_id=1, source_target_pairs={{0,16},{8,24},{16,0},{24,8},{1,17},{9,25},{17,1},{25,9},{2,18},{10... | collective-permute-start | bytes 589832 | tf_op jit(solution)/shard_map/ppermute | solution.py:696
  37.3 10.8 %collective-permute-start.14 = (bf16[64,1152]{1,0:T(8,128)(2,1)S(1)}, bf16[64,1152]{1,0:T(8,128)(2,1)S(1)}, u32[]{:S(2)}, u32[]{:S(2)}) collective-permute-start(bf16[64,1152]{1,0:T(8,128)(2,1)S(1)} %get-tuple-element.50.refs_5_.refs_8_), channel_id=1, source_target_pairs={{0,6},{2,4},{4,2},{6,0},{1,7},{3,5},{5,3},{7,1},{8,14},{10,12},{12... | collective-permute-start | bytes 442376 | tf_op jit(solution)/shard_map/ppermute | solution.py:696
  41.6 22.0 %copy-start.8 = (bf16[2,3,16,1024]{3,2,1,0:T(8,128)(2,1)}, bf16[2,3,16,1024]{3,2,1,0:T(8,128)(2,1)S(1)}, u32[]{:S(2)}) copy-start(bf16[2,3,16,1024]{3,2,1,0:T(8,128)(2,1)S(1)} %collective-permute-done.7.refs_1_) | copy-start | bytes 589828
  41.6 22.0 %all-to-all-start.1 = ((bf16[8,16,2048]{2,1,0:T(8,128)(2,1)}), bf16[8,16,2048]{2,1,0:T(8,128)(2,1)S(1)}, u32[]{:S(2)}, u32[]{:S(2)}) async-start(bf16[8,16,2048]{2,1,0:T(8,128)(2,1)} %bitcast.12), calls=%async_computation.1 | async-start | bytes 1048576 | tf_op jit(solution)/shard_map/all_to_all | solution.py:802
  45.1 18.5 %collective-permute-start.10 = (bf16[2,7,16,1024]{3,2,1,0:T(8,128)(2,1)S(1)}, bf16[2,7,16,1024]{3,2,1,0:T(8,128)(2,1)S(1)}, u32[]{:S(2)}, u32[]{:S(2)}) collective-permute-start(bf16[2,7,16,1024]{3,2,1,0:T(8,128)(2,1)S(1)} %get-tuple-element.41.refs_0_), channel_id=1, source_target_pairs={{0,1},{1,0},{2,3},{3,2},{4,5},{5,4},{6,7},{7,6},{8,9},{9,8},{10,11... | collective-permute-start | bytes 1376264 | tf_op jit(solution)/shard_map/ppermute | solution.py:696
  45.5 10.0 %collective-permute-start.13 = (bf16[64,1152]{1,0:T(8,128)(2,1)S(1)}, bf16[64,1152]{1,0:T(8,128)(2,1)S(1)}, u32[]{:S(2)}, u32[]{:S(2)}) collective-permute-start(bf16[64,1152]{1,0:T(8,128)(2,1)S(1)} %get-tuple-element.50.refs_5_.refs_8_), channel_id=1, source_target_pairs={{0,4},{2,6},{4,0},{6,2},{1,5},{3,7},{5,1},{7,3},{8,12},{10,14},{12... | collective-permute-start | bytes 442376 | tf_op jit(solution)/shard_map/ppermute | solution.py:696
  48.0 15.6 %copy-start.9 = (bf16[2,3,16,1024]{3,2,1,0:T(8,128)(2,1)}, bf16[2,3,16,1024]{3,2,1,0:T(8,128)(2,1)S(1)}, u32[]{:S(2)}) copy-start(bf16[2,3,16,1024]{3,2,1,0:T(8,128)(2,1)S(1)} %collective-permute-done.9.refs_3_) | copy-start | bytes 589828
  48.0 12.6 %collective-permute-start.15 = (bf16[2,3,16,1024]{3,2,1,0:T(8,128)(2,1)S(1)}, bf16[2,3,16,1024]{3,2,1,0:T(8,128)(2,1)S(1)}, u32[]{:S(2)}, u32[]{:S(2)}) collective-permute-start(bf16[2,3,16,1024]{3,2,1,0:T(8,128)(2,1)S(1)} %collective-permute-done.9.refs_3_), channel_id=1, source_target_pairs={{0,1},{1,0},{2,3},{3,2},{4,5},{5,4},{6,7},{7,6},{8,9},{9,8},{10,11... | collective-permute-start | bytes 589832 | tf_op jit(solution)/shard_map/ppermute | solution.py:696
  48.1 15.6 %copy-start.14 = (bf16[64,1152]{1,0:T(8,128)(2,1)}, bf16[64,1152]{1,0:T(8,128)(2,1)S(1)}, u32[]{:S(2)}) copy-start(bf16[64,1152]{1,0:T(8,128)(2,1)S(1)} %collective-permute-done.14.refs_11_) | copy-start | bytes 442372
  48.1 13.1 %collective-permute-start.11 = (bf16[2,3,16,1024]{3,2,1,0:T(8,128)(2,1)S(1)}, bf16[2,3,16,1024]{3,2,1,0:T(8,128)(2,1)S(1)}, u32[]{:S(2)}, u32[]{:S(2)}) collective-permute-start(bf16[2,3,16,1024]{3,2,1,0:T(8,128)(2,1)S(1)} %collective-permute-done.7.refs_1_), channel_id=1, source_target_pairs={{0,1},{1,0},{2,3},{3,2},{4,5},{5,4},{6,7},{7,6},{8,9},{9,8},{10,11... | collective-permute-start | bytes 589832 | tf_op jit(solution)/shard_map/ppermute | solution.py:696
  48.6 15.1 %copy-start.10 = (bf16[2,3,16,1024]{3,2,1,0:T(8,128)(2,1)}, bf16[2,3,16,1024]{3,2,1,0:T(8,128)(2,1)S(1)}, u32[]{:S(2)}) copy-start(bf16[2,3,16,1024]{3,2,1,0:T(8,128)(2,1)S(1)} %collective-permute-done.8.refs_2_) | copy-start | bytes 589828
  48.6 12.7 %collective-permute-start.12 = (bf16[2,3,16,1024]{3,2,1,0:T(8,128)(2,1)S(1)}, bf16[2,3,16,1024]{3,2,1,0:T(8,128)(2,1)S(1)}, u32[]{:S(2)}, u32[]{:S(2)}) collective-permute-start(bf16[2,3,16,1024]{3,2,1,0:T(8,128)(2,1)S(1)} %collective-permute-done.8.refs_2_), channel_id=1, source_target_pairs={{0,1},{1,0},{2,3},{3,2},{4,5},{5,4},{6,7},{7,6},{8,9},{9,8},{10,11... | collective-permute-start | bytes 589832 | tf_op jit(solution)/shard_map/ppermute | solution.py:696
  55.5 5.1 %collective-permute-start.16 = (bf16[64,1152]{1,0:T(8,128)(2,1)S(1)}, bf16[64,1152]{1,0:T(8,128)(2,1)S(1)}, u32[]{:S(2)}, u32[]{:S(2)}) collective-permute-start(bf16[64,1152]{1,0:T(8,128)(2,1)S(1)} %get-tuple-element.50.refs_5_.refs_8_), channel_id=1, source_target_pairs={{0,2},{2,0},{4,6},{6,4},{1,3},{3,1},{5,7},{7,5},{8,10},{10,8},{12,... | collective-permute-start | bytes 442376 | tf_op jit(solution)/shard_map/ppermute | solution.py:696
  60.7 1.4 %collective-permute-start.18 = (bf16[64,1152]{1,0:T(8,128)(2,1)S(1)}, bf16[64,1152]{1,0:T(8,128)(2,1)S(1)}, u32[]{:S(2)}, u32[]{:S(2)}) collective-permute-start(bf16[64,1152]{1,0:T(8,128)(2,1)S(1)} %collective-permute-done.16.refs_9_), channel_id=1, source_target_pairs={{0,1},{1,0},{2,3},{3,2},{4,5},{5,4},{6,7},{7,6},{8,9},{9,8},{10,11... | collective-permute-start | bytes 442376 | tf_op jit(solution)/shard_map/ppermute | solution.py:696
  60.7 1.6 %collective-permute-start.17 = (bf16[64,1152]{1,0:T(8,128)(2,1)S(1)}, bf16[64,1152]{1,0:T(8,128)(2,1)S(1)}, u32[]{:S(2)}, u32[]{:S(2)}) collective-permute-start(bf16[64,1152]{1,0:T(8,128)(2,1)S(1)} %get-tuple-element.50.refs_5_.refs_8_), channel_id=1, source_target_pairs={{0,1},{1,0},{2,3},{3,2},{4,5},{5,4},{6,7},{7,6},{8,9},{9,8},{10,11... | collective-permute-start | bytes 442376 | tf_op jit(solution)/shard_map/ppermute | solution.py:696
  61.2 1.4 %collective-permute-start.19 = (bf16[64,1152]{1,0:T(8,128)(2,1)S(1)}, bf16[64,1152]{1,0:T(8,128)(2,1)S(1)}, u32[]{:S(2)}, u32[]{:S(2)}) collective-permute-start(bf16[64,1152]{1,0:T(8,128)(2,1)S(1)} %collective-permute-done.13.refs_10_), channel_id=1, source_target_pairs={{0,1},{1,0},{2,3},{3,2},{4,5},{5,4},{6,7},{7,6},{8,9},{9,8},{10,11... | collective-permute-start | bytes 442376 | tf_op jit(solution)/shard_map/ppermute | solution.py:696
  61.3 2.3 %collective-permute-start.20 = (bf16[64,1152]{1,0:T(8,128)(2,1)S(1)}, bf16[64,1152]{1,0:T(8,128)(2,1)}, u32[]{:S(2)}, u32[]{:S(2)}) collective-permute-start(bf16[64,1152]{1,0:T(8,128)(2,1)S(1)} %collective-permute-done.14.refs_11_), channel_id=1, source_target_pairs={{0,1},{1,0},{2,3},{3,2},{4,5},{5,4},{6,7},{7,6},{8,9},{9,8},{10,11... | collective-permute-start | bytes 442376 | tf_op jit(solution)/shard_map/ppermute | solution.py:696
  (11 other events, 31.9 us)

commit v17 on v15

--- a/solution.py
+++ b/solution.py
@@ -792,7 +792,7 @@
     mine = [slices[0]] + [across(slices[step], "expert", step) for step in range(1, experts)]
     mine[:2] = lax.optimization_barrier(tuple(mine[:2]))
     near = [small] + [across(small, "dp", step) for step in range(1, replicas - 1)]
-    near[:2] = lax.optimization_barrier(tuple(near[:2]))
+    *near[:2], out = lax.optimization_barrier((*near[:2], out))
     last = across(near[0], "dp", replicas - 1)
     *near, mine[-1] = lax.optimization_barrier((*near, mine[-1]))
     near.append(last)

time: 63.3 us -> 63.3 us (level)
  starting transfers between devices: 26.2 us -> 29.1 us
  waiting for transfers between devices: 14.6 us -> 11.7 us
    ppermute x17, waiting for transfers between devices: 8.27 us -> 5.32 us  [across(): return lax.ppermute(block, axis, [(i, i ^ distance) for i in range(size)])]
    ppermute x17, starting transfers between devices: 11.1 us -> 14 us  [across(): return lax.ppermute(block, axis, [(i, i ^ distance) for i in range(size)])]
  transfers between devices with their start and end apart: 23 -> 23, of which waited for: 7 -> 6; matrix products, arithmetic and copies ran while one was open for 0% -> 0% of each run, Pallas kernels for 19% -> 19%
where the time goes in v17:
time: 63.3 us; the launch traced here: 62.9 us
  starting transfers between devices  29.1 us (46%)
  Pallas kernels  19.7 us (31%)
  waiting for transfers between devices  11.7 us (18%)
  local copies, waits for them, and re-layouts  1.52 us (2%)
  between operations  0.91 us (1%)
    ppermute x17, starting transfers between devices, across(): return lax.ppermute(block, axis, [(i, i ^ distance) for i in range(size)])  14 us
    pallas_call x1, Pallas kernels, on_device_two_phases(): call(chain_kernel, 'chain', 50, [HBM] * 7, [((experts, 2, rows, part), bf...  7.1 us
    all_to_all x1, waiting for transfers between devices, on_device_two_phases(): lax.all_to_all(send, sections, split_axis=0, concat_axis=0, tiled=True)  6.33 us
    ppermute x4, starting transfers between devices, on_device_two_phases(): lax.ppermute(block, ('dp', 'segment'), slab_route(replicas, turn // 2, tu...  6.29 us
    pallas_call x1, Pallas kernels, on_device_two_phases(): call(functools.partial(gradient_kernel, experts, sources, sizes), 'gradie...  5.83 us
    ppermute x17, waiting for transfers between devices, across(): return lax.ppermute(block, axis, [(i, i ^ distance) for i in range(size)])  5.32 us
    all_to_all x1, starting transfers between devices, on_device_two_phases(): lax.all_to_all(send, sections, split_axis=0, concat_axis=0, tiled=True)  5.29 us
    all_to_all x1, starting transfers between devices, on_device_two_phases(): lax.all_to_all(out.reshape(groups, rows, part), sections, split_axis=0, c...  3.5 us
  transfers between devices with their start and end apart: 23, of which 6 were waited for; matrix products, arithmetic and copies ran while one was open for 0% of the time, Pallas kernels for 19%

profile of v17, /device:TPU:0, one launch (start us, length us, event | category | flops | bytes accessed | tf_op | source)
XLA Modules:
  0.0 62.9 jit_solution(15296947711854263505)
XLA Ops:
  0.6 0.5 collective-permute-start
  1.2 0.1 collective-permute-start.1
  1.2 2.4 %pack.1._ = bf16[8,2,16,2048]{3,2,1,0:T(8,128)(2,1)} custom-call(s32[16]{0:T(128)} %refs_22_.1, bf16[16,4,2048]{2,1,0:T(4,128)(2,1)} %hidden.3, bf16[16,4,2048]{2,1,0:T(4,128)(2,1)} %cot.3), custom_call_target="tpu_custom_call" | custom-call | bytes 1048576 | tf_op jit(solution)/shard_map/pack/pallas_call | solution.py:727
  3.6 5.3 %all-to-all-start = ((bf16[8,2,16,2048]{3,2,1,0:T(8,128)(2,1)}), bf16[8,2,16,2048]{3,2,1,0:T(8,128)(2,1)S(1)}, u32[]{:S(2)}, u32[]{:S(2)}) async-start(bf16[8,2,16,2048]{3,2,1,0:T(8,128)(2,1)} %pack.1._), calls=%async_computation | async-start | bytes 2097152 | tf_op jit(solution)/shard_map/all_to_all | solution.py:757
  8.9 0.5 collective-permute-start.2
  9.4 2.3 %slabs.1 = (bf16[80,1024]{1,0:T(8,128)(2,1)}, bf16[80,1024]{1,0:T(8,128)(2,1)}, bf16[80,1024]{1,0:T(8,128)(2,1)}, bf16[80,1024]{1,0:T(8,128)(2,1)}) custom-call(s32[16]{0:T(128)} %refs_22_.1, bf16[16,4,2048]{2,1,0:T(4,128)(2,1)} %hidden.3, bf16[16,4,2048]{2,1,0:T(4,128)(2,1)} %cot.3, bf16[8,2,16,2048]{3,2,1,0:T(8,128)(2,1)} %pack.1._), custom_call_target="tpu_custom_call" | custom-call | bytes 1048576 | tf_op jit(solution)/shard_map/slabs/pallas_call | solution.py:741
  11.7 1.6 %collective-permute-start.3 = (bf16[80,1024]{1,0:T(8,128)(2,1)}, bf16[80,1024]{1,0:T(8,128)(2,1)S(1)}, u32[]{:S(2)}, u32[]{:S(2)}) collective-permute-start(bf16[80,1024]{1,0:T(8,128)(2,1)} %get-tuple-element.31), channel_id=1, source_target_pairs={{0,0},{1,4},{2,2},{3,6},{4,1},{5,5},{6,3},{7,7},{8,8},{9,12},{10,1... | collective-permute-start | bytes 491528 | tf_op jit(solution)/shard_map/ppermute | solution.py:760
  13.3 3.1 %collective-permute-start.4 = (bf16[80,1024]{1,0:T(8,128)(2,1)}, bf16[80,1024]{1,0:T(8,128)(2,1)}, u32[]{:S(2)}, u32[]{:S(2)}) collective-permute-start(bf16[80,1024]{1,0:T(8,128)(2,1)} %get-tuple-element.32), channel_id=1, source_target_pairs={{0,1},{1,5},{2,3},{3,7},{4,0},{5,4},{6,2},{7,6},{8,9},{9,13},{10,1... | collective-permute-start | bytes 491528 | tf_op jit(solution)/shard_map/ppermute | solution.py:760
  16.4 1.6 %collective-permute-start.5 = (bf16[80,1024]{1,0:T(8,128)(2,1)}, bf16[80,1024]{1,0:T(8,128)(2,1)}, u32[]{:S(2)}, u32[]{:S(2)}) collective-permute-start(bf16[80,1024]{1,0:T(8,128)(2,1)} %get-tuple-element.33), channel_id=1, source_target_pairs={{0,2},{1,6},{2,0},{3,4},{4,3},{5,7},{6,1},{7,5},{8,10},{9,14},{10,... | collective-permute-start | bytes 491528 | tf_op jit(solution)/shard_map/ppermute | solution.py:760
  18.0 6.3 %all-to-all-done = bf16[8,2,16,2048]{3,2,1,0:T(8,128)(2,1)S(1)} async-done(((bf16[8,2,16,2048]{3,2,1,0:T(8,128)(2,1)}), bf16[8,2,16,2048]{3,2,1,0:T(8,128)(2,1)S(1)}, u32[]{:S(2)}, u32[]{:S(2)}) %all-to-all-start) | async-done | bytes 1048608 | tf_op jit(solution)/shard_map/all_to_all | solution.py:757
  24.3 7.1 %chain.1 = (bf16[4,2,16,2048]{3,2,1,0:T(8,128)(2,1)S(1)}, bf16[64,1152]{1,0:T(8,128)(2,1)S(1)}) custom-call(bf16[4,2,2,16,2048]{4,3,2,1,0:T(8,128)(2,1)S(1)} %bitcast.7, bf16[4096,256]{1,0:T(8,128)(2,1)S(1)} %bitcast.11, bf16[256,4096]{1,0:T(8,128)(2,1)} %bitcast.17, bf16[1,4096]{1,0:T(2,128)(2,1)S(1)} %bitcast.15, ...), custom_call_target="tpu_custom_call" | custom-call | flops 939524096 | bytes 10485760 | tf_op jit(solution)/shard_map/chain/pallas_call | solution.py:763
  31.5 2.2 %repack.1 = (bf16[2,7,16,1024]{3,2,1,0:T(8,128)(2,1)S(1)}, bf16[2,3,16,1024]{3,2,1,0:T(8,128)(2,1)S(1)}, bf16[2,3,16,1024]{3,2,1,0:T(8,128)(2,1)S(1)}, bf16[2,3,16,1024]{3,2,1,0:T(8,128)(2,1)S(1)}) custom-call(bf16[80,1024]{1,0:T(8,128)(2,1)S(1)} %collective-permute-done.3.refs_0_, bf16[80,1024]{1,0:T(8,128)(2,1)} %collective-permute-done.4.refs_1_, ...), custom_call_target="tpu_custom_call" | custom-call | bytes 1048576 | tf_op jit(solution)/shard_map/repack/pallas_call | solution.py:782
  33.7 0.6 collective-permute-start.7
  34.3 2.4 %collective-permute-start.9 = (bf16[64,1152]{1,0:T(8,128)(2,1)S(1)}, bf16[64,1152]{1,0:T(8,128)(2,1)S(1)}, u32[]{:S(2)}, u32[]{:S(2)}) collective-permute-start(bf16[64,1152]{1,0:T(8,128)(2,1)S(1)} %get-tuple-element.50.refs_5_.refs_8_), channel_id=1, source_target_pairs={{0,2},{2,0},{4,6},{6,4},{1,3},{3,1},{5,7},{7,5},{8,10},{10,8},{12,... | collective-permute-start | bytes 442376 | tf_op jit(solution)/shard_map/ppermute | solution.py:696
  36.6 1.5 %collective-permute-start.11 = (bf16[2,3,16,1024]{3,2,1,0:T(8,128)(2,1)S(1)}, bf16[2,3,16,1024]{3,2,1,0:T(8,128)(2,1)S(1)}, u32[]{:S(2)}, u32[]{:S(2)}) collective-permute-start(bf16[2,3,16,1024]{3,2,1,0:T(8,128)(2,1)S(1)} %get-tuple-element.48), channel_id=1, source_target_pairs={{0,24},{8,16},{16,8},{24,0},{1,25},{9,17},{17,9},{25,1},{2,26},{10... | collective-permute-start | bytes 589832 | tf_op jit(solution)/shard_map/ppermute | solution.py:696
  38.1 1.8 %collective-permute-start.10 = (bf16[64,1152]{1,0:T(8,128)(2,1)S(1)}, bf16[64,1152]{1,0:T(8,128)(2,1)S(1)}, u32[]{:S(2)}, u32[]{:S(2)}) collective-permute-start(bf16[64,1152]{1,0:T(8,128)(2,1)S(1)} %get-tuple-element.50.refs_5_.refs_8_), channel_id=1, source_target_pairs={{0,4},{2,6},{4,0},{6,2},{1,5},{3,7},{5,1},{7,3},{8,12},{10,14},{12... | collective-permute-start | bytes 442376 | tf_op jit(solution)/shard_map/ppermute | solution.py:696
  39.9 1.5 %collective-permute-start.8 = (bf16[2,3,16,1024]{3,2,1,0:T(8,128)(2,1)S(1)}, bf16[2,3,16,1024]{3,2,1,0:T(8,128)(2,1)S(1)}, u32[]{:S(2)}, u32[]{:S(2)}) collective-permute-start(bf16[2,3,16,1024]{3,2,1,0:T(8,128)(2,1)S(1)} %get-tuple-element.43), channel_id=1, source_target_pairs={{0,16},{8,24},{16,0},{24,8},{1,17},{9,25},{17,1},{25,9},{2,18},{10... | collective-permute-start | bytes 589832 | tf_op jit(solution)/shard_map/ppermute | solution.py:696
  41.4 3.5 %all-to-all-start.1 = ((bf16[8,16,2048]{2,1,0:T(8,128)(2,1)}), bf16[8,16,2048]{2,1,0:T(8,128)(2,1)S(1)}, u32[]{:S(2)}, u32[]{:S(2)}) async-start(bf16[8,16,2048]{2,1,0:T(8,128)(2,1)} %bitcast.12), calls=%async_computation.1 | async-start | bytes 1048576 | tf_op jit(solution)/shard_map/all_to_all | solution.py:802
  44.9 0.5 collective-permute-start.12
  45.4 3.1 %collective-permute-start.16 = (bf16[64,1152]{1,0:T(8,128)(2,1)S(1)}, bf16[64,1152]{1,0:T(8,128)(2,1)S(1)}, u32[]{:S(2)}, u32[]{:S(2)}) collective-permute-start(bf16[64,1152]{1,0:T(8,128)(2,1)S(1)} %get-tuple-element.50.refs_5_.refs_8_), channel_id=1, source_target_pairs={{0,6},{2,4},{4,2},{6,0},{1,7},{3,5},{5,3},{7,1},{8,14},{10,12},{12... | collective-permute-start | bytes 442376 | tf_op jit(solution)/shard_map/ppermute | solution.py:696
  48.6 0.5 collective-permute-start.18
  49.2 4.0 %collective-permute-done.16.refs_11_ = bf16[64,1152]{1,0:T(8,128)(2,1)S(1)} collective-permute-done((bf16[64,1152]{1,0:T(8,128)(2,1)S(1)}, bf16[64,1152]{1,0:T(8,128)(2,1)S(1)}, u32[]{:S(2)}, u32[]{:S(2)}) %collective-permute-start.16) | collective-permute-done | bytes 147488 | tf_op jit(solution)/shard_map/ppermute | solution.py:696
  53.2 0.5 collective-permute-start.14
  53.8 0.4 collective-permute-start.20
  54.2 0.4 collective-permute-done.13.refs_5_
  54.6 0.3 collective-permute-done.14.refs_6_
  54.9 0.3 collective-permute-done.15.refs_7_
  55.2 0.3 collective-permute-done.20.refs_15_
  55.7 0.2 copy-done.13
  55.9 0.5 copy-done.6
  56.3 0.8 %copy-done.7 = bf16[2,7,16,1024]{3,2,1,0:T(8,128)(2,1)} copy-done((bf16[2,7,16,1024]{3,2,1,0:T(8,128)(2,1)}, bf16[2,7,16,1024]{3,2,1,0:T(8,128)(2,1)S(1)}, u32[]{:S(2)}) %copy-start.7) | copy-done | bytes 458776
  57.1 5.8 %gradients.1 = (bf16[16,4,2048]{2,1,0:T(4,128)(2,1)}, bf16[1024,256]{1,0:T(8,128)(2,1)}, bf16[256,1024]{1,0:T(8,128)(2,1)}) custom-call(bf16[2,7,16,1024]{3,2,1,0:T(8,128)(2,1)} %copy-done.3, bf16[2,3,16,1024]{3,2,1,0:T(8,128)(2,1)} %copy-done.8, bf16[2,3,16,1024]{3,2,1,0:T(8,128)(2,1)} %copy-done.10, bf16[2,3,16,1024]{3,2,1,0:T(8,128)(2,1)} %copy-done.9, ...), custom_call_target="tpu_custom_call" | custom-call | bytes 1048576 | tf_op jit(solution)/shard_map/gradients/pallas_call | solution.py:808
  (57 shorter events, 0.4 us)
Async XLA Ops:
  0.6 8.3 %copy-start.4 = (bf16[1,1,4096]{2,1,0:T(2,128)(2,1)S(1)}, bf16[1,1,4096]{2,1,0:T(2,128)(2,1)}, u32[]{:S(2)}) copy-start(bf16[1,1,4096]{2,1,0:T(2,128)(2,1)} %param.11) | copy-start | bytes 24580
  0.6 17.4 %collective-permute-start = (bf16[4096,256]{1,0:T(8,128)(2,1)}, bf16[4096,256]{1,0:T(8,128)(2,1)}, u32[]{:S(2)}, u32[]{:S(2)}) collective-permute-start(bf16[4096,256]{1,0:T(8,128)(2,1)} %bitcast.9), channel_id=1, source_target_pairs={{0,1},{1,0},{2,3},{3,2},{4,5},{5,4},{6,7},{7,6},{8,9},{9,8},{10,11... | collective-permute-start | bytes 6291464 | tf_op jit(solution)/shard_map/ppermute | solution.py:696
  1.2 23.2 %collective-permute-start.1 = (bf16[256,4096]{1,0:T(8,128)(2,1)}, bf16[256,4096]{1,0:T(8,128)(2,1)}, u32[]{:S(2)}, u32[]{:S(2)}) collective-permute-start(bf16[256,4096]{1,0:T(8,128)(2,1)} %bitcast.16), channel_id=1, source_target_pairs={{0,1},{1,0},{2,3},{3,2},{4,5},{5,4},{6,7},{7,6},{8,9},{9,8},{10,11... | collective-permute-start | bytes 6291464 | tf_op jit(solution)/shard_map/ppermute | solution.py:696
  3.6 20.7 %copy-start = (bf16[1,1,4096,256]{3,2,1,0:T(8,128)(2,1)S(1)}, bf16[1,1,4096,256]{3,2,1,0:T(8,128)(2,1)}, u32[]{:S(2)}) copy-start(bf16[1,1,4096,256]{3,2,1,0:T(8,128)(2,1)} %param.9) | copy-start | bytes 6291460
  3.6 20.7 %all-to-all-start = ((bf16[8,2,16,2048]{3,2,1,0:T(8,128)(2,1)}), bf16[8,2,16,2048]{3,2,1,0:T(8,128)(2,1)S(1)}, u32[]{:S(2)}, u32[]{:S(2)}) async-start(bf16[8,2,16,2048]{3,2,1,0:T(8,128)(2,1)} %pack.1._), calls=%async_computation | async-start | bytes 2097152 | tf_op jit(solution)/shard_map/all_to_all | solution.py:757
  8.9 7.5 %collective-permute-start.2 = (bf16[1,4096]{1,0:T(2,128)(2,1)S(1)}, bf16[1,4096]{1,0:T(2,128)(2,1)S(1)}, u32[]{:S(2)}, u32[]{:S(2)}) collective-permute-start(bf16[1,4096]{1,0:T(2,128)(2,1)S(1)} %bitcast.14), channel_id=1, source_target_pairs={{0,1},{1,0},{2,3},{3,2},{4,5},{5,4},{6,7},{7,6},{8,9},{9,8},{10,11... | collective-permute-start | bytes 24584 | tf_op jit(solution)/shard_map/ppermute | solution.py:696
  11.7 19.8 %collective-permute-start.3 = (bf16[80,1024]{1,0:T(8,128)(2,1)}, bf16[80,1024]{1,0:T(8,128)(2,1)S(1)}, u32[]{:S(2)}, u32[]{:S(2)}) collective-permute-start(bf16[80,1024]{1,0:T(8,128)(2,1)} %get-tuple-element.31), channel_id=1, source_target_pairs={{0,0},{1,4},{2,2},{3,6},{4,1},{5,5},{6,3},{7,7},{8,8},{9,12},{10,1... | collective-permute-start | bytes 491528 | tf_op jit(solution)/shard_map/ppermute | solution.py:760
  13.3 18.2 %collective-permute-start.4 = (bf16[80,1024]{1,0:T(8,128)(2,1)}, bf16[80,1024]{1,0:T(8,128)(2,1)}, u32[]{:S(2)}, u32[]{:S(2)}) collective-permute-start(bf16[80,1024]{1,0:T(8,128)(2,1)} %get-tuple-element.32), channel_id=1, source_target_pairs={{0,1},{1,5},{2,3},{3,7},{4,0},{5,4},{6,2},{7,6},{8,9},{9,13},{10,1... | collective-permute-start | bytes 491528 | tf_op jit(solution)/shard_map/ppermute | solution.py:760
  16.4 15.0 %copy-start.5 = (bf16[1,4096]{1,0:T(2,128)(2,1)}, bf16[1,4096]{1,0:T(2,128)(2,1)S(1)}, u32[]{:S(2)}) copy-start(bf16[1,4096]{1,0:T(2,128)(2,1)S(1)} %collective-permute-done.2.other_gain.refs_21_) | copy-start | bytes 24580
  16.4 15.1 %collective-permute-start.5 = (bf16[80,1024]{1,0:T(8,128)(2,1)}, bf16[80,1024]{1,0:T(8,128)(2,1)}, u32[]{:S(2)}, u32[]{:S(2)}) collective-permute-start(bf16[80,1024]{1,0:T(8,128)(2,1)} %get-tuple-element.33), channel_id=1, source_target_pairs={{0,2},{1,6},{2,0},{3,4},{4,3},{5,7},{6,1},{7,5},{8,10},{9,14},{10,... | collective-permute-start | bytes 491528 | tf_op jit(solution)/shard_map/ppermute | solution.py:760
  18.0 13.5 %collective-permute-start.6 = (bf16[80,1024]{1,0:T(8,128)(2,1)}, bf16[80,1024]{1,0:T(8,128)(2,1)}, u32[]{:S(2)}, u32[]{:S(2)}) collective-permute-start(bf16[80,1024]{1,0:T(8,128)(2,1)} %get-tuple-element.34), channel_id=1, source_target_pairs={{0,3},{1,7},{2,1},{3,5},{4,2},{5,6},{6,0},{7,4},{8,11},{9,15},{10,... | collective-permute-start | bytes 491528 | tf_op jit(solution)/shard_map/ppermute | solution.py:760
  31.5 10.0 %copy-start.2 = (bf16[4,2,16,2048]{3,2,1,0:T(8,128)(2,1)}, bf16[4,2,16,2048]{3,2,1,0:T(8,128)(2,1)S(1)}, u32[]{:S(2)}) copy-start(bf16[4,2,16,2048]{3,2,1,0:T(8,128)(2,1)S(1)} %get-tuple-element.53) | copy-start | bytes 1572868
  31.5 24.1 %copy-start.1 = (bf16[64,1152]{1,0:T(8,128)(2,1)}, bf16[64,1152]{1,0:T(8,128)(2,1)S(1)}, u32[]{:S(2)}) copy-start(bf16[64,1152]{1,0:T(8,128)(2,1)S(1)} %get-tuple-element.50.refs_5_.refs_8_) | copy-start | bytes 442372
  33.7 21.9 %copy-start.3 = (bf16[2,7,16,1024]{3,2,1,0:T(8,128)(2,1)}, bf16[2,7,16,1024]{3,2,1,0:T(8,128)(2,1)S(1)}, u32[]{:S(2)}) copy-start(bf16[2,7,16,1024]{3,2,1,0:T(8,128)(2,1)S(1)} %get-tuple-element.41.refs_0_) | copy-start | bytes 1376260
  33.7 11.2 %collective-permute-start.7 = (bf16[2,3,16,1024]{3,2,1,0:T(8,128)(2,1)S(1)}, bf16[2,3,16,1024]{3,2,1,0:T(8,128)(2,1)S(1)}, u32[]{:S(2)}, u32[]{:S(2)}) collective-permute-start(bf16[2,3,16,1024]{3,2,1,0:T(8,128)(2,1)S(1)} %get-tuple-element.40), channel_id=1, source_target_pairs={{0,8},{8,0},{16,24},{24,16},{1,9},{9,1},{17,25},{25,17},{2,10},{10... | collective-permute-start | bytes 589832 | tf_op jit(solution)/shard_map/ppermute | solution.py:696
  34.3 7.1 %collective-permute-start.9 = (bf16[64,1152]{1,0:T(8,128)(2,1)S(1)}, bf16[64,1152]{1,0:T(8,128)(2,1)S(1)}, u32[]{:S(2)}, u32[]{:S(2)}) collective-permute-start(bf16[64,1152]{1,0:T(8,128)(2,1)S(1)} %get-tuple-element.50.refs_5_.refs_8_), channel_id=1, source_target_pairs={{0,2},{2,0},{4,6},{6,4},{1,3},{3,1},{5,7},{7,5},{8,10},{10,8},{12,... | collective-permute-start | bytes 442376 | tf_op jit(solution)/shard_map/ppermute | solution.py:696
  36.6 11.9 %collective-permute-start.11 = (bf16[2,3,16,1024]{3,2,1,0:T(8,128)(2,1)S(1)}, bf16[2,3,16,1024]{3,2,1,0:T(8,128)(2,1)S(1)}, u32[]{:S(2)}, u32[]{:S(2)}) collective-permute-start(bf16[2,3,16,1024]{3,2,1,0:T(8,128)(2,1)S(1)} %get-tuple-element.48), channel_id=1, source_target_pairs={{0,24},{8,16},{16,8},{24,0},{1,25},{9,17},{17,9},{25,1},{2,26},{10... | collective-permute-start | bytes 589832 | tf_op jit(solution)/shard_map/ppermute | solution.py:696
  38.1 10.4 %collective-permute-start.10 = (bf16[64,1152]{1,0:T(8,128)(2,1)S(1)}, bf16[64,1152]{1,0:T(8,128)(2,1)S(1)}, u32[]{:S(2)}, u32[]{:S(2)}) collective-permute-start(bf16[64,1152]{1,0:T(8,128)(2,1)S(1)} %get-tuple-element.50.refs_5_.refs_8_), channel_id=1, source_target_pairs={{0,4},{2,6},{4,0},{6,2},{1,5},{3,7},{5,1},{7,3},{8,12},{10,14},{12... | collective-permute-start | bytes 442376 | tf_op jit(solution)/shard_map/ppermute | solution.py:696
  39.9 9.2 %collective-permute-start.8 = (bf16[2,3,16,1024]{3,2,1,0:T(8,128)(2,1)S(1)}, bf16[2,3,16,1024]{3,2,1,0:T(8,128)(2,1)S(1)}, u32[]{:S(2)}, u32[]{:S(2)}) collective-permute-start(bf16[2,3,16,1024]{3,2,1,0:T(8,128)(2,1)S(1)} %get-tuple-element.43), channel_id=1, source_target_pairs={{0,16},{8,24},{16,0},{24,8},{1,17},{9,25},{17,1},{25,9},{2,18},{10... | collective-permute-start | bytes 589832 | tf_op jit(solution)/shard_map/ppermute | solution.py:696
  41.4 14.2 %copy-start.14 = (bf16[64,1152]{1,0:T(8,128)(2,1)}, bf16[64,1152]{1,0:T(8,128)(2,1)S(1)}, u32[]{:S(2)}) copy-start(bf16[64,1152]{1,0:T(8,128)(2,1)S(1)} %collective-permute-done.9.refs_9_) | copy-start | bytes 442372
  41.4 14.1 %all-to-all-start.1 = ((bf16[8,16,2048]{2,1,0:T(8,128)(2,1)}), bf16[8,16,2048]{2,1,0:T(8,128)(2,1)S(1)}, u32[]{:S(2)}, u32[]{:S(2)}) async-start(bf16[8,16,2048]{2,1,0:T(8,128)(2,1)} %bitcast.12), calls=%async_computation.1 | async-start | bytes 1048576 | tf_op jit(solution)/shard_map/all_to_all | solution.py:802
  44.9 10.6 %copy-start.8 = (bf16[2,3,16,1024]{3,2,1,0:T(8,128)(2,1)}, bf16[2,3,16,1024]{3,2,1,0:T(8,128)(2,1)S(1)}, u32[]{:S(2)}) copy-start(bf16[2,3,16,1024]{3,2,1,0:T(8,128)(2,1)S(1)} %collective-permute-done.7.refs_1_) | copy-start | bytes 589828
  44.9 10.6 %collective-permute-start.12 = (bf16[2,7,16,1024]{3,2,1,0:T(8,128)(2,1)S(1)}, bf16[2,7,16,1024]{3,2,1,0:T(8,128)(2,1)S(1)}, u32[]{:S(2)}, u32[]{:S(2)}) collective-permute-start(bf16[2,7,16,1024]{3,2,1,0:T(8,128)(2,1)S(1)} %get-tuple-element.41.refs_0_), channel_id=1, source_target_pairs={{0,1},{1,0},{2,3},{3,2},{4,5},{5,4},{6,7},{7,6},{8,9},{9,8},{10,11... | collective-permute-start | bytes 1376264 | tf_op jit(solution)/shard_map/ppermute | solution.py:696
  45.4 7.8 %collective-permute-start.16 = (bf16[64,1152]{1,0:T(8,128)(2,1)S(1)}, bf16[64,1152]{1,0:T(8,128)(2,1)S(1)}, u32[]{:S(2)}, u32[]{:S(2)}) collective-permute-start(bf16[64,1152]{1,0:T(8,128)(2,1)S(1)} %get-tuple-element.50.refs_5_.refs_8_), channel_id=1, source_target_pairs={{0,6},{2,4},{4,2},{6,0},{1,7},{3,5},{5,3},{7,1},{8,14},{10,12},{12... | collective-permute-start | bytes 442376 | tf_op jit(solution)/shard_map/ppermute | solution.py:696
  48.5 7.1 %copy-start.9 = (bf16[2,3,16,1024]{3,2,1,0:T(8,128)(2,1)}, bf16[2,3,16,1024]{3,2,1,0:T(8,128)(2,1)S(1)}, u32[]{:S(2)}) copy-start(bf16[2,3,16,1024]{3,2,1,0:T(8,128)(2,1)S(1)} %collective-permute-done.11.refs_3_) | copy-start | bytes 589828
  48.5 4.7 %collective-permute-start.17 = (bf16[64,1152]{1,0:T(8,128)(2,1)S(1)}, bf16[64,1152]{1,0:T(8,128)(2,1)S(1)}, u32[]{:S(2)}, u32[]{:S(2)}) collective-permute-start(bf16[64,1152]{1,0:T(8,128)(2,1)S(1)} %get-tuple-element.50.refs_5_.refs_8_), channel_id=1, source_target_pairs={{0,1},{1,0},{2,3},{3,2},{4,5},{5,4},{6,7},{7,6},{8,9},{9,8},{10,11... | collective-permute-start | bytes 442376 | tf_op jit(solution)/shard_map/ppermute | solution.py:696
  48.6 5.1 %collective-permute-start.18 = (bf16[64,1152]{1,0:T(8,128)(2,1)S(1)}, bf16[64,1152]{1,0:T(8,128)(2,1)}, u32[]{:S(2)}, u32[]{:S(2)}) collective-permute-start(bf16[64,1152]{1,0:T(8,128)(2,1)S(1)} %collective-permute-done.9.refs_9_), channel_id=1, source_target_pairs={{0,1},{1,0},{2,3},{3,2},{4,5},{5,4},{6,7},{7,6},{8,9},{9,8},{10,11... | collective-permute-start | bytes 442376 | tf_op jit(solution)/shard_map/ppermute | solution.py:696
  49.1 4.7 %collective-permute-start.19 = (bf16[64,1152]{1,0:T(8,128)(2,1)S(1)}, bf16[64,1152]{1,0:T(8,128)(2,1)S(1)}, u32[]{:S(2)}, u32[]{:S(2)}) collective-permute-start(bf16[64,1152]{1,0:T(8,128)(2,1)S(1)} %collective-permute-done.10.refs_10_), channel_id=1, source_target_pairs={{0,1},{1,0},{2,3},{3,2},{4,5},{5,4},{6,7},{7,6},{8,9},{9,8},{10,11... | collective-permute-start | bytes 442376 | tf_op jit(solution)/shard_map/ppermute | solution.py:696
  53.2 1.4 %collective-permute-start.13 = (bf16[2,3,16,1024]{3,2,1,0:T(8,128)(2,1)S(1)}, bf16[2,3,16,1024]{3,2,1,0:T(8,128)(2,1)S(1)}, u32[]{:S(2)}, u32[]{:S(2)}) collective-permute-start(bf16[2,3,16,1024]{3,2,1,0:T(8,128)(2,1)S(1)} %collective-permute-done.7.refs_1_), channel_id=1, source_target_pairs={{0,1},{1,0},{2,3},{3,2},{4,5},{5,4},{6,7},{7,6},{8,9},{9,8},{10,11... | collective-permute-start | bytes 589832 | tf_op jit(solution)/shard_map/ppermute | solution.py:696
  53.2 1.7 %collective-permute-start.14 = (bf16[2,3,16,1024]{3,2,1,0:T(8,128)(2,1)S(1)}, bf16[2,3,16,1024]{3,2,1,0:T(8,128)(2,1)S(1)}, u32[]{:S(2)}, u32[]{:S(2)}) collective-permute-start(bf16[2,3,16,1024]{3,2,1,0:T(8,128)(2,1)S(1)} %collective-permute-done.8.refs_2_), channel_id=1, source_target_pairs={{0,1},{1,0},{2,3},{3,2},{4,5},{5,4},{6,7},{7,6},{8,9},{9,8},{10,11... | collective-permute-start | bytes 589832 | tf_op jit(solution)/shard_map/ppermute | solution.py:696
  53.7 1.5 %collective-permute-start.15 = (bf16[2,3,16,1024]{3,2,1,0:T(8,128)(2,1)S(1)}, bf16[2,3,16,1024]{3,2,1,0:T(8,128)(2,1)S(1)}, u32[]{:S(2)}, u32[]{:S(2)}) collective-permute-start(bf16[2,3,16,1024]{3,2,1,0:T(8,128)(2,1)S(1)} %collective-permute-done.11.refs_3_), channel_id=1, source_target_pairs={{0,1},{1,0},{2,3},{3,2},{4,5},{5,4},{6,7},{7,6},{8,9},{9,8},{10,11... | collective-permute-start | bytes 589832 | tf_op jit(solution)/shard_map/ppermute | solution.py:696
  53.8 1.7 %collective-permute-start.20 = (bf16[64,1152]{1,0:T(8,128)(2,1)S(1)}, bf16[64,1152]{1,0:T(8,128)(2,1)}, u32[]{:S(2)}, u32[]{:S(2)}) collective-permute-start(bf16[64,1152]{1,0:T(8,128)(2,1)S(1)} %collective-permute-done.16.refs_11_), channel_id=1, source_target_pairs={{0,1},{1,0},{2,3},{3,2},{4,5},{5,4},{6,7},{7,6},{8,9},{9,8},{10,11... | collective-permute-start | bytes 442376 | tf_op jit(solution)/shard_map/ppermute | solution.py:696
  (10 other events, 23.8 us)

commit v18 on v15

--- a/solution.py
+++ b/solution.py
@@ -791,11 +791,11 @@
     small, *slices = lax.optimization_barrier((small, *slices))
     mine = [slices[0]] + [across(slices[step], "expert", step) for step in range(1, experts)]
     mine[:2] = lax.optimization_barrier(tuple(mine[:2]))
-    near = [small] + [across(small, "dp", step) for step in range(1, replicas - 1)]
+    near = [small] + [across(small, "dp", step) for step in range(2, replicas)]
     near[:2] = lax.optimization_barrier(tuple(near[:2]))
-    last = across(near[0], "dp", replicas - 1)
+    beside = across(near[0], "dp", 1)
     *near, mine[-1] = lax.optimization_barrier((*near, mine[-1]))
-    near.append(last)
+    near.insert(1, beside)
     theirs = [across(block, "segment", 1) for block in mine]
     smalls = near + [across(piece, "segment", 1) for piece in near]
 

time: 63.3 us -> 64.9 us (1.025)
  waiting for transfers between devices: 14.6 us -> 16.1 us
    ppermute x17, waiting for transfers between devices: 8.27 us -> 9.76 us  [across(): return lax.ppermute(block, axis, [(i, i ^ distance) for i in range(size)])]
  transfers between devices with their start and end apart: 23 -> 23, of which waited for: 7 -> 7; matrix products, arithmetic and copies ran while one was open for 0% -> 0% of each run, Pallas kernels for 19% -> 18%
where the time goes in v18:
time: 64.9 us; the launch traced here: 64.5 us
  starting transfers between devices  26.3 us (41%)
  Pallas kernels  19.7 us (30%)
  waiting for transfers between devices  16.1 us (25%)
  local copies, waits for them, and re-layouts  1.52 us (2%)
  between operations  0.9 us (1%)
    ppermute x17, starting transfers between devices, across(): return lax.ppermute(block, axis, [(i, i ^ distance) for i in range(size)])  11.2 us
    ppermute x17, waiting for transfers between devices, across(): return lax.ppermute(block, axis, [(i, i ^ distance) for i in range(size)])  9.76 us
    pallas_call x1, Pallas kernels, on_device_two_phases(): call(chain_kernel, 'chain', 50, [HBM] * 7, [((experts, 2, rows, part), bf...  7.1 us
    all_to_all x1, waiting for transfers between devices, on_device_two_phases(): lax.all_to_all(send, sections, split_axis=0, concat_axis=0, tiled=True)  6.33 us
    ppermute x4, starting transfers between devices, on_device_two_phases(): lax.ppermute(block, ('dp', 'segment'), slab_route(replicas, turn // 2, tu...  6.29 us
    pallas_call x1, Pallas kernels, on_device_two_phases(): call(functools.partial(gradient_kernel, experts, sources, sizes), 'gradie...  5.83 us
    all_to_all x1, starting transfers between devices, on_device_two_phases(): lax.all_to_all(send, sections, split_axis=0, concat_axis=0, tiled=True)  5.29 us
    all_to_all x1, starting transfers between devices, on_device_two_phases(): lax.all_to_all(out.reshape(groups, rows, part), sections, split_axis=0, c...  3.51 us
  transfers between devices with their start and end apart: 23, of which 7 were waited for; matrix products, arithmetic and copies ran while one was open for 0% of the time, Pallas kernels for 18%

profile of v18, /device:TPU:0, one launch (start us, length us, event | category | flops | bytes accessed | tf_op | source)
XLA Modules:
  0.0 64.5 jit_solution(12307454207640612472)
XLA Ops:
  0.6 0.5 collective-permute-start
  1.2 2.4 %pack.1._ = bf16[8,2,16,2048]{3,2,1,0:T(8,128)(2,1)} custom-call(s32[16]{0:T(128)} %refs_22_.1, bf16[16,4,2048]{2,1,0:T(4,128)(2,1)} %hidden.3, bf16[16,4,2048]{2,1,0:T(4,128)(2,1)} %cot.3), custom_call_target="tpu_custom_call" | custom-call | bytes 1048576 | tf_op jit(solution)/shard_map/pack/pallas_call | solution.py:727
  3.6 5.3 %all-to-all-start = ((bf16[8,2,16,2048]{3,2,1,0:T(8,128)(2,1)}), bf16[8,2,16,2048]{3,2,1,0:T(8,128)(2,1)S(1)}, u32[]{:S(2)}, u32[]{:S(2)}) async-start(bf16[8,2,16,2048]{3,2,1,0:T(8,128)(2,1)} %pack.1._), calls=%async_computation | async-start | bytes 2097152 | tf_op jit(solution)/shard_map/all_to_all | solution.py:757
  8.9 0.5 collective-permute-start.2
  9.4 2.3 %slabs.1 = (bf16[80,1024]{1,0:T(8,128)(2,1)}, bf16[80,1024]{1,0:T(8,128)(2,1)}, bf16[80,1024]{1,0:T(8,128)(2,1)}, bf16[80,1024]{1,0:T(8,128)(2,1)}) custom-call(s32[16]{0:T(128)} %refs_22_.1, bf16[16,4,2048]{2,1,0:T(4,128)(2,1)} %hidden.3, bf16[16,4,2048]{2,1,0:T(4,128)(2,1)} %cot.3, bf16[8,2,16,2048]{3,2,1,0:T(8,128)(2,1)} %pack.1._), custom_call_target="tpu_custom_call" | custom-call | bytes 1048576 | tf_op jit(solution)/shard_map/slabs/pallas_call | solution.py:741
  11.7 1.6 %collective-permute-start.3 = (bf16[80,1024]{1,0:T(8,128)(2,1)}, bf16[80,1024]{1,0:T(8,128)(2,1)S(1)}, u32[]{:S(2)}, u32[]{:S(2)}) collective-permute-start(bf16[80,1024]{1,0:T(8,128)(2,1)} %get-tuple-element.30), channel_id=1, source_target_pairs={{0,0},{1,4},{2,2},{3,6},{4,1},{5,5},{6,3},{7,7},{8,8},{9,12},{10,1... | collective-permute-start | bytes 491528 | tf_op jit(solution)/shard_map/ppermute | solution.py:760
  13.3 3.1 %collective-permute-start.4 = (bf16[80,1024]{1,0:T(8,128)(2,1)}, bf16[80,1024]{1,0:T(8,128)(2,1)}, u32[]{:S(2)}, u32[]{:S(2)}) collective-permute-start(bf16[80,1024]{1,0:T(8,128)(2,1)} %get-tuple-element.31), channel_id=1, source_target_pairs={{0,1},{1,5},{2,3},{3,7},{4,0},{5,4},{6,2},{7,6},{8,9},{9,13},{10,1... | collective-permute-start | bytes 491528 | tf_op jit(solution)/shard_map/ppermute | solution.py:760
  16.4 1.6 %collective-permute-start.5 = (bf16[80,1024]{1,0:T(8,128)(2,1)}, bf16[80,1024]{1,0:T(8,128)(2,1)}, u32[]{:S(2)}, u32[]{:S(2)}) collective-permute-start(bf16[80,1024]{1,0:T(8,128)(2,1)} %get-tuple-element.32), channel_id=1, source_target_pairs={{0,2},{1,6},{2,0},{3,4},{4,3},{5,7},{6,1},{7,5},{8,10},{9,14},{10,... | collective-permute-start | bytes 491528 | tf_op jit(solution)/shard_map/ppermute | solution.py:760
  18.0 6.3 %all-to-all-done = bf16[8,2,16,2048]{3,2,1,0:T(8,128)(2,1)S(1)} async-done(((bf16[8,2,16,2048]{3,2,1,0:T(8,128)(2,1)}), bf16[8,2,16,2048]{3,2,1,0:T(8,128)(2,1)S(1)}, u32[]{:S(2)}, u32[]{:S(2)}) %all-to-all-start) | async-done | bytes 1048608 | tf_op jit(solution)/shard_map/all_to_all | solution.py:757
  24.3 7.1 %chain.1 = (bf16[4,2,16,2048]{3,2,1,0:T(8,128)(2,1)S(1)}, bf16[64,1152]{1,0:T(8,128)(2,1)S(1)}) custom-call(bf16[4,2,2,16,2048]{4,3,2,1,0:T(8,128)(2,1)S(1)} %bitcast.7, bf16[4096,256]{1,0:T(8,128)(2,1)S(1)} %bitcast.11, bf16[256,4096]{1,0:T(8,128)(2,1)} %bitcast.17, bf16[1,4096]{1,0:T(2,128)(2,1)S(1)} %bitcast.15, ...), custom_call_target="tpu_custom_call" | custom-call | flops 939524096 | bytes 10485760 | tf_op jit(solution)/shard_map/chain/pallas_call | solution.py:763
  31.5 2.2 %repack.1 = (bf16[2,7,16,1024]{3,2,1,0:T(8,128)(2,1)S(1)}, bf16[2,3,16,1024]{3,2,1,0:T(8,128)(2,1)S(1)}, bf16[2,3,16,1024]{3,2,1,0:T(8,128)(2,1)S(1)}, bf16[2,3,16,1024]{3,2,1,0:T(8,128)(2,1)S(1)}) custom-call(bf16[80,1024]{1,0:T(8,128)(2,1)S(1)} %collective-permute-done.3.refs_0_, bf16[80,1024]{1,0:T(8,128)(2,1)} %collective-permute-done.4.refs_1_, ...), custom_call_target="tpu_custom_call" | custom-call | bytes 1048576 | tf_op jit(solution)/shard_map/repack/pallas_call | solution.py:782
  33.7 0.6 collective-permute-start.7
  34.3 1.5 %collective-permute-start.11 = (bf16[2,3,16,1024]{3,2,1,0:T(8,128)(2,1)S(1)}, bf16[2,3,16,1024]{3,2,1,0:T(8,128)(2,1)S(1)}, u32[]{:S(2)}, u32[]{:S(2)}) collective-permute-start(bf16[2,3,16,1024]{3,2,1,0:T(8,128)(2,1)S(1)} %get-tuple-element.46), channel_id=1, source_target_pairs={{0,24},{8,16},{16,8},{24,0},{1,25},{9,17},{17,9},{25,1},{2,26},{10... | collective-permute-start | bytes 589832 | tf_op jit(solution)/shard_map/ppermute | solution.py:696
  35.8 2.6 %collective-permute-start.9 = (bf16[64,1152]{1,0:T(8,128)(2,1)S(1)}, bf16[64,1152]{1,0:T(8,128)(2,1)S(1)}, u32[]{:S(2)}, u32[]{:S(2)}) collective-permute-start(bf16[64,1152]{1,0:T(8,128)(2,1)S(1)} %get-tuple-element.48.refs_5_.refs_8_), channel_id=1, source_target_pairs={{0,4},{2,6},{4,0},{6,2},{1,5},{3,7},{5,1},{7,3},{8,12},{10,14},{12... | collective-permute-start | bytes 442376 | tf_op jit(solution)/shard_map/ppermute | solution.py:696
  38.4 2.1 %collective-permute-start.10 = (bf16[64,1152]{1,0:T(8,128)(2,1)S(1)}, bf16[64,1152]{1,0:T(8,128)(2,1)S(1)}, u32[]{:S(2)}, u32[]{:S(2)}) collective-permute-start(bf16[64,1152]{1,0:T(8,128)(2,1)S(1)} %get-tuple-element.48.refs_5_.refs_8_), channel_id=1, source_target_pairs={{0,6},{2,4},{4,2},{6,0},{1,7},{3,5},{5,3},{7,1},{8,14},{10,12},{12... | collective-permute-start | bytes 442376 | tf_op jit(solution)/shard_map/ppermute | solution.py:696
  40.5 0.7 %collective-permute-start.8 = (bf16[2,3,16,1024]{3,2,1,0:T(8,128)(2,1)S(1)}, bf16[2,3,16,1024]{3,2,1,0:T(8,128)(2,1)S(1)}, u32[]{:S(2)}, u32[]{:S(2)}) collective-permute-start(bf16[2,3,16,1024]{3,2,1,0:T(8,128)(2,1)S(1)} %get-tuple-element.42), channel_id=1, source_target_pairs={{0,16},{8,24},{16,0},{24,8},{1,17},{9,25},{17,1},{25,9},{2,18},{10... | collective-permute-start | bytes 589832 | tf_op jit(solution)/shard_map/ppermute | solution.py:696
  41.2 3.5 %all-to-all-start.1 = ((bf16[8,16,2048]{2,1,0:T(8,128)(2,1)}), bf16[8,16,2048]{2,1,0:T(8,128)(2,1)S(1)}, u32[]{:S(2)}, u32[]{:S(2)}) async-start(bf16[8,16,2048]{2,1,0:T(8,128)(2,1)} %bitcast.12), calls=%async_computation.1 | async-start | bytes 1048576 | tf_op jit(solution)/shard_map/all_to_all | solution.py:802
  44.7 0.6 collective-permute-start.12
  45.3 4.4 %collective-permute-done.9.refs_10_ = bf16[64,1152]{1,0:T(8,128)(2,1)S(1)} collective-permute-done((bf16[64,1152]{1,0:T(8,128)(2,1)S(1)}, bf16[64,1152]{1,0:T(8,128)(2,1)S(1)}, u32[]{:S(2)}, u32[]{:S(2)}) %collective-permute-start.9) | collective-permute-done | bytes 147488 | tf_op jit(solution)/shard_map/ppermute | solution.py:696
  49.6 0.4 collective-permute-start.16
  50.1 0.5 collective-permute-start.19
  50.7 4.1 %collective-permute-done.16.refs_9_ = bf16[64,1152]{1,0:T(8,128)(2,1)S(1)} collective-permute-done((bf16[64,1152]{1,0:T(8,128)(2,1)S(1)}, bf16[64,1152]{1,0:T(8,128)(2,1)S(1)}, u32[]{:S(2)}, u32[]{:S(2)}) %collective-permute-start.16) | collective-permute-done | bytes 147488 | tf_op jit(solution)/shard_map/ppermute | solution.py:696
  54.8 0.5 collective-permute-start.14
  55.4 0.4 collective-permute-start.18
  55.8 0.4 collective-permute-done.13.refs_5_
  56.2 0.3 collective-permute-done.14.refs_6_
  56.5 0.3 collective-permute-done.15.refs_7_
  56.8 0.3 collective-permute-done.18.refs_13_
  57.3 0.2 copy-done.13
  57.5 0.5 copy-done.6
  57.9 0.8 %copy-done.7 = bf16[2,7,16,1024]{3,2,1,0:T(8,128)(2,1)} copy-done((bf16[2,7,16,1024]{3,2,1,0:T(8,128)(2,1)}, bf16[2,7,16,1024]{3,2,1,0:T(8,128)(2,1)S(1)}, u32[]{:S(2)}) %copy-start.7) | copy-done | bytes 458776
  58.7 5.8 %gradients.1 = (bf16[16,4,2048]{2,1,0:T(4,128)(2,1)}, bf16[1024,256]{1,0:T(8,128)(2,1)}, bf16[256,1024]{1,0:T(8,128)(2,1)}) custom-call(bf16[2,7,16,1024]{3,2,1,0:T(8,128)(2,1)} %copy-done.3, bf16[2,3,16,1024]{3,2,1,0:T(8,128)(2,1)} %copy-done.8, bf16[2,3,16,1024]{3,2,1,0:T(8,128)(2,1)} %copy-done.10, bf16[2,3,16,1024]{3,2,1,0:T(8,128)(2,1)} %copy-done.9, ...), custom_call_target="tpu_custom_call" | custom-call | bytes 1048576 | tf_op jit(solution)/shard_map/gradients/pallas_call | solution.py:808
  (57 shorter events, 0.4 us)
Async XLA Ops:
  0.6 8.3 %copy-start.4 = (bf16[1,1,4096]{2,1,0:T(2,128)(2,1)S(1)}, bf16[1,1,4096]{2,1,0:T(2,128)(2,1)}, u32[]{:S(2)}) copy-start(bf16[1,1,4096]{2,1,0:T(2,128)(2,1)} %param.11) | copy-start | bytes 24580
  0.6 17.4 %collective-permute-start = (bf16[4096,256]{1,0:T(8,128)(2,1)}, bf16[4096,256]{1,0:T(8,128)(2,1)}, u32[]{:S(2)}, u32[]{:S(2)}) collective-permute-start(bf16[4096,256]{1,0:T(8,128)(2,1)} %bitcast.9), channel_id=1, source_target_pairs={{0,1},{1,0},{2,3},{3,2},{4,5},{5,4},{6,7},{7,6},{8,9},{9,8},{10,11... | collective-permute-start | bytes 6291464 | tf_op jit(solution)/shard_map/ppermute | solution.py:696
  1.2 23.2 %collective-permute-start.1 = (bf16[256,4096]{1,0:T(8,128)(2,1)}, bf16[256,4096]{1,0:T(8,128)(2,1)}, u32[]{:S(2)}, u32[]{:S(2)}) collective-permute-start(bf16[256,4096]{1,0:T(8,128)(2,1)} %bitcast.16), channel_id=1, source_target_pairs={{0,1},{1,0},{2,3},{3,2},{4,5},{5,4},{6,7},{7,6},{8,9},{9,8},{10,11... | collective-permute-start | bytes 6291464 | tf_op jit(solution)/shard_map/ppermute | solution.py:696
  3.6 20.7 %copy-start = (bf16[1,1,4096,256]{3,2,1,0:T(8,128)(2,1)S(1)}, bf16[1,1,4096,256]{3,2,1,0:T(8,128)(2,1)}, u32[]{:S(2)}) copy-start(bf16[1,1,4096,256]{3,2,1,0:T(8,128)(2,1)} %param.9) | copy-start | bytes 6291460
  3.6 20.7 %all-to-all-start = ((bf16[8,2,16,2048]{3,2,1,0:T(8,128)(2,1)}), bf16[8,2,16,2048]{3,2,1,0:T(8,128)(2,1)S(1)}, u32[]{:S(2)}, u32[]{:S(2)}) async-start(bf16[8,2,16,2048]{3,2,1,0:T(8,128)(2,1)} %pack.1._), calls=%async_computation | async-start | bytes 2097152 | tf_op jit(solution)/shard_map/all_to_all | solution.py:757
  8.9 7.5 %collective-permute-start.2 = (bf16[1,4096]{1,0:T(2,128)(2,1)S(1)}, bf16[1,4096]{1,0:T(2,128)(2,1)S(1)}, u32[]{:S(2)}, u32[]{:S(2)}) collective-permute-start(bf16[1,4096]{1,0:T(2,128)(2,1)S(1)} %bitcast.14), channel_id=1, source_target_pairs={{0,1},{1,0},{2,3},{3,2},{4,5},{5,4},{6,7},{7,6},{8,9},{9,8},{10,11... | collective-permute-start | bytes 24584 | tf_op jit(solution)/shard_map/ppermute | solution.py:696
  11.7 19.8 %collective-permute-start.3 = (bf16[80,1024]{1,0:T(8,128)(2,1)}, bf16[80,1024]{1,0:T(8,128)(2,1)S(1)}, u32[]{:S(2)}, u32[]{:S(2)}) collective-permute-start(bf16[80,1024]{1,0:T(8,128)(2,1)} %get-tuple-element.30), channel_id=1, source_target_pairs={{0,0},{1,4},{2,2},{3,6},{4,1},{5,5},{6,3},{7,7},{8,8},{9,12},{10,1... | collective-permute-start | bytes 491528 | tf_op jit(solution)/shard_map/ppermute | solution.py:760
  13.3 18.2 %collective-permute-start.4 = (bf16[80,1024]{1,0:T(8,128)(2,1)}, bf16[80,1024]{1,0:T(8,128)(2,1)}, u32[]{:S(2)}, u32[]{:S(2)}) collective-permute-start(bf16[80,1024]{1,0:T(8,128)(2,1)} %get-tuple-element.31), channel_id=1, source_target_pairs={{0,1},{1,5},{2,3},{3,7},{4,0},{5,4},{6,2},{7,6},{8,9},{9,13},{10,1... | collective-permute-start | bytes 491528 | tf_op jit(solution)/shard_map/ppermute | solution.py:760
  16.4 15.0 %copy-start.5 = (bf16[1,4096]{1,0:T(2,128)(2,1)}, bf16[1,4096]{1,0:T(2,128)(2,1)S(1)}, u32[]{:S(2)}) copy-start(bf16[1,4096]{1,0:T(2,128)(2,1)S(1)} %collective-permute-done.2.other_gain.refs_21_) | copy-start | bytes 24580
  16.4 15.1 %collective-permute-start.5 = (bf16[80,1024]{1,0:T(8,128)(2,1)}, bf16[80,1024]{1,0:T(8,128)(2,1)}, u32[]{:S(2)}, u32[]{:S(2)}) collective-permute-start(bf16[80,1024]{1,0:T(8,128)(2,1)} %get-tuple-element.32), channel_id=1, source_target_pairs={{0,2},{1,6},{2,0},{3,4},{4,3},{5,7},{6,1},{7,5},{8,10},{9,14},{10,... | collective-permute-start | bytes 491528 | tf_op jit(solution)/shard_map/ppermute | solution.py:760
  18.0 13.5 %collective-permute-start.6 = (bf16[80,1024]{1,0:T(8,128)(2,1)}, bf16[80,1024]{1,0:T(8,128)(2,1)}, u32[]{:S(2)}, u32[]{:S(2)}) collective-permute-start(bf16[80,1024]{1,0:T(8,128)(2,1)} %get-tuple-element.33), channel_id=1, source_target_pairs={{0,3},{1,7},{2,1},{3,5},{4,2},{5,6},{6,0},{7,4},{8,11},{9,15},{10,... | collective-permute-start | bytes 491528 | tf_op jit(solution)/shard_map/ppermute | solution.py:760
  31.5 9.7 %copy-start.2 = (bf16[4,2,16,2048]{3,2,1,0:T(8,128)(2,1)}, bf16[4,2,16,2048]{3,2,1,0:T(8,128)(2,1)S(1)}, u32[]{:S(2)}) copy-start(bf16[4,2,16,2048]{3,2,1,0:T(8,128)(2,1)S(1)} %get-tuple-element.51) | copy-start | bytes 1572868
  31.5 25.7 %copy-start.1 = (bf16[64,1152]{1,0:T(8,128)(2,1)}, bf16[64,1152]{1,0:T(8,128)(2,1)S(1)}, u32[]{:S(2)}) copy-start(bf16[64,1152]{1,0:T(8,128)(2,1)S(1)} %get-tuple-element.48.refs_5_.refs_8_) | copy-start | bytes 442372
  33.7 23.5 %copy-start.3 = (bf16[2,7,16,1024]{3,2,1,0:T(8,128)(2,1)}, bf16[2,7,16,1024]{3,2,1,0:T(8,128)(2,1)S(1)}, u32[]{:S(2)}) copy-start(bf16[2,7,16,1024]{3,2,1,0:T(8,128)(2,1)S(1)} %get-tuple-element.40.refs_0_) | copy-start | bytes 1376260
  33.7 11.0 %collective-permute-start.7 = (bf16[2,3,16,1024]{3,2,1,0:T(8,128)(2,1)S(1)}, bf16[2,3,16,1024]{3,2,1,0:T(8,128)(2,1)S(1)}, u32[]{:S(2)}, u32[]{:S(2)}) collective-permute-start(bf16[2,3,16,1024]{3,2,1,0:T(8,128)(2,1)S(1)} %get-tuple-element.39), channel_id=1, source_target_pairs={{0,8},{8,0},{16,24},{24,16},{1,9},{9,1},{17,25},{25,17},{2,10},{10... | collective-permute-start | bytes 589832 | tf_op jit(solution)/shard_map/ppermute | solution.py:696
  34.3 15.8 %collective-permute-start.11 = (bf16[2,3,16,1024]{3,2,1,0:T(8,128)(2,1)S(1)}, bf16[2,3,16,1024]{3,2,1,0:T(8,128)(2,1)S(1)}, u32[]{:S(2)}, u32[]{:S(2)}) collective-permute-start(bf16[2,3,16,1024]{3,2,1,0:T(8,128)(2,1)S(1)} %get-tuple-element.46), channel_id=1, source_target_pairs={{0,24},{8,16},{16,8},{24,0},{1,25},{9,17},{17,9},{25,1},{2,26},{10... | collective-permute-start | bytes 589832 | tf_op jit(solution)/shard_map/ppermute | solution.py:696
  35.8 13.9 %collective-permute-start.9 = (bf16[64,1152]{1,0:T(8,128)(2,1)S(1)}, bf16[64,1152]{1,0:T(8,128)(2,1)S(1)}, u32[]{:S(2)}, u32[]{:S(2)}) collective-permute-start(bf16[64,1152]{1,0:T(8,128)(2,1)S(1)} %get-tuple-element.48.refs_5_.refs_8_), channel_id=1, source_target_pairs={{0,4},{2,6},{4,0},{6,2},{1,5},{3,7},{5,1},{7,3},{8,12},{10,14},{12... | collective-permute-start | bytes 442376 | tf_op jit(solution)/shard_map/ppermute | solution.py:696
  38.4 11.7 %collective-permute-start.10 = (bf16[64,1152]{1,0:T(8,128)(2,1)S(1)}, bf16[64,1152]{1,0:T(8,128)(2,1)S(1)}, u32[]{:S(2)}, u32[]{:S(2)}) collective-permute-start(bf16[64,1152]{1,0:T(8,128)(2,1)S(1)} %get-tuple-element.48.refs_5_.refs_8_), channel_id=1, source_target_pairs={{0,6},{2,4},{4,2},{6,0},{1,7},{3,5},{5,3},{7,1},{8,14},{10,12},{12... | collective-permute-start | bytes 442376 | tf_op jit(solution)/shard_map/ppermute | solution.py:696
  40.5 10.1 %collective-permute-start.8 = (bf16[2,3,16,1024]{3,2,1,0:T(8,128)(2,1)S(1)}, bf16[2,3,16,1024]{3,2,1,0:T(8,128)(2,1)S(1)}, u32[]{:S(2)}, u32[]{:S(2)}) collective-permute-start(bf16[2,3,16,1024]{3,2,1,0:T(8,128)(2,1)S(1)} %get-tuple-element.42), channel_id=1, source_target_pairs={{0,16},{8,24},{16,0},{24,8},{1,17},{9,25},{17,1},{25,9},{2,18},{10... | collective-permute-start | bytes 589832 | tf_op jit(solution)/shard_map/ppermute | solution.py:696
  41.2 15.9 %all-to-all-start.1 = ((bf16[8,16,2048]{2,1,0:T(8,128)(2,1)}), bf16[8,16,2048]{2,1,0:T(8,128)(2,1)S(1)}, u32[]{:S(2)}, u32[]{:S(2)}) async-start(bf16[8,16,2048]{2,1,0:T(8,128)(2,1)} %bitcast.12), calls=%async_computation.1 | async-start | bytes 1048576 | tf_op jit(solution)/shard_map/all_to_all | solution.py:802
  44.7 12.5 %copy-start.8 = (bf16[2,3,16,1024]{3,2,1,0:T(8,128)(2,1)}, bf16[2,3,16,1024]{3,2,1,0:T(8,128)(2,1)S(1)}, u32[]{:S(2)}) copy-start(bf16[2,3,16,1024]{3,2,1,0:T(8,128)(2,1)S(1)} %collective-permute-done.7.refs_1_) | copy-start | bytes 589828
  44.7 12.4 %collective-permute-start.12 = (bf16[2,7,16,1024]{3,2,1,0:T(8,128)(2,1)S(1)}, bf16[2,7,16,1024]{3,2,1,0:T(8,128)(2,1)S(1)}, u32[]{:S(2)}, u32[]{:S(2)}) collective-permute-start(bf16[2,7,16,1024]{3,2,1,0:T(8,128)(2,1)S(1)} %get-tuple-element.40.refs_0_), channel_id=1, source_target_pairs={{0,1},{1,0},{2,3},{3,2},{4,5},{5,4},{6,7},{7,6},{8,9},{9,8},{10,11... | collective-permute-start | bytes 1376264 | tf_op jit(solution)/shard_map/ppermute | solution.py:696
  49.6 7.5 %copy-start.14 = (bf16[64,1152]{1,0:T(8,128)(2,1)}, bf16[64,1152]{1,0:T(8,128)(2,1)S(1)}, u32[]{:S(2)}) copy-start(bf16[64,1152]{1,0:T(8,128)(2,1)S(1)} %collective-permute-done.9.refs_10_) | copy-start | bytes 442372
  49.6 5.1 %collective-permute-start.16 = (bf16[64,1152]{1,0:T(8,128)(2,1)S(1)}, bf16[64,1152]{1,0:T(8,128)(2,1)S(1)}, u32[]{:S(2)}, u32[]{:S(2)}) collective-permute-start(bf16[64,1152]{1,0:T(8,128)(2,1)S(1)} %get-tuple-element.48.refs_5_.refs_8_), channel_id=1, source_target_pairs={{0,2},{2,0},{4,6},{6,4},{1,3},{3,1},{5,7},{7,5},{8,10},{10,8},{12,... | collective-permute-start | bytes 442376 | tf_op jit(solution)/shard_map/ppermute | solution.py:696
  50.0 7.2 %copy-start.9 = (bf16[2,3,16,1024]{3,2,1,0:T(8,128)(2,1)}, bf16[2,3,16,1024]{3,2,1,0:T(8,128)(2,1)S(1)}, u32[]{:S(2)}) copy-start(bf16[2,3,16,1024]{3,2,1,0:T(8,128)(2,1)S(1)} %collective-permute-done.11.refs_3_) | copy-start | bytes 589828
  50.0 4.7 %collective-permute-start.17 = (bf16[64,1152]{1,0:T(8,128)(2,1)S(1)}, bf16[64,1152]{1,0:T(8,128)(2,1)S(1)}, u32[]{:S(2)}, u32[]{:S(2)}) collective-permute-start(bf16[64,1152]{1,0:T(8,128)(2,1)S(1)} %get-tuple-element.48.refs_5_.refs_8_), channel_id=1, source_target_pairs={{0,1},{1,0},{2,3},{3,2},{4,5},{5,4},{6,7},{7,6},{8,9},{9,8},{10,11... | collective-permute-start | bytes 442376 | tf_op jit(solution)/shard_map/ppermute | solution.py:696
  50.1 5.2 %collective-permute-start.19 = (bf16[64,1152]{1,0:T(8,128)(2,1)S(1)}, bf16[64,1152]{1,0:T(8,128)(2,1)}, u32[]{:S(2)}, u32[]{:S(2)}) collective-permute-start(bf16[64,1152]{1,0:T(8,128)(2,1)S(1)} %collective-permute-done.9.refs_10_), channel_id=1, source_target_pairs={{0,1},{1,0},{2,3},{3,2},{4,5},{5,4},{6,7},{7,6},{8,9},{9,8},{10,11... | collective-permute-start | bytes 442376 | tf_op jit(solution)/shard_map/ppermute | solution.py:696
  50.6 4.8 %collective-permute-start.20 = (bf16[64,1152]{1,0:T(8,128)(2,1)S(1)}, bf16[64,1152]{1,0:T(8,128)(2,1)S(1)}, u32[]{:S(2)}, u32[]{:S(2)}) collective-permute-start(bf16[64,1152]{1,0:T(8,128)(2,1)S(1)} %collective-permute-done.10.refs_11_), channel_id=1, source_target_pairs={{0,1},{1,0},{2,3},{3,2},{4,5},{5,4},{6,7},{7,6},{8,9},{9,8},{10,11... | collective-permute-start | bytes 442376 | tf_op jit(solution)/shard_map/ppermute | solution.py:696
  54.8 1.4 %collective-permute-start.13 = (bf16[2,3,16,1024]{3,2,1,0:T(8,128)(2,1)S(1)}, bf16[2,3,16,1024]{3,2,1,0:T(8,128)(2,1)S(1)}, u32[]{:S(2)}, u32[]{:S(2)}) collective-permute-start(bf16[2,3,16,1024]{3,2,1,0:T(8,128)(2,1)S(1)} %collective-permute-done.7.refs_1_), channel_id=1, source_target_pairs={{0,1},{1,0},{2,3},{3,2},{4,5},{5,4},{6,7},{7,6},{8,9},{9,8},{10,11... | collective-permute-start | bytes 589832 | tf_op jit(solution)/shard_map/ppermute | solution.py:696
  54.8 1.7 %collective-permute-start.14 = (bf16[2,3,16,1024]{3,2,1,0:T(8,128)(2,1)S(1)}, bf16[2,3,16,1024]{3,2,1,0:T(8,128)(2,1)S(1)}, u32[]{:S(2)}, u32[]{:S(2)}) collective-permute-start(bf16[2,3,16,1024]{3,2,1,0:T(8,128)(2,1)S(1)} %collective-permute-done.8.refs_2_), channel_id=1, source_target_pairs={{0,1},{1,0},{2,3},{3,2},{4,5},{5,4},{6,7},{7,6},{8,9},{9,8},{10,11... | collective-permute-start | bytes 589832 | tf_op jit(solution)/shard_map/ppermute | solution.py:696
  55.3 1.5 %collective-permute-start.15 = (bf16[2,3,16,1024]{3,2,1,0:T(8,128)(2,1)S(1)}, bf16[2,3,16,1024]{3,2,1,0:T(8,128)(2,1)S(1)}, u32[]{:S(2)}, u32[]{:S(2)}) collective-permute-start(bf16[2,3,16,1024]{3,2,1,0:T(8,128)(2,1)S(1)} %collective-permute-done.11.refs_3_), channel_id=1, source_target_pairs={{0,1},{1,0},{2,3},{3,2},{4,5},{5,4},{6,7},{7,6},{8,9},{9,8},{10,11... | collective-permute-start | bytes 589832 | tf_op jit(solution)/shard_map/ppermute | solution.py:696
  55.4 1.7 %collective-permute-start.18 = (bf16[64,1152]{1,0:T(8,128)(2,1)S(1)}, bf16[64,1152]{1,0:T(8,128)(2,1)}, u32[]{:S(2)}, u32[]{:S(2)}) collective-permute-start(bf16[64,1152]{1,0:T(8,128)(2,1)S(1)} %collective-permute-done.16.refs_9_), channel_id=1, source_target_pairs={{0,1},{1,0},{2,3},{3,2},{4,5},{5,4},{6,7},{7,6},{8,9},{9,8},{10,11... | collective-permute-start | bytes 442376 | tf_op jit(solution)/shard_map/ppermute | solution.py:696
  (10 other events, 24.0 us)

commit v19 on v15

--- a/solution.py
+++ b/solution.py
@@ -808,7 +808,7 @@
     out_hidden, grad_dn, grad_upper = call(
         functools.partial(gradient_kernel, experts, sources, sizes),
         "gradients",
-        60,
+        48,
         [HBM] * (2 * experts + sources + 8),
         [(hidden_in.shape, bf16), ((slab, rank), bf16), ((rank, slab), bf16)],
         [

time: 63.3 us -> 76.6 us (1.21)
  local copies, waits for them, and re-layouts: 1.52 us -> 14.5 us
  Pallas kernels: 19.7 us -> 21.2 us
  waiting for transfers between devices: 14.6 us -> 13.4 us
    unnamed x38 -> x44, local copies, waits for them, and re-layouts: 1.52 us -> 14.5 us
    ppermute x17, waiting for transfers between devices: 8.27 us -> 7.12 us  [across(): return lax.ppermute(block, axis, [(i, i ^ distance) for i in range(size)])]
    pallas_call x1, Pallas kernels: 2.16 us -> 2.94 us  [on_device_two_phases(): call(functools.partial(repack_kernel, length, capacity), 'repack', 16, [V...]
  transfers between devices with their start and end apart: 23 -> 23, of which waited for: 7 -> 4; matrix products, arithmetic and copies ran while one was open for 0% -> 0% of each run, Pallas kernels for 19% -> 15%
where the time goes in v19:
time: 76.6 us; the launch traced here: 75.9 us
  starting transfers between devices  26 us (34%)
  Pallas kernels  21.2 us (28%)
  local copies, waits for them, and re-layouts  14.5 us (19%)
  waiting for transfers between devices  13.4 us (17%)
  between operations  0.81 us (1%)
    unnamed x44, local copies, waits for them, and re-layouts  14.5 us
    ppermute x17, starting transfers between devices, across(): return lax.ppermute(block, axis, [(i, i ^ distance) for i in range(size)])  10.9 us
    ppermute x17, waiting for transfers between devices, across(): return lax.ppermute(block, axis, [(i, i ^ distance) for i in range(size)])  7.12 us
    pallas_call x1, Pallas kernels, on_device_two_phases(): call(chain_kernel, 'chain', 50, [HBM] * 7, [((experts, 2, rows, part), bf...  7.09 us
    pallas_call x1, Pallas kernels, on_device_two_phases(): call(functools.partial(gradient_kernel, experts, sources, sizes), 'gradie...  6.53 us
    all_to_all x1, waiting for transfers between devices, on_device_two_phases(): lax.all_to_all(send, sections, split_axis=0, concat_axis=0, tiled=True)  6.32 us
    ppermute x4, starting transfers between devices, on_device_two_phases(): lax.ppermute(block, ('dp', 'segment'), slab_route(replicas, turn // 2, tu...  6.28 us
    all_to_all x1, starting transfers between devices, on_device_two_phases(): lax.all_to_all(send, sections, split_axis=0, concat_axis=0, tiled=True)  5.29 us
  transfers between devices with their start and end apart: 23, of which 4 were waited for; matrix products, arithmetic and copies ran while one was open for 0% of the time, Pallas kernels for 15%

profile of v19, /device:TPU:0, one launch (start us, length us, event | category | flops | bytes accessed | tf_op | source)
XLA Modules:
  0.0 75.9 jit_solution(10802704749679064569)
XLA Ops:
  1.2 2.4 %pack.1._ = bf16[8,2,16,2048]{3,2,1,0:T(8,128)(2,1)} custom-call(s32[16]{0:T(128)} %refs_22_.1, bf16[16,4,2048]{2,1,0:T(4,128)(2,1)} %hidden.3, bf16[16,4,2048]{2,1,0:T(4,128)(2,1)} %cot.3), custom_call_target="tpu_custom_call" | custom-call | bytes 1048576 | tf_op jit(solution)/shard_map/pack/pallas_call | solution.py:727
  3.6 5.3 %all-to-all-start = ((bf16[8,2,16,2048]{3,2,1,0:T(8,128)(2,1)}), bf16[8,2,16,2048]{3,2,1,0:T(8,128)(2,1)S(1)}, u32[]{:S(2)}, u32[]{:S(2)}) async-start(bf16[8,2,16,2048]{3,2,1,0:T(8,128)(2,1)} %pack.1._), calls=%async_computation | async-start | bytes 2097152 | tf_op jit(solution)/shard_map/all_to_all | solution.py:757
  9.4 2.3 %slabs.1 = (bf16[80,1024]{1,0:T(8,128)(2,1)}, bf16[80,1024]{1,0:T(8,128)(2,1)}, bf16[80,1024]{1,0:T(8,128)(2,1)}, bf16[80,1024]{1,0:T(8,128)(2,1)}) custom-call(s32[16]{0:T(128)} %refs_22_.1, bf16[16,4,2048]{2,1,0:T(4,128)(2,1)} %hidden.3, bf16[16,4,2048]{2,1,0:T(4,128)(2,1)} %cot.3, bf16[8,2,16,2048]{3,2,1,0:T(8,128)(2,1)} %pack.1._), custom_call_target="tpu_custom_call" | custom-call | bytes 1048576 | tf_op jit(solution)/shard_map/slabs/pallas_call | solution.py:741
  11.7 1.6 %collective-permute-start.3 = (bf16[80,1024]{1,0:T(8,128)(2,1)}, bf16[80,1024]{1,0:T(8,128)(2,1)S(1)}, u32[]{:S(2)}, u32[]{:S(2)}) collective-permute-start(bf16[80,1024]{1,0:T(8,128)(2,1)} %get-tuple-element.30), channel_id=1, source_target_pairs={{0,0},{1,4},{2,2},{3,6},{4,1},{5,5},{6,3},{7,7},{8,8},{9,12},{10,1... | collective-permute-start | bytes 491528 | tf_op jit(solution)/shard_map/ppermute | solution.py:760
  13.3 3.1 %collective-permute-start.4 = (bf16[80,1024]{1,0:T(8,128)(2,1)}, bf16[80,1024]{1,0:T(8,128)(2,1)}, u32[]{:S(2)}, u32[]{:S(2)}) collective-permute-start(bf16[80,1024]{1,0:T(8,128)(2,1)} %get-tuple-element.31), channel_id=1, source_target_pairs={{0,1},{1,5},{2,3},{3,7},{4,0},{5,4},{6,2},{7,6},{8,9},{9,13},{10,1... | collective-permute-start | bytes 491528 | tf_op jit(solution)/shard_map/ppermute | solution.py:760
  16.4 1.6 %collective-permute-start.5 = (bf16[80,1024]{1,0:T(8,128)(2,1)}, bf16[80,1024]{1,0:T(8,128)(2,1)}, u32[]{:S(2)}, u32[]{:S(2)}) collective-permute-start(bf16[80,1024]{1,0:T(8,128)(2,1)} %get-tuple-element.32), channel_id=1, source_target_pairs={{0,2},{1,6},{2,0},{3,4},{4,3},{5,7},{6,1},{7,5},{8,10},{9,14},{10,... | collective-permute-start | bytes 491528 | tf_op jit(solution)/shard_map/ppermute | solution.py:760
  18.0 6.3 %all-to-all-done = bf16[8,2,16,2048]{3,2,1,0:T(8,128)(2,1)S(1)} async-done(((bf16[8,2,16,2048]{3,2,1,0:T(8,128)(2,1)}), bf16[8,2,16,2048]{3,2,1,0:T(8,128)(2,1)S(1)}, u32[]{:S(2)}, u32[]{:S(2)}) %all-to-all-start) | async-done | bytes 1048608 | tf_op jit(solution)/shard_map/all_to_all | solution.py:757
  24.3 7.1 %chain.1 = (bf16[4,2,16,2048]{3,2,1,0:T(8,128)(2,1)S(1)}, bf16[64,1152]{1,0:T(8,128)(2,1)S(1)}) custom-call(bf16[4,2,2,16,2048]{4,3,2,1,0:T(8,128)(2,1)S(1)} %bitcast.7, bf16[4096,256]{1,0:T(8,128)(2,1)S(1)} %bitcast.10, bf16[256,4096]{1,0:T(8,128)(2,1)} %bitcast.17, bf16[1,4096]{1,0:T(2,128)(2,1)S(1)} %bitcast.14, ...), custom_call_target="tpu_custom_call" | custom-call | flops 939524096 | bytes 10485760 | tf_op jit(solution)/shard_map/chain/pallas_call | solution.py:763
  31.5 2.9 %repack.1 = (bf16[2,7,16,1024]{3,2,1,0:T(8,128)(2,1)S(1)}, bf16[2,3,16,1024]{3,2,1,0:T(8,128)(2,1)}, bf16[2,3,16,1024]{3,2,1,0:T(8,128)(2,1)}, bf16[2,3,16,1024]{3,2,1,0:T(8,128)(2,1)}) custom-call(bf16[80,1024]{1,0:T(8,128)(2,1)S(1)} %collective-permute-done.3.refs_0_, bf16[80,1024]{1,0:T(8,128)(2,1)} %collective-permute-done.4.refs_1_, ...), custom_call_target="tpu_custom_call" | custom-call | bytes 1048576 | tf_op jit(solution)/shard_map/repack/pallas_call | solution.py:782
  34.5 0.8 copy-done.2
  35.7 1.5 %collective-permute-start.11 = (bf16[2,3,16,1024]{3,2,1,0:T(8,128)(2,1)}, bf16[2,3,16,1024]{3,2,1,0:T(8,128)(2,1)}, u32[]{:S(2)}, u32[]{:S(2)}) collective-permute-start(bf16[2,3,16,1024]{3,2,1,0:T(8,128)(2,1)} %get-tuple-element.46), channel_id=1, source_target_pairs={{0,24},{8,16},{16,8},{24,0},{1,25},{9,17},{17,9},{25,1},{2,26},{10... | collective-permute-start | bytes 589832 | tf_op jit(solution)/shard_map/ppermute | solution.py:696
  37.2 2.4 %collective-permute-start.9 = (bf16[64,1152]{1,0:T(8,128)(2,1)S(1)}, bf16[64,1152]{1,0:T(8,128)(2,1)}, u32[]{:S(2)}, u32[]{:S(2)}) collective-permute-start(bf16[64,1152]{1,0:T(8,128)(2,1)S(1)} %get-tuple-element.48.refs_5_.refs_8_), channel_id=1, source_target_pairs={{0,2},{2,0},{4,6},{6,4},{1,3},{3,1},{5,7},{7,5},{8,10},{10,8},{12,... | collective-permute-start | bytes 442376 | tf_op jit(solution)/shard_map/ppermute | solution.py:696
  39.7 1.7 %collective-permute-start.10 = (bf16[64,1152]{1,0:T(8,128)(2,1)S(1)}, bf16[64,1152]{1,0:T(8,128)(2,1)}, u32[]{:S(2)}, u32[]{:S(2)}) collective-permute-start(bf16[64,1152]{1,0:T(8,128)(2,1)S(1)} %get-tuple-element.48.refs_5_.refs_8_), channel_id=1, source_target_pairs={{0,4},{2,6},{4,0},{6,2},{1,5},{3,7},{5,1},{7,3},{8,12},{10,14},{12... | collective-permute-start | bytes 442376 | tf_op jit(solution)/shard_map/ppermute | solution.py:696
  41.4 1.5 %collective-permute-start.8 = (bf16[2,3,16,1024]{3,2,1,0:T(8,128)(2,1)}, bf16[2,3,16,1024]{3,2,1,0:T(8,128)(2,1)}, u32[]{:S(2)}, u32[]{:S(2)}) collective-permute-start(bf16[2,3,16,1024]{3,2,1,0:T(8,128)(2,1)} %get-tuple-element.42), channel_id=1, source_target_pairs={{0,16},{8,24},{16,0},{24,8},{1,17},{9,25},{17,1},{25,9},{2,18},{10... | collective-permute-start | bytes 589832 | tf_op jit(solution)/shard_map/ppermute | solution.py:696
  42.9 3.5 %all-to-all-start.1 = ((bf16[8,16,2048]{2,1,0:T(8,128)(2,1)}), bf16[8,16,2048]{2,1,0:T(8,128)(2,1)S(1)}, u32[]{:S(2)}, u32[]{:S(2)}) async-start(bf16[8,16,2048]{2,1,0:T(8,128)(2,1)} %bitcast.12), calls=%async_computation.1 | async-start | bytes 1048576 | tf_op jit(solution)/shard_map/all_to_all | solution.py:802
  47.0 1.9 %collective-permute-done.10.refs_10_ = bf16[64,1152]{1,0:T(8,128)(2,1)} collective-permute-done((bf16[64,1152]{1,0:T(8,128)(2,1)S(1)}, bf16[64,1152]{1,0:T(8,128)(2,1)}, u32[]{:S(2)}, u32[]{:S(2)}) %collective-permute-start.10) | collective-permute-done | bytes 147488 | tf_op jit(solution)/shard_map/ppermute | solution.py:696
  50.1 4.5 %collective-permute-done.16.refs_11_ = bf16[64,1152]{1,0:T(8,128)(2,1)S(1)} collective-permute-done((bf16[64,1152]{1,0:T(8,128)(2,1)S(1)}, bf16[64,1152]{1,0:T(8,128)(2,1)S(1)}, u32[]{:S(2)}, u32[]{:S(2)}) %collective-permute-start.16) | collective-permute-done | bytes 147488 | tf_op jit(solution)/shard_map/ppermute | solution.py:696
  54.6 0.7 copy-done.12
  56.5 0.7 copy-done.16
  58.3 0.7 copy-done.4
  59.0 0.7 copy-done.6
  59.7 0.7 copy-done.8
  61.1 1.0 %copy-done.3 = bf16[2,7,16,1024]{3,2,1,0:T(8,128)(2,1)S(1)} copy-done((bf16[2,7,16,1024]{3,2,1,0:T(8,128)(2,1)S(1)}, bf16[2,7,16,1024]{3,2,1,0:T(8,128)(2,1)}, u32[]{:S(2)}) %copy-start.3) | copy-done | bytes 458776
  62.1 0.9 %copy-done.5 = bf16[2,3,16,1024]{3,2,1,0:T(8,128)(2,1)S(1)} copy-done((bf16[2,3,16,1024]{3,2,1,0:T(8,128)(2,1)S(1)}, bf16[2,3,16,1024]{3,2,1,0:T(8,128)(2,1)}, u32[]{:S(2)}) %copy-start.5) | copy-done | bytes 196632
  63.0 0.9 %copy-done.7 = bf16[2,3,16,1024]{3,2,1,0:T(8,128)(2,1)S(1)} copy-done((bf16[2,3,16,1024]{3,2,1,0:T(8,128)(2,1)S(1)}, bf16[2,3,16,1024]{3,2,1,0:T(8,128)(2,1)}, u32[]{:S(2)}) %copy-start.7) | copy-done | bytes 196632
  63.9 0.9 %copy-done.9 = bf16[2,3,16,1024]{3,2,1,0:T(8,128)(2,1)S(1)} copy-done((bf16[2,3,16,1024]{3,2,1,0:T(8,128)(2,1)S(1)}, bf16[2,3,16,1024]{3,2,1,0:T(8,128)(2,1)}, u32[]{:S(2)}) %copy-start.9) | copy-done | bytes 196632
  64.9 0.9 %copy-done.11 = bf16[64,1152]{1,0:T(8,128)(2,1)S(1)} copy-done((bf16[64,1152]{1,0:T(8,128)(2,1)S(1)}, bf16[64,1152]{1,0:T(8,128)(2,1)}, u32[]{:S(2)}) %copy-start.11) | copy-done | bytes 147480
  65.8 0.9 %copy-done.13 = bf16[64,1152]{1,0:T(8,128)(2,1)S(1)} copy-done((bf16[64,1152]{1,0:T(8,128)(2,1)S(1)}, bf16[64,1152]{1,0:T(8,128)(2,1)}, u32[]{:S(2)}) %copy-start.13) | copy-done | bytes 147480
  66.7 0.9 %copy-done.15 = bf16[64,1152]{1,0:T(8,128)(2,1)S(1)} copy-done((bf16[64,1152]{1,0:T(8,128)(2,1)S(1)}, bf16[64,1152]{1,0:T(8,128)(2,1)}, u32[]{:S(2)}) %copy-start.15) | copy-done | bytes 147480
  67.6 0.9 %copy-done.17 = bf16[64,1152]{1,0:T(8,128)(2,1)S(1)} copy-done((bf16[64,1152]{1,0:T(8,128)(2,1)S(1)}, bf16[64,1152]{1,0:T(8,128)(2,1)}, u32[]{:S(2)}) %copy-start.17) | copy-done | bytes 147480
  68.5 0.9 %copy-done.19 = bf16[64,1152]{1,0:T(8,128)(2,1)S(1)} copy-done((bf16[64,1152]{1,0:T(8,128)(2,1)S(1)}, bf16[64,1152]{1,0:T(8,128)(2,1)}, u32[]{:S(2)}) %copy-start.19) | copy-done | bytes 147480
  69.4 6.5 %gradients.1 = (bf16[16,4,2048]{2,1,0:T(4,128)(2,1)}, bf16[1024,256]{1,0:T(8,128)(2,1)}, bf16[256,1024]{1,0:T(8,128)(2,1)}) custom-call(bf16[2,7,16,1024]{3,2,1,0:T(8,128)(2,1)S(1)} %copy-done.3, bf16[2,3,16,1024]{3,2,1,0:T(8,128)(2,1)S(1)} %collective-permute-done.7.refs_1_, bf16[2,3,16,1024]{3,2,1,0:T(8,128)(2,1)} %collective-permute-done.8.refs_2_, ...), custom_call_target="tpu_custom_call" | custom-call | bytes 1048576 | tf_op jit(solution)/shard_map/gradients/pallas_call | solution.py:808
  (63 shorter events, 6.5 us)
Async XLA Ops:
  0.6 8.3 %copy-start.20 = (bf16[1,1,4096]{2,1,0:T(2,128)(2,1)S(1)}, bf16[1,1,4096]{2,1,0:T(2,128)(2,1)}, u32[]{:S(2)}) copy-start(bf16[1,1,4096]{2,1,0:T(2,128)(2,1)} %param.11) | copy-start | bytes 24580
  0.6 17.4 %collective-permute-start = (bf16[4096,256]{1,0:T(8,128)(2,1)}, bf16[4096,256]{1,0:T(8,128)(2,1)}, u32[]{:S(2)}, u32[]{:S(2)}) collective-permute-start(bf16[4096,256]{1,0:T(8,128)(2,1)} %bitcast.9), channel_id=1, source_target_pairs={{0,1},{1,0},{2,3},{3,2},{4,5},{5,4},{6,7},{7,6},{8,9},{9,8},{10,11... | collective-permute-start | bytes 6291464 | tf_op jit(solution)/shard_map/ppermute | solution.py:696
  1.2 23.2 %collective-permute-start.1 = (bf16[256,4096]{1,0:T(8,128)(2,1)}, bf16[256,4096]{1,0:T(8,128)(2,1)}, u32[]{:S(2)}, u32[]{:S(2)}) collective-permute-start(bf16[256,4096]{1,0:T(8,128)(2,1)} %bitcast.16), channel_id=1, source_target_pairs={{0,1},{1,0},{2,3},{3,2},{4,5},{5,4},{6,7},{7,6},{8,9},{9,8},{10,11... | collective-permute-start | bytes 6291464 | tf_op jit(solution)/shard_map/ppermute | solution.py:696
  3.6 20.7 %copy-start = (bf16[1,1,4096,256]{3,2,1,0:T(8,128)(2,1)S(1)}, bf16[1,1,4096,256]{3,2,1,0:T(8,128)(2,1)}, u32[]{:S(2)}) copy-start(bf16[1,1,4096,256]{3,2,1,0:T(8,128)(2,1)} %param.9) | copy-start | bytes 6291460
  3.6 20.7 %all-to-all-start = ((bf16[8,2,16,2048]{3,2,1,0:T(8,128)(2,1)}), bf16[8,2,16,2048]{3,2,1,0:T(8,128)(2,1)S(1)}, u32[]{:S(2)}, u32[]{:S(2)}) async-start(bf16[8,2,16,2048]{3,2,1,0:T(8,128)(2,1)} %pack.1._), calls=%async_computation | async-start | bytes 2097152 | tf_op jit(solution)/shard_map/all_to_all | solution.py:757
  8.9 7.5 %collective-permute-start.2 = (bf16[1,4096]{1,0:T(2,128)(2,1)S(1)}, bf16[1,4096]{1,0:T(2,128)(2,1)S(1)}, u32[]{:S(2)}, u32[]{:S(2)}) collective-permute-start(bf16[1,4096]{1,0:T(2,128)(2,1)S(1)} %bitcast.13), channel_id=1, source_target_pairs={{0,1},{1,0},{2,3},{3,2},{4,5},{5,4},{6,7},{7,6},{8,9},{9,8},{10,11... | collective-permute-start | bytes 24584 | tf_op jit(solution)/shard_map/ppermute | solution.py:696
  11.7 19.7 %collective-permute-start.3 = (bf16[80,1024]{1,0:T(8,128)(2,1)}, bf16[80,1024]{1,0:T(8,128)(2,1)S(1)}, u32[]{:S(2)}, u32[]{:S(2)}) collective-permute-start(bf16[80,1024]{1,0:T(8,128)(2,1)} %get-tuple-element.30), channel_id=1, source_target_pairs={{0,0},{1,4},{2,2},{3,6},{4,1},{5,5},{6,3},{7,7},{8,8},{9,12},{10,1... | collective-permute-start | bytes 491528 | tf_op jit(solution)/shard_map/ppermute | solution.py:760
  13.3 18.2 %collective-permute-start.4 = (bf16[80,1024]{1,0:T(8,128)(2,1)}, bf16[80,1024]{1,0:T(8,128)(2,1)}, u32[]{:S(2)}, u32[]{:S(2)}) collective-permute-start(bf16[80,1024]{1,0:T(8,128)(2,1)} %get-tuple-element.31), channel_id=1, source_target_pairs={{0,1},{1,5},{2,3},{3,7},{4,0},{5,4},{6,2},{7,6},{8,9},{9,13},{10,1... | collective-permute-start | bytes 491528 | tf_op jit(solution)/shard_map/ppermute | solution.py:760
  16.4 15.1 %collective-permute-start.5 = (bf16[80,1024]{1,0:T(8,128)(2,1)}, bf16[80,1024]{1,0:T(8,128)(2,1)}, u32[]{:S(2)}, u32[]{:S(2)}) collective-permute-start(bf16[80,1024]{1,0:T(8,128)(2,1)} %get-tuple-element.32), channel_id=1, source_target_pairs={{0,2},{1,6},{2,0},{3,4},{4,3},{5,7},{6,1},{7,5},{8,10},{9,14},{10,... | collective-permute-start | bytes 491528 | tf_op jit(solution)/shard_map/ppermute | solution.py:760
  18.0 13.5 %collective-permute-start.6 = (bf16[80,1024]{1,0:T(8,128)(2,1)}, bf16[80,1024]{1,0:T(8,128)(2,1)}, u32[]{:S(2)}, u32[]{:S(2)}) collective-permute-start(bf16[80,1024]{1,0:T(8,128)(2,1)} %get-tuple-element.33), channel_id=1, source_target_pairs={{0,3},{1,7},{2,1},{3,5},{4,2},{5,6},{6,0},{7,4},{8,11},{9,15},{10,... | collective-permute-start | bytes 491528 | tf_op jit(solution)/shard_map/ppermute | solution.py:760
  31.4 11.4 %copy-start.1 = (bf16[4,2,16,2048]{3,2,1,0:T(8,128)(2,1)}, bf16[4,2,16,2048]{3,2,1,0:T(8,128)(2,1)S(1)}, u32[]{:S(2)}) copy-start(bf16[4,2,16,2048]{3,2,1,0:T(8,128)(2,1)S(1)} %get-tuple-element.51) | copy-start | bytes 1572868
  31.5 29.6 %copy-start.21 = (s32[16]{0:T(128)S(1)}, s32[16]{0:T(128)}, u32[]{:S(2)}) copy-start(s32[16]{0:T(128)} %refs_22_.1) | copy-start | bytes 196
  35.2 11.2 %collective-permute-start.7 = (bf16[2,3,16,1024]{3,2,1,0:T(8,128)(2,1)}, bf16[2,3,16,1024]{3,2,1,0:T(8,128)(2,1)S(1)}, u32[]{:S(2)}, u32[]{:S(2)}) collective-permute-start(bf16[2,3,16,1024]{3,2,1,0:T(8,128)(2,1)} %get-tuple-element.39), channel_id=1, source_target_pairs={{0,8},{8,0},{16,24},{24,16},{1,9},{9,1},{17,25},{25,17},{2,10},{10... | collective-permute-start | bytes 589832 | tf_op jit(solution)/shard_map/ppermute | solution.py:696
  35.7 13.2 %collective-permute-start.11 = (bf16[2,3,16,1024]{3,2,1,0:T(8,128)(2,1)}, bf16[2,3,16,1024]{3,2,1,0:T(8,128)(2,1)}, u32[]{:S(2)}, u32[]{:S(2)}) collective-permute-start(bf16[2,3,16,1024]{3,2,1,0:T(8,128)(2,1)} %get-tuple-element.46), channel_id=1, source_target_pairs={{0,24},{8,16},{16,8},{24,0},{1,25},{9,17},{17,9},{25,1},{2,26},{10... | collective-permute-start | bytes 589832 | tf_op jit(solution)/shard_map/ppermute | solution.py:696
  37.2 9.6 %collective-permute-start.9 = (bf16[64,1152]{1,0:T(8,128)(2,1)S(1)}, bf16[64,1152]{1,0:T(8,128)(2,1)}, u32[]{:S(2)}, u32[]{:S(2)}) collective-permute-start(bf16[64,1152]{1,0:T(8,128)(2,1)S(1)} %get-tuple-element.48.refs_5_.refs_8_), channel_id=1, source_target_pairs={{0,2},{2,0},{4,6},{6,4},{1,3},{3,1},{5,7},{7,5},{8,10},{10,8},{12,... | collective-permute-start | bytes 442376 | tf_op jit(solution)/shard_map/ppermute | solution.py:696
  39.7 9.3 %collective-permute-start.10 = (bf16[64,1152]{1,0:T(8,128)(2,1)S(1)}, bf16[64,1152]{1,0:T(8,128)(2,1)}, u32[]{:S(2)}, u32[]{:S(2)}) collective-permute-start(bf16[64,1152]{1,0:T(8,128)(2,1)S(1)} %get-tuple-element.48.refs_5_.refs_8_), channel_id=1, source_target_pairs={{0,4},{2,6},{4,0},{6,2},{1,5},{3,7},{5,1},{7,3},{8,12},{10,14},{12... | collective-permute-start | bytes 442376 | tf_op jit(solution)/shard_map/ppermute | solution.py:696
  41.4 8.7 %collective-permute-start.8 = (bf16[2,3,16,1024]{3,2,1,0:T(8,128)(2,1)}, bf16[2,3,16,1024]{3,2,1,0:T(8,128)(2,1)}, u32[]{:S(2)}, u32[]{:S(2)}) collective-permute-start(bf16[2,3,16,1024]{3,2,1,0:T(8,128)(2,1)} %get-tuple-element.42), channel_id=1, source_target_pairs={{0,16},{8,24},{16,0},{24,8},{1,17},{9,25},{17,1},{25,9},{2,18},{10... | collective-permute-start | bytes 589832 | tf_op jit(solution)/shard_map/ppermute | solution.py:696
  42.9 18.2 %all-to-all-start.1 = ((bf16[8,16,2048]{2,1,0:T(8,128)(2,1)}), bf16[8,16,2048]{2,1,0:T(8,128)(2,1)S(1)}, u32[]{:S(2)}, u32[]{:S(2)}) async-start(bf16[8,16,2048]{2,1,0:T(8,128)(2,1)} %bitcast.12), calls=%async_computation.1 | async-start | bytes 1048576 | tf_op jit(solution)/shard_map/all_to_all | solution.py:802
  46.4 14.7 %collective-permute-start.12 = (bf16[2,7,16,1024]{3,2,1,0:T(8,128)(2,1)}, bf16[2,7,16,1024]{3,2,1,0:T(8,128)(2,1)S(1)}, u32[]{:S(2)}, u32[]{:S(2)}) collective-permute-start(bf16[2,7,16,1024]{3,2,1,0:T(8,128)(2,1)} %copy-done.2), channel_id=1, source_target_pairs={{0,1},{1,0},{2,3},{3,2},{4,5},{5,4},{6,7},{7,6},{8,9},{9,8},{10,11... | collective-permute-start | bytes 1376264 | tf_op jit(solution)/shard_map/ppermute | solution.py:696
  46.8 7.8 %collective-permute-start.16 = (bf16[64,1152]{1,0:T(8,128)(2,1)S(1)}, bf16[64,1152]{1,0:T(8,128)(2,1)S(1)}, u32[]{:S(2)}, u32[]{:S(2)}) collective-permute-start(bf16[64,1152]{1,0:T(8,128)(2,1)S(1)} %get-tuple-element.48.refs_5_.refs_8_), channel_id=1, source_target_pairs={{0,6},{2,4},{4,2},{6,0},{1,7},{3,5},{5,3},{7,1},{8,14},{10,12},{12... | collective-permute-start | bytes 442376 | tf_op jit(solution)/shard_map/ppermute | solution.py:696
  49.0 5.7 %collective-permute-start.17 = (bf16[64,1152]{1,0:T(8,128)(2,1)S(1)}, bf16[64,1152]{1,0:T(8,128)(2,1)S(1)}, u32[]{:S(2)}, u32[]{:S(2)}) collective-permute-start(bf16[64,1152]{1,0:T(8,128)(2,1)S(1)} %get-tuple-element.48.refs_5_.refs_8_), channel_id=1, source_target_pairs={{0,1},{1,0},{2,3},{3,2},{4,5},{5,4},{6,7},{7,6},{8,9},{9,8},{10,11... | collective-permute-start | bytes 442376 | tf_op jit(solution)/shard_map/ppermute | solution.py:696
  49.0 6.8 %collective-permute-start.18 = (bf16[64,1152]{1,0:T(8,128)(2,1)}, bf16[64,1152]{1,0:T(8,128)(2,1)S(1)}, u32[]{:S(2)}, u32[]{:S(2)}) collective-permute-start(bf16[64,1152]{1,0:T(8,128)(2,1)} %collective-permute-done.9.refs_9_), channel_id=1, source_target_pairs={{0,1},{1,0},{2,3},{3,2},{4,5},{5,4},{6,7},{7,6},{8,9},{9,8},{10,11... | collective-permute-start | bytes 442376 | tf_op jit(solution)/shard_map/ppermute | solution.py:696
  50.1 6.4 %collective-permute-start.19 = (bf16[64,1152]{1,0:T(8,128)(2,1)}, bf16[64,1152]{1,0:T(8,128)(2,1)S(1)}, u32[]{:S(2)}, u32[]{:S(2)}) collective-permute-start(bf16[64,1152]{1,0:T(8,128)(2,1)} %collective-permute-done.10.refs_10_), channel_id=1, source_target_pairs={{0,1},{1,0},{2,3},{3,2},{4,5},{5,4},{6,7},{7,6},{8,9},{9,8},{10,11... | collective-permute-start | bytes 442376 | tf_op jit(solution)/shard_map/ppermute | solution.py:696
  54.6 3.7 %collective-permute-start.13 = (bf16[2,3,16,1024]{3,2,1,0:T(8,128)(2,1)S(1)}, bf16[2,3,16,1024]{3,2,1,0:T(8,128)(2,1)S(1)}, u32[]{:S(2)}, u32[]{:S(2)}) collective-permute-start(bf16[2,3,16,1024]{3,2,1,0:T(8,128)(2,1)S(1)} %collective-permute-done.7.refs_1_), channel_id=1, source_target_pairs={{0,1},{1,0},{2,3},{3,2},{4,5},{5,4},{6,7},{7,6},{8,9},{9,8},{10,11... | collective-permute-start | bytes 589832 | tf_op jit(solution)/shard_map/ppermute | solution.py:696
  55.3 3.7 %collective-permute-start.14 = (bf16[2,3,16,1024]{3,2,1,0:T(8,128)(2,1)}, bf16[2,3,16,1024]{3,2,1,0:T(8,128)(2,1)S(1)}, u32[]{:S(2)}, u32[]{:S(2)}) collective-permute-start(bf16[2,3,16,1024]{3,2,1,0:T(8,128)(2,1)} %collective-permute-done.8.refs_2_), channel_id=1, source_target_pairs={{0,1},{1,0},{2,3},{3,2},{4,5},{5,4},{6,7},{7,6},{8,9},{9,8},{10,11... | collective-permute-start | bytes 589832 | tf_op jit(solution)/shard_map/ppermute | solution.py:696
  56.5 3.2 %collective-permute-start.15 = (bf16[2,3,16,1024]{3,2,1,0:T(8,128)(2,1)}, bf16[2,3,16,1024]{3,2,1,0:T(8,128)(2,1)S(1)}, u32[]{:S(2)}, u32[]{:S(2)}) collective-permute-start(bf16[2,3,16,1024]{3,2,1,0:T(8,128)(2,1)} %collective-permute-done.11.refs_3_), channel_id=1, source_target_pairs={{0,1},{1,0},{2,3},{3,2},{4,5},{5,4},{6,7},{7,6},{8,9},{9,8},{10,11... | collective-permute-start | bytes 589832 | tf_op jit(solution)/shard_map/ppermute | solution.py:696
  57.1 3.2 %collective-permute-start.20 = (bf16[64,1152]{1,0:T(8,128)(2,1)S(1)}, bf16[64,1152]{1,0:T(8,128)(2,1)S(1)}, u32[]{:S(2)}, u32[]{:S(2)}) collective-permute-start(bf16[64,1152]{1,0:T(8,128)(2,1)S(1)} %collective-permute-done.16.refs_11_), channel_id=1, source_target_pairs={{0,1},{1,0},{2,3},{3,2},{4,5},{5,4},{6,7},{7,6},{8,9},{9,8},{10,11... | collective-permute-start | bytes 442376 | tf_op jit(solution)/shard_map/ppermute | solution.py:696
  61.1 1.0 %copy-start.3 = (bf16[2,7,16,1024]{3,2,1,0:T(8,128)(2,1)S(1)}, bf16[2,7,16,1024]{3,2,1,0:T(8,128)(2,1)}, u32[]{:S(2)}) copy-start(bf16[2,7,16,1024]{3,2,1,0:T(8,128)(2,1)} %copy-done.2) | copy-start | bytes 1376260
  62.1 0.9 %copy-start.5 = (bf16[2,3,16,1024]{3,2,1,0:T(8,128)(2,1)S(1)}, bf16[2,3,16,1024]{3,2,1,0:T(8,128)(2,1)}, u32[]{:S(2)}) copy-start(bf16[2,3,16,1024]{3,2,1,0:T(8,128)(2,1)} %copy-done.4) | copy-start | bytes 589828
  63.0 0.9 %copy-start.7 = (bf16[2,3,16,1024]{3,2,1,0:T(8,128)(2,1)S(1)}, bf16[2,3,16,1024]{3,2,1,0:T(8,128)(2,1)}, u32[]{:S(2)}) copy-start(bf16[2,3,16,1024]{3,2,1,0:T(8,128)(2,1)} %copy-done.6) | copy-start | bytes 589828
  63.9 0.9 %copy-start.9 = (bf16[2,3,16,1024]{3,2,1,0:T(8,128)(2,1)S(1)}, bf16[2,3,16,1024]{3,2,1,0:T(8,128)(2,1)}, u32[]{:S(2)}) copy-start(bf16[2,3,16,1024]{3,2,1,0:T(8,128)(2,1)} %copy-done.8) | copy-start | bytes 589828
  64.9 0.9 %copy-start.11 = (bf16[64,1152]{1,0:T(8,128)(2,1)S(1)}, bf16[64,1152]{1,0:T(8,128)(2,1)}, u32[]{:S(2)}) copy-start(bf16[64,1152]{1,0:T(8,128)(2,1)} %copy-done.10) | copy-start | bytes 442372
  (13 other events, 9.8 us)

commit v20 on v15

--- a/solution.py
+++ b/solution.py
@@ -353,10 +353,12 @@
         cut.wait()
 
 
-def unpack(sizes, id_buf, back, out):
-    length, capacity, slots = sizes
+def unpack_kernel(length, capacity, slots, ids, back, _, out, id_buf, sem):
+    copy = pltpu.make_async_copy(ids, id_buf, sem)
+    copy.start()
     groups, rows, width = back.shape
     s_local = out.shape[0]
+    copy.wait()
     ids_row = spread_ids(id_buf, (8, s_local * length), length)[:1]
     place, _ = placements(ids_row, length, capacity, slots)
     moved = matmul(place, back[...].reshape(groups * rows, width), TRANS_LHS)
@@ -518,13 +520,13 @@
             small[pl.ds(start, rows), cols] = value[e * rows : (e + 1) * rows]
 
 
-def gradient_kernel(experts, sources, sizes, *refs):
+def gradient_kernel(experts, sources, *refs):
     sides, refs = refs[: 2 * experts], refs[2 * experts :]
     smalls, refs = refs[:sources], refs[sources:]
     own, other, refs = refs[:3], refs[3:6], refs[6:]
-    ids, back_in, out_hidden, grad_dn, grad_upper = refs[:5]
-    (id_buf, back, result, dn_buf, up_buf, gain_buf, wide_buf, small, moments, turned, lows, grads,
-     dn_out, up_out, small_sems, wide_sems, sems) = refs[5:]
+    grad_dn, grad_upper = refs[:2]
+    (dn_buf, up_buf, gain_buf, wide_buf, small, moments, turned, lows, grads,
+     dn_out, up_out, small_sems, wide_sems, sems) = refs[2:]
     core = lax.axis_index("segment")
     place = lax.axis_index("dp")
     rows, slab = smalls[0].shape[0], sides[0].shape[3]
@@ -548,10 +550,6 @@
             for at, (source, target) in enumerate(moves)
         ]
 
-    early = [
-        pltpu.make_async_copy(ids, id_buf, sems.at[4]),
-        pltpu.make_async_copy(back_in, back, sems.at[5]),
-    ]
     small_copies = [
         pltpu.make_async_copy(
             source, small.at[at * rows : (at + 1) * rows], small_sems.at[at]
@@ -575,7 +573,7 @@
         ]
         for col in chunks
     ]
-    for copy in early + small_copies:
+    for copy in small_copies:
         copy.start()
 
     @pl.when(core == 0)
@@ -591,11 +589,7 @@
     for copies in wide_copies:
         for copy in copies:
             copy.start()
-    for copy in early:
-        copy.wait()
-    unpack(sizes, id_buf, back, result)
-    leaving = [pltpu.make_async_copy(result, out_hidden, sems.at[6])]
-    leaving[0].start()
+    leaving = []
     for copy in small_copies + weight_copies(own[1], own[2], other[0], other[2]):
         copy.wait()
 
@@ -794,6 +788,7 @@
     near = [small] + [across(small, "dp", step) for step in range(1, replicas - 1)]
     near[:2] = lax.optimization_barrier(tuple(near[:2]))
     last = across(near[0], "dp", replicas - 1)
+    near[2], out = lax.optimization_barrier((near[2], out))
     *near, mine[-1] = lax.optimization_barrier((*near, mine[-1]))
     near.append(last)
     theirs = [across(block, "segment", 1) for block in mine]
@@ -805,16 +800,13 @@
 
     sources = 2 * replicas
     all_tokens = sources * tokens
-    out_hidden, grad_dn, grad_upper = call(
-        functools.partial(gradient_kernel, experts, sources, sizes),
+    grad_dn, grad_upper = call(
+        functools.partial(gradient_kernel, experts, sources),
         "gradients",
         60,
-        [HBM] * (2 * experts + sources + 8),
-        [(hidden_in.shape, bf16), ((slab, rank), bf16), ((rank, slab), bf16)],
+        [HBM] * (2 * experts + sources + 6),
+        [((slab, rank), bf16), ((rank, slab), bf16)],
         [
-            pltpu.SMEM(cluster_ids.shape, jnp.int32),
-            pltpu.VMEM(back.shape, bf16),
-            pltpu.VMEM(hidden_in.shape, bf16),
             pltpu.VMEM((slab, rank), bf16),
             pltpu.VMEM((rank, slab), bf16),
             pltpu.VMEM((2, 1, slab), bf16),
@@ -831,7 +823,15 @@
             pltpu.SemaphoreType.DMA((7 + 2 * (slab // 256),)),
         ],
         outs_in=HBM,
-    )(*mine, *theirs, *smalls, *own, *other, cluster_ids, back)
+    )(*mine, *theirs, *smalls, *own, *other)
+    (out_hidden,) = call(
+        functools.partial(unpack_kernel, *sizes),
+        "unpack",
+        60,
+        [HBM, VMEM, HBM],
+        [(hidden_in.shape, bf16)],
+        [pltpu.SMEM(cluster_ids.shape, jnp.int32), pltpu.SemaphoreType.DMA],
+    )(cluster_ids, back, grad_dn)
     return (out_hidden, grad_dn[None, None], grad_upper[None, None])
 
 

time: 63.3 us -> 70.2 us (1.11)
  Pallas kernels: 19.7 us -> 22.5 us
  starting transfers between devices: 26.2 us -> 29 us
    ppermute x17, starting transfers between devices: 11.1 us -> 13.9 us  [across(): return lax.ppermute(block, axis, [(i, i ^ distance) for i in range(size)])]
    pallas_call x1 -> x2, Pallas kernels: 5.83 us -> 8.57 us  [the longest x1 5.74 us: on_device_two_phases(): call(functools.partial(gradient_kernel, experts, sources), 'gradients', 6...]
    unnamed x38 -> x42, local copies, waits for them, and re-layouts: 1.52 us -> 2.16 us
  transfers between devices with their start and end apart: 23 -> 23, of which waited for: 7 -> 7; matrix products, arithmetic and copies ran while one was open for 0% -> 0% of each run, Pallas kernels for 19% -> 25%
where the time goes in v20:
time: 70.2 us; the launch traced here: 69.8 us
  starting transfers between devices  29 us (41%)
  Pallas kernels  22.5 us (32%)
  waiting for transfers between devices  15.3 us (22%)
  local copies, waits for them, and re-layouts  2.16 us (3%)
  between operations  0.94 us (1%)
    ppermute x17, starting transfers between devices, across(): return lax.ppermute(block, axis, [(i, i ^ distance) for i in range(size)])  13.9 us
    ppermute x17, waiting for transfers between devices, across(): return lax.ppermute(block, axis, [(i, i ^ distance) for i in range(size)])  8.95 us
    pallas_call x1, Pallas kernels, on_device_two_phases(): call(chain_kernel, 'chain', 50, [HBM] * 7, [((experts, 2, rows, part), bf...  7.1 us
    all_to_all x1, waiting for transfers between devices, on_device_two_phases(): lax.all_to_all(send, sections, split_axis=0, concat_axis=0, tiled=True)  6.31 us
    ppermute x4, starting transfers between devices, on_device_two_phases(): lax.ppermute(block, ('dp', 'segment'), slab_route(replicas, turn // 2, tu...  6.29 us
    pallas_call x1, Pallas kernels, on_device_two_phases(): call(functools.partial(gradient_kernel, experts, sources), 'gradients', 6...  5.74 us
    all_to_all x1, starting transfers between devices, on_device_two_phases(): lax.all_to_all(send, sections, split_axis=0, concat_axis=0, tiled=True)  5.29 us
    all_to_all x1, starting transfers between devices, on_device_two_phases(): lax.all_to_all(out.reshape(groups, rows, part), sections, split_axis=0, c...  3.5 us
  transfers between devices with their start and end apart: 23, of which 7 were waited for; matrix products, arithmetic and copies ran while one was open for 0% of the time, Pallas kernels for 25%

profile of v20, /device:TPU:0, one launch (start us, length us, event | category | flops | bytes accessed | tf_op | source)
XLA Modules:
  0.0 69.8 jit_solution(16946885989173441224)
XLA Ops:
  0.6 0.5 collective-permute-start
  1.2 2.4 %pack.1._ = bf16[8,2,16,2048]{3,2,1,0:T(8,128)(2,1)} custom-call(s32[16]{0:T(128)} %ids.5, bf16[16,4,2048]{2,1,0:T(4,128)(2,1)} %hidden.3, bf16[16,4,2048]{2,1,0:T(4,128)(2,1)} %cot.3), custom_call_target="tpu_custom_call" | custom-call | bytes 1048576 | tf_op jit(solution)/shard_map/pack/pallas_call | solution.py:721
  3.6 5.3 %all-to-all-start = ((bf16[8,2,16,2048]{3,2,1,0:T(8,128)(2,1)}), bf16[8,2,16,2048]{3,2,1,0:T(8,128)(2,1)S(1)}, u32[]{:S(2)}, u32[]{:S(2)}) async-start(bf16[8,2,16,2048]{3,2,1,0:T(8,128)(2,1)} %pack.1._), calls=%async_computation | async-start | bytes 2097152 | tf_op jit(solution)/shard_map/all_to_all | solution.py:751
  8.9 0.5 collective-permute-start.2
  9.4 2.3 %slabs.1 = (bf16[80,1024]{1,0:T(8,128)(2,1)}, bf16[80,1024]{1,0:T(8,128)(2,1)}, bf16[80,1024]{1,0:T(8,128)(2,1)}, bf16[80,1024]{1,0:T(8,128)(2,1)}) custom-call(s32[16]{0:T(128)} %ids.5, bf16[16,4,2048]{2,1,0:T(4,128)(2,1)} %hidden.3, bf16[16,4,2048]{2,1,0:T(4,128)(2,1)} %cot.3, bf16[8,2,16,2048]{3,2,1,0:T(8,128)(2,1)} %pack.1._), custom_call_target="tpu_custom_call" | custom-call | bytes 1048576 | tf_op jit(solution)/shard_map/slabs/pallas_call | solution.py:735
  11.7 1.6 %collective-permute-start.3 = (bf16[80,1024]{1,0:T(8,128)(2,1)}, bf16[80,1024]{1,0:T(8,128)(2,1)S(1)}, u32[]{:S(2)}, u32[]{:S(2)}) collective-permute-start(bf16[80,1024]{1,0:T(8,128)(2,1)} %get-tuple-element.31), channel_id=1, source_target_pairs={{0,0},{1,4},{2,2},{3,6},{4,1},{5,5},{6,3},{7,7},{8,8},{9,12},{10,1... | collective-permute-start | bytes 491528 | tf_op jit(solution)/shard_map/ppermute | solution.py:754
  13.3 3.1 %collective-permute-start.4 = (bf16[80,1024]{1,0:T(8,128)(2,1)}, bf16[80,1024]{1,0:T(8,128)(2,1)}, u32[]{:S(2)}, u32[]{:S(2)}) collective-permute-start(bf16[80,1024]{1,0:T(8,128)(2,1)} %get-tuple-element.32), channel_id=1, source_target_pairs={{0,1},{1,5},{2,3},{3,7},{4,0},{5,4},{6,2},{7,6},{8,9},{9,13},{10,1... | collective-permute-start | bytes 491528 | tf_op jit(solution)/shard_map/ppermute | solution.py:754
  16.4 1.6 %collective-permute-start.5 = (bf16[80,1024]{1,0:T(8,128)(2,1)}, bf16[80,1024]{1,0:T(8,128)(2,1)}, u32[]{:S(2)}, u32[]{:S(2)}) collective-permute-start(bf16[80,1024]{1,0:T(8,128)(2,1)} %get-tuple-element.33), channel_id=1, source_target_pairs={{0,2},{1,6},{2,0},{3,4},{4,3},{5,7},{6,1},{7,5},{8,10},{9,14},{10,... | collective-permute-start | bytes 491528 | tf_op jit(solution)/shard_map/ppermute | solution.py:754
  18.0 6.3 %all-to-all-done = bf16[8,2,16,2048]{3,2,1,0:T(8,128)(2,1)S(1)} async-done(((bf16[8,2,16,2048]{3,2,1,0:T(8,128)(2,1)}), bf16[8,2,16,2048]{3,2,1,0:T(8,128)(2,1)S(1)}, u32[]{:S(2)}, u32[]{:S(2)}) %all-to-all-start) | async-done | bytes 1048608 | tf_op jit(solution)/shard_map/all_to_all | solution.py:751
  24.3 7.1 %chain.1 = (bf16[4,2,16,2048]{3,2,1,0:T(8,128)(2,1)S(1)}, bf16[64,1152]{1,0:T(8,128)(2,1)S(1)}) custom-call(bf16[4,2,2,16,2048]{4,3,2,1,0:T(8,128)(2,1)S(1)} %bitcast.7, bf16[4096,256]{1,0:T(8,128)(2,1)S(1)} %bitcast.11, bf16[256,4096]{1,0:T(8,128)(2,1)} %bitcast.17, bf16[1,4096]{1,0:T(2,128)(2,1)S(1)} %bitcast.15, ...), custom_call_target="tpu_custom_call" | custom-call | flops 939524096 | bytes 10485760 | tf_op jit(solution)/shard_map/chain/pallas_call | solution.py:757
  31.5 2.2 %repack.1 = (bf16[2,7,16,1024]{3,2,1,0:T(8,128)(2,1)S(1)}, bf16[2,3,16,1024]{3,2,1,0:T(8,128)(2,1)S(1)}, bf16[2,3,16,1024]{3,2,1,0:T(8,128)(2,1)S(1)}, bf16[2,3,16,1024]{3,2,1,0:T(8,128)(2,1)S(1)}) custom-call(bf16[80,1024]{1,0:T(8,128)(2,1)S(1)} %collective-permute-done.3.refs_0_, bf16[80,1024]{1,0:T(8,128)(2,1)} %collective-permute-done.4.refs_1_, ...), custom_call_target="tpu_custom_call" | custom-call | bytes 1048576 | tf_op jit(solution)/shard_map/repack/pallas_call | solution.py:776
  33.7 0.6 collective-permute-start.8
  34.3 2.6 %collective-permute-start.7 = (bf16[64,1152]{1,0:T(8,128)(2,1)S(1)}, bf16[64,1152]{1,0:T(8,128)(2,1)S(1)}, u32[]{:S(2)}, u32[]{:S(2)}) collective-permute-start(bf16[64,1152]{1,0:T(8,128)(2,1)S(1)} %get-tuple-element.52.refs_5_.refs_8_), channel_id=1, source_target_pairs={{0,4},{2,6},{4,0},{6,2},{1,5},{3,7},{5,1},{7,3},{8,12},{10,14},{12... | collective-permute-start | bytes 442376 | tf_op jit(solution)/shard_map/ppermute | solution.py:690
  36.8 1.5 %collective-permute-start.11 = (bf16[2,3,16,1024]{3,2,1,0:T(8,128)(2,1)S(1)}, bf16[2,3,16,1024]{3,2,1,0:T(8,128)(2,1)S(1)}, u32[]{:S(2)}, u32[]{:S(2)}) collective-permute-start(bf16[2,3,16,1024]{3,2,1,0:T(8,128)(2,1)S(1)} %get-tuple-element.50), channel_id=1, source_target_pairs={{0,24},{8,16},{16,8},{24,0},{1,25},{9,17},{17,9},{25,1},{2,26},{10... | collective-permute-start | bytes 589832 | tf_op jit(solution)/shard_map/ppermute | solution.py:690
  38.3 1.6 %collective-permute-start.10 = (bf16[64,1152]{1,0:T(8,128)(2,1)S(1)}, bf16[64,1152]{1,0:T(8,128)(2,1)S(1)}, u32[]{:S(2)}, u32[]{:S(2)}) collective-permute-start(bf16[64,1152]{1,0:T(8,128)(2,1)S(1)} %get-tuple-element.52.refs_5_.refs_8_), channel_id=1, source_target_pairs={{0,2},{2,0},{4,6},{6,4},{1,3},{3,1},{5,7},{7,5},{8,10},{10,8},{12,... | collective-permute-start | bytes 442376 | tf_op jit(solution)/shard_map/ppermute | solution.py:690
  39.9 1.5 %collective-permute-start.9 = (bf16[2,3,16,1024]{3,2,1,0:T(8,128)(2,1)S(1)}, bf16[2,3,16,1024]{3,2,1,0:T(8,128)(2,1)S(1)}, u32[]{:S(2)}, u32[]{:S(2)}) collective-permute-start(bf16[2,3,16,1024]{3,2,1,0:T(8,128)(2,1)S(1)} %get-tuple-element.46), channel_id=1, source_target_pairs={{0,16},{8,24},{16,0},{24,8},{1,17},{9,25},{17,1},{25,9},{2,18},{10... | collective-permute-start | bytes 589832 | tf_op jit(solution)/shard_map/ppermute | solution.py:690
  41.4 3.6 %collective-permute-done.7.refs_10_ = bf16[64,1152]{1,0:T(8,128)(2,1)S(1)} collective-permute-done((bf16[64,1152]{1,0:T(8,128)(2,1)S(1)}, bf16[64,1152]{1,0:T(8,128)(2,1)S(1)}, u32[]{:S(2)}, u32[]{:S(2)}) %collective-permute-start.7) | collective-permute-done | bytes 147488 | tf_op jit(solution)/shard_map/ppermute | solution.py:690
  45.1 3.5 %all-to-all-start.1 = ((bf16[8,16,2048]{2,1,0:T(8,128)(2,1)}), bf16[8,16,2048]{2,1,0:T(8,128)(2,1)S(1)}, u32[]{:S(2)}, u32[]{:S(2)}) async-start(bf16[8,16,2048]{2,1,0:T(8,128)(2,1)} %bitcast.12), calls=%async_computation.1 | async-start | bytes 1048576 | tf_op jit(solution)/shard_map/all_to_all | solution.py:797
  48.6 3.3 %collective-permute-start.16 = (bf16[64,1152]{1,0:T(8,128)(2,1)S(1)}, bf16[64,1152]{1,0:T(8,128)(2,1)S(1)}, u32[]{:S(2)}, u32[]{:S(2)}) collective-permute-start(bf16[64,1152]{1,0:T(8,128)(2,1)S(1)} %get-tuple-element.52.refs_5_.refs_8_), channel_id=1, source_target_pairs={{0,6},{2,4},{4,2},{6,0},{1,7},{3,5},{5,3},{7,1},{8,14},{10,12},{12... | collective-permute-start | bytes 442376 | tf_op jit(solution)/shard_map/ppermute | solution.py:690
  52.1 0.3 collective-permute-start.18
  52.6 4.2 %collective-permute-done.16.refs_11_ = bf16[64,1152]{1,0:T(8,128)(2,1)S(1)} collective-permute-done((bf16[64,1152]{1,0:T(8,128)(2,1)S(1)}, bf16[64,1152]{1,0:T(8,128)(2,1)S(1)}, u32[]{:S(2)}, u32[]{:S(2)}) %collective-permute-start.16) | collective-permute-done | bytes 147488 | tf_op jit(solution)/shard_map/ppermute | solution.py:690
  56.8 0.5 collective-permute-start.14
  57.4 0.4 collective-permute-start.20
  57.8 0.4 collective-permute-done.13.refs_5_
  58.2 0.3 collective-permute-done.14.refs_6_
  58.5 0.3 collective-permute-done.15.refs_7_
  58.8 0.2 collective-permute-done.20.refs_15_
  59.2 0.3 copy-done.13
  59.6 0.8 %copy-done.7 = bf16[2,7,16,1024]{3,2,1,0:T(8,128)(2,1)} copy-done((bf16[2,7,16,1024]{3,2,1,0:T(8,128)(2,1)}, bf16[2,7,16,1024]{3,2,1,0:T(8,128)(2,1)S(1)}, u32[]{:S(2)}) %copy-start.7) | copy-done | bytes 458776
  60.4 5.7 %gradients.1 = (bf16[1024,256]{1,0:T(8,128)(2,1)}, bf16[256,1024]{1,0:T(8,128)(2,1)}) custom-call(bf16[2,7,16,1024]{3,2,1,0:T(8,128)(2,1)} %copy-done.3, bf16[2,3,16,1024]{3,2,1,0:T(8,128)(2,1)} %copy-done.8, bf16[2,3,16,1024]{3,2,1,0:T(8,128)(2,1)} %copy-done.10, bf16[2,3,16,1024]{3,2,1,0:T(8,128)(2,1)} %copy-done.9, bf16[2,7,16,1024]{3,2,1,0:T(8,128)(2,1)} %copy-done.7, ...), custom_call_target="tpu_custom_call" | custom-call | bytes 1048576 | tf_op jit(solution)/shard_map/gradients/pallas_call | solution.py:803
  66.2 0.8 %copy-done.6 = bf16[8,16,2048]{2,1,0:T(8,128)(2,1)} copy-done((bf16[8,16,2048]{2,1,0:T(8,128)(2,1)}, bf16[8,16,2048]{2,1,0:T(8,128)(2,1)S(1)}, u32[]{:S(2)}) %copy-start.6) | copy-done | bytes 524312
  67.0 2.8 %unpack.1 = bf16[16,4,2048]{2,1,0:T(4,128)(2,1)} custom-call(s32[16]{0:T(128)} %ids.5, bf16[8,16,2048]{2,1,0:T(8,128)(2,1)} %copy-done.6, bf16[1024,256]{1,0:T(8,128)(2,1)} %get-tuple-element.55._), custom_call_target="tpu_custom_call" | custom-call | bytes 1048576 | tf_op jit(solution)/shard_map/unpack/pallas_call | solution.py:827
  (62 shorter events, 0.9 us)
Async XLA Ops:
  0.6 8.3 %copy-start.4 = (bf16[1,1,4096]{2,1,0:T(2,128)(2,1)S(1)}, bf16[1,1,4096]{2,1,0:T(2,128)(2,1)}, u32[]{:S(2)}) copy-start(bf16[1,1,4096]{2,1,0:T(2,128)(2,1)} %param.11) | copy-start | bytes 24580
  0.6 17.4 %collective-permute-start = (bf16[4096,256]{1,0:T(8,128)(2,1)}, bf16[4096,256]{1,0:T(8,128)(2,1)}, u32[]{:S(2)}, u32[]{:S(2)}) collective-permute-start(bf16[4096,256]{1,0:T(8,128)(2,1)} %bitcast.9), channel_id=1, source_target_pairs={{0,1},{1,0},{2,3},{3,2},{4,5},{5,4},{6,7},{7,6},{8,9},{9,8},{10,11... | collective-permute-start | bytes 6291464 | tf_op jit(solution)/shard_map/ppermute | solution.py:690
  1.2 23.2 %collective-permute-start.1 = (bf16[256,4096]{1,0:T(8,128)(2,1)}, bf16[256,4096]{1,0:T(8,128)(2,1)}, u32[]{:S(2)}, u32[]{:S(2)}) collective-permute-start(bf16[256,4096]{1,0:T(8,128)(2,1)} %bitcast.16), channel_id=1, source_target_pairs={{0,1},{1,0},{2,3},{3,2},{4,5},{5,4},{6,7},{7,6},{8,9},{9,8},{10,11... | collective-permute-start | bytes 6291464 | tf_op jit(solution)/shard_map/ppermute | solution.py:690
  3.6 20.7 %copy-start = (bf16[1,1,4096,256]{3,2,1,0:T(8,128)(2,1)S(1)}, bf16[1,1,4096,256]{3,2,1,0:T(8,128)(2,1)}, u32[]{:S(2)}) copy-start(bf16[1,1,4096,256]{3,2,1,0:T(8,128)(2,1)} %param.9) | copy-start | bytes 6291460
  3.6 20.7 %all-to-all-start = ((bf16[8,2,16,2048]{3,2,1,0:T(8,128)(2,1)}), bf16[8,2,16,2048]{3,2,1,0:T(8,128)(2,1)S(1)}, u32[]{:S(2)}, u32[]{:S(2)}) async-start(bf16[8,2,16,2048]{3,2,1,0:T(8,128)(2,1)} %pack.1._), calls=%async_computation | async-start | bytes 2097152 | tf_op jit(solution)/shard_map/all_to_all | solution.py:751
  8.9 7.5 %collective-permute-start.2 = (bf16[1,4096]{1,0:T(2,128)(2,1)S(1)}, bf16[1,4096]{1,0:T(2,128)(2,1)S(1)}, u32[]{:S(2)}, u32[]{:S(2)}) collective-permute-start(bf16[1,4096]{1,0:T(2,128)(2,1)S(1)} %bitcast.14), channel_id=1, source_target_pairs={{0,1},{1,0},{2,3},{3,2},{4,5},{5,4},{6,7},{7,6},{8,9},{9,8},{10,11... | collective-permute-start | bytes 24584 | tf_op jit(solution)/shard_map/ppermute | solution.py:690
  11.7 19.7 %collective-permute-start.3 = (bf16[80,1024]{1,0:T(8,128)(2,1)}, bf16[80,1024]{1,0:T(8,128)(2,1)S(1)}, u32[]{:S(2)}, u32[]{:S(2)}) collective-permute-start(bf16[80,1024]{1,0:T(8,128)(2,1)} %get-tuple-element.31), channel_id=1, source_target_pairs={{0,0},{1,4},{2,2},{3,6},{4,1},{5,5},{6,3},{7,7},{8,8},{9,12},{10,1... | collective-permute-start | bytes 491528 | tf_op jit(solution)/shard_map/ppermute | solution.py:754
  13.3 18.2 %collective-permute-start.4 = (bf16[80,1024]{1,0:T(8,128)(2,1)}, bf16[80,1024]{1,0:T(8,128)(2,1)}, u32[]{:S(2)}, u32[]{:S(2)}) collective-permute-start(bf16[80,1024]{1,0:T(8,128)(2,1)} %get-tuple-element.32), channel_id=1, source_target_pairs={{0,1},{1,5},{2,3},{3,7},{4,0},{5,4},{6,2},{7,6},{8,9},{9,13},{10,1... | collective-permute-start | bytes 491528 | tf_op jit(solution)/shard_map/ppermute | solution.py:754
  16.4 15.0 %copy-start.5 = (bf16[1,4096]{1,0:T(2,128)(2,1)}, bf16[1,4096]{1,0:T(2,128)(2,1)S(1)}, u32[]{:S(2)}) copy-start(bf16[1,4096]{1,0:T(2,128)(2,1)S(1)} %collective-permute-done.2.other_gain.refs_21_) | copy-start | bytes 24580
  16.4 15.1 %collective-permute-start.5 = (bf16[80,1024]{1,0:T(8,128)(2,1)}, bf16[80,1024]{1,0:T(8,128)(2,1)}, u32[]{:S(2)}, u32[]{:S(2)}) collective-permute-start(bf16[80,1024]{1,0:T(8,128)(2,1)} %get-tuple-element.33), channel_id=1, source_target_pairs={{0,2},{1,6},{2,0},{3,4},{4,3},{5,7},{6,1},{7,5},{8,10},{9,14},{10,... | collective-permute-start | bytes 491528 | tf_op jit(solution)/shard_map/ppermute | solution.py:754
  18.0 13.5 %collective-permute-start.6 = (bf16[80,1024]{1,0:T(8,128)(2,1)}, bf16[80,1024]{1,0:T(8,128)(2,1)}, u32[]{:S(2)}, u32[]{:S(2)}) collective-permute-start(bf16[80,1024]{1,0:T(8,128)(2,1)} %get-tuple-element.34), channel_id=1, source_target_pairs={{0,3},{1,7},{2,1},{3,5},{4,2},{5,6},{6,0},{7,4},{8,11},{9,15},{10,... | collective-permute-start | bytes 491528 | tf_op jit(solution)/shard_map/ppermute | solution.py:754
  31.4 13.6 %copy-start.2 = (bf16[4,2,16,2048]{3,2,1,0:T(8,128)(2,1)}, bf16[4,2,16,2048]{3,2,1,0:T(8,128)(2,1)S(1)}, u32[]{:S(2)}) copy-start(bf16[4,2,16,2048]{3,2,1,0:T(8,128)(2,1)S(1)} %get-tuple-element.41) | copy-start | bytes 1572868
  31.4 27.5 %copy-start.1 = (bf16[64,1152]{1,0:T(8,128)(2,1)}, bf16[64,1152]{1,0:T(8,128)(2,1)S(1)}, u32[]{:S(2)}) copy-start(bf16[64,1152]{1,0:T(8,128)(2,1)S(1)} %get-tuple-element.52.refs_5_.refs_8_) | copy-start | bytes 442372
  33.7 25.3 %copy-start.3 = (bf16[2,7,16,1024]{3,2,1,0:T(8,128)(2,1)}, bf16[2,7,16,1024]{3,2,1,0:T(8,128)(2,1)S(1)}, u32[]{:S(2)}) copy-start(bf16[2,7,16,1024]{3,2,1,0:T(8,128)(2,1)S(1)} %get-tuple-element.44.refs_0_) | copy-start | bytes 1376260
  33.7 11.3 %collective-permute-start.8 = (bf16[2,3,16,1024]{3,2,1,0:T(8,128)(2,1)S(1)}, bf16[2,3,16,1024]{3,2,1,0:T(8,128)(2,1)S(1)}, u32[]{:S(2)}, u32[]{:S(2)}) collective-permute-start(bf16[2,3,16,1024]{3,2,1,0:T(8,128)(2,1)S(1)} %get-tuple-element.43), channel_id=1, source_target_pairs={{0,8},{8,0},{16,24},{24,16},{1,9},{9,1},{17,25},{25,17},{2,10},{10... | collective-permute-start | bytes 589832 | tf_op jit(solution)/shard_map/ppermute | solution.py:690
  34.3 10.7 %collective-permute-start.7 = (bf16[64,1152]{1,0:T(8,128)(2,1)S(1)}, bf16[64,1152]{1,0:T(8,128)(2,1)S(1)}, u32[]{:S(2)}, u32[]{:S(2)}) collective-permute-start(bf16[64,1152]{1,0:T(8,128)(2,1)S(1)} %get-tuple-element.52.refs_5_.refs_8_), channel_id=1, source_target_pairs={{0,4},{2,6},{4,0},{6,2},{1,5},{3,7},{5,1},{7,3},{8,12},{10,14},{12... | collective-permute-start | bytes 442376 | tf_op jit(solution)/shard_map/ppermute | solution.py:690
  36.8 15.1 %collective-permute-start.11 = (bf16[2,3,16,1024]{3,2,1,0:T(8,128)(2,1)S(1)}, bf16[2,3,16,1024]{3,2,1,0:T(8,128)(2,1)S(1)}, u32[]{:S(2)}, u32[]{:S(2)}) collective-permute-start(bf16[2,3,16,1024]{3,2,1,0:T(8,128)(2,1)S(1)} %get-tuple-element.50), channel_id=1, source_target_pairs={{0,24},{8,16},{16,8},{24,0},{1,25},{9,17},{17,9},{25,1},{2,26},{10... | collective-permute-start | bytes 589832 | tf_op jit(solution)/shard_map/ppermute | solution.py:690
  38.3 10.2 %collective-permute-start.10 = (bf16[64,1152]{1,0:T(8,128)(2,1)S(1)}, bf16[64,1152]{1,0:T(8,128)(2,1)S(1)}, u32[]{:S(2)}, u32[]{:S(2)}) collective-permute-start(bf16[64,1152]{1,0:T(8,128)(2,1)S(1)} %get-tuple-element.52.refs_5_.refs_8_), channel_id=1, source_target_pairs={{0,2},{2,0},{4,6},{6,4},{1,3},{3,1},{5,7},{7,5},{8,10},{10,8},{12,... | collective-permute-start | bytes 442376 | tf_op jit(solution)/shard_map/ppermute | solution.py:690
  39.9 12.5 %collective-permute-start.9 = (bf16[2,3,16,1024]{3,2,1,0:T(8,128)(2,1)S(1)}, bf16[2,3,16,1024]{3,2,1,0:T(8,128)(2,1)S(1)}, u32[]{:S(2)}, u32[]{:S(2)}) collective-permute-start(bf16[2,3,16,1024]{3,2,1,0:T(8,128)(2,1)S(1)} %get-tuple-element.46), channel_id=1, source_target_pairs={{0,16},{8,24},{16,0},{24,8},{1,17},{9,25},{17,1},{25,9},{2,18},{10... | collective-permute-start | bytes 589832 | tf_op jit(solution)/shard_map/ppermute | solution.py:690
  45.0 14.0 %copy-start.14 = (bf16[64,1152]{1,0:T(8,128)(2,1)}, bf16[64,1152]{1,0:T(8,128)(2,1)S(1)}, u32[]{:S(2)}) copy-start(bf16[64,1152]{1,0:T(8,128)(2,1)S(1)} %collective-permute-done.7.refs_10_) | copy-start | bytes 442372
  45.0 14.0 %copy-start.8 = (bf16[2,3,16,1024]{3,2,1,0:T(8,128)(2,1)}, bf16[2,3,16,1024]{3,2,1,0:T(8,128)(2,1)S(1)}, u32[]{:S(2)}) copy-start(bf16[2,3,16,1024]{3,2,1,0:T(8,128)(2,1)S(1)} %collective-permute-done.8.refs_1_) | copy-start | bytes 589828
  45.0 14.0 %collective-permute-start.12 = (bf16[2,7,16,1024]{3,2,1,0:T(8,128)(2,1)S(1)}, bf16[2,7,16,1024]{3,2,1,0:T(8,128)(2,1)S(1)}, u32[]{:S(2)}, u32[]{:S(2)}) collective-permute-start(bf16[2,7,16,1024]{3,2,1,0:T(8,128)(2,1)S(1)} %get-tuple-element.44.refs_0_), channel_id=1, source_target_pairs={{0,1},{1,0},{2,3},{3,2},{4,5},{5,4},{6,7},{7,6},{8,9},{9,8},{10,11... | collective-permute-start | bytes 1376264 | tf_op jit(solution)/shard_map/ppermute | solution.py:690
  45.1 21.1 %all-to-all-start.1 = ((bf16[8,16,2048]{2,1,0:T(8,128)(2,1)}), bf16[8,16,2048]{2,1,0:T(8,128)(2,1)S(1)}, u32[]{:S(2)}, u32[]{:S(2)}) async-start(bf16[8,16,2048]{2,1,0:T(8,128)(2,1)} %bitcast.12), calls=%async_computation.1 | async-start | bytes 1048576 | tf_op jit(solution)/shard_map/all_to_all | solution.py:797
  48.6 10.4 %copy-start.15 = (bf16[64,1152]{1,0:T(8,128)(2,1)}, bf16[64,1152]{1,0:T(8,128)(2,1)S(1)}, u32[]{:S(2)}) copy-start(bf16[64,1152]{1,0:T(8,128)(2,1)S(1)} %collective-permute-done.10.refs_9_) | copy-start | bytes 442372
  48.6 8.2 %collective-permute-start.16 = (bf16[64,1152]{1,0:T(8,128)(2,1)S(1)}, bf16[64,1152]{1,0:T(8,128)(2,1)S(1)}, u32[]{:S(2)}, u32[]{:S(2)}) collective-permute-start(bf16[64,1152]{1,0:T(8,128)(2,1)S(1)} %get-tuple-element.52.refs_5_.refs_8_), channel_id=1, source_target_pairs={{0,6},{2,4},{4,2},{6,0},{1,7},{3,5},{5,3},{7,1},{8,14},{10,12},{12... | collective-permute-start | bytes 442376 | tf_op jit(solution)/shard_map/ppermute | solution.py:690
  51.9 4.9 %collective-permute-start.17 = (bf16[64,1152]{1,0:T(8,128)(2,1)S(1)}, bf16[64,1152]{1,0:T(8,128)(2,1)S(1)}, u32[]{:S(2)}, u32[]{:S(2)}) collective-permute-start(bf16[64,1152]{1,0:T(8,128)(2,1)S(1)} %get-tuple-element.52.refs_5_.refs_8_), channel_id=1, source_target_pairs={{0,1},{1,0},{2,3},{3,2},{4,5},{5,4},{6,7},{7,6},{8,9},{9,8},{10,11... | collective-permute-start | bytes 442376 | tf_op jit(solution)/shard_map/ppermute | solution.py:690
  52.1 5.2 %collective-permute-start.18 = (bf16[64,1152]{1,0:T(8,128)(2,1)S(1)}, bf16[64,1152]{1,0:T(8,128)(2,1)S(1)}, u32[]{:S(2)}, u32[]{:S(2)}) collective-permute-start(bf16[64,1152]{1,0:T(8,128)(2,1)S(1)} %collective-permute-done.10.refs_9_), channel_id=1, source_target_pairs={{0,1},{1,0},{2,3},{3,2},{4,5},{5,4},{6,7},{7,6},{8,9},{9,8},{10,11... | collective-permute-start | bytes 442376 | tf_op jit(solution)/shard_map/ppermute | solution.py:690
  52.4 5.0 %collective-permute-start.19 = (bf16[64,1152]{1,0:T(8,128)(2,1)S(1)}, bf16[64,1152]{1,0:T(8,128)(2,1)S(1)}, u32[]{:S(2)}, u32[]{:S(2)}) collective-permute-start(bf16[64,1152]{1,0:T(8,128)(2,1)S(1)} %collective-permute-done.7.refs_10_), channel_id=1, source_target_pairs={{0,1},{1,0},{2,3},{3,2},{4,5},{5,4},{6,7},{7,6},{8,9},{9,8},{10,11... | collective-permute-start | bytes 442376 | tf_op jit(solution)/shard_map/ppermute | solution.py:690
  56.8 1.4 %collective-permute-start.13 = (bf16[2,3,16,1024]{3,2,1,0:T(8,128)(2,1)S(1)}, bf16[2,3,16,1024]{3,2,1,0:T(8,128)(2,1)S(1)}, u32[]{:S(2)}, u32[]{:S(2)}) collective-permute-start(bf16[2,3,16,1024]{3,2,1,0:T(8,128)(2,1)S(1)} %collective-permute-done.8.refs_1_), channel_id=1, source_target_pairs={{0,1},{1,0},{2,3},{3,2},{4,5},{5,4},{6,7},{7,6},{8,9},{9,8},{10,11... | collective-permute-start | bytes 589832 | tf_op jit(solution)/shard_map/ppermute | solution.py:690
  56.8 1.7 %collective-permute-start.14 = (bf16[2,3,16,1024]{3,2,1,0:T(8,128)(2,1)S(1)}, bf16[2,3,16,1024]{3,2,1,0:T(8,128)(2,1)S(1)}, u32[]{:S(2)}, u32[]{:S(2)}) collective-permute-start(bf16[2,3,16,1024]{3,2,1,0:T(8,128)(2,1)S(1)} %collective-permute-done.9.refs_2_), channel_id=1, source_target_pairs={{0,1},{1,0},{2,3},{3,2},{4,5},{5,4},{6,7},{7,6},{8,9},{9,8},{10,11... | collective-permute-start | bytes 589832 | tf_op jit(solution)/shard_map/ppermute | solution.py:690
  57.3 1.5 %collective-permute-start.15 = (bf16[2,3,16,1024]{3,2,1,0:T(8,128)(2,1)S(1)}, bf16[2,3,16,1024]{3,2,1,0:T(8,128)(2,1)S(1)}, u32[]{:S(2)}, u32[]{:S(2)}) collective-permute-start(bf16[2,3,16,1024]{3,2,1,0:T(8,128)(2,1)S(1)} %collective-permute-done.11.refs_3_), channel_id=1, source_target_pairs={{0,1},{1,0},{2,3},{3,2},{4,5},{5,4},{6,7},{7,6},{8,9},{9,8},{10,11... | collective-permute-start | bytes 589832 | tf_op jit(solution)/shard_map/ppermute | solution.py:690
  57.4 1.6 %collective-permute-start.20 = (bf16[64,1152]{1,0:T(8,128)(2,1)S(1)}, bf16[64,1152]{1,0:T(8,128)(2,1)S(1)}, u32[]{:S(2)}, u32[]{:S(2)}) collective-permute-start(bf16[64,1152]{1,0:T(8,128)(2,1)S(1)} %collective-permute-done.16.refs_11_), channel_id=1, source_target_pairs={{0,1},{1,0},{2,3},{3,2},{4,5},{5,4},{6,7},{7,6},{8,9},{9,8},{10,11... | collective-permute-start | bytes 442376 | tf_op jit(solution)/shard_map/ppermute | solution.py:690
  (12 other events, 26.3 us)

commit v21 on v15

--- a/solution.py
+++ b/solution.py
@@ -243,26 +243,35 @@
 def pack_kernel(length, capacity, slots, ids, hidden, cot, send, id_buf, buf, packed, sems):
     groups, _, rows, part = send.shape
     tokens = hidden.shape[0] * length
+    strip = part // 4
     arriving = [
         pltpu.make_async_copy(source, target, sems.at[at])
         for at, (source, target) in enumerate(
             ((ids, id_buf), (hidden, buf.at[0]), (cot, buf.at[1]))
         )
     ]
-    leaving = [
-        pltpu.make_async_copy(packed.at[:, at], send.at[:, at], sems.at[3 + at]) for at in range(2)
-    ]
     for copy in arriving:
         copy.start()
     arriving[0].wait()
     ids_row = spread_ids(id_buf, (8, tokens), length)[:1]
     place, _ = placements(ids_row, length, capacity, slots)
+    leaving = []
     for which in range(2):
         arriving[1 + which].wait()
-        moved = matmul(place, buf[which].reshape(tokens, part)).astype(jnp.bfloat16)
-        for group in range(groups):
-            packed[group, which] = moved[group * rows : (group + 1) * rows]
-        leaving[which].start()
+        for col in range(0, part, strip):
+            here = slice(col, col + strip)
+            moved = matmul(place, buf[which, :, :, here].reshape(tokens, strip))
+            moved = moved.astype(jnp.bfloat16)
+            for group in range(groups):
+                packed[group, which, :, here] = moved[group * rows : (group + 1) * rows]
+            leaving.append(
+                pltpu.make_async_copy(
+                    packed.at[:, which, :, here],
+                    send.at[:, which, :, here],
+                    sems.at[3 + len(leaving)],
+                )
+            )
+            leaving[-1].start()
     for copy in leaving:
         copy.wait()
 
@@ -424,6 +433,8 @@
     ]
     arriving[0].start()
     fetch(0)
+    fetch(1)
+    arriving[1].start()
     waits = [copies(own, at) for at in range(2)]
     cols = range(0, width, CHUNK)
 
@@ -459,8 +470,6 @@
     inverse_0 = inverse_of(entering, mean_0)
     waits[0][0].wait()
     waits[0][2].wait()
-    arriving[1].start()
-    fetch(1)
     pre_0 = down(entering, mean_0, inverse_0, 0)
     act_0 = gelu_value(pre_0).astype(jnp.bfloat16)
     slope_0 = gelu_slope(pre_0)
@@ -734,7 +743,7 @@
             pltpu.SMEM(cluster_ids.shape, jnp.int32),
             pltpu.VMEM((2,) + hidden_in.shape, bf16),
             pltpu.VMEM((groups, 2, rows, part), bf16),
-            pltpu.SemaphoreType.DMA((5,)),
+            pltpu.SemaphoreType.DMA((11,)),
         ],
         outs_in=HBM,
     )(cluster_ids, hidden_in, cotangent)

time: 63.3 us -> 63.9 us (level)
    pallas_call x1, Pallas kernels: 2.37 us -> 3.08 us  [on_device_two_phases(): call(functools.partial(pack_kernel, *sizes), 'pack', 60, [HBM] * 3, [((gr...]
where the time goes in v21:
time: 63.9 us; the launch traced here: 63.6 us
  starting transfers between devices  26.2 us (41%)
  Pallas kernels  20.3 us (32%)
  waiting for transfers between devices  14.6 us (23%)
  local copies, waits for them, and re-layouts  1.52 us (2%)
  between operations  0.91 us (1%)
    ppermute x17, starting transfers between devices, across(): return lax.ppermute(block, axis, [(i, i ^ distance) for i in range(size)])  11.1 us
    ppermute x17, waiting for transfers between devices, across(): return lax.ppermute(block, axis, [(i, i ^ distance) for i in range(size)])  8.28 us
    pallas_call x1, Pallas kernels, on_device_two_phases(): call(chain_kernel, 'chain', 50, [HBM] * 7, [((experts, 2, rows, part), bf...  7 us
    all_to_all x1, waiting for transfers between devices, on_device_two_phases(): lax.all_to_all(send, sections, split_axis=0, concat_axis=0, tiled=True)  6.33 us
    ppermute x4, starting transfers between devices, on_device_two_phases(): lax.ppermute(block, ('dp', 'segment'), slab_route(replicas, turn // 2, tu...  6.28 us
    pallas_call x1, Pallas kernels, on_device_two_phases(): call(functools.partial(gradient_kernel, experts, sources, sizes), 'gradie...  5.83 us
    all_to_all x1, starting transfers between devices, on_device_two_phases(): lax.all_to_all(send, sections, split_axis=0, concat_axis=0, tiled=True)  5.29 us
    all_to_all x1, starting transfers between devices, on_device_two_phases(): lax.all_to_all(out.reshape(groups, rows, part), sections, split_axis=0, c...  3.49 us
  transfers between devices with their start and end apart: 23, of which 7 were waited for; matrix products, arithmetic and copies ran while one was open for 0% of the time, Pallas kernels for 19%

profile of v21, /device:TPU:0, one launch (start us, length us, event | category | flops | bytes accessed | tf_op | source)
XLA Modules:
  0.0 63.6 jit_solution(14137058911308639936)
XLA Ops:
  0.6 0.5 collective-permute-start
  1.2 3.1 %pack.1._ = bf16[8,2,16,2048]{3,2,1,0:T(8,128)(2,1)} custom-call(s32[16]{0:T(128)} %refs_22_.1, bf16[16,4,2048]{2,1,0:T(4,128)(2,1)} %hidden.3, bf16[16,4,2048]{2,1,0:T(4,128)(2,1)} %cot.3), custom_call_target="tpu_custom_call" | custom-call | bytes 1048576 | tf_op jit(solution)/shard_map/pack/pallas_call | solution.py:736
  4.3 5.3 %all-to-all-start = ((bf16[8,2,16,2048]{3,2,1,0:T(8,128)(2,1)}), bf16[8,2,16,2048]{3,2,1,0:T(8,128)(2,1)S(1)}, u32[]{:S(2)}, u32[]{:S(2)}) async-start(bf16[8,2,16,2048]{3,2,1,0:T(8,128)(2,1)} %pack.1._), calls=%async_computation | async-start | bytes 2097152 | tf_op jit(solution)/shard_map/all_to_all | solution.py:766
  9.6 0.5 collective-permute-start.2
  10.1 2.3 %slabs.1 = (bf16[80,1024]{1,0:T(8,128)(2,1)}, bf16[80,1024]{1,0:T(8,128)(2,1)}, bf16[80,1024]{1,0:T(8,128)(2,1)}, bf16[80,1024]{1,0:T(8,128)(2,1)}) custom-call(s32[16]{0:T(128)} %refs_22_.1, bf16[16,4,2048]{2,1,0:T(4,128)(2,1)} %hidden.3, bf16[16,4,2048]{2,1,0:T(4,128)(2,1)} %cot.3, bf16[8,2,16,2048]{3,2,1,0:T(8,128)(2,1)} %pack.1._), custom_call_target="tpu_custom_call" | custom-call | bytes 1048576 | tf_op jit(solution)/shard_map/slabs/pallas_call | solution.py:750
  12.4 1.6 %collective-permute-start.3 = (bf16[80,1024]{1,0:T(8,128)(2,1)}, bf16[80,1024]{1,0:T(8,128)(2,1)S(1)}, u32[]{:S(2)}, u32[]{:S(2)}) collective-permute-start(bf16[80,1024]{1,0:T(8,128)(2,1)} %get-tuple-element.30), channel_id=1, source_target_pairs={{0,0},{1,4},{2,2},{3,6},{4,1},{5,5},{6,3},{7,7},{8,8},{9,12},{10,1... | collective-permute-start | bytes 491528 | tf_op jit(solution)/shard_map/ppermute | solution.py:769
  14.0 3.1 %collective-permute-start.4 = (bf16[80,1024]{1,0:T(8,128)(2,1)}, bf16[80,1024]{1,0:T(8,128)(2,1)}, u32[]{:S(2)}, u32[]{:S(2)}) collective-permute-start(bf16[80,1024]{1,0:T(8,128)(2,1)} %get-tuple-element.31), channel_id=1, source_target_pairs={{0,1},{1,5},{2,3},{3,7},{4,0},{5,4},{6,2},{7,6},{8,9},{9,13},{10,1... | collective-permute-start | bytes 491528 | tf_op jit(solution)/shard_map/ppermute | solution.py:769
  17.1 1.6 %collective-permute-start.5 = (bf16[80,1024]{1,0:T(8,128)(2,1)}, bf16[80,1024]{1,0:T(8,128)(2,1)}, u32[]{:S(2)}, u32[]{:S(2)}) collective-permute-start(bf16[80,1024]{1,0:T(8,128)(2,1)} %get-tuple-element.32), channel_id=1, source_target_pairs={{0,2},{1,6},{2,0},{3,4},{4,3},{5,7},{6,1},{7,5},{8,10},{9,14},{10,... | collective-permute-start | bytes 491528 | tf_op jit(solution)/shard_map/ppermute | solution.py:769
  18.7 6.3 %all-to-all-done = bf16[8,2,16,2048]{3,2,1,0:T(8,128)(2,1)S(1)} async-done(((bf16[8,2,16,2048]{3,2,1,0:T(8,128)(2,1)}), bf16[8,2,16,2048]{3,2,1,0:T(8,128)(2,1)S(1)}, u32[]{:S(2)}, u32[]{:S(2)}) %all-to-all-start) | async-done | bytes 1048608 | tf_op jit(solution)/shard_map/all_to_all | solution.py:766
  25.0 7.0 %chain.1 = (bf16[4,2,16,2048]{3,2,1,0:T(8,128)(2,1)S(1)}, bf16[64,1152]{1,0:T(8,128)(2,1)S(1)}) custom-call(bf16[4,2,2,16,2048]{4,3,2,1,0:T(8,128)(2,1)S(1)} %bitcast.7, bf16[4096,256]{1,0:T(8,128)(2,1)S(1)} %bitcast.11, bf16[256,4096]{1,0:T(8,128)(2,1)} %bitcast.17, bf16[1,4096]{1,0:T(2,128)(2,1)S(1)} %bitcast.15, ...), custom_call_target="tpu_custom_call" | custom-call | flops 939524096 | bytes 10485760 | tf_op jit(solution)/shard_map/chain/pallas_call | solution.py:772
  32.1 2.2 %repack.1 = (bf16[2,7,16,1024]{3,2,1,0:T(8,128)(2,1)S(1)}, bf16[2,3,16,1024]{3,2,1,0:T(8,128)(2,1)S(1)}, bf16[2,3,16,1024]{3,2,1,0:T(8,128)(2,1)S(1)}, bf16[2,3,16,1024]{3,2,1,0:T(8,128)(2,1)S(1)}) custom-call(bf16[80,1024]{1,0:T(8,128)(2,1)S(1)} %collective-permute-done.3.refs_0_, bf16[80,1024]{1,0:T(8,128)(2,1)} %collective-permute-done.4.refs_1_, ...), custom_call_target="tpu_custom_call" | custom-call | bytes 1048576 | tf_op jit(solution)/shard_map/repack/pallas_call | solution.py:791
  34.3 0.6 collective-permute-start.7
  34.9 1.5 %collective-permute-start.11 = (bf16[2,3,16,1024]{3,2,1,0:T(8,128)(2,1)S(1)}, bf16[2,3,16,1024]{3,2,1,0:T(8,128)(2,1)S(1)}, u32[]{:S(2)}, u32[]{:S(2)}) collective-permute-start(bf16[2,3,16,1024]{3,2,1,0:T(8,128)(2,1)S(1)} %get-tuple-element.46), channel_id=1, source_target_pairs={{0,24},{8,16},{16,8},{24,0},{1,25},{9,17},{17,9},{25,1},{2,26},{10... | collective-permute-start | bytes 589832 | tf_op jit(solution)/shard_map/ppermute | solution.py:705
  36.4 2.4 %collective-permute-start.9 = (bf16[64,1152]{1,0:T(8,128)(2,1)S(1)}, bf16[64,1152]{1,0:T(8,128)(2,1)S(1)}, u32[]{:S(2)}, u32[]{:S(2)}) collective-permute-start(bf16[64,1152]{1,0:T(8,128)(2,1)S(1)} %get-tuple-element.48.refs_5_.refs_8_), channel_id=1, source_target_pairs={{0,2},{2,0},{4,6},{6,4},{1,3},{3,1},{5,7},{7,5},{8,10},{10,8},{12,... | collective-permute-start | bytes 442376 | tf_op jit(solution)/shard_map/ppermute | solution.py:705
  38.8 1.8 %collective-permute-start.10 = (bf16[64,1152]{1,0:T(8,128)(2,1)S(1)}, bf16[64,1152]{1,0:T(8,128)(2,1)S(1)}, u32[]{:S(2)}, u32[]{:S(2)}) collective-permute-start(bf16[64,1152]{1,0:T(8,128)(2,1)S(1)} %get-tuple-element.48.refs_5_.refs_8_), channel_id=1, source_target_pairs={{0,4},{2,6},{4,0},{6,2},{1,5},{3,7},{5,1},{7,3},{8,12},{10,14},{12... | collective-permute-start | bytes 442376 | tf_op jit(solution)/shard_map/ppermute | solution.py:705
  40.6 1.5 %collective-permute-start.8 = (bf16[2,3,16,1024]{3,2,1,0:T(8,128)(2,1)S(1)}, bf16[2,3,16,1024]{3,2,1,0:T(8,128)(2,1)S(1)}, u32[]{:S(2)}, u32[]{:S(2)}) collective-permute-start(bf16[2,3,16,1024]{3,2,1,0:T(8,128)(2,1)S(1)} %get-tuple-element.42), channel_id=1, source_target_pairs={{0,16},{8,24},{16,0},{24,8},{1,17},{9,25},{17,1},{25,9},{2,18},{10... | collective-permute-start | bytes 589832 | tf_op jit(solution)/shard_map/ppermute | solution.py:705
  42.0 3.5 %all-to-all-start.1 = ((bf16[8,16,2048]{2,1,0:T(8,128)(2,1)}), bf16[8,16,2048]{2,1,0:T(8,128)(2,1)S(1)}, u32[]{:S(2)}, u32[]{:S(2)}) async-start(bf16[8,16,2048]{2,1,0:T(8,128)(2,1)} %bitcast.12), calls=%async_computation.1 | async-start | bytes 1048576 | tf_op jit(solution)/shard_map/all_to_all | solution.py:811
  45.6 0.5 collective-permute-start.12
  46.0 0.2 collective-permute-start.16
  46.3 0.5 collective-permute-start.18
  46.8 1.9 %collective-permute-done.8.refs_2_ = bf16[2,3,16,1024]{3,2,1,0:T(8,128)(2,1)S(1)} collective-permute-done((bf16[2,3,16,1024]{3,2,1,0:T(8,128)(2,1)S(1)}, bf16[2,3,16,1024]{3,2,1,0:T(8,128)(2,1)S(1)}, u32[]{:S(2)}, u32[]{:S(2)}) %collective-permute-start.8) | collective-permute-done | bytes 196640 | tf_op jit(solution)/shard_map/ppermute | solution.py:705
  48.7 5.1 %collective-permute-done.16.refs_11_ = bf16[64,1152]{1,0:T(8,128)(2,1)S(1)} collective-permute-done((bf16[64,1152]{1,0:T(8,128)(2,1)S(1)}, bf16[64,1152]{1,0:T(8,128)(2,1)S(1)}, u32[]{:S(2)}, u32[]{:S(2)}) %collective-permute-start.16) | collective-permute-done | bytes 147488 | tf_op jit(solution)/shard_map/ppermute | solution.py:705
  53.8 0.5 collective-permute-start.14
  54.4 0.4 collective-permute-start.20
  54.8 0.4 collective-permute-done.13.refs_5_
  55.2 0.3 collective-permute-done.14.refs_6_
  55.5 0.3 collective-permute-done.15.refs_7_
  55.8 0.3 collective-permute-done.20.refs_15_
  56.3 0.2 copy-done.13
  56.5 0.5 copy-done.6
  57.0 0.8 %copy-done.7 = bf16[2,7,16,1024]{3,2,1,0:T(8,128)(2,1)} copy-done((bf16[2,7,16,1024]{3,2,1,0:T(8,128)(2,1)}, bf16[2,7,16,1024]{3,2,1,0:T(8,128)(2,1)S(1)}, u32[]{:S(2)}) %copy-start.7) | copy-done | bytes 458776
  57.7 5.8 %gradients.1 = (bf16[16,4,2048]{2,1,0:T(4,128)(2,1)}, bf16[1024,256]{1,0:T(8,128)(2,1)}, bf16[256,1024]{1,0:T(8,128)(2,1)}) custom-call(bf16[2,7,16,1024]{3,2,1,0:T(8,128)(2,1)} %copy-done.3, bf16[2,3,16,1024]{3,2,1,0:T(8,128)(2,1)} %copy-done.8, bf16[2,3,16,1024]{3,2,1,0:T(8,128)(2,1)} %copy-done.10, bf16[2,3,16,1024]{3,2,1,0:T(8,128)(2,1)} %copy-done.9, ...), custom_call_target="tpu_custom_call" | custom-call | bytes 1048576 | tf_op jit(solution)/shard_map/gradients/pallas_call | solution.py:817
  (57 shorter events, 0.4 us)
Async XLA Ops:
  0.6 18.1 %collective-permute-start = (bf16[4096,256]{1,0:T(8,128)(2,1)}, bf16[4096,256]{1,0:T(8,128)(2,1)}, u32[]{:S(2)}, u32[]{:S(2)}) collective-permute-start(bf16[4096,256]{1,0:T(8,128)(2,1)} %bitcast.9), channel_id=1, source_target_pairs={{0,1},{1,0},{2,3},{3,2},{4,5},{5,4},{6,7},{7,6},{8,9},{9,8},{10,11... | collective-permute-start | bytes 6291464 | tf_op jit(solution)/shard_map/ppermute | solution.py:705
  1.2 23.9 %collective-permute-start.1 = (bf16[256,4096]{1,0:T(8,128)(2,1)}, bf16[256,4096]{1,0:T(8,128)(2,1)}, u32[]{:S(2)}, u32[]{:S(2)}) collective-permute-start(bf16[256,4096]{1,0:T(8,128)(2,1)} %bitcast.16), channel_id=1, source_target_pairs={{0,1},{1,0},{2,3},{3,2},{4,5},{5,4},{6,7},{7,6},{8,9},{9,8},{10,11... | collective-permute-start | bytes 6291464 | tf_op jit(solution)/shard_map/ppermute | solution.py:705
  4.3 20.7 %copy-start = (bf16[1,1,4096,256]{3,2,1,0:T(8,128)(2,1)S(1)}, bf16[1,1,4096,256]{3,2,1,0:T(8,128)(2,1)}, u32[]{:S(2)}) copy-start(bf16[1,1,4096,256]{3,2,1,0:T(8,128)(2,1)} %param.9) | copy-start | bytes 6291460
  4.3 20.7 %all-to-all-start = ((bf16[8,2,16,2048]{3,2,1,0:T(8,128)(2,1)}), bf16[8,2,16,2048]{3,2,1,0:T(8,128)(2,1)S(1)}, u32[]{:S(2)}, u32[]{:S(2)}) async-start(bf16[8,2,16,2048]{3,2,1,0:T(8,128)(2,1)} %pack.1._), calls=%async_computation | async-start | bytes 2097152 | tf_op jit(solution)/shard_map/all_to_all | solution.py:766
  9.6 7.5 %collective-permute-start.2 = (bf16[1,4096]{1,0:T(2,128)(2,1)S(1)}, bf16[1,4096]{1,0:T(2,128)(2,1)S(1)}, u32[]{:S(2)}, u32[]{:S(2)}) collective-permute-start(bf16[1,4096]{1,0:T(2,128)(2,1)S(1)} %bitcast.14), channel_id=1, source_target_pairs={{0,1},{1,0},{2,3},{3,2},{4,5},{5,4},{6,7},{7,6},{8,9},{9,8},{10,11... | collective-permute-start | bytes 24584 | tf_op jit(solution)/shard_map/ppermute | solution.py:705
  12.4 19.7 %collective-permute-start.3 = (bf16[80,1024]{1,0:T(8,128)(2,1)}, bf16[80,1024]{1,0:T(8,128)(2,1)S(1)}, u32[]{:S(2)}, u32[]{:S(2)}) collective-permute-start(bf16[80,1024]{1,0:T(8,128)(2,1)} %get-tuple-element.30), channel_id=1, source_target_pairs={{0,0},{1,4},{2,2},{3,6},{4,1},{5,5},{6,3},{7,7},{8,8},{9,12},{10,1... | collective-permute-start | bytes 491528 | tf_op jit(solution)/shard_map/ppermute | solution.py:769
  14.0 18.1 %collective-permute-start.4 = (bf16[80,1024]{1,0:T(8,128)(2,1)}, bf16[80,1024]{1,0:T(8,128)(2,1)}, u32[]{:S(2)}, u32[]{:S(2)}) collective-permute-start(bf16[80,1024]{1,0:T(8,128)(2,1)} %get-tuple-element.31), channel_id=1, source_target_pairs={{0,1},{1,5},{2,3},{3,7},{4,0},{5,4},{6,2},{7,6},{8,9},{9,13},{10,1... | collective-permute-start | bytes 491528 | tf_op jit(solution)/shard_map/ppermute | solution.py:769
  17.1 14.9 %copy-start.5 = (bf16[1,4096]{1,0:T(2,128)(2,1)}, bf16[1,4096]{1,0:T(2,128)(2,1)S(1)}, u32[]{:S(2)}) copy-start(bf16[1,4096]{1,0:T(2,128)(2,1)S(1)} %collective-permute-done.2.other_gain.refs_21_) | copy-start | bytes 24580
  17.1 15.0 %collective-permute-start.5 = (bf16[80,1024]{1,0:T(8,128)(2,1)}, bf16[80,1024]{1,0:T(8,128)(2,1)}, u32[]{:S(2)}, u32[]{:S(2)}) collective-permute-start(bf16[80,1024]{1,0:T(8,128)(2,1)} %get-tuple-element.32), channel_id=1, source_target_pairs={{0,2},{1,6},{2,0},{3,4},{4,3},{5,7},{6,1},{7,5},{8,10},{9,14},{10,... | collective-permute-start | bytes 491528 | tf_op jit(solution)/shard_map/ppermute | solution.py:769
  18.7 13.4 %collective-permute-start.6 = (bf16[80,1024]{1,0:T(8,128)(2,1)}, bf16[80,1024]{1,0:T(8,128)(2,1)}, u32[]{:S(2)}, u32[]{:S(2)}) collective-permute-start(bf16[80,1024]{1,0:T(8,128)(2,1)} %get-tuple-element.33), channel_id=1, source_target_pairs={{0,3},{1,7},{2,1},{3,5},{4,2},{5,6},{6,0},{7,4},{8,11},{9,15},{10,... | collective-permute-start | bytes 491528 | tf_op jit(solution)/shard_map/ppermute | solution.py:769
  32.1 10.0 %copy-start.2 = (bf16[4,2,16,2048]{3,2,1,0:T(8,128)(2,1)}, bf16[4,2,16,2048]{3,2,1,0:T(8,128)(2,1)S(1)}, u32[]{:S(2)}) copy-start(bf16[4,2,16,2048]{3,2,1,0:T(8,128)(2,1)S(1)} %get-tuple-element.51) | copy-start | bytes 1572868
  32.1 24.1 %copy-start.1 = (bf16[64,1152]{1,0:T(8,128)(2,1)}, bf16[64,1152]{1,0:T(8,128)(2,1)S(1)}, u32[]{:S(2)}) copy-start(bf16[64,1152]{1,0:T(8,128)(2,1)S(1)} %get-tuple-element.48.refs_5_.refs_8_) | copy-start | bytes 442372
  34.3 21.9 %copy-start.3 = (bf16[2,7,16,1024]{3,2,1,0:T(8,128)(2,1)}, bf16[2,7,16,1024]{3,2,1,0:T(8,128)(2,1)S(1)}, u32[]{:S(2)}) copy-start(bf16[2,7,16,1024]{3,2,1,0:T(8,128)(2,1)S(1)} %get-tuple-element.40.refs_0_) | copy-start | bytes 1376260
  34.3 11.2 %collective-permute-start.7 = (bf16[2,3,16,1024]{3,2,1,0:T(8,128)(2,1)S(1)}, bf16[2,3,16,1024]{3,2,1,0:T(8,128)(2,1)S(1)}, u32[]{:S(2)}, u32[]{:S(2)}) collective-permute-start(bf16[2,3,16,1024]{3,2,1,0:T(8,128)(2,1)S(1)} %get-tuple-element.39), channel_id=1, source_target_pairs={{0,8},{8,0},{16,24},{24,16},{1,9},{9,1},{17,25},{25,17},{2,10},{10... | collective-permute-start | bytes 589832 | tf_op jit(solution)/shard_map/ppermute | solution.py:705
  34.9 11.4 %collective-permute-start.11 = (bf16[2,3,16,1024]{3,2,1,0:T(8,128)(2,1)S(1)}, bf16[2,3,16,1024]{3,2,1,0:T(8,128)(2,1)S(1)}, u32[]{:S(2)}, u32[]{:S(2)}) collective-permute-start(bf16[2,3,16,1024]{3,2,1,0:T(8,128)(2,1)S(1)} %get-tuple-element.46), channel_id=1, source_target_pairs={{0,24},{8,16},{16,8},{24,0},{1,25},{9,17},{17,9},{25,1},{2,26},{10... | collective-permute-start | bytes 589832 | tf_op jit(solution)/shard_map/ppermute | solution.py:705
  36.4 9.6 %collective-permute-start.9 = (bf16[64,1152]{1,0:T(8,128)(2,1)S(1)}, bf16[64,1152]{1,0:T(8,128)(2,1)S(1)}, u32[]{:S(2)}, u32[]{:S(2)}) collective-permute-start(bf16[64,1152]{1,0:T(8,128)(2,1)S(1)} %get-tuple-element.48.refs_5_.refs_8_), channel_id=1, source_target_pairs={{0,2},{2,0},{4,6},{6,4},{1,3},{3,1},{5,7},{7,5},{8,10},{10,8},{12,... | collective-permute-start | bytes 442376 | tf_op jit(solution)/shard_map/ppermute | solution.py:705
  38.8 7.4 %collective-permute-start.10 = (bf16[64,1152]{1,0:T(8,128)(2,1)S(1)}, bf16[64,1152]{1,0:T(8,128)(2,1)S(1)}, u32[]{:S(2)}, u32[]{:S(2)}) collective-permute-start(bf16[64,1152]{1,0:T(8,128)(2,1)S(1)} %get-tuple-element.48.refs_5_.refs_8_), channel_id=1, source_target_pairs={{0,4},{2,6},{4,0},{6,2},{1,5},{3,7},{5,1},{7,3},{8,12},{10,14},{12... | collective-permute-start | bytes 442376 | tf_op jit(solution)/shard_map/ppermute | solution.py:705
  40.6 8.1 %collective-permute-start.8 = (bf16[2,3,16,1024]{3,2,1,0:T(8,128)(2,1)S(1)}, bf16[2,3,16,1024]{3,2,1,0:T(8,128)(2,1)S(1)}, u32[]{:S(2)}, u32[]{:S(2)}) collective-permute-start(bf16[2,3,16,1024]{3,2,1,0:T(8,128)(2,1)S(1)} %get-tuple-element.42), channel_id=1, source_target_pairs={{0,16},{8,24},{16,0},{24,8},{1,17},{9,25},{17,1},{25,9},{2,18},{10... | collective-permute-start | bytes 589832 | tf_op jit(solution)/shard_map/ppermute | solution.py:705
  42.0 14.1 %all-to-all-start.1 = ((bf16[8,16,2048]{2,1,0:T(8,128)(2,1)}), bf16[8,16,2048]{2,1,0:T(8,128)(2,1)S(1)}, u32[]{:S(2)}, u32[]{:S(2)}) async-start(bf16[8,16,2048]{2,1,0:T(8,128)(2,1)} %bitcast.12), calls=%async_computation.1 | async-start | bytes 1048576 | tf_op jit(solution)/shard_map/all_to_all | solution.py:811
  45.5 10.6 %copy-start.8 = (bf16[2,3,16,1024]{3,2,1,0:T(8,128)(2,1)}, bf16[2,3,16,1024]{3,2,1,0:T(8,128)(2,1)S(1)}, u32[]{:S(2)}) copy-start(bf16[2,3,16,1024]{3,2,1,0:T(8,128)(2,1)S(1)} %collective-permute-done.7.refs_1_) | copy-start | bytes 589828
  45.6 10.6 %collective-permute-start.12 = (bf16[2,7,16,1024]{3,2,1,0:T(8,128)(2,1)S(1)}, bf16[2,7,16,1024]{3,2,1,0:T(8,128)(2,1)S(1)}, u32[]{:S(2)}, u32[]{:S(2)}) collective-permute-start(bf16[2,7,16,1024]{3,2,1,0:T(8,128)(2,1)S(1)} %get-tuple-element.40.refs_0_), channel_id=1, source_target_pairs={{0,1},{1,0},{2,3},{3,2},{4,5},{5,4},{6,7},{7,6},{8,9},{9,8},{10,11... | collective-permute-start | bytes 1376264 | tf_op jit(solution)/shard_map/ppermute | solution.py:705
  46.0 10.2 %copy-start.14 = (bf16[64,1152]{1,0:T(8,128)(2,1)}, bf16[64,1152]{1,0:T(8,128)(2,1)S(1)}, u32[]{:S(2)}) copy-start(bf16[64,1152]{1,0:T(8,128)(2,1)S(1)} %collective-permute-done.9.refs_9_) | copy-start | bytes 442372
  46.0 7.8 %collective-permute-start.16 = (bf16[64,1152]{1,0:T(8,128)(2,1)S(1)}, bf16[64,1152]{1,0:T(8,128)(2,1)S(1)}, u32[]{:S(2)}, u32[]{:S(2)}) collective-permute-start(bf16[64,1152]{1,0:T(8,128)(2,1)S(1)} %get-tuple-element.48.refs_5_.refs_8_), channel_id=1, source_target_pairs={{0,6},{2,4},{4,2},{6,0},{1,7},{3,5},{5,3},{7,1},{8,14},{10,12},{12... | collective-permute-start | bytes 442376 | tf_op jit(solution)/shard_map/ppermute | solution.py:705
  46.2 10.0 %copy-start.15 = (bf16[64,1152]{1,0:T(8,128)(2,1)}, bf16[64,1152]{1,0:T(8,128)(2,1)S(1)}, u32[]{:S(2)}) copy-start(bf16[64,1152]{1,0:T(8,128)(2,1)S(1)} %collective-permute-done.10.refs_10_) | copy-start | bytes 442372
  46.3 10.0 %copy-start.9 = (bf16[2,3,16,1024]{3,2,1,0:T(8,128)(2,1)}, bf16[2,3,16,1024]{3,2,1,0:T(8,128)(2,1)S(1)}, u32[]{:S(2)}) copy-start(bf16[2,3,16,1024]{3,2,1,0:T(8,128)(2,1)S(1)} %collective-permute-done.11.refs_3_) | copy-start | bytes 589828
  46.3 7.5 %collective-permute-start.17 = (bf16[64,1152]{1,0:T(8,128)(2,1)S(1)}, bf16[64,1152]{1,0:T(8,128)(2,1)S(1)}, u32[]{:S(2)}, u32[]{:S(2)}) collective-permute-start(bf16[64,1152]{1,0:T(8,128)(2,1)S(1)} %get-tuple-element.48.refs_5_.refs_8_), channel_id=1, source_target_pairs={{0,1},{1,0},{2,3},{3,2},{4,5},{5,4},{6,7},{7,6},{8,9},{9,8},{10,11... | collective-permute-start | bytes 442376 | tf_op jit(solution)/shard_map/ppermute | solution.py:705
  46.3 8.0 %collective-permute-start.18 = (bf16[64,1152]{1,0:T(8,128)(2,1)S(1)}, bf16[64,1152]{1,0:T(8,128)(2,1)}, u32[]{:S(2)}, u32[]{:S(2)}) collective-permute-start(bf16[64,1152]{1,0:T(8,128)(2,1)S(1)} %collective-permute-done.9.refs_9_), channel_id=1, source_target_pairs={{0,1},{1,0},{2,3},{3,2},{4,5},{5,4},{6,7},{7,6},{8,9},{9,8},{10,11... | collective-permute-start | bytes 442376 | tf_op jit(solution)/shard_map/ppermute | solution.py:705
  48.7 5.7 %collective-permute-start.19 = (bf16[64,1152]{1,0:T(8,128)(2,1)S(1)}, bf16[64,1152]{1,0:T(8,128)(2,1)S(1)}, u32[]{:S(2)}, u32[]{:S(2)}) collective-permute-start(bf16[64,1152]{1,0:T(8,128)(2,1)S(1)} %collective-permute-done.10.refs_10_), channel_id=1, source_target_pairs={{0,1},{1,0},{2,3},{3,2},{4,5},{5,4},{6,7},{7,6},{8,9},{9,8},{10,11... | collective-permute-start | bytes 442376 | tf_op jit(solution)/shard_map/ppermute | solution.py:705
  53.8 1.4 %collective-permute-start.13 = (bf16[2,3,16,1024]{3,2,1,0:T(8,128)(2,1)S(1)}, bf16[2,3,16,1024]{3,2,1,0:T(8,128)(2,1)S(1)}, u32[]{:S(2)}, u32[]{:S(2)}) collective-permute-start(bf16[2,3,16,1024]{3,2,1,0:T(8,128)(2,1)S(1)} %collective-permute-done.7.refs_1_), channel_id=1, source_target_pairs={{0,1},{1,0},{2,3},{3,2},{4,5},{5,4},{6,7},{7,6},{8,9},{9,8},{10,11... | collective-permute-start | bytes 589832 | tf_op jit(solution)/shard_map/ppermute | solution.py:705
  53.8 1.7 %collective-permute-start.14 = (bf16[2,3,16,1024]{3,2,1,0:T(8,128)(2,1)S(1)}, bf16[2,3,16,1024]{3,2,1,0:T(8,128)(2,1)S(1)}, u32[]{:S(2)}, u32[]{:S(2)}) collective-permute-start(bf16[2,3,16,1024]{3,2,1,0:T(8,128)(2,1)S(1)} %collective-permute-done.8.refs_2_), channel_id=1, source_target_pairs={{0,1},{1,0},{2,3},{3,2},{4,5},{5,4},{6,7},{7,6},{8,9},{9,8},{10,11... | collective-permute-start | bytes 589832 | tf_op jit(solution)/shard_map/ppermute | solution.py:705
  54.3 1.5 %collective-permute-start.15 = (bf16[2,3,16,1024]{3,2,1,0:T(8,128)(2,1)S(1)}, bf16[2,3,16,1024]{3,2,1,0:T(8,128)(2,1)S(1)}, u32[]{:S(2)}, u32[]{:S(2)}) collective-permute-start(bf16[2,3,16,1024]{3,2,1,0:T(8,128)(2,1)S(1)} %collective-permute-done.11.refs_3_), channel_id=1, source_target_pairs={{0,1},{1,0},{2,3},{3,2},{4,5},{5,4},{6,7},{7,6},{8,9},{9,8},{10,11... | collective-permute-start | bytes 589832 | tf_op jit(solution)/shard_map/ppermute | solution.py:705
  54.4 1.7 %collective-permute-start.20 = (bf16[64,1152]{1,0:T(8,128)(2,1)S(1)}, bf16[64,1152]{1,0:T(8,128)(2,1)}, u32[]{:S(2)}, u32[]{:S(2)}) collective-permute-start(bf16[64,1152]{1,0:T(8,128)(2,1)S(1)} %collective-permute-done.16.refs_11_), channel_id=1, source_target_pairs={{0,1},{1,0},{2,3},{3,2},{4,5},{5,4},{6,7},{7,6},{8,9},{9,8},{10,11... | collective-permute-start | bytes 442376 | tf_op jit(solution)/shard_map/ppermute | solution.py:705
  (10 other events, 26.8 us)

commit v22 on v15

--- a/solution.py
+++ b/solution.py
@@ -797,7 +797,10 @@
     *near, mine[-1] = lax.optimization_barrier((*near, mine[-1]))
     near.append(last)
     theirs = [across(block, "segment", 1) for block in mine]
-    smalls = near + [across(piece, "segment", 1) for piece in near]
+    swapped = [across(piece, "segment", 1) for piece in near[:-1]]
+    near[-1], *rest = lax.optimization_barrier((near[-1], *theirs[1:], *swapped))
+    theirs[1:], swapped = rest[: experts - 1], rest[experts - 1 :]
+    smalls = near + swapped + [across(near[-1], "segment", 1)]
 
     back = lax.all_to_all(
         out.reshape(groups, rows, part), sections, split_axis=0, concat_axis=0, tiled=True

time: 63.3 us -> 71 us (1.12)
  starting transfers between devices: 26.2 us -> 31.9 us
  waiting for transfers between devices: 14.6 us -> 15.9 us
    all_to_all x1, waiting for transfers between devices: 0.01 us -> 5.11 us  [on_device_two_phases(): lax.all_to_all(out.reshape(groups, rows, part), sections, split_axis=0, c...]
    all_to_all x1, starting transfers between devices: 3.49 us -> 7.85 us  [on_device_two_phases(): lax.all_to_all(out.reshape(groups, rows, part), sections, split_axis=0, c...]
    ppermute x17, waiting for transfers between devices: 8.27 us -> 4.44 us  [across(): return lax.ppermute(block, axis, [(i, i ^ distance) for i in range(size)])]
    ppermute x17, starting transfers between devices: 11.1 us -> 12.5 us  [across(): return lax.ppermute(block, axis, [(i, i ^ distance) for i in range(size)])]
    unnamed x38 -> x40, local copies, waits for them, and re-layouts: 1.52 us -> 2.12 us
  transfers between devices with their start and end apart: 23 -> 23, of which waited for: 7 -> 5; matrix products, arithmetic and copies ran while one was open for 0% -> 0% of each run, Pallas kernels for 19% -> 17%
where the time goes in v22:
time: 71 us; the launch traced here: 70.6 us
  starting transfers between devices  31.9 us (45%)
  Pallas kernels  19.7 us (28%)
  waiting for transfers between devices  15.9 us (22%)
  local copies, waits for them, and re-layouts  2.12 us (3%)
  between operations  0.93 us (1%)
    ppermute x17, starting transfers between devices, across(): return lax.ppermute(block, axis, [(i, i ^ distance) for i in range(size)])  12.5 us
    all_to_all x1, starting transfers between devices, on_device_two_phases(): lax.all_to_all(out.reshape(groups, rows, part), sections, split_axis=0, c...  7.85 us
    pallas_call x1, Pallas kernels, on_device_two_phases(): call(chain_kernel, 'chain', 50, [HBM] * 7, [((experts, 2, rows, part), bf...  7.1 us
    all_to_all x1, waiting for transfers between devices, on_device_two_phases(): lax.all_to_all(send, sections, split_axis=0, concat_axis=0, tiled=True)  6.33 us
    ppermute x4, starting transfers between devices, on_device_two_phases(): lax.ppermute(block, ('dp', 'segment'), slab_route(replicas, turn // 2, tu...  6.29 us
    pallas_call x1, Pallas kernels, on_device_two_phases(): call(functools.partial(gradient_kernel, experts, sources, sizes), 'gradie...  5.83 us
    all_to_all x1, starting transfers between devices, on_device_two_phases(): lax.all_to_all(send, sections, split_axis=0, concat_axis=0, tiled=True)  5.29 us
    all_to_all x1, waiting for transfers between devices, on_device_two_phases(): lax.all_to_all(out.reshape(groups, rows, part), sections, split_axis=0, c...  5.11 us
  transfers between devices with their start and end apart: 23, of which 5 were waited for; matrix products, arithmetic and copies ran while one was open for 0% of the time, Pallas kernels for 17%

profile of v22, /device:TPU:0, one launch (start us, length us, event | category | flops | bytes accessed | tf_op | source)
XLA Modules:
  0.0 70.6 jit_solution(8232280126360852102)
XLA Ops:
  0.6 0.5 collective-permute-start
  1.2 2.4 %pack.1._ = bf16[8,2,16,2048]{3,2,1,0:T(8,128)(2,1)} custom-call(s32[16]{0:T(128)} %refs_22_.1, bf16[16,4,2048]{2,1,0:T(4,128)(2,1)} %hidden.3, bf16[16,4,2048]{2,1,0:T(4,128)(2,1)} %cot.3), custom_call_target="tpu_custom_call" | custom-call | bytes 1048576 | tf_op jit(solution)/shard_map/pack/pallas_call | solution.py:727
  3.6 5.3 %all-to-all-start = ((bf16[8,2,16,2048]{3,2,1,0:T(8,128)(2,1)}), bf16[8,2,16,2048]{3,2,1,0:T(8,128)(2,1)S(1)}, u32[]{:S(2)}, u32[]{:S(2)}) async-start(bf16[8,2,16,2048]{3,2,1,0:T(8,128)(2,1)} %pack.1._), calls=%async_computation | async-start | bytes 2097152 | tf_op jit(solution)/shard_map/all_to_all | solution.py:757
  8.9 0.5 collective-permute-start.2
  9.4 2.3 %slabs.1 = (bf16[80,1024]{1,0:T(8,128)(2,1)}, bf16[80,1024]{1,0:T(8,128)(2,1)}, bf16[80,1024]{1,0:T(8,128)(2,1)}, bf16[80,1024]{1,0:T(8,128)(2,1)}) custom-call(s32[16]{0:T(128)} %refs_22_.1, bf16[16,4,2048]{2,1,0:T(4,128)(2,1)} %hidden.3, bf16[16,4,2048]{2,1,0:T(4,128)(2,1)} %cot.3, bf16[8,2,16,2048]{3,2,1,0:T(8,128)(2,1)} %pack.1._), custom_call_target="tpu_custom_call" | custom-call | bytes 1048576 | tf_op jit(solution)/shard_map/slabs/pallas_call | solution.py:741
  11.7 1.6 %collective-permute-start.3 = (bf16[80,1024]{1,0:T(8,128)(2,1)}, bf16[80,1024]{1,0:T(8,128)(2,1)S(1)}, u32[]{:S(2)}, u32[]{:S(2)}) collective-permute-start(bf16[80,1024]{1,0:T(8,128)(2,1)} %get-tuple-element.37), channel_id=1, source_target_pairs={{0,0},{1,4},{2,2},{3,6},{4,1},{5,5},{6,3},{7,7},{8,8},{9,12},{10,1... | collective-permute-start | bytes 491528 | tf_op jit(solution)/shard_map/ppermute | solution.py:760
  13.3 3.1 %collective-permute-start.4 = (bf16[80,1024]{1,0:T(8,128)(2,1)}, bf16[80,1024]{1,0:T(8,128)(2,1)}, u32[]{:S(2)}, u32[]{:S(2)}) collective-permute-start(bf16[80,1024]{1,0:T(8,128)(2,1)} %get-tuple-element.38), channel_id=1, source_target_pairs={{0,1},{1,5},{2,3},{3,7},{4,0},{5,4},{6,2},{7,6},{8,9},{9,13},{10,1... | collective-permute-start | bytes 491528 | tf_op jit(solution)/shard_map/ppermute | solution.py:760
  16.4 1.6 %collective-permute-start.5 = (bf16[80,1024]{1,0:T(8,128)(2,1)}, bf16[80,1024]{1,0:T(8,128)(2,1)}, u32[]{:S(2)}, u32[]{:S(2)}) collective-permute-start(bf16[80,1024]{1,0:T(8,128)(2,1)} %get-tuple-element.39), channel_id=1, source_target_pairs={{0,2},{1,6},{2,0},{3,4},{4,3},{5,7},{6,1},{7,5},{8,10},{9,14},{10,... | collective-permute-start | bytes 491528 | tf_op jit(solution)/shard_map/ppermute | solution.py:760
  18.0 6.3 %all-to-all-done = bf16[8,2,16,2048]{3,2,1,0:T(8,128)(2,1)S(1)} async-done(((bf16[8,2,16,2048]{3,2,1,0:T(8,128)(2,1)}), bf16[8,2,16,2048]{3,2,1,0:T(8,128)(2,1)S(1)}, u32[]{:S(2)}, u32[]{:S(2)}) %all-to-all-start) | async-done | bytes 1048608 | tf_op jit(solution)/shard_map/all_to_all | solution.py:757
  24.4 7.1 %chain.1 = (bf16[4,2,16,2048]{3,2,1,0:T(8,128)(2,1)S(1)}, bf16[64,1152]{1,0:T(8,128)(2,1)S(1)}) custom-call(bf16[4,2,2,16,2048]{4,3,2,1,0:T(8,128)(2,1)S(1)} %bitcast.7, bf16[4096,256]{1,0:T(8,128)(2,1)S(1)} %bitcast.11, bf16[256,4096]{1,0:T(8,128)(2,1)} %bitcast.17, bf16[1,4096]{1,0:T(2,128)(2,1)S(1)} %bitcast.15, ...), custom_call_target="tpu_custom_call" | custom-call | flops 939524096 | bytes 10485760 | tf_op jit(solution)/shard_map/chain/pallas_call | solution.py:763
  31.5 2.2 %repack.1 = (bf16[2,7,16,1024]{3,2,1,0:T(8,128)(2,1)S(1)}, bf16[2,3,16,1024]{3,2,1,0:T(8,128)(2,1)S(1)}, bf16[2,3,16,1024]{3,2,1,0:T(8,128)(2,1)S(1)}, bf16[2,3,16,1024]{3,2,1,0:T(8,128)(2,1)S(1)}) custom-call(bf16[80,1024]{1,0:T(8,128)(2,1)S(1)} %collective-permute-done.3.refs_0_, bf16[80,1024]{1,0:T(8,128)(2,1)} %collective-permute-done.4.refs_1_, ...), custom_call_target="tpu_custom_call" | custom-call | bytes 1048576 | tf_op jit(solution)/shard_map/repack/pallas_call | solution.py:782
  33.7 0.9 %collective-permute-start.11 = (bf16[2,3,16,1024]{3,2,1,0:T(8,128)(2,1)S(1)}, bf16[2,3,16,1024]{3,2,1,0:T(8,128)(2,1)S(1)}, u32[]{:S(2)}, u32[]{:S(2)}) collective-permute-start(bf16[2,3,16,1024]{3,2,1,0:T(8,128)(2,1)S(1)} %get-tuple-element.53), channel_id=1, source_target_pairs={{0,24},{8,16},{16,8},{24,0},{1,25},{9,17},{17,9},{25,1},{2,26},{10... | collective-permute-start | bytes 589832 | tf_op jit(solution)/shard_map/ppermute | solution.py:696
  34.6 1.2 %collective-permute-start.7 = (bf16[2,3,16,1024]{3,2,1,0:T(8,128)(2,1)S(1)}, bf16[2,3,16,1024]{3,2,1,0:T(8,128)(2,1)S(1)}, u32[]{:S(2)}, u32[]{:S(2)}) collective-permute-start(bf16[2,3,16,1024]{3,2,1,0:T(8,128)(2,1)S(1)} %get-tuple-element.46), channel_id=1, source_target_pairs={{0,8},{8,0},{16,24},{24,16},{1,9},{9,1},{17,25},{25,17},{2,10},{10... | collective-permute-start | bytes 589832 | tf_op jit(solution)/shard_map/ppermute | solution.py:696
  35.8 2.3 %collective-permute-start.9 = (bf16[64,1152]{1,0:T(8,128)(2,1)S(1)}, bf16[64,1152]{1,0:T(8,128)(2,1)S(1)}, u32[]{:S(2)}, u32[]{:S(2)}) collective-permute-start(bf16[64,1152]{1,0:T(8,128)(2,1)S(1)} %get-tuple-element.55.refs_5_.refs_8_), channel_id=1, source_target_pairs={{0,2},{2,0},{4,6},{6,4},{1,3},{3,1},{5,7},{7,5},{8,10},{10,8},{12,... | collective-permute-start | bytes 442376 | tf_op jit(solution)/shard_map/ppermute | solution.py:696
  38.1 1.8 %collective-permute-start.10 = (bf16[64,1152]{1,0:T(8,128)(2,1)S(1)}, bf16[64,1152]{1,0:T(8,128)(2,1)S(1)}, u32[]{:S(2)}, u32[]{:S(2)}) collective-permute-start(bf16[64,1152]{1,0:T(8,128)(2,1)S(1)} %get-tuple-element.55.refs_5_.refs_8_), channel_id=1, source_target_pairs={{0,4},{2,6},{4,0},{6,2},{1,5},{3,7},{5,1},{7,3},{8,12},{10,14},{12... | collective-permute-start | bytes 442376 | tf_op jit(solution)/shard_map/ppermute | solution.py:696
  40.0 1.5 %collective-permute-start.8 = (bf16[2,3,16,1024]{3,2,1,0:T(8,128)(2,1)S(1)}, bf16[2,3,16,1024]{3,2,1,0:T(8,128)(2,1)S(1)}, u32[]{:S(2)}, u32[]{:S(2)}) collective-permute-start(bf16[2,3,16,1024]{3,2,1,0:T(8,128)(2,1)S(1)} %get-tuple-element.49), channel_id=1, source_target_pairs={{0,16},{8,24},{16,0},{24,8},{1,17},{9,25},{17,1},{25,9},{2,18},{10... | collective-permute-start | bytes 589832 | tf_op jit(solution)/shard_map/ppermute | solution.py:696
  41.4 2.8 %collective-permute-done.9.refs_9_ = bf16[64,1152]{1,0:T(8,128)(2,1)S(1)} collective-permute-done((bf16[64,1152]{1,0:T(8,128)(2,1)S(1)}, bf16[64,1152]{1,0:T(8,128)(2,1)S(1)}, u32[]{:S(2)}, u32[]{:S(2)}) %collective-permute-start.9) | collective-permute-done | bytes 147488 | tf_op jit(solution)/shard_map/ppermute | solution.py:696
  44.2 1.3 %collective-permute-start.13 = (bf16[64,1152]{1,0:T(8,128)(2,1)S(1)}, bf16[64,1152]{1,0:T(8,128)(2,1)S(1)}, u32[]{:S(2)}, u32[]{:S(2)}) collective-permute-start(bf16[64,1152]{1,0:T(8,128)(2,1)S(1)} %get-tuple-element.55.refs_5_.refs_8_), channel_id=1, source_target_pairs={{0,6},{2,4},{4,2},{6,0},{1,7},{3,5},{5,3},{7,1},{8,14},{10,12},{12... | collective-permute-start | bytes 442376 | tf_op jit(solution)/shard_map/ppermute | solution.py:696
  45.6 7.8 %all-to-all-start.1 = ((bf16[8,16,2048]{2,1,0:T(8,128)(2,1)}), bf16[8,16,2048]{2,1,0:T(8,128)(2,1)S(1)}, u32[]{:S(2)}, u32[]{:S(2)}) async-start(bf16[8,16,2048]{2,1,0:T(8,128)(2,1)} %bitcast.12), calls=%async_computation.1 | async-start | bytes 1048576 | tf_op jit(solution)/shard_map/all_to_all | solution.py:805
  53.5 0.6 collective-permute-start.12
  54.1 0.4 collective-permute-start.14
  54.6 0.1 collective-permute-start.15
  54.7 0.4 collective-permute-start.16
  55.1 0.6 collective-permute-done.18.refs_13_
  55.7 0.4 collective-permute-start.19
  56.1 1.0 %collective-permute-done.19.refs_14_ = bf16[64,1152]{1,0:T(8,128)(2,1)S(1)} collective-permute-done((bf16[64,1152]{1,0:T(8,128)(2,1)S(1)}, bf16[64,1152]{1,0:T(8,128)(2,1)S(1)}, u32[]{:S(2)}, u32[]{:S(2)}) %collective-permute-start.19) | collective-permute-done | bytes 147488 | tf_op jit(solution)/shard_map/ppermute | solution.py:696
  57.1 0.6 copy-done.19
  57.7 0.4 collective-permute-start.20
  58.1 5.1 %all-to-all-done.1.refs_23_ = bf16[8,16,2048]{2,1,0:T(8,128)(2,1)S(1)} async-done(((bf16[8,16,2048]{2,1,0:T(8,128)(2,1)}), bf16[8,16,2048]{2,1,0:T(8,128)(2,1)S(1)}, u32[]{:S(2)}, u32[]{:S(2)}) %all-to-all-start.1) | async-done | bytes 524320 | tf_op jit(solution)/shard_map/all_to_all | solution.py:805
  63.3 0.7 copy-done.6
  64.0 0.8 %copy-done.7 = bf16[2,7,16,1024]{3,2,1,0:T(8,128)(2,1)} copy-done((bf16[2,7,16,1024]{3,2,1,0:T(8,128)(2,1)}, bf16[2,7,16,1024]{3,2,1,0:T(8,128)(2,1)S(1)}, u32[]{:S(2)}) %copy-start.7) | copy-done | bytes 458776
  64.8 5.8 %gradients.1 = (bf16[16,4,2048]{2,1,0:T(4,128)(2,1)}, bf16[1024,256]{1,0:T(8,128)(2,1)}, bf16[256,1024]{1,0:T(8,128)(2,1)}) custom-call(bf16[2,7,16,1024]{3,2,1,0:T(8,128)(2,1)} %copy-done.3, bf16[2,3,16,1024]{3,2,1,0:T(8,128)(2,1)} %copy-done.9, bf16[2,3,16,1024]{3,2,1,0:T(8,128)(2,1)} %copy-done.10, bf16[2,3,16,1024]{3,2,1,0:T(8,128)(2,1)} %copy-done.8, ...), custom_call_target="tpu_custom_call" | custom-call | bytes 1048576 | tf_op jit(solution)/shard_map/gradients/pallas_call | solution.py:811
  (59 shorter events, 0.4 us)
Async XLA Ops:
  0.6 17.4 %collective-permute-start = (bf16[4096,256]{1,0:T(8,128)(2,1)}, bf16[4096,256]{1,0:T(8,128)(2,1)}, u32[]{:S(2)}, u32[]{:S(2)}) collective-permute-start(bf16[4096,256]{1,0:T(8,128)(2,1)} %bitcast.9), channel_id=1, source_target_pairs={{0,1},{1,0},{2,3},{3,2},{4,5},{5,4},{6,7},{7,6},{8,9},{9,8},{10,11... | collective-permute-start | bytes 6291464 | tf_op jit(solution)/shard_map/ppermute | solution.py:696
  1.2 23.2 %collective-permute-start.1 = (bf16[256,4096]{1,0:T(8,128)(2,1)}, bf16[256,4096]{1,0:T(8,128)(2,1)}, u32[]{:S(2)}, u32[]{:S(2)}) collective-permute-start(bf16[256,4096]{1,0:T(8,128)(2,1)} %bitcast.16), channel_id=1, source_target_pairs={{0,1},{1,0},{2,3},{3,2},{4,5},{5,4},{6,7},{7,6},{8,9},{9,8},{10,11... | collective-permute-start | bytes 6291464 | tf_op jit(solution)/shard_map/ppermute | solution.py:696
  3.6 20.7 %copy-start = (bf16[1,1,4096,256]{3,2,1,0:T(8,128)(2,1)S(1)}, bf16[1,1,4096,256]{3,2,1,0:T(8,128)(2,1)}, u32[]{:S(2)}) copy-start(bf16[1,1,4096,256]{3,2,1,0:T(8,128)(2,1)} %param.9) | copy-start | bytes 6291460
  3.6 20.7 %all-to-all-start = ((bf16[8,2,16,2048]{3,2,1,0:T(8,128)(2,1)}), bf16[8,2,16,2048]{3,2,1,0:T(8,128)(2,1)S(1)}, u32[]{:S(2)}, u32[]{:S(2)}) async-start(bf16[8,2,16,2048]{3,2,1,0:T(8,128)(2,1)} %pack.1._), calls=%async_computation | async-start | bytes 2097152 | tf_op jit(solution)/shard_map/all_to_all | solution.py:757
  8.9 7.5 %collective-permute-start.2 = (bf16[1,4096]{1,0:T(2,128)(2,1)S(1)}, bf16[1,4096]{1,0:T(2,128)(2,1)S(1)}, u32[]{:S(2)}, u32[]{:S(2)}) collective-permute-start(bf16[1,4096]{1,0:T(2,128)(2,1)S(1)} %bitcast.14), channel_id=1, source_target_pairs={{0,1},{1,0},{2,3},{3,2},{4,5},{5,4},{6,7},{7,6},{8,9},{9,8},{10,11... | collective-permute-start | bytes 24584 | tf_op jit(solution)/shard_map/ppermute | solution.py:696
  11.7 19.8 %collective-permute-start.3 = (bf16[80,1024]{1,0:T(8,128)(2,1)}, bf16[80,1024]{1,0:T(8,128)(2,1)S(1)}, u32[]{:S(2)}, u32[]{:S(2)}) collective-permute-start(bf16[80,1024]{1,0:T(8,128)(2,1)} %get-tuple-element.37), channel_id=1, source_target_pairs={{0,0},{1,4},{2,2},{3,6},{4,1},{5,5},{6,3},{7,7},{8,8},{9,12},{10,1... | collective-permute-start | bytes 491528 | tf_op jit(solution)/shard_map/ppermute | solution.py:760
  13.3 18.2 %collective-permute-start.4 = (bf16[80,1024]{1,0:T(8,128)(2,1)}, bf16[80,1024]{1,0:T(8,128)(2,1)}, u32[]{:S(2)}, u32[]{:S(2)}) collective-permute-start(bf16[80,1024]{1,0:T(8,128)(2,1)} %get-tuple-element.38), channel_id=1, source_target_pairs={{0,1},{1,5},{2,3},{3,7},{4,0},{5,4},{6,2},{7,6},{8,9},{9,13},{10,1... | collective-permute-start | bytes 491528 | tf_op jit(solution)/shard_map/ppermute | solution.py:760
  16.4 15.0 %copy-start.5 = (bf16[1,4096]{1,0:T(2,128)(2,1)}, bf16[1,4096]{1,0:T(2,128)(2,1)S(1)}, u32[]{:S(2)}) copy-start(bf16[1,4096]{1,0:T(2,128)(2,1)S(1)} %collective-permute-done.2.other_gain.refs_21_) | copy-start | bytes 24580
  16.4 15.1 %collective-permute-start.5 = (bf16[80,1024]{1,0:T(8,128)(2,1)}, bf16[80,1024]{1,0:T(8,128)(2,1)}, u32[]{:S(2)}, u32[]{:S(2)}) collective-permute-start(bf16[80,1024]{1,0:T(8,128)(2,1)} %get-tuple-element.39), channel_id=1, source_target_pairs={{0,2},{1,6},{2,0},{3,4},{4,3},{5,7},{6,1},{7,5},{8,10},{9,14},{10,... | collective-permute-start | bytes 491528 | tf_op jit(solution)/shard_map/ppermute | solution.py:760
  18.0 13.5 %collective-permute-start.6 = (bf16[80,1024]{1,0:T(8,128)(2,1)}, bf16[80,1024]{1,0:T(8,128)(2,1)}, u32[]{:S(2)}, u32[]{:S(2)}) collective-permute-start(bf16[80,1024]{1,0:T(8,128)(2,1)} %get-tuple-element.40), channel_id=1, source_target_pairs={{0,3},{1,7},{2,1},{3,5},{4,2},{5,6},{6,0},{7,4},{8,11},{9,15},{10,... | collective-permute-start | bytes 491528 | tf_op jit(solution)/shard_map/ppermute | solution.py:760
  31.5 14.1 %copy-start.2 = (bf16[4,2,16,2048]{3,2,1,0:T(8,128)(2,1)}, bf16[4,2,16,2048]{3,2,1,0:T(8,128)(2,1)S(1)}, u32[]{:S(2)}) copy-start(bf16[4,2,16,2048]{3,2,1,0:T(8,128)(2,1)S(1)} %get-tuple-element.65) | copy-start | bytes 1572868
  31.5 31.7 %copy-start.1 = (bf16[64,1152]{1,0:T(8,128)(2,1)}, bf16[64,1152]{1,0:T(8,128)(2,1)S(1)}, u32[]{:S(2)}) copy-start(bf16[64,1152]{1,0:T(8,128)(2,1)S(1)} %get-tuple-element.55.refs_5_.refs_8_) | copy-start | bytes 442372
  33.7 29.5 %copy-start.3 = (bf16[2,7,16,1024]{3,2,1,0:T(8,128)(2,1)}, bf16[2,7,16,1024]{3,2,1,0:T(8,128)(2,1)S(1)}, u32[]{:S(2)}) copy-start(bf16[2,7,16,1024]{3,2,1,0:T(8,128)(2,1)S(1)} %get-tuple-element.47.refs_0_) | copy-start | bytes 1376260
  33.7 11.8 %collective-permute-start.11 = (bf16[2,3,16,1024]{3,2,1,0:T(8,128)(2,1)S(1)}, bf16[2,3,16,1024]{3,2,1,0:T(8,128)(2,1)S(1)}, u32[]{:S(2)}, u32[]{:S(2)}) collective-permute-start(bf16[2,3,16,1024]{3,2,1,0:T(8,128)(2,1)S(1)} %get-tuple-element.53), channel_id=1, source_target_pairs={{0,24},{8,16},{16,8},{24,0},{1,25},{9,17},{17,9},{25,1},{2,26},{10... | collective-permute-start | bytes 589832 | tf_op jit(solution)/shard_map/ppermute | solution.py:696
  34.6 18.9 %collective-permute-start.7 = (bf16[2,3,16,1024]{3,2,1,0:T(8,128)(2,1)S(1)}, bf16[2,3,16,1024]{3,2,1,0:T(8,128)(2,1)S(1)}, u32[]{:S(2)}, u32[]{:S(2)}) collective-permute-start(bf16[2,3,16,1024]{3,2,1,0:T(8,128)(2,1)S(1)} %get-tuple-element.46), channel_id=1, source_target_pairs={{0,8},{8,0},{16,24},{24,16},{1,9},{9,1},{17,25},{25,17},{2,10},{10... | collective-permute-start | bytes 589832 | tf_op jit(solution)/shard_map/ppermute | solution.py:696
  35.8 8.4 %collective-permute-start.9 = (bf16[64,1152]{1,0:T(8,128)(2,1)S(1)}, bf16[64,1152]{1,0:T(8,128)(2,1)S(1)}, u32[]{:S(2)}, u32[]{:S(2)}) collective-permute-start(bf16[64,1152]{1,0:T(8,128)(2,1)S(1)} %get-tuple-element.55.refs_5_.refs_8_), channel_id=1, source_target_pairs={{0,2},{2,0},{4,6},{6,4},{1,3},{3,1},{5,7},{7,5},{8,10},{10,8},{12,... | collective-permute-start | bytes 442376 | tf_op jit(solution)/shard_map/ppermute | solution.py:696
  38.1 7.4 %collective-permute-start.10 = (bf16[64,1152]{1,0:T(8,128)(2,1)S(1)}, bf16[64,1152]{1,0:T(8,128)(2,1)S(1)}, u32[]{:S(2)}, u32[]{:S(2)}) collective-permute-start(bf16[64,1152]{1,0:T(8,128)(2,1)S(1)} %get-tuple-element.55.refs_5_.refs_8_), channel_id=1, source_target_pairs={{0,4},{2,6},{4,0},{6,2},{1,5},{3,7},{5,1},{7,3},{8,12},{10,14},{12... | collective-permute-start | bytes 442376 | tf_op jit(solution)/shard_map/ppermute | solution.py:696
  40.0 14.2 %collective-permute-start.8 = (bf16[2,3,16,1024]{3,2,1,0:T(8,128)(2,1)S(1)}, bf16[2,3,16,1024]{3,2,1,0:T(8,128)(2,1)S(1)}, u32[]{:S(2)}, u32[]{:S(2)}) collective-permute-start(bf16[2,3,16,1024]{3,2,1,0:T(8,128)(2,1)S(1)} %get-tuple-element.49), channel_id=1, source_target_pairs={{0,16},{8,24},{16,0},{24,8},{1,17},{9,25},{17,1},{25,9},{2,18},{10... | collective-permute-start | bytes 589832 | tf_op jit(solution)/shard_map/ppermute | solution.py:696
  44.2 19.0 %copy-start.14 = (bf16[64,1152]{1,0:T(8,128)(2,1)}, bf16[64,1152]{1,0:T(8,128)(2,1)S(1)}, u32[]{:S(2)}) copy-start(bf16[64,1152]{1,0:T(8,128)(2,1)S(1)} %collective-permute-done.9.refs_9_) | copy-start | bytes 442372
  44.2 10.3 %collective-permute-start.13 = (bf16[64,1152]{1,0:T(8,128)(2,1)S(1)}, bf16[64,1152]{1,0:T(8,128)(2,1)S(1)}, u32[]{:S(2)}, u32[]{:S(2)}) collective-permute-start(bf16[64,1152]{1,0:T(8,128)(2,1)S(1)} %get-tuple-element.55.refs_5_.refs_8_), channel_id=1, source_target_pairs={{0,6},{2,4},{4,2},{6,0},{1,7},{3,5},{5,3},{7,1},{8,14},{10,12},{12... | collective-permute-start | bytes 442376 | tf_op jit(solution)/shard_map/ppermute | solution.py:696
  45.5 17.7 %copy-start.15 = (bf16[64,1152]{1,0:T(8,128)(2,1)}, bf16[64,1152]{1,0:T(8,128)(2,1)S(1)}, u32[]{:S(2)}) copy-start(bf16[64,1152]{1,0:T(8,128)(2,1)S(1)} %collective-permute-done.10.refs_10_) | copy-start | bytes 442372
  45.5 17.7 %copy-start.8 = (bf16[2,3,16,1024]{3,2,1,0:T(8,128)(2,1)}, bf16[2,3,16,1024]{3,2,1,0:T(8,128)(2,1)S(1)}, u32[]{:S(2)}) copy-start(bf16[2,3,16,1024]{3,2,1,0:T(8,128)(2,1)S(1)} %collective-permute-done.11.refs_3_) | copy-start | bytes 589828
  45.5 9.1 %collective-permute-start.17 = (bf16[64,1152]{1,0:T(8,128)(2,1)S(1)}, bf16[64,1152]{1,0:T(8,128)(2,1)S(1)}, u32[]{:S(2)}, u32[]{:S(2)}) collective-permute-start(bf16[64,1152]{1,0:T(8,128)(2,1)S(1)} %get-tuple-element.55.refs_5_.refs_8_), channel_id=1, source_target_pairs={{0,1},{1,0},{2,3},{3,2},{4,5},{5,4},{6,7},{7,6},{8,9},{9,8},{10,11... | collective-permute-start | bytes 442376 | tf_op jit(solution)/shard_map/ppermute | solution.py:696
  45.6 17.6 %all-to-all-start.1 = ((bf16[8,16,2048]{2,1,0:T(8,128)(2,1)}), bf16[8,16,2048]{2,1,0:T(8,128)(2,1)S(1)}, u32[]{:S(2)}, u32[]{:S(2)}) async-start(bf16[8,16,2048]{2,1,0:T(8,128)(2,1)} %bitcast.12), calls=%async_computation.1 | async-start | bytes 1048576 | tf_op jit(solution)/shard_map/all_to_all | solution.py:805
  53.5 9.8 %copy-start.9 = (bf16[2,3,16,1024]{3,2,1,0:T(8,128)(2,1)}, bf16[2,3,16,1024]{3,2,1,0:T(8,128)(2,1)S(1)}, u32[]{:S(2)}) copy-start(bf16[2,3,16,1024]{3,2,1,0:T(8,128)(2,1)S(1)} %collective-permute-done.7.refs_1_) | copy-start | bytes 589828
  53.5 9.7 %collective-permute-start.12 = (bf16[2,7,16,1024]{3,2,1,0:T(8,128)(2,1)S(1)}, bf16[2,7,16,1024]{3,2,1,0:T(8,128)(2,1)S(1)}, u32[]{:S(2)}, u32[]{:S(2)}) collective-permute-start(bf16[2,7,16,1024]{3,2,1,0:T(8,128)(2,1)S(1)} %get-tuple-element.47.refs_0_), channel_id=1, source_target_pairs={{0,1},{1,0},{2,3},{3,2},{4,5},{5,4},{6,7},{7,6},{8,9},{9,8},{10,11... | collective-permute-start | bytes 1376264 | tf_op jit(solution)/shard_map/ppermute | solution.py:696
  54.0 1.7 %collective-permute-start.18 = (bf16[64,1152]{1,0:T(8,128)(2,1)S(1)}, bf16[64,1152]{1,0:T(8,128)(2,1)S(1)}, u32[]{:S(2)}, u32[]{:S(2)}) collective-permute-start(bf16[64,1152]{1,0:T(8,128)(2,1)S(1)} %collective-permute-done.9.refs_9_), channel_id=1, source_target_pairs={{0,1},{1,0},{2,3},{3,2},{4,5},{5,4},{6,7},{7,6},{8,9},{9,8},{10,11... | collective-permute-start | bytes 442376 | tf_op jit(solution)/shard_map/ppermute | solution.py:696
  54.1 3.0 %collective-permute-start.14 = (bf16[2,3,16,1024]{3,2,1,0:T(8,128)(2,1)S(1)}, bf16[2,3,16,1024]{3,2,1,0:T(8,128)(2,1)S(1)}, u32[]{:S(2)}, u32[]{:S(2)}) collective-permute-start(bf16[2,3,16,1024]{3,2,1,0:T(8,128)(2,1)S(1)} %collective-permute-done.7.refs_1_), channel_id=1, source_target_pairs={{0,1},{1,0},{2,3},{3,2},{4,5},{5,4},{6,7},{7,6},{8,9},{9,8},{10,11... | collective-permute-start | bytes 589832 | tf_op jit(solution)/shard_map/ppermute | solution.py:696
  54.6 2.5 %collective-permute-start.15 = (bf16[2,3,16,1024]{3,2,1,0:T(8,128)(2,1)S(1)}, bf16[2,3,16,1024]{3,2,1,0:T(8,128)(2,1)S(1)}, u32[]{:S(2)}, u32[]{:S(2)}) collective-permute-start(bf16[2,3,16,1024]{3,2,1,0:T(8,128)(2,1)S(1)} %collective-permute-done.8.refs_2_), channel_id=1, source_target_pairs={{0,1},{1,0},{2,3},{3,2},{4,5},{5,4},{6,7},{7,6},{8,9},{9,8},{10,11... | collective-permute-start | bytes 589832 | tf_op jit(solution)/shard_map/ppermute | solution.py:696
  54.7 2.5 %collective-permute-start.16 = (bf16[2,3,16,1024]{3,2,1,0:T(8,128)(2,1)S(1)}, bf16[2,3,16,1024]{3,2,1,0:T(8,128)(2,1)S(1)}, u32[]{:S(2)}, u32[]{:S(2)}) collective-permute-start(bf16[2,3,16,1024]{3,2,1,0:T(8,128)(2,1)S(1)} %collective-permute-done.11.refs_3_), channel_id=1, source_target_pairs={{0,1},{1,0},{2,3},{3,2},{4,5},{5,4},{6,7},{7,6},{8,9},{9,8},{10,11... | collective-permute-start | bytes 589832 | tf_op jit(solution)/shard_map/ppermute | solution.py:696
  55.7 1.4 %collective-permute-start.19 = (bf16[64,1152]{1,0:T(8,128)(2,1)S(1)}, bf16[64,1152]{1,0:T(8,128)(2,1)S(1)}, u32[]{:S(2)}, u32[]{:S(2)}) collective-permute-start(bf16[64,1152]{1,0:T(8,128)(2,1)S(1)} %collective-permute-done.10.refs_10_), channel_id=1, source_target_pairs={{0,1},{1,0},{2,3},{3,2},{4,5},{5,4},{6,7},{7,6},{8,9},{9,8},{10,11... | collective-permute-start | bytes 442376 | tf_op jit(solution)/shard_map/ppermute | solution.py:696
  57.7 5.5 %collective-permute-start.20 = (bf16[64,1152]{1,0:T(8,128)(2,1)S(1)}, bf16[64,1152]{1,0:T(8,128)(2,1)}, u32[]{:S(2)}, u32[]{:S(2)}) collective-permute-start(bf16[64,1152]{1,0:T(8,128)(2,1)S(1)} %collective-permute-done.13.refs_11_), channel_id=1, source_target_pairs={{0,1},{1,0},{2,3},{3,2},{4,5},{5,4},{6,7},{7,6},{8,9},{9,8},{10,11... | collective-permute-start | bytes 442376 | tf_op jit(solution)/shard_map/ppermute | solution.py:696
  (11 other events, 56.5 us)

commit v23 on v15

--- a/solution.py
+++ b/solution.py
@@ -518,8 +518,15 @@
             small[pl.ds(start, rows), cols] = value[e * rows : (e + 1) * rows]
 
 
+def stack_kernel(*refs):
+    at = 0
+    for block in refs[:-1]:
+        refs[-1][:, at : at + block.shape[1]] = block[...]
+        at += block.shape[1]
+
+
 def gradient_kernel(experts, sources, sizes, *refs):
-    sides, refs = refs[: 2 * experts], refs[2 * experts :]
+    sides, refs = refs[:2], refs[2:]
     smalls, refs = refs[:sources], refs[sources:]
     own, other, refs = refs[:3], refs[3:6], refs[6:]
     ids, back_in, out_hidden, grad_dn, grad_upper = refs[:5]
@@ -529,8 +536,8 @@
     place = lax.axis_index("dp")
     rows, slab = smalls[0].shape[0], sides[0].shape[3]
     replicas = sources // 2
-    blocks = [side.shape[1] for side in sides[:experts]]
-    starts = [sum(blocks[:step]) for step in range(experts)]
+    others = replicas - 1
+    starts = [0] + [experts + step * others for step in range(1, experts)]
     rank = dn_buf.shape[1]
     columns = 256
     chunks = range(0, slab, columns)
@@ -562,13 +569,7 @@
         [
             pltpu.make_async_copy(
                 side.at[:, :, :, col : col + columns],
-                wide_buf.at[
-                    at // experts,
-                    :,
-                    starts[at % experts] : starts[at % experts] + blocks[at % experts],
-                    :,
-                    col : col + columns,
-                ],
+                wide_buf.at[at, :, :, :, col : col + columns],
                 wide_sems.at[col // columns, at],
             )
             for at, side in enumerate(sides)
@@ -790,13 +791,19 @@
     )(*slabs, recv, small)
     small, *slices = lax.optimization_barrier((small, *slices))
     mine = [slices[0]] + [across(slices[step], "expert", step) for step in range(1, experts)]
-    mine[:2] = lax.optimization_barrier(tuple(mine[:2]))
     near = [small] + [across(small, "dp", step) for step in range(1, replicas - 1)]
     near[:2] = lax.optimization_barrier(tuple(near[:2]))
     last = across(near[0], "dp", replicas - 1)
-    *near, mine[-1] = lax.optimization_barrier((*near, mine[-1]))
+    (stacked,) = call(
+        stack_kernel,
+        "stack",
+        16,
+        [VMEM] * experts,
+        [((2, replicas * experts, rows, slab), bf16)],
+    )(*mine)
+    *near, stacked = lax.optimization_barrier((*near, stacked))
     near.append(last)
-    theirs = [across(block, "segment", 1) for block in mine]
+    theirs = across(stacked, "segment", 1)
     smalls = near + [across(piece, "segment", 1) for piece in near]
 
     back = lax.all_to_all(
@@ -809,7 +816,7 @@
         functools.partial(gradient_kernel, experts, sources, sizes),
         "gradients",
         60,
-        [HBM] * (2 * experts + sources + 8),
+        [HBM] * (2 + sources + 8),
         [(hidden_in.shape, bf16), ((slab, rank), bf16), ((rank, slab), bf16)],
         [
             pltpu.SMEM(cluster_ids.shape, jnp.int32),
@@ -827,11 +834,11 @@
             pltpu.VMEM((slab, rank), bf16),
             pltpu.VMEM((slab // 256, rank, 256), bf16),
             pltpu.SemaphoreType.DMA((sources,)),
-            pltpu.SemaphoreType.DMA((slab // 256, 2 * experts)),
+            pltpu.SemaphoreType.DMA((slab // 256, 2)),
             pltpu.SemaphoreType.DMA((7 + 2 * (slab // 256),)),
         ],
         outs_in=HBM,
-    )(*mine, *theirs, *smalls, *own, *other, cluster_ids, back)
+    )(stacked, theirs, *smalls, *own, *other, cluster_ids, back)
     return (out_hidden, grad_dn[None, None], grad_upper[None, None])
 
 

time: 63.3 us -> 70 us (1.11)
  waiting for transfers between devices: 14.6 us -> 18.7 us
  local copies, waits for them, and re-layouts: 1.52 us -> 2.55 us
  starting transfers between devices: 26.2 us -> 27.2 us
    ppermute x17 -> x14, waiting for transfers between devices: 8.27 us -> 12.3 us  [across(): return lax.ppermute(block, axis, [(i, i ^ distance) for i in range(size)])]
    unnamed x38 -> x26, local copies, waits for them, and re-layouts: 1.52 us -> 2.55 us
    ppermute x17 -> x14, starting transfers between devices: 11.1 us -> 11.5 us  [across(): return lax.ppermute(block, axis, [(i, i ^ distance) for i in range(size)])]
  transfers between devices with their start and end apart: 23 -> 20, of which waited for: 7 -> 7; matrix products, arithmetic and copies ran while one was open for 0% -> 0% of each run, Pallas kernels for 19% -> 17%
where the time goes in v23:
time: 70 us; the launch traced here: 69.6 us
  starting transfers between devices  27.2 us (39%)
  Pallas kernels  20.2 us (29%)
  waiting for transfers between devices  18.7 us (27%)
  local copies, waits for them, and re-layouts  2.55 us (4%)
  between operations  0.85 us (1%)
    ppermute x14, waiting for transfers between devices, across(): return lax.ppermute(block, axis, [(i, i ^ distance) for i in range(size)])  12.3 us
    ppermute x14, starting transfers between devices, across(): return lax.ppermute(block, axis, [(i, i ^ distance) for i in range(size)])  11.5 us
    pallas_call x1, Pallas kernels, on_device_two_phases(): call(chain_kernel, 'chain', 50, [HBM] * 7, [((experts, 2, rows, part), bf...  7.1 us
    all_to_all x1, waiting for transfers between devices, on_device_two_phases(): lax.all_to_all(send, sections, split_axis=0, concat_axis=0, tiled=True)  6.3 us
    ppermute x4, starting transfers between devices, on_device_two_phases(): lax.ppermute(block, ('dp', 'segment'), slab_route(replicas, turn // 2, tu...  6.29 us
    pallas_call x1, Pallas kernels, on_device_two_phases(): call(functools.partial(gradient_kernel, experts, sources, sizes), 'gradie...  6.19 us
    all_to_all x1, starting transfers between devices, on_device_two_phases(): lax.all_to_all(send, sections, split_axis=0, concat_axis=0, tiled=True)  5.29 us
    all_to_all x1, starting transfers between devices, on_device_two_phases(): lax.all_to_all(out.reshape(groups, rows, part), sections, split_axis=0, c...  4.12 us
  transfers between devices with their start and end apart: 20, of which 7 were waited for; matrix products, arithmetic and copies ran while one was open for 0% of the time, Pallas kernels for 17%

profile of v23, /device:TPU:0, one launch (start us, length us, event | category | flops | bytes accessed | tf_op | source)
XLA Modules:
  0.0 69.6 jit_solution(17035211927363830661)
XLA Ops:
  0.6 0.5 collective-permute-start
  1.2 0.1 collective-permute-start.1
  1.2 2.4 %pack.1._ = bf16[8,2,16,2048]{3,2,1,0:T(8,128)(2,1)} custom-call(s32[16]{0:T(128)} %refs_16_.1, bf16[16,4,2048]{2,1,0:T(4,128)(2,1)} %hidden.3, bf16[16,4,2048]{2,1,0:T(4,128)(2,1)} %cot.3), custom_call_target="tpu_custom_call" | custom-call | bytes 1048576 | tf_op jit(solution)/shard_map/pack/pallas_call | solution.py:728
  3.7 5.3 %all-to-all-start = ((bf16[8,2,16,2048]{3,2,1,0:T(8,128)(2,1)}), bf16[8,2,16,2048]{3,2,1,0:T(8,128)(2,1)S(1)}, u32[]{:S(2)}, u32[]{:S(2)}) async-start(bf16[8,2,16,2048]{3,2,1,0:T(8,128)(2,1)} %pack.1._), calls=%async_computation | async-start | bytes 2097152 | tf_op jit(solution)/shard_map/all_to_all | solution.py:758
  9.0 0.5 collective-permute-start.2
  9.5 2.3 %slabs.1 = (bf16[80,1024]{1,0:T(8,128)(2,1)}, bf16[80,1024]{1,0:T(8,128)(2,1)}, bf16[80,1024]{1,0:T(8,128)(2,1)}, bf16[80,1024]{1,0:T(8,128)(2,1)}) custom-call(s32[16]{0:T(128)} %refs_16_.1, bf16[16,4,2048]{2,1,0:T(4,128)(2,1)} %hidden.3, bf16[16,4,2048]{2,1,0:T(4,128)(2,1)} %cot.3, bf16[8,2,16,2048]{3,2,1,0:T(8,128)(2,1)} %pack.1._), custom_call_target="tpu_custom_call" | custom-call | bytes 1048576 | tf_op jit(solution)/shard_map/slabs/pallas_call | solution.py:742
  11.8 1.6 %collective-permute-start.3 = (bf16[80,1024]{1,0:T(8,128)(2,1)}, bf16[80,1024]{1,0:T(8,128)(2,1)S(1)}, u32[]{:S(2)}, u32[]{:S(2)}) collective-permute-start(bf16[80,1024]{1,0:T(8,128)(2,1)} %get-tuple-element.28), channel_id=1, source_target_pairs={{0,0},{1,4},{2,2},{3,6},{4,1},{5,5},{6,3},{7,7},{8,8},{9,12},{10,1... | collective-permute-start | bytes 491528 | tf_op jit(solution)/shard_map/ppermute | solution.py:761
  13.4 3.1 %collective-permute-start.4 = (bf16[80,1024]{1,0:T(8,128)(2,1)}, bf16[80,1024]{1,0:T(8,128)(2,1)}, u32[]{:S(2)}, u32[]{:S(2)}) collective-permute-start(bf16[80,1024]{1,0:T(8,128)(2,1)} %get-tuple-element.29), channel_id=1, source_target_pairs={{0,1},{1,5},{2,3},{3,7},{4,0},{5,4},{6,2},{7,6},{8,9},{9,13},{10,1... | collective-permute-start | bytes 491528 | tf_op jit(solution)/shard_map/ppermute | solution.py:761
  16.5 1.6 %collective-permute-start.5 = (bf16[80,1024]{1,0:T(8,128)(2,1)}, bf16[80,1024]{1,0:T(8,128)(2,1)}, u32[]{:S(2)}, u32[]{:S(2)}) collective-permute-start(bf16[80,1024]{1,0:T(8,128)(2,1)} %get-tuple-element.30), channel_id=1, source_target_pairs={{0,2},{1,6},{2,0},{3,4},{4,3},{5,7},{6,1},{7,5},{8,10},{9,14},{10,... | collective-permute-start | bytes 491528 | tf_op jit(solution)/shard_map/ppermute | solution.py:761
  18.1 6.3 %all-to-all-done = bf16[8,2,16,2048]{3,2,1,0:T(8,128)(2,1)S(1)} async-done(((bf16[8,2,16,2048]{3,2,1,0:T(8,128)(2,1)}), bf16[8,2,16,2048]{3,2,1,0:T(8,128)(2,1)S(1)}, u32[]{:S(2)}, u32[]{:S(2)}) %all-to-all-start) | async-done | bytes 1048608 | tf_op jit(solution)/shard_map/all_to_all | solution.py:758
  24.4 7.1 %chain.1 = (bf16[4,2,16,2048]{3,2,1,0:T(8,128)(2,1)S(1)}, bf16[64,1152]{1,0:T(8,128)(2,1)S(1)}) custom-call(bf16[4,2,2,16,2048]{4,3,2,1,0:T(8,128)(2,1)S(1)} %bitcast.7, bf16[4096,256]{1,0:T(8,128)(2,1)S(1)} %bitcast.11, bf16[256,4096]{1,0:T(8,128)(2,1)} %bitcast.17, bf16[1,4096]{1,0:T(2,128)(2,1)S(1)} %bitcast.15, ...), custom_call_target="tpu_custom_call" | custom-call | flops 939524096 | bytes 10485760 | tf_op jit(solution)/shard_map/chain/pallas_call | solution.py:764
  31.6 2.2 %repack.1 = (bf16[2,7,16,1024]{3,2,1,0:T(8,128)(2,1)S(1)}, bf16[2,3,16,1024]{3,2,1,0:T(8,128)(2,1)S(1)}, bf16[2,3,16,1024]{3,2,1,0:T(8,128)(2,1)S(1)}, bf16[2,3,16,1024]{3,2,1,0:T(8,128)(2,1)S(1)}) custom-call(bf16[80,1024]{1,0:T(8,128)(2,1)S(1)} %collective-permute-done.3.refs_0_, bf16[80,1024]{1,0:T(8,128)(2,1)} %collective-permute-done.4.refs_1_, ...), custom_call_target="tpu_custom_call" | custom-call | bytes 1048576 | tf_op jit(solution)/shard_map/repack/pallas_call | solution.py:783
  33.7 0.6 collective-permute-start.9
  34.3 0.9 %collective-permute-start.10 = (bf16[2,3,16,1024]{3,2,1,0:T(8,128)(2,1)S(1)}, bf16[2,3,16,1024]{3,2,1,0:T(8,128)(2,1)S(1)}, u32[]{:S(2)}, u32[]{:S(2)}) collective-permute-start(bf16[2,3,16,1024]{3,2,1,0:T(8,128)(2,1)S(1)} %get-tuple-element.41), channel_id=1, source_target_pairs={{0,16},{8,24},{16,0},{24,8},{1,17},{9,25},{17,1},{25,9},{2,18},{10... | collective-permute-start | bytes 589832 | tf_op jit(solution)/shard_map/ppermute | solution.py:697
  35.2 2.1 %collective-permute-start.11 = (bf16[2,3,16,1024]{3,2,1,0:T(8,128)(2,1)S(1)}, bf16[2,3,16,1024]{3,2,1,0:T(8,128)(2,1)S(1)}, u32[]{:S(2)}, u32[]{:S(2)}) collective-permute-start(bf16[2,3,16,1024]{3,2,1,0:T(8,128)(2,1)S(1)} %get-tuple-element.42), channel_id=1, source_target_pairs={{0,24},{8,16},{16,8},{24,0},{1,25},{9,17},{17,9},{25,1},{2,26},{10... | collective-permute-start | bytes 589832 | tf_op jit(solution)/shard_map/ppermute | solution.py:697
  37.3 1.6 %collective-permute-start.7 = (bf16[64,1152]{1,0:T(8,128)(2,1)S(1)}, bf16[64,1152]{1,0:T(8,128)(2,1)S(1)}, u32[]{:S(2)}, u32[]{:S(2)}) collective-permute-start(bf16[64,1152]{1,0:T(8,128)(2,1)S(1)} %get-tuple-element.44.refs_5_.refs_2_), channel_id=1, source_target_pairs={{0,2},{2,0},{4,6},{6,4},{1,3},{3,1},{5,7},{7,5},{8,10},{10,8},{12,... | collective-permute-start | bytes 442376 | tf_op jit(solution)/shard_map/ppermute | solution.py:697
  38.9 2.6 %collective-permute-start.8 = (bf16[64,1152]{1,0:T(8,128)(2,1)S(1)}, bf16[64,1152]{1,0:T(8,128)(2,1)}, u32[]{:S(2)}, u32[]{:S(2)}) collective-permute-start(bf16[64,1152]{1,0:T(8,128)(2,1)S(1)} %get-tuple-element.44.refs_5_.refs_2_), channel_id=1, source_target_pairs={{0,4},{2,6},{4,0},{6,2},{1,5},{3,7},{5,1},{7,3},{8,12},{10,14},{12... | collective-permute-start | bytes 442376 | tf_op jit(solution)/shard_map/ppermute | solution.py:697
  41.5 3.1 %collective-permute-done.7.refs_3_ = bf16[64,1152]{1,0:T(8,128)(2,1)S(1)} collective-permute-done((bf16[64,1152]{1,0:T(8,128)(2,1)S(1)}, bf16[64,1152]{1,0:T(8,128)(2,1)S(1)}, u32[]{:S(2)}, u32[]{:S(2)}) %collective-permute-start.7) | collective-permute-done | bytes 147488 | tf_op jit(solution)/shard_map/ppermute | solution.py:697
  44.5 1.2 %collective-permute-done.10.refs_2_ = bf16[2,3,16,1024]{3,2,1,0:T(8,128)(2,1)S(1)} collective-permute-done((bf16[2,3,16,1024]{3,2,1,0:T(8,128)(2,1)S(1)}, bf16[2,3,16,1024]{3,2,1,0:T(8,128)(2,1)S(1)}, u32[]{:S(2)}, u32[]{:S(2)}) %collective-permute-start.10) | collective-permute-done | bytes 196640 | tf_op jit(solution)/shard_map/ppermute | solution.py:697
  45.8 1.9 %collective-permute-done.8.refs_4_ = bf16[64,1152]{1,0:T(8,128)(2,1)} collective-permute-done((bf16[64,1152]{1,0:T(8,128)(2,1)S(1)}, bf16[64,1152]{1,0:T(8,128)(2,1)}, u32[]{:S(2)}, u32[]{:S(2)}) %collective-permute-start.8) | collective-permute-done | bytes 147488 | tf_op jit(solution)/shard_map/ppermute | solution.py:697
  47.7 4.1 %all-to-all-start.1 = ((bf16[8,16,2048]{2,1,0:T(8,128)(2,1)}), bf16[8,16,2048]{2,1,0:T(8,128)(2,1)S(1)}, u32[]{:S(2)}, u32[]{:S(2)}) async-start(bf16[8,16,2048]{2,1,0:T(8,128)(2,1)} %bitcast.12), calls=%async_computation.1 | async-start | bytes 1048576 | tf_op jit(solution)/shard_map/all_to_all | solution.py:809
  51.8 2.0 %collective-permute-start.13 = (bf16[64,1152]{1,0:T(8,128)(2,1)S(1)}, bf16[64,1152]{1,0:T(8,128)(2,1)S(1)}, u32[]{:S(2)}, u32[]{:S(2)}) collective-permute-start(bf16[64,1152]{1,0:T(8,128)(2,1)S(1)} %get-tuple-element.44.refs_5_.refs_2_), channel_id=1, source_target_pairs={{0,6},{2,4},{4,2},{6,0},{1,7},{3,5},{5,3},{7,1},{8,14},{10,12},{12... | collective-permute-start | bytes 442376 | tf_op jit(solution)/shard_map/ppermute | solution.py:697
  53.8 0.2 collective-permute-start.14
  54.0 0.3 collective-permute-start.15
  54.3 0.2 collective-permute-start.16
  54.5 5.5 %collective-permute-done.13.refs_5_ = bf16[64,1152]{1,0:T(8,128)(2,1)S(1)} collective-permute-done((bf16[64,1152]{1,0:T(8,128)(2,1)S(1)}, bf16[64,1152]{1,0:T(8,128)(2,1)S(1)}, u32[]{:S(2)}, u32[]{:S(2)}) %collective-permute-start.13) | collective-permute-done | bytes 147488 | tf_op jit(solution)/shard_map/ppermute | solution.py:697
  60.1 0.7 %copy-done.12 = bf16[64,1152]{1,0:T(8,128)(2,1)} copy-done((bf16[64,1152]{1,0:T(8,128)(2,1)}, bf16[64,1152]{1,0:T(8,128)(2,1)S(1)}, u32[]{:S(2)}) %copy-start.12) | copy-done | bytes 147480
  60.8 0.7 %collective-permute-done.17.refs_9_ = bf16[64,1152]{1,0:T(8,128)(2,1)} collective-permute-done((bf16[64,1152]{1,0:T(8,128)(2,1)S(1)}, bf16[64,1152]{1,0:T(8,128)(2,1)}, u32[]{:S(2)}, u32[]{:S(2)}) %collective-permute-start.17) | collective-permute-done | bytes 147488 | tf_op jit(solution)/shard_map/ppermute | solution.py:697
  61.5 0.1 all-to-all-done.1.refs_17_
  61.6 0.8 %copy-done.6 = bf16[8,16,2048]{2,1,0:T(8,128)(2,1)} copy-done((bf16[8,16,2048]{2,1,0:T(8,128)(2,1)}, bf16[8,16,2048]{2,1,0:T(8,128)(2,1)S(1)}, u32[]{:S(2)}) %copy-start.6) | copy-done | bytes 524312
  62.4 1.0 %copy-done.7 = bf16[2,16,16,1024]{3,2,1,0:T(8,128)(2,1)} copy-done((bf16[2,16,16,1024]{3,2,1,0:T(8,128)(2,1)}, bf16[2,16,16,1024]{3,2,1,0:T(8,128)(2,1)S(1)}, u32[]{:S(2)}) %copy-start.7) | copy-done | bytes 1048600
  63.4 6.2 %gradients.1 = (bf16[16,4,2048]{2,1,0:T(4,128)(2,1)}, bf16[1024,256]{1,0:T(8,128)(2,1)}, bf16[256,1024]{1,0:T(8,128)(2,1)}) custom-call(bf16[2,16,16,1024]{3,2,1,0:T(8,128)(2,1)} %copy-done.1, bf16[2,16,16,1024]{3,2,1,0:T(8,128)(2,1)} %copy-done.7, bf16[64,1152]{1,0:T(8,128)(2,1)} %copy-done.2, bf16[64,1152]{1,0:T(8,128)(2,1)} %copy-done.8, ...), custom_call_target="tpu_custom_call" | custom-call | bytes 1048576 | tf_op jit(solution)/shard_map/gradients/pallas_call | solution.py:815
  (40 shorter events, 0.2 us)
Async XLA Ops:
  0.6 8.3 %copy-start.4 = (bf16[1,1,4096]{2,1,0:T(2,128)(2,1)S(1)}, bf16[1,1,4096]{2,1,0:T(2,128)(2,1)}, u32[]{:S(2)}) copy-start(bf16[1,1,4096]{2,1,0:T(2,128)(2,1)} %param.11) | copy-start | bytes 24580
  0.6 17.4 %collective-permute-start = (bf16[4096,256]{1,0:T(8,128)(2,1)}, bf16[4096,256]{1,0:T(8,128)(2,1)}, u32[]{:S(2)}, u32[]{:S(2)}) collective-permute-start(bf16[4096,256]{1,0:T(8,128)(2,1)} %bitcast.9), channel_id=1, source_target_pairs={{0,1},{1,0},{2,3},{3,2},{4,5},{5,4},{6,7},{7,6},{8,9},{9,8},{10,11... | collective-permute-start | bytes 6291464 | tf_op jit(solution)/shard_map/ppermute | solution.py:697
  1.2 23.2 %collective-permute-start.1 = (bf16[256,4096]{1,0:T(8,128)(2,1)}, bf16[256,4096]{1,0:T(8,128)(2,1)}, u32[]{:S(2)}, u32[]{:S(2)}) collective-permute-start(bf16[256,4096]{1,0:T(8,128)(2,1)} %bitcast.16), channel_id=1, source_target_pairs={{0,1},{1,0},{2,3},{3,2},{4,5},{5,4},{6,7},{7,6},{8,9},{9,8},{10,11... | collective-permute-start | bytes 6291464 | tf_op jit(solution)/shard_map/ppermute | solution.py:697
  3.7 20.7 %copy-start = (bf16[1,1,4096,256]{3,2,1,0:T(8,128)(2,1)S(1)}, bf16[1,1,4096,256]{3,2,1,0:T(8,128)(2,1)}, u32[]{:S(2)}) copy-start(bf16[1,1,4096,256]{3,2,1,0:T(8,128)(2,1)} %param.9) | copy-start | bytes 6291460
  3.7 20.7 %all-to-all-start = ((bf16[8,2,16,2048]{3,2,1,0:T(8,128)(2,1)}), bf16[8,2,16,2048]{3,2,1,0:T(8,128)(2,1)S(1)}, u32[]{:S(2)}, u32[]{:S(2)}) async-start(bf16[8,2,16,2048]{3,2,1,0:T(8,128)(2,1)} %pack.1._), calls=%async_computation | async-start | bytes 2097152 | tf_op jit(solution)/shard_map/all_to_all | solution.py:758
  9.0 7.5 %collective-permute-start.2 = (bf16[1,4096]{1,0:T(2,128)(2,1)S(1)}, bf16[1,4096]{1,0:T(2,128)(2,1)S(1)}, u32[]{:S(2)}, u32[]{:S(2)}) collective-permute-start(bf16[1,4096]{1,0:T(2,128)(2,1)S(1)} %bitcast.14), channel_id=1, source_target_pairs={{0,1},{1,0},{2,3},{3,2},{4,5},{5,4},{6,7},{7,6},{8,9},{9,8},{10,11... | collective-permute-start | bytes 24584 | tf_op jit(solution)/shard_map/ppermute | solution.py:697
  11.8 19.7 %collective-permute-start.3 = (bf16[80,1024]{1,0:T(8,128)(2,1)}, bf16[80,1024]{1,0:T(8,128)(2,1)S(1)}, u32[]{:S(2)}, u32[]{:S(2)}) collective-permute-start(bf16[80,1024]{1,0:T(8,128)(2,1)} %get-tuple-element.28), channel_id=1, source_target_pairs={{0,0},{1,4},{2,2},{3,6},{4,1},{5,5},{6,3},{7,7},{8,8},{9,12},{10,1... | collective-permute-start | bytes 491528 | tf_op jit(solution)/shard_map/ppermute | solution.py:761
  13.4 18.2 %collective-permute-start.4 = (bf16[80,1024]{1,0:T(8,128)(2,1)}, bf16[80,1024]{1,0:T(8,128)(2,1)}, u32[]{:S(2)}, u32[]{:S(2)}) collective-permute-start(bf16[80,1024]{1,0:T(8,128)(2,1)} %get-tuple-element.29), channel_id=1, source_target_pairs={{0,1},{1,5},{2,3},{3,7},{4,0},{5,4},{6,2},{7,6},{8,9},{9,13},{10,1... | collective-permute-start | bytes 491528 | tf_op jit(solution)/shard_map/ppermute | solution.py:761
  16.5 15.0 %copy-start.5 = (bf16[1,4096]{1,0:T(2,128)(2,1)}, bf16[1,4096]{1,0:T(2,128)(2,1)S(1)}, u32[]{:S(2)}) copy-start(bf16[1,4096]{1,0:T(2,128)(2,1)S(1)} %collective-permute-done.2.other_gain.refs_15_) | copy-start | bytes 24580
  16.5 15.1 %collective-permute-start.5 = (bf16[80,1024]{1,0:T(8,128)(2,1)}, bf16[80,1024]{1,0:T(8,128)(2,1)}, u32[]{:S(2)}, u32[]{:S(2)}) collective-permute-start(bf16[80,1024]{1,0:T(8,128)(2,1)} %get-tuple-element.30), channel_id=1, source_target_pairs={{0,2},{1,6},{2,0},{3,4},{4,3},{5,7},{6,1},{7,5},{8,10},{9,14},{10,... | collective-permute-start | bytes 491528 | tf_op jit(solution)/shard_map/ppermute | solution.py:761
  18.1 13.5 %collective-permute-start.6 = (bf16[80,1024]{1,0:T(8,128)(2,1)}, bf16[80,1024]{1,0:T(8,128)(2,1)}, u32[]{:S(2)}, u32[]{:S(2)}) collective-permute-start(bf16[80,1024]{1,0:T(8,128)(2,1)} %get-tuple-element.31), channel_id=1, source_target_pairs={{0,3},{1,7},{2,1},{3,5},{4,2},{5,6},{6,0},{7,4},{8,11},{9,15},{10,... | collective-permute-start | bytes 491528 | tf_op jit(solution)/shard_map/ppermute | solution.py:761
  31.5 16.2 %copy-start.3 = (bf16[4,2,16,2048]{3,2,1,0:T(8,128)(2,1)}, bf16[4,2,16,2048]{3,2,1,0:T(8,128)(2,1)S(1)}, u32[]{:S(2)}) copy-start(bf16[4,2,16,2048]{3,2,1,0:T(8,128)(2,1)S(1)} %get-tuple-element.47) | copy-start | bytes 1572868
  31.5 22.3 %copy-start.2 = (bf16[64,1152]{1,0:T(8,128)(2,1)}, bf16[64,1152]{1,0:T(8,128)(2,1)S(1)}, u32[]{:S(2)}) copy-start(bf16[64,1152]{1,0:T(8,128)(2,1)S(1)} %get-tuple-element.44.refs_5_.refs_2_) | copy-start | bytes 442372
  33.7 10.8 %collective-permute-start.9 = (bf16[2,3,16,1024]{3,2,1,0:T(8,128)(2,1)S(1)}, bf16[2,3,16,1024]{3,2,1,0:T(8,128)(2,1)S(1)}, u32[]{:S(2)}, u32[]{:S(2)}) collective-permute-start(bf16[2,3,16,1024]{3,2,1,0:T(8,128)(2,1)S(1)} %get-tuple-element.40), channel_id=1, source_target_pairs={{0,8},{8,0},{16,24},{24,16},{1,9},{9,1},{17,25},{25,17},{2,10},{10... | collective-permute-start | bytes 589832 | tf_op jit(solution)/shard_map/ppermute | solution.py:697
  34.3 11.4 %collective-permute-start.10 = (bf16[2,3,16,1024]{3,2,1,0:T(8,128)(2,1)S(1)}, bf16[2,3,16,1024]{3,2,1,0:T(8,128)(2,1)S(1)}, u32[]{:S(2)}, u32[]{:S(2)}) collective-permute-start(bf16[2,3,16,1024]{3,2,1,0:T(8,128)(2,1)S(1)} %get-tuple-element.41), channel_id=1, source_target_pairs={{0,16},{8,24},{16,0},{24,8},{1,17},{9,25},{17,1},{25,9},{2,18},{10... | collective-permute-start | bytes 589832 | tf_op jit(solution)/shard_map/ppermute | solution.py:697
  35.2 10.6 %collective-permute-start.11 = (bf16[2,3,16,1024]{3,2,1,0:T(8,128)(2,1)S(1)}, bf16[2,3,16,1024]{3,2,1,0:T(8,128)(2,1)S(1)}, u32[]{:S(2)}, u32[]{:S(2)}) collective-permute-start(bf16[2,3,16,1024]{3,2,1,0:T(8,128)(2,1)S(1)} %get-tuple-element.42), channel_id=1, source_target_pairs={{0,24},{8,16},{16,8},{24,0},{1,25},{9,17},{17,9},{25,1},{2,26},{10... | collective-permute-start | bytes 589832 | tf_op jit(solution)/shard_map/ppermute | solution.py:697
  37.3 7.2 %collective-permute-start.7 = (bf16[64,1152]{1,0:T(8,128)(2,1)S(1)}, bf16[64,1152]{1,0:T(8,128)(2,1)S(1)}, u32[]{:S(2)}, u32[]{:S(2)}) collective-permute-start(bf16[64,1152]{1,0:T(8,128)(2,1)S(1)} %get-tuple-element.44.refs_5_.refs_2_), channel_id=1, source_target_pairs={{0,2},{2,0},{4,6},{6,4},{1,3},{3,1},{5,7},{7,5},{8,10},{10,8},{12,... | collective-permute-start | bytes 442376 | tf_op jit(solution)/shard_map/ppermute | solution.py:697
  38.9 8.8 %collective-permute-start.8 = (bf16[64,1152]{1,0:T(8,128)(2,1)S(1)}, bf16[64,1152]{1,0:T(8,128)(2,1)}, u32[]{:S(2)}, u32[]{:S(2)}) collective-permute-start(bf16[64,1152]{1,0:T(8,128)(2,1)S(1)} %get-tuple-element.44.refs_5_.refs_2_), channel_id=1, source_target_pairs={{0,4},{2,6},{4,0},{6,2},{1,5},{3,7},{5,1},{7,3},{8,12},{10,14},{12... | collective-permute-start | bytes 442376 | tf_op jit(solution)/shard_map/ppermute | solution.py:697
  44.5 17.1 %copy-start.8 = (bf16[64,1152]{1,0:T(8,128)(2,1)}, bf16[64,1152]{1,0:T(8,128)(2,1)S(1)}, u32[]{:S(2)}) copy-start(bf16[64,1152]{1,0:T(8,128)(2,1)S(1)} %collective-permute-done.7.refs_3_) | copy-start | bytes 442372
  45.8 15.8 %copy-start.1 = (bf16[2,16,16,1024]{3,2,1,0:T(8,128)(2,1)}, bf16[2,16,16,1024]{3,2,1,0:T(8,128)(2,1)S(1)}, u32[]{:S(2)}) copy-start(bf16[2,16,16,1024]{3,2,1,0:T(8,128)(2,1)S(1)} %stack.1.refs_0_) | copy-start | bytes 3145732
  47.7 13.9 %collective-permute-start.12 = (bf16[2,16,16,1024]{3,2,1,0:T(8,128)(2,1)S(1)}, bf16[2,16,16,1024]{3,2,1,0:T(8,128)(2,1)S(1)}, u32[]{:S(2)}, u32[]{:S(2)}) collective-permute-start(bf16[2,16,16,1024]{3,2,1,0:T(8,128)(2,1)S(1)} %stack.1.refs_0_), channel_id=1, source_target_pairs={{0,1},{1,0},{2,3},{3,2},{4,5},{5,4},{6,7},{7,6},{8,9},{9,8},{10,11... | collective-permute-start | bytes 3145736 | tf_op jit(solution)/shard_map/ppermute | solution.py:697
  47.7 13.9 %all-to-all-start.1 = ((bf16[8,16,2048]{2,1,0:T(8,128)(2,1)}), bf16[8,16,2048]{2,1,0:T(8,128)(2,1)S(1)}, u32[]{:S(2)}, u32[]{:S(2)}) async-start(bf16[8,16,2048]{2,1,0:T(8,128)(2,1)} %bitcast.12), calls=%async_computation.1 | async-start | bytes 1048576 | tf_op jit(solution)/shard_map/all_to_all | solution.py:809
  51.8 8.2 %collective-permute-start.13 = (bf16[64,1152]{1,0:T(8,128)(2,1)S(1)}, bf16[64,1152]{1,0:T(8,128)(2,1)S(1)}, u32[]{:S(2)}, u32[]{:S(2)}) collective-permute-start(bf16[64,1152]{1,0:T(8,128)(2,1)S(1)} %get-tuple-element.44.refs_5_.refs_2_), channel_id=1, source_target_pairs={{0,6},{2,4},{4,2},{6,0},{1,7},{3,5},{5,3},{7,1},{8,14},{10,12},{12... | collective-permute-start | bytes 442376 | tf_op jit(solution)/shard_map/ppermute | solution.py:697
  53.8 6.2 %collective-permute-start.14 = (bf16[64,1152]{1,0:T(8,128)(2,1)S(1)}, bf16[64,1152]{1,0:T(8,128)(2,1)S(1)}, u32[]{:S(2)}, u32[]{:S(2)}) collective-permute-start(bf16[64,1152]{1,0:T(8,128)(2,1)S(1)} %get-tuple-element.44.refs_5_.refs_2_), channel_id=1, source_target_pairs={{0,1},{1,0},{2,3},{3,2},{4,5},{5,4},{6,7},{7,6},{8,9},{9,8},{10,11... | collective-permute-start | bytes 442376 | tf_op jit(solution)/shard_map/ppermute | solution.py:697
  54.0 6.0 %collective-permute-start.15 = (bf16[64,1152]{1,0:T(8,128)(2,1)S(1)}, bf16[64,1152]{1,0:T(8,128)(2,1)S(1)}, u32[]{:S(2)}, u32[]{:S(2)}) collective-permute-start(bf16[64,1152]{1,0:T(8,128)(2,1)S(1)} %collective-permute-done.7.refs_3_), channel_id=1, source_target_pairs={{0,1},{1,0},{2,3},{3,2},{4,5},{5,4},{6,7},{7,6},{8,9},{9,8},{10,11... | collective-permute-start | bytes 442376 | tf_op jit(solution)/shard_map/ppermute | solution.py:697
  54.3 5.7 %collective-permute-start.16 = (bf16[64,1152]{1,0:T(8,128)(2,1)}, bf16[64,1152]{1,0:T(8,128)(2,1)S(1)}, u32[]{:S(2)}, u32[]{:S(2)}) collective-permute-start(bf16[64,1152]{1,0:T(8,128)(2,1)} %collective-permute-done.8.refs_4_), channel_id=1, source_target_pairs={{0,1},{1,0},{2,3},{3,2},{4,5},{5,4},{6,7},{7,6},{8,9},{9,8},{10,11... | collective-permute-start | bytes 442376 | tf_op jit(solution)/shard_map/ppermute | solution.py:697
  60.0 1.6 %copy-start.9 = (bf16[64,1152]{1,0:T(8,128)(2,1)}, bf16[64,1152]{1,0:T(8,128)(2,1)S(1)}, u32[]{:S(2)}) copy-start(bf16[64,1152]{1,0:T(8,128)(2,1)S(1)} %collective-permute-done.13.refs_5_) | copy-start | bytes 442372
  60.0 1.5 %collective-permute-start.17 = (bf16[64,1152]{1,0:T(8,128)(2,1)S(1)}, bf16[64,1152]{1,0:T(8,128)(2,1)}, u32[]{:S(2)}, u32[]{:S(2)}) collective-permute-start(bf16[64,1152]{1,0:T(8,128)(2,1)S(1)} %collective-permute-done.13.refs_5_), channel_id=1, source_target_pairs={{0,1},{1,0},{2,3},{3,2},{4,5},{5,4},{6,7},{7,6},{8,9},{9,8},{10,11... | collective-permute-start | bytes 442376 | tf_op jit(solution)/shard_map/ppermute | solution.py:697
  60.0 1.6 %copy-start.10 = (bf16[64,1152]{1,0:T(8,128)(2,1)}, bf16[64,1152]{1,0:T(8,128)(2,1)S(1)}, u32[]{:S(2)}) copy-start(bf16[64,1152]{1,0:T(8,128)(2,1)S(1)} %collective-permute-done.14.refs_6_) | copy-start | bytes 442372
  60.0 1.6 %copy-start.11 = (bf16[64,1152]{1,0:T(8,128)(2,1)}, bf16[64,1152]{1,0:T(8,128)(2,1)S(1)}, u32[]{:S(2)}) copy-start(bf16[64,1152]{1,0:T(8,128)(2,1)S(1)} %collective-permute-done.15.refs_7_) | copy-start | bytes 442372
  61.6 0.8 %copy-start.6 = (bf16[8,16,2048]{2,1,0:T(8,128)(2,1)}, bf16[8,16,2048]{2,1,0:T(8,128)(2,1)S(1)}, u32[]{:S(2)}) copy-start(bf16[8,16,2048]{2,1,0:T(8,128)(2,1)S(1)} %all-to-all-done.1.refs_17_) | copy-start | bytes 1572868
  62.4 1.0 %copy-start.7 = (bf16[2,16,16,1024]{3,2,1,0:T(8,128)(2,1)}, bf16[2,16,16,1024]{3,2,1,0:T(8,128)(2,1)S(1)}, u32[]{:S(2)}) copy-start(bf16[2,16,16,1024]{3,2,1,0:T(8,128)(2,1)S(1)} %collective-permute-done.12.refs_1_) | copy-start | bytes 3145732
  (1 other events, 0.8 us)
